TPU v7x, 32 devices: a whole 2x2x4 slice. The times are simulated.
32 devices in a mesh: lon: 16 (over z, y, x), lat: 2 (over core).
Axes of the slice: x: 2, y: 2, z: 4, core: 2. Of those that a mesh axis runs over, the one named last changes fastest.
Arguments:
- tokens: bfloat16 [384, 48, 2, 512], P('lon', 'lat'), may hold values from -6 to 6
- qkv_weight: bfloat16 [2, 512, 1536], P(None, 'lon'), may hold values from -0.25 to 0.25
- out_weight: bfloat16 [2, 512, 512], P(None, 'lon'), may hold values from -0.25 to 0.25
- up_weight: bfloat16 [2, 512, 2048], P(None, 'lon'), may hold values from -0.25 to 0.25
- down_weight: bfloat16 [2, 512, 2048], P(None, 'lon'), may hold values from -0.125 to 0.125
- norm_gain: float32 [2, 2, 512], replicated, may hold values from 0.25 to 1.75
- logit_scale: float32 [2, 16], replicated, may hold values from 2 to 20
Outputs:
- mixed: bfloat16 [384, 48, 2, 512], P('lon', 'lat')
All inputs are finite; a program needn't handle non-finite values.
Results may differ from a plain program's by a relative error of at most 0.014.
Values may be sent and summed in bfloat16 or wider, within the bound.
No kernel may reach another device: no remote copies, remote signals or barrier semaphores. Data moves between devices by JAX's collectives and lax.ppermute only.
A program may use at most 128 MiB of HBM per device.

v0:
```python
import math

import jax
import jax.numpy as jnp
from jax import lax
from jax.sharding import PartitionSpec as P

HEADS = 16
WLON = 12
WLAT = 6
LEVELS = 2


def shifted_2(block, axis, distance):
    devices = range(lax.axis_size(axis))
    route = [((i - distance) % len(devices), i) for i in devices]
    return lax.ppermute(block, axis, route)


def layer_norm(value, gain_row):
    averaged = jnp.mean(value, -1, keepdims=True)
    centred = value - averaged
    variance = jnp.mean(centred * centred, -1, keepdims=True)
    return centred / jnp.sqrt(variance + 1e-05) * gain_row


def to_windows(local_cells):
    col_count, row_count, levels, features = local_cells.shape
    arranged = local_cells.reshape(
        col_count // WLON, WLON, row_count // WLAT, WLAT, levels, features
    )
    arranged = arranged.transpose(0, 2, 1, 3, 4, 5)
    return arranged.reshape(-1, WLON * WLAT * levels, features)


def from_windows(windows, col_count, row_count):
    features = windows.shape[-1]
    arranged = windows.reshape(col_count // WLON, row_count // WLAT, WLON, WLAT, LEVELS, features)
    arranged = arranged.transpose(0, 2, 1, 3, 4, 5)
    return arranged.reshape(col_count, row_count, LEVELS, features)


def window_groups(col_count, row_count, row_start, total_rows):
    lat_rows = row_start + jnp.arange(row_count, dtype=jnp.int32)
    wrapped = (lat_rows >= total_rows - WLAT // 2).astype(jnp.float32)
    flags = jnp.broadcast_to(wrapped[None, :, None], (col_count, row_count, LEVELS))
    flags = flags.reshape(col_count // WLON, WLON, row_count // WLAT, WLAT, LEVELS).transpose(
        0, 2, 1, 3, 4
    )
    return flags.reshape(-1, WLON * WLAT * LEVELS)


def unit_rows(vectors):
    length = jnp.sqrt(jnp.sum(vectors * vectors, -1, keepdims=True))
    return vectors / jnp.maximum(length, 0.5 * math.sqrt(vectors.shape[-1]))


def attend(triples, window_count, window_cells, sharpness_all, allowed):
    features = triples.shape[-1] // 3
    head_dim = features // HEADS
    grouped = triples.reshape(window_count, window_cells, 3, HEADS, head_dim)
    query_unit = unit_rows(grouped[:, :, 0].astype(jnp.float32))
    key_unit = unit_rows(grouped[:, :, 1].astype(jnp.float32))
    values = grouped[:, :, 2]
    scores = jnp.einsum("wqhd,wkhd->whqk", query_unit, key_unit, precision=lax.Precision.HIGHEST)
    scores = scores * sharpness_all[None, :, None, None]
    weights = jnp.exp(scores)
    if allowed is not None:
        weights = weights * allowed[:, None]
    weights = (weights / jnp.sum(weights, -1, keepdims=True)).astype(jnp.bfloat16)
    attended = jnp.einsum("whqk,wkhd->wqhd", weights, values, preferred_element_type=jnp.float32)
    return attended.astype(jnp.bfloat16).reshape(window_count * window_cells, features)


def down_columns(hidden, portion):
    return lax.dot_general(
        hidden, portion, (((1,), (1,)), ((), ())), preferred_element_type=jnp.float32
    )


def block_pass(local_cells, appliers, gain_pair, sharpness_all, row_start, total_rows, shifted):
    qkv_apply, out_apply, up_apply, down_apply = appliers
    col_count, row_count = (local_cells.shape[0], local_cells.shape[1])
    windows = to_windows(local_cells)
    window_count, window_cells, features = windows.shape
    token_rows = windows.reshape(window_count * window_cells, features)
    allowed = None
    if shifted:
        groups = window_groups(col_count, row_count, row_start, total_rows)
        allowed = (groups[:, :, None] == groups[:, None, :]).astype(jnp.float32)
    triples = qkv_apply(token_rows).astype(jnp.bfloat16)
    attended = attend(triples, window_count, window_cells, sharpness_all, allowed)
    projected = out_apply(attended)
    middle = (token_rows.astype(jnp.float32) + layer_norm(projected, gain_pair[0])).astype(
        jnp.bfloat16
    )
    hidden = jax.nn.gelu(up_apply(middle)).astype(jnp.bfloat16)
    down_sum = down_apply(hidden)
    result = (middle.astype(jnp.float32) + layer_norm(down_sum, gain_pair[1])).astype(jnp.bfloat16)
    return from_windows(result.reshape(window_count, window_cells, features), col_count, row_count)


def per_device(tokens, qkv_weight, out_weight, up_weight, down_weight, norm_gain, logit_scale):
    row_count = tokens.shape[1]
    row_start = lax.axis_index("lat") * row_count
    total_rows = row_count * lax.axis_size("lat")
    half_lon = WLON // 2
    half_lat = WLAT // 2

    def make_appliers(block_index):

        def qkv_apply(token_rows):
            full_panel = lax.all_gather(qkv_weight[block_index], "lon", axis=0, tiled=True)
            return jnp.dot(token_rows, full_panel, preferred_element_type=jnp.float32)

        def out_apply(attended):
            full_panel = lax.all_gather(out_weight[block_index], "lon", axis=0, tiled=True)
            return jnp.dot(attended, full_panel, preferred_element_type=jnp.float32)

        def up_apply(middle):
            full_panel = lax.all_gather(up_weight[block_index], "lon", axis=0, tiled=True)
            return jnp.dot(middle, full_panel, preferred_element_type=jnp.float32)

        def down_apply(hidden):
            return down_columns(
                hidden, lax.all_gather(down_weight[block_index], "lon", axis=0, tiled=True)
            )

        return (qkv_apply, out_apply, up_apply, down_apply)

    plain_out = block_pass(
        tokens, make_appliers(0), norm_gain[0], logit_scale[0], row_start, total_rows, False
    )
    ahead_cols = shifted_2(plain_out[:half_lon], "lon", -1)
    shifted_cols = jnp.concatenate([plain_out[half_lon:], ahead_cols], 0)
    upper_rows = shifted_2(shifted_cols[:, :half_lat], "lat", -1)
    rolled = jnp.concatenate([shifted_cols[:, half_lat:], upper_rows], 1)
    second = block_pass(
        rolled, make_appliers(1), norm_gain[1], logit_scale[1], row_start, total_rows, True
    )
    lower_rows = shifted_2(second[:, -half_lat:], "lat", 1)
    back_rows = jnp.concatenate([lower_rows, second[:, :-half_lat]], 1)
    behind_cols = shifted_2(back_rows[-half_lon:], "lon", 1)
    return jnp.concatenate([behind_cols, back_rows[:-half_lon]], 0)


def solution(mesh):
    placed = (
        P("lon", "lat", None, None),
        P(None, "lon", None),
        P(None, "lon", None),
        P(None, "lon", None),
        P(None, "lon", None),
        P(),
        P(),
    )
    return jax.shard_map(
        per_device,
        mesh=mesh,
        in_specs=placed,
        out_specs=P("lon", "lat", None, None),
        check_vma=False,
    )
```

profile of v0, /device:TPU:0, one launch (start us, length us, event | category | flops | bytes accessed | tf_op | source)
XLA Modules:
  0.0 418.7 jit_solution(8697471395353146778)
XLA Ops:
  6.5 1.8 fusion.59
  8.4 1.7 fusion.57
  10.1 1.7 fusion.58
  11.9 0.5 all-gather.21.cloned.1.call-update
  12.5 0.5 all-gather.23.cloned.1.call-update
  13.1 0.5 all-gather.25.cloned.1.call-update
  13.6 0.8 copy.65
  14.5 0.5 reshape_reshape.12
  15.0 48.8 %all-gather.1 = bf16[1,512,512]{2,1,0:T(8,128)(2,1)} all-gather(bf16[1,32,512]{2,1,0:T(8,128)(2,1)S(1)} %get-tuple-element.20), channel_id=3, replica_groups=mesh['lon'=16,'lat'=2] {'lon'}, dimensions={1}, use_global_device_ids=true | all-gather | bytes 557056 | tf_op jit(solution)/shard_map/all_gather | solution.py:117
  63.8 0.6 fusion.61
  64.4 41.3 %all-gather.5 = bf16[1,512,512]{2,1,0:T(8,128)(2,1)} all-gather(bf16[1,32,512]{2,1,0:T(8,128)(2,1)S(1)} %get-tuple-element.19), channel_id=7, replica_groups=mesh['lon'=16,'lat'=2] {'lon'}, dimensions={1}, use_global_device_ids=true | all-gather | bytes 557056 | tf_op jit(solution)/shard_map/all_gather | solution.py:117
  105.7 5.2 %convolution_convert_fusion.1 = bf16[1152,1536]{1,0:T(8,128)(2,1)} fusion(bf16[1152,512]{1,0:T(8,128)(2,1)S(1)} %reshape_reshape.12, bf16[1,512,1536]{2,1,0:T(8,128)(2,1)} %all-gather.15.cloned.1.call-done), kind=kOutput, calls=%fused_computation.27 | convolution fusion | flops 1813708800 | bytes 6291456 | tf_op jit(solution)/shard_map/dot_general | solution.py:114
  110.9 4.5 %copy.19 = bf16[1152,1536]{0,1:T(8,128)(2,1)S(1)} copy(bf16[1152,1536]{1,0:T(8,128)(2,1)} %convolution_convert_fusion.1) | data formatting | bytes 7077888 | tf_op jit(solution)/shard_map/convert_element_type | solution.py:91
  115.4 9.2 %reshape.130 = bf16[8,144,3,16,32]{1,0,4,3,2:T(8,128)(2,1)} reshape(bf16[1152,1536]{0,1:T(8,128)(2,1)S(1)} %copy.19) | data formatting | bytes 7077888 | tf_op jit(solution)/shard_map/reshape | solution.py:61
  124.6 3.4 fusion.20
  128.0 0.6 copy-done
  128.6 1.1 convert_divide_fusion.3
  129.8 22.2 %fusion = (f32[8,16,144]{2,1,0:T(8,128)S(1)}, f32[8,16,144,144]{2,3,1,0:T(8,128)}) fusion(f32[16]{0:T(128)S(1)} %get-tuple-element.26, f32[8,144,16,32]{1,0,3,2:T(8,128)S(1)} %get-tuple-element.12, f32[8,144,16,32]{1,0,3,2:T(8,128)S(1)} %get-tuple-element.11), kind=kOutput, calls=%fused_computation.4 | convolution fusion | flops 1024505856 | bytes 15409216 | tf_op jit(solution)/shard_map/wqhd,wkhd->whqk/dot_general | solution.py:65
  152.0 8.2 %convert_bitcast_fusion.1 = bf16[8,144,16,32]{1,3,2,0:T(8,128)(2,1)S(1)} fusion(f32[8,16,144,144]{2,3,1,0:T(8,128)} %get-tuple-element.28, f32[8,16,144]{2,1,0:T(8,128)S(1)} %get-tuple-element.27, f32[16]{0:T(128)S(1)} %get-tuple-element.26, bf16[8,144,1,16,32]{1,0,4,3,2:T(8,128)(2,1)S(1)} %slice-done), kind=kOutput, calls=%fused_computation.67 | convolution fusion | flops 178421760 | bytes 13049920 | tf_op jit(solution)/shard_map/whqk,wkhd->wqhd/dot_general | solution.py:71
  160.2 1.4 copy.24
  161.6 2.3 reshape.131
  163.9 2.0 fusion.62
  165.9 0.5 multiply_reduce_fusion.3
  166.5 0.6 add_convert_fusion.3
  167.1 31.3 %all-gather.19.cloned.1.call-done = bf16[1,512,2048]{2,1,0:T(8,128)(2,1)} async-done(((bf16[1,32,2048]{2,1,0:T(8,128)(2,1)}), bf16[1,512,2048]{2,1,0:T(8,128)(2,1)}) %all-gather.19.cloned.1.call-update) | async-done | bytes 2097168 | tf_op jit(solution)/shard_map/all_gather | solution.py:126
  198.4 8.3 %fusion.63 = (f32[1152]{0:T(1024)}, f32[1152,512]{1,0:T(8,128)S(1)}) fusion(bf16[1,512,2048]{2,1,0:T(8,128)(2,1)} %all-gather.19.cloned.1.call-done, bf16[1152,512]{1,0:T(8,128)(2,1)S(1)} %add_convert_fusion.3, bf16[1,512,2048]{2,1,0:T(8,128)(2,1)} %all-gather.17.cloned.1.call-done), kind=kOutput, calls=%fused_computation.114 | convolution fusion | flops 4853660672 | bytes 7737856 | tf_op jit(solution)/shard_map/dot_general | solution.py:76
  206.7 0.8 broadcast_multiply_fusion.2
  207.5 0.5 multiply_reduce_fusion.2
  208.0 0.6 add_convert_fusion.2
  208.6 0.5 reshape_reshape.13
  209.1 1.2 copy.25
  210.5 2.9 collective-permute-start
  213.7 1.3 compare_convert_fusion
  215.0 0.7 slice.125
  215.7 4.7 %collective-permute-done = bf16[6,24,2,512]{3,2,1,0:T(2,128)(2,1)S(1)} collective-permute-done((bf16[6,24,2,512]{3,2,1,0:T(2,128)(2,1)S(1)}, bf16[6,24,2,512]{3,2,1,0:T(2,128)(2,1)S(1)}, u32[]{:S(2)}, u32[]{:S(2)}) %collective-permute-start) | collective-permute-done | bytes 294944 | tf_op jit(solution)/shard_map/ppermute | solution.py:17
  220.7 1.8 fusion.43
  222.5 1.5 pad_maximum_fusion.1
  224.0 0.8 copy.26
  224.8 0.5 reshape_reshape.14
  225.3 33.8 %all-gather.21.cloned.1.call-done = bf16[1,512,1536]{2,1,0:T(8,128)(2,1)} async-done(((bf16[1,32,1536]{2,1,0:T(8,128)(2,1)}), bf16[1,512,1536]{2,1,0:T(8,128)(2,1)}) %all-gather.21.cloned.1.call-update) | async-done | bytes 1572880 | tf_op jit(solution)/shard_map/all_gather | solution.py:113
  259.1 5.2 %convolution_convert_fusion = bf16[1152,1536]{1,0:T(8,128)(2,1)} fusion(bf16[1152,512]{1,0:T(8,128)(2,1)S(1)} %reshape_reshape.14, bf16[1,512,1536]{2,1,0:T(8,128)(2,1)} %all-gather.21.cloned.1.call-done), kind=kOutput, calls=%fused_computation.26 | convolution fusion | flops 1813708800 | bytes 6291456 | tf_op jit(solution)/shard_map/dot_general | solution.py:114
  264.3 4.4 %copy.27 = bf16[1152,1536]{0,1:T(8,128)(2,1)S(1)} copy(bf16[1152,1536]{1,0:T(8,128)(2,1)} %convolution_convert_fusion) | data formatting | bytes 7077888 | tf_op jit(solution)/shard_map/convert_element_type | solution.py:91
  268.7 9.2 %reshape.134 = bf16[8,144,3,16,32]{1,0,4,3,2:T(8,128)(2,1)} reshape(bf16[1152,1536]{0,1:T(8,128)(2,1)S(1)} %copy.27) | data formatting | bytes 7077888 | tf_op jit(solution)/shard_map/reshape | solution.py:61
  277.8 3.4 fusion.22
  281.3 0.6 copy-done.1
  281.9 1.1 convert_divide_fusion.1
  283.1 23.6 %fusion.1 = (f32[8,16,144]{2,1,0:T(8,128)S(1)}, f32[8,16,144,144]{2,3,1,0:T(8,128)}) fusion(f32[8,144,144]{1,2,0:T(8,128)S(1)} %copy-done.2, f32[16]{0:T(128)S(1)} %get-tuple-element.25, f32[8,144,16,32]{1,0,3,2:T(8,128)S(1)} %get-tuple-element.10, f32[8,144,16,32]{1,0,3,2:T(8,128)S(1)} %get-tuple-element.9), kind=kOutput, calls=%fused_computation.5 | convolution fusion | flops 1027160064 | bytes 16072768 | tf_op jit(solution)/shard_map/wqhd,wkhd->whqk/dot_general | solution.py:65
  306.7 8.6 %convert_bitcast_fusion = bf16[8,144,16,32]{1,3,2,0:T(8,128)(2,1)S(1)} fusion(f32[8,16,144,144]{2,3,1,0:T(8,128)} %get-tuple-element.34, f32[8,16,144]{2,1,0:T(8,128)S(1)} %get-tuple-element.33, f32[8,144,144]{1,2,0:T(8,128)S(1)} %copy-done.2, f32[16]{0:T(128)S(1)} %get-tuple-element.25, bf16[8,144,1,16,32]{1,0,4,3,2:T(8,128)(2,1)S(1)} %slice-done.1), kind=kOutput, calls=%fused_computation.66 | convolution fusion | flops 181075968 | bytes 13713472 | tf_op jit(solution)/shard_map/whqk,wkhd->wqhd/dot_general | solution.py:71
  315.3 1.4 copy.34
  316.7 2.3 reshape.135
  319.0 2.0 fusion.66
  321.1 0.5 multiply_reduce_fusion.1
  321.6 0.6 add_convert_fusion.1
  322.2 61.0 %all-gather.25.cloned.1.call-done = bf16[1,512,2048]{2,1,0:T(8,128)(2,1)} async-done(((bf16[1,32,2048]{2,1,0:T(8,128)(2,1)}), bf16[1,512,2048]{2,1,0:T(8,128)(2,1)}) %all-gather.25.cloned.1.call-update) | async-done | bytes 2097168 | tf_op jit(solution)/shard_map/all_gather | solution.py:126
  383.2 7.7 %fusion.67 = (f32[1152]{0:T(1024)S(1)}, f32[1152,512]{1,0:T(8,128)S(1)}) fusion(bf16[1,512,2048]{2,1,0:T(8,128)(2,1)} %all-gather.25.cloned.1.call-done, bf16[1152,512]{1,0:T(8,128)(2,1)S(1)} %add_convert_fusion.1, bf16[1,512,2048]{2,1,0:T(8,128)(2,1)} %all-gather.23.cloned.1.call-done), kind=kOutput, calls=%fused_computation.116 | convolution fusion | flops 4853660672 | bytes 7737856 | tf_op jit(solution)/shard_map/dot_general | solution.py:76
  391.5 0.8 copy-done.8
  392.2 0.6 add_convert_fusion
  392.8 0.5 reshape_reshape.15
  393.3 1.2 copy.35
  394.7 0.7 slice.133
  395.4 0.6 collective-permute-done.2
  396.4 1.3 collective-permute-start.3
  397.8 11.4 %collective-permute-done.3 = bf16[6,24,2,512]{3,2,1,0:T(2,128)(2,1)S(1)} collective-permute-done((bf16[6,24,2,512]{3,2,1,0:T(2,128)(2,1)S(1)}, bf16[6,24,2,512]{3,2,1,0:T(2,128)(2,1)S(1)}, u32[]{:S(2)}, u32[]{:S(2)}) %collective-permute-start.3) | collective-permute-done | bytes 294944 | tf_op jit(solution)/shard_map/ppermute | solution.py:17
  409.1 2.5 fusion.42
  (71 shorter events, 2.5 us)
Async XLA Ops:
  6.5 7.1 %copy-start.11 = (bf16[24,24,2,512]{3,2,1,0:T(2,128)(2,1)S(1)}, bf16[24,24,2,512]{3,2,1,0:T(2,128)(2,1)}, u32[]{:S(2)}) copy-start(bf16[24,24,2,512]{3,2,1,0:T(2,128)(2,1)} %param.7) | copy-start | bytes 3538948
  6.5 99.2 %all-gather.15.cloned.1.call-start = ((), (), s32[]{:S(2)}) async-start(), calls=%async_computation | async-start | bytes 1671168 | tf_op jit(solution)/shard_map/all_gather | solution.py:113
  8.3 158.7 %all-gather.17.cloned.1.call-start = ((), (), s32[]{:S(2)}) async-start(), calls=%async_computation.1 | async-start | bytes 2228224 | tf_op jit(solution)/shard_map/all_gather | solution.py:121
  10.1 188.3 %all-gather.19.cloned.1.call-start = ((), (), s32[]{:S(2)}) async-start(), calls=%async_computation.2 | async-start | bytes 2228224 | tf_op jit(solution)/shard_map/all_gather | solution.py:126
  11.9 247.2 %all-gather.21.cloned.1.call-start = ((), (), s32[]{:S(2)}) async-start(), calls=%async_computation.3 | async-start | bytes 1671168 | tf_op jit(solution)/shard_map/all_gather | solution.py:113
  12.4 309.7 %all-gather.23.cloned.1.call-start = ((), (), s32[]{:S(2)}) async-start(), calls=%async_computation.4 | async-start | bytes 2228224 | tf_op jit(solution)/shard_map/all_gather | solution.py:121
  13.0 370.2 %all-gather.25.cloned.1.call-start = ((), (), s32[]{:S(2)}) async-start(), calls=%async_computation.5 | async-start | bytes 2228224 | tf_op jit(solution)/shard_map/all_gather | solution.py:126
  13.6 1.4 copy-start.16
  13.6 1.4 copy-start.12
  13.6 50.2 %copy-start.15 = (f32[2,2,512]{2,1,0:T(2,128)S(1)}, f32[2,2,512]{2,1,0:T(2,128)}, u32[]{:S(2)}) copy-start(f32[2,2,512]{2,1,0:T(2,128)} %param.12) | copy-start | bytes 24580
  15.0 90.7 %copy-start.3 = (bf16[1152,512]{1,0:T(8,128)(2,1)}, bf16[1152,512]{1,0:T(8,128)(2,1)S(1)}, u32[]{:S(2)}) copy-start(bf16[1152,512]{1,0:T(8,128)(2,1)S(1)} %reshape_reshape.12) | copy-start | bytes 3538948
  124.6 4.1 copy-start
  129.7 22.3 %slice-start = ((bf16[8,144,3,16,32]{1,0,4,3,2:T(8,128)(2,1)}), bf16[8,144,1,16,32]{1,0,4,3,2:T(8,128)(2,1)S(1)}, s32[]{:S(2)}) async-start(bf16[8,144,3,16,32]{1,0,4,3,2:T(8,128)(2,1)} %reshape.130), calls=%async_computation.6 | async-start | bytes 4194304 | tf_op jit(solution)/shard_map/slice | solution.py:64
  163.9 2.5 copy-start.4
  163.9 2.5 copy-start.14
  167.0 39.7 %copy-start.9 = (bf16[1152,512]{1,0:T(8,128)(2,1)}, bf16[1152,512]{1,0:T(8,128)(2,1)S(1)}, u32[]{:S(2)}) copy-start(bf16[1152,512]{1,0:T(8,128)(2,1)S(1)} %add_convert_fusion.3) | copy-start | bytes 3538948
  206.7 1.3 copy-start.13
  206.7 1.3 copy-start.10
  210.5 9.9 %collective-permute-start = (bf16[6,24,2,512]{3,2,1,0:T(2,128)(2,1)S(1)}, bf16[6,24,2,512]{3,2,1,0:T(2,128)(2,1)S(1)}, u32[]{:S(2)}, u32[]{:S(2)}) collective-permute-start(bf16[6,24,2,512]{3,2,1,0:T(2,128)(2,1)S(1)} %slice.126), channel_id=1, source_target_pairs={{2,0},{4,2},{6,4},{8,6},{10,8},{12,10},{14,12},{16,14},{18,16},{20... | collective-permute-start | bytes 884744 | tf_op jit(solution)/shard_map/ppermute | solution.py:17
  220.6 1.9 collective-permute-start.1
  225.3 33.8 %copy-start.5 = (bf16[1152,512]{1,0:T(8,128)(2,1)}, bf16[1152,512]{1,0:T(8,128)(2,1)S(1)}, u32[]{:S(2)}) copy-start(bf16[1152,512]{1,0:T(8,128)(2,1)S(1)} %reshape_reshape.14) | copy-start | bytes 3538948
  277.8 4.0 copy-start.1
  281.9 1.3 copy-start.2
  283.1 23.6 %slice-start.1 = ((bf16[8,144,3,16,32]{1,0,4,3,2:T(8,128)(2,1)}), bf16[8,144,1,16,32]{1,0,4,3,2:T(8,128)(2,1)S(1)}, s32[]{:S(2)}) async-start(bf16[8,144,3,16,32]{1,0,4,3,2:T(8,128)(2,1)} %reshape.134), calls=%async_computation.7 | async-start | bytes 4194304 | tf_op jit(solution)/shard_map/slice | solution.py:64
  319.0 2.5 copy-start.6
  322.1 68.8 %copy-start.7 = (bf16[1152,512]{1,0:T(8,128)(2,1)}, bf16[1152,512]{1,0:T(8,128)(2,1)S(1)}, u32[]{:S(2)}) copy-start(bf16[1152,512]{1,0:T(8,128)(2,1)S(1)} %add_convert_fusion.1) | copy-start | bytes 3538948
  391.0 1.3 copy-start.8
  394.6 1.4 collective-permute-start.2
  396.4 12.7 %collective-permute-start.3 = (bf16[6,24,2,512]{3,2,1,0:T(2,128)(2,1)S(1)}, bf16[6,24,2,512]{3,2,1,0:T(2,128)(2,1)S(1)}, u32[]{:S(2)}, u32[]{:S(2)}) collective-permute-start(bf16[6,24,2,512]{3,2,1,0:T(2,128)(2,1)S(1)} %pad_maximum_fusion.2), channel_id=1, source_target_pairs={{30,0},{0,2},{2,4},{4,6},{6,8},{8,10},{10,12},{12,14},{14,16},{16,... | collective-permute-start | bytes 884744 | tf_op jit(solution)/shard_map/ppermute | solution.py:17
Sparse Core Ops, SparseCore 0:
  10.1 62.8 all-gather.14
  75.8 60.4 all-gather.16
  139.0 59.3 all-gather.18
  201.0 58.0 all-gather.20
  261.7 59.4 all-gather.22
  323.8 59.3 all-gather.24
where the time goes:
time: 422 us; the launch traced here: 419 us
  waiting for transfers between devices  145 us (34%)
  matrix products  93.1 us (22%)
  blocking collectives  90.1 us (21%)
  local copies, waits for them, and re-layouts  50.4 us (12%)
  other arithmetic  21.8 us (5%)
  between operations  14.2 us (3%)
  starting transfers between devices  4.59 us (1%)
    all_gather x2, waiting for transfers between devices, down_apply(): lax.all_gather(down_weight[block_index], 'lon', axis=0, tiled=True)  92.4 us
    all_gather x2, blocking collectives, out_apply(): lax.all_gather(out_weight[block_index], 'lon', axis=0, tiled=True)  90.1 us
    dot_general x2, matrix products, attend(): jnp.einsum('wqhd,wkhd->whqk', query_unit, key_unit, precision=lax.Precisi...  45.8 us
    all_gather x2, waiting for transfers between devices, qkv_apply(): lax.all_gather(qkv_weight[block_index], 'lon', axis=0, tiled=True)  33.8 us
    reshape x2, local copies, waits for them, and re-layouts, attend(): grouped = triples.reshape(window_count, window_cells, 3, HEADS, head_dim)  18.3 us
    dot_general x2, matrix products, attend(): jnp.einsum('whqk,wkhd->wqhd', weights, values, preferred_element_type=jnp...  16.8 us
    ppermute x4, waiting for transfers between devices, shifted_2(): return lax.ppermute(block, axis, route)  16.7 us
    dot_general x2, matrix products, down_columns(): lax.dot_general(hidden, portion, (((1,), (1,)), ((), ())), preferred_elem...  16.1 us
  transfers between devices with their start and end apart: 10, of which 6 were waited for; matrix products, arithmetic and copies ran while one was open for 35% of the time, Pallas kernels for 0%

commit v1 on v0

v1 whole, which is shorter than its diff:
```python
import functools
import math

import numpy as np

import jax
import jax.numpy as jnp
from jax import lax
from jax.experimental import pallas as pl
from jax.experimental.pallas import tpu as pltpu
from jax.sharding import PartitionSpec as P

HEADS = 16
HEAD = 32
WLON = 12
WLAT = 6
LEVELS = 2
CELLS = WLON * WLAT * LEVELS
MAIN = 128
REST = CELLS - MAIN
GROUP = 8
WIDE = GROUP * HEAD
ANY = pl.BlockSpec(memory_space=pl.ANY)
NT = (((1,), (1,)), ((), ()))


def dot(a, b, dims=(((1,), (0,)), ((), ()))):
    return lax.dot_general(a, b, dims, preferred_element_type=jnp.float32)


def layer_norm(value, gain_row):
    averaged = jnp.mean(value, -1, keepdims=True)
    centred = value - averaged
    variance = jnp.mean(centred * centred, -1, keepdims=True)
    return centred * lax.rsqrt(variance + 1e-05) * gain_row


def relayed(rows, lat_size):
    return lat_size == 2 and rows % 32 == 0


def cut_kernel(half, qkv_ref, out_ref, up_ref, down_ref, *refs):
    chunks, sems = refs[:-1], refs[-1]
    first = pl.multiple_of(lax.axis_index("lat") * half, 16)
    copies = []
    for index, target in enumerate(chunks):
        block, part = divmod(index, 2)
        place = 0
        for source in ((qkv_ref, out_ref), (up_ref, down_ref))[part]:
            width = source.shape[2]
            copies.append(
                pltpu.make_async_copy(
                    source.at[block, pl.ds(first, half), :],
                    target.at[0, :, pl.ds(place, width)],
                    sems.at[len(copies)],
                )
            )
            place += width
    for copy in copies:
        copy.start()
    for copy in copies:
        copy.wait()


def cut_chunks(qkv_weight, out_weight, up_weight, down_weight):
    blocks, rows, _ = qkv_weight.shape
    widths = (
        qkv_weight.shape[2] + out_weight.shape[2],
        up_weight.shape[2] + down_weight.shape[2],
    )
    return pl.pallas_call(
        functools.partial(cut_kernel, rows // 2),
        out_shape=[
            jax.ShapeDtypeStruct((1, rows // 2, width), jnp.bfloat16) for width in widths * blocks
        ],
        in_specs=[ANY] * 4,
        out_specs=[ANY] * (2 * blocks),
        scratch_shapes=[pltpu.SemaphoreType.DMA((4 * blocks,))],
    )(qkv_weight, out_weight, up_weight, down_weight)


def send(block, lon_size, move):
    pairs = []
    for lon in range(lon_size):
        for core in range(2):
            z, y, x, core_to = move(lon // 4, lon // 2 % 2, lon % 2, core)
            pairs.append((lon * 2 + core, (z * 4 + y * 2 + x) * 2 + core_to))
    return lax.ppermute(block, ("lon", "lat"), pairs)


def relay(own, lon_size):
    depth = lon_size // 4
    column = [own] + [
        send(own, lon_size, lambda z, y, x, c, step=step: ((z + step) % depth, y, x, c))
        for step in range(1, depth)
    ]
    column = jnp.concatenate(column, 0)
    beside = send(
        column, lon_size, lambda z, y, x, c: (z, y, 1 - x, c) if c == 0 else (z, 1 - y, x, c)
    )
    first = jnp.concatenate([column, beside], 0)
    second = send(
        first, lon_size, lambda z, y, x, c: (z, 1 - y, x, c) if c == 0 else (z, y, 1 - x, c)
    )
    swap = lambda z, y, x, c: (z, y, x, 1 - c)
    return [first, second, send(first, lon_size, swap), send(second, lon_size, swap)]


def load_pieces(pieces, w_ref, sem):
    if len(pieces) == 1:
        copy = pltpu.make_async_copy(pieces[0].at[0], w_ref, sem)
        copy.start()
        copy.wait()
        return
    depth = pieces[0].shape[0] // 2
    half = pieces[0].shape[1]
    lon, lat = lax.axis_index("lon"), lax.axis_index("lat")
    z, y, x = lon // 4, lon // 2 % 2, lon % 2
    for index, piece in enumerate(pieces):
        core = lat if index < 2 else 1 - lat
        if index % 2 == 0:
            squares = (y * 2 + x, jnp.where(core == 0, y * 2 + 1 - x, (1 - y) * 2 + x))
        else:
            squares = (
                jnp.where(core == 0, (1 - y) * 2 + x, y * 2 + 1 - x),
                (1 - y) * 2 + 1 - x,
            )
        for j in range(2 * depth):
            shard = (z + depth - j % depth) % depth * 4 + squares[j // depth]
            row = pl.multiple_of((shard * 2 + core) * half, 16)
            pltpu.make_async_copy(piece.at[j], w_ref.at[pl.ds(row, half), :], sem).start()
    pltpu.make_async_copy(w_ref, w_ref, sem).wait()


def attend_kernel(shifted, row_windows, count, *refs):
    x_ref, pieces = refs[0], refs[1 : 1 + count]
    gain_ref, sharp_ref = refs[1 + count : 3 + count]
    allow_ref = refs[3 + count] if shifted else None
    out_ref, w_ref, vt_ref, sem = refs[-4:]
    features = x_ref.shape[-1]

    @pl.when(pl.program_id(0) == 0)
    def _():
        load_pieces(pieces, w_ref, sem)
        vt_ref[...] = w_ref[:, 2 * features : 3 * features].T

    tokens = x_ref[0]
    queries = dot(tokens, w_ref[:, :features]).astype(jnp.bfloat16).astype(jnp.float32)
    keys = dot(tokens, w_ref[:, features : 2 * features]).astype(jnp.bfloat16).astype(jnp.float32)
    values = dot(vt_ref[...], tokens, NT).astype(jnp.bfloat16)

    channel = lax.broadcasted_iota(jnp.int32, (WIDE, WIDE), 0) // HEAD
    same_head = jnp.where(
        channel == lax.broadcasted_iota(jnp.int32, (WIDE, WIDE), 1) // HEAD, 1.0, 0.0
    ).astype(jnp.bfloat16)
    lane_head = lax.broadcasted_iota(jnp.int32, (1, WIDE), 1) // HEAD
    diagonal = (
        lax.broadcasted_iota(jnp.int32, (WIDE, MAIN), 0) // HEAD
        == lax.broadcasted_iota(jnp.int32, (WIDE, MAIN), 1) // REST
    )
    if shifted:
        last = jnp.logical_and(
            pl.program_id(0) % row_windows == row_windows - 1,
            lax.axis_index("lat") == lax.axis_size("lat") - 1,
        )
        allow = jnp.where(last, allow_ref[...], 1.0)
        allow_main = jnp.concatenate([allow[:, :MAIN]] * 2, 1)
        allow_rest = allow[:, MAIN:]

    def units(part):
        squares = (part * part).astype(jnp.bfloat16)
        length2 = dot(squares, same_head)
        return part * lax.rsqrt(jnp.maximum(length2, 0.25 * HEAD))

    main_rows, rest_rows = [], []
    for group in range(HEADS // GROUP):
        lanes = slice(group * WIDE, (group + 1) * WIDE)
        query = (units(queries[:, lanes]) * sharp_ref[:, lanes]).astype(jnp.bfloat16)
        key = units(keys[:, lanes]).astype(jnp.bfloat16)
        value = values[lanes]

        def masked(rows, head):
            return jnp.where(lane_head == head, rows, jnp.zeros_like(rows))

        def weights(stacked, allowed):
            scores = dot(key, stacked, NT)
            powers = jnp.exp2(scores)
            if shifted:
                powers = powers * allowed
            return powers.astype(jnp.bfloat16), 1.0 / jnp.sum(powers, 0, keepdims=True)

        for pair in range(GROUP // 2):
            stacked = jnp.concatenate(
                [masked(query[:MAIN], 2 * pair), masked(query[:MAIN], 2 * pair + 1)], 0
            )
            weight, inverse = weights(stacked, allow_main if shifted else None)
            both = dot(value[2 * pair * HEAD : 2 * (pair + 1) * HEAD], weight) * inverse
            main_rows += [both[:HEAD, :MAIN], both[HEAD:, MAIN:]]
        stacked = jnp.concatenate([masked(query[MAIN:], head) for head in range(GROUP)], 0)
        weight, inverse = weights(stacked, allow_rest if shifted else None)
        rest = dot(value, weight) * inverse
        rest_rows.append(jnp.where(diagonal, rest, 0.0))
    attended = jnp.concatenate(
        [jnp.concatenate(main_rows, 0).T, jnp.concatenate(rest_rows, 0).T], 0
    ).astype(jnp.bfloat16)
    projected = dot(attended, w_ref[:, 3 * features :])
    rest = projected[MAIN : MAIN + REST]
    for head in range(1, GROUP):
        rest = rest + projected[MAIN + head * REST : MAIN + (head + 1) * REST]
    projected = jnp.concatenate([projected[:MAIN], rest], 0)
    middle = tokens.astype(jnp.float32) + layer_norm(projected, gain_ref[...])
    out_ref[0] = middle.astype(jnp.bfloat16)


def allowed_pairs():
    token = np.arange(CELLS)
    side = token // LEVELS % WLAT >= WLAT // 2
    rest = np.tile(side[MAIN:], GROUP)
    return (side[:, None] == np.concatenate([side[:MAIN], rest])[None, :]).astype(np.float32)


def attend(windows, pieces, gain, sharp, shifted, row_windows):
    count, cells, features = windows.shape
    whole = lambda shape: pl.BlockSpec(shape, lambda i: (0,) * len(shape))
    block = pl.BlockSpec((1, cells, features), lambda i: (i, 0, 0))
    extra = (jnp.asarray(allowed_pairs()),) if shifted else ()
    return pl.pallas_call(
        functools.partial(attend_kernel, shifted, row_windows, len(pieces)),
        grid=(count,),
        out_shape=jax.ShapeDtypeStruct(windows.shape, jnp.bfloat16),
        in_specs=[block]
        + [ANY] * len(pieces)
        + [whole((1, features))] * 2
        + [whole(e.shape) for e in extra],
        out_specs=block,
        scratch_shapes=[
            pltpu.VMEM((features, 4 * features), jnp.bfloat16),
            pltpu.VMEM((features, features), jnp.bfloat16),
            pltpu.SemaphoreType.DMA,
        ],
        compiler_params=pltpu.CompilerParams(vmem_limit_bytes=40 * 2**20),
        cost_estimate=pl.CostEstimate(
            flops=count * 11_000_000_00, bytes_accessed=6_000_000, transcendentals=0
        ),
    )(windows, *pieces, gain, sharp, *extra)


def feed_kernel(count, hidden_size, chunk, *refs):
    x_ref, pieces = refs[0], refs[1 : 1 + count]
    gain_ref, out_ref, w_ref, sem = refs[1 + count :]

    @pl.when(pl.program_id(0) == 0)
    def _():
        load_pieces(pieces, w_ref, sem)

    tokens = x_ref[...]
    total = jnp.zeros(tokens.shape, jnp.float32)
    for start in range(0, hidden_size, chunk):
        grown = dot(tokens, w_ref[:, start : start + chunk])
        hidden = jax.nn.gelu(grown).astype(jnp.bfloat16)
        total = total + dot(
            hidden, w_ref[:, hidden_size + start : hidden_size + start + chunk], NT
        )
    result = tokens.astype(jnp.float32) + layer_norm(total, gain_ref[...])
    out_ref[...] = result.astype(jnp.bfloat16)


def feed(rows, pieces, gain, hidden_size):
    count, features = rows.shape
    tile = 2 * CELLS
    block = pl.BlockSpec((tile, features), lambda i: (i, 0))
    return pl.pallas_call(
        functools.partial(feed_kernel, len(pieces), hidden_size, 512),
        grid=(count // tile,),
        out_shape=jax.ShapeDtypeStruct(rows.shape, jnp.bfloat16),
        in_specs=[block]
        + [ANY] * len(pieces)
        + [pl.BlockSpec((1, features), lambda i: (0, 0))],
        out_specs=block,
        scratch_shapes=[
            pltpu.VMEM((features, 2 * hidden_size), jnp.bfloat16),
            pltpu.SemaphoreType.DMA,
        ],
        compiler_params=pltpu.CompilerParams(vmem_limit_bytes=40 * 2**20),
        cost_estimate=pl.CostEstimate(
            flops=4 * count * features * hidden_size, bytes_accessed=8_000_000, transcendentals=0
        ),
    )(rows, *pieces, gain)


def to_windows(cells):
    cols, rows, levels, features = cells.shape
    arranged = cells.reshape(cols // WLON, WLON, rows // WLAT, WLAT, levels, features)
    return arranged.transpose(0, 2, 1, 3, 4, 5).reshape(-1, CELLS, features)


def from_windows(windows, cols, rows):
    features = windows.shape[-1]
    arranged = windows.reshape(cols // WLON, rows // WLAT, WLON, WLAT, LEVELS, features)
    return arranged.transpose(0, 2, 1, 3, 4, 5).reshape(cols, rows, LEVELS, features)


def shift_from(block, lon_step, lat_step):
    lons, lats = lax.axis_size("lon"), lax.axis_size("lat")
    pairs = []
    for lon in range(lons):
        for lat in range(lats):
            source = (lon + lon_step) % lons * lats + (lat + lat_step) % lats
            pairs.append((source, lon * lats + lat))
    return lax.ppermute(block, ("lon", "lat"), pairs)


def roll_on(cells):
    c, r = WLON // 2, WLAT // 2
    ahead = shift_from(cells[:c, r:], 1, 0)
    above = shift_from(cells[c:, :r], 0, 1)
    corner = shift_from(cells[:c, :r], 1, 1)
    return jnp.concatenate(
        [
            jnp.concatenate([cells[c:, r:], ahead], 0),
            jnp.concatenate([above, corner], 0),
        ],
        1,
    )


def roll_back(cells):
    c, r = WLON // 2, WLAT // 2
    behind = shift_from(cells[-c:, :-r], -1, 0)
    below = shift_from(cells[:-c, -r:], 0, -1)
    corner = shift_from(cells[-c:, -r:], -1, -1)
    return jnp.concatenate(
        [
            jnp.concatenate([corner, below], 0),
            jnp.concatenate([behind, cells[:-c, :-r]], 0),
        ],
        1,
    )


def per_device(tokens, qkv_weight, out_weight, up_weight, down_weight, norm_gain, logit_scale):
    cols, rows, _, features = tokens.shape
    hidden_size = up_weight.shape[-1]
    lon_size = lax.axis_size("lon")
    if relayed(qkv_weight.shape[1], lax.axis_size("lat")):
        chunks = cut_chunks(qkv_weight, out_weight, up_weight, down_weight)
        gathered = [relay(chunk, lon_size) for chunk in chunks]
    else:
        gathered = []
        for block in range(2):
            for pair in ((qkv_weight, out_weight), (up_weight, down_weight)):
                joined = jnp.concatenate([weight[block] for weight in pair], 1)
                gathered.append([lax.all_gather(joined, "lon", axis=0, tiled=True)[None]])
    sharp = jnp.repeat(logit_scale * math.log2(math.e), HEAD, axis=1)

    def block_pass(cells, block, shifted):
        windows = to_windows(cells)
        middle = attend(
            windows,
            gathered[2 * block],
            norm_gain[block, :1],
            sharp[block : block + 1],
            shifted,
            rows // WLAT,
        )
        result = feed(
            middle.reshape(-1, features), gathered[2 * block + 1], norm_gain[block, 1:], hidden_size
        )
        return from_windows(result.reshape(windows.shape), cols, rows)

    rolled = roll_on(block_pass(tokens, 0, False))
    return roll_back(block_pass(rolled, 1, True))


def solution(mesh):
    placed = (
        P("lon", "lat", None, None),
        P(None, "lon", None),
        P(None, "lon", None),
        P(None, "lon", None),
        P(None, "lon", None),
        P(),
        P(),
    )
    return jax.shard_map(
        per_device,
        mesh=mesh,
        in_specs=placed,
        out_specs=P("lon", "lat", None, None),
        check_vma=False,
    )
```

time: 422 us -> 216 us (0.51)
  waiting for transfers between devices: 145 us -> 43.2 us
  matrix products: 93.1 us -> 0 us
  blocking collectives: 90.1 us -> 0 us
  Pallas kernels: 0 us -> 88.6 us
  starting transfers between devices: 4.59 us -> 39 us
  other arithmetic: 21.8 us -> 7.78 us
  between operations: 14.2 us -> 0.35 us
  local copies, waits for them, and re-layouts: 50.4 us -> 36.8 us
    all_gather x6 -> x0, waiting for transfers between devices: 126 us -> none  [the longest x2 92.4 us: down_apply(): lax.all_gather(down_weight[block_index], 'lon', axis=0, tiled=True)]
    dot_general x10 -> x0, matrix products: 93.1 us -> none  [the longest x2 45.8 us: attend(): jnp.einsum('wqhd,wkhd->whqk', query_unit, key_unit, precision=lax.Precisi...]
    all_gather x2 -> x0, blocking collectives: 90.1 us -> none  [out_apply(): lax.all_gather(out_weight[block_index], 'lon', axis=0, tiled=True)]
    pallas_call x0 -> x5, Pallas kernels: none -> 88.6 us  [the longest x2 48.6 us: attend(): pl.pallas_call(functools.partial(attend_kernel, shifted, row_windows, len...]
    ppermute x4 -> x34, starting transfers between devices: 4.39 us -> 39 us  [the longest x28 33.9 us: send(): return lax.ppermute(block, ('lon', 'lat'), pairs)]
    ppermute x4 -> x34, waiting for transfers between devices: 16.7 us -> 43.2 us  [the longest x28 31.6 us: send(): return lax.ppermute(block, ('lon', 'lat'), pairs)]
    reshape x5 -> x3, local copies, waits for them, and re-layouts: 23.7 us -> 7.88 us  [the longest x2 5.95 us: to_windows(): return arranged.transpose(0, 2, 1, 3, 4, 5).reshape(-1, CELLS, features)]
    convert_element_type x4 -> x0, local copies, waits for them, and re-layouts: 11.7 us -> none  [the longest x2 8.89 us: block_pass(): triples = qkv_apply(token_rows).astype(jnp.bfloat16)]
  transfers between devices with their start and end apart: 10 -> 34, of which waited for: 6 -> 8; matrix products, arithmetic and copies ran while one was open for 35% -> 16% of each run, Pallas kernels for 0% -> 29%
where the time goes in v1:
time: 216 us
  Pallas kernels  88.6 us (41%)
  waiting for transfers between devices  43.2 us (20%)
  starting transfers between devices  39 us (18%)
  local copies, waits for them, and re-layouts  36.8 us (17%)
  other arithmetic  7.78 us (4%)
    pallas_call x2, Pallas kernels, attend(): pl.pallas_call(functools.partial(attend_kernel, shifted, row_windows, len...  48.6 us
    ppermute x28, starting transfers between devices, send(): return lax.ppermute(block, ('lon', 'lat'), pairs)  33.9 us
    ppermute x28, waiting for transfers between devices, send(): return lax.ppermute(block, ('lon', 'lat'), pairs)  31.6 us
    pallas_call x2, Pallas kernels, feed(): pl.pallas_call(functools.partial(feed_kernel, len(pieces), hidden_size, 5...  26.9 us
    pallas_call x1, Pallas kernels, cut_chunks(): pl.pallas_call(functools.partial(cut_kernel, rows // 2), out_shape=[jax.S...  13.1 us
    unnamed x34, local copies, waits for them, and re-layouts  12.7 us
    ppermute x6, waiting for transfers between devices, shift_from(): return lax.ppermute(block, ('lon', 'lat'), pairs)  11.6 us
    reshape x2, local copies, waits for them, and re-layouts, to_windows(): return arranged.transpose(0, 2, 1, 3, 4, 5).reshape(-1, CELLS, features)  5.95 us
  transfers between devices with their start and end apart: 34, of which 8 were waited for; matrix products, arithmetic and copies ran while one was open for 16% of the time, Pallas kernels for 29%

profile of v1, /device:TPU:0, one launch (start us, length us, event | category | flops | bytes accessed | tf_op | source)
XLA Modules:
  0.0 215.7 jit_solution(11348424298957662659)
XLA Ops:
  0.0 13.1 %shard_map.82 = (bf16[1,16,2048]{2,1,0:T(8,128)(2,1)}, bf16[1,16,4096]{2,1,0:T(8,128)(2,1)}, bf16[1,16,2048]{2,1,0:T(8,128)(2,1)}, bf16[1,16,4096]{2,1,0:T(8,128)(2,1)}) custom-call(bf16[2,32,1536]{2,1,0:T(8,128)(2,1)} %qkv_ref.1, bf16[2,32,512]{2,1,0:T(8,128)(2,1)} %out_ref.1, bf16[2,32,2048]{2,1,0:T(8,128)(2,1)} %up_ref.1, bf16[2,32,2048]{2,1,0:T(8,128)(2,1)} %down_ref.1), custom_call_target="tpu_custom_call" | custom-call | tf_op jit(solution)/shard_map/pallas_call | solution.py:71
  13.1 3.1 %collective-permute-start = (bf16[1,16,2048]{2,1,0:T(8,128)(2,1)}, bf16[1,16,2048]{2,1,0:T(8,128)(2,1)S(1)}, u32[]{:S(2)}, u32[]{:S(2)}) collective-permute-start(bf16[1,16,2048]{2,1,0:T(8,128)(2,1)} %get-tuple-element.9), channel_id=1, source_target_pairs={{0,8},{1,9},{2,10},{3,11},{4,12},{5,13},{6,14},{7,15},{8,16},{9,17... | collective-permute-start | bytes 196616 | tf_op jit(solution)/shard_map/ppermute | solution.py:88
  16.2 2.6 %collective-permute-start.1 = (bf16[1,16,2048]{2,1,0:T(8,128)(2,1)}, bf16[1,16,2048]{2,1,0:T(8,128)(2,1)}, u32[]{:S(2)}, u32[]{:S(2)}) collective-permute-start(bf16[1,16,2048]{2,1,0:T(8,128)(2,1)} %get-tuple-element.9), channel_id=1, source_target_pairs={{0,16},{1,17},{2,18},{3,19},{4,20},{5,21},{6,22},{7,23},{8,24},{9,... | collective-permute-start | bytes 196616 | tf_op jit(solution)/shard_map/ppermute | solution.py:88
  18.8 1.3 collective-permute-start.2
  20.1 0.7 collective-permute-start.7
  21.1 1.5 constant_dynamic-update-slice_fusion.4
  22.7 0.8 slice_bitcast_fusion
  23.4 0.7 broadcast_multiply_fusion
  24.1 1.0 constant_dynamic-update-slice_fusion.9
  25.3 1.9 copy.16
  27.2 3.0 %reshape.36.refs_0_ = bf16[8,144,512]{2,1,0:T(8,128)(2,1)S(1)} reshape(bf16[2,4,12,6,2,512]{5,4,3,2,1,0:T(2,128)(2,1)} %bitcast.34) | data formatting | bytes 2359296 | tf_op jit(solution)/shard_map/reshape | solution.py:294
  30.2 2.9 %collective-permute-start.9 = (bf16[1,16,4096]{2,1,0:T(8,128)(2,1)}, bf16[1,16,4096]{2,1,0:T(8,128)(2,1)S(1)}, u32[]{:S(2)}, u32[]{:S(2)}) collective-permute-start(bf16[1,16,4096]{2,1,0:T(8,128)(2,1)} %get-tuple-element.10), channel_id=1, source_target_pairs={{0,24},{1,25},{2,26},{3,27},{4,28},{5,29},{6,30},{7,31},{8,0},{9,1... | collective-permute-start | bytes 393224 | tf_op jit(solution)/shard_map/ppermute | solution.py:88
  33.1 0.6 constant_dynamic-update-slice_fusion.3
  34.3 1.5 constant_dynamic-update-slice_fusion.2
  35.8 1.5 collective-permute-start.18
  37.2 0.9 pad_maximum_fusion.2
  38.2 1.5 constant_dynamic-update-slice_fusion.1
  39.6 0.7 collective-permute-done.17
  40.3 2.3 %collective-permute-start.19 = (bf16[1,16,2048]{2,1,0:T(8,128)(2,1)}, bf16[1,16,2048]{2,1,0:T(8,128)(2,1)S(1)}, u32[]{:S(2)}, u32[]{:S(2)}) collective-permute-start(bf16[1,16,2048]{2,1,0:T(8,128)(2,1)} %get-tuple-element.11), channel_id=1, source_target_pairs={{0,24},{1,25},{2,26},{3,27},{4,28},{5,29},{6,30},{7,31},{8,0},{9,1... | collective-permute-start | bytes 196616 | tf_op jit(solution)/shard_map/ppermute | solution.py:88
  42.6 0.6 constant_dynamic-update-slice_fusion.13
  43.3 0.6 constant_dynamic-update-slice_fusion.12
  43.9 1.4 collective-permute-done.19
  45.3 3.6 %collective-permute-start.25 = (bf16[1,16,4096]{2,1,0:T(8,128)(2,1)S(1)}, bf16[1,16,4096]{2,1,0:T(8,128)(2,1)S(1)}, u32[]{:S(2)}, u32[]{:S(2)}) collective-permute-start(bf16[1,16,4096]{2,1,0:T(8,128)(2,1)S(1)} %copy-done.7), channel_id=1, source_target_pairs={{0,16},{1,17},{2,18},{3,19},{4,20},{5,21},{6,22},{7,23},{8,24},{9,... | collective-permute-start | bytes 393224 | tf_op jit(solution)/shard_map/ppermute | solution.py:88
  48.9 0.6 constant_dynamic-update-slice_fusion.11
  49.6 3.8 %collective-permute-start.26 = (bf16[1,16,4096]{2,1,0:T(8,128)(2,1)S(1)}, bf16[1,16,4096]{2,1,0:T(8,128)(2,1)S(1)}, u32[]{:S(2)}, u32[]{:S(2)}) collective-permute-start(bf16[1,16,4096]{2,1,0:T(8,128)(2,1)S(1)} %copy-done.7), channel_id=1, source_target_pairs={{0,24},{1,25},{2,26},{3,27},{4,28},{5,29},{6,30},{7,31},{8,0},{9,1... | collective-permute-start | bytes 393224 | tf_op jit(solution)/shard_map/ppermute | solution.py:88
  53.3 1.5 collective-permute-start.3
  55.4 1.0 pad_maximum_fusion
  56.4 1.6 collective-permute-start.10
  58.6 0.9 constant_dynamic-update-slice_fusion.7
  59.6 2.8 %collective-permute-done.3 = bf16[4,16,2048]{2,1,0:T(8,128)(2,1)S(1)} collective-permute-done((bf16[4,16,2048]{2,1,0:T(8,128)(2,1)S(1)}, bf16[4,16,2048]{2,1,0:T(8,128)(2,1)S(1)}, u32[]{:S(2)}, u32[]{:S(2)}) %collective-permute-start.3) | collective-permute-done | bytes 262176 | tf_op jit(solution)/shard_map/ppermute | solution.py:88
  62.4 1.7 collective-permute-start.4
  64.1 15.2 %collective-permute-done.10 = bf16[4,16,4096]{2,1,0:T(8,128)(2,1)S(1)} collective-permute-done((bf16[4,16,4096]{2,1,0:T(8,128)(2,1)S(1)}, bf16[4,16,4096]{2,1,0:T(8,128)(2,1)S(1)}, u32[]{:S(2)}, u32[]{:S(2)}) %collective-permute-start.10) | collective-permute-done | bytes 524320 | tf_op jit(solution)/shard_map/ppermute | solution.py:88
  79.3 1.7 collective-permute-start.11
  81.6 0.7 constant_dynamic-update-slice_fusion.10.refs_1_
  82.7 7.8 %collective-permute-done.27 = bf16[4,16,4096]{2,1,0:T(8,128)(2,1)S(1)} collective-permute-done((bf16[4,16,4096]{2,1,0:T(8,128)(2,1)S(1)}, bf16[4,16,4096]{2,1,0:T(8,128)(2,1)S(1)}, u32[]{:S(2)}, u32[]{:S(2)}) %collective-permute-start.27) | collective-permute-done | bytes 524320 | tf_op jit(solution)/shard_map/ppermute | solution.py:88
  90.5 3.7 %collective-permute-done.11.refs_2_ = bf16[8,16,4096]{2,1,0:T(8,128)(2,1)S(1)} collective-permute-done((bf16[8,16,4096]{2,1,0:T(8,128)(2,1)S(1)}, bf16[8,16,4096]{2,1,0:T(8,128)(2,1)S(1)}, u32[]{:S(2)}, u32[]{:S(2)}) %collective-permute-start.11) | collective-permute-done | bytes 1048608 | tf_op jit(solution)/shard_map/ppermute | solution.py:88
  94.2 1.7 collective-permute-start.28
  95.9 25.0 %shard_map.83 = bf16[8,144,512]{2,1,0:T(8,128)(2,1)S(1)} custom-call(bf16[8,144,512]{2,1,0:T(8,128)(2,1)S(1)} %reshape.36.refs_0_, bf16[8,16,2048]{2,1,0:T(8,128)(2,1)S(1)} %constant_dynamic-update-slice_fusion.refs_1_, bf16[8,16,2048]{2,1,0:T(8,128)(2,1)S(1)} %collective-permute-done.4.refs_2_, bf16[8,16,2048]{2,1,0:T(8,128)(2,1)S(1)} %collective-permute-done.5.refs_3_, ...), custom_call_target="tpu_custom_call" | custom-call | flops 8800000000 | bytes 6000000 | tf_op jit(solution)/shard_map/pallas_call | solution.py:227
  121.0 14.8 %shard_map.84 = bf16[1152,512]{1,0:T(8,128)(2,1)S(1)} custom-call(bf16[1152,512]{1,0:T(8,128)(2,1)S(1)} %bitcast.27, bf16[8,16,4096]{2,1,0:T(8,128)(2,1)S(1)} %constant_dynamic-update-slice_fusion.5.refs_1_, bf16[8,16,4096]{2,1,0:T(8,128)(2,1)S(1)} %collective-permute-done.11.refs_2_, bf16[8,16,4096]{2,1,0:T(8,128)(2,1)S(1)} %collective-permute-done.12.refs_3_, ...), custom_call_target="tpu_custom_call" | custom-call | flops 4831838208 | bytes 8000000 | tf_op jit(solution)/shard_map/pallas_call | solution.py:272
  135.8 1.3 reshape_reshape.6
  137.1 2.5 %copy.12 = bf16[2,4,12,6,2,512]{5,4,3,1,2,0:T(2,128)(2,1)S(1)} copy(bf16[2,4,12,6,2,512]{5,4,3,2,1,0:T(2,128)(2,1)} %reshape_reshape.6) | data formatting | bytes 2359296 | tf_op jit(solution)/shard_map/reshape;reshape | solution.py:299
  139.6 0.9 slice.67
  140.5 0.7 slice.68
  142.0 0.6 slice.69
  142.6 1.1 collective-permute-start.16
  143.7 0.7 broadcast_in_dim.11
  144.4 0.8 broadcast_in_dim.12.refs_6_
  145.7 3.3 %collective-permute-done.16 = bf16[6,3,2,512]{3,2,1,0:T(2,128)(2,1)} collective-permute-done((bf16[6,3,2,512]{3,2,1,0:T(2,128)(2,1)}, bf16[6,3,2,512]{3,2,1,0:T(2,128)(2,1)}, u32[]{:S(2)}, u32[]{:S(2)}) %collective-permute-start.16) | collective-permute-done | bytes 36896 | tf_op jit(solution)/shard_map/ppermute | solution.py:310
  148.9 0.7 collective-permute-start.29
  149.6 2.6 %maximum_maximum_fusion = bf16[24,24,2,512]{3,2,1,0:T(2,128)(2,1)S(1)} fusion(bf16[6,3,2,512]{3,2,1,0:T(2,128)(2,1)} %collective-permute-done.16, bf16[18,3,2,512]{3,2,1,0:T(2,128)(2,1)} %collective-permute-done.15, bf16[6,21,2,512]{3,2,1,0:T(2,128)(2,1)S(1)} %collective-permute-done.14, bf16[18,21,2,512]{3,2,1,0:T(2,128)(2,1)S(1)} %slice.66), kind=kLoop, calls=%fused_computation | loop fusion | flops 1769472 | bytes 2359296 | tf_op jit(solution)/shard_map/concatenate | solution.py:318
  152.2 1.9 copy.13
  154.1 3.0 %reshape.40.refs_0_ = bf16[8,144,512]{2,1,0:T(8,128)(2,1)S(1)} reshape(bf16[2,4,12,6,2,512]{5,4,3,2,1,0:T(2,128)(2,1)} %copy.13) | data formatting | bytes 2359296 | tf_op jit(solution)/shard_map/reshape | solution.py:294
  157.1 0.8 copy-done.1
  157.9 0.8 copy-done.3
  158.7 1.0 copy-done.2
  159.8 1.0 copy-done.4
  160.8 23.6 %shard_map.85 = bf16[8,144,512]{2,1,0:T(8,128)(2,1)S(1)} custom-call(bf16[8,144,512]{2,1,0:T(8,128)(2,1)S(1)} %reshape.40.refs_0_, bf16[8,16,2048]{2,1,0:T(8,128)(2,1)} %constant_dynamic-update-slice_fusion.10.refs_1_, bf16[8,16,2048]{2,1,0:T(8,128)(2,1)} %collective-permute-done.21.refs_2_, bf16[8,16,2048]{2,1,0:T(8,128)(2,1)S(1)} %copy-done.2, ...), custom_call_target="tpu_custom_call" | custom-call | flops 8800000000 | bytes 6000000 | tf_op jit(solution)/shard_map/pallas_call | solution.py:227
  184.4 12.1 %shard_map.86 = bf16[1152,512]{1,0:T(8,128)(2,1)S(1)} custom-call(bf16[1152,512]{1,0:T(8,128)(2,1)S(1)} %bitcast.26, bf16[8,16,4096]{2,1,0:T(8,128)(2,1)S(1)} %constant_dynamic-update-slice_fusion.15.refs_1_, bf16[8,16,4096]{2,1,0:T(8,128)(2,1)} %collective-permute-done.28.refs_2_, bf16[8,16,4096]{2,1,0:T(8,128)(2,1)} %collective-permute-done.29.refs_3_, ...), custom_call_target="tpu_custom_call" | custom-call | flops 4831838208 | bytes 8000000 | tf_op jit(solution)/shard_map/pallas_call | solution.py:272
  196.6 1.3 reshape_reshape.7
  197.9 2.5 %copy.14 = bf16[2,12,4,6,2,512]{5,4,3,2,1,0:T(2,128)(2,1)S(1)} copy(bf16[2,12,4,6,2,512]{5,4,3,1,2,0:T(2,128)(2,1)} %bitcast.33) | data formatting | bytes 2359296 | tf_op jit(solution)/shard_map/transpose | solution.py:300
  200.5 1.5 collective-permute-start.33
  202.4 1.9 collective-permute-start.31
  204.9 8.3 %collective-permute-done.31 = bf16[6,3,2,512]{3,2,1,0:T(2,128)(2,1)S(1)} collective-permute-done((bf16[6,3,2,512]{3,2,1,0:T(2,128)(2,1)S(1)}, bf16[6,3,2,512]{3,2,1,0:T(2,128)(2,1)S(1)}, u32[]{:S(2)}, u32[]{:S(2)}) %collective-permute-start.31) | collective-permute-done | bytes 36896 | tf_op jit(solution)/shard_map/ppermute | solution.py:310
  213.2 2.5 %maximum_maximum_fusion.1 = bf16[24,24,2,512]{3,2,1,0:T(2,128)(2,1)} fusion(bf16[18,21,2,512]{3,2,1,0:T(2,128)(2,1)S(1)} %slice.73, bf16[6,21,2,512]{3,2,1,0:T(2,128)(2,1)S(1)} %collective-permute-done.33, bf16[18,3,2,512]{3,2,1,0:T(2,128)(2,1)S(1)} %collective-permute-done.32, bf16[6,3,2,512]{3,2,1,0:T(2,128)(2,1)S(1)} %collective-permute-done.31), kind=kLoop, calls=%fused_computation.1 | loop fusion | flops 1769472 | bytes 2359296 | tf_op jit(solution)/shard_map/concatenate | solution.py:332
  (76 shorter events, 6.0 us)
Async XLA Ops:
  0.0 25.3 %copy-start.6 = (bf16[24,24,2,512]{3,2,1,0:T(2,128)(2,1)S(1)}, bf16[24,24,2,512]{3,2,1,0:T(2,128)(2,1)}, u32[]{:S(2)}) copy-start(bf16[24,24,2,512]{3,2,1,0:T(2,128)(2,1)} %param.8) | copy-start | bytes 3538948
  13.1 17.1 %collective-permute-start = (bf16[1,16,2048]{2,1,0:T(8,128)(2,1)}, bf16[1,16,2048]{2,1,0:T(8,128)(2,1)S(1)}, u32[]{:S(2)}, u32[]{:S(2)}) collective-permute-start(bf16[1,16,2048]{2,1,0:T(8,128)(2,1)} %get-tuple-element.9), channel_id=1, source_target_pairs={{0,8},{1,9},{2,10},{3,11},{4,12},{5,13},{6,14},{7,15},{8,16},{9,17... | collective-permute-start | bytes 196616 | tf_op jit(solution)/shard_map/ppermute | solution.py:88
  16.2 17.5 %collective-permute-start.1 = (bf16[1,16,2048]{2,1,0:T(8,128)(2,1)}, bf16[1,16,2048]{2,1,0:T(8,128)(2,1)}, u32[]{:S(2)}, u32[]{:S(2)}) collective-permute-start(bf16[1,16,2048]{2,1,0:T(8,128)(2,1)} %get-tuple-element.9), channel_id=1, source_target_pairs={{0,16},{1,17},{2,18},{3,19},{4,20},{5,21},{6,22},{7,23},{8,24},{9,... | collective-permute-start | bytes 196616 | tf_op jit(solution)/shard_map/ppermute | solution.py:88
  18.8 17.0 %collective-permute-start.2 = (bf16[1,16,2048]{2,1,0:T(8,128)(2,1)}, bf16[1,16,2048]{2,1,0:T(8,128)(2,1)}, u32[]{:S(2)}, u32[]{:S(2)}) collective-permute-start(bf16[1,16,2048]{2,1,0:T(8,128)(2,1)} %get-tuple-element.9), channel_id=1, source_target_pairs={{0,24},{1,25},{2,26},{3,27},{4,28},{5,29},{6,30},{7,31},{8,0},{9,1... | collective-permute-start | bytes 196616 | tf_op jit(solution)/shard_map/ppermute | solution.py:88
  20.1 29.5 %collective-permute-start.7 = (bf16[1,16,4096]{2,1,0:T(8,128)(2,1)}, bf16[1,16,4096]{2,1,0:T(8,128)(2,1)S(1)}, u32[]{:S(2)}, u32[]{:S(2)}) collective-permute-start(bf16[1,16,4096]{2,1,0:T(8,128)(2,1)} %get-tuple-element.10), channel_id=1, source_target_pairs={{0,8},{1,9},{2,10},{3,11},{4,12},{5,13},{6,14},{7,15},{8,16},{9,17... | collective-permute-start | bytes 393224 | tf_op jit(solution)/shard_map/ppermute | solution.py:88
  20.8 32.6 %collective-permute-start.8 = (bf16[1,16,4096]{2,1,0:T(8,128)(2,1)}, bf16[1,16,4096]{2,1,0:T(8,128)(2,1)}, u32[]{:S(2)}, u32[]{:S(2)}) collective-permute-start(bf16[1,16,4096]{2,1,0:T(8,128)(2,1)} %get-tuple-element.10), channel_id=1, source_target_pairs={{0,16},{1,17},{2,18},{3,19},{4,20},{5,21},{6,22},{7,23},{8,24},{9,... | collective-permute-start | bytes 393224 | tf_op jit(solution)/shard_map/ppermute | solution.py:88
  30.2 15.1 %copy-start.7 = (bf16[1,16,4096]{2,1,0:T(8,128)(2,1)S(1)}, bf16[1,16,4096]{2,1,0:T(8,128)(2,1)}, u32[]{:S(2)}) copy-start(bf16[1,16,4096]{2,1,0:T(8,128)(2,1)} %get-tuple-element.12) | copy-start | bytes 393220
  30.2 18.7 %copy-start.9 = (bf16[1,16,2048]{2,1,0:T(8,128)(2,1)S(1)}, bf16[1,16,2048]{2,1,0:T(8,128)(2,1)}, u32[]{:S(2)}) copy-start(bf16[1,16,2048]{2,1,0:T(8,128)(2,1)} %get-tuple-element.11) | copy-start | bytes 196612
  30.2 25.2 %copy-start.8 = (bf16[1,16,4096]{2,1,0:T(8,128)(2,1)S(1)}, bf16[1,16,4096]{2,1,0:T(8,128)(2,1)}, u32[]{:S(2)}) copy-start(bf16[1,16,4096]{2,1,0:T(8,128)(2,1)} %get-tuple-element.10) | copy-start | bytes 393220
  30.2 24.6 %collective-permute-start.9 = (bf16[1,16,4096]{2,1,0:T(8,128)(2,1)}, bf16[1,16,4096]{2,1,0:T(8,128)(2,1)S(1)}, u32[]{:S(2)}, u32[]{:S(2)}) collective-permute-start(bf16[1,16,4096]{2,1,0:T(8,128)(2,1)} %get-tuple-element.10), channel_id=1, source_target_pairs={{0,24},{1,25},{2,26},{3,27},{4,28},{5,29},{6,30},{7,31},{8,0},{9,1... | collective-permute-start | bytes 393224 | tf_op jit(solution)/shard_map/ppermute | solution.py:88
  33.7 6.6 %collective-permute-start.17 = (bf16[1,16,2048]{2,1,0:T(8,128)(2,1)}, bf16[1,16,2048]{2,1,0:T(8,128)(2,1)S(1)}, u32[]{:S(2)}, u32[]{:S(2)}) collective-permute-start(bf16[1,16,2048]{2,1,0:T(8,128)(2,1)} %get-tuple-element.11), channel_id=1, source_target_pairs={{0,8},{1,9},{2,10},{3,11},{4,12},{5,13},{6,14},{7,15},{8,16},{9,17... | collective-permute-start | bytes 196616 | tf_op jit(solution)/shard_map/ppermute | solution.py:88
  35.8 7.4 %collective-permute-start.18 = (bf16[1,16,2048]{2,1,0:T(8,128)(2,1)}, bf16[1,16,2048]{2,1,0:T(8,128)(2,1)S(1)}, u32[]{:S(2)}, u32[]{:S(2)}) collective-permute-start(bf16[1,16,2048]{2,1,0:T(8,128)(2,1)} %get-tuple-element.11), channel_id=1, source_target_pairs={{0,16},{1,17},{2,18},{3,19},{4,20},{5,21},{6,22},{7,23},{8,24},{9,... | collective-permute-start | bytes 196616 | tf_op jit(solution)/shard_map/ppermute | solution.py:88
  40.3 5.0 %collective-permute-start.19 = (bf16[1,16,2048]{2,1,0:T(8,128)(2,1)}, bf16[1,16,2048]{2,1,0:T(8,128)(2,1)S(1)}, u32[]{:S(2)}, u32[]{:S(2)}) collective-permute-start(bf16[1,16,2048]{2,1,0:T(8,128)(2,1)} %get-tuple-element.11), channel_id=1, source_target_pairs={{0,24},{1,25},{2,26},{3,27},{4,28},{5,29},{6,30},{7,31},{8,0},{9,1... | collective-permute-start | bytes 196616 | tf_op jit(solution)/shard_map/ppermute | solution.py:88
  43.2 13.2 %collective-permute-start.24 = (bf16[1,16,4096]{2,1,0:T(8,128)(2,1)}, bf16[1,16,4096]{2,1,0:T(8,128)(2,1)S(1)}, u32[]{:S(2)}, u32[]{:S(2)}) collective-permute-start(bf16[1,16,4096]{2,1,0:T(8,128)(2,1)} %get-tuple-element.12), channel_id=1, source_target_pairs={{0,8},{1,9},{2,10},{3,11},{4,12},{5,13},{6,14},{7,15},{8,16},{9,17... | collective-permute-start | bytes 393224 | tf_op jit(solution)/shard_map/ppermute | solution.py:88
  45.3 12.6 %collective-permute-start.25 = (bf16[1,16,4096]{2,1,0:T(8,128)(2,1)S(1)}, bf16[1,16,4096]{2,1,0:T(8,128)(2,1)S(1)}, u32[]{:S(2)}, u32[]{:S(2)}) collective-permute-start(bf16[1,16,4096]{2,1,0:T(8,128)(2,1)S(1)} %copy-done.7), channel_id=1, source_target_pairs={{0,16},{1,17},{2,18},{3,19},{4,20},{5,21},{6,22},{7,23},{8,24},{9,... | collective-permute-start | bytes 393224 | tf_op jit(solution)/shard_map/ppermute | solution.py:88
  49.6 8.4 %collective-permute-start.26 = (bf16[1,16,4096]{2,1,0:T(8,128)(2,1)S(1)}, bf16[1,16,4096]{2,1,0:T(8,128)(2,1)S(1)}, u32[]{:S(2)}, u32[]{:S(2)}) collective-permute-start(bf16[1,16,4096]{2,1,0:T(8,128)(2,1)S(1)} %copy-done.7), channel_id=1, source_target_pairs={{0,24},{1,25},{2,26},{3,27},{4,28},{5,29},{6,30},{7,31},{8,0},{9,1... | collective-permute-start | bytes 393224 | tf_op jit(solution)/shard_map/ppermute | solution.py:88
  53.3 9.1 %collective-permute-start.3 = (bf16[4,16,2048]{2,1,0:T(8,128)(2,1)S(1)}, bf16[4,16,2048]{2,1,0:T(8,128)(2,1)S(1)}, u32[]{:S(2)}, u32[]{:S(2)}) collective-permute-start(bf16[4,16,2048]{2,1,0:T(8,128)(2,1)S(1)} %pad_maximum_fusion.2), channel_id=1, source_target_pairs={{0,2},{1,5},{2,0},{3,7},{4,6},{5,1},{6,4},{7,3},{8,10},{9,13},{10,... | collective-permute-start | bytes 786440 | tf_op jit(solution)/shard_map/ppermute | solution.py:88
  54.8 26.8 %collective-permute-start.20 = (bf16[4,16,2048]{2,1,0:T(8,128)(2,1)S(1)}, bf16[4,16,2048]{2,1,0:T(8,128)(2,1)S(1)}, u32[]{:S(2)}, u32[]{:S(2)}) collective-permute-start(bf16[4,16,2048]{2,1,0:T(8,128)(2,1)S(1)} %pad_maximum_fusion.3), channel_id=1, source_target_pairs={{0,2},{1,5},{2,0},{3,7},{4,6},{5,1},{6,4},{7,3},{8,10},{9,13},{10,... | collective-permute-start | bytes 786440 | tf_op jit(solution)/shard_map/ppermute | solution.py:88
  56.4 6.1 %copy-start = (bf16[8,16,2048]{2,1,0:T(8,128)(2,1)S(1)}, bf16[8,16,2048]{2,1,0:T(8,128)(2,1)}, u32[]{:S(2)}) copy-start(bf16[8,16,2048]{2,1,0:T(8,128)(2,1)} %constant_dynamic-update-slice_fusion.1) | copy-start | bytes 1572868
  56.4 22.9 %collective-permute-start.10 = (bf16[4,16,4096]{2,1,0:T(8,128)(2,1)S(1)}, bf16[4,16,4096]{2,1,0:T(8,128)(2,1)S(1)}, u32[]{:S(2)}, u32[]{:S(2)}) collective-permute-start(bf16[4,16,4096]{2,1,0:T(8,128)(2,1)S(1)} %pad_maximum_fusion), channel_id=1, source_target_pairs={{0,2},{1,5},{2,0},{3,7},{4,6},{5,1},{6,4},{7,3},{8,10},{9,13},{10,... | collective-permute-start | bytes 1572872 | tf_op jit(solution)/shard_map/ppermute | solution.py:88
  58.0 32.5 %collective-permute-start.27 = (bf16[4,16,4096]{2,1,0:T(8,128)(2,1)S(1)}, bf16[4,16,4096]{2,1,0:T(8,128)(2,1)S(1)}, u32[]{:S(2)}, u32[]{:S(2)}) collective-permute-start(bf16[4,16,4096]{2,1,0:T(8,128)(2,1)S(1)} %pad_maximum_fusion.1), channel_id=1, source_target_pairs={{0,2},{1,5},{2,0},{3,7},{4,6},{5,1},{6,4},{7,3},{8,10},{9,13},{10,... | collective-permute-start | bytes 1572872 | tf_op jit(solution)/shard_map/ppermute | solution.py:88
  62.4 18.7 %collective-permute-start.4 = (bf16[8,16,2048]{2,1,0:T(8,128)(2,1)S(1)}, bf16[8,16,2048]{2,1,0:T(8,128)(2,1)S(1)}, u32[]{:S(2)}, u32[]{:S(2)}) collective-permute-start(bf16[8,16,2048]{2,1,0:T(8,128)(2,1)S(1)} %constant_dynamic-update-slice_fusion.refs_1_), channel_id=1, source_target_pairs={{0,4},{1,3},{2,6},{3,1},{4,0},{5,7},{6,2},{7,5},{8,12},{9,11},{10,... | collective-permute-start | bytes 1572872 | tf_op jit(solution)/shard_map/ppermute | solution.py:88
  79.3 14.9 %collective-permute-start.11 = (bf16[8,16,4096]{2,1,0:T(8,128)(2,1)S(1)}, bf16[8,16,4096]{2,1,0:T(8,128)(2,1)S(1)}, u32[]{:S(2)}, u32[]{:S(2)}) collective-permute-start(bf16[8,16,4096]{2,1,0:T(8,128)(2,1)S(1)} %constant_dynamic-update-slice_fusion.5.refs_1_), channel_id=1, source_target_pairs={{0,4},{1,3},{2,6},{3,1},{4,0},{5,7},{6,2},{7,5},{8,12},{9,11},{10,... | collective-permute-start | bytes 3145736 | tf_op jit(solution)/shard_map/ppermute | solution.py:88
  81.0 13.2 %collective-permute-start.5 = (bf16[8,16,2048]{2,1,0:T(8,128)(2,1)S(1)}, bf16[8,16,2048]{2,1,0:T(8,128)(2,1)S(1)}, u32[]{:S(2)}, u32[]{:S(2)}) collective-permute-start(bf16[8,16,2048]{2,1,0:T(8,128)(2,1)S(1)} %constant_dynamic-update-slice_fusion.refs_1_), channel_id=1, source_target_pairs={{0,1},{1,0},{2,3},{3,2},{4,5},{5,4},{6,7},{7,6},{8,9},{9,8},{10,11... | collective-permute-start | bytes 1572872 | tf_op jit(solution)/shard_map/ppermute | solution.py:88
  81.1 14.8 %collective-permute-start.6 = (bf16[8,16,2048]{2,1,0:T(8,128)(2,1)S(1)}, bf16[8,16,2048]{2,1,0:T(8,128)(2,1)S(1)}, u32[]{:S(2)}, u32[]{:S(2)}) collective-permute-start(bf16[8,16,2048]{2,1,0:T(8,128)(2,1)S(1)} %collective-permute-done.4.refs_2_), channel_id=1, source_target_pairs={{0,1},{1,0},{2,3},{3,2},{4,5},{5,4},{6,7},{7,6},{8,9},{9,8},{10,11... | collective-permute-start | bytes 1572872 | tf_op jit(solution)/shard_map/ppermute | solution.py:88
  82.3 59.4 %collective-permute-start.21 = (bf16[8,16,2048]{2,1,0:T(8,128)(2,1)}, bf16[8,16,2048]{2,1,0:T(8,128)(2,1)}, u32[]{:S(2)}, u32[]{:S(2)}) collective-permute-start(bf16[8,16,2048]{2,1,0:T(8,128)(2,1)} %constant_dynamic-update-slice_fusion.10.refs_1_), channel_id=1, source_target_pairs={{0,4},{1,3},{2,6},{3,1},{4,0},{5,7},{6,2},{7,5},{8,12},{9,11},{10,... | collective-permute-start | bytes 1572872 | tf_op jit(solution)/shard_map/ppermute | solution.py:88
  90.5 30.4 %collective-permute-start.12 = (bf16[8,16,4096]{2,1,0:T(8,128)(2,1)S(1)}, bf16[8,16,4096]{2,1,0:T(8,128)(2,1)S(1)}, u32[]{:S(2)}, u32[]{:S(2)}) collective-permute-start(bf16[8,16,4096]{2,1,0:T(8,128)(2,1)S(1)} %constant_dynamic-update-slice_fusion.5.refs_1_), channel_id=1, source_target_pairs={{0,1},{1,0},{2,3},{3,2},{4,5},{5,4},{6,7},{7,6},{8,9},{9,8},{10,11... | collective-permute-start | bytes 3145736 | tf_op jit(solution)/shard_map/ppermute | solution.py:88
  94.2 26.8 %collective-permute-start.13 = (bf16[8,16,4096]{2,1,0:T(8,128)(2,1)S(1)}, bf16[8,16,4096]{2,1,0:T(8,128)(2,1)S(1)}, u32[]{:S(2)}, u32[]{:S(2)}) collective-permute-start(bf16[8,16,4096]{2,1,0:T(8,128)(2,1)S(1)} %collective-permute-done.11.refs_2_), channel_id=1, source_target_pairs={{0,1},{1,0},{2,3},{3,2},{4,5},{5,4},{6,7},{7,6},{8,9},{9,8},{10,11... | collective-permute-start | bytes 3145736 | tf_op jit(solution)/shard_map/ppermute | solution.py:88
  94.2 48.4 %collective-permute-start.28 = (bf16[8,16,4096]{2,1,0:T(8,128)(2,1)S(1)}, bf16[8,16,4096]{2,1,0:T(8,128)(2,1)}, u32[]{:S(2)}, u32[]{:S(2)}) collective-permute-start(bf16[8,16,4096]{2,1,0:T(8,128)(2,1)S(1)} %constant_dynamic-update-slice_fusion.15.refs_1_), channel_id=1, source_target_pairs={{0,4},{1,3},{2,6},{3,1},{4,0},{5,7},{6,2},{7,5},{8,12},{9,11},{10,... | collective-permute-start | bytes 3145736 | tf_op jit(solution)/shard_map/ppermute | solution.py:88
  140.5 9.2 %collective-permute-start.14 = (bf16[6,21,2,512]{3,2,1,0:T(2,128)(2,1)}, bf16[6,21,2,512]{3,2,1,0:T(2,128)(2,1)S(1)}, u32[]{:S(2)}, u32[]{:S(2)}) collective-permute-start(bf16[6,21,2,512]{3,2,1,0:T(2,128)(2,1)} %slice.67), channel_id=1, source_target_pairs={{2,0},{3,1},{4,2},{5,3},{6,4},{7,5},{8,6},{9,7},{10,8},{11,9},{12,... | collective-permute-start | bytes 774152 | tf_op jit(solution)/shard_map/ppermute | solution.py:310
  141.2 8.4 %collective-permute-start.15 = (bf16[18,3,2,512]{3,2,1,0:T(2,128)(2,1)}, bf16[18,3,2,512]{3,2,1,0:T(2,128)(2,1)}, u32[]{:S(2)}, u32[]{:S(2)}) collective-permute-start(bf16[18,3,2,512]{3,2,1,0:T(2,128)(2,1)} %slice.68), channel_id=1, source_target_pairs={{1,0},{0,1},{3,2},{2,3},{5,4},{4,5},{7,6},{6,7},{9,8},{8,9},{11,10... | collective-permute-start | bytes 331784 | tf_op jit(solution)/shard_map/ppermute | solution.py:310
  141.4 15.7 %collective-permute-start.22 = (bf16[8,16,2048]{2,1,0:T(8,128)(2,1)}, bf16[8,16,2048]{2,1,0:T(8,128)(2,1)S(1)}, u32[]{:S(2)}, u32[]{:S(2)}) collective-permute-start(bf16[8,16,2048]{2,1,0:T(8,128)(2,1)} %constant_dynamic-update-slice_fusion.10.refs_1_), channel_id=1, source_target_pairs={{0,1},{1,0},{2,3},{3,2},{4,5},{5,4},{6,7},{7,6},{8,9},{9,8},{10,11... | collective-permute-start | bytes 1572872 | tf_op jit(solution)/shard_map/ppermute | solution.py:88
  141.7 16.2 %collective-permute-start.23 = (bf16[8,16,2048]{2,1,0:T(8,128)(2,1)}, bf16[8,16,2048]{2,1,0:T(8,128)(2,1)S(1)}, u32[]{:S(2)}, u32[]{:S(2)}) collective-permute-start(bf16[8,16,2048]{2,1,0:T(8,128)(2,1)} %collective-permute-done.21.refs_2_), channel_id=1, source_target_pairs={{0,1},{1,0},{2,3},{3,2},{4,5},{5,4},{6,7},{7,6},{8,9},{9,8},{10,11... | collective-permute-start | bytes 1572872 | tf_op jit(solution)/shard_map/ppermute | solution.py:88
  142.6 6.4 %collective-permute-start.16 = (bf16[6,3,2,512]{3,2,1,0:T(2,128)(2,1)}, bf16[6,3,2,512]{3,2,1,0:T(2,128)(2,1)}, u32[]{:S(2)}, u32[]{:S(2)}) collective-permute-start(bf16[6,3,2,512]{3,2,1,0:T(2,128)(2,1)} %slice.69), channel_id=1, source_target_pairs={{3,0},{2,1},{5,2},{4,3},{7,4},{6,5},{9,6},{8,7},{11,8},{10,9},{13,... | collective-permute-start | bytes 110600 | tf_op jit(solution)/shard_map/ppermute | solution.py:310
  148.9 35.5 %collective-permute-start.29 = (bf16[8,16,4096]{2,1,0:T(8,128)(2,1)S(1)}, bf16[8,16,4096]{2,1,0:T(8,128)(2,1)}, u32[]{:S(2)}, u32[]{:S(2)}) collective-permute-start(bf16[8,16,4096]{2,1,0:T(8,128)(2,1)S(1)} %constant_dynamic-update-slice_fusion.15.refs_1_), channel_id=1, source_target_pairs={{0,1},{1,0},{2,3},{3,2},{4,5},{5,4},{6,7},{7,6},{8,9},{9,8},{10,11... | collective-permute-start | bytes 3145736 | tf_op jit(solution)/shard_map/ppermute | solution.py:88
  149.6 34.8 %collective-permute-start.30 = (bf16[8,16,4096]{2,1,0:T(8,128)(2,1)}, bf16[8,16,4096]{2,1,0:T(8,128)(2,1)}, u32[]{:S(2)}, u32[]{:S(2)}) collective-permute-start(bf16[8,16,4096]{2,1,0:T(8,128)(2,1)} %collective-permute-done.28.refs_2_), channel_id=1, source_target_pairs={{0,1},{1,0},{2,3},{3,2},{4,5},{5,4},{6,7},{7,6},{8,9},{9,8},{10,11... | collective-permute-start | bytes 3145736 | tf_op jit(solution)/shard_map/ppermute | solution.py:88
  154.1 4.6 %copy-start.5 = (f32[144,256]{1,0:T(8,128)S(1)}, f32[144,256]{1,0:T(8,128)}, u32[]{:S(2)}) copy-start(f32[144,256]{1,0:T(8,128)} %constant.4.clone.refs_7_) | copy-start | bytes 442372
  157.1 0.8 copy-start.1
  157.9 0.8 copy-start.3
  158.7 1.0 copy-start.2
  159.8 1.0 copy-start.4
  200.5 12.7 %collective-permute-start.33 = (bf16[6,21,2,512]{3,2,1,0:T(2,128)(2,1)S(1)}, bf16[6,21,2,512]{3,2,1,0:T(2,128)(2,1)S(1)}, u32[]{:S(2)}, u32[]{:S(2)}) collective-permute-start(bf16[6,21,2,512]{3,2,1,0:T(2,128)(2,1)S(1)} %slice.72), channel_id=1, source_target_pairs={{30,0},{31,1},{0,2},{1,3},{2,4},{3,5},{4,6},{5,7},{6,8},{7,9},{8,1... | collective-permute-start | bytes 774152 | tf_op jit(solution)/shard_map/ppermute | solution.py:310
  202.1 11.1 %collective-permute-start.32 = (bf16[18,3,2,512]{3,2,1,0:T(2,128)(2,1)S(1)}, bf16[18,3,2,512]{3,2,1,0:T(2,128)(2,1)S(1)}, u32[]{:S(2)}, u32[]{:S(2)}) collective-permute-start(bf16[18,3,2,512]{3,2,1,0:T(2,128)(2,1)S(1)} %slice.71), channel_id=1, source_target_pairs={{1,0},{0,1},{3,2},{2,3},{5,4},{4,5},{7,6},{6,7},{9,8},{8,9},{11,10... | collective-permute-start | bytes 331784 | tf_op jit(solution)/shard_map/ppermute | solution.py:310
  202.4 10.8 %collective-permute-start.31 = (bf16[6,3,2,512]{3,2,1,0:T(2,128)(2,1)S(1)}, bf16[6,3,2,512]{3,2,1,0:T(2,128)(2,1)S(1)}, u32[]{:S(2)}, u32[]{:S(2)}) collective-permute-start(bf16[6,3,2,512]{3,2,1,0:T(2,128)(2,1)S(1)} %slice.70), channel_id=1, source_target_pairs={{31,0},{30,1},{1,2},{0,3},{3,4},{2,5},{5,6},{4,7},{7,8},{6,9},{9,1... | collective-permute-start | bytes 110600 | tf_op jit(solution)/shard_map/ppermute | solution.py:310

commit v2 on v1

--- a/solution.py
+++ b/solution.py
@@ -39,76 +39,29 @@
     return lat_size == 2 and rows % 32 == 0
 
 
-def cut_kernel(half, qkv_ref, out_ref, up_ref, down_ref, *refs):
-    chunks, sems = refs[:-1], refs[-1]
+def cut_kernel(half, qkv_ref, out_ref, up_ref, down_ref, *chunks):
     first = pl.multiple_of(lax.axis_index("lat") * half, 16)
-    copies = []
-    for index, target in enumerate(chunks):
-        block, part = divmod(index, 2)
+    for block, target in enumerate(chunks):
         place = 0
-        for source in ((qkv_ref, out_ref), (up_ref, down_ref))[part]:
+        for source in (qkv_ref, out_ref, up_ref, down_ref):
             width = source.shape[2]
-            copies.append(
-                pltpu.make_async_copy(
-                    source.at[block, pl.ds(first, half), :],
-                    target.at[0, :, pl.ds(place, width)],
-                    sems.at[len(copies)],
-                )
-            )
+            target[:, place : place + width] = source[block, pl.ds(first, half), :]
             place += width
-    for copy in copies:
-        copy.start()
-    for copy in copies:
-        copy.wait()
 
 
 def cut_chunks(qkv_weight, out_weight, up_weight, down_weight):
+    weights = (qkv_weight, out_weight, up_weight, down_weight)
     blocks, rows, _ = qkv_weight.shape
-    widths = (
-        qkv_weight.shape[2] + out_weight.shape[2],
-        up_weight.shape[2] + down_weight.shape[2],
-    )
+    width = sum(weight.shape[2] for weight in weights)
     return pl.pallas_call(
         functools.partial(cut_kernel, rows // 2),
-        out_shape=[
-            jax.ShapeDtypeStruct((1, rows // 2, width), jnp.bfloat16) for width in widths * blocks
-        ],
-        in_specs=[ANY] * 4,
-        out_specs=[ANY] * (2 * blocks),
-        scratch_shapes=[pltpu.SemaphoreType.DMA((4 * blocks,))],
-    )(qkv_weight, out_weight, up_weight, down_weight)
-
-
-def send(block, lon_size, move):
-    pairs = []
-    for lon in range(lon_size):
-        for core in range(2):
-            z, y, x, core_to = move(lon // 4, lon // 2 % 2, lon % 2, core)
-            pairs.append((lon * 2 + core, (z * 4 + y * 2 + x) * 2 + core_to))
-    return lax.ppermute(block, ("lon", "lat"), pairs)
-
-
-def relay(own, lon_size):
-    depth = lon_size // 4
-    column = [own] + [
-        send(own, lon_size, lambda z, y, x, c, step=step: ((z + step) % depth, y, x, c))
-        for step in range(1, depth)
-    ]
-    column = jnp.concatenate(column, 0)
-    beside = send(
-        column, lon_size, lambda z, y, x, c: (z, y, 1 - x, c) if c == 0 else (z, 1 - y, x, c)
-    )
-    first = jnp.concatenate([column, beside], 0)
-    second = send(
-        first, lon_size, lambda z, y, x, c: (z, 1 - y, x, c) if c == 0 else (z, y, 1 - x, c)
-    )
-    swap = lambda z, y, x, c: (z, y, x, 1 - c)
-    return [first, second, send(first, lon_size, swap), send(second, lon_size, swap)]
-
-
-def load_pieces(pieces, w_ref, sem):
+        out_shape=[jax.ShapeDtypeStruct((rows // 2, width), jnp.bfloat16)] * blocks,
+    )(*weights)
+
+
+def load_pieces(pieces, w_ref, sem, first):
     if len(pieces) == 1:
-        copy = pltpu.make_async_copy(pieces[0].at[0], w_ref, sem)
+        copy = pltpu.make_async_copy(pieces[0].at[:, pl.ds(first, w_ref.shape[1])], w_ref, sem)
         copy.start()
         copy.wait()
         return
@@ -141,7 +94,7 @@
 
     @pl.when(pl.program_id(0) == 0)
     def _():
-        load_pieces(pieces, w_ref, sem)
+        load_pieces(pieces, w_ref, sem, 0)
         vt_ref[...] = w_ref[:, 2 * features : 3 * features].T
 
     tokens = x_ref[0]
@@ -251,7 +204,7 @@
 
     @pl.when(pl.program_id(0) == 0)
     def _():
-        load_pieces(pieces, w_ref, sem)
+        load_pieces(pieces, w_ref, sem, 4 * w_ref.shape[0])
 
     tokens = x_ref[...]
     total = jnp.zeros(tokens.shape, jnp.float32)
@@ -344,27 +297,25 @@
     lon_size = lax.axis_size("lon")
     if relayed(qkv_weight.shape[1], lax.axis_size("lat")):
         chunks = cut_chunks(qkv_weight, out_weight, up_weight, down_weight)
-        gathered = [relay(chunk, lon_size) for chunk in chunks]
+        gathered = [lax.all_gather(chunk, ("lon", "lat"), axis=0, tiled=True) for chunk in chunks]
     else:
-        gathered = []
-        for block in range(2):
-            for pair in ((qkv_weight, out_weight), (up_weight, down_weight)):
-                joined = jnp.concatenate([weight[block] for weight in pair], 1)
-                gathered.append([lax.all_gather(joined, "lon", axis=0, tiled=True)[None]])
+        weights = (qkv_weight, out_weight, up_weight, down_weight)
+        chunks = [jnp.concatenate([weight[block] for weight in weights], 1) for block in range(2)]
+        gathered = [lax.all_gather(chunk, "lon", axis=0, tiled=True) for chunk in chunks]
     sharp = jnp.repeat(logit_scale * math.log2(math.e), HEAD, axis=1)
 
     def block_pass(cells, block, shifted):
         windows = to_windows(cells)
         middle = attend(
             windows,
-            gathered[2 * block],
+            [gathered[block]],
             norm_gain[block, :1],
             sharp[block : block + 1],
             shifted,
             rows // WLAT,
         )
         result = feed(
-            middle.reshape(-1, features), gathered[2 * block + 1], norm_gain[block, 1:], hidden_size
+            middle.reshape(-1, features), [gathered[block]], norm_gain[block, 1:], hidden_size
         )
         return from_windows(result.reshape(windows.shape), cols, rows)
 

time: 216 us -> 212 us (0.981)
  waiting for transfers between devices: 43.2 us -> 107 us
  starting transfers between devices: 39 us -> 7.91 us
  local copies, waits for them, and re-layouts: 36.8 us -> 13.6 us
  Pallas kernels: 88.6 us -> 65.7 us
  between operations: 0.35 us -> 13.6 us
  other arithmetic: 7.78 us -> 4.22 us
    all_gather x0 -> x2, waiting for transfers between devices: none -> 93.2 us  [per_device(): lax.all_gather(chunk, ('lon', 'lat'), axis=0, tiled=True)]
    ppermute x28 -> x0, starting transfers between devices: 33.9 us -> none  [send(): return lax.ppermute(block, ('lon', 'lat'), pairs)]
    ppermute x28 -> x0, waiting for transfers between devices: 31.6 us -> none  [send(): return lax.ppermute(block, ('lon', 'lat'), pairs)]
    pallas_call x1, Pallas kernels: 13.1 us -> 2.05 us  [cut_chunks(): pl.pallas_call(functools.partial(cut_kernel, rows // 2), out_shape=[jax.S...]
    pallas_call x2, Pallas kernels: 26.9 us -> 19 us  [feed(): pl.pallas_call(functools.partial(feed_kernel, len(pieces), hidden_size, 5...]
    unnamed x34 -> x12, local copies, waits for them, and re-layouts: 12.7 us -> 5.78 us
    reshape x2, local copies, waits for them, and re-layouts: 5.95 us -> 0.98 us  [to_windows(): return arranged.transpose(0, 2, 1, 3, 4, 5).reshape(-1, CELLS, features)]
    pallas_call x2, Pallas kernels: 48.6 us -> 44.7 us  [attend(): pl.pallas_call(functools.partial(attend_kernel, shifted, row_windows, len...]
  transfers between devices with their start and end apart: 34 -> 8, of which waited for: 8 -> 5; matrix products, arithmetic and copies ran while one was open for 16% -> 4% of each run, Pallas kernels for 29% -> 15%
where the time goes in v2:
time: 212 us
  waiting for transfers between devices  107 us (50%)
  Pallas kernels  65.7 us (31%)
  local copies, waits for them, and re-layouts  13.6 us (6%)
  between operations  13.6 us (6%)
  starting transfers between devices  7.91 us (4%)
  other arithmetic  4.22 us (2%)
    all_gather x2, waiting for transfers between devices, per_device(): lax.all_gather(chunk, ('lon', 'lat'), axis=0, tiled=True)  93.2 us
    pallas_call x2, Pallas kernels, attend(): pl.pallas_call(functools.partial(attend_kernel, shifted, row_windows, len...  44.7 us
    pallas_call x2, Pallas kernels, feed(): pl.pallas_call(functools.partial(feed_kernel, len(pieces), hidden_size, 5...  19 us
    ppermute x6, waiting for transfers between devices, shift_from(): return lax.ppermute(block, ('lon', 'lat'), pairs)  12.7 us
    ppermute x6, starting transfers between devices, shift_from(): return lax.ppermute(block, ('lon', 'lat'), pairs)  7.87 us
    unnamed x12, local copies, waits for them, and re-layouts  5.78 us
  transfers between devices with their start and end apart: 8, of which 5 were waited for; matrix products, arithmetic and copies ran while one was open for 4% of the time, Pallas kernels for 15%

profile of v2, /device:TPU:0, one launch (start us, length us, event | category | flops | bytes accessed | tf_op | source)
XLA Modules:
  0.0 211.8 jit_solution(1145910517945112319)
XLA Ops:
  6.5 0.0 copy-start.5
  6.5 0.0 copy-start.3
  6.5 0.0 all-gather.3.cloned.1.call-start
  6.5 2.0 shard_map.82
  8.6 0.0 all-gather.3.cloned.1.call-update
  8.6 0.0 all-gather.5.cloned.1.call-start
  8.7 0.7 all-gather.5.cloned.1.call-update
  9.4 0.0 copy-done.5
  9.4 0.1 broadcast_in_dim.9
  9.5 0.1 broadcast_in_dim.10.refs_3_
  9.6 0.0 copy-done.3
  9.6 0.8 copy.16
  10.4 0.0 copy-start.4
  10.4 0.5 reshape.36.refs_0_
  10.9 0.2 copy-done.4
  11.1 71.4 %all-gather.3.cloned.1.call-done.refs_1_ = bf16[512,6144]{1,0:T(8,128)(2,1)} async-done(((bf16[16,6144]{1,0:T(8,128)(2,1)}), bf16[512,6144]{1,0:T(8,128)(2,1)}) %all-gather.3.cloned.1.call-update) | async-done | bytes 6291472 | tf_op jit(solution)/shard_map/all_gather | solution.py:300
  82.5 0.0 copy-start.1
  82.5 2.8 %copy-done.1 = bf16[512,6144]{1,0:T(8,128)(2,1)S(1)} copy-done((bf16[512,6144]{1,0:T(8,128)(2,1)S(1)}, bf16[512,6144]{1,0:T(8,128)(2,1)}, u32[]{:S(2)}) %copy-start.1) | copy-done | bytes 6291480
  85.3 22.3 %shard_map.83 = bf16[8,144,512]{2,1,0:T(8,128)(2,1)S(1)} custom-call(bf16[8,144,512]{2,1,0:T(8,128)(2,1)S(1)} %reshape.36.refs_0_, bf16[512,6144]{1,0:T(8,128)(2,1)S(1)} %copy-done.1, f32[1,512]{1,0:T(1,128)S(1)} %get-tuple-element.11.refs_2_, f32[1,512]{1,0:T(1,128)S(1)} %broadcast_in_dim.10.refs_3_), custom_call_target="tpu_custom_call" | custom-call | flops 8800000000 | bytes 6000000 | tf_op jit(solution)/shard_map/pallas_call | solution.py:180
  107.6 9.5 %shard_map.84 = bf16[1152,512]{1,0:T(8,128)(2,1)S(1)} custom-call(bf16[1152,512]{1,0:T(8,128)(2,1)S(1)} %bitcast.27, bf16[512,6144]{1,0:T(8,128)(2,1)S(1)} %copy-done.1, f32[1,512]{1,0:T(1,128)S(1)} %get-tuple-element.10.refs_2_), custom_call_target="tpu_custom_call" | custom-call | flops 4831838208 | bytes 8000000 | tf_op jit(solution)/shard_map/pallas_call | solution.py:225
  117.1 0.5 reshape_reshape.6
  117.6 1.2 copy.12
  118.7 0.2 slice.67
  118.9 2.8 %collective-permute-start = (bf16[6,21,2,512]{3,2,1,0:T(2,128)(2,1)S(1)}, bf16[6,21,2,512]{3,2,1,0:T(2,128)(2,1)S(1)}, u32[]{:S(2)}, u32[]{:S(2)}) collective-permute-start(bf16[6,21,2,512]{3,2,1,0:T(2,128)(2,1)S(1)} %slice.67), channel_id=1, source_target_pairs={{2,0},{3,1},{4,2},{5,3},{6,4},{7,5},{8,6},{9,7},{10,8},{11,9},{12,... | collective-permute-start | bytes 774152 | tf_op jit(solution)/shard_map/ppermute | solution.py:263
  121.7 0.1 slice.68
  121.8 0.1 collective-permute-start.1
  121.9 1.8 collective-permute-start.2
  123.7 0.1 broadcast_in_dim.11
  123.8 0.1 broadcast_in_dim.12.refs_3_
  123.9 0.5 slice.66
  124.4 4.2 %collective-permute-done.2 = bf16[6,3,2,512]{3,2,1,0:T(2,128)(2,1)S(1)} collective-permute-done((bf16[6,3,2,512]{3,2,1,0:T(2,128)(2,1)S(1)}, bf16[6,3,2,512]{3,2,1,0:T(2,128)(2,1)S(1)}, u32[]{:S(2)}, u32[]{:S(2)}) %collective-permute-start.2) | collective-permute-done | bytes 36896 | tf_op jit(solution)/shard_map/ppermute | solution.py:263
  128.6 0.0 collective-permute-done.1
  128.6 0.0 collective-permute-done
  128.6 1.7 maximum_maximum_fusion
  130.3 0.8 copy.13
  131.1 0.0 copy-start.2
  131.1 0.5 reshape.40.refs_0_
  131.6 21.8 %all-gather.5.cloned.1.call-done.refs_1_ = bf16[512,6144]{1,0:T(8,128)(2,1)} async-done(((bf16[16,6144]{1,0:T(8,128)(2,1)}), bf16[512,6144]{1,0:T(8,128)(2,1)}) %all-gather.5.cloned.1.call-update) | async-done | bytes 6291472 | tf_op jit(solution)/shard_map/all_gather | solution.py:300
  153.4 0.0 copy-done.2
  153.5 0.0 copy-start
  153.5 2.8 %copy-done = bf16[512,6144]{1,0:T(8,128)(2,1)S(1)} copy-done((bf16[512,6144]{1,0:T(8,128)(2,1)S(1)}, bf16[512,6144]{1,0:T(8,128)(2,1)}, u32[]{:S(2)}) %copy-start) | copy-done | bytes 6291480
  156.2 22.4 %shard_map.85 = bf16[8,144,512]{2,1,0:T(8,128)(2,1)S(1)} custom-call(bf16[8,144,512]{2,1,0:T(8,128)(2,1)S(1)} %reshape.40.refs_0_, bf16[512,6144]{1,0:T(8,128)(2,1)S(1)} %copy-done, f32[1,512]{1,0:T(1,128)S(1)} %get-tuple-element.12.refs_2_, f32[1,512]{1,0:T(1,128)S(1)} %broadcast_in_dim.12.refs_3_, f32[144,256]{1,0:T(8,128)S(1)} %copy-done.2), custom_call_target="tpu_custom_call" | custom-call | flops 8800000000 | bytes 6000000 | tf_op jit(solution)/shard_map/pallas_call | solution.py:180
  178.6 9.5 %shard_map.86 = bf16[1152,512]{1,0:T(8,128)(2,1)S(1)} custom-call(bf16[1152,512]{1,0:T(8,128)(2,1)S(1)} %bitcast.26, bf16[512,6144]{1,0:T(8,128)(2,1)S(1)} %copy-done, f32[1,512]{1,0:T(1,128)S(1)} %get-tuple-element.9.refs_2_), custom_call_target="tpu_custom_call" | custom-call | flops 4831838208 | bytes 8000000 | tf_op jit(solution)/shard_map/pallas_call | solution.py:225
  188.1 0.5 reshape_reshape.7
  188.6 1.2 copy.14
  189.8 0.2 slice.72
  190.0 1.5 collective-permute-start.5
  191.5 0.1 slice.71
  191.6 0.1 collective-permute-start.4
  191.7 1.7 collective-permute-start.3
  193.3 0.5 slice.73
  193.9 8.3 %collective-permute-done.3 = bf16[6,3,2,512]{3,2,1,0:T(2,128)(2,1)S(1)} collective-permute-done((bf16[6,3,2,512]{3,2,1,0:T(2,128)(2,1)S(1)}, bf16[6,3,2,512]{3,2,1,0:T(2,128)(2,1)S(1)}, u32[]{:S(2)}, u32[]{:S(2)}) %collective-permute-start.3) | collective-permute-done | bytes 36896 | tf_op jit(solution)/shard_map/ppermute | solution.py:263
  202.2 0.0 collective-permute-done.4
  202.2 0.3 collective-permute-done.5
  202.4 2.5 %maximum_maximum_fusion.1 = bf16[24,24,2,512]{3,2,1,0:T(2,128)(2,1)} fusion(bf16[18,21,2,512]{3,2,1,0:T(2,128)(2,1)S(1)} %slice.73, bf16[6,21,2,512]{3,2,1,0:T(2,128)(2,1)S(1)} %collective-permute-done.5, bf16[18,3,2,512]{3,2,1,0:T(2,128)(2,1)S(1)} %collective-permute-done.4, bf16[6,3,2,512]{3,2,1,0:T(2,128)(2,1)S(1)} %collective-permute-done.3), kind=kLoop, calls=%fused_computation.1 | loop fusion | flops 1769472 | bytes 2359296 | tf_op jit(solution)/shard_map/concatenate | solution.py:285
  (5 shorter events, 0.1 us)
Async XLA Ops:
  6.5 2.8 %copy-start.5 = (f32[2,16]{1,0:T(2,128)S(1)}, f32[2,16]{1,0:T(2,128)}, u32[]{:S(2)}) copy-start(f32[2,16]{1,0:T(2,128)} %param.14) | copy-start | bytes 388
  6.5 3.0 %copy-start.3 = (bf16[24,24,2,512]{3,2,1,0:T(2,128)(2,1)S(1)}, bf16[24,24,2,512]{3,2,1,0:T(2,128)(2,1)}, u32[]{:S(2)}) copy-start(bf16[24,24,2,512]{3,2,1,0:T(2,128)(2,1)} %param.8) | copy-start | bytes 3538948
  6.5 75.9 %all-gather.3.cloned.1.call-start = ((), (), s32[]{:S(2)}) async-start(), calls=%async_computation | async-start | bytes 6488064 | tf_op jit(solution)/shard_map/all_gather | solution.py:300
  8.6 144.8 %all-gather.5.cloned.1.call-start = ((), (), s32[]{:S(2)}) async-start(), calls=%async_computation.1 | async-start | bytes 6488064 | tf_op jit(solution)/shard_map/all_gather | solution.py:300
  10.4 0.7 copy-start.4
  82.5 2.8 %copy-start.1 = (bf16[512,6144]{1,0:T(8,128)(2,1)S(1)}, bf16[512,6144]{1,0:T(8,128)(2,1)}, u32[]{:S(2)}) copy-start(bf16[512,6144]{1,0:T(8,128)(2,1)} %all-gather.3.cloned.1.call-done.refs_1_) | copy-start | bytes 18874372
  118.9 9.7 %collective-permute-start = (bf16[6,21,2,512]{3,2,1,0:T(2,128)(2,1)S(1)}, bf16[6,21,2,512]{3,2,1,0:T(2,128)(2,1)S(1)}, u32[]{:S(2)}, u32[]{:S(2)}) collective-permute-start(bf16[6,21,2,512]{3,2,1,0:T(2,128)(2,1)S(1)} %slice.67), channel_id=1, source_target_pairs={{2,0},{3,1},{4,2},{5,3},{6,4},{7,5},{8,6},{9,7},{10,8},{11,9},{12,... | collective-permute-start | bytes 774152 | tf_op jit(solution)/shard_map/ppermute | solution.py:263
  121.8 6.8 %collective-permute-start.1 = (bf16[18,3,2,512]{3,2,1,0:T(2,128)(2,1)S(1)}, bf16[18,3,2,512]{3,2,1,0:T(2,128)(2,1)S(1)}, u32[]{:S(2)}, u32[]{:S(2)}) collective-permute-start(bf16[18,3,2,512]{3,2,1,0:T(2,128)(2,1)S(1)} %slice.68), channel_id=1, source_target_pairs={{1,0},{0,1},{3,2},{2,3},{5,4},{4,5},{7,6},{6,7},{9,8},{8,9},{11,10... | collective-permute-start | bytes 331784 | tf_op jit(solution)/shard_map/ppermute | solution.py:263
  121.9 6.7 %collective-permute-start.2 = (bf16[6,3,2,512]{3,2,1,0:T(2,128)(2,1)S(1)}, bf16[6,3,2,512]{3,2,1,0:T(2,128)(2,1)S(1)}, u32[]{:S(2)}, u32[]{:S(2)}) collective-permute-start(bf16[6,3,2,512]{3,2,1,0:T(2,128)(2,1)S(1)} %slice.69), channel_id=1, source_target_pairs={{3,0},{2,1},{5,2},{4,3},{7,4},{6,5},{9,6},{8,7},{11,8},{10,9},{13,... | collective-permute-start | bytes 110600 | tf_op jit(solution)/shard_map/ppermute | solution.py:263
  131.1 22.3 %copy-start.2 = (f32[144,256]{1,0:T(8,128)S(1)}, f32[144,256]{1,0:T(8,128)}, u32[]{:S(2)}) copy-start(f32[144,256]{1,0:T(8,128)} %constant.4.clone.refs_4_) | copy-start | bytes 442372
  153.5 2.8 %copy-start = (bf16[512,6144]{1,0:T(8,128)(2,1)S(1)}, bf16[512,6144]{1,0:T(8,128)(2,1)}, u32[]{:S(2)}) copy-start(bf16[512,6144]{1,0:T(8,128)(2,1)} %all-gather.5.cloned.1.call-done.refs_1_) | copy-start | bytes 18874372
  190.0 12.4 %collective-permute-start.5 = (bf16[6,21,2,512]{3,2,1,0:T(2,128)(2,1)S(1)}, bf16[6,21,2,512]{3,2,1,0:T(2,128)(2,1)S(1)}, u32[]{:S(2)}, u32[]{:S(2)}) collective-permute-start(bf16[6,21,2,512]{3,2,1,0:T(2,128)(2,1)S(1)} %slice.72), channel_id=1, source_target_pairs={{30,0},{31,1},{0,2},{1,3},{2,4},{3,5},{4,6},{5,7},{6,8},{7,9},{8,1... | collective-permute-start | bytes 774152 | tf_op jit(solution)/shard_map/ppermute | solution.py:263
  191.6 10.6 %collective-permute-start.4 = (bf16[18,3,2,512]{3,2,1,0:T(2,128)(2,1)S(1)}, bf16[18,3,2,512]{3,2,1,0:T(2,128)(2,1)S(1)}, u32[]{:S(2)}, u32[]{:S(2)}) collective-permute-start(bf16[18,3,2,512]{3,2,1,0:T(2,128)(2,1)S(1)} %slice.71), channel_id=1, source_target_pairs={{1,0},{0,1},{3,2},{2,3},{5,4},{4,5},{7,6},{6,7},{9,8},{8,9},{11,10... | collective-permute-start | bytes 331784 | tf_op jit(solution)/shard_map/ppermute | solution.py:263
  191.7 10.5 %collective-permute-start.3 = (bf16[6,3,2,512]{3,2,1,0:T(2,128)(2,1)S(1)}, bf16[6,3,2,512]{3,2,1,0:T(2,128)(2,1)S(1)}, u32[]{:S(2)}, u32[]{:S(2)}) collective-permute-start(bf16[6,3,2,512]{3,2,1,0:T(2,128)(2,1)S(1)} %slice.70), channel_id=1, source_target_pairs={{31,0},{30,1},{1,2},{0,3},{3,4},{2,5},{5,6},{4,7},{7,8},{6,9},{9,1... | collective-permute-start | bytes 110600 | tf_op jit(solution)/shard_map/ppermute | solution.py:263
Sparse Core Ops, SparseCore 0:
  10.2 72.1 all-gather.2
  85.3 68.0 all-gather.4

commit v3 on v2

--- a/solution.py
+++ b/solution.py
@@ -87,82 +87,59 @@
 
 def attend_kernel(shifted, row_windows, count, *refs):
     x_ref, pieces = refs[0], refs[1 : 1 + count]
-    gain_ref, sharp_ref = refs[1 + count : 3 + count]
-    allow_ref = refs[3 + count] if shifted else None
-    out_ref, w_ref, vt_ref, sem = refs[-4:]
-    features = x_ref.shape[-1]
+    gain_ref, sharp_ref, ones_ref = refs[1 + count : 4 + count]
+    allow_ref = refs[4 + count] if shifted else None
+    out_ref, w_ref, sem = refs[-3:]
+    held, _, features = x_ref.shape
 
     @pl.when(pl.program_id(0) == 0)
     def _():
         load_pieces(pieces, w_ref, sem, 0)
-        vt_ref[...] = w_ref[:, 2 * features : 3 * features].T
-
-    tokens = x_ref[0]
-    queries = dot(tokens, w_ref[:, :features]).astype(jnp.bfloat16).astype(jnp.float32)
-    keys = dot(tokens, w_ref[:, features : 2 * features]).astype(jnp.bfloat16).astype(jnp.float32)
-    values = dot(vt_ref[...], tokens, NT).astype(jnp.bfloat16)
-
+
+    tokens = x_ref[...].reshape(held * CELLS, features)
     channel = lax.broadcasted_iota(jnp.int32, (WIDE, WIDE), 0) // HEAD
     same_head = jnp.where(
         channel == lax.broadcasted_iota(jnp.int32, (WIDE, WIDE), 1) // HEAD, 1.0, 0.0
     ).astype(jnp.bfloat16)
     lane_head = lax.broadcasted_iota(jnp.int32, (1, WIDE), 1) // HEAD
-    diagonal = (
-        lax.broadcasted_iota(jnp.int32, (WIDE, MAIN), 0) // HEAD
-        == lax.broadcasted_iota(jnp.int32, (WIDE, MAIN), 1) // REST
-    )
-    if shifted:
-        last = jnp.logical_and(
-            pl.program_id(0) % row_windows == row_windows - 1,
-            lax.axis_index("lat") == lax.axis_size("lat") - 1,
-        )
-        allow = jnp.where(last, allow_ref[...], 1.0)
-        allow_main = jnp.concatenate([allow[:, :MAIN]] * 2, 1)
-        allow_rest = allow[:, MAIN:]
+    masks = [jnp.where(lane_head == head, 1.0, 0.0).astype(jnp.bfloat16) for head in range(GROUP)]
 
     def units(part):
-        squares = (part * part).astype(jnp.bfloat16)
-        length2 = dot(squares, same_head)
+        rounded = part.astype(jnp.bfloat16)
+        length2 = dot(rounded * rounded, same_head)
         return part * lax.rsqrt(jnp.maximum(length2, 0.25 * HEAD))
 
-    main_rows, rest_rows = [], []
+    attended = [[] for _ in range(held)]
     for group in range(HEADS // GROUP):
-        lanes = slice(group * WIDE, (group + 1) * WIDE)
-        query = (units(queries[:, lanes]) * sharp_ref[:, lanes]).astype(jnp.bfloat16)
-        key = units(keys[:, lanes]).astype(jnp.bfloat16)
-        value = values[lanes]
-
-        def masked(rows, head):
-            return jnp.where(lane_head == head, rows, jnp.zeros_like(rows))
-
-        def weights(stacked, allowed):
-            scores = dot(key, stacked, NT)
-            powers = jnp.exp2(scores)
+        lanes = [slice(n * features + group * WIDE, n * features + (group + 1) * WIDE) for n in range(3)]
+        queries = (units(dot(tokens, w_ref[:, lanes[0]])) * sharp_ref[:, lanes[0]]).astype(jnp.bfloat16)
+        keys = units(dot(tokens, w_ref[:, lanes[1]])).astype(jnp.bfloat16)
+        values = dot(tokens, w_ref[:, lanes[2]]).astype(jnp.bfloat16)
+        for window in range(held):
+            own = slice(window * CELLS, (window + 1) * CELLS)
+            query, key, value = queries[own], keys[own], values[own]
+            stacked = jnp.concatenate([query * mask for mask in masks], 0)
+            main = jnp.exp2(dot(stacked, key[:MAIN], NT)).astype(jnp.bfloat16)
+            rest_keys = jnp.concatenate([key[MAIN:] * mask for mask in masks], 0)
+            rest = jnp.exp2(dot(query, rest_keys, NT)).astype(jnp.bfloat16)
+            parts = [main[head * CELLS : (head + 1) * CELLS] for head in range(GROUP)] + [rest]
             if shifted:
-                powers = powers * allowed
-            return powers.astype(jnp.bfloat16), 1.0 / jnp.sum(powers, 0, keepdims=True)
-
-        for pair in range(GROUP // 2):
+                last = jnp.logical_and(
+                    (pl.program_id(0) * held + window) % row_windows == row_windows - 1,
+                    lax.axis_index("lat") == lax.axis_size("lat") - 1,
+                )
+                allow = jnp.where(last, allow_ref[...], 1.0).astype(jnp.bfloat16)
+                parts = [part * allow[:, :MAIN] for part in parts[:-1]] + [rest * allow[:, MAIN:]]
+            weights = jnp.concatenate(parts, 1)
             stacked = jnp.concatenate(
-                [masked(query[:MAIN], 2 * pair), masked(query[:MAIN], 2 * pair + 1)], 0
+                [value[:MAIN] * mask for mask in masks] + [value[MAIN:] * mask for mask in masks], 0
             )
-            weight, inverse = weights(stacked, allow_main if shifted else None)
-            both = dot(value[2 * pair * HEAD : 2 * (pair + 1) * HEAD], weight) * inverse
-            main_rows += [both[:HEAD, :MAIN], both[HEAD:, MAIN:]]
-        stacked = jnp.concatenate([masked(query[MAIN:], head) for head in range(GROUP)], 0)
-        weight, inverse = weights(stacked, allow_rest if shifted else None)
-        rest = dot(value, weight) * inverse
-        rest_rows.append(jnp.where(diagonal, rest, 0.0))
-    attended = jnp.concatenate(
-        [jnp.concatenate(main_rows, 0).T, jnp.concatenate(rest_rows, 0).T], 0
-    ).astype(jnp.bfloat16)
+            total = dot(weights, ones_ref[...])
+            attended[window].append((dot(weights, stacked) / total).astype(jnp.bfloat16))
+    attended = jnp.concatenate([jnp.concatenate(parts, 1) for parts in attended], 0)
     projected = dot(attended, w_ref[:, 3 * features :])
-    rest = projected[MAIN : MAIN + REST]
-    for head in range(1, GROUP):
-        rest = rest + projected[MAIN + head * REST : MAIN + (head + 1) * REST]
-    projected = jnp.concatenate([projected[:MAIN], rest], 0)
     middle = tokens.astype(jnp.float32) + layer_norm(projected, gain_ref[...])
-    out_ref[0] = middle.astype(jnp.bfloat16)
+    out_ref[...] = middle.astype(jnp.bfloat16).reshape(out_ref.shape)
 
 
 def allowed_pairs():
@@ -172,30 +149,36 @@
     return (side[:, None] == np.concatenate([side[:MAIN], rest])[None, :]).astype(np.float32)
 
 
-def attend(windows, pieces, gain, sharp, shifted, row_windows):
+def head_columns():
+    rows = np.concatenate([np.repeat(np.arange(GROUP), MAIN), np.repeat(np.arange(GROUP), REST)])
+    return (rows[:, None] == np.arange(WIDE)[None, :] // HEAD).astype(np.float32)
+
+
+def attend(windows, pieces, gain, sharp, shifted, row_windows, held=2):
     count, cells, features = windows.shape
     whole = lambda shape: pl.BlockSpec(shape, lambda i: (0,) * len(shape))
-    block = pl.BlockSpec((1, cells, features), lambda i: (i, 0, 0))
+    block = pl.BlockSpec((held, cells, features), lambda i: (i, 0, 0))
+    ones = jnp.asarray(head_columns(), jnp.bfloat16)
     extra = (jnp.asarray(allowed_pairs()),) if shifted else ()
     return pl.pallas_call(
         functools.partial(attend_kernel, shifted, row_windows, len(pieces)),
-        grid=(count,),
+        grid=(count // held,),
         out_shape=jax.ShapeDtypeStruct(windows.shape, jnp.bfloat16),
         in_specs=[block]
         + [ANY] * len(pieces)
         + [whole((1, features))] * 2
+        + [whole(ones.shape)]
         + [whole(e.shape) for e in extra],
         out_specs=block,
         scratch_shapes=[
             pltpu.VMEM((features, 4 * features), jnp.bfloat16),
-            pltpu.VMEM((features, features), jnp.bfloat16),
             pltpu.SemaphoreType.DMA,
         ],
         compiler_params=pltpu.CompilerParams(vmem_limit_bytes=40 * 2**20),
         cost_estimate=pl.CostEstimate(
-            flops=count * 11_000_000_00, bytes_accessed=6_000_000, transcendentals=0
+            flops=count * 1_000_000_000, bytes_accessed=6_000_000, transcendentals=0
         ),
-    )(windows, *pieces, gain, sharp, *extra)
+    )(windows, *pieces, gain, sharp, ones, *extra)
 
 
 def feed_kernel(count, hidden_size, chunk, *refs):
@@ -210,11 +193,13 @@
     total = jnp.zeros(tokens.shape, jnp.float32)
     for start in range(0, hidden_size, chunk):
         grown = dot(tokens, w_ref[:, start : start + chunk])
-        hidden = jax.nn.gelu(grown).astype(jnp.bfloat16)
+        slope = math.sqrt(2.0 / math.pi)
+        bent = jnp.tanh(grown * (grown * grown * (0.044715 * slope) + slope))
+        hidden = (grown + grown * bent).astype(jnp.bfloat16)
         total = total + dot(
             hidden, w_ref[:, hidden_size + start : hidden_size + start + chunk], NT
         )
-    result = tokens.astype(jnp.float32) + layer_norm(total, gain_ref[...])
+    result = tokens.astype(jnp.float32) + layer_norm(0.5 * total, gain_ref[...])
     out_ref[...] = result.astype(jnp.bfloat16)
 
 

time: 212 us -> 207 us (0.976)
  Pallas kernels: 65.7 us -> 49.3 us
  waiting for transfers between devices: 107 us -> 118 us
    pallas_call x2, Pallas kernels: 44.7 us -> 29.4 us  [attend(): pl.pallas_call(functools.partial(attend_kernel, shifted, row_windows, len...]
    all_gather x2, waiting for transfers between devices: 93.2 us -> 102 us  [per_device(): lax.all_gather(chunk, ('lon', 'lat'), axis=0, tiled=True)]
    ppermute x6, waiting for transfers between devices: 12.7 us -> 16.1 us  [shift_from(): return lax.ppermute(block, ('lon', 'lat'), pairs)]
    unnamed x12 -> x16, local copies, waits for them, and re-layouts: 5.78 us -> 5.78 us
  transfers between devices with their start and end apart: 8 -> 8, of which waited for: 5 -> 5; matrix products, arithmetic and copies ran while one was open for 4% -> 4% of each run, Pallas kernels for 15% -> 12%
where the time goes in v3:
time: 207 us
  waiting for transfers between devices  118 us (57%)
  Pallas kernels  49.3 us (24%)
  local copies, waits for them, and re-layouts  13.6 us (7%)
  between operations  13.6 us (7%)
  starting transfers between devices  7.89 us (4%)
  other arithmetic  4.22 us (2%)
    all_gather x2, waiting for transfers between devices, per_device(): lax.all_gather(chunk, ('lon', 'lat'), axis=0, tiled=True)  102 us
    pallas_call x2, Pallas kernels, attend(): pl.pallas_call(functools.partial(attend_kernel, shifted, row_windows, len...  29.4 us
    pallas_call x2, Pallas kernels, feed(): pl.pallas_call(functools.partial(feed_kernel, len(pieces), hidden_size, 5...  17.8 us
    ppermute x6, waiting for transfers between devices, shift_from(): return lax.ppermute(block, ('lon', 'lat'), pairs)  16.1 us
    ppermute x6, starting transfers between devices, shift_from(): return lax.ppermute(block, ('lon', 'lat'), pairs)  7.85 us
    unnamed x16, local copies, waits for them, and re-layouts  5.78 us
  transfers between devices with their start and end apart: 8, of which 5 were waited for; matrix products, arithmetic and copies ran while one was open for 4% of the time, Pallas kernels for 12%

profile of v3, /device:TPU:0, one launch (start us, length us, event | category | flops | bytes accessed | tf_op | source)
XLA Modules:
  0.0 207.1 jit_solution(16341222914395147650)
XLA Ops:
  6.5 0.0 copy-start.7
  6.5 0.0 copy-start.5
  6.5 0.0 all-gather.3.cloned.1.call-start
  6.5 2.0 shard_map.100
  8.6 0.0 all-gather.3.cloned.1.call-update
  8.6 0.0 all-gather.5.cloned.1.call-start
  8.7 0.7 all-gather.5.cloned.1.call-update
  9.4 0.0 copy-done.7
  9.4 0.1 broadcast_in_dim.9
  9.5 0.1 broadcast_in_dim.10.refs_3_
  9.5 0.0 copy-done.5
  9.5 0.8 copy.18
  10.4 0.0 copy-start.6
  10.4 0.0 copy-start.3
  10.4 0.5 reshape.36.refs_0_
  10.9 0.2 copy-done.6
  11.1 71.4 %all-gather.3.cloned.1.call-done.refs_1_ = bf16[512,6144]{1,0:T(8,128)(2,1)} async-done(((bf16[16,6144]{1,0:T(8,128)(2,1)}), bf16[512,6144]{1,0:T(8,128)(2,1)}) %all-gather.3.cloned.1.call-update) | async-done | bytes 6291472 | tf_op jit(solution)/shard_map/all_gather | solution.py:285
  82.5 0.0 copy-done.3
  82.5 0.0 copy-start.2
  82.5 2.8 %copy-done.2 = bf16[512,6144]{1,0:T(8,128)(2,1)S(1)} copy-done((bf16[512,6144]{1,0:T(8,128)(2,1)S(1)}, bf16[512,6144]{1,0:T(8,128)(2,1)}, u32[]{:S(2)}) %copy-start.2) | copy-done | bytes 6291480
  85.3 14.7 %shard_map.101 = bf16[8,144,512]{2,1,0:T(8,128)(2,1)S(1)} custom-call(bf16[8,144,512]{2,1,0:T(8,128)(2,1)S(1)} %reshape.36.refs_0_, bf16[512,6144]{1,0:T(8,128)(2,1)S(1)} %copy-done.2, f32[1,512]{1,0:T(1,128)S(1)} %get-tuple-element.11.refs_2_, f32[1,512]{1,0:T(1,128)S(1)} %broadcast_in_dim.10.refs_3_, bf16[1152,256]{1,0:T(8,128)(2,1)S(1)} %copy-done.3), custom_call_target="tpu_custom_call" | custom-call | flops 8000000000 | bytes 6000000 | tf_op jit(solution)/shard_map/pallas_call | solution.py:163
  100.0 9.1 %shard_map.102 = bf16[1152,512]{1,0:T(8,128)(2,1)S(1)} custom-call(bf16[1152,512]{1,0:T(8,128)(2,1)S(1)} %bitcast.27, bf16[512,6144]{1,0:T(8,128)(2,1)S(1)} %copy-done.2, f32[1,512]{1,0:T(1,128)S(1)} %get-tuple-element.10.refs_2_), custom_call_target="tpu_custom_call" | custom-call | flops 4831838208 | bytes 8000000 | tf_op jit(solution)/shard_map/pallas_call | solution.py:210
  109.1 0.5 reshape_reshape.6
  109.6 1.2 copy.14
  110.8 0.2 slice.67
  111.0 2.8 %collective-permute-start = (bf16[6,21,2,512]{3,2,1,0:T(2,128)(2,1)S(1)}, bf16[6,21,2,512]{3,2,1,0:T(2,128)(2,1)S(1)}, u32[]{:S(2)}, u32[]{:S(2)}) collective-permute-start(bf16[6,21,2,512]{3,2,1,0:T(2,128)(2,1)S(1)} %slice.67), channel_id=1, source_target_pairs={{2,0},{3,1},{4,2},{5,3},{6,4},{7,5},{8,6},{9,7},{10,8},{11,9},{12,... | collective-permute-start | bytes 774152 | tf_op jit(solution)/shard_map/ppermute | solution.py:248
  113.7 0.1 slice.68
  113.8 0.1 collective-permute-start.1
  113.9 1.8 collective-permute-start.2
  115.7 0.1 broadcast_in_dim.11
  115.8 0.1 broadcast_in_dim.12.refs_3_
  115.9 0.5 slice.66
  116.4 7.6 %collective-permute-done.2 = bf16[6,3,2,512]{3,2,1,0:T(2,128)(2,1)S(1)} collective-permute-done((bf16[6,3,2,512]{3,2,1,0:T(2,128)(2,1)S(1)}, bf16[6,3,2,512]{3,2,1,0:T(2,128)(2,1)S(1)}, u32[]{:S(2)}, u32[]{:S(2)}) %collective-permute-start.2) | collective-permute-done | bytes 36896 | tf_op jit(solution)/shard_map/ppermute | solution.py:248
  124.0 0.0 collective-permute-done.1
  124.0 0.0 collective-permute-done
  124.0 1.7 maximum_maximum_fusion
  125.7 0.8 copy.15
  126.5 0.0 copy-start.4
  126.6 0.5 reshape.40.refs_0_
  127.1 30.2 %all-gather.5.cloned.1.call-done.refs_1_ = bf16[512,6144]{1,0:T(8,128)(2,1)} async-done(((bf16[16,6144]{1,0:T(8,128)(2,1)}), bf16[512,6144]{1,0:T(8,128)(2,1)}) %all-gather.5.cloned.1.call-update) | async-done | bytes 6291472 | tf_op jit(solution)/shard_map/all_gather | solution.py:285
  157.2 0.0 copy-done.4
  157.2 0.0 copy-start
  157.2 2.8 %copy-done = bf16[512,6144]{1,0:T(8,128)(2,1)S(1)} copy-done((bf16[512,6144]{1,0:T(8,128)(2,1)S(1)}, bf16[512,6144]{1,0:T(8,128)(2,1)}, u32[]{:S(2)}) %copy-start) | copy-done | bytes 6291480
  160.0 0.0 copy-start.1
  160.0 14.7 %shard_map.103 = bf16[8,144,512]{2,1,0:T(8,128)(2,1)S(1)} custom-call(bf16[8,144,512]{2,1,0:T(8,128)(2,1)S(1)} %reshape.40.refs_0_, bf16[512,6144]{1,0:T(8,128)(2,1)S(1)} %copy-done, f32[1,512]{1,0:T(1,128)S(1)} %get-tuple-element.12.refs_2_, f32[1,512]{1,0:T(1,128)S(1)} %broadcast_in_dim.12.refs_3_, bf16[1152,256]{1,0:T(8,128)(2,1)S(1)} %copy-done.3, ...), custom_call_target="tpu_custom_call" | custom-call | flops 8000000000 | bytes 6000000 | tf_op jit(solution)/shard_map/pallas_call | solution.py:163
  174.8 0.0 copy-done.1
  174.8 8.7 %shard_map.104 = bf16[1152,512]{1,0:T(8,128)(2,1)S(1)} custom-call(bf16[1152,512]{1,0:T(8,128)(2,1)S(1)} %bitcast.26, bf16[512,6144]{1,0:T(8,128)(2,1)S(1)} %copy-done.1, f32[1,512]{1,0:T(1,128)S(1)} %get-tuple-element.9.refs_2_), custom_call_target="tpu_custom_call" | custom-call | flops 4831838208 | bytes 8000000 | tf_op jit(solution)/shard_map/pallas_call | solution.py:210
  183.5 0.5 reshape_reshape.7
  184.0 1.2 copy.16
  185.1 0.2 slice.72
  185.3 1.5 collective-permute-start.5
  186.8 0.1 slice.71
  186.9 0.1 collective-permute-start.4
  187.0 1.7 collective-permute-start.3
  188.7 0.5 slice.73
  189.2 8.3 %collective-permute-done.3 = bf16[6,3,2,512]{3,2,1,0:T(2,128)(2,1)S(1)} collective-permute-done((bf16[6,3,2,512]{3,2,1,0:T(2,128)(2,1)S(1)}, bf16[6,3,2,512]{3,2,1,0:T(2,128)(2,1)S(1)}, u32[]{:S(2)}, u32[]{:S(2)}) %collective-permute-start.3) | collective-permute-done | bytes 36896 | tf_op jit(solution)/shard_map/ppermute | solution.py:248
  197.5 0.0 collective-permute-done.4
  197.5 0.3 collective-permute-done.5
  197.8 2.5 %maximum_maximum_fusion.1 = bf16[24,24,2,512]{3,2,1,0:T(2,128)(2,1)} fusion(bf16[18,21,2,512]{3,2,1,0:T(2,128)(2,1)S(1)} %slice.73, bf16[6,21,2,512]{3,2,1,0:T(2,128)(2,1)S(1)} %collective-permute-done.5, bf16[18,3,2,512]{3,2,1,0:T(2,128)(2,1)S(1)} %collective-permute-done.4, bf16[6,3,2,512]{3,2,1,0:T(2,128)(2,1)S(1)} %collective-permute-done.3), kind=kLoop, calls=%fused_computation.1 | loop fusion | flops 1769472 | bytes 2359296 | tf_op jit(solution)/shard_map/concatenate | solution.py:270
  (5 shorter events, 0.1 us)
Async XLA Ops:
  6.5 2.8 %copy-start.7 = (f32[2,16]{1,0:T(2,128)S(1)}, f32[2,16]{1,0:T(2,128)}, u32[]{:S(2)}) copy-start(f32[2,16]{1,0:T(2,128)} %param.16) | copy-start | bytes 388
  6.5 3.0 %copy-start.5 = (bf16[24,24,2,512]{3,2,1,0:T(2,128)(2,1)S(1)}, bf16[24,24,2,512]{3,2,1,0:T(2,128)(2,1)}, u32[]{:S(2)}) copy-start(bf16[24,24,2,512]{3,2,1,0:T(2,128)(2,1)} %param.10) | copy-start | bytes 3538948
  6.5 75.9 %all-gather.3.cloned.1.call-start = ((), (), s32[]{:S(2)}) async-start(), calls=%async_computation | async-start | bytes 6488064 | tf_op jit(solution)/shard_map/all_gather | solution.py:285
  8.6 148.6 %all-gather.5.cloned.1.call-start = ((), (), s32[]{:S(2)}) async-start(), calls=%async_computation.1 | async-start | bytes 6488064 | tf_op jit(solution)/shard_map/all_gather | solution.py:285
  10.4 0.7 copy-start.6
  10.4 72.1 %copy-start.3 = (bf16[1152,256]{1,0:T(8,128)(2,1)S(1)}, bf16[1152,256]{1,0:T(8,128)(2,1)}, u32[]{:S(2)}) copy-start(bf16[1152,256]{1,0:T(8,128)(2,1)} %constant.6.clone.refs_4_) | copy-start | bytes 1769476
  82.5 2.8 %copy-start.2 = (bf16[512,6144]{1,0:T(8,128)(2,1)S(1)}, bf16[512,6144]{1,0:T(8,128)(2,1)}, u32[]{:S(2)}) copy-start(bf16[512,6144]{1,0:T(8,128)(2,1)} %all-gather.3.cloned.1.call-done.refs_1_) | copy-start | bytes 18874372
  111.0 13.1 %collective-permute-start = (bf16[6,21,2,512]{3,2,1,0:T(2,128)(2,1)S(1)}, bf16[6,21,2,512]{3,2,1,0:T(2,128)(2,1)S(1)}, u32[]{:S(2)}, u32[]{:S(2)}) collective-permute-start(bf16[6,21,2,512]{3,2,1,0:T(2,128)(2,1)S(1)} %slice.67), channel_id=1, source_target_pairs={{2,0},{3,1},{4,2},{5,3},{6,4},{7,5},{8,6},{9,7},{10,8},{11,9},{12,... | collective-permute-start | bytes 774152 | tf_op jit(solution)/shard_map/ppermute | solution.py:248
  113.8 10.2 %collective-permute-start.1 = (bf16[18,3,2,512]{3,2,1,0:T(2,128)(2,1)S(1)}, bf16[18,3,2,512]{3,2,1,0:T(2,128)(2,1)S(1)}, u32[]{:S(2)}, u32[]{:S(2)}) collective-permute-start(bf16[18,3,2,512]{3,2,1,0:T(2,128)(2,1)S(1)} %slice.68), channel_id=1, source_target_pairs={{1,0},{0,1},{3,2},{2,3},{5,4},{4,5},{7,6},{6,7},{9,8},{8,9},{11,10... | collective-permute-start | bytes 331784 | tf_op jit(solution)/shard_map/ppermute | solution.py:248
  113.9 10.1 %collective-permute-start.2 = (bf16[6,3,2,512]{3,2,1,0:T(2,128)(2,1)S(1)}, bf16[6,3,2,512]{3,2,1,0:T(2,128)(2,1)S(1)}, u32[]{:S(2)}, u32[]{:S(2)}) collective-permute-start(bf16[6,3,2,512]{3,2,1,0:T(2,128)(2,1)S(1)} %slice.69), channel_id=1, source_target_pairs={{3,0},{2,1},{5,2},{4,3},{7,4},{6,5},{9,6},{8,7},{11,8},{10,9},{13,... | collective-permute-start | bytes 110600 | tf_op jit(solution)/shard_map/ppermute | solution.py:248
  126.5 30.7 %copy-start.4 = (f32[144,256]{1,0:T(8,128)S(1)}, f32[144,256]{1,0:T(8,128)}, u32[]{:S(2)}) copy-start(f32[144,256]{1,0:T(8,128)} %constant.7.clone.refs_5_) | copy-start | bytes 442372
  157.2 2.8 %copy-start = (bf16[512,6144]{1,0:T(8,128)(2,1)S(1)}, bf16[512,6144]{1,0:T(8,128)(2,1)}, u32[]{:S(2)}) copy-start(bf16[512,6144]{1,0:T(8,128)(2,1)} %all-gather.5.cloned.1.call-done.refs_1_) | copy-start | bytes 18874372
  160.0 14.7 %copy-start.1 = (bf16[512,6144]{1,0:T(8,128)(2,1)S(1)}, bf16[512,6144]{1,0:T(8,128)(2,1)}, u32[]{:S(2)}) copy-start(bf16[512,6144]{1,0:T(8,128)(2,1)} %all-gather.5.cloned.1.call-done.refs_1_) | copy-start | bytes 18874372
  185.3 12.4 %collective-permute-start.5 = (bf16[6,21,2,512]{3,2,1,0:T(2,128)(2,1)S(1)}, bf16[6,21,2,512]{3,2,1,0:T(2,128)(2,1)S(1)}, u32[]{:S(2)}, u32[]{:S(2)}) collective-permute-start(bf16[6,21,2,512]{3,2,1,0:T(2,128)(2,1)S(1)} %slice.72), channel_id=1, source_target_pairs={{30,0},{31,1},{0,2},{1,3},{2,4},{3,5},{4,6},{5,7},{6,8},{7,9},{8,1... | collective-permute-start | bytes 774152 | tf_op jit(solution)/shard_map/ppermute | solution.py:248
  186.9 10.6 %collective-permute-start.4 = (bf16[18,3,2,512]{3,2,1,0:T(2,128)(2,1)S(1)}, bf16[18,3,2,512]{3,2,1,0:T(2,128)(2,1)S(1)}, u32[]{:S(2)}, u32[]{:S(2)}) collective-permute-start(bf16[18,3,2,512]{3,2,1,0:T(2,128)(2,1)S(1)} %slice.71), channel_id=1, source_target_pairs={{1,0},{0,1},{3,2},{2,3},{5,4},{4,5},{7,6},{6,7},{9,8},{8,9},{11,10... | collective-permute-start | bytes 331784 | tf_op jit(solution)/shard_map/ppermute | solution.py:248
  187.0 10.5 %collective-permute-start.3 = (bf16[6,3,2,512]{3,2,1,0:T(2,128)(2,1)S(1)}, bf16[6,3,2,512]{3,2,1,0:T(2,128)(2,1)S(1)}, u32[]{:S(2)}, u32[]{:S(2)}) collective-permute-start(bf16[6,3,2,512]{3,2,1,0:T(2,128)(2,1)S(1)} %slice.70), channel_id=1, source_target_pairs={{31,0},{30,1},{1,2},{0,3},{3,4},{2,5},{5,6},{4,7},{7,8},{6,9},{9,1... | collective-permute-start | bytes 110600 | tf_op jit(solution)/shard_map/ppermute | solution.py:248
Sparse Core Ops, SparseCore 0:
  10.2 72.1 all-gather.2
  85.3 71.8 all-gather.4

commit v4 on v3

--- a/solution.py
+++ b/solution.py
@@ -39,24 +39,81 @@
     return lat_size == 2 and rows % 32 == 0
 
 
-def cut_kernel(half, qkv_ref, out_ref, up_ref, down_ref, *chunks):
+def cut_rows(half, sources, block, target):
     first = pl.multiple_of(lax.axis_index("lat") * half, 16)
-    for block, target in enumerate(chunks):
-        place = 0
-        for source in (qkv_ref, out_ref, up_ref, down_ref):
-            width = source.shape[2]
-            target[:, place : place + width] = source[block, pl.ds(first, half), :]
-            place += width
-
-
-def cut_chunks(qkv_weight, out_weight, up_weight, down_weight):
-    weights = (qkv_weight, out_weight, up_weight, down_weight)
-    blocks, rows, _ = qkv_weight.shape
+    place = 0
+    for source in sources:
+        width = source.shape[2]
+        target[:, place : place + width] = source[block, pl.ds(first, half), :]
+        place += width
+
+
+def first_kernel(half, qkv_ref, out_ref, up_ref, down_ref, early_ref, late_ref):
+    cut_rows(half, (qkv_ref, out_ref), 0, early_ref)
+    cut_rows(half, (up_ref, down_ref), 1, late_ref)
+
+
+def first_cut(qkv_weight, out_weight, up_weight, down_weight):
+    half = qkv_weight.shape[1] // 2
+    widths = (
+        qkv_weight.shape[2] + out_weight.shape[2],
+        up_weight.shape[2] + down_weight.shape[2],
+    )
+    return pl.pallas_call(
+        functools.partial(first_kernel, half),
+        out_shape=[jax.ShapeDtypeStruct((half, width), jnp.bfloat16) for width in widths],
+    )(qkv_weight, out_weight, up_weight, down_weight)
+
+
+def join_kernel(count, block, *refs):
+    pieces, sources, column_ref = refs[:count], refs[count:-2], refs[-2]
+    for index, piece in enumerate(pieces):
+        column_ref[index] = piece[...]
+    cut_rows(pieces[0].shape[0], sources, block, refs[-1])
+
+
+def last_join_kernel(*refs):
+    for index, piece in enumerate(refs[:-1]):
+        refs[-1][index] = piece[...]
+
+
+def join(pieces, weights=(), block=0):
+    half = pieces[0].shape[0]
+    column = jax.ShapeDtypeStruct((len(pieces),) + pieces[0].shape, jnp.bfloat16)
+    if not weights:
+        return pl.pallas_call(last_join_kernel, out_shape=column)(*pieces), None
     width = sum(weight.shape[2] for weight in weights)
     return pl.pallas_call(
-        functools.partial(cut_kernel, rows // 2),
-        out_shape=[jax.ShapeDtypeStruct((rows // 2, width), jnp.bfloat16)] * blocks,
-    )(*weights)
+        functools.partial(join_kernel, len(pieces), block),
+        out_shape=[column, jax.ShapeDtypeStruct((half, width), jnp.bfloat16)],
+    )(*pieces, *weights)
+
+
+def send(block, lon_size, move):
+    pairs = []
+    for lon in range(lon_size):
+        for core in range(2):
+            z, y, x, core_to = move(lon // 4, lon // 2 % 2, lon % 2, core)
+            pairs.append((lon * 2 + core, (z * 4 + y * 2 + x) * 2 + core_to))
+    return lax.ppermute(block, ("lon", "lat"), pairs)
+
+
+def along_z(own, lon_size):
+    depth = lon_size // 4
+    return [own] + [
+        send(own, lon_size, lambda z, y, x, c, step=step: ((z + step) % depth, y, x, c))
+        for step in range(1, depth)
+    ]
+
+
+def spread(column, lon_size):
+    one = lambda z, y, x, c: (z, y, 1 - x, c) if c == 0 else (z, 1 - y, x, c)
+    other = lambda z, y, x, c: (z, 1 - y, x, c) if c == 0 else (z, y, 1 - x, c)
+    beside = send(column, lon_size, one)
+    across = send(column, lon_size, other)
+    corner = send(beside, lon_size, other)
+    own = [column, beside, across, corner]
+    return own + [send(part, lon_size, lambda z, y, x, c: (z, y, x, 1 - c)) for part in own]
 
 
 def load_pieces(pieces, w_ref, sem, first):
@@ -65,23 +122,22 @@
         copy.start()
         copy.wait()
         return
-    depth = pieces[0].shape[0] // 2
-    half = pieces[0].shape[1]
+    depth, half, _ = pieces[0].shape
     lon, lat = lax.axis_index("lon"), lax.axis_index("lat")
     z, y, x = lon // 4, lon // 2 % 2, lon % 2
+    by_x, by_y = y * 2 + 1 - x, (1 - y) * 2 + x
     for index, piece in enumerate(pieces):
-        core = lat if index < 2 else 1 - lat
-        if index % 2 == 0:
-            squares = (y * 2 + x, jnp.where(core == 0, y * 2 + 1 - x, (1 - y) * 2 + x))
-        else:
-            squares = (
-                jnp.where(core == 0, (1 - y) * 2 + x, y * 2 + 1 - x),
-                (1 - y) * 2 + 1 - x,
-            )
-        for j in range(2 * depth):
-            shard = (z + depth - j % depth) % depth * 4 + squares[j // depth]
+        core = lat if index < 4 else 1 - lat
+        square = (
+            y * 2 + x,
+            jnp.where(core == 0, by_x, by_y),
+            jnp.where(core == 0, by_y, by_x),
+            (1 - y) * 2 + 1 - x,
+        )[index % 4]
+        for step in range(depth):
+            shard = (z + depth - step) % depth * 4 + square
             row = pl.multiple_of((shard * 2 + core) * half, 16)
-            pltpu.make_async_copy(piece.at[j], w_ref.at[pl.ds(row, half), :], sem).start()
+            pltpu.make_async_copy(piece.at[step], w_ref.at[pl.ds(row, half), :], sem).start()
     pltpu.make_async_copy(w_ref, w_ref, sem).wait()
 
 
@@ -187,7 +243,7 @@
 
     @pl.when(pl.program_id(0) == 0)
     def _():
-        load_pieces(pieces, w_ref, sem, 4 * w_ref.shape[0])
+        load_pieces(pieces, w_ref, sem, 0)
 
     tokens = x_ref[...]
     total = jnp.zeros(tokens.shape, jnp.float32)
@@ -280,27 +336,35 @@
     cols, rows, _, features = tokens.shape
     hidden_size = up_weight.shape[-1]
     lon_size = lax.axis_size("lon")
+    weights = (qkv_weight, out_weight, up_weight, down_weight)
     if relayed(qkv_weight.shape[1], lax.axis_size("lat")):
-        chunks = cut_chunks(qkv_weight, out_weight, up_weight, down_weight)
-        gathered = [lax.all_gather(chunk, ("lon", "lat"), axis=0, tiled=True) for chunk in chunks]
+        own, late = first_cut(*weights)
+        late = [lax.all_gather(late, ("lon", "lat"), axis=0, tiled=True)]
+        gathered = []
+        for cut, block in ((weights[2:], 0), (weights[:2], 1), ((), 0)):
+            column, own = join(along_z(own, lon_size), cut, block)
+            gathered.append(spread(column, lon_size))
+        gathered.append(late)
     else:
-        weights = (qkv_weight, out_weight, up_weight, down_weight)
-        chunks = [jnp.concatenate([weight[block] for weight in weights], 1) for block in range(2)]
-        gathered = [lax.all_gather(chunk, "lon", axis=0, tiled=True) for chunk in chunks]
+        gathered = []
+        for block in range(2):
+            for pair in (weights[:2], weights[2:]):
+                chunk = jnp.concatenate([weight[block] for weight in pair], 1)
+                gathered.append([lax.all_gather(chunk, "lon", axis=0, tiled=True)])
     sharp = jnp.repeat(logit_scale * math.log2(math.e), HEAD, axis=1)
 
     def block_pass(cells, block, shifted):
         windows = to_windows(cells)
         middle = attend(
             windows,
-            [gathered[block]],
+            gathered[2 * block],
             norm_gain[block, :1],
             sharp[block : block + 1],
             shifted,
             rows // WLAT,
         )
         result = feed(
-            middle.reshape(-1, features), [gathered[block]], norm_gain[block, 1:], hidden_size
+            middle.reshape(-1, features), gathered[2 * block + 1], norm_gain[block, 1:], hidden_size
         )
         return from_windows(result.reshape(windows.shape), cols, rows)
 

time: 207 us -> 198 us (0.957)
  waiting for transfers between devices: 118 us -> 57.7 us
  starting transfers between devices: 7.89 us -> 33.1 us
  Pallas kernels: 49.3 us -> 63 us
  local copies, waits for them, and re-layouts: 13.6 us -> 26 us
    all_gather x2 -> x1, waiting for transfers between devices: 102 us -> 0.01 us  [per_device(): late = [lax.all_gather(late, ('lon', 'lat'), axis=0, tiled=True)]]
    ppermute x0 -> x30, waiting for transfers between devices: none -> 43.3 us  [send(): return lax.ppermute(block, ('lon', 'lat'), pairs)]
    ppermute x0 -> x30, starting transfers between devices: none -> 26.8 us  [send(): return lax.ppermute(block, ('lon', 'lat'), pairs)]
    pallas_call x1 -> x4, Pallas kernels: 2.04 us -> 7.63 us  [the longest x2 4.02 us: join(): pl.pallas_call(functools.partial(join_kernel, len(pieces), block), out_sh...]
    unnamed x16 -> x50, local copies, waits for them, and re-layouts: 5.78 us -> 10.9 us
    reshape x2, local copies, waits for them, and re-layouts: 0.98 us -> 6.03 us  [to_windows(): return arranged.transpose(0, 2, 1, 3, 4, 5).reshape(-1, CELLS, features)]
    pallas_call x2, Pallas kernels: 17.8 us -> 22.2 us  [feed(): pl.pallas_call(functools.partial(feed_kernel, len(pieces), hidden_size, 5...]
    pallas_call x2, Pallas kernels: 29.4 us -> 33.2 us  [attend(): pl.pallas_call(functools.partial(attend_kernel, shifted, row_windows, len...]
  transfers between devices with their start and end apart: 8 -> 37, of which waited for: 5 -> 12; matrix products, arithmetic and copies ran while one was open for 4% -> 8% of each run, Pallas kernels for 12% -> 27%
where the time goes in v4:
time: 198 us
  Pallas kernels  63 us (32%)
  waiting for transfers between devices  57.7 us (29%)
  starting transfers between devices  33.1 us (17%)
  local copies, waits for them, and re-layouts  26 us (13%)
  between operations  13.8 us (7%)
  other arithmetic  4.24 us (2%)
    ppermute x30, waiting for transfers between devices, send(): return lax.ppermute(block, ('lon', 'lat'), pairs)  43.3 us
    pallas_call x2, Pallas kernels, attend(): pl.pallas_call(functools.partial(attend_kernel, shifted, row_windows, len...  33.2 us
    ppermute x30, starting transfers between devices, send(): return lax.ppermute(block, ('lon', 'lat'), pairs)  26.8 us
    pallas_call x2, Pallas kernels, feed(): pl.pallas_call(functools.partial(feed_kernel, len(pieces), hidden_size, 5...  22.2 us
    ppermute x6, waiting for transfers between devices, shift_from(): return lax.ppermute(block, ('lon', 'lat'), pairs)  14.5 us
    unnamed x50, local copies, waits for them, and re-layouts  10.9 us
    ppermute x6, starting transfers between devices, shift_from(): return lax.ppermute(block, ('lon', 'lat'), pairs)  6.27 us
    reshape x2, local copies, waits for them, and re-layouts, to_windows(): return arranged.transpose(0, 2, 1, 3, 4, 5).reshape(-1, CELLS, features)  6.03 us
  transfers between devices with their start and end apart: 37, of which 12 were waited for; matrix products, arithmetic and copies ran while one was open for 8% of the time, Pallas kernels for 27%

profile of v4, /device:TPU:0, one launch (start us, length us, event | category | flops | bytes accessed | tf_op | source)
XLA Modules:
  0.0 197.8 jit_solution(13175395869603000749)
XLA Ops:
  6.5 2.0 shard_map.100
  8.5 3.1 %collective-permute-start = (bf16[16,2048]{1,0:T(8,128)(2,1)}, bf16[16,2048]{1,0:T(8,128)(2,1)S(1)}, u32[]{:S(2)}, u32[]{:S(2)}) collective-permute-start(bf16[16,2048]{1,0:T(8,128)(2,1)} %get-tuple-element.11.refs_0_), channel_id=1, source_target_pairs={{0,8},{1,9},{2,10},{3,11},{4,12},{5,13},{6,14},{7,15},{8,16},{9,17... | collective-permute-start | bytes 196616 | tf_op jit(solution)/shard_map/ppermute | solution.py:98
  11.6 2.6 %collective-permute-start.1 = (bf16[16,2048]{1,0:T(8,128)(2,1)}, bf16[16,2048]{1,0:T(8,128)(2,1)S(1)}, u32[]{:S(2)}, u32[]{:S(2)}) collective-permute-start(bf16[16,2048]{1,0:T(8,128)(2,1)} %get-tuple-element.11.refs_0_), channel_id=1, source_target_pairs={{0,16},{1,17},{2,18},{3,19},{4,20},{5,21},{6,22},{7,23},{8,24},{9,... | collective-permute-start | bytes 196616 | tf_op jit(solution)/shard_map/ppermute | solution.py:98
  14.2 1.3 collective-permute-start.2
  15.5 0.8 collective-permute-done.refs_1_
  16.4 2.5 %collective-permute-done.1.refs_2_ = bf16[16,2048]{1,0:T(8,128)(2,1)S(1)} collective-permute-done((bf16[16,2048]{1,0:T(8,128)(2,1)}, bf16[16,2048]{1,0:T(8,128)(2,1)S(1)}, u32[]{:S(2)}, u32[]{:S(2)}) %collective-permute-start.1) | collective-permute-done | bytes 65568 | tf_op jit(solution)/shard_map/ppermute | solution.py:98
  19.5 0.6 copy-done.19
  20.1 2.0 shard_map.101
  22.1 1.2 collective-permute-start.10
  23.3 2.6 %collective-permute-start.11 = (bf16[16,4096]{1,0:T(8,128)(2,1)}, bf16[16,4096]{1,0:T(8,128)(2,1)S(1)}, u32[]{:S(2)}, u32[]{:S(2)}) collective-permute-start(bf16[16,4096]{1,0:T(8,128)(2,1)} %get-tuple-element.13.refs_0_), channel_id=1, source_target_pairs={{0,16},{1,17},{2,18},{3,19},{4,20},{5,21},{6,22},{7,23},{8,24},{9,... | collective-permute-start | bytes 393224 | tf_op jit(solution)/shard_map/ppermute | solution.py:98
  26.0 5.4 %collective-permute-done.10.refs_1_ = bf16[16,4096]{1,0:T(8,128)(2,1)S(1)} collective-permute-done((bf16[16,4096]{1,0:T(8,128)(2,1)}, bf16[16,4096]{1,0:T(8,128)(2,1)S(1)}, u32[]{:S(2)}, u32[]{:S(2)}) %collective-permute-start.10) | collective-permute-done | bytes 131104 | tf_op jit(solution)/shard_map/ppermute | solution.py:98
  31.5 5.9 %collective-permute-done.11.refs_2_ = bf16[16,4096]{1,0:T(8,128)(2,1)S(1)} collective-permute-done((bf16[16,4096]{1,0:T(8,128)(2,1)}, bf16[16,4096]{1,0:T(8,128)(2,1)S(1)}, u32[]{:S(2)}, u32[]{:S(2)}) %collective-permute-start.11) | collective-permute-done | bytes 131104 | tf_op jit(solution)/shard_map/ppermute | solution.py:98
  37.4 0.6 copy-done.15
  38.1 0.7 copy-done.16
  38.8 2.1 %shard_map.103 = (bf16[4,16,4096]{2,1,0:T(8,128)(2,1)}, bf16[16,2048]{1,0:T(8,128)(2,1)}) custom-call(bf16[16,4096]{1,0:T(8,128)(2,1)} %get-tuple-element.13.refs_0_, bf16[16,4096]{1,0:T(8,128)(2,1)} %copy-done.14, bf16[16,4096]{1,0:T(8,128)(2,1)} %copy-done.15, bf16[16,4096]{1,0:T(8,128)(2,1)} %copy-done.16, bf16[2,32,1536]{2,1,0:T(8,128)(2,1)} %refs_4_.3, ...), custom_call_target="tpu_custom_call" | custom-call | tf_op jit(solution)/shard_map/pallas_call | solution.py:86
  40.8 1.0 collective-permute-start.13
  41.8 1.1 collective-permute-start.3
  42.8 2.4 %collective-permute-start.23 = (bf16[16,2048]{1,0:T(8,128)(2,1)}, bf16[16,2048]{1,0:T(8,128)(2,1)S(1)}, u32[]{:S(2)}, u32[]{:S(2)}) collective-permute-start(bf16[16,2048]{1,0:T(8,128)(2,1)} %get-tuple-element.15.refs_0_), channel_id=1, source_target_pairs={{0,8},{1,9},{2,10},{3,11},{4,12},{5,13},{6,14},{7,15},{8,16},{9,17... | collective-permute-start | bytes 196616 | tf_op jit(solution)/shard_map/ppermute | solution.py:98
  45.2 1.3 collective-permute-start.24
  46.5 1.1 collective-permute-start.25
  47.6 2.9 %collective-permute-done.23.refs_1_ = bf16[16,2048]{1,0:T(8,128)(2,1)S(1)} collective-permute-done((bf16[16,2048]{1,0:T(8,128)(2,1)}, bf16[16,2048]{1,0:T(8,128)(2,1)S(1)}, u32[]{:S(2)}, u32[]{:S(2)}) %collective-permute-start.23) | collective-permute-done | bytes 65568 | tf_op jit(solution)/shard_map/ppermute | solution.py:98
  50.5 1.4 collective-permute-start.4
  51.9 2.1 %collective-permute-done.24.refs_2_ = bf16[16,2048]{1,0:T(8,128)(2,1)S(1)} collective-permute-done((bf16[16,2048]{1,0:T(8,128)(2,1)}, bf16[16,2048]{1,0:T(8,128)(2,1)S(1)}, u32[]{:S(2)}, u32[]{:S(2)}) %collective-permute-start.24) | collective-permute-done | bytes 65568 | tf_op jit(solution)/shard_map/ppermute | solution.py:98
  54.0 7.8 %collective-permute-done.3.refs_2_ = bf16[4,16,2048]{2,1,0:T(8,128)(2,1)S(1)} collective-permute-done((bf16[4,16,2048]{2,1,0:T(8,128)(2,1)}, bf16[4,16,2048]{2,1,0:T(8,128)(2,1)S(1)}, u32[]{:S(2)}, u32[]{:S(2)}) %collective-permute-start.3) | collective-permute-done | bytes 262176 | tf_op jit(solution)/shard_map/ppermute | solution.py:98
  61.9 0.7 collective-permute-start.5
  62.6 1.3 collective-permute-start.14
  63.9 0.7 collective-permute-start.15
  64.7 0.5 collective-permute-start.8
  65.2 8.4 %collective-permute-done.5.refs_4_ = bf16[4,16,2048]{2,1,0:T(8,128)(2,1)} collective-permute-done((bf16[4,16,2048]{2,1,0:T(8,128)(2,1)S(1)}, bf16[4,16,2048]{2,1,0:T(8,128)(2,1)}, u32[]{:S(2)}, u32[]{:S(2)}) %collective-permute-start.5) | collective-permute-done | bytes 262176 | tf_op jit(solution)/shard_map/ppermute | solution.py:98
  73.6 1.9 copy.18
  75.6 3.0 %reshape.36.refs_0_ = bf16[8,144,512]{2,1,0:T(8,128)(2,1)S(1)} reshape(bf16[2,4,12,6,2,512]{5,4,3,2,1,0:T(2,128)(2,1)} %bitcast.34) | data formatting | bytes 2359296 | tf_op jit(solution)/shard_map/reshape | solution.py:288
  78.8 1.7 shard_map.105.refs_1_
  80.4 0.5 collective-permute-start.16
  81.0 0.6 collective-permute-start.17
  81.6 7.0 %collective-permute-done.15.refs_4_ = bf16[4,16,4096]{2,1,0:T(8,128)(2,1)} collective-permute-done((bf16[4,16,4096]{2,1,0:T(8,128)(2,1)S(1)}, bf16[4,16,4096]{2,1,0:T(8,128)(2,1)}, u32[]{:S(2)}, u32[]{:S(2)}) %collective-permute-start.15) | collective-permute-done | bytes 524320 | tf_op jit(solution)/shard_map/ppermute | solution.py:98
  88.7 0.9 copy-done.5
  89.6 0.9 copy-done.7
  90.6 1.1 copy-done.10
  91.7 16.5 %shard_map.102 = bf16[8,144,512]{2,1,0:T(8,128)(2,1)S(1)} custom-call(bf16[8,144,512]{2,1,0:T(8,128)(2,1)S(1)} %reshape.36.refs_0_, bf16[4,16,2048]{2,1,0:T(8,128)(2,1)S(1)} %copy-done.3, bf16[4,16,2048]{2,1,0:T(8,128)(2,1)S(1)} %copy-done.5, bf16[4,16,2048]{2,1,0:T(8,128)(2,1)} %collective-permute-done.4.refs_3_, ...), custom_call_target="tpu_custom_call" | custom-call | flops 8000000000 | bytes 6000000 | tf_op jit(solution)/shard_map/pallas_call | solution.py:219
  108.3 2.0 %collective-permute-start.28 = (bf16[4,16,2048]{2,1,0:T(8,128)(2,1)}, bf16[4,16,2048]{2,1,0:T(8,128)(2,1)}, u32[]{:S(2)}, u32[]{:S(2)}) collective-permute-start(bf16[4,16,2048]{2,1,0:T(8,128)(2,1)} %collective-permute-done.26.refs_2_), channel_id=1, source_target_pairs={{0,4},{1,3},{2,6},{3,1},{4,0},{5,7},{6,2},{7,5},{8,12},{9,11},{10,... | collective-permute-start | bytes 786440 | tf_op jit(solution)/shard_map/ppermute | solution.py:98
  110.3 13.8 %shard_map.104 = bf16[1152,512]{1,0:T(8,128)(2,1)S(1)} custom-call(bf16[1152,512]{1,0:T(8,128)(2,1)S(1)} %bitcast.26, bf16[4,16,4096]{2,1,0:T(8,128)(2,1)S(1)} %copy-done.2, bf16[4,16,4096]{2,1,0:T(8,128)(2,1)S(1)} %collective-permute-done.13.refs_2_, bf16[4,16,4096]{2,1,0:T(8,128)(2,1)S(1)} %collective-permute-done.14.refs_3_, ...), custom_call_target="tpu_custom_call" | custom-call | flops 4831838208 | bytes 8000000 | tf_op jit(solution)/shard_map/pallas_call | solution.py:266
  124.1 0.5 reshape_reshape.6
  124.6 1.2 copy.14
  126.0 3.6 %collective-permute-start.20 = (bf16[6,21,2,512]{3,2,1,0:T(2,128)(2,1)S(1)}, bf16[6,21,2,512]{3,2,1,0:T(2,128)(2,1)S(1)}, u32[]{:S(2)}, u32[]{:S(2)}) collective-permute-start(bf16[6,21,2,512]{3,2,1,0:T(2,128)(2,1)S(1)} %slice.67), channel_id=1, source_target_pairs={{2,0},{3,1},{4,2},{5,3},{6,4},{7,5},{8,6},{9,7},{10,8},{11,9},{12,... | collective-permute-start | bytes 774152 | tf_op jit(solution)/shard_map/ppermute | solution.py:304
  129.8 1.9 collective-permute-start.22
  131.9 0.5 slice.66
  132.5 0.5 collective-permute-start.30
  133.0 3.0 %collective-permute-done.22 = bf16[6,3,2,512]{3,2,1,0:T(2,128)(2,1)S(1)} collective-permute-done((bf16[6,3,2,512]{3,2,1,0:T(2,128)(2,1)S(1)}, bf16[6,3,2,512]{3,2,1,0:T(2,128)(2,1)S(1)}, u32[]{:S(2)}, u32[]{:S(2)}) %collective-permute-start.22) | collective-permute-done | bytes 36896 | tf_op jit(solution)/shard_map/ppermute | solution.py:304
  136.0 0.5 collective-permute-start.32
  136.5 1.7 maximum_maximum_fusion
  138.2 1.9 copy.15
  140.2 3.0 %reshape.40.refs_0_ = bf16[8,144,512]{2,1,0:T(8,128)(2,1)S(1)} reshape(bf16[2,4,12,6,2,512]{5,4,3,2,1,0:T(2,128)(2,1)} %copy.15) | data formatting | bytes 2359296 | tf_op jit(solution)/shard_map/reshape | solution.py:288
  143.2 1.1 copy-done.11
  144.3 16.7 %shard_map.106 = bf16[8,144,512]{2,1,0:T(8,128)(2,1)S(1)} custom-call(bf16[8,144,512]{2,1,0:T(8,128)(2,1)S(1)} %reshape.40.refs_0_, bf16[4,16,2048]{2,1,0:T(8,128)(2,1)S(1)} %copy-done, bf16[4,16,2048]{2,1,0:T(8,128)(2,1)} %collective-permute-done.26.refs_2_, bf16[4,16,2048]{2,1,0:T(8,128)(2,1)S(1)} %collective-permute-done.27.refs_3_, ...), custom_call_target="tpu_custom_call" | custom-call | flops 8000000000 | bytes 6000000 | tf_op jit(solution)/shard_map/pallas_call | solution.py:219
  160.9 1.0 copy-done.8
  162.0 2.2 %copy-done.1 = bf16[512,4096]{1,0:T(8,128)(2,1)S(1)} copy-done((bf16[512,4096]{1,0:T(8,128)(2,1)S(1)}, bf16[512,4096]{1,0:T(8,128)(2,1)}, u32[]{:S(2)}) %copy-start.1) | copy-done | bytes 4194328
  164.1 1.3 copy-done.9
  165.4 8.4 %shard_map.107 = bf16[1152,512]{1,0:T(8,128)(2,1)S(1)} custom-call(bf16[1152,512]{1,0:T(8,128)(2,1)S(1)} %bitcast.27, bf16[512,4096]{1,0:T(8,128)(2,1)S(1)} %copy-done.1, f32[1,512]{1,0:T(1,128)S(1)} %get-tuple-element.17.refs_2_), custom_call_target="tpu_custom_call" | custom-call | flops 4831838208 | bytes 8000000 | tf_op jit(solution)/shard_map/pallas_call | solution.py:266
  173.8 0.5 reshape_reshape.7
  174.3 1.2 copy.16
  176.0 0.5 collective-permute-start.33
  176.5 0.5 slice.73
  177.0 11.5 %collective-permute-done.33 = bf16[6,3,2,512]{3,2,1,0:T(2,128)(2,1)S(1)} collective-permute-done((bf16[6,3,2,512]{3,2,1,0:T(2,128)(2,1)S(1)}, bf16[6,3,2,512]{3,2,1,0:T(2,128)(2,1)S(1)}, u32[]{:S(2)}, u32[]{:S(2)}) %collective-permute-start.33) | collective-permute-done | bytes 36896 | tf_op jit(solution)/shard_map/ppermute | solution.py:304
  188.5 2.5 %maximum_maximum_fusion.1 = bf16[24,24,2,512]{3,2,1,0:T(2,128)(2,1)} fusion(bf16[18,21,2,512]{3,2,1,0:T(2,128)(2,1)S(1)} %slice.73, bf16[6,21,2,512]{3,2,1,0:T(2,128)(2,1)S(1)} %collective-permute-done.35, bf16[18,3,2,512]{3,2,1,0:T(2,128)(2,1)S(1)} %collective-permute-done.34, bf16[6,3,2,512]{3,2,1,0:T(2,128)(2,1)S(1)} %collective-permute-done.33), kind=kLoop, calls=%fused_computation.1 | loop fusion | flops 1769472 | bytes 2359296 | tf_op jit(solution)/shard_map/concatenate | solution.py:326
  (94 shorter events, 2.3 us)
Async XLA Ops:
  6.5 58.1 %copy-start.24 = (f32[2,16]{1,0:T(2,128)S(1)}, f32[2,16]{1,0:T(2,128)}, u32[]{:S(2)}) copy-start(f32[2,16]{1,0:T(2,128)} %param.16) | copy-start | bytes 388
  6.5 67.0 %copy-start.13 = (bf16[24,24,2,512]{3,2,1,0:T(2,128)(2,1)S(1)}, bf16[24,24,2,512]{3,2,1,0:T(2,128)(2,1)}, u32[]{:S(2)}) copy-start(bf16[24,24,2,512]{3,2,1,0:T(2,128)(2,1)} %param.10) | copy-start | bytes 3538948
  6.5 155.4 %all-gather.2.cloned.1.call-start = ((), (), s32[]{:S(2)}) async-start(), calls=%async_computation | async-start | bytes 4325376 | tf_op jit(solution)/shard_map/all_gather | solution.py:342
  8.5 7.8 %collective-permute-start = (bf16[16,2048]{1,0:T(8,128)(2,1)}, bf16[16,2048]{1,0:T(8,128)(2,1)S(1)}, u32[]{:S(2)}, u32[]{:S(2)}) collective-permute-start(bf16[16,2048]{1,0:T(8,128)(2,1)} %get-tuple-element.11.refs_0_), channel_id=1, source_target_pairs={{0,8},{1,9},{2,10},{3,11},{4,12},{5,13},{6,14},{7,15},{8,16},{9,17... | collective-permute-start | bytes 196616 | tf_op jit(solution)/shard_map/ppermute | solution.py:98
  11.6 7.3 %collective-permute-start.1 = (bf16[16,2048]{1,0:T(8,128)(2,1)}, bf16[16,2048]{1,0:T(8,128)(2,1)S(1)}, u32[]{:S(2)}, u32[]{:S(2)}) collective-permute-start(bf16[16,2048]{1,0:T(8,128)(2,1)} %get-tuple-element.11.refs_0_), channel_id=1, source_target_pairs={{0,16},{1,17},{2,18},{3,19},{4,20},{5,21},{6,22},{7,23},{8,24},{9,... | collective-permute-start | bytes 196616 | tf_op jit(solution)/shard_map/ppermute | solution.py:98
  14.2 4.9 %collective-permute-start.2 = (bf16[16,2048]{1,0:T(8,128)(2,1)}, bf16[16,2048]{1,0:T(8,128)(2,1)S(1)}, u32[]{:S(2)}, u32[]{:S(2)}) collective-permute-start(bf16[16,2048]{1,0:T(8,128)(2,1)} %get-tuple-element.11.refs_0_), channel_id=1, source_target_pairs={{0,24},{1,25},{2,26},{3,27},{4,28},{5,29},{6,30},{7,31},{8,0},{9,1... | collective-permute-start | bytes 196616 | tf_op jit(solution)/shard_map/ppermute | solution.py:98
  16.4 2.8 %copy-start.17 = (bf16[16,2048]{1,0:T(8,128)(2,1)}, bf16[16,2048]{1,0:T(8,128)(2,1)S(1)}, u32[]{:S(2)}) copy-start(bf16[16,2048]{1,0:T(8,128)(2,1)S(1)} %collective-permute-done.refs_1_) | copy-start | bytes 196612
  18.9 0.6 copy-start.18
  19.5 0.6 copy-start.19
  22.1 9.4 %collective-permute-start.10 = (bf16[16,4096]{1,0:T(8,128)(2,1)}, bf16[16,4096]{1,0:T(8,128)(2,1)S(1)}, u32[]{:S(2)}, u32[]{:S(2)}) collective-permute-start(bf16[16,4096]{1,0:T(8,128)(2,1)} %get-tuple-element.13.refs_0_), channel_id=1, source_target_pairs={{0,8},{1,9},{2,10},{3,11},{4,12},{5,13},{6,14},{7,15},{8,16},{9,17... | collective-permute-start | bytes 393224 | tf_op jit(solution)/shard_map/ppermute | solution.py:98
  23.3 14.1 %collective-permute-start.11 = (bf16[16,4096]{1,0:T(8,128)(2,1)}, bf16[16,4096]{1,0:T(8,128)(2,1)S(1)}, u32[]{:S(2)}, u32[]{:S(2)}) collective-permute-start(bf16[16,4096]{1,0:T(8,128)(2,1)} %get-tuple-element.13.refs_0_), channel_id=1, source_target_pairs={{0,16},{1,17},{2,18},{3,19},{4,20},{5,21},{6,22},{7,23},{8,24},{9,... | collective-permute-start | bytes 393224 | tf_op jit(solution)/shard_map/ppermute | solution.py:98
  25.9 11.5 %collective-permute-start.12 = (bf16[16,4096]{1,0:T(8,128)(2,1)}, bf16[16,4096]{1,0:T(8,128)(2,1)S(1)}, u32[]{:S(2)}, u32[]{:S(2)}) collective-permute-start(bf16[16,4096]{1,0:T(8,128)(2,1)} %get-tuple-element.13.refs_0_), channel_id=1, source_target_pairs={{0,24},{1,25},{2,26},{3,27},{4,28},{5,29},{6,30},{7,31},{8,0},{9,1... | collective-permute-start | bytes 393224 | tf_op jit(solution)/shard_map/ppermute | solution.py:98
  31.5 6.0 %copy-start.14 = (bf16[16,4096]{1,0:T(8,128)(2,1)}, bf16[16,4096]{1,0:T(8,128)(2,1)S(1)}, u32[]{:S(2)}) copy-start(bf16[16,4096]{1,0:T(8,128)(2,1)S(1)} %collective-permute-done.10.refs_1_) | copy-start | bytes 393220
  37.4 0.7 copy-start.15
  38.1 0.7 copy-start.16
  40.8 23.1 %collective-permute-start.13 = (bf16[4,16,4096]{2,1,0:T(8,128)(2,1)}, bf16[4,16,4096]{2,1,0:T(8,128)(2,1)S(1)}, u32[]{:S(2)}, u32[]{:S(2)}) collective-permute-start(bf16[4,16,4096]{2,1,0:T(8,128)(2,1)} %get-tuple-element.14.refs_1_), channel_id=1, source_target_pairs={{0,2},{1,5},{2,0},{3,7},{4,6},{5,1},{6,4},{7,3},{8,10},{9,13},{10,... | collective-permute-start | bytes 1572872 | tf_op jit(solution)/shard_map/ppermute | solution.py:98
  41.8 20.1 %collective-permute-start.3 = (bf16[4,16,2048]{2,1,0:T(8,128)(2,1)}, bf16[4,16,2048]{2,1,0:T(8,128)(2,1)S(1)}, u32[]{:S(2)}, u32[]{:S(2)}) collective-permute-start(bf16[4,16,2048]{2,1,0:T(8,128)(2,1)} %get-tuple-element.12.refs_1_), channel_id=1, source_target_pairs={{0,2},{1,5},{2,0},{3,7},{4,6},{5,1},{6,4},{7,3},{8,10},{9,13},{10,... | collective-permute-start | bytes 786440 | tf_op jit(solution)/shard_map/ppermute | solution.py:98
  42.8 7.7 %collective-permute-start.23 = (bf16[16,2048]{1,0:T(8,128)(2,1)}, bf16[16,2048]{1,0:T(8,128)(2,1)S(1)}, u32[]{:S(2)}, u32[]{:S(2)}) collective-permute-start(bf16[16,2048]{1,0:T(8,128)(2,1)} %get-tuple-element.15.refs_0_), channel_id=1, source_target_pairs={{0,8},{1,9},{2,10},{3,11},{4,12},{5,13},{6,14},{7,15},{8,16},{9,17... | collective-permute-start | bytes 196616 | tf_op jit(solution)/shard_map/ppermute | solution.py:98
  45.2 8.8 %collective-permute-start.24 = (bf16[16,2048]{1,0:T(8,128)(2,1)}, bf16[16,2048]{1,0:T(8,128)(2,1)S(1)}, u32[]{:S(2)}, u32[]{:S(2)}) collective-permute-start(bf16[16,2048]{1,0:T(8,128)(2,1)} %get-tuple-element.15.refs_0_), channel_id=1, source_target_pairs={{0,16},{1,17},{2,18},{3,19},{4,20},{5,21},{6,22},{7,23},{8,24},{9,... | collective-permute-start | bytes 196616 | tf_op jit(solution)/shard_map/ppermute | solution.py:98
  46.5 16.1 %collective-permute-start.25 = (bf16[16,2048]{1,0:T(8,128)(2,1)}, bf16[16,2048]{1,0:T(8,128)(2,1)S(1)}, u32[]{:S(2)}, u32[]{:S(2)}) collective-permute-start(bf16[16,2048]{1,0:T(8,128)(2,1)} %get-tuple-element.15.refs_0_), channel_id=1, source_target_pairs={{0,24},{1,25},{2,26},{3,27},{4,28},{5,29},{6,30},{7,31},{8,0},{9,1... | collective-permute-start | bytes 196616 | tf_op jit(solution)/shard_map/ppermute | solution.py:98
  50.5 25.0 %copy-start.20 = (bf16[16,2048]{1,0:T(8,128)(2,1)}, bf16[16,2048]{1,0:T(8,128)(2,1)S(1)}, u32[]{:S(2)}) copy-start(bf16[16,2048]{1,0:T(8,128)(2,1)S(1)} %collective-permute-done.23.refs_1_) | copy-start | bytes 196612
  50.5 14.1 %collective-permute-start.4 = (bf16[4,16,2048]{2,1,0:T(8,128)(2,1)}, bf16[4,16,2048]{2,1,0:T(8,128)(2,1)}, u32[]{:S(2)}, u32[]{:S(2)}) collective-permute-start(bf16[4,16,2048]{2,1,0:T(8,128)(2,1)} %get-tuple-element.12.refs_1_), channel_id=1, source_target_pairs={{0,4},{1,3},{2,6},{3,1},{4,0},{5,7},{6,2},{7,5},{8,12},{9,11},{10,... | collective-permute-start | bytes 786440 | tf_op jit(solution)/shard_map/ppermute | solution.py:98
  54.0 21.5 %copy-start.21 = (bf16[16,2048]{1,0:T(8,128)(2,1)}, bf16[16,2048]{1,0:T(8,128)(2,1)S(1)}, u32[]{:S(2)}) copy-start(bf16[16,2048]{1,0:T(8,128)(2,1)S(1)} %collective-permute-done.24.refs_2_) | copy-start | bytes 196612
  54.0 10.7 %collective-permute-start.6 = (bf16[4,16,2048]{2,1,0:T(8,128)(2,1)}, bf16[4,16,2048]{2,1,0:T(8,128)(2,1)S(1)}, u32[]{:S(2)}, u32[]{:S(2)}) collective-permute-start(bf16[4,16,2048]{2,1,0:T(8,128)(2,1)} %get-tuple-element.12.refs_1_), channel_id=1, source_target_pairs={{0,1},{1,0},{2,3},{3,2},{4,5},{5,4},{6,7},{7,6},{8,9},{9,8},{10,11... | collective-permute-start | bytes 786440 | tf_op jit(solution)/shard_map/ppermute | solution.py:98
  61.8 13.7 %copy-start.4 = (bf16[4,16,2048]{2,1,0:T(8,128)(2,1)}, bf16[4,16,2048]{2,1,0:T(8,128)(2,1)S(1)}, u32[]{:S(2)}) copy-start(bf16[4,16,2048]{2,1,0:T(8,128)(2,1)S(1)} %collective-permute-done.3.refs_2_) | copy-start | bytes 786436
  61.9 11.7 %collective-permute-start.5 = (bf16[4,16,2048]{2,1,0:T(8,128)(2,1)S(1)}, bf16[4,16,2048]{2,1,0:T(8,128)(2,1)}, u32[]{:S(2)}, u32[]{:S(2)}) collective-permute-start(bf16[4,16,2048]{2,1,0:T(8,128)(2,1)S(1)} %collective-permute-done.3.refs_2_), channel_id=1, source_target_pairs={{0,4},{1,3},{2,6},{3,1},{4,0},{5,7},{6,2},{7,5},{8,12},{9,11},{10,... | collective-permute-start | bytes 786440 | tf_op jit(solution)/shard_map/ppermute | solution.py:98
  62.6 12.9 %copy-start.22 = (bf16[16,2048]{1,0:T(8,128)(2,1)}, bf16[16,2048]{1,0:T(8,128)(2,1)S(1)}, u32[]{:S(2)}) copy-start(bf16[16,2048]{1,0:T(8,128)(2,1)S(1)} %collective-permute-done.25.refs_3_) | copy-start | bytes 196612
  62.6 18.4 %collective-permute-start.14 = (bf16[4,16,4096]{2,1,0:T(8,128)(2,1)}, bf16[4,16,4096]{2,1,0:T(8,128)(2,1)S(1)}, u32[]{:S(2)}, u32[]{:S(2)}) collective-permute-start(bf16[4,16,4096]{2,1,0:T(8,128)(2,1)} %get-tuple-element.14.refs_1_), channel_id=1, source_target_pairs={{0,4},{1,3},{2,6},{3,1},{4,0},{5,7},{6,2},{7,5},{8,12},{9,11},{10,... | collective-permute-start | bytes 1572872 | tf_op jit(solution)/shard_map/ppermute | solution.py:98
  63.9 24.8 %collective-permute-start.15 = (bf16[4,16,4096]{2,1,0:T(8,128)(2,1)S(1)}, bf16[4,16,4096]{2,1,0:T(8,128)(2,1)}, u32[]{:S(2)}, u32[]{:S(2)}) collective-permute-start(bf16[4,16,4096]{2,1,0:T(8,128)(2,1)S(1)} %collective-permute-done.13.refs_2_), channel_id=1, source_target_pairs={{0,4},{1,3},{2,6},{3,1},{4,0},{5,7},{6,2},{7,5},{8,12},{9,11},{10,... | collective-permute-start | bytes 1572872 | tf_op jit(solution)/shard_map/ppermute | solution.py:98
  64.6 15.8 %collective-permute-start.7 = (bf16[4,16,2048]{2,1,0:T(8,128)(2,1)S(1)}, bf16[4,16,2048]{2,1,0:T(8,128)(2,1)}, u32[]{:S(2)}, u32[]{:S(2)}) collective-permute-start(bf16[4,16,2048]{2,1,0:T(8,128)(2,1)S(1)} %collective-permute-done.3.refs_2_), channel_id=1, source_target_pairs={{0,1},{1,0},{2,3},{3,2},{4,5},{5,4},{6,7},{7,6},{8,9},{9,8},{10,11... | collective-permute-start | bytes 786440 | tf_op jit(solution)/shard_map/ppermute | solution.py:98
  64.7 10.8 %copy-start.6 = (bf16[4,16,2048]{2,1,0:T(8,128)(2,1)}, bf16[4,16,2048]{2,1,0:T(8,128)(2,1)S(1)}, u32[]{:S(2)}) copy-start(bf16[4,16,2048]{2,1,0:T(8,128)(2,1)S(1)} %collective-permute-done.6.refs_5_) | copy-start | bytes 786436
  64.7 16.2 %collective-permute-start.8 = (bf16[4,16,2048]{2,1,0:T(8,128)(2,1)}, bf16[4,16,2048]{2,1,0:T(8,128)(2,1)}, u32[]{:S(2)}, u32[]{:S(2)}) collective-permute-start(bf16[4,16,2048]{2,1,0:T(8,128)(2,1)} %collective-permute-done.4.refs_3_), channel_id=1, source_target_pairs={{0,1},{1,0},{2,3},{3,2},{4,5},{5,4},{6,7},{7,6},{8,9},{9,8},{10,11... | collective-permute-start | bytes 786440 | tf_op jit(solution)/shard_map/ppermute | solution.py:98
  73.6 8.0 %collective-permute-start.9 = (bf16[4,16,2048]{2,1,0:T(8,128)(2,1)}, bf16[4,16,2048]{2,1,0:T(8,128)(2,1)}, u32[]{:S(2)}, u32[]{:S(2)}) collective-permute-start(bf16[4,16,2048]{2,1,0:T(8,128)(2,1)} %collective-permute-done.5.refs_4_), channel_id=1, source_target_pairs={{0,1},{1,0},{2,3},{3,2},{4,5},{5,4},{6,7},{7,6},{8,9},{9,8},{10,11... | collective-permute-start | bytes 786440 | tf_op jit(solution)/shard_map/ppermute | solution.py:98
  75.5 3.2 %copy-start.23 = (f32[2,2,512]{2,1,0:T(2,128)S(1)}, f32[2,2,512]{2,1,0:T(2,128)}, u32[]{:S(2)}) copy-start(f32[2,2,512]{2,1,0:T(2,128)} %param.15) | copy-start | bytes 24580
  75.5 4.9 %copy-start.2 = (bf16[4,16,4096]{2,1,0:T(8,128)(2,1)S(1)}, bf16[4,16,4096]{2,1,0:T(8,128)(2,1)}, u32[]{:S(2)}) copy-start(bf16[4,16,4096]{2,1,0:T(8,128)(2,1)} %get-tuple-element.14.refs_1_) | copy-start | bytes 1572868
  75.6 13.1 %copy-start.3 = (bf16[4,16,2048]{2,1,0:T(8,128)(2,1)S(1)}, bf16[4,16,2048]{2,1,0:T(8,128)(2,1)}, u32[]{:S(2)}) copy-start(bf16[4,16,2048]{2,1,0:T(8,128)(2,1)} %get-tuple-element.12.refs_1_) | copy-start | bytes 786436
  80.4 27.8 %collective-permute-start.16 = (bf16[4,16,4096]{2,1,0:T(8,128)(2,1)S(1)}, bf16[4,16,4096]{2,1,0:T(8,128)(2,1)S(1)}, u32[]{:S(2)}, u32[]{:S(2)}) collective-permute-start(bf16[4,16,4096]{2,1,0:T(8,128)(2,1)S(1)} %copy-done.2), channel_id=1, source_target_pairs={{0,1},{1,0},{2,3},{3,2},{4,5},{5,4},{6,7},{7,6},{8,9},{9,8},{10,11... | collective-permute-start | bytes 1572872 | tf_op jit(solution)/shard_map/ppermute | solution.py:98
  81.0 27.2 %collective-permute-start.26 = (bf16[4,16,2048]{2,1,0:T(8,128)(2,1)}, bf16[4,16,2048]{2,1,0:T(8,128)(2,1)}, u32[]{:S(2)}, u32[]{:S(2)}) collective-permute-start(bf16[4,16,2048]{2,1,0:T(8,128)(2,1)} %shard_map.105.refs_1_), channel_id=1, source_target_pairs={{0,2},{1,5},{2,0},{3,7},{4,6},{5,1},{6,4},{7,3},{8,10},{9,13},{10,... | collective-permute-start | bytes 786440 | tf_op jit(solution)/shard_map/ppermute | solution.py:98
  81.0 29.3 %collective-permute-start.17 = (bf16[4,16,4096]{2,1,0:T(8,128)(2,1)S(1)}, bf16[4,16,4096]{2,1,0:T(8,128)(2,1)S(1)}, u32[]{:S(2)}, u32[]{:S(2)}) collective-permute-start(bf16[4,16,4096]{2,1,0:T(8,128)(2,1)S(1)} %collective-permute-done.13.refs_2_), channel_id=1, source_target_pairs={{0,1},{1,0},{2,3},{3,2},{4,5},{5,4},{6,7},{7,6},{8,9},{9,8},{10,11... | collective-permute-start | bytes 1572872 | tf_op jit(solution)/shard_map/ppermute | solution.py:98
  81.6 28.7 %collective-permute-start.18 = (bf16[4,16,4096]{2,1,0:T(8,128)(2,1)S(1)}, bf16[4,16,4096]{2,1,0:T(8,128)(2,1)S(1)}, u32[]{:S(2)}, u32[]{:S(2)}) collective-permute-start(bf16[4,16,4096]{2,1,0:T(8,128)(2,1)S(1)} %collective-permute-done.14.refs_3_), channel_id=1, source_target_pairs={{0,1},{1,0},{2,3},{3,2},{4,5},{5,4},{6,7},{7,6},{8,9},{9,8},{10,11... | collective-permute-start | bytes 1572872 | tf_op jit(solution)/shard_map/ppermute | solution.py:98
  88.7 21.6 %collective-permute-start.19 = (bf16[4,16,4096]{2,1,0:T(8,128)(2,1)}, bf16[4,16,4096]{2,1,0:T(8,128)(2,1)S(1)}, u32[]{:S(2)}, u32[]{:S(2)}) collective-permute-start(bf16[4,16,4096]{2,1,0:T(8,128)(2,1)} %collective-permute-done.15.refs_4_), channel_id=1, source_target_pairs={{0,1},{1,0},{2,3},{3,2},{4,5},{5,4},{6,7},{7,6},{8,9},{9,8},{10,11... | collective-permute-start | bytes 1572872 | tf_op jit(solution)/shard_map/ppermute | solution.py:98
  88.7 1.0 copy-start.5
  89.6 0.9 copy-start.7
  90.6 1.1 copy-start.10
  91.7 16.5 %copy-start = (bf16[4,16,2048]{2,1,0:T(8,128)(2,1)S(1)}, bf16[4,16,2048]{2,1,0:T(8,128)(2,1)}, u32[]{:S(2)}) copy-start(bf16[4,16,2048]{2,1,0:T(8,128)(2,1)} %shard_map.105.refs_1_) | copy-start | bytes 786436
  108.2 24.2 %collective-permute-start.27 = (bf16[4,16,2048]{2,1,0:T(8,128)(2,1)S(1)}, bf16[4,16,2048]{2,1,0:T(8,128)(2,1)S(1)}, u32[]{:S(2)}, u32[]{:S(2)}) collective-permute-start(bf16[4,16,2048]{2,1,0:T(8,128)(2,1)S(1)} %copy-done), channel_id=1, source_target_pairs={{0,4},{1,3},{2,6},{3,1},{4,0},{5,7},{6,2},{7,5},{8,12},{9,11},{10,... | collective-permute-start | bytes 786440 | tf_op jit(solution)/shard_map/ppermute | solution.py:98
  108.3 24.2 %collective-permute-start.28 = (bf16[4,16,2048]{2,1,0:T(8,128)(2,1)}, bf16[4,16,2048]{2,1,0:T(8,128)(2,1)}, u32[]{:S(2)}, u32[]{:S(2)}) collective-permute-start(bf16[4,16,2048]{2,1,0:T(8,128)(2,1)} %collective-permute-done.26.refs_2_), channel_id=1, source_target_pairs={{0,4},{1,3},{2,6},{3,1},{4,0},{5,7},{6,2},{7,5},{8,12},{9,11},{10,... | collective-permute-start | bytes 786440 | tf_op jit(solution)/shard_map/ppermute | solution.py:98
  126.0 10.5 %collective-permute-start.20 = (bf16[6,21,2,512]{3,2,1,0:T(2,128)(2,1)S(1)}, bf16[6,21,2,512]{3,2,1,0:T(2,128)(2,1)S(1)}, u32[]{:S(2)}, u32[]{:S(2)}) collective-permute-start(bf16[6,21,2,512]{3,2,1,0:T(2,128)(2,1)S(1)} %slice.67), channel_id=1, source_target_pairs={{2,0},{3,1},{4,2},{5,3},{6,4},{7,5},{8,6},{9,7},{10,8},{11,9},{12,... | collective-permute-start | bytes 774152 | tf_op jit(solution)/shard_map/ppermute | solution.py:304
  129.7 6.3 %collective-permute-start.21 = (bf16[18,3,2,512]{3,2,1,0:T(2,128)(2,1)S(1)}, bf16[18,3,2,512]{3,2,1,0:T(2,128)(2,1)S(1)}, u32[]{:S(2)}, u32[]{:S(2)}) collective-permute-start(bf16[18,3,2,512]{3,2,1,0:T(2,128)(2,1)S(1)} %slice.68), channel_id=1, source_target_pairs={{1,0},{0,1},{3,2},{2,3},{5,4},{4,5},{7,6},{6,7},{9,8},{8,9},{11,10... | collective-permute-start | bytes 331784 | tf_op jit(solution)/shard_map/ppermute | solution.py:304
  129.8 6.2 %collective-permute-start.22 = (bf16[6,3,2,512]{3,2,1,0:T(2,128)(2,1)S(1)}, bf16[6,3,2,512]{3,2,1,0:T(2,128)(2,1)S(1)}, u32[]{:S(2)}, u32[]{:S(2)}) collective-permute-start(bf16[6,3,2,512]{3,2,1,0:T(2,128)(2,1)S(1)} %slice.69), channel_id=1, source_target_pairs={{3,0},{2,1},{5,2},{4,3},{7,4},{6,5},{9,6},{8,7},{11,8},{10,9},{13,... | collective-permute-start | bytes 110600 | tf_op jit(solution)/shard_map/ppermute | solution.py:304
  132.4 10.7 %collective-permute-start.29 = (bf16[4,16,2048]{2,1,0:T(8,128)(2,1)S(1)}, bf16[4,16,2048]{2,1,0:T(8,128)(2,1)S(1)}, u32[]{:S(2)}, u32[]{:S(2)}) collective-permute-start(bf16[4,16,2048]{2,1,0:T(8,128)(2,1)S(1)} %copy-done), channel_id=1, source_target_pairs={{0,1},{1,0},{2,3},{3,2},{4,5},{5,4},{6,7},{7,6},{8,9},{9,8},{10,11... | collective-permute-start | bytes 786440 | tf_op jit(solution)/shard_map/ppermute | solution.py:98
  132.5 10.7 %collective-permute-start.30 = (bf16[4,16,2048]{2,1,0:T(8,128)(2,1)}, bf16[4,16,2048]{2,1,0:T(8,128)(2,1)S(1)}, u32[]{:S(2)}, u32[]{:S(2)}) collective-permute-start(bf16[4,16,2048]{2,1,0:T(8,128)(2,1)} %collective-permute-done.26.refs_2_), channel_id=1, source_target_pairs={{0,1},{1,0},{2,3},{3,2},{4,5},{5,4},{6,7},{7,6},{8,9},{9,8},{10,11... | collective-permute-start | bytes 786440 | tf_op jit(solution)/shard_map/ppermute | solution.py:98
  136.0 7.2 %collective-permute-start.31 = (bf16[4,16,2048]{2,1,0:T(8,128)(2,1)S(1)}, bf16[4,16,2048]{2,1,0:T(8,128)(2,1)S(1)}, u32[]{:S(2)}, u32[]{:S(2)}) collective-permute-start(bf16[4,16,2048]{2,1,0:T(8,128)(2,1)S(1)} %collective-permute-done.27.refs_3_), channel_id=1, source_target_pairs={{0,1},{1,0},{2,3},{3,2},{4,5},{5,4},{6,7},{7,6},{8,9},{9,8},{10,11... | collective-permute-start | bytes 786440 | tf_op jit(solution)/shard_map/ppermute | solution.py:98
  136.0 7.2 %collective-permute-start.32 = (bf16[4,16,2048]{2,1,0:T(8,128)(2,1)}, bf16[4,16,2048]{2,1,0:T(8,128)(2,1)S(1)}, u32[]{:S(2)}, u32[]{:S(2)}) collective-permute-start(bf16[4,16,2048]{2,1,0:T(8,128)(2,1)} %collective-permute-done.28.refs_4_), channel_id=1, source_target_pairs={{0,1},{1,0},{2,3},{3,2},{4,5},{5,4},{6,7},{7,6},{8,9},{9,8},{10,11... | collective-permute-start | bytes 786440 | tf_op jit(solution)/shard_map/ppermute | solution.py:98
  140.1 3.0 %copy-start.12 = (f32[144,256]{1,0:T(8,128)S(1)}, f32[144,256]{1,0:T(8,128)}, u32[]{:S(2)}) copy-start(f32[144,256]{1,0:T(8,128)} %constant.7.clone.refs_12_) | copy-start | bytes 442372
  143.2 1.1 copy-start.11
  160.9 1.0 copy-start.8
  162.0 2.2 %copy-start.1 = (bf16[512,4096]{1,0:T(8,128)(2,1)S(1)}, bf16[512,4096]{1,0:T(8,128)(2,1)}, u32[]{:S(2)}) copy-start(bf16[512,4096]{1,0:T(8,128)(2,1)} %all-gather.2.cloned.1.call-done.refs_1_) | copy-start | bytes 12582916
  164.1 1.3 copy-start.9
  175.7 12.8 %collective-permute-start.35 = (bf16[6,21,2,512]{3,2,1,0:T(2,128)(2,1)S(1)}, bf16[6,21,2,512]{3,2,1,0:T(2,128)(2,1)S(1)}, u32[]{:S(2)}, u32[]{:S(2)}) collective-permute-start(bf16[6,21,2,512]{3,2,1,0:T(2,128)(2,1)S(1)} %slice.72), channel_id=1, source_target_pairs={{30,0},{31,1},{0,2},{1,3},{2,4},{3,5},{4,6},{5,7},{6,8},{7,9},{8,1... | collective-permute-start | bytes 774152 | tf_op jit(solution)/shard_map/ppermute | solution.py:304
  175.8 12.7 %collective-permute-start.34 = (bf16[18,3,2,512]{3,2,1,0:T(2,128)(2,1)S(1)}, bf16[18,3,2,512]{3,2,1,0:T(2,128)(2,1)S(1)}, u32[]{:S(2)}, u32[]{:S(2)}) collective-permute-start(bf16[18,3,2,512]{3,2,1,0:T(2,128)(2,1)S(1)} %slice.71), channel_id=1, source_target_pairs={{1,0},{0,1},{3,2},{2,3},{5,4},{4,5},{7,6},{6,7},{9,8},{8,9},{11,10... | collective-permute-start | bytes 331784 | tf_op jit(solution)/shard_map/ppermute | solution.py:304
  176.0 12.5 %collective-permute-start.33 = (bf16[6,3,2,512]{3,2,1,0:T(2,128)(2,1)S(1)}, bf16[6,3,2,512]{3,2,1,0:T(2,128)(2,1)S(1)}, u32[]{:S(2)}, u32[]{:S(2)}) collective-permute-start(bf16[6,3,2,512]{3,2,1,0:T(2,128)(2,1)S(1)} %slice.70), channel_id=1, source_target_pairs={{31,0},{30,1},{1,2},{0,3},{3,4},{2,5},{5,6},{4,7},{7,8},{6,9},{9,1... | collective-permute-start | bytes 110600 | tf_op jit(solution)/shard_map/ppermute | solution.py:304
Sparse Core Ops, SparseCore 0:
  10.2 75.2 all-gather.1

commit v5 on v4

v5 whole, which is shorter than its diff:
```python
import functools
import math

import numpy as np

import jax
import jax.numpy as jnp
from jax import lax
from jax.experimental import pallas as pl
from jax.experimental.pallas import tpu as pltpu
from jax.sharding import PartitionSpec as P

HEADS = 16
HEAD = 32
WLON = 12
WLAT = 6
LEVELS = 2
CELLS = WLON * WLAT * LEVELS
MAIN = 128
REST = CELLS - MAIN
QUARTER = CELLS // 4
GROUP = 8
WIDE = GROUP * HEAD
ANY = pl.BlockSpec(memory_space=pl.ANY)
NT = (((1,), (1,)), ((), ()))


def dot(a, b, dims=(((1,), (0,)), ((), ()))):
    return lax.dot_general(a, b, dims, preferred_element_type=jnp.float32)


def layer_norm(value, gain_row):
    averaged = jnp.mean(value, -1, keepdims=True)
    centred = value - averaged
    variance = jnp.mean(centred * centred, -1, keepdims=True)
    return centred * lax.rsqrt(variance + 1e-05) * gain_row


def relayed(rows, lat_size):
    return lat_size == 2 and rows % 32 == 0


def join_kernel(count, block, waits, *refs):
    pieces, sources, outs = refs[:count], refs[count:-2], refs[-2:]
    if not count:
        outs = (None, refs[-1])
        sources = refs[:-1]
    sources = sources[: len(sources) - waits]
    for index, piece in enumerate(pieces):
        outs[0][index] = piece[...]
    half = outs[1].shape[0]
    first = pl.multiple_of(lax.axis_index("lat") * half, 16)
    place = 0
    for source in sources:
        width = source.shape[2]
        outs[1][:, place : place + width] = source[block, pl.ds(first, half), :]
        place += width


def last_join_kernel(count, *refs):
    for index, piece in enumerate(refs[:count]):
        refs[-1][index] = piece[...]


def join(pieces, weights=(), block=0, after=()):
    count = len(pieces)
    column = [jax.ShapeDtypeStruct((count,) + piece.shape, jnp.bfloat16) for piece in pieces[:1]]
    held = [pl.BlockSpec(memory_space=pltpu.VMEM)] * (count + len(weights))
    specs = held + [ANY] * len(after)
    if not weights:
        kernel, out_shape = functools.partial(last_join_kernel, count), column
    else:
        kernel = functools.partial(join_kernel, count, block, len(after))
        width = sum(weight.shape[2] for weight in weights)
        chunk = jax.ShapeDtypeStruct((weights[0].shape[1] // 2, width), jnp.bfloat16)
        out_shape = column + [chunk]
    outs = pl.pallas_call(kernel, out_shape=out_shape, in_specs=specs)(*pieces, *weights, *after)
    outs = list(outs)
    return (outs + [None])[:2] if pieces else [None, outs[0]]


def send(block, move):
    pairs = []
    for lon in range(lax.axis_size("lon")):
        for core in range(2):
            z, y, x, core_to = move(lon // 4, lon // 2 % 2, lon % 2, core)
            pairs.append((lon * 2 + core, (z * 4 + y * 2 + x) * 2 + core_to))
    return lax.ppermute(block, ("lon", "lat"), pairs)


def along_z(own):
    depth = lax.axis_size("lon") // 4
    return [own] + [
        send(own, lambda z, y, x, c, step=step: ((z + step) % depth, y, x, c))
        for step in range(1, depth)
    ]


def one_way(z, y, x, c):
    return (z, y, 1 - x, c) if c == 0 else (z, 1 - y, x, c)


def other_way(z, y, x, c):
    return (z, 1 - y, x, c) if c == 0 else (z, y, 1 - x, c)


def swap(z, y, x, c):
    return z, y, x, 1 - c


def tied(array, after):
    return lax.optimization_barrier((array, after))[0]


def whole_pieces(column, beside, across, corner, after=()):
    own = [column, beside, across, corner]
    return own + [send(part, swap) for part in own[:-1]] + [send(tied(corner, after), swap)]


def load_pieces(pieces, w_ref, sem, first):
    if len(pieces) == 1:
        copy = pltpu.make_async_copy(pieces[0].at[:, pl.ds(first, w_ref.shape[1])], w_ref, sem)
        copy.start()
        copy.wait()
        return
    depth, half, _ = pieces[0].shape
    lon, lat = lax.axis_index("lon"), lax.axis_index("lat")
    z, y, x = lon // 4, lon // 2 % 2, lon % 2
    by_x, by_y = y * 2 + 1 - x, (1 - y) * 2 + x
    for index, piece in enumerate(pieces):
        core = lat if index < 4 else 1 - lat
        square = (
            y * 2 + x,
            jnp.where(core == 0, by_x, by_y),
            jnp.where(core == 0, by_y, by_x),
            (1 - y) * 2 + 1 - x,
        )[index % 4]
        for step in range(depth):
            shard = (z + depth - step) % depth * 4 + square
            row = pl.multiple_of((shard * 2 + core) * half, 16)
            pltpu.make_async_copy(piece.at[step], w_ref.at[pl.ds(row, half), :], sem).start()
    pltpu.make_async_copy(w_ref, w_ref, sem).wait()


def rolled_window(left_ref, right_ref, left_low, right_low, place, last):
    quarters = []
    for side, low in ((left_ref, left_low), (right_ref, right_low)):
        quarters.append(side[place, 1].astype(jnp.float32))
        following = side[jnp.minimum(place + 1, last), 0].astype(jnp.float32)
        quarters.append(jnp.where(place == last, low.astype(jnp.float32), following))
    return jnp.concatenate(quarters, 0).astype(jnp.bfloat16)


def attend_kernel(shifted, row_windows, count, lows, *refs):
    sources = 4 if shifted else 1
    x_refs, pieces = refs[:sources], refs[sources : sources + count]
    gain_ref, sharp_ref, ones_ref = refs[sources + count : sources + count + 3]
    allow_ref = refs[sources + count + 3] if shifted else None
    out_ref, w_ref, sem = refs[-3:]
    held, _, features = out_ref.shape

    @pl.when(pl.program_id(0) == 0)
    def _():
        load_pieces(pieces, w_ref, sem, 0)

    if shifted:
        left_ref, right_ref, left_low, right_low = x_refs
        tokens = jnp.concatenate(
            [
                rolled_window(
                    left_ref,
                    right_ref,
                    left_low[lows[0]],
                    right_low[lows[1]],
                    pl.program_id(0) * held + window,
                    row_windows - 1,
                )
                for window in range(held)
            ],
            0,
        )
    else:
        tokens = x_refs[0][...].reshape(held * CELLS, features)
    channel = lax.broadcasted_iota(jnp.int32, (WIDE, WIDE), 0) // HEAD
    same_head = jnp.where(
        channel == lax.broadcasted_iota(jnp.int32, (WIDE, WIDE), 1) // HEAD, 1.0, 0.0
    ).astype(jnp.bfloat16)
    lane_head = lax.broadcasted_iota(jnp.int32, (1, WIDE), 1) // HEAD
    masks = [jnp.where(lane_head == head, 1.0, 0.0).astype(jnp.bfloat16) for head in range(GROUP)]

    def units(part):
        rounded = part.astype(jnp.bfloat16)
        length2 = dot(rounded * rounded, same_head)
        return part * lax.rsqrt(jnp.maximum(length2, 0.25 * HEAD))

    attended = [[] for _ in range(held)]
    for group in range(HEADS // GROUP):
        lanes = [slice(n * features + group * WIDE, n * features + (group + 1) * WIDE) for n in range(3)]
        queries = (units(dot(tokens, w_ref[:, lanes[0]])) * sharp_ref[:, lanes[0]]).astype(jnp.bfloat16)
        keys = units(dot(tokens, w_ref[:, lanes[1]])).astype(jnp.bfloat16)
        values = dot(tokens, w_ref[:, lanes[2]]).astype(jnp.bfloat16)
        for window in range(held):
            own = slice(window * CELLS, (window + 1) * CELLS)
            query, key, value = queries[own], keys[own], values[own]
            stacked = jnp.concatenate([query * mask for mask in masks], 0)
            main = jnp.exp2(dot(stacked, key[:MAIN], NT)).astype(jnp.bfloat16)
            rest_keys = jnp.concatenate([key[MAIN:] * mask for mask in masks], 0)
            rest = jnp.exp2(dot(query, rest_keys, NT)).astype(jnp.bfloat16)
            parts = [main[head * CELLS : (head + 1) * CELLS] for head in range(GROUP)] + [rest]
            if shifted:
                last = jnp.logical_and(
                    (pl.program_id(0) * held + window) % row_windows == row_windows - 1,
                    lax.axis_index("lat") == lax.axis_size("lat") - 1,
                )
                allow = jnp.where(last, allow_ref[...], 1.0).astype(jnp.bfloat16)
                parts = [part * allow[:, :MAIN] for part in parts[:-1]] + [rest * allow[:, MAIN:]]
            weights = jnp.concatenate(parts, 1)
            stacked = jnp.concatenate(
                [value[:MAIN] * mask for mask in masks] + [value[MAIN:] * mask for mask in masks], 0
            )
            total = dot(weights, ones_ref[...])
            attended[window].append((dot(weights, stacked) / total).astype(jnp.bfloat16))
    attended = jnp.concatenate([jnp.concatenate(parts, 1) for parts in attended], 0)
    projected = dot(attended, w_ref[:, 3 * features :])
    middle = tokens.astype(jnp.float32) + layer_norm(projected, gain_ref[...])
    out_ref[...] = middle.astype(jnp.bfloat16).reshape(out_ref.shape)


def allowed_pairs():
    side = np.arange(CELLS) // QUARTER % 2
    rest = np.tile(side[MAIN:], GROUP)
    return (side[:, None] == np.concatenate([side[:MAIN], rest])[None, :]).astype(np.float32)


def head_columns():
    rows = np.concatenate([np.repeat(np.arange(GROUP), MAIN), np.repeat(np.arange(GROUP), REST)])
    return (rows[:, None] == np.arange(WIDE)[None, :] // HEAD).astype(np.float32)


def attend(sources, lows, pieces, gain, sharp, row_windows, after=(), held=2):
    shifted = len(sources) > 1
    features = sources[0].shape[-1]
    whole = lambda shape: pl.BlockSpec(shape, lambda i: (0,) * len(shape))
    block = pl.BlockSpec((held, CELLS, features), lambda i: (i, 0, 0))
    ones = jnp.asarray(head_columns(), jnp.bfloat16)
    extra = (jnp.asarray(allowed_pairs()),) if shifted else ()
    return pl.pallas_call(
        functools.partial(attend_kernel, shifted, row_windows, len(pieces), lows),
        grid=(row_windows // held,),
        out_shape=jax.ShapeDtypeStruct((row_windows, CELLS, features), jnp.bfloat16),
        in_specs=([whole(source.shape) for source in sources] if shifted else [block])
        + [ANY] * len(pieces)
        + [whole((1, features))] * 2
        + [whole(ones.shape)]
        + [whole(e.shape) for e in extra]
        + [ANY] * len(after),
        out_specs=block,
        scratch_shapes=[
            pltpu.VMEM((features, 4 * features), jnp.bfloat16),
            pltpu.SemaphoreType.DMA,
        ],
        compiler_params=pltpu.CompilerParams(vmem_limit_bytes=24 * 2**20),
        cost_estimate=pl.CostEstimate(
            flops=row_windows * 2_000_000_000, bytes_accessed=6_000_000, transcendentals=0
        ),
    )(*sources, *pieces, gain, sharp, ones, *extra, *after)


def feed_kernel(count, hidden_size, chunk, edge, *refs):
    x_ref, pieces, gain_ref = refs[0], refs[1 : 1 + count], refs[1 + count]
    left_ref, right_ref, edge_ref, w_ref, sem = refs[-5:]
    held, _, features = x_ref.shape

    @pl.when(pl.program_id(0) == 0)
    def _():
        load_pieces(pieces, w_ref, sem, 0)

    tokens = x_ref[...].reshape(held * CELLS, features)
    total = jnp.zeros(tokens.shape, jnp.float32)
    for start in range(0, hidden_size, chunk):
        grown = dot(tokens, w_ref[:, start : start + chunk])
        slope = math.sqrt(2.0 / math.pi)
        bent = jnp.tanh(grown * (grown * grown * (0.044715 * slope) + slope))
        hidden = (grown + grown * bent).astype(jnp.bfloat16)
        total = total + dot(
            hidden, w_ref[:, hidden_size + start : hidden_size + start + chunk], NT
        )
    result = tokens.astype(jnp.float32) + layer_norm(0.5 * total, gain_ref[...])
    edge_window, edge_half = edge
    for window in range(held):
        for side, target in enumerate((left_ref, right_ref)):
            for half in range(2):
                start = window * CELLS + (side * 2 + half) * QUARTER
                quarter = result[start : start + QUARTER].astype(jnp.bfloat16)
                target[window, half] = quarter
                if half == edge_half and window == edge_window % held:

                    @pl.when(pl.program_id(0) == edge_window // held)
                    def _(quarter=quarter, side=side):
                        edge_ref[side] = quarter


def feed(windows, pieces, gain, hidden_size, edge, after=(), held=2):
    count, cells, features = windows.shape
    block = pl.BlockSpec((held, cells, features), lambda i: (i, 0, 0))
    side = pl.BlockSpec((held, 2, QUARTER, features), lambda i: (i, 0, 0, 0))
    return pl.pallas_call(
        functools.partial(feed_kernel, len(pieces), hidden_size, 512, edge),
        grid=(count // held,),
        out_shape=[jax.ShapeDtypeStruct((count, 2, QUARTER, features), jnp.bfloat16)] * 2
        + [jax.ShapeDtypeStruct((2, QUARTER, features), jnp.bfloat16)],
        in_specs=[block]
        + [ANY] * len(pieces)
        + [pl.BlockSpec((1, features), lambda i: (0, 0))]
        + [ANY] * len(after),
        out_specs=[side, side, pl.BlockSpec((2, QUARTER, features), lambda i: (0, 0, 0))],
        scratch_shapes=[
            pltpu.VMEM((features, 2 * hidden_size), jnp.bfloat16),
            pltpu.SemaphoreType.DMA,
        ],
        compiler_params=pltpu.CompilerParams(vmem_limit_bytes=24 * 2**20),
        cost_estimate=pl.CostEstimate(
            flops=6 * count * cells * features * hidden_size,
            bytes_accessed=8_000_000,
            transcendentals=0,
        ),
    )(windows, *pieces, gain, *after)


def shift_from(block, lon_step, lat_step):
    lons, lats = lax.axis_size("lon"), lax.axis_size("lat")
    pairs = []
    for lon in range(lons):
        for lat in range(lats):
            source = (lon + lon_step) % lons * lats + (lat + lat_step) % lats
            pairs.append((source, lon * lats + lat))
    return lax.ppermute(block, ("lon", "lat"), pairs)


def to_windows(cells):
    cols, rows, levels, features = cells.shape
    c, r = WLON // 2, WLAT // 2
    arranged = cells.reshape(cols // WLON, 2, c, rows // WLAT, 2, r, levels, features)
    arranged = arranged.transpose(0, 3, 1, 4, 2, 5, 6, 7)
    return arranged.reshape(cols // WLON, rows // WLAT, CELLS, features)


def strip(quarters):
    features = quarters.shape[-1]
    c, r = WLON // 2, WLAT // 2
    arranged = quarters.reshape(-1, c, r, LEVELS, features).transpose(1, 0, 2, 3, 4)
    return arranged.reshape(c, -1, LEVELS, features)


def back_in_place(sides, behind, below, corner):
    features = behind.shape[-1]
    flat = lambda side: side.reshape(-1, QUARTER, features)[:-1]
    c, r = WLON // 2, WLAT // 2
    own = jnp.concatenate([strip(flat(side)) for side in sides[:-1]], 0)
    tops = jnp.concatenate([strip(low[None]) for low in below], 0)
    first = jnp.concatenate([strip(corner[None]), strip(flat(behind))], 1)
    return jnp.concatenate([first, jnp.concatenate([tops, own], 1)], 0)


def per_device(tokens, qkv_weight, out_weight, up_weight, down_weight, norm_gain, logit_scale):
    cols, rows, _, features = tokens.shape
    hidden_size = up_weight.shape[-1]
    row_windows = rows // WLAT
    weights = (qkv_weight, out_weight, up_weight, down_weight)
    relay = relayed(qkv_weight.shape[1], lax.axis_size("lat"))
    sharp = jnp.repeat(logit_scale * math.log2(math.e), HEAD, axis=1)
    windows = to_windows(tokens)

    def attention(block, sources, lows, pieces, after=()):
        return attend(
            sources,
            lows,
            pieces,
            norm_gain[block, :1],
            sharp[block : block + 1],
            row_windows,
            after,
        )

    def forward(block, middle, pieces, edge, after=()):
        return feed(middle, pieces, norm_gain[block, 1:], hidden_size, edge, after)

    low_edge, high_edge = (0, 0), (row_windows - 1, 1)
    if relay:
        _, own = join([], weights[:2], 0)
        column, own = join(along_z(own), weights[2:], 0, (windows,))
        beside, across = send(column, one_way), send(column, other_way)
        corner = send(beside, other_way)
        pieces = whole_pieces(column, beside, across, corner)
        column, own = join(along_z(own), weights[:2], 1, (beside, across))
        beside, across = send(column, one_way), send(column, other_way)
        middle_0 = attention(0, [windows[0]], None, pieces)
        corner = send(tied(beside, middle_0), other_way)
        middle_1 = attention(0, [windows[1]], None, pieces, (middle_0,))
        feed_pieces = whole_pieces(column, beside, across, corner, middle_1)
        column, own = join(along_z(own), weights[2:], 1, (middle_1, beside, across))
        beside, across = send(column, one_way), send(column, other_way)
        left, right, low_0 = forward(0, middle_0, feed_pieces, low_edge)
        corner = send(tied(beside, low_0), other_way)
        last_column, _ = join(along_z(own), (), 0, (low_0, beside, across))
        last_beside, last_across = send(last_column, one_way), send(last_column, other_way)
        left_1, right_1, low_1 = forward(0, middle_1, feed_pieces, low_edge, (low_0,))
        pieces = whole_pieces(column, beside, across, corner, low_1)
        last_corner = send(tied(last_beside, low_1), other_way)
    else:
        gathered = []
        for block in range(2):
            for pair in (weights[:2], weights[2:]):
                chunk = jnp.concatenate([weight[block] for weight in pair], 1)
                gathered.append([lax.all_gather(chunk, "lon", axis=0, tiled=True)])
        first_pieces, feed_pieces, pieces, last_pieces = gathered
        middle_0 = attention(0, [windows[0]], None, first_pieces)
        middle_1 = attention(0, [windows[1]], None, first_pieces)
        left, right, low_0 = forward(0, middle_0, feed_pieces, low_edge)
        left_1, right_1, low_1 = forward(0, middle_1, feed_pieces, low_edge)
    ahead = shift_from(left, 1, 0)
    ahead_low = shift_from(low_0, 1, 1)
    below_0 = shift_from(low_0, 0, 1)
    below_1 = shift_from(low_1, 0, 1)

    middle_0 = attention(1, [right, left_1, below_0, below_1], (1, 0), pieces)
    if relay:
        last_pieces = whole_pieces(last_column, last_beside, last_across, last_corner, middle_0)
    middle_1 = attention(1, [right_1, ahead, below_1, ahead_low], (1, 0), pieces, (middle_0,))
    left_1, right_1, high_1 = forward(1, middle_1, last_pieces, high_edge)
    behind = shift_from(right_1, -1, 0)
    corner = shift_from(high_1, -1, -1)
    above_1 = shift_from(high_1, 0, -1)
    left, right, high_0 = forward(1, middle_0, last_pieces, high_edge, (high_1,))
    above_0 = shift_from(high_0, 0, -1)
    return back_in_place(
        (left, right, left_1, right_1), behind, (above_0[0], above_0[1], above_1[0]), corner[1]
    )


def solution(mesh):
    placed = (
        P("lon", "lat", None, None),
        P(None, "lon", None),
        P(None, "lon", None),
        P(None, "lon", None),
        P(None, "lon", None),
        P(),
        P(),
    )
    return jax.shard_map(
        per_device,
        mesh=mesh,
        in_specs=placed,
        out_specs=P("lon", "lat", None, None),
        check_vma=False,
    )
```

time: 198 us -> 213 us (1.076)
  Pallas kernels: 63 us -> 87.8 us
  waiting for transfers between devices: 57.7 us -> 42.9 us
  between operations: 13.8 us -> 0.66 us
  starting transfers between devices: 33.1 us -> 42.4 us
  local copies, waits for them, and re-layouts: 26 us -> 35 us
    pallas_call x2 -> x4, Pallas kernels: 22.2 us -> 39.6 us  [feed(): pl.pallas_call(functools.partial(feed_kernel, len(pieces), hidden_size, 5...]
    unnamed x50 -> x122, local copies, waits for them, and re-layouts: 10.9 us -> 24 us
    ppermute x30 -> x40, waiting for transfers between devices: 43.3 us -> 33.3 us  [send(): return lax.ppermute(block, ('lon', 'lat'), pairs)]
    ppermute x30 -> x40, starting transfers between devices: 26.8 us -> 35 us  [send(): return lax.ppermute(block, ('lon', 'lat'), pairs)]
    pallas_call x2 -> x4, Pallas kernels: 33.2 us -> 38.7 us  [attend(): pl.pallas_call(functools.partial(attend_kernel, shifted, row_windows, len...]
    ppermute x6 -> x8, waiting for transfers between devices: 14.5 us -> 9.57 us  [shift_from(): return lax.ppermute(block, ('lon', 'lat'), pairs)]
    squeeze x1 -> x3, local copies, waits for them, and re-layouts: 0.01 us -> 4 us  [the longest x1 2.02 us: per_device(): middle_1 = attention(0, [windows[1]], None, pieces, (middle_0,))]
    reshape x3 -> x10, local copies, waits for them, and re-layouts: 7.95 us -> 4.69 us  [the longest x1 2.09 us: to_windows(): cells.reshape(cols // WLON, 2, c, rows // WLAT, 2, r, levels, features)]
  transfers between devices with their start and end apart: 37 -> 48, of which waited for: 12 -> 9; matrix products, arithmetic and copies ran while one was open for 8% -> 5% of each run, Pallas kernels for 27% -> 30%
where the time goes in v5:
time: 213 us; the launch traced here: 212 us
  Pallas kernels  87.8 us (41%)
  waiting for transfers between devices  42.9 us (20%)
  starting transfers between devices  42.4 us (20%)
  local copies, waits for them, and re-layouts  35 us (16%)
  other arithmetic  2.91 us (1%)
    pallas_call x4, Pallas kernels, feed(): pl.pallas_call(functools.partial(feed_kernel, len(pieces), hidden_size, 5...  39.6 us
    pallas_call x4, Pallas kernels, attend(): pl.pallas_call(functools.partial(attend_kernel, shifted, row_windows, len...  38.7 us
    ppermute x40, starting transfers between devices, send(): return lax.ppermute(block, ('lon', 'lat'), pairs)  35 us
    ppermute x40, waiting for transfers between devices, send(): return lax.ppermute(block, ('lon', 'lat'), pairs)  33.3 us
    unnamed x122, local copies, waits for them, and re-layouts  24 us
    ppermute x8, waiting for transfers between devices, shift_from(): return lax.ppermute(block, ('lon', 'lat'), pairs)  9.57 us
    pallas_call x5, Pallas kernels, join(): pl.pallas_call(kernel, out_shape=out_shape, in_specs=specs)  9.47 us
    ppermute x8, starting transfers between devices, shift_from(): return lax.ppermute(block, ('lon', 'lat'), pairs)  7.43 us
  transfers between devices with their start and end apart: 48, of which 9 were waited for; matrix products, arithmetic and copies ran while one was open for 5% of the time, Pallas kernels for 30%

profile of v5, /device:TPU:0, one launch (start us, length us, event | category | flops | bytes accessed | tf_op | source)
XLA Modules:
  0.0 211.6 jit_solution(5017602680463259157)
XLA Ops:
  0.0 1.6 shard_map.127.refs_0_
  1.6 3.0 %collective-permute-start = (bf16[16,2048]{1,0:T(8,128)(2,1)}, bf16[16,2048]{1,0:T(8,128)(2,1)S(1)}, u32[]{:S(2)}, u32[]{:S(2)}) collective-permute-start(bf16[16,2048]{1,0:T(8,128)(2,1)} %shard_map.127.refs_0_), channel_id=1, source_target_pairs={{0,8},{1,9},{2,10},{3,11},{4,12},{5,13},{6,14},{7,15},{8,16},{9,17... | collective-permute-start | bytes 196616 | tf_op jit(solution)/shard_map/ppermute | solution.py:88
  4.6 2.6 %collective-permute-start.1 = (bf16[16,2048]{1,0:T(8,128)(2,1)}, bf16[16,2048]{1,0:T(8,128)(2,1)S(1)}, u32[]{:S(2)}, u32[]{:S(2)}) collective-permute-start(bf16[16,2048]{1,0:T(8,128)(2,1)} %shard_map.127.refs_0_), channel_id=1, source_target_pairs={{0,16},{1,17},{2,18},{3,19},{4,20},{5,21},{6,22},{7,23},{8,24},{9,... | collective-permute-start | bytes 196616 | tf_op jit(solution)/shard_map/ppermute | solution.py:88
  7.2 1.3 collective-permute-start.2
  8.5 2.1 copy.20
  10.6 1.3 reshape.58.refs_6_
  13.2 2.0 shard_map.128
  15.2 1.8 collective-permute-start.3
  16.9 1.5 collective-permute-start.4
  18.4 6.0 %collective-permute-done.3.refs_2_.refs_6_ = bf16[4,16,2048]{2,1,0:T(8,128)(2,1)S(1)} collective-permute-done((bf16[4,16,2048]{2,1,0:T(8,128)(2,1)}, bf16[4,16,2048]{2,1,0:T(8,128)(2,1)S(1)}, u32[]{:S(2)}, u32[]{:S(2)}) %collective-permute-start.3) | collective-permute-done | bytes 262176 | tf_op jit(solution)/shard_map/ppermute | solution.py:88
  24.4 1.7 collective-permute-start.5
  26.1 1.8 fusion
  28.4 1.4 collective-permute-start.11
  30.0 0.8 collective-permute-done.5.refs_4_
  30.8 5.3 %collective-permute-done.10.refs_1_ = bf16[16,4096]{1,0:T(8,128)(2,1)S(1)} collective-permute-done((bf16[16,4096]{1,0:T(8,128)(2,1)S(1)}, bf16[16,4096]{1,0:T(8,128)(2,1)S(1)}, u32[]{:S(2)}, u32[]{:S(2)}) %collective-permute-start.10) | collective-permute-done | bytes 131104 | tf_op jit(solution)/shard_map/ppermute | solution.py:88
  36.1 2.0 squeeze.22.refs_0_
  38.3 2.0 squeeze.24.refs_0_
  40.7 5.7 %collective-permute-done.12.refs_3_ = bf16[16,4096]{1,0:T(8,128)(2,1)S(1)} collective-permute-done((bf16[16,4096]{1,0:T(8,128)(2,1)S(1)}, bf16[16,4096]{1,0:T(8,128)(2,1)S(1)}, u32[]{:S(2)}, u32[]{:S(2)}) %collective-permute-start.12) | collective-permute-done | bytes 131104 | tf_op jit(solution)/shard_map/ppermute | solution.py:88
  47.1 2.0 shard_map.131
  50.0 2.1 collective-permute-start.14
  52.8 0.9 copy-done.9
  53.7 0.9 copy-done.12
  54.7 0.9 copy-done.24
  55.6 0.9 copy-done.27
  56.6 0.9 copy-done.30
  57.5 0.9 copy-done.33
  58.5 1.1 copy-done.35
  59.6 10.6 %shard_map.129.refs_12_.refs_0_ = bf16[4,144,512]{2,1,0:T(8,128)(2,1)S(1)} custom-call(bf16[4,144,512]{2,1,0:T(8,128)(2,1)S(1)} %squeeze.24.refs_0_, bf16[4,16,2048]{2,1,0:T(8,128)(2,1)S(1)} %copy-done.24, bf16[4,16,2048]{2,1,0:T(8,128)(2,1)S(1)} %copy-done.9, bf16[4,16,2048]{2,1,0:T(8,128)(2,1)S(1)} %copy-done.12, bf16[4,16,2048]{2,1,0:T(8,128)(2,1)S(1)} %copy-done.27, ...), custom_call_target="tpu_custom_call" | custom-call | flops 8000000000 | bytes 6000000 | tf_op jit(solution)/shard_map/pallas_call | solution.py:247
  70.9 10.6 %shard_map.130.refs_0_.refs_6_ = bf16[4,144,512]{2,1,0:T(8,128)(2,1)S(1)} custom-call(bf16[4,144,512]{2,1,0:T(8,128)(2,1)S(1)} %squeeze.22.refs_0_, bf16[4,16,2048]{2,1,0:T(8,128)(2,1)S(1)} %copy-done.25, bf16[4,16,2048]{2,1,0:T(8,128)(2,1)S(1)} %copy-done.10, bf16[4,16,2048]{2,1,0:T(8,128)(2,1)S(1)} %copy-done.13, bf16[4,16,2048]{2,1,0:T(8,128)(2,1)S(1)} %copy-done.28, ...), custom_call_target="tpu_custom_call" | custom-call | flops 8000000000 | bytes 6000000 | tf_op jit(solution)/shard_map/pallas_call | solution.py:247
  81.6 0.8 copy-done
  82.9 6.1 %collective-permute-done.23.refs_1_ = bf16[16,2048]{1,0:T(8,128)(2,1)S(1)} collective-permute-done((bf16[16,2048]{1,0:T(8,128)(2,1)S(1)}, bf16[16,2048]{1,0:T(8,128)(2,1)S(1)}, u32[]{:S(2)}, u32[]{:S(2)}) %collective-permute-start.23) | collective-permute-done | bytes 65568 | tf_op jit(solution)/shard_map/ppermute | solution.py:88
  89.0 5.5 %collective-permute-done.24.refs_2_ = bf16[16,2048]{1,0:T(8,128)(2,1)S(1)} collective-permute-done((bf16[16,2048]{1,0:T(8,128)(2,1)S(1)}, bf16[16,2048]{1,0:T(8,128)(2,1)S(1)}, u32[]{:S(2)}, u32[]{:S(2)}) %collective-permute-start.24) | collective-permute-done | bytes 65568 | tf_op jit(solution)/shard_map/ppermute | solution.py:88
  95.2 3.6 %collective-permute-done.25.refs_3_ = bf16[16,2048]{1,0:T(8,128)(2,1)S(1)} collective-permute-done((bf16[16,2048]{1,0:T(8,128)(2,1)S(1)}, bf16[16,2048]{1,0:T(8,128)(2,1)S(1)}, u32[]{:S(2)}, u32[]{:S(2)}) %collective-permute-start.25) | collective-permute-done | bytes 65568 | tf_op jit(solution)/shard_map/ppermute | solution.py:88
  99.4 2.0 shard_map.134
  101.4 1.7 collective-permute-start.26
  103.4 0.8 copy-done.19
  104.2 3.0 %collective-permute-start.35 = (bf16[16,4096]{1,0:T(8,128)(2,1)}, bf16[16,4096]{1,0:T(8,128)(2,1)}, u32[]{:S(2)}, u32[]{:S(2)}) collective-permute-start(bf16[16,4096]{1,0:T(8,128)(2,1)} %get-tuple-element.44.refs_0_), channel_id=1, source_target_pairs={{0,16},{1,17},{2,18},{3,19},{4,20},{5,21},{6,22},{7,23},{8,24},{9,... | collective-permute-start | bytes 393224 | tf_op jit(solution)/shard_map/ppermute | solution.py:88
  107.2 0.8 collective-permute-start.36
  108.0 1.0 copy-done.5
  109.1 1.0 copy-done.20
  110.1 1.1 copy-done.40
  111.2 9.3 %shard_map.132 = (bf16[4,2,36,512]{3,2,1,0:T(8,128)(2,1)S(1)}, bf16[4,2,36,512]{3,2,1,0:T(8,128)(2,1)S(1)}, bf16[2,36,512]{2,1,0:T(8,128)(2,1)S(1)}) custom-call(bf16[4,144,512]{2,1,0:T(8,128)(2,1)S(1)} %copy-done.40, bf16[4,16,4096]{2,1,0:T(8,128)(2,1)S(1)} %copy-done.16, bf16[4,16,4096]{2,1,0:T(8,128)(2,1)S(1)} %copy-done.3, ...), custom_call_target="tpu_custom_call" | custom-call | flops 3623878656 | bytes 8000000 | tf_op jit(solution)/shard_map/pallas_call | solution.py:307
  121.9 0.7 copy-done.45
  123.3 1.7 collective-permute-start.28
  125.0 2.0 shard_map.137.refs_1_
  127.3 1.0 copy-done.18
  128.4 1.0 copy-done.21
  129.4 9.3 %shard_map.133 = (bf16[4,2,36,512]{3,2,1,0:T(8,128)(2,1)S(1)}, bf16[4,2,36,512]{3,2,1,0:T(8,128)(2,1)S(1)}, bf16[2,36,512]{2,1,0:T(8,128)(2,1)S(1)}) custom-call(bf16[4,144,512]{2,1,0:T(8,128)(2,1)S(1)} %copy-done.1, bf16[4,16,4096]{2,1,0:T(8,128)(2,1)S(1)} %copy-done.16, bf16[4,16,4096]{2,1,0:T(8,128)(2,1)S(1)} %copy-done.3, ...), custom_call_target="tpu_custom_call" | custom-call | flops 3623878656 | bytes 8000000 | tf_op jit(solution)/shard_map/pallas_call | solution.py:307
  139.5 0.7 copy-done.43
  141.0 1.6 collective-permute-start.22
  142.6 1.6 collective-permute-start.38
  144.2 1.3 collective-permute-start.20
  145.5 0.8 collective-permute-start.39
  146.4 1.1 copy-done.36
  147.5 1.0 copy-done.44
  148.4 1.0 copy-done.46
  149.4 8.7 %shard_map.135.refs_16_.refs_0_ = bf16[4,144,512]{2,1,0:T(8,128)(2,1)S(1)} custom-call(bf16[4,2,36,512]{3,2,1,0:T(8,128)(2,1)S(1)} %copy-done.46, bf16[4,2,36,512]{3,2,1,0:T(8,128)(2,1)S(1)} %copy-done.44, bf16[2,36,512]{2,1,0:T(8,128)(2,1)S(1)} %collective-permute-done.33.refs_2_, bf16[2,36,512]{2,1,0:T(8,128)(2,1)S(1)} %collective-permute-done.21.refs_3_.refs_2_, ...), custom_call_target="tpu_custom_call" | custom-call | flops 8000000000 | bytes 6000000 | tf_op jit(solution)/shard_map/pallas_call | solution.py:247
  158.2 5.6 %collective-permute-start.42 = (bf16[4,16,4096]{2,1,0:T(8,128)(2,1)S(1)}, bf16[4,16,4096]{2,1,0:T(8,128)(2,1)S(1)}, u32[]{:S(2)}, u32[]{:S(2)}) collective-permute-start(bf16[4,16,4096]{2,1,0:T(8,128)(2,1)S(1)} %collective-permute-done.38.refs_3_), channel_id=1, source_target_pairs={{0,1},{1,0},{2,3},{3,2},{4,5},{5,4},{6,7},{7,6},{8,9},{9,8},{10,11... | collective-permute-start | bytes 1572872 | tf_op jit(solution)/shard_map/ppermute | solution.py:88
  163.8 8.7 %shard_map.136.refs_0_ = bf16[4,144,512]{2,1,0:T(8,128)(2,1)S(1)} custom-call(bf16[4,2,36,512]{3,2,1,0:T(8,128)(2,1)S(1)} %copy-done.42, bf16[4,2,36,512]{3,2,1,0:T(8,128)(2,1)S(1)} %collective-permute-done.20.refs_1_, bf16[2,36,512]{2,1,0:T(8,128)(2,1)S(1)} %collective-permute-done.21.refs_3_.refs_2_, ...), custom_call_target="tpu_custom_call" | custom-call | flops 8000000000 | bytes 6000000 | tf_op jit(solution)/shard_map/pallas_call | solution.py:247
  172.6 10.5 %shard_map.138 = (bf16[4,2,36,512]{3,2,1,0:T(8,128)(2,1)S(1)}, bf16[4,2,36,512]{3,2,1,0:T(8,128)(2,1)S(1)}, bf16[2,36,512]{2,1,0:T(8,128)(2,1)S(1)}) custom-call(bf16[4,144,512]{2,1,0:T(8,128)(2,1)S(1)} %shard_map.136.refs_0_, bf16[4,16,4096]{2,1,0:T(8,128)(2,1)S(1)} %copy-done.7, bf16[4,16,4096]{2,1,0:T(8,128)(2,1)S(1)} %collective-permute-done.37.refs_2_, ...), custom_call_target="tpu_custom_call" | custom-call | flops 3623878656 | bytes 8000000 | tf_op jit(solution)/shard_map/pallas_call | solution.py:307
  183.1 10.5 %shard_map.139 = (bf16[4,2,36,512]{3,2,1,0:T(8,128)(2,1)S(1)}, bf16[4,2,36,512]{3,2,1,0:T(8,128)(2,1)S(1)}, bf16[2,36,512]{2,1,0:T(8,128)(2,1)S(1)}) custom-call(bf16[4,144,512]{2,1,0:T(8,128)(2,1)S(1)} %shard_map.135.refs_16_.refs_0_, bf16[4,16,4096]{2,1,0:T(8,128)(2,1)S(1)} %copy-done.7, bf16[4,16,4096]{2,1,0:T(8,128)(2,1)S(1)} %collective-permute-done.37.refs_2_, ...), custom_call_target="tpu_custom_call" | custom-call | flops 3623878656 | bytes 8000000 | tf_op jit(solution)/shard_map/pallas_call | solution.py:307
  194.1 2.8 %collective-permute-start.45 = (bf16[4,2,36,512]{3,2,1,0:T(8,128)(2,1)S(1)}, bf16[4,2,36,512]{3,2,1,0:T(8,128)(2,1)S(1)}, u32[]{:S(2)}, u32[]{:S(2)}) collective-permute-start(bf16[4,2,36,512]{3,2,1,0:T(8,128)(2,1)S(1)} %get-tuple-element.48), channel_id=1, source_target_pairs={{30,0},{31,1},{0,2},{1,3},{2,4},{3,5},{4,6},{5,7},{6,8},{7,9},{8,1... | collective-permute-start | bytes 884744 | tf_op jit(solution)/shard_map/ppermute | solution.py:337
  198.7 9.6 %collective-permute-done.44 = bf16[2,36,512]{2,1,0:T(8,128)(2,1)S(1)} collective-permute-done((bf16[2,36,512]{2,1,0:T(8,128)(2,1)S(1)}, bf16[2,36,512]{2,1,0:T(8,128)(2,1)S(1)}, u32[]{:S(2)}, u32[]{:S(2)}) %collective-permute-start.44) | collective-permute-done | bytes 73760 | tf_op jit(solution)/shard_map/ppermute | solution.py:337
  208.7 2.9 %maximum_maximum_fusion = bf16[24,24,2,512]{3,2,1,0:T(2,128)(2,1)} fusion(bf16[6,21,2,512]{3,2,1,0:T(2,128)(2,1)S(1)} %bitcast.38, bf16[6,21,2,512]{3,2,1,0:T(2,128)(2,1)S(1)} %bitcast.39, bf16[6,21,2,512]{3,2,1,0:T(2,128)(2,1)S(1)} %bitcast.40, bf16[6,3,2,512]{3,2,1,0:T(2,128)(2,1)S(1)} %reshape_transpose_reshape_broadcast_in_dim_squeeze.15, ...), kind=kLoop, calls=%fused_computation | loop fusion | flops 4128768 | bytes 2359296 | tf_op jit(solution)/shard_map/concatenate | solution.py:362
  (199 shorter events, 14.1 us)
Async XLA Ops:
  1.6 10.4 %collective-permute-start = (bf16[16,2048]{1,0:T(8,128)(2,1)}, bf16[16,2048]{1,0:T(8,128)(2,1)S(1)}, u32[]{:S(2)}, u32[]{:S(2)}) collective-permute-start(bf16[16,2048]{1,0:T(8,128)(2,1)} %shard_map.127.refs_0_), channel_id=1, source_target_pairs={{0,8},{1,9},{2,10},{3,11},{4,12},{5,13},{6,14},{7,15},{8,16},{9,17... | collective-permute-start | bytes 196616 | tf_op jit(solution)/shard_map/ppermute | solution.py:88
  4.6 7.3 %collective-permute-start.1 = (bf16[16,2048]{1,0:T(8,128)(2,1)}, bf16[16,2048]{1,0:T(8,128)(2,1)S(1)}, u32[]{:S(2)}, u32[]{:S(2)}) collective-permute-start(bf16[16,2048]{1,0:T(8,128)(2,1)} %shard_map.127.refs_0_), channel_id=1, source_target_pairs={{0,16},{1,17},{2,18},{3,19},{4,20},{5,21},{6,22},{7,23},{8,24},{9,... | collective-permute-start | bytes 196616 | tf_op jit(solution)/shard_map/ppermute | solution.py:88
  7.2 4.9 %collective-permute-start.2 = (bf16[16,2048]{1,0:T(8,128)(2,1)}, bf16[16,2048]{1,0:T(8,128)(2,1)S(1)}, u32[]{:S(2)}, u32[]{:S(2)}) collective-permute-start(bf16[16,2048]{1,0:T(8,128)(2,1)} %shard_map.127.refs_0_), channel_id=1, source_target_pairs={{0,24},{1,25},{2,26},{3,27},{4,28},{5,29},{6,30},{7,31},{8,0},{9,1... | collective-permute-start | bytes 196616 | tf_op jit(solution)/shard_map/ppermute | solution.py:88
  15.1 12.8 %copy-start.47 = (bf16[16,4096]{1,0:T(8,128)(2,1)S(1)}, bf16[16,4096]{1,0:T(8,128)(2,1)}, u32[]{:S(2)}) copy-start(bf16[16,4096]{1,0:T(8,128)(2,1)} %get-tuple-element.30.refs_0_) | copy-start | bytes 393220
  15.1 13.2 %copy-start.60 = (f32[2,16]{1,0:T(2,128)S(1)}, f32[2,16]{1,0:T(2,128)}, u32[]{:S(2)}) copy-start(f32[2,16]{1,0:T(2,128)} %param.19) | copy-start | bytes 388
  15.1 13.2 %copy-start.23 = (bf16[4,16,2048]{2,1,0:T(8,128)(2,1)S(1)}, bf16[4,16,2048]{2,1,0:T(8,128)(2,1)}, u32[]{:S(2)}) copy-start(bf16[4,16,2048]{2,1,0:T(8,128)(2,1)} %get-tuple-element.29.refs_1_) | copy-start | bytes 786436
  15.2 9.3 %collective-permute-start.3 = (bf16[4,16,2048]{2,1,0:T(8,128)(2,1)}, bf16[4,16,2048]{2,1,0:T(8,128)(2,1)S(1)}, u32[]{:S(2)}, u32[]{:S(2)}) collective-permute-start(bf16[4,16,2048]{2,1,0:T(8,128)(2,1)} %get-tuple-element.29.refs_1_), channel_id=1, source_target_pairs={{0,2},{1,5},{2,0},{3,7},{4,6},{5,1},{6,4},{7,3},{8,10},{9,13},{10,... | collective-permute-start | bytes 786440 | tf_op jit(solution)/shard_map/ppermute | solution.py:88
  16.9 12.9 %collective-permute-start.4 = (bf16[4,16,2048]{2,1,0:T(8,128)(2,1)}, bf16[4,16,2048]{2,1,0:T(8,128)(2,1)S(1)}, u32[]{:S(2)}, u32[]{:S(2)}) collective-permute-start(bf16[4,16,2048]{2,1,0:T(8,128)(2,1)} %get-tuple-element.29.refs_1_), channel_id=1, source_target_pairs={{0,4},{1,3},{2,6},{3,1},{4,0},{5,7},{6,2},{7,5},{8,12},{9,11},{10,... | collective-permute-start | bytes 786440 | tf_op jit(solution)/shard_map/ppermute | solution.py:88
  24.4 22.0 %copy-start.8 = (bf16[4,16,2048]{2,1,0:T(8,128)(2,1)}, bf16[4,16,2048]{2,1,0:T(8,128)(2,1)S(1)}, u32[]{:S(2)}) copy-start(bf16[4,16,2048]{2,1,0:T(8,128)(2,1)S(1)} %collective-permute-done.3.refs_2_.refs_6_) | copy-start | bytes 786436
  24.4 6.4 %collective-permute-start.5 = (bf16[4,16,2048]{2,1,0:T(8,128)(2,1)S(1)}, bf16[4,16,2048]{2,1,0:T(8,128)(2,1)S(1)}, u32[]{:S(2)}, u32[]{:S(2)}) collective-permute-start(bf16[4,16,2048]{2,1,0:T(8,128)(2,1)S(1)} %collective-permute-done.3.refs_2_.refs_6_), channel_id=1, source_target_pairs={{0,4},{1,3},{2,6},{3,1},{4,0},{5,7},{6,2},{7,5},{8,12},{9,11},{10,... | collective-permute-start | bytes 786440 | tf_op jit(solution)/shard_map/ppermute | solution.py:88
  27.9 8.2 %collective-permute-start.10 = (bf16[16,4096]{1,0:T(8,128)(2,1)S(1)}, bf16[16,4096]{1,0:T(8,128)(2,1)S(1)}, u32[]{:S(2)}, u32[]{:S(2)}) collective-permute-start(bf16[16,4096]{1,0:T(8,128)(2,1)S(1)} %copy-done.47), channel_id=1, source_target_pairs={{0,8},{1,9},{2,10},{3,11},{4,12},{5,13},{6,14},{7,15},{8,16},{9,17... | collective-permute-start | bytes 393224 | tf_op jit(solution)/shard_map/ppermute | solution.py:88
  28.3 21.0 %collective-permute-start.6 = (bf16[4,16,2048]{2,1,0:T(8,128)(2,1)S(1)}, bf16[4,16,2048]{2,1,0:T(8,128)(2,1)S(1)}, u32[]{:S(2)}, u32[]{:S(2)}) collective-permute-start(bf16[4,16,2048]{2,1,0:T(8,128)(2,1)S(1)} %copy-done.23), channel_id=1, source_target_pairs={{0,1},{1,0},{2,3},{3,2},{4,5},{5,4},{6,7},{7,6},{8,9},{9,8},{10,11... | collective-permute-start | bytes 786440 | tf_op jit(solution)/shard_map/ppermute | solution.py:88
  28.4 11.9 %collective-permute-start.11 = (bf16[16,4096]{1,0:T(8,128)(2,1)S(1)}, bf16[16,4096]{1,0:T(8,128)(2,1)S(1)}, u32[]{:S(2)}, u32[]{:S(2)}) collective-permute-start(bf16[16,4096]{1,0:T(8,128)(2,1)S(1)} %copy-done.47), channel_id=1, source_target_pairs={{0,16},{1,17},{2,18},{3,19},{4,20},{5,21},{6,22},{7,23},{8,24},{9,... | collective-permute-start | bytes 393224 | tf_op jit(solution)/shard_map/ppermute | solution.py:88
  29.8 16.6 %copy-start.11 = (bf16[4,16,2048]{2,1,0:T(8,128)(2,1)}, bf16[4,16,2048]{2,1,0:T(8,128)(2,1)S(1)}, u32[]{:S(2)}) copy-start(bf16[4,16,2048]{2,1,0:T(8,128)(2,1)S(1)} %collective-permute-done.4.refs_3_.refs_7_) | copy-start | bytes 786436
  29.8 22.2 %collective-permute-start.7 = (bf16[4,16,2048]{2,1,0:T(8,128)(2,1)S(1)}, bf16[4,16,2048]{2,1,0:T(8,128)(2,1)S(1)}, u32[]{:S(2)}, u32[]{:S(2)}) collective-permute-start(bf16[4,16,2048]{2,1,0:T(8,128)(2,1)S(1)} %collective-permute-done.3.refs_2_.refs_6_), channel_id=1, source_target_pairs={{0,1},{1,0},{2,3},{3,2},{4,5},{5,4},{6,7},{7,6},{8,9},{9,8},{10,11... | collective-permute-start | bytes 786440 | tf_op jit(solution)/shard_map/ppermute | solution.py:88
  30.8 21.9 %collective-permute-start.8 = (bf16[4,16,2048]{2,1,0:T(8,128)(2,1)S(1)}, bf16[4,16,2048]{2,1,0:T(8,128)(2,1)}, u32[]{:S(2)}, u32[]{:S(2)}) collective-permute-start(bf16[4,16,2048]{2,1,0:T(8,128)(2,1)S(1)} %collective-permute-done.4.refs_3_.refs_7_), channel_id=1, source_target_pairs={{0,1},{1,0},{2,3},{3,2},{4,5},{5,4},{6,7},{7,6},{8,9},{9,8},{10,11... | collective-permute-start | bytes 786440 | tf_op jit(solution)/shard_map/ppermute | solution.py:88
  36.1 16.7 %collective-permute-start.9 = (bf16[4,16,2048]{2,1,0:T(8,128)(2,1)S(1)}, bf16[4,16,2048]{2,1,0:T(8,128)(2,1)}, u32[]{:S(2)}, u32[]{:S(2)}) collective-permute-start(bf16[4,16,2048]{2,1,0:T(8,128)(2,1)S(1)} %collective-permute-done.5.refs_4_), channel_id=1, source_target_pairs={{0,1},{1,0},{2,3},{3,2},{4,5},{5,4},{6,7},{7,6},{8,9},{9,8},{10,11... | collective-permute-start | bytes 786440 | tf_op jit(solution)/shard_map/ppermute | solution.py:88
  40.3 6.1 %collective-permute-start.12 = (bf16[16,4096]{1,0:T(8,128)(2,1)S(1)}, bf16[16,4096]{1,0:T(8,128)(2,1)S(1)}, u32[]{:S(2)}, u32[]{:S(2)}) collective-permute-start(bf16[16,4096]{1,0:T(8,128)(2,1)S(1)} %copy-done.47), channel_id=1, source_target_pairs={{0,24},{1,25},{2,26},{3,27},{4,28},{5,29},{6,30},{7,31},{8,0},{9,1... | collective-permute-start | bytes 393224 | tf_op jit(solution)/shard_map/ppermute | solution.py:88
  49.1 21.1 %collective-permute-start.13 = (bf16[4,16,4096]{2,1,0:T(8,128)(2,1)}, bf16[4,16,4096]{2,1,0:T(8,128)(2,1)S(1)}, u32[]{:S(2)}, u32[]{:S(2)}) collective-permute-start(bf16[4,16,4096]{2,1,0:T(8,128)(2,1)} %get-tuple-element.31.refs_1_), channel_id=1, source_target_pairs={{0,2},{1,5},{2,0},{3,7},{4,6},{5,1},{6,4},{7,3},{8,10},{9,13},{10,... | collective-permute-start | bytes 1572872 | tf_op jit(solution)/shard_map/ppermute | solution.py:88
  50.0 32.4 %collective-permute-start.14 = (bf16[4,16,4096]{2,1,0:T(8,128)(2,1)}, bf16[4,16,4096]{2,1,0:T(8,128)(2,1)S(1)}, u32[]{:S(2)}, u32[]{:S(2)}) collective-permute-start(bf16[4,16,4096]{2,1,0:T(8,128)(2,1)} %get-tuple-element.31.refs_1_), channel_id=1, source_target_pairs={{0,4},{1,3},{2,6},{3,1},{4,0},{5,7},{6,2},{7,5},{8,12},{9,11},{10,... | collective-permute-start | bytes 1572872 | tf_op jit(solution)/shard_map/ppermute | solution.py:88
  52.8 50.3 %collective-permute-start.16 = (bf16[4,16,4096]{2,1,0:T(8,128)(2,1)}, bf16[4,16,4096]{2,1,0:T(8,128)(2,1)}, u32[]{:S(2)}, u32[]{:S(2)}) collective-permute-start(bf16[4,16,4096]{2,1,0:T(8,128)(2,1)} %get-tuple-element.31.refs_1_), channel_id=1, source_target_pairs={{0,1},{1,0},{2,3},{3,2},{4,5},{5,4},{6,7},{7,6},{8,9},{9,8},{10,11... | collective-permute-start | bytes 1572872 | tf_op jit(solution)/shard_map/ppermute | solution.py:88
  59.5 11.4 %copy-start.28 = (bf16[4,16,2048]{2,1,0:T(8,128)(2,1)S(1)}, bf16[4,16,2048]{2,1,0:T(8,128)(2,1)}, u32[]{:S(2)}) copy-start(bf16[4,16,2048]{2,1,0:T(8,128)(2,1)} %copy-done.26) | copy-start | bytes 786436
  59.5 11.4 %copy-start.31 = (bf16[4,16,2048]{2,1,0:T(8,128)(2,1)S(1)}, bf16[4,16,2048]{2,1,0:T(8,128)(2,1)}, u32[]{:S(2)}) copy-start(bf16[4,16,2048]{2,1,0:T(8,128)(2,1)} %copy-done.29) | copy-start | bytes 786436
  70.2 12.7 %copy-start.52 = (bf16[16,2048]{1,0:T(8,128)(2,1)S(1)}, bf16[16,2048]{1,0:T(8,128)(2,1)}, u32[]{:S(2)}) copy-start(bf16[16,2048]{1,0:T(8,128)(2,1)} %get-tuple-element.38.refs_0_) | copy-start | bytes 196612
  70.2 12.2 %collective-permute-start.15 = (bf16[4,16,4096]{2,1,0:T(8,128)(2,1)S(1)}, bf16[4,16,4096]{2,1,0:T(8,128)(2,1)S(1)}, u32[]{:S(2)}, u32[]{:S(2)}) collective-permute-start(bf16[4,16,4096]{2,1,0:T(8,128)(2,1)S(1)} %collective-permute-done.13.refs_2_.refs_7_), channel_id=1, source_target_pairs={{0,4},{1,3},{2,6},{3,1},{4,0},{5,7},{6,2},{7,5},{8,12},{9,11},{10,... | collective-permute-start | bytes 1572872 | tf_op jit(solution)/shard_map/ppermute | solution.py:88
  70.3 33.1 %collective-permute-start.17 = (bf16[4,16,4096]{2,1,0:T(8,128)(2,1)S(1)}, bf16[4,16,4096]{2,1,0:T(8,128)(2,1)}, u32[]{:S(2)}, u32[]{:S(2)}) collective-permute-start(bf16[4,16,4096]{2,1,0:T(8,128)(2,1)S(1)} %collective-permute-done.13.refs_2_.refs_7_), channel_id=1, source_target_pairs={{0,1},{1,0},{2,3},{3,2},{4,5},{5,4},{6,7},{7,6},{8,9},{9,8},{10,11... | collective-permute-start | bytes 1572872 | tf_op jit(solution)/shard_map/ppermute | solution.py:88
  82.4 16.4 %copy-start.4 = (bf16[4,16,4096]{2,1,0:T(8,128)(2,1)}, bf16[4,16,4096]{2,1,0:T(8,128)(2,1)S(1)}, u32[]{:S(2)}) copy-start(bf16[4,16,4096]{2,1,0:T(8,128)(2,1)S(1)} %collective-permute-done.14.refs_3_.refs_8_) | copy-start | bytes 1572868
  82.4 21.0 %collective-permute-start.18 = (bf16[4,16,4096]{2,1,0:T(8,128)(2,1)S(1)}, bf16[4,16,4096]{2,1,0:T(8,128)(2,1)S(1)}, u32[]{:S(2)}, u32[]{:S(2)}) collective-permute-start(bf16[4,16,4096]{2,1,0:T(8,128)(2,1)S(1)} %collective-permute-done.14.refs_3_.refs_8_), channel_id=1, source_target_pairs={{0,1},{1,0},{2,3},{3,2},{4,5},{5,4},{6,7},{7,6},{8,9},{9,8},{10,11... | collective-permute-start | bytes 1572872 | tf_op jit(solution)/shard_map/ppermute | solution.py:88
  82.5 25.6 %copy-start.17 = (bf16[4,16,4096]{2,1,0:T(8,128)(2,1)}, bf16[4,16,4096]{2,1,0:T(8,128)(2,1)S(1)}, u32[]{:S(2)}) copy-start(bf16[4,16,4096]{2,1,0:T(8,128)(2,1)S(1)} %collective-permute-done.15.refs_4_) | copy-start | bytes 1572868
  82.5 24.8 %collective-permute-start.19 = (bf16[4,16,4096]{2,1,0:T(8,128)(2,1)S(1)}, bf16[4,16,4096]{2,1,0:T(8,128)(2,1)}, u32[]{:S(2)}, u32[]{:S(2)}) collective-permute-start(bf16[4,16,4096]{2,1,0:T(8,128)(2,1)S(1)} %collective-permute-done.15.refs_4_), channel_id=1, source_target_pairs={{0,1},{1,0},{2,3},{3,2},{4,5},{5,4},{6,7},{7,6},{8,9},{9,8},{10,11... | collective-permute-start | bytes 1572872 | tf_op jit(solution)/shard_map/ppermute | solution.py:88
  82.9 25.1 %copy-start.3 = (bf16[4,16,4096]{2,1,0:T(8,128)(2,1)S(1)}, bf16[4,16,4096]{2,1,0:T(8,128)(2,1)}, u32[]{:S(2)}) copy-start(bf16[4,16,4096]{2,1,0:T(8,128)(2,1)} %copy-done.2) | copy-start | bytes 1572868
  82.9 25.1 %copy-start.16 = (bf16[4,16,4096]{2,1,0:T(8,128)(2,1)S(1)}, bf16[4,16,4096]{2,1,0:T(8,128)(2,1)}, u32[]{:S(2)}) copy-start(bf16[4,16,4096]{2,1,0:T(8,128)(2,1)} %get-tuple-element.31.refs_1_) | copy-start | bytes 1572868
  82.9 6.1 %collective-permute-start.23 = (bf16[16,2048]{1,0:T(8,128)(2,1)S(1)}, bf16[16,2048]{1,0:T(8,128)(2,1)S(1)}, u32[]{:S(2)}, u32[]{:S(2)}) collective-permute-start(bf16[16,2048]{1,0:T(8,128)(2,1)S(1)} %copy-done.52), channel_id=1, source_target_pairs={{0,8},{1,9},{2,10},{3,11},{4,12},{5,13},{6,14},{7,15},{8,16},{9,17... | collective-permute-start | bytes 196616 | tf_op jit(solution)/shard_map/ppermute | solution.py:88
  89.0 5.5 %collective-permute-start.24 = (bf16[16,2048]{1,0:T(8,128)(2,1)S(1)}, bf16[16,2048]{1,0:T(8,128)(2,1)S(1)}, u32[]{:S(2)}, u32[]{:S(2)}) collective-permute-start(bf16[16,2048]{1,0:T(8,128)(2,1)S(1)} %copy-done.52), channel_id=1, source_target_pairs={{0,16},{1,17},{2,18},{3,19},{4,20},{5,21},{6,22},{7,23},{8,24},{9,... | collective-permute-start | bytes 196616 | tf_op jit(solution)/shard_map/ppermute | solution.py:88
  94.5 4.3 %collective-permute-start.25 = (bf16[16,2048]{1,0:T(8,128)(2,1)S(1)}, bf16[16,2048]{1,0:T(8,128)(2,1)S(1)}, u32[]{:S(2)}, u32[]{:S(2)}) collective-permute-start(bf16[16,2048]{1,0:T(8,128)(2,1)S(1)} %copy-done.52), channel_id=1, source_target_pairs={{0,24},{1,25},{2,26},{3,27},{4,28},{5,29},{6,30},{7,31},{8,0},{9,1... | collective-permute-start | bytes 196616 | tf_op jit(solution)/shard_map/ppermute | solution.py:88
  101.4 21.2 %collective-permute-start.26 = (bf16[4,16,2048]{2,1,0:T(8,128)(2,1)}, bf16[4,16,2048]{2,1,0:T(8,128)(2,1)}, u32[]{:S(2)}, u32[]{:S(2)}) collective-permute-start(bf16[4,16,2048]{2,1,0:T(8,128)(2,1)} %get-tuple-element.39.refs_4_), channel_id=1, source_target_pairs={{0,2},{1,5},{2,0},{3,7},{4,6},{5,1},{6,4},{7,3},{8,10},{9,13},{10,... | collective-permute-start | bytes 786440 | tf_op jit(solution)/shard_map/ppermute | solution.py:88
  103.1 20.1 %collective-permute-start.27 = (bf16[4,16,2048]{2,1,0:T(8,128)(2,1)}, bf16[4,16,2048]{2,1,0:T(8,128)(2,1)}, u32[]{:S(2)}, u32[]{:S(2)}) collective-permute-start(bf16[4,16,2048]{2,1,0:T(8,128)(2,1)} %get-tuple-element.39.refs_4_), channel_id=1, source_target_pairs={{0,4},{1,3},{2,6},{3,1},{4,0},{5,7},{6,2},{7,5},{8,12},{9,11},{10,... | collective-permute-start | bytes 786440 | tf_op jit(solution)/shard_map/ppermute | solution.py:88
  103.4 19.3 %collective-permute-start.34 = (bf16[16,4096]{1,0:T(8,128)(2,1)}, bf16[16,4096]{1,0:T(8,128)(2,1)S(1)}, u32[]{:S(2)}, u32[]{:S(2)}) collective-permute-start(bf16[16,4096]{1,0:T(8,128)(2,1)} %get-tuple-element.44.refs_0_), channel_id=1, source_target_pairs={{0,8},{1,9},{2,10},{3,11},{4,12},{5,13},{6,14},{7,15},{8,16},{9,17... | collective-permute-start | bytes 393224 | tf_op jit(solution)/shard_map/ppermute | solution.py:88
  104.2 19.1 %collective-permute-start.35 = (bf16[16,4096]{1,0:T(8,128)(2,1)}, bf16[16,4096]{1,0:T(8,128)(2,1)}, u32[]{:S(2)}, u32[]{:S(2)}) collective-permute-start(bf16[16,4096]{1,0:T(8,128)(2,1)} %get-tuple-element.44.refs_0_), channel_id=1, source_target_pairs={{0,16},{1,17},{2,18},{3,19},{4,20},{5,21},{6,22},{7,23},{8,24},{9,... | collective-permute-start | bytes 393224 | tf_op jit(solution)/shard_map/ppermute | solution.py:88
  107.2 17.8 %collective-permute-start.36 = (bf16[16,4096]{1,0:T(8,128)(2,1)}, bf16[16,4096]{1,0:T(8,128)(2,1)}, u32[]{:S(2)}, u32[]{:S(2)}) collective-permute-start(bf16[16,4096]{1,0:T(8,128)(2,1)} %get-tuple-element.44.refs_0_), channel_id=1, source_target_pairs={{0,24},{1,25},{2,26},{3,27},{4,28},{5,29},{6,30},{7,31},{8,0},{9,1... | collective-permute-start | bytes 393224 | tf_op jit(solution)/shard_map/ppermute | solution.py:88
  122.6 17.6 %collective-permute-start.29 = (bf16[4,16,2048]{2,1,0:T(8,128)(2,1)}, bf16[4,16,2048]{2,1,0:T(8,128)(2,1)}, u32[]{:S(2)}, u32[]{:S(2)}) collective-permute-start(bf16[4,16,2048]{2,1,0:T(8,128)(2,1)} %get-tuple-element.39.refs_4_), channel_id=1, source_target_pairs={{0,1},{1,0},{2,3},{3,2},{4,5},{5,4},{6,7},{7,6},{8,9},{9,8},{10,11... | collective-permute-start | bytes 786440 | tf_op jit(solution)/shard_map/ppermute | solution.py:88
  122.7 18.3 %collective-permute-start.30 = (bf16[4,16,2048]{2,1,0:T(8,128)(2,1)}, bf16[4,16,2048]{2,1,0:T(8,128)(2,1)}, u32[]{:S(2)}, u32[]{:S(2)}) collective-permute-start(bf16[4,16,2048]{2,1,0:T(8,128)(2,1)} %collective-permute-done.26.refs_5_), channel_id=1, source_target_pairs={{0,1},{1,0},{2,3},{3,2},{4,5},{5,4},{6,7},{7,6},{8,9},{9,8},{10,11... | collective-permute-start | bytes 786440 | tf_op jit(solution)/shard_map/ppermute | solution.py:88
  123.2 19.4 %collective-permute-start.31 = (bf16[4,16,2048]{2,1,0:T(8,128)(2,1)}, bf16[4,16,2048]{2,1,0:T(8,128)(2,1)}, u32[]{:S(2)}, u32[]{:S(2)}) collective-permute-start(bf16[4,16,2048]{2,1,0:T(8,128)(2,1)} %collective-permute-done.27.refs_6_), channel_id=1, source_target_pairs={{0,1},{1,0},{2,3},{3,2},{4,5},{5,4},{6,7},{7,6},{8,9},{9,8},{10,11... | collective-permute-start | bytes 786440 | tf_op jit(solution)/shard_map/ppermute | solution.py:88
  123.3 17.0 %collective-permute-start.28 = (bf16[4,16,2048]{2,1,0:T(8,128)(2,1)}, bf16[4,16,2048]{2,1,0:T(8,128)(2,1)}, u32[]{:S(2)}, u32[]{:S(2)}) collective-permute-start(bf16[4,16,2048]{2,1,0:T(8,128)(2,1)} %collective-permute-done.26.refs_5_), channel_id=1, source_target_pairs={{0,4},{1,3},{2,6},{3,1},{4,0},{5,7},{6,2},{7,5},{8,12},{9,11},{10,... | collective-permute-start | bytes 786440 | tf_op jit(solution)/shard_map/ppermute | solution.py:88
  127.0 15.6 %copy-start.7 = (bf16[4,16,4096]{2,1,0:T(8,128)(2,1)S(1)}, bf16[4,16,4096]{2,1,0:T(8,128)(2,1)}, u32[]{:S(2)}) copy-start(bf16[4,16,4096]{2,1,0:T(8,128)(2,1)} %shard_map.137.refs_1_) | copy-start | bytes 1572868
  127.0 13.8 %collective-permute-start.37 = (bf16[4,16,4096]{2,1,0:T(8,128)(2,1)}, bf16[4,16,4096]{2,1,0:T(8,128)(2,1)S(1)}, u32[]{:S(2)}, u32[]{:S(2)}) collective-permute-start(bf16[4,16,4096]{2,1,0:T(8,128)(2,1)} %shard_map.137.refs_1_), channel_id=1, source_target_pairs={{0,2},{1,5},{2,0},{3,7},{4,6},{5,1},{6,4},{7,3},{8,10},{9,13},{10,... | collective-permute-start | bytes 1572872 | tf_op jit(solution)/shard_map/ppermute | solution.py:88
  129.4 17.0 %copy-start.38 = (f32[144,256]{1,0:T(8,128)S(1)}, f32[144,256]{1,0:T(8,128)}, u32[]{:S(2)}) copy-start(f32[144,256]{1,0:T(8,128)} %constant.7.clone.refs_15_) | copy-start | bytes 442372
  140.2 5.3 %collective-permute-start.32 = (bf16[4,16,2048]{2,1,0:T(8,128)(2,1)}, bf16[4,16,2048]{2,1,0:T(8,128)(2,1)S(1)}, u32[]{:S(2)}, u32[]{:S(2)}) collective-permute-start(bf16[4,16,2048]{2,1,0:T(8,128)(2,1)} %collective-permute-done.28.refs_7_), channel_id=1, source_target_pairs={{0,1},{1,0},{2,3},{3,2},{4,5},{5,4},{6,7},{7,6},{8,9},{9,8},{10,11... | collective-permute-start | bytes 786440 | tf_op jit(solution)/shard_map/ppermute | solution.py:88
  140.3 3.9 %collective-permute-start.21 = (bf16[2,36,512]{2,1,0:T(8,128)(2,1)S(1)}, bf16[2,36,512]{2,1,0:T(8,128)(2,1)S(1)}, u32[]{:S(2)}, u32[]{:S(2)}) collective-permute-start(bf16[2,36,512]{2,1,0:T(8,128)(2,1)S(1)} %get-tuple-element.37), channel_id=1, source_target_pairs={{1,0},{0,1},{3,2},{2,3},{5,4},{4,5},{7,6},{6,7},{9,8},{8,9},{11,10... | collective-permute-start | bytes 221192 | tf_op jit(solution)/shard_map/ppermute | solution.py:337
  140.8 3.4 %collective-permute-start.33 = (bf16[2,36,512]{2,1,0:T(8,128)(2,1)S(1)}, bf16[2,36,512]{2,1,0:T(8,128)(2,1)S(1)}, u32[]{:S(2)}, u32[]{:S(2)}) collective-permute-start(bf16[2,36,512]{2,1,0:T(8,128)(2,1)S(1)} %copy-done.15), channel_id=1, source_target_pairs={{1,0},{0,1},{3,2},{2,3},{5,4},{4,5},{7,6},{6,7},{9,8},{8,9},{11,10... | collective-permute-start | bytes 221192 | tf_op jit(solution)/shard_map/ppermute | solution.py:337
  141.0 22.8 %collective-permute-start.22 = (bf16[2,36,512]{2,1,0:T(8,128)(2,1)S(1)}, bf16[2,36,512]{2,1,0:T(8,128)(2,1)S(1)}, u32[]{:S(2)}, u32[]{:S(2)}) collective-permute-start(bf16[2,36,512]{2,1,0:T(8,128)(2,1)S(1)} %copy-done.15), channel_id=1, source_target_pairs={{3,0},{2,1},{5,2},{4,3},{7,4},{6,5},{9,6},{8,7},{11,8},{10,9},{13,... | collective-permute-start | bytes 221192 | tf_op jit(solution)/shard_map/ppermute | solution.py:337
  142.6 15.5 %collective-permute-start.38 = (bf16[4,16,4096]{2,1,0:T(8,128)(2,1)S(1)}, bf16[4,16,4096]{2,1,0:T(8,128)(2,1)S(1)}, u32[]{:S(2)}, u32[]{:S(2)}) collective-permute-start(bf16[4,16,4096]{2,1,0:T(8,128)(2,1)S(1)} %copy-done.7), channel_id=1, source_target_pairs={{0,4},{1,3},{2,6},{3,1},{4,0},{5,7},{6,2},{7,5},{8,12},{9,11},{10,... | collective-permute-start | bytes 1572872 | tf_op jit(solution)/shard_map/ppermute | solution.py:88
  144.2 28.4 %collective-permute-start.40 = (bf16[4,16,4096]{2,1,0:T(8,128)(2,1)S(1)}, bf16[4,16,4096]{2,1,0:T(8,128)(2,1)S(1)}, u32[]{:S(2)}, u32[]{:S(2)}) collective-permute-start(bf16[4,16,4096]{2,1,0:T(8,128)(2,1)S(1)} %copy-done.7), channel_id=1, source_target_pairs={{0,1},{1,0},{2,3},{3,2},{4,5},{5,4},{6,7},{7,6},{8,9},{9,8},{10,11... | collective-permute-start | bytes 1572872 | tf_op jit(solution)/shard_map/ppermute | solution.py:88
  144.2 19.6 %collective-permute-start.20 = (bf16[4,2,36,512]{3,2,1,0:T(8,128)(2,1)}, bf16[4,2,36,512]{3,2,1,0:T(8,128)(2,1)S(1)}, u32[]{:S(2)}, u32[]{:S(2)}) collective-permute-start(bf16[4,2,36,512]{3,2,1,0:T(8,128)(2,1)} %copy-done.22), channel_id=1, source_target_pairs={{2,0},{3,1},{4,2},{5,3},{6,4},{7,5},{8,6},{9,7},{10,8},{11,9},{12,... | collective-permute-start | bytes 884744 | tf_op jit(solution)/shard_map/ppermute | solution.py:337
  145.5 12.7 %collective-permute-start.39 = (bf16[4,16,4096]{2,1,0:T(8,128)(2,1)S(1)}, bf16[4,16,4096]{2,1,0:T(8,128)(2,1)S(1)}, u32[]{:S(2)}, u32[]{:S(2)}) collective-permute-start(bf16[4,16,4096]{2,1,0:T(8,128)(2,1)S(1)} %collective-permute-done.37.refs_2_), channel_id=1, source_target_pairs={{0,4},{1,3},{2,6},{3,1},{4,0},{5,7},{6,2},{7,5},{8,12},{9,11},{10,... | collective-permute-start | bytes 1572872 | tf_op jit(solution)/shard_map/ppermute | solution.py:88
  149.4 14.4 %copy-start.37 = (bf16[1152,256]{1,0:T(8,128)(2,1)S(1)}, bf16[1152,256]{1,0:T(8,128)(2,1)}, u32[]{:S(2)}) copy-start(bf16[1152,256]{1,0:T(8,128)(2,1)} %constant.6.clone.refs_11_.refs_14_) | copy-start | bytes 1769476
  149.4 14.4 %copy-start.42 = (bf16[4,2,36,512]{3,2,1,0:T(8,128)(2,1)S(1)}, bf16[4,2,36,512]{3,2,1,0:T(8,128)(2,1)}, u32[]{:S(2)}) copy-start(bf16[4,2,36,512]{3,2,1,0:T(8,128)(2,1)} %copy-done.41) | copy-start | bytes 884740
  158.1 14.5 %collective-permute-start.41 = (bf16[4,16,4096]{2,1,0:T(8,128)(2,1)S(1)}, bf16[4,16,4096]{2,1,0:T(8,128)(2,1)S(1)}, u32[]{:S(2)}, u32[]{:S(2)}) collective-permute-start(bf16[4,16,4096]{2,1,0:T(8,128)(2,1)S(1)} %collective-permute-done.37.refs_2_), channel_id=1, source_target_pairs={{0,1},{1,0},{2,3},{3,2},{4,5},{5,4},{6,7},{7,6},{8,9},{9,8},{10,11... | collective-permute-start | bytes 1572872 | tf_op jit(solution)/shard_map/ppermute | solution.py:88
  158.2 14.4 %collective-permute-start.42 = (bf16[4,16,4096]{2,1,0:T(8,128)(2,1)S(1)}, bf16[4,16,4096]{2,1,0:T(8,128)(2,1)S(1)}, u32[]{:S(2)}, u32[]{:S(2)}) collective-permute-start(bf16[4,16,4096]{2,1,0:T(8,128)(2,1)S(1)} %collective-permute-done.38.refs_3_), channel_id=1, source_target_pairs={{0,1},{1,0},{2,3},{3,2},{4,5},{5,4},{6,7},{7,6},{8,9},{9,8},{10,11... | collective-permute-start | bytes 1572872 | tf_op jit(solution)/shard_map/ppermute | solution.py:88
  163.8 8.8 %collective-permute-start.43 = (bf16[4,16,4096]{2,1,0:T(8,128)(2,1)S(1)}, bf16[4,16,4096]{2,1,0:T(8,128)(2,1)S(1)}, u32[]{:S(2)}, u32[]{:S(2)}) collective-permute-start(bf16[4,16,4096]{2,1,0:T(8,128)(2,1)S(1)} %collective-permute-done.39.refs_4_), channel_id=1, source_target_pairs={{0,1},{1,0},{2,3},{3,2},{4,5},{5,4},{6,7},{7,6},{8,9},{9,8},{10,11... | collective-permute-start | bytes 1572872 | tf_op jit(solution)/shard_map/ppermute | solution.py:88
  193.6 5.0 %collective-permute-start.46 = (bf16[2,36,512]{2,1,0:T(8,128)(2,1)S(1)}, bf16[2,36,512]{2,1,0:T(8,128)(2,1)S(1)}, u32[]{:S(2)}, u32[]{:S(2)}) collective-permute-start(bf16[2,36,512]{2,1,0:T(8,128)(2,1)S(1)} %get-tuple-element.49), channel_id=1, source_target_pairs={{1,0},{0,1},{3,2},{2,3},{5,4},{4,5},{7,6},{6,7},{9,8},{8,9},{11,10... | collective-permute-start | bytes 221192 | tf_op jit(solution)/shard_map/ppermute | solution.py:337
  194.1 14.2 %collective-permute-start.45 = (bf16[4,2,36,512]{3,2,1,0:T(8,128)(2,1)S(1)}, bf16[4,2,36,512]{3,2,1,0:T(8,128)(2,1)S(1)}, u32[]{:S(2)}, u32[]{:S(2)}) collective-permute-start(bf16[4,2,36,512]{3,2,1,0:T(8,128)(2,1)S(1)} %get-tuple-element.48), channel_id=1, source_target_pairs={{30,0},{31,1},{0,2},{1,3},{2,4},{3,5},{4,6},{5,7},{6,8},{7,9},{8,1... | collective-permute-start | bytes 884744 | tf_op jit(solution)/shard_map/ppermute | solution.py:337
  197.0 1.7 collective-permute-start.47
  197.1 11.1 %collective-permute-start.44 = (bf16[2,36,512]{2,1,0:T(8,128)(2,1)S(1)}, bf16[2,36,512]{2,1,0:T(8,128)(2,1)S(1)}, u32[]{:S(2)}, u32[]{:S(2)}) collective-permute-start(bf16[2,36,512]{2,1,0:T(8,128)(2,1)S(1)} %get-tuple-element.47.refs_10_), channel_id=1, source_target_pairs={{31,0},{30,1},{1,2},{0,3},{3,4},{2,5},{5,6},{4,7},{7,8},{6,9},{9,1... | collective-permute-start | bytes 221192 | tf_op jit(solution)/shard_map/ppermute | solution.py:337
  (45 other events, 147.9 us)

commit v6 on v5

v6 whole, which is shorter than its diff:
```python
import functools
import math

import numpy as np

import jax
import jax.numpy as jnp
from jax import lax
from jax.experimental import pallas as pl
from jax.experimental.pallas import tpu as pltpu
from jax.sharding import PartitionSpec as P

HEADS = 16
HEAD = 32
WLON = 12
WLAT = 6
LEVELS = 2
CELLS = WLON * WLAT * LEVELS
MAIN = 128
REST = CELLS - MAIN
QUARTER = CELLS // 4
GROUP = 8
WIDE = GROUP * HEAD
ANY = pl.BlockSpec(memory_space=pl.ANY)
NT = (((1,), (1,)), ((), ()))


def dot(a, b, dims=(((1,), (0,)), ((), ()))):
    return lax.dot_general(a, b, dims, preferred_element_type=jnp.float32)


def layer_norm(value, gain_row):
    averaged = jnp.mean(value, -1, keepdims=True)
    centred = value - averaged
    variance = jnp.mean(centred * centred, -1, keepdims=True)
    return centred * lax.rsqrt(variance + 1e-05) * gain_row


def relayed(rows, lat_size):
    return lat_size == 2 and rows % 32 == 0


def join_kernel(sizes, cuts, waits, *refs):
    outs = refs[len(refs) - len(sizes) - len(cuts) :]
    place = 0
    for size, column_ref in zip(sizes, outs):
        for index in range(size):
            column_ref[index] = refs[place + index][...]
        place += size
    for (block, count), chunk_ref in zip(cuts, outs[len(sizes) :]):
        half = chunk_ref.shape[0]
        first = pl.multiple_of(lax.axis_index("lat") * half, 16)
        start = 0
        for source in refs[place : place + count]:
            width = source.shape[2]
            chunk_ref[:, start : start + width] = source[block, pl.ds(first, half), :]
            start += width
        place += count


def join(columns, cuts=(), after=()):
    pieces = [piece for column in columns for piece in column]
    sources = [weight for _, weights in cuts for weight in weights]
    out_shape = [
        jax.ShapeDtypeStruct((len(column),) + column[0].shape, jnp.bfloat16) for column in columns
    ]
    for _, weights in cuts:
        width = sum(weight.shape[2] for weight in weights)
        out_shape.append(jax.ShapeDtypeStruct((weights[0].shape[1] // 2, width), jnp.bfloat16))
    kernel = functools.partial(
        join_kernel,
        [len(column) for column in columns],
        [(block, len(weights)) for block, weights in cuts],
        len(after),
    )
    held = pl.BlockSpec(memory_space=pltpu.VMEM)
    return pl.pallas_call(
        kernel,
        out_shape=out_shape,
        in_specs=[held] * (len(pieces) + len(sources)) + [ANY] * len(after),
        compiler_params=pltpu.CompilerParams(vmem_limit_bytes=8 * 2**20),
    )(*pieces, *sources, *after)


def send(block, move):
    pairs = []
    for lon in range(lax.axis_size("lon")):
        for core in range(2):
            z, y, x, core_to = move(lon // 4, lon // 2 % 2, lon % 2, core)
            pairs.append((lon * 2 + core, (z * 4 + y * 2 + x) * 2 + core_to))
    return lax.ppermute(block, ("lon", "lat"), pairs)


def along_z(own):
    depth = lax.axis_size("lon") // 4
    return [own] + [
        send(own, lambda z, y, x, c, step=step: ((z + step) % depth, y, x, c))
        for step in range(1, depth)
    ]


def swap(z, y, x, c):
    return z, y, x, 1 - c


def tied(array, after):
    return lax.optimization_barrier((array, after))[0]


def to_neighbours(column):
    return [
        send(column, lambda z, y, x, c: (z, y, 1 - x, c)),
        send(column, lambda z, y, x, c: (z, 1 - y, x, c)),
        send(column, lambda z, y, x, c: (z, 1 - y, 1 - x, c)),
    ]


def whole_pieces(column, received, after=None):
    sent = received if after is None else [tied(part, after) for part in received]
    return [column] + received + [send(part, swap) for part in [column] + sent]


def load_pieces(pieces, w_ref, stage_ref, sem):
    if len(pieces) == 1:
        copy = pltpu.make_async_copy(pieces[0], w_ref, sem.at[0])
        copy.start()
        copy.wait()
        return
    depth, half, _ = pieces[0].shape
    copies = [
        pltpu.make_async_copy(piece, stage_ref.at[index], sem.at[index])
        for index, piece in enumerate(pieces)
    ]
    for copy in copies:
        copy.start()
    lon, lat = lax.axis_index("lon"), lax.axis_index("lat")
    z, y, x = lon // 4, lon // 2 % 2, lon % 2
    squares = (y * 2 + x, y * 2 + 1 - x, (1 - y) * 2 + x, (1 - y) * 2 + 1 - x)
    for index, copy in enumerate(copies):
        core = lat if index < 4 else 1 - lat
        copy.wait()
        for step in range(depth):
            shard = (z + depth - step) % depth * 4 + squares[index % 4]
            row = pl.multiple_of((shard * 2 + core) * half, 16)
            w_ref[pl.ds(row, half), :] = stage_ref[index, step]


def load_scratch(pieces, rows, width):
    stage = (len(pieces),) + pieces[0].shape if len(pieces) > 1 else (1, 1, 16, 128)
    return [
        pltpu.VMEM((rows, width), jnp.bfloat16),
        pltpu.VMEM(stage, jnp.bfloat16),
        pltpu.SemaphoreType.DMA((len(pieces),)),
    ]


def rolled_window(place, row_windows, sides, ahead_ref, low_ref, ahead_low_ref):
    (left_0, right_0), (left_1, right_1) = sides
    first = place < row_windows
    row = place % row_windows
    following = jnp.minimum(row + 1, row_windows - 1)
    wide = lambda quarter: quarter.astype(jnp.float32)
    pick = lambda a, b: jnp.where(first, wide(a), wide(b))
    low = lambda quarter, value: jnp.where(row == row_windows - 1, quarter, value)
    quarters = [
        pick(right_0[row, 1], right_1[row, 1]),
        low(pick(low_ref[1], low_ref[3]), pick(right_0[following, 0], right_1[following, 0])),
        pick(left_1[row, 1], ahead_ref[row, 1]),
        low(pick(low_ref[2], ahead_low_ref[0]), pick(left_1[following, 0], ahead_ref[following, 0])),
    ]
    return jnp.concatenate(quarters, 0).astype(jnp.bfloat16)


def attend_kernel(shifted, row_windows, count, *refs):
    sources = 7 if shifted else 1
    x_refs, pieces = refs[:sources], refs[sources : sources + count]
    gain_ref, sharp_ref, ones_ref = refs[sources + count : sources + count + 3]
    allow_ref = refs[sources + count + 3] if shifted else None
    out_ref, w_ref, stage_ref, sem = refs[-4:]
    held, _, features = out_ref.shape

    @pl.when(pl.program_id(0) == 0)
    def _():
        load_pieces(pieces, w_ref, stage_ref, sem)

    if shifted:
        sides = (x_refs[0:2], x_refs[2:4])
        tokens = jnp.concatenate(
            [
                rolled_window(pl.program_id(0) * held + window, row_windows, sides, *x_refs[4:])
                for window in range(held)
            ],
            0,
        )
    else:
        tokens = x_refs[0][...].reshape(held * CELLS, features)
    channel = lax.broadcasted_iota(jnp.int32, (WIDE, WIDE), 0) // HEAD
    same_head = jnp.where(
        channel == lax.broadcasted_iota(jnp.int32, (WIDE, WIDE), 1) // HEAD, 1.0, 0.0
    ).astype(jnp.bfloat16)
    lane_head = lax.broadcasted_iota(jnp.int32, (1, WIDE), 1) // HEAD
    masks = [jnp.where(lane_head == head, 1.0, 0.0).astype(jnp.bfloat16) for head in range(GROUP)]

    def units(part):
        rounded = part.astype(jnp.bfloat16)
        length2 = dot(rounded * rounded, same_head)
        return part * lax.rsqrt(jnp.maximum(length2, 0.25 * HEAD))

    attended = [[] for _ in range(held)]
    for group in range(HEADS // GROUP):
        lanes = [slice(n * features + group * WIDE, n * features + (group + 1) * WIDE) for n in range(3)]
        queries = (units(dot(tokens, w_ref[:, lanes[0]])) * sharp_ref[:, lanes[0]]).astype(jnp.bfloat16)
        keys = units(dot(tokens, w_ref[:, lanes[1]])).astype(jnp.bfloat16)
        values = dot(tokens, w_ref[:, lanes[2]]).astype(jnp.bfloat16)
        for window in range(held):
            own = slice(window * CELLS, (window + 1) * CELLS)
            query, key, value = queries[own], keys[own], values[own]
            stacked = jnp.concatenate([query * mask for mask in masks], 0)
            main = jnp.exp2(dot(stacked, key[:MAIN], NT)).astype(jnp.bfloat16)
            rest_keys = jnp.concatenate([key[MAIN:] * mask for mask in masks], 0)
            rest = jnp.exp2(dot(query, rest_keys, NT)).astype(jnp.bfloat16)
            parts = [main[head * CELLS : (head + 1) * CELLS] for head in range(GROUP)] + [rest]
            if shifted:
                last = jnp.logical_and(
                    (pl.program_id(0) * held + window) % row_windows == row_windows - 1,
                    lax.axis_index("lat") == lax.axis_size("lat") - 1,
                )
                allow = jnp.where(last, allow_ref[...], 1.0).astype(jnp.bfloat16)
                parts = [part * allow[:, :MAIN] for part in parts[:-1]] + [rest * allow[:, MAIN:]]
            weights = jnp.concatenate(parts, 1)
            stacked = jnp.concatenate(
                [value[:MAIN] * mask for mask in masks] + [value[MAIN:] * mask for mask in masks], 0
            )
            total = dot(weights, ones_ref[...])
            attended[window].append((dot(weights, stacked) / total).astype(jnp.bfloat16))
    attended = jnp.concatenate([jnp.concatenate(parts, 1) for parts in attended], 0)
    projected = dot(attended, w_ref[:, 3 * features :])
    middle = tokens.astype(jnp.float32) + layer_norm(projected, gain_ref[...])
    out_ref[...] = middle.astype(jnp.bfloat16).reshape(out_ref.shape)


def allowed_pairs():
    side = np.arange(CELLS) // QUARTER % 2
    rest = np.tile(side[MAIN:], GROUP)
    return (side[:, None] == np.concatenate([side[:MAIN], rest])[None, :]).astype(np.float32)


def head_columns():
    rows = np.concatenate([np.repeat(np.arange(GROUP), MAIN), np.repeat(np.arange(GROUP), REST)])
    return (rows[:, None] == np.arange(WIDE)[None, :] // HEAD).astype(np.float32)


def attend(sources, pieces, gain, sharp, row_windows, after=(), held=2):
    shifted = len(sources) > 1
    features = sources[0].shape[-1]
    count = 2 * row_windows
    whole = lambda shape: pl.BlockSpec(shape, lambda i: (0,) * len(shape))
    block = pl.BlockSpec((held, CELLS, features), lambda i: (i, 0, 0))
    ones = jnp.asarray(head_columns(), jnp.bfloat16)
    extra = (jnp.asarray(allowed_pairs()),) if shifted else ()
    return pl.pallas_call(
        functools.partial(attend_kernel, shifted, row_windows, len(pieces)),
        grid=(count // held,),
        out_shape=jax.ShapeDtypeStruct((count, CELLS, features), jnp.bfloat16),
        in_specs=([whole(source.shape) for source in sources] if shifted else [block])
        + [ANY] * len(pieces)
        + [whole((1, features))] * 2
        + [whole(ones.shape)]
        + [whole(e.shape) for e in extra]
        + [ANY] * len(after),
        out_specs=block,
        scratch_shapes=load_scratch(pieces, features, 4 * features),
        compiler_params=pltpu.CompilerParams(vmem_limit_bytes=24 * 2**20),
        cost_estimate=pl.CostEstimate(
            flops=count * 2_000_000_000, bytes_accessed=6_000_000, transcendentals=0
        ),
    )(*sources, *pieces, gain, sharp, ones, *extra, *after)


def feed_kernel(count, hidden_size, chunk, edge, *refs):
    x_ref, pieces, gain_ref = refs[0], refs[1 : 1 + count], refs[1 + count]
    left_ref, right_ref, edge_ref, w_ref, stage_ref, sem = refs[-6:]
    held, _, features = x_ref.shape

    @pl.when(pl.program_id(0) == 0)
    def _():
        load_pieces(pieces, w_ref, stage_ref, sem)

    tokens = x_ref[...].reshape(held * CELLS, features)
    total = jnp.zeros(tokens.shape, jnp.float32)
    for start in range(0, hidden_size, chunk):
        grown = dot(tokens, w_ref[:, start : start + chunk])
        slope = math.sqrt(2.0 / math.pi)
        bent = jnp.tanh(grown * (grown * grown * (0.044715 * slope) + slope))
        hidden = (grown + grown * bent).astype(jnp.bfloat16)
        total = total + dot(
            hidden, w_ref[:, hidden_size + start : hidden_size + start + chunk], NT
        )
    result = tokens.astype(jnp.float32) + layer_norm(0.5 * total, gain_ref[...])
    edge_window, edge_half = edge
    for window in range(held):
        for side, target in enumerate((left_ref, right_ref)):
            for half in range(2):
                start = window * CELLS + (side * 2 + half) * QUARTER
                quarter = result[start : start + QUARTER].astype(jnp.bfloat16)
                target[window, half] = quarter
                if half == edge_half and window == edge_window % held:

                    @pl.when(pl.program_id(0) == edge_window // held)
                    def _(quarter=quarter, side=side):
                        edge_ref[side] = quarter


def feed(windows, column, pieces, gain, hidden_size, edge, after=(), held=2):
    count, cells, features = windows.shape
    count = count // 2
    block = pl.BlockSpec((held, cells, features), lambda i: (i + column * count // held, 0, 0))
    side = pl.BlockSpec((held, 2, QUARTER, features), lambda i: (i, 0, 0, 0))
    return pl.pallas_call(
        functools.partial(feed_kernel, len(pieces), hidden_size, 512, edge),
        grid=(count // held,),
        out_shape=[jax.ShapeDtypeStruct((count, 2, QUARTER, features), jnp.bfloat16)] * 2
        + [jax.ShapeDtypeStruct((2, QUARTER, features), jnp.bfloat16)],
        in_specs=[block]
        + [ANY] * len(pieces)
        + [pl.BlockSpec((1, features), lambda i: (0, 0))]
        + [ANY] * len(after),
        out_specs=[side, side, pl.BlockSpec((2, QUARTER, features), lambda i: (0, 0, 0))],
        scratch_shapes=load_scratch(pieces, features, 2 * hidden_size),
        compiler_params=pltpu.CompilerParams(vmem_limit_bytes=24 * 2**20),
        cost_estimate=pl.CostEstimate(
            flops=8 * count * cells * features * hidden_size,
            bytes_accessed=8_000_000,
            transcendentals=0,
        ),
    )(windows, *pieces, gain, *after)


def shift_from(block, lon_step, lat_step):
    lons, lats = lax.axis_size("lon"), lax.axis_size("lat")
    pairs = []
    for lon in range(lons):
        for lat in range(lats):
            source = (lon + lon_step) % lons * lats + (lat + lat_step) % lats
            pairs.append((source, lon * lats + lat))
    return lax.ppermute(block, ("lon", "lat"), pairs)


def to_windows(cells):
    cols, rows, levels, features = cells.shape
    c, r = WLON // 2, WLAT // 2
    arranged = cells.reshape(cols // WLON, 2, c, rows // WLAT, 2, r, levels, features)
    arranged = arranged.transpose(0, 3, 1, 4, 2, 5, 6, 7)
    return arranged.reshape(-1, CELLS, features)


def strip(quarters):
    features = quarters.shape[-1]
    c, r = WLON // 2, WLAT // 2
    arranged = quarters.reshape(-1, c, r, LEVELS, features).transpose(1, 0, 2, 3, 4)
    return arranged.reshape(c, -1, LEVELS, features)


def back_in_place(sides, behind, below, corner):
    features = behind.shape[-1]
    flat = lambda side: side.reshape(-1, QUARTER, features)[:-1]
    c, r = WLON // 2, WLAT // 2
    own = jnp.concatenate([strip(flat(side)) for side in sides[:-1]], 0)
    tops = jnp.concatenate([strip(low[None]) for low in below], 0)
    first = jnp.concatenate([strip(corner[None]), strip(flat(behind))], 1)
    return jnp.concatenate([first, jnp.concatenate([tops, own], 1)], 0)


def per_device(tokens, qkv_weight, out_weight, up_weight, down_weight, norm_gain, logit_scale):
    cols, rows, _, features = tokens.shape
    hidden_size = up_weight.shape[-1]
    row_windows = rows // WLAT
    weights = (qkv_weight, out_weight, up_weight, down_weight)
    relay = relayed(qkv_weight.shape[1], lax.axis_size("lat"))
    spread = np.arange(HEADS)[:, None] == np.arange(features)[None, :] // HEAD
    sharp = logit_scale[:, :, None] * jnp.asarray(spread * math.log2(math.e), jnp.float32)[None]
    sharp = jnp.sum(sharp, 1)
    windows = to_windows(tokens)

    def attention(block, sources, pieces, after=()):
        return attend(
            sources, pieces, norm_gain[block, :1], sharp[block : block + 1], row_windows, after
        )

    def forward(block, middle, column, pieces, edge, after=()):
        return feed(middle, column, pieces, norm_gain[block, 1:], hidden_size, edge, after)

    low_edge, high_edge = (0, 0), (row_windows - 1, 1)
    if relay:
        attend_weights, feed_weights = weights[:2], weights[2:]
        (own,) = join([], [(0, attend_weights)])
        column, feed_own, own = join(
            [along_z(own)], [(0, feed_weights), (1, attend_weights)], (windows,)
        )
        pieces = whole_pieces(column, to_neighbours(column))
        feed_column, column, last_own = join(
            [along_z(feed_own), along_z(own)], [(1, feed_weights)]
        )
        feed_received = to_neighbours(feed_column)
        middle = attention(0, [windows], pieces, (feed_column,))
        feed_pieces = whole_pieces(feed_column, feed_received, middle)
        received = to_neighbours(tied(column, middle))
        left_0, right_0, low_0 = forward(0, middle, 0, feed_pieces, low_edge)
        left_1, right_1, low_1 = forward(0, middle, 1, feed_pieces, low_edge, (low_0,))
        pieces = whole_pieces(column, received, low_1)
        (last_column,) = join([along_z(last_own)], (), (low_1,))
        received = to_neighbours(last_column)
        after = (last_column,)
    else:
        gathered = []
        for block in range(2):
            for pair in (weights[:2], weights[2:]):
                chunk = jnp.concatenate([weight[block] for weight in pair], 1)
                gathered.append([lax.all_gather(chunk, "lon", axis=0, tiled=True)])
        first_pieces, feed_pieces, pieces, last_pieces = gathered
        middle = attention(0, [windows], first_pieces)
        left_0, right_0, low_0 = forward(0, middle, 0, feed_pieces, low_edge)
        left_1, right_1, low_1 = forward(0, middle, 1, feed_pieces, low_edge)
        after = ()
    ahead = shift_from(left_0, 1, 0)
    low = jnp.concatenate([low_0, low_1], 0)
    ahead_low = shift_from(low_0, 1, 1)
    below = shift_from(low, 0, 1)
    sources = [left_0, right_0, left_1, right_1, ahead, below, ahead_low]
    middle = attention(1, sources, pieces, after)
    if relay:
        last_pieces = whole_pieces(last_column, received, middle)
    left_1, right_1, high_1 = forward(1, middle, 1, last_pieces, high_edge)
    behind = shift_from(right_1, -1, 0)
    corner = shift_from(high_1, -1, -1)
    left_0, right_0, high_0 = forward(1, middle, 0, last_pieces, high_edge, (high_1,))
    above = shift_from(jnp.concatenate([high_0, high_1], 0), 0, -1)
    return back_in_place(
        (left_0, right_0, left_1, right_1), behind, (above[0], above[1], above[2]), corner[1]
    )


def solution(mesh):
    placed = (
        P("lon", "lat", None, None),
        P(None, "lon", None),
        P(None, "lon", None),
        P(None, "lon", None),
        P(None, "lon", None),
        P(),
        P(),
    )
    return jax.shard_map(
        per_device,
        mesh=mesh,
        in_specs=placed,
        out_specs=P("lon", "lat", None, None),
        check_vma=False,
    )
```

time: 213 us -> 151 us (0.71)
  Pallas kernels: 87.8 us -> 49.1 us
  local copies, waits for them, and re-layouts: 35 us -> 5.9 us
  waiting for transfers between devices: 42.9 us -> 47.4 us
  starting transfers between devices: 42.4 us -> 45.5 us
    unnamed x122 -> x22, local copies, waits for them, and re-layouts: 24 us -> 1.82 us
    pallas_call x4, Pallas kernels: 39.6 us -> 19.3 us  [feed(): pl.pallas_call(functools.partial(feed_kernel, len(pieces), hidden_size, 5...]
    pallas_call x5 -> x4, Pallas kernels: 9.47 us -> 0.14 us  [join(): pl.pallas_call(kernel, out_shape=out_shape, in_specs=[held] * (len(pieces...]
    pallas_call x4 -> x2, Pallas kernels: 38.7 us -> 29.6 us  [attend(): pl.pallas_call(functools.partial(attend_kernel, shifted, row_windows, len...]
    ppermute x8 -> x6, waiting for transfers between devices: 9.57 us -> 16.1 us  [shift_from(): return lax.ppermute(block, ('lon', 'lat'), pairs)]
    ppermute x40, starting transfers between devices: 35 us -> 40.4 us  [send(): return lax.ppermute(block, ('lon', 'lat'), pairs)]
    squeeze x3 -> x1, local copies, waits for them, and re-layouts: 4 us -> 0.01 us  [forward(): norm_gain[block, 1:]]
    ppermute x8 -> x6, starting transfers between devices: 7.43 us -> 5.08 us  [shift_from(): return lax.ppermute(block, ('lon', 'lat'), pairs)]
  transfers between devices with their start and end apart: 48 -> 46, of which waited for: 9 -> 18; matrix products, arithmetic and copies ran while one was open for 5% -> 3% of each run, Pallas kernels for 30% -> 26%
where the time goes in v6:
time: 151 us
  Pallas kernels  49.1 us (33%)
  waiting for transfers between devices  47.4 us (31%)
  starting transfers between devices  45.5 us (30%)
  local copies, waits for them, and re-layouts  5.9 us (4%)
  other arithmetic  3.04 us (2%)
    ppermute x40, starting transfers between devices, send(): return lax.ppermute(block, ('lon', 'lat'), pairs)  40.4 us
    ppermute x40, waiting for transfers between devices, send(): return lax.ppermute(block, ('lon', 'lat'), pairs)  31.3 us
    pallas_call x2, Pallas kernels, attend(): pl.pallas_call(functools.partial(attend_kernel, shifted, row_windows, len...  29.6 us
    pallas_call x4, Pallas kernels, feed(): pl.pallas_call(functools.partial(feed_kernel, len(pieces), hidden_size, 5...  19.3 us
    ppermute x6, waiting for transfers between devices, shift_from(): return lax.ppermute(block, ('lon', 'lat'), pairs)  16.1 us
    ppermute x6, starting transfers between devices, shift_from(): return lax.ppermute(block, ('lon', 'lat'), pairs)  5.08 us
  transfers between devices with their start and end apart: 46, of which 18 were waited for; matrix products, arithmetic and copies ran while one was open for 3% of the time, Pallas kernels for 26%

profile of v6, /device:TPU:0, one launch (start us, length us, event | category | flops | bytes accessed | tf_op | source)
XLA Modules:
  0.0 151.2 jit_solution(4753749960339101755)
XLA Ops:
  0.0 0.9 copy-done.2
  0.9 0.8 copy-done.4
  1.8 3.0 %collective-permute-start = (bf16[16,2048]{1,0:T(8,128)(2,1)S(1)}, bf16[16,2048]{1,0:T(8,128)(2,1)S(1)}, u32[]{:S(2)}, u32[]{:S(2)}) collective-permute-start(bf16[16,2048]{1,0:T(8,128)(2,1)S(1)} %shard_map.109.refs_0_), channel_id=1, source_target_pairs={{0,8},{1,9},{2,10},{3,11},{4,12},{5,13},{6,14},{7,15},{8,16},{9,17... | collective-permute-start | bytes 196616 | tf_op jit(solution)/shard_map/ppermute | solution.py:91
  4.8 2.6 %collective-permute-start.1 = (bf16[16,2048]{1,0:T(8,128)(2,1)S(1)}, bf16[16,2048]{1,0:T(8,128)(2,1)S(1)}, u32[]{:S(2)}, u32[]{:S(2)}) collective-permute-start(bf16[16,2048]{1,0:T(8,128)(2,1)S(1)} %shard_map.109.refs_0_), channel_id=1, source_target_pairs={{0,16},{1,17},{2,18},{3,19},{4,20},{5,21},{6,22},{7,23},{8,24},{9,... | collective-permute-start | bytes 196616 | tf_op jit(solution)/shard_map/ppermute | solution.py:91
  7.4 1.3 collective-permute-start.2
  8.7 2.1 %copy.23 = bf16[2,2,6,4,2,3,2,512]{7,6,5,2,4,1,3,0:T(2,128)(2,1)S(1)} copy(bf16[2,2,6,4,2,3,2,512]{7,6,5,4,3,2,1,0:T(2,128)(2,1)} %bitcast.32) | data formatting | bytes 2359296 | tf_op jit(solution)/shard_map/reshape | solution.py:352
  10.9 0.5 reshape.45.refs_8_.refs_0_
  11.4 0.5 collective-permute-done.1.refs_2_
  11.9 0.2 collective-permute-done.2.refs_3_
  12.2 1.6 %collective-permute-start.13 = (bf16[16,2048]{1,0:T(8,128)(2,1)S(1)}, bf16[16,2048]{1,0:T(8,128)(2,1)S(1)}, u32[]{:S(2)}, u32[]{:S(2)}) collective-permute-start(bf16[16,2048]{1,0:T(8,128)(2,1)S(1)} %get-tuple-element.35.refs_4_), channel_id=1, source_target_pairs={{0,8},{1,9},{2,10},{3,11},{4,12},{5,13},{6,14},{7,15},{8,16},{9,17... | collective-permute-start | bytes 196616 | tf_op jit(solution)/shard_map/ppermute | solution.py:91
  13.8 2.0 %collective-permute-start.14 = (bf16[16,2048]{1,0:T(8,128)(2,1)S(1)}, bf16[16,2048]{1,0:T(8,128)(2,1)S(1)}, u32[]{:S(2)}, u32[]{:S(2)}) collective-permute-start(bf16[16,2048]{1,0:T(8,128)(2,1)S(1)} %get-tuple-element.35.refs_4_), channel_id=1, source_target_pairs={{0,16},{1,17},{2,18},{3,19},{4,20},{5,21},{6,22},{7,23},{8,24},{9,... | collective-permute-start | bytes 196616 | tf_op jit(solution)/shard_map/ppermute | solution.py:91
  15.8 0.4 collective-permute-start.15
  16.3 1.5 collective-permute-start.3
  17.8 1.5 %collective-permute-start.4 = (bf16[4,16,2048]{2,1,0:T(8,128)(2,1)S(1)}, bf16[4,16,2048]{2,1,0:T(8,128)(2,1)S(1)}, u32[]{:S(2)}, u32[]{:S(2)}) collective-permute-start(bf16[4,16,2048]{2,1,0:T(8,128)(2,1)S(1)} %get-tuple-element.33.refs_1_), channel_id=1, source_target_pairs={{0,4},{1,5},{2,6},{3,7},{4,0},{5,1},{6,2},{7,3},{8,12},{9,13},{10,... | collective-permute-start | bytes 786440 | tf_op jit(solution)/shard_map/ppermute | solution.py:91
  19.3 2.0 %collective-permute-start.5 = (bf16[4,16,2048]{2,1,0:T(8,128)(2,1)S(1)}, bf16[4,16,2048]{2,1,0:T(8,128)(2,1)S(1)}, u32[]{:S(2)}, u32[]{:S(2)}) collective-permute-start(bf16[4,16,2048]{2,1,0:T(8,128)(2,1)S(1)} %get-tuple-element.33.refs_1_), channel_id=1, source_target_pairs={{0,6},{1,7},{2,4},{3,5},{4,2},{5,3},{6,0},{7,1},{8,14},{9,15},{10,... | collective-permute-start | bytes 786440 | tf_op jit(solution)/shard_map/ppermute | solution.py:91
  21.4 2.4 %collective-permute-start.11 = (bf16[16,4096]{1,0:T(8,128)(2,1)S(1)}, bf16[16,4096]{1,0:T(8,128)(2,1)S(1)}, u32[]{:S(2)}, u32[]{:S(2)}) collective-permute-start(bf16[16,4096]{1,0:T(8,128)(2,1)S(1)} %get-tuple-element.34.refs_0_), channel_id=1, source_target_pairs={{0,16},{1,17},{2,18},{3,19},{4,20},{5,21},{6,22},{7,23},{8,24},{9,... | collective-permute-start | bytes 393224 | tf_op jit(solution)/shard_map/ppermute | solution.py:91
  23.8 5.4 %collective-permute-done.10.refs_1_ = bf16[16,4096]{1,0:T(8,128)(2,1)S(1)} collective-permute-done((bf16[16,4096]{1,0:T(8,128)(2,1)S(1)}, bf16[16,4096]{1,0:T(8,128)(2,1)S(1)}, u32[]{:S(2)}, u32[]{:S(2)}) %collective-permute-start.10) | collective-permute-done | bytes 131104 | tf_op jit(solution)/shard_map/ppermute | solution.py:91
  29.2 0.5 collective-permute-start.7
  29.7 0.8 collective-permute-done.4.refs_3_
  30.4 0.5 collective-permute-start.9
  31.0 1.3 collective-permute-done.11.refs_2_
  32.4 0.7 collective-permute-start.12
  33.1 4.3 %collective-permute-done.12.refs_3_ = bf16[16,4096]{1,0:T(8,128)(2,1)S(1)} collective-permute-done((bf16[16,4096]{1,0:T(8,128)(2,1)S(1)}, bf16[16,4096]{1,0:T(8,128)(2,1)S(1)}, u32[]{:S(2)}, u32[]{:S(2)}) %collective-permute-start.12) | collective-permute-done | bytes 131104 | tf_op jit(solution)/shard_map/ppermute | solution.py:91
  37.4 0.5 collective-permute-start.16
  37.9 0.8 collective-permute-start.17
  38.7 2.3 %collective-permute-start.18 = (bf16[4,16,4096]{2,1,0:T(8,128)(2,1)S(1)}, bf16[4,16,4096]{2,1,0:T(8,128)(2,1)S(1)}, u32[]{:S(2)}, u32[]{:S(2)}) collective-permute-start(bf16[4,16,4096]{2,1,0:T(8,128)(2,1)S(1)} %get-tuple-element.36.refs_12_.refs_1_), channel_id=1, source_target_pairs={{0,6},{1,7},{2,4},{3,5},{4,2},{5,3},{6,0},{7,1},{8,14},{9,15},{10,... | collective-permute-start | bytes 1572872 | tf_op jit(solution)/shard_map/ppermute | solution.py:91
  41.0 14.7 %shard_map.112.refs_0_ = bf16[8,144,512]{2,1,0:T(8,128)(2,1)S(1)} custom-call(bf16[8,144,512]{2,1,0:T(8,128)(2,1)S(1)} %reshape.45.refs_8_.refs_0_, bf16[4,16,2048]{2,1,0:T(8,128)(2,1)S(1)} %get-tuple-element.33.refs_1_, bf16[4,16,2048]{2,1,0:T(8,128)(2,1)S(1)} %collective-permute-done.3.refs_2_, bf16[4,16,2048]{2,1,0:T(8,128)(2,1)S(1)} %collective-permute-done.4.refs_3_, ...), custom_call_target="tpu_custom_call" | custom-call | flops 16000000000 | bytes 6000000 | tf_op jit(solution)/shard_map/pallas_call | solution.py:261
  55.7 0.5 collective-permute-start.20
  56.2 6.0 %collective-permute-done.17.refs_3_ = bf16[4,16,4096]{2,1,0:T(8,128)(2,1)S(1)} collective-permute-done((bf16[4,16,4096]{2,1,0:T(8,128)(2,1)S(1)}, bf16[4,16,4096]{2,1,0:T(8,128)(2,1)S(1)}, u32[]{:S(2)}, u32[]{:S(2)}) %collective-permute-start.17) | collective-permute-done | bytes 524320 | tf_op jit(solution)/shard_map/ppermute | solution.py:91
  62.2 0.5 collective-permute-start.22
  62.8 0.4 collective-permute-start.26
  63.2 0.9 collective-permute-done.21.refs_7_
  64.1 0.7 collective-permute-start.27
  64.8 1.4 collective-permute-start.28
  66.3 4.8 %shard_map.113 = (bf16[4,2,36,512]{3,2,1,0:T(8,128)(2,1)S(1)}, bf16[4,2,36,512]{3,2,1,0:T(8,128)(2,1)S(1)}, bf16[2,36,512]{2,1,0:T(8,128)(2,1)S(1)}) custom-call(bf16[8,144,512]{2,1,0:T(8,128)(2,1)S(1)} %shard_map.112.refs_0_, bf16[4,16,4096]{2,1,0:T(8,128)(2,1)S(1)} %get-tuple-element.36.refs_12_.refs_1_, ...), custom_call_target="tpu_custom_call" | custom-call | flops 4831838208 | bytes 8000000 | tf_op jit(solution)/shard_map/pallas_call | solution.py:319
  71.1 0.8 collective-permute-done.26.refs_8_
  71.9 4.2 %collective-permute-start.34 = (bf16[16,4096]{1,0:T(8,128)(2,1)S(1)}, bf16[16,4096]{1,0:T(8,128)(2,1)S(1)}, u32[]{:S(2)}, u32[]{:S(2)}) collective-permute-start(bf16[16,4096]{1,0:T(8,128)(2,1)S(1)} %get-tuple-element.51.refs_0_), channel_id=1, source_target_pairs={{0,16},{1,17},{2,18},{3,19},{4,20},{5,21},{6,22},{7,23},{8,24},{9,... | collective-permute-start | bytes 393224 | tf_op jit(solution)/shard_map/ppermute | solution.py:91
  76.1 2.0 %collective-permute-done.27.refs_9_ = bf16[4,16,2048]{2,1,0:T(8,128)(2,1)S(1)} collective-permute-done((bf16[4,16,2048]{2,1,0:T(8,128)(2,1)S(1)}, bf16[4,16,2048]{2,1,0:T(8,128)(2,1)S(1)}, u32[]{:S(2)}, u32[]{:S(2)}) %collective-permute-start.27) | collective-permute-done | bytes 262176 | tf_op jit(solution)/shard_map/ppermute | solution.py:91
  78.1 3.7 %collective-permute-start.35 = (bf16[16,4096]{1,0:T(8,128)(2,1)S(1)}, bf16[16,4096]{1,0:T(8,128)(2,1)S(1)}, u32[]{:S(2)}, u32[]{:S(2)}) collective-permute-start(bf16[16,4096]{1,0:T(8,128)(2,1)S(1)} %get-tuple-element.51.refs_0_), channel_id=1, source_target_pairs={{0,24},{1,25},{2,26},{3,27},{4,28},{5,29},{6,30},{7,31},{8,0},{9,1... | collective-permute-start | bytes 393224 | tf_op jit(solution)/shard_map/ppermute | solution.py:91
  81.7 1.6 %collective-permute-start.23 = (bf16[4,2,36,512]{3,2,1,0:T(8,128)(2,1)S(1)}, bf16[4,2,36,512]{3,2,1,0:T(8,128)(2,1)S(1)}, u32[]{:S(2)}, u32[]{:S(2)}) collective-permute-start(bf16[4,2,36,512]{3,2,1,0:T(8,128)(2,1)S(1)} %get-tuple-element.40.refs_0_), channel_id=1, source_target_pairs={{2,0},{3,1},{4,2},{5,3},{6,4},{7,5},{8,6},{9,7},{10,8},{11,9},{12,... | collective-permute-start | bytes 884744 | tf_op jit(solution)/shard_map/ppermute | solution.py:346
  83.4 4.8 %shard_map.114 = (bf16[4,2,36,512]{3,2,1,0:T(8,128)(2,1)S(1)}, bf16[4,2,36,512]{3,2,1,0:T(8,128)(2,1)S(1)}, bf16[2,36,512]{2,1,0:T(8,128)(2,1)S(1)}) custom-call(bf16[8,144,512]{2,1,0:T(8,128)(2,1)S(1)} %shard_map.112.refs_0_, bf16[4,16,4096]{2,1,0:T(8,128)(2,1)S(1)} %get-tuple-element.36.refs_12_.refs_1_, ...), custom_call_target="tpu_custom_call" | custom-call | flops 4831838208 | bytes 8000000 | tf_op jit(solution)/shard_map/pallas_call | solution.py:319
  88.4 0.5 collective-permute-start.31
  89.0 3.7 %collective-permute-done.25.refs_6_ = bf16[2,36,512]{2,1,0:T(8,128)(2,1)S(1)} collective-permute-done((bf16[2,36,512]{2,1,0:T(8,128)(2,1)S(1)}, bf16[2,36,512]{2,1,0:T(8,128)(2,1)S(1)}, u32[]{:S(2)}, u32[]{:S(2)}) %collective-permute-start.25) | collective-permute-done | bytes 73760 | tf_op jit(solution)/shard_map/ppermute | solution.py:346
  92.8 1.4 collective-permute-done.24.refs_5_
  94.1 1.0 collective-permute-start.36
  95.1 1.5 %collective-permute-start.37 = (bf16[4,16,4096]{2,1,0:T(8,128)(2,1)S(1)}, bf16[4,16,4096]{2,1,0:T(8,128)(2,1)S(1)}, u32[]{:S(2)}, u32[]{:S(2)}) collective-permute-start(bf16[4,16,4096]{2,1,0:T(8,128)(2,1)S(1)} %shard_map.115.refs_19_.refs_1_), channel_id=1, source_target_pairs={{0,4},{1,5},{2,6},{3,7},{4,0},{5,1},{6,2},{7,3},{8,12},{9,13},{10,... | collective-permute-start | bytes 1572872 | tf_op jit(solution)/shard_map/ppermute | solution.py:91
  96.6 1.0 collective-permute-start.38
  97.6 14.9 %shard_map.116.refs_0_ = bf16[8,144,512]{2,1,0:T(8,128)(2,1)S(1)} custom-call(bf16[4,2,36,512]{3,2,1,0:T(8,128)(2,1)S(1)} %get-tuple-element.40.refs_0_, bf16[4,2,36,512]{3,2,1,0:T(8,128)(2,1)S(1)} %get-tuple-element.41.refs_1_, bf16[4,2,36,512]{3,2,1,0:T(8,128)(2,1)S(1)} %get-tuple-element.43.refs_2_, ...), custom_call_target="tpu_custom_call" | custom-call | flops 16000000000 | bytes 6000000 | tf_op jit(solution)/shard_map/pallas_call | solution.py:261
  112.6 0.5 collective-permute-start.40
  113.1 6.9 %collective-permute-done.37.refs_3_ = bf16[4,16,4096]{2,1,0:T(8,128)(2,1)S(1)} collective-permute-done((bf16[4,16,4096]{2,1,0:T(8,128)(2,1)S(1)}, bf16[4,16,4096]{2,1,0:T(8,128)(2,1)S(1)}, u32[]{:S(2)}, u32[]{:S(2)}) %collective-permute-start.37) | collective-permute-done | bytes 524320 | tf_op jit(solution)/shard_map/ppermute | solution.py:91
  120.0 0.5 collective-permute-start.42
  120.5 1.4 collective-permute-done.41.refs_7_
  121.9 0.7 collective-permute-done.42.refs_8_
  122.7 4.8 %shard_map.117 = (bf16[4,2,36,512]{3,2,1,0:T(8,128)(2,1)S(1)}, bf16[4,2,36,512]{3,2,1,0:T(8,128)(2,1)S(1)}, bf16[2,36,512]{2,1,0:T(8,128)(2,1)S(1)}) custom-call(bf16[8,144,512]{2,1,0:T(8,128)(2,1)S(1)} %shard_map.116.refs_0_, bf16[4,16,4096]{2,1,0:T(8,128)(2,1)S(1)} %shard_map.115.refs_19_.refs_1_, ...), custom_call_target="tpu_custom_call" | custom-call | flops 4831838208 | bytes 8000000 | tf_op jit(solution)/shard_map/pallas_call | solution.py:319
  127.5 4.8 %shard_map.118 = (bf16[4,2,36,512]{3,2,1,0:T(8,128)(2,1)S(1)}, bf16[4,2,36,512]{3,2,1,0:T(8,128)(2,1)S(1)}, bf16[2,36,512]{2,1,0:T(8,128)(2,1)S(1)}) custom-call(bf16[8,144,512]{2,1,0:T(8,128)(2,1)S(1)} %shard_map.116.refs_0_, bf16[4,16,4096]{2,1,0:T(8,128)(2,1)S(1)} %shard_map.115.refs_19_.refs_1_, ...), custom_call_target="tpu_custom_call" | custom-call | flops 4831838208 | bytes 8000000 | tf_op jit(solution)/shard_map/pallas_call | solution.py:319
  132.4 0.2 collective-permute-start.45
  132.6 0.7 collective-permute-start.43
  133.3 2.5 %collective-permute-start.44 = (bf16[4,2,36,512]{3,2,1,0:T(8,128)(2,1)S(1)}, bf16[4,2,36,512]{3,2,1,0:T(8,128)(2,1)S(1)}, u32[]{:S(2)}, u32[]{:S(2)}) collective-permute-start(bf16[4,2,36,512]{3,2,1,0:T(8,128)(2,1)S(1)} %get-tuple-element.56), channel_id=1, source_target_pairs={{30,0},{31,1},{0,2},{1,3},{2,4},{3,5},{4,6},{5,7},{6,8},{7,9},{8,1... | collective-permute-start | bytes 884744 | tf_op jit(solution)/shard_map/ppermute | solution.py:346
  135.9 0.2 copy.21
  136.3 0.2 copy.20
  136.7 0.2 copy.19
  136.9 3.6 %collective-permute-done.43 = bf16[2,36,512]{2,1,0:T(8,128)(2,1)S(1)} collective-permute-done((bf16[2,36,512]{2,1,0:T(8,128)(2,1)S(1)}, bf16[2,36,512]{2,1,0:T(8,128)(2,1)S(1)}, u32[]{:S(2)}, u32[]{:S(2)}) %collective-permute-start.43) | collective-permute-done | bytes 73760 | tf_op jit(solution)/shard_map/ppermute | solution.py:346
  140.6 7.3 %collective-permute-done.44 = bf16[4,2,36,512]{3,2,1,0:T(8,128)(2,1)S(1)} collective-permute-done((bf16[4,2,36,512]{3,2,1,0:T(8,128)(2,1)S(1)}, bf16[4,2,36,512]{3,2,1,0:T(8,128)(2,1)S(1)}, u32[]{:S(2)}, u32[]{:S(2)}) %collective-permute-start.44) | collective-permute-done | bytes 294944 | tf_op jit(solution)/shard_map/ppermute | solution.py:346
  148.3 2.9 %maximum_maximum_fusion = bf16[24,24,2,512]{3,2,1,0:T(2,128)(2,1)} fusion(bf16[6,21,2,512]{3,2,1,0:T(2,128)(2,1)S(1)} %bitcast.33, bf16[6,21,2,512]{3,2,1,0:T(2,128)(2,1)S(1)} %bitcast.34, bf16[6,21,2,512]{3,2,1,0:T(2,128)(2,1)S(1)} %bitcast.35, bf16[6,3,2,512]{3,2,1,0:T(2,128)(2,1)S(1)} %reshape_transpose_reshape_broadcast_in_dim_squeeze.15, ...), kind=kLoop, calls=%fused_computation | loop fusion | flops 4128768 | bytes 2359296 | tf_op jit(solution)/shard_map/concatenate | solution.py:371
  (86 shorter events, 1.9 us)
Async XLA Ops:
  0.0 0.9 copy-start.2
  0.9 0.8 copy-start.4
  1.8 9.6 %collective-permute-start = (bf16[16,2048]{1,0:T(8,128)(2,1)S(1)}, bf16[16,2048]{1,0:T(8,128)(2,1)S(1)}, u32[]{:S(2)}, u32[]{:S(2)}) collective-permute-start(bf16[16,2048]{1,0:T(8,128)(2,1)S(1)} %shard_map.109.refs_0_), channel_id=1, source_target_pairs={{0,8},{1,9},{2,10},{3,11},{4,12},{5,13},{6,14},{7,15},{8,16},{9,17... | collective-permute-start | bytes 196616 | tf_op jit(solution)/shard_map/ppermute | solution.py:91
  4.8 7.1 %collective-permute-start.1 = (bf16[16,2048]{1,0:T(8,128)(2,1)S(1)}, bf16[16,2048]{1,0:T(8,128)(2,1)S(1)}, u32[]{:S(2)}, u32[]{:S(2)}) collective-permute-start(bf16[16,2048]{1,0:T(8,128)(2,1)S(1)} %shard_map.109.refs_0_), channel_id=1, source_target_pairs={{0,16},{1,17},{2,18},{3,19},{4,20},{5,21},{6,22},{7,23},{8,24},{9,... | collective-permute-start | bytes 196616 | tf_op jit(solution)/shard_map/ppermute | solution.py:91
  7.4 4.7 %collective-permute-start.2 = (bf16[16,2048]{1,0:T(8,128)(2,1)S(1)}, bf16[16,2048]{1,0:T(8,128)(2,1)S(1)}, u32[]{:S(2)}, u32[]{:S(2)}) collective-permute-start(bf16[16,2048]{1,0:T(8,128)(2,1)S(1)} %shard_map.109.refs_0_), channel_id=1, source_target_pairs={{0,24},{1,25},{2,26},{3,27},{4,28},{5,29},{6,30},{7,31},{8,0},{9,1... | collective-permute-start | bytes 196616 | tf_op jit(solution)/shard_map/ppermute | solution.py:91
  10.8 1.3 copy-start
  10.8 1.3 copy-start.1
  10.8 1.3 copy-start.3
  10.9 1.3 copy-start.5
  11.4 12.4 %copy-start.9 = (f32[2,2,512]{2,1,0:T(2,128)S(1)}, f32[2,2,512]{2,1,0:T(2,128)}, u32[]{:S(2)}) copy-start(f32[2,2,512]{2,1,0:T(2,128)} %param.16) | copy-start | bytes 24580
  11.4 19.6 %copy-start.8 = (f32[16,512]{1,0:T(8,128)S(1)}, f32[16,512]{1,0:T(8,128)}, u32[]{:S(2)}) copy-start(f32[16,512]{1,0:T(8,128)} %constant.8.clone) | copy-start | bytes 98308
  11.4 19.6 %copy-start.10 = (f32[2,16]{1,0:T(2,128)S(1)}, f32[2,16]{1,0:T(2,128)}, u32[]{:S(2)}) copy-start(f32[2,16]{1,0:T(2,128)} %param.17) | copy-start | bytes 388
  12.2 28.8 %copy-start.6 = (bf16[1152,256]{1,0:T(8,128)(2,1)S(1)}, bf16[1152,256]{1,0:T(8,128)(2,1)}, u32[]{:S(2)}) copy-start(bf16[1152,256]{1,0:T(8,128)(2,1)} %constant.9.clone.refs_11_.refs_17_) | copy-start | bytes 1769476
  12.2 7.1 %collective-permute-start.13 = (bf16[16,2048]{1,0:T(8,128)(2,1)S(1)}, bf16[16,2048]{1,0:T(8,128)(2,1)S(1)}, u32[]{:S(2)}, u32[]{:S(2)}) collective-permute-start(bf16[16,2048]{1,0:T(8,128)(2,1)S(1)} %get-tuple-element.35.refs_4_), channel_id=1, source_target_pairs={{0,8},{1,9},{2,10},{3,11},{4,12},{5,13},{6,14},{7,15},{8,16},{9,17... | collective-permute-start | bytes 196616 | tf_op jit(solution)/shard_map/ppermute | solution.py:91
  13.8 7.4 %collective-permute-start.14 = (bf16[16,2048]{1,0:T(8,128)(2,1)S(1)}, bf16[16,2048]{1,0:T(8,128)(2,1)S(1)}, u32[]{:S(2)}, u32[]{:S(2)}) collective-permute-start(bf16[16,2048]{1,0:T(8,128)(2,1)S(1)} %get-tuple-element.35.refs_4_), channel_id=1, source_target_pairs={{0,16},{1,17},{2,18},{3,19},{4,20},{5,21},{6,22},{7,23},{8,24},{9,... | collective-permute-start | bytes 196616 | tf_op jit(solution)/shard_map/ppermute | solution.py:91
  15.8 5.5 %collective-permute-start.15 = (bf16[16,2048]{1,0:T(8,128)(2,1)S(1)}, bf16[16,2048]{1,0:T(8,128)(2,1)S(1)}, u32[]{:S(2)}, u32[]{:S(2)}) collective-permute-start(bf16[16,2048]{1,0:T(8,128)(2,1)S(1)} %get-tuple-element.35.refs_4_), channel_id=1, source_target_pairs={{0,24},{1,25},{2,26},{3,27},{4,28},{5,29},{6,30},{7,31},{8,0},{9,1... | collective-permute-start | bytes 196616 | tf_op jit(solution)/shard_map/ppermute | solution.py:91
  16.3 12.9 %collective-permute-start.3 = (bf16[4,16,2048]{2,1,0:T(8,128)(2,1)S(1)}, bf16[4,16,2048]{2,1,0:T(8,128)(2,1)S(1)}, u32[]{:S(2)}, u32[]{:S(2)}) collective-permute-start(bf16[4,16,2048]{2,1,0:T(8,128)(2,1)S(1)} %get-tuple-element.33.refs_1_), channel_id=1, source_target_pairs={{0,2},{1,3},{2,0},{3,1},{4,6},{5,7},{6,4},{7,5},{8,10},{9,11},{10,... | collective-permute-start | bytes 786440 | tf_op jit(solution)/shard_map/ppermute | solution.py:91
  17.8 12.7 %collective-permute-start.4 = (bf16[4,16,2048]{2,1,0:T(8,128)(2,1)S(1)}, bf16[4,16,2048]{2,1,0:T(8,128)(2,1)S(1)}, u32[]{:S(2)}, u32[]{:S(2)}) collective-permute-start(bf16[4,16,2048]{2,1,0:T(8,128)(2,1)S(1)} %get-tuple-element.33.refs_1_), channel_id=1, source_target_pairs={{0,4},{1,5},{2,6},{3,7},{4,0},{5,1},{6,2},{7,3},{8,12},{9,13},{10,... | collective-permute-start | bytes 786440 | tf_op jit(solution)/shard_map/ppermute | solution.py:91
  19.3 11.2 %collective-permute-start.5 = (bf16[4,16,2048]{2,1,0:T(8,128)(2,1)S(1)}, bf16[4,16,2048]{2,1,0:T(8,128)(2,1)S(1)}, u32[]{:S(2)}, u32[]{:S(2)}) collective-permute-start(bf16[4,16,2048]{2,1,0:T(8,128)(2,1)S(1)} %get-tuple-element.33.refs_1_), channel_id=1, source_target_pairs={{0,6},{1,7},{2,4},{3,5},{4,2},{5,3},{6,0},{7,1},{8,14},{9,15},{10,... | collective-permute-start | bytes 786440 | tf_op jit(solution)/shard_map/ppermute | solution.py:91
  21.2 7.9 %collective-permute-start.10 = (bf16[16,4096]{1,0:T(8,128)(2,1)S(1)}, bf16[16,4096]{1,0:T(8,128)(2,1)S(1)}, u32[]{:S(2)}, u32[]{:S(2)}) collective-permute-start(bf16[16,4096]{1,0:T(8,128)(2,1)S(1)} %get-tuple-element.34.refs_0_), channel_id=1, source_target_pairs={{0,8},{1,9},{2,10},{3,11},{4,12},{5,13},{6,14},{7,15},{8,16},{9,17... | collective-permute-start | bytes 393224 | tf_op jit(solution)/shard_map/ppermute | solution.py:91
  21.4 11.0 %collective-permute-start.11 = (bf16[16,4096]{1,0:T(8,128)(2,1)S(1)}, bf16[16,4096]{1,0:T(8,128)(2,1)S(1)}, u32[]{:S(2)}, u32[]{:S(2)}) collective-permute-start(bf16[16,4096]{1,0:T(8,128)(2,1)S(1)} %get-tuple-element.34.refs_0_), channel_id=1, source_target_pairs={{0,16},{1,17},{2,18},{3,19},{4,20},{5,21},{6,22},{7,23},{8,24},{9,... | collective-permute-start | bytes 393224 | tf_op jit(solution)/shard_map/ppermute | solution.py:91
  29.2 8.7 %collective-permute-start.6 = (bf16[4,16,2048]{2,1,0:T(8,128)(2,1)S(1)}, bf16[4,16,2048]{2,1,0:T(8,128)(2,1)S(1)}, u32[]{:S(2)}, u32[]{:S(2)}) collective-permute-start(bf16[4,16,2048]{2,1,0:T(8,128)(2,1)S(1)} %get-tuple-element.33.refs_1_), channel_id=1, source_target_pairs={{0,1},{1,0},{2,3},{3,2},{4,5},{5,4},{6,7},{7,6},{8,9},{9,8},{10,11... | collective-permute-start | bytes 786440 | tf_op jit(solution)/shard_map/ppermute | solution.py:91
  29.2 9.5 %collective-permute-start.7 = (bf16[4,16,2048]{2,1,0:T(8,128)(2,1)S(1)}, bf16[4,16,2048]{2,1,0:T(8,128)(2,1)S(1)}, u32[]{:S(2)}, u32[]{:S(2)}) collective-permute-start(bf16[4,16,2048]{2,1,0:T(8,128)(2,1)S(1)} %collective-permute-done.3.refs_2_), channel_id=1, source_target_pairs={{0,1},{1,0},{2,3},{3,2},{4,5},{5,4},{6,7},{7,6},{8,9},{9,8},{10,11... | collective-permute-start | bytes 786440 | tf_op jit(solution)/shard_map/ppermute | solution.py:91
  30.4 10.5 %collective-permute-start.8 = (bf16[4,16,2048]{2,1,0:T(8,128)(2,1)S(1)}, bf16[4,16,2048]{2,1,0:T(8,128)(2,1)S(1)}, u32[]{:S(2)}, u32[]{:S(2)}) collective-permute-start(bf16[4,16,2048]{2,1,0:T(8,128)(2,1)S(1)} %collective-permute-done.4.refs_3_), channel_id=1, source_target_pairs={{0,1},{1,0},{2,3},{3,2},{4,5},{5,4},{6,7},{7,6},{8,9},{9,8},{10,11... | collective-permute-start | bytes 786440 | tf_op jit(solution)/shard_map/ppermute | solution.py:91
  30.4 10.5 %collective-permute-start.9 = (bf16[4,16,2048]{2,1,0:T(8,128)(2,1)S(1)}, bf16[4,16,2048]{2,1,0:T(8,128)(2,1)S(1)}, u32[]{:S(2)}, u32[]{:S(2)}) collective-permute-start(bf16[4,16,2048]{2,1,0:T(8,128)(2,1)S(1)} %collective-permute-done.5.refs_4_), channel_id=1, source_target_pairs={{0,1},{1,0},{2,3},{3,2},{4,5},{5,4},{6,7},{7,6},{8,9},{9,8},{10,11... | collective-permute-start | bytes 786440 | tf_op jit(solution)/shard_map/ppermute | solution.py:91
  32.4 5.0 %collective-permute-start.12 = (bf16[16,4096]{1,0:T(8,128)(2,1)S(1)}, bf16[16,4096]{1,0:T(8,128)(2,1)S(1)}, u32[]{:S(2)}, u32[]{:S(2)}) collective-permute-start(bf16[16,4096]{1,0:T(8,128)(2,1)S(1)} %get-tuple-element.34.refs_0_), channel_id=1, source_target_pairs={{0,24},{1,25},{2,26},{3,27},{4,28},{5,29},{6,30},{7,31},{8,0},{9,1... | collective-permute-start | bytes 393224 | tf_op jit(solution)/shard_map/ppermute | solution.py:91
  37.4 18.3 %collective-permute-start.16 = (bf16[4,16,4096]{2,1,0:T(8,128)(2,1)S(1)}, bf16[4,16,4096]{2,1,0:T(8,128)(2,1)S(1)}, u32[]{:S(2)}, u32[]{:S(2)}) collective-permute-start(bf16[4,16,4096]{2,1,0:T(8,128)(2,1)S(1)} %get-tuple-element.36.refs_12_.refs_1_), channel_id=1, source_target_pairs={{0,2},{1,3},{2,0},{3,1},{4,6},{5,7},{6,4},{7,5},{8,10},{9,11},{10,... | collective-permute-start | bytes 1572872 | tf_op jit(solution)/shard_map/ppermute | solution.py:91
  37.9 24.3 %collective-permute-start.17 = (bf16[4,16,4096]{2,1,0:T(8,128)(2,1)S(1)}, bf16[4,16,4096]{2,1,0:T(8,128)(2,1)S(1)}, u32[]{:S(2)}, u32[]{:S(2)}) collective-permute-start(bf16[4,16,4096]{2,1,0:T(8,128)(2,1)S(1)} %get-tuple-element.36.refs_12_.refs_1_), channel_id=1, source_target_pairs={{0,4},{1,5},{2,6},{3,7},{4,0},{5,1},{6,2},{7,3},{8,12},{9,13},{10,... | collective-permute-start | bytes 1572872 | tf_op jit(solution)/shard_map/ppermute | solution.py:91
  38.7 23.5 %collective-permute-start.18 = (bf16[4,16,4096]{2,1,0:T(8,128)(2,1)S(1)}, bf16[4,16,4096]{2,1,0:T(8,128)(2,1)S(1)}, u32[]{:S(2)}, u32[]{:S(2)}) collective-permute-start(bf16[4,16,4096]{2,1,0:T(8,128)(2,1)S(1)} %get-tuple-element.36.refs_12_.refs_1_), channel_id=1, source_target_pairs={{0,6},{1,7},{2,4},{3,5},{4,2},{5,3},{6,0},{7,1},{8,14},{9,15},{10,... | collective-permute-start | bytes 1572872 | tf_op jit(solution)/shard_map/ppermute | solution.py:91
  41.0 21.7 %collective-permute-start.19 = (bf16[4,16,4096]{2,1,0:T(8,128)(2,1)S(1)}, bf16[4,16,4096]{2,1,0:T(8,128)(2,1)S(1)}, u32[]{:S(2)}, u32[]{:S(2)}) collective-permute-start(bf16[4,16,4096]{2,1,0:T(8,128)(2,1)S(1)} %get-tuple-element.36.refs_12_.refs_1_), channel_id=1, source_target_pairs={{0,1},{1,0},{2,3},{3,2},{4,5},{5,4},{6,7},{7,6},{8,9},{9,8},{10,11... | collective-permute-start | bytes 1572872 | tf_op jit(solution)/shard_map/ppermute | solution.py:91
  55.7 7.1 %collective-permute-start.20 = (bf16[4,16,4096]{2,1,0:T(8,128)(2,1)S(1)}, bf16[4,16,4096]{2,1,0:T(8,128)(2,1)S(1)}, u32[]{:S(2)}, u32[]{:S(2)}) collective-permute-start(bf16[4,16,4096]{2,1,0:T(8,128)(2,1)S(1)} %collective-permute-done.16.refs_2_), channel_id=1, source_target_pairs={{0,1},{1,0},{2,3},{3,2},{4,5},{5,4},{6,7},{7,6},{8,9},{9,8},{10,11... | collective-permute-start | bytes 1572872 | tf_op jit(solution)/shard_map/ppermute | solution.py:91
  62.2 1.9 %collective-permute-start.21 = (bf16[4,16,4096]{2,1,0:T(8,128)(2,1)S(1)}, bf16[4,16,4096]{2,1,0:T(8,128)(2,1)S(1)}, u32[]{:S(2)}, u32[]{:S(2)}) collective-permute-start(bf16[4,16,4096]{2,1,0:T(8,128)(2,1)S(1)} %collective-permute-done.17.refs_3_), channel_id=1, source_target_pairs={{0,1},{1,0},{2,3},{3,2},{4,5},{5,4},{6,7},{7,6},{8,9},{9,8},{10,11... | collective-permute-start | bytes 1572872 | tf_op jit(solution)/shard_map/ppermute | solution.py:91
  62.2 2.7 %collective-permute-start.22 = (bf16[4,16,4096]{2,1,0:T(8,128)(2,1)S(1)}, bf16[4,16,4096]{2,1,0:T(8,128)(2,1)S(1)}, u32[]{:S(2)}, u32[]{:S(2)}) collective-permute-start(bf16[4,16,4096]{2,1,0:T(8,128)(2,1)S(1)} %collective-permute-done.18.refs_4_), channel_id=1, source_target_pairs={{0,1},{1,0},{2,3},{3,2},{4,5},{5,4},{6,7},{7,6},{8,9},{9,8},{10,11... | collective-permute-start | bytes 1572872 | tf_op jit(solution)/shard_map/ppermute | solution.py:91
  62.7 26.2 %collective-permute-start.29 = (bf16[4,16,2048]{2,1,0:T(8,128)(2,1)S(1)}, bf16[4,16,2048]{2,1,0:T(8,128)(2,1)S(1)}, u32[]{:S(2)}, u32[]{:S(2)}) collective-permute-start(bf16[4,16,2048]{2,1,0:T(8,128)(2,1)S(1)} %get-tuple-element.47.refs_7_), channel_id=1, source_target_pairs={{0,1},{1,0},{2,3},{3,2},{4,5},{5,4},{6,7},{7,6},{8,9},{9,8},{10,11... | collective-permute-start | bytes 786440 | tf_op jit(solution)/shard_map/ppermute | solution.py:91
  62.7 25.5 %collective-permute-start.33 = (bf16[16,4096]{1,0:T(8,128)(2,1)S(1)}, bf16[16,4096]{1,0:T(8,128)(2,1)S(1)}, u32[]{:S(2)}, u32[]{:S(2)}) collective-permute-start(bf16[16,4096]{1,0:T(8,128)(2,1)S(1)} %get-tuple-element.51.refs_0_), channel_id=1, source_target_pairs={{0,8},{1,9},{2,10},{3,11},{4,12},{5,13},{6,14},{7,15},{8,16},{9,17... | collective-permute-start | bytes 393224 | tf_op jit(solution)/shard_map/ppermute | solution.py:91
  62.8 9.1 %collective-permute-start.26 = (bf16[4,16,2048]{2,1,0:T(8,128)(2,1)S(1)}, bf16[4,16,2048]{2,1,0:T(8,128)(2,1)S(1)}, u32[]{:S(2)}, u32[]{:S(2)}) collective-permute-start(bf16[4,16,2048]{2,1,0:T(8,128)(2,1)S(1)} %get-tuple-element.47.refs_7_), channel_id=1, source_target_pairs={{0,2},{1,3},{2,0},{3,1},{4,6},{5,7},{6,4},{7,5},{8,10},{9,11},{10,... | collective-permute-start | bytes 786440 | tf_op jit(solution)/shard_map/ppermute | solution.py:91
  64.1 14.0 %collective-permute-start.27 = (bf16[4,16,2048]{2,1,0:T(8,128)(2,1)S(1)}, bf16[4,16,2048]{2,1,0:T(8,128)(2,1)S(1)}, u32[]{:S(2)}, u32[]{:S(2)}) collective-permute-start(bf16[4,16,2048]{2,1,0:T(8,128)(2,1)S(1)} %get-tuple-element.47.refs_7_), channel_id=1, source_target_pairs={{0,4},{1,5},{2,6},{3,7},{4,0},{5,1},{6,2},{7,3},{8,12},{9,13},{10,... | collective-permute-start | bytes 786440 | tf_op jit(solution)/shard_map/ppermute | solution.py:91
  64.8 16.9 %collective-permute-start.28 = (bf16[4,16,2048]{2,1,0:T(8,128)(2,1)S(1)}, bf16[4,16,2048]{2,1,0:T(8,128)(2,1)S(1)}, u32[]{:S(2)}, u32[]{:S(2)}) collective-permute-start(bf16[4,16,2048]{2,1,0:T(8,128)(2,1)S(1)} %get-tuple-element.47.refs_7_), channel_id=1, source_target_pairs={{0,6},{1,7},{2,4},{3,5},{4,2},{5,3},{6,0},{7,1},{8,14},{9,15},{10,... | collective-permute-start | bytes 786440 | tf_op jit(solution)/shard_map/ppermute | solution.py:91
  71.9 16.4 %collective-permute-start.34 = (bf16[16,4096]{1,0:T(8,128)(2,1)S(1)}, bf16[16,4096]{1,0:T(8,128)(2,1)S(1)}, u32[]{:S(2)}, u32[]{:S(2)}) collective-permute-start(bf16[16,4096]{1,0:T(8,128)(2,1)S(1)} %get-tuple-element.51.refs_0_), channel_id=1, source_target_pairs={{0,16},{1,17},{2,18},{3,19},{4,20},{5,21},{6,22},{7,23},{8,24},{9,... | collective-permute-start | bytes 393224 | tf_op jit(solution)/shard_map/ppermute | solution.py:91
  78.1 10.3 %collective-permute-start.35 = (bf16[16,4096]{1,0:T(8,128)(2,1)S(1)}, bf16[16,4096]{1,0:T(8,128)(2,1)S(1)}, u32[]{:S(2)}, u32[]{:S(2)}) collective-permute-start(bf16[16,4096]{1,0:T(8,128)(2,1)S(1)} %get-tuple-element.51.refs_0_), channel_id=1, source_target_pairs={{0,24},{1,25},{2,26},{3,27},{4,28},{5,29},{6,30},{7,31},{8,0},{9,1... | collective-permute-start | bytes 393224 | tf_op jit(solution)/shard_map/ppermute | solution.py:91
  81.7 15.9 %collective-permute-start.23 = (bf16[4,2,36,512]{3,2,1,0:T(8,128)(2,1)S(1)}, bf16[4,2,36,512]{3,2,1,0:T(8,128)(2,1)S(1)}, u32[]{:S(2)}, u32[]{:S(2)}) collective-permute-start(bf16[4,2,36,512]{3,2,1,0:T(8,128)(2,1)S(1)} %get-tuple-element.40.refs_0_), channel_id=1, source_target_pairs={{2,0},{3,1},{4,2},{5,3},{6,4},{7,5},{8,6},{9,7},{10,8},{11,9},{12,... | collective-permute-start | bytes 884744 | tf_op jit(solution)/shard_map/ppermute | solution.py:346
  88.2 9.4 %copy-start.7 = (f32[144,256]{1,0:T(8,128)S(1)}, f32[144,256]{1,0:T(8,128)}, u32[]{:S(2)}) copy-start(f32[144,256]{1,0:T(8,128)} %constant.10.clone.refs_18_) | copy-start | bytes 442372
  88.2 4.5 %collective-permute-start.25 = (bf16[2,36,512]{2,1,0:T(8,128)(2,1)S(1)}, bf16[2,36,512]{2,1,0:T(8,128)(2,1)S(1)}, u32[]{:S(2)}, u32[]{:S(2)}) collective-permute-start(bf16[2,36,512]{2,1,0:T(8,128)(2,1)S(1)} %get-tuple-element.42.refs_10_), channel_id=1, source_target_pairs={{3,0},{2,1},{5,2},{4,3},{7,4},{6,5},{9,6},{8,7},{11,8},{10,9},{13,... | collective-permute-start | bytes 221192 | tf_op jit(solution)/shard_map/ppermute | solution.py:346
  88.3 6.8 %collective-permute-start.30 = (bf16[4,16,2048]{2,1,0:T(8,128)(2,1)S(1)}, bf16[4,16,2048]{2,1,0:T(8,128)(2,1)S(1)}, u32[]{:S(2)}, u32[]{:S(2)}) collective-permute-start(bf16[4,16,2048]{2,1,0:T(8,128)(2,1)S(1)} %collective-permute-done.26.refs_8_), channel_id=1, source_target_pairs={{0,1},{1,0},{2,3},{3,2},{4,5},{5,4},{6,7},{7,6},{8,9},{9,8},{10,11... | collective-permute-start | bytes 786440 | tf_op jit(solution)/shard_map/ppermute | solution.py:91
  88.4 8.2 %collective-permute-start.31 = (bf16[4,16,2048]{2,1,0:T(8,128)(2,1)S(1)}, bf16[4,16,2048]{2,1,0:T(8,128)(2,1)S(1)}, u32[]{:S(2)}, u32[]{:S(2)}) collective-permute-start(bf16[4,16,2048]{2,1,0:T(8,128)(2,1)S(1)} %collective-permute-done.27.refs_9_), channel_id=1, source_target_pairs={{0,1},{1,0},{2,3},{3,2},{4,5},{5,4},{6,7},{7,6},{8,9},{9,8},{10,11... | collective-permute-start | bytes 786440 | tf_op jit(solution)/shard_map/ppermute | solution.py:91
  88.9 8.7 %collective-permute-start.32 = (bf16[4,16,2048]{2,1,0:T(8,128)(2,1)S(1)}, bf16[4,16,2048]{2,1,0:T(8,128)(2,1)S(1)}, u32[]{:S(2)}, u32[]{:S(2)}) collective-permute-start(bf16[4,16,2048]{2,1,0:T(8,128)(2,1)S(1)} %collective-permute-done.28.refs_10_), channel_id=1, source_target_pairs={{0,1},{1,0},{2,3},{3,2},{4,5},{5,4},{6,7},{7,6},{8,9},{9,8},{10,11... | collective-permute-start | bytes 786440 | tf_op jit(solution)/shard_map/ppermute | solution.py:91
  92.7 1.4 collective-permute-start.24
  94.1 18.5 %collective-permute-start.36 = (bf16[4,16,4096]{2,1,0:T(8,128)(2,1)S(1)}, bf16[4,16,4096]{2,1,0:T(8,128)(2,1)S(1)}, u32[]{:S(2)}, u32[]{:S(2)}) collective-permute-start(bf16[4,16,4096]{2,1,0:T(8,128)(2,1)S(1)} %shard_map.115.refs_19_.refs_1_), channel_id=1, source_target_pairs={{0,2},{1,3},{2,0},{3,1},{4,6},{5,7},{6,4},{7,5},{8,10},{9,11},{10,... | collective-permute-start | bytes 1572872 | tf_op jit(solution)/shard_map/ppermute | solution.py:91
  95.1 24.9 %collective-permute-start.37 = (bf16[4,16,4096]{2,1,0:T(8,128)(2,1)S(1)}, bf16[4,16,4096]{2,1,0:T(8,128)(2,1)S(1)}, u32[]{:S(2)}, u32[]{:S(2)}) collective-permute-start(bf16[4,16,4096]{2,1,0:T(8,128)(2,1)S(1)} %shard_map.115.refs_19_.refs_1_), channel_id=1, source_target_pairs={{0,4},{1,5},{2,6},{3,7},{4,0},{5,1},{6,2},{7,3},{8,12},{9,13},{10,... | collective-permute-start | bytes 1572872 | tf_op jit(solution)/shard_map/ppermute | solution.py:91
  96.6 23.4 %collective-permute-start.38 = (bf16[4,16,4096]{2,1,0:T(8,128)(2,1)S(1)}, bf16[4,16,4096]{2,1,0:T(8,128)(2,1)S(1)}, u32[]{:S(2)}, u32[]{:S(2)}) collective-permute-start(bf16[4,16,4096]{2,1,0:T(8,128)(2,1)S(1)} %shard_map.115.refs_19_.refs_1_), channel_id=1, source_target_pairs={{0,6},{1,7},{2,4},{3,5},{4,2},{5,3},{6,0},{7,1},{8,14},{9,15},{10,... | collective-permute-start | bytes 1572872 | tf_op jit(solution)/shard_map/ppermute | solution.py:91
  97.6 22.9 %collective-permute-start.39 = (bf16[4,16,4096]{2,1,0:T(8,128)(2,1)S(1)}, bf16[4,16,4096]{2,1,0:T(8,128)(2,1)S(1)}, u32[]{:S(2)}, u32[]{:S(2)}) collective-permute-start(bf16[4,16,4096]{2,1,0:T(8,128)(2,1)S(1)} %shard_map.115.refs_19_.refs_1_), channel_id=1, source_target_pairs={{0,1},{1,0},{2,3},{3,2},{4,5},{5,4},{6,7},{7,6},{8,9},{9,8},{10,11... | collective-permute-start | bytes 1572872 | tf_op jit(solution)/shard_map/ppermute | solution.py:91
  112.6 8.0 %collective-permute-start.40 = (bf16[4,16,4096]{2,1,0:T(8,128)(2,1)S(1)}, bf16[4,16,4096]{2,1,0:T(8,128)(2,1)S(1)}, u32[]{:S(2)}, u32[]{:S(2)}) collective-permute-start(bf16[4,16,4096]{2,1,0:T(8,128)(2,1)S(1)} %collective-permute-done.36.refs_2_), channel_id=1, source_target_pairs={{0,1},{1,0},{2,3},{3,2},{4,5},{5,4},{6,7},{7,6},{8,9},{9,8},{10,11... | collective-permute-start | bytes 1572872 | tf_op jit(solution)/shard_map/ppermute | solution.py:91
  120.0 1.9 %collective-permute-start.41 = (bf16[4,16,4096]{2,1,0:T(8,128)(2,1)S(1)}, bf16[4,16,4096]{2,1,0:T(8,128)(2,1)S(1)}, u32[]{:S(2)}, u32[]{:S(2)}) collective-permute-start(bf16[4,16,4096]{2,1,0:T(8,128)(2,1)S(1)} %collective-permute-done.37.refs_3_), channel_id=1, source_target_pairs={{0,1},{1,0},{2,3},{3,2},{4,5},{5,4},{6,7},{7,6},{8,9},{9,8},{10,11... | collective-permute-start | bytes 1572872 | tf_op jit(solution)/shard_map/ppermute | solution.py:91
  120.0 2.7 %collective-permute-start.42 = (bf16[4,16,4096]{2,1,0:T(8,128)(2,1)S(1)}, bf16[4,16,4096]{2,1,0:T(8,128)(2,1)S(1)}, u32[]{:S(2)}, u32[]{:S(2)}) collective-permute-start(bf16[4,16,4096]{2,1,0:T(8,128)(2,1)S(1)} %collective-permute-done.38.refs_4_), channel_id=1, source_target_pairs={{0,1},{1,0},{2,3},{3,2},{4,5},{5,4},{6,7},{7,6},{8,9},{9,8},{10,11... | collective-permute-start | bytes 1572872 | tf_op jit(solution)/shard_map/ppermute | solution.py:91
  132.4 8.1 %collective-permute-start.45 = (bf16[4,36,512]{2,1,0:T(8,128)(2,1)S(1)}, bf16[4,36,512]{2,1,0:T(8,128)(2,1)S(1)}, u32[]{:S(2)}, u32[]{:S(2)}) collective-permute-start(bf16[4,36,512]{2,1,0:T(8,128)(2,1)S(1)} %pad_maximum_fusion.1), channel_id=1, source_target_pairs={{1,0},{0,1},{3,2},{2,3},{5,4},{4,5},{7,6},{6,7},{9,8},{8,9},{11,10... | collective-permute-start | bytes 442376 | tf_op jit(solution)/shard_map/ppermute | solution.py:346
  132.6 7.9 %collective-permute-start.43 = (bf16[2,36,512]{2,1,0:T(8,128)(2,1)S(1)}, bf16[2,36,512]{2,1,0:T(8,128)(2,1)S(1)}, u32[]{:S(2)}, u32[]{:S(2)}) collective-permute-start(bf16[2,36,512]{2,1,0:T(8,128)(2,1)S(1)} %get-tuple-element.55.refs_10_), channel_id=1, source_target_pairs={{31,0},{30,1},{1,2},{0,3},{3,4},{2,5},{5,6},{4,7},{7,8},{6,9},{9,1... | collective-permute-start | bytes 221192 | tf_op jit(solution)/shard_map/ppermute | solution.py:346
  133.3 14.7 %collective-permute-start.44 = (bf16[4,2,36,512]{3,2,1,0:T(8,128)(2,1)S(1)}, bf16[4,2,36,512]{3,2,1,0:T(8,128)(2,1)S(1)}, u32[]{:S(2)}, u32[]{:S(2)}) collective-permute-start(bf16[4,2,36,512]{3,2,1,0:T(8,128)(2,1)S(1)} %get-tuple-element.56), channel_id=1, source_target_pairs={{30,0},{31,1},{0,2},{1,3},{2,4},{3,5},{4,6},{5,7},{6,8},{7,9},{8,1... | collective-permute-start | bytes 884744 | tf_op jit(solution)/shard_map/ppermute | solution.py:346

commit v7 on v6

--- a/solution.py
+++ b/solution.py
@@ -20,6 +20,7 @@
 REST = CELLS - MAIN
 QUARTER = CELLS // 4
 GROUP = 8
+PART = 4
 WIDE = GROUP * HEAD
 ANY = pl.BlockSpec(memory_space=pl.ANY)
 NT = (((1,), (1,)), ((), ()))
@@ -36,49 +37,52 @@
     return centred * lax.rsqrt(variance + 1e-05) * gain_row
 
 
-def relayed(rows, lat_size):
-    return lat_size == 2 and rows % 32 == 0
-
-
-def join_kernel(sizes, cuts, waits, *refs):
-    outs = refs[len(refs) - len(sizes) - len(cuts) :]
-    place = 0
-    for size, column_ref in zip(sizes, outs):
-        for index in range(size):
-            column_ref[index] = refs[place + index][...]
-        place += size
-    for (block, count), chunk_ref in zip(cuts, outs[len(sizes) :]):
-        half = chunk_ref.shape[0]
+def relayed(rows, lon_size, lat_size):
+    return lat_size == 2 and rows % 32 == 0 and lon_size == 16
+
+
+def join_kernel(columns, cuts, *refs):
+    outs = refs[len(refs) - sum(len(widths) for _, widths in columns) - len(cuts) :]
+    place, out = 0, 0
+    for count, widths in columns:
+        row = 0
+        for piece in refs[place : place + count]:
+            start = 0
+            for target, width in zip(outs[out : out + len(widths)], widths):
+                target[row : row + piece.shape[0]] = piece[:, :, start : start + width]
+                start += width
+            row += piece.shape[0]
+        place, out = place + count, out + len(widths)
+    for blocks, chunk_ref in zip(cuts, outs[out:]):
+        half = chunk_ref.shape[1]
         first = pl.multiple_of(lax.axis_index("lat") * half, 16)
         start = 0
-        for source in refs[place : place + count]:
+        for block, source in zip(blocks, refs[place : place + len(blocks)]):
             width = source.shape[2]
-            chunk_ref[:, start : start + width] = source[block, pl.ds(first, half), :]
+            chunk_ref[0, :, start : start + width] = source[block, pl.ds(first, half), :]
             start += width
-        place += count
-
-
-def join(columns, cuts=(), after=()):
+        place += len(blocks)
+
+
+def join(columns, cuts=(), after=(), widths=None):
     pieces = [piece for column in columns for piece in column]
-    sources = [weight for _, weights in cuts for weight in weights]
-    out_shape = [
-        jax.ShapeDtypeStruct((len(column),) + column[0].shape, jnp.bfloat16) for column in columns
-    ]
-    for _, weights in cuts:
-        width = sum(weight.shape[2] for weight in weights)
-        out_shape.append(jax.ShapeDtypeStruct((weights[0].shape[1] // 2, width), jnp.bfloat16))
-    kernel = functools.partial(
-        join_kernel,
-        [len(column) for column in columns],
-        [(block, len(weights)) for block, weights in cuts],
-        len(after),
-    )
+    sources = [weight for cut in cuts for _, weight in cut]
+    out_shape, sizes = [], []
+    for column in columns:
+        count, half, width = column[0].shape
+        count = sum(piece.shape[0] for piece in column)
+        sizes.append((len(column), widths or (width,)))
+        for part in widths or (width,):
+            out_shape.append(jax.ShapeDtypeStruct((count, half, part), jnp.bfloat16))
+    for cut in cuts:
+        width = sum(weight.shape[2] for _, weight in cut)
+        out_shape.append(jax.ShapeDtypeStruct((1, cut[0][1].shape[1] // 2, width), jnp.bfloat16))
     held = pl.BlockSpec(memory_space=pltpu.VMEM)
     return pl.pallas_call(
-        kernel,
+        functools.partial(join_kernel, sizes, [[block for block, _ in cut] for cut in cuts]),
         out_shape=out_shape,
         in_specs=[held] * (len(pieces) + len(sources)) + [ANY] * len(after),
-        compiler_params=pltpu.CompilerParams(vmem_limit_bytes=8 * 2**20),
+        compiler_params=pltpu.CompilerParams(vmem_limit_bytes=10 * 2**20),
     )(*pieces, *sources, *after)
 
 
@@ -91,12 +95,16 @@
     return lax.ppermute(block, ("lon", "lat"), pairs)
 
 
-def along_z(own):
-    depth = lax.axis_size("lon") // 4
-    return [own] + [
-        send(own, lambda z, y, x, c, step=step: ((z + step) % depth, y, x, c))
-        for step in range(1, depth)
-    ]
+def across_z(block, bit):
+    return send(block, lambda z, y, x, c: (z ^ bit, y, x, c))
+
+
+def along_z(block, after=()):
+    bit = 2
+    while bit < lax.axis_size("lon") // 4:
+        (block,) = join([[block, across_z(block, bit)]], (), after)
+        bit *= 2
+    return block
 
 
 def swap(z, y, x, c):
@@ -126,7 +134,8 @@
         copy.start()
         copy.wait()
         return
-    depth, half, _ = pieces[0].shape
+    half = pieces[0].shape[-2]
+    lon_size = lax.axis_size("lon")
     copies = [
         pltpu.make_async_copy(piece, stage_ref.at[index], sem.at[index])
         for index, piece in enumerate(pieces)
@@ -136,13 +145,16 @@
     lon, lat = lax.axis_index("lon"), lax.axis_index("lat")
     z, y, x = lon // 4, lon // 2 % 2, lon % 2
     squares = (y * 2 + x, y * 2 + 1 - x, (1 - y) * 2 + x, (1 - y) * 2 + 1 - x)
+    joined = len(pieces) == 2
     for index, copy in enumerate(copies):
-        core = lat if index < 4 else 1 - lat
+        core = lat if index < len(pieces) // 2 else 1 - lat
         copy.wait()
-        for step in range(depth):
-            shard = (z + depth - step) % depth * 4 + squares[index % 4]
-            row = pl.multiple_of((shard * 2 + core) * half, 16)
-            w_ref[pl.ds(row, half), :] = stage_ref[index, step]
+        for column in range(4) if joined else (index % 4,):
+            for step in range(lon_size // 4):
+                shard = (z ^ step) * 4 + squares[column]
+                row = pl.multiple_of((shard * 2 + core) * half, 16)
+                place = column * (lon_size // 4) + step if joined else step
+                w_ref[pl.ds(row, half), :] = stage_ref[index, place]
 
 
 def load_scratch(pieces, rows, width):
@@ -199,7 +211,11 @@
         channel == lax.broadcasted_iota(jnp.int32, (WIDE, WIDE), 1) // HEAD, 1.0, 0.0
     ).astype(jnp.bfloat16)
     lane_head = lax.broadcasted_iota(jnp.int32, (1, WIDE), 1) // HEAD
-    masks = [jnp.where(lane_head == head, 1.0, 0.0).astype(jnp.bfloat16) for head in range(GROUP)]
+    ones = lambda condition: jnp.where(condition, 1.0, 0.0).astype(jnp.bfloat16)
+    pairs = [ones(lane_head % PART == head) for head in range(PART)]
+    halves = [ones(lane_head // PART == part) for part in range(2)]
+    masks = [ones(lane_head == head) for head in range(GROUP)]
+    narrow = [ones(lane_head[:, :MAIN] == head) for head in range(PART)]
 
     def units(part):
         rounded = part.astype(jnp.bfloat16)
@@ -215,24 +231,37 @@
         for window in range(held):
             own = slice(window * CELLS, (window + 1) * CELLS)
             query, key, value = queries[own], keys[own], values[own]
-            stacked = jnp.concatenate([query * mask for mask in masks], 0)
-            main = jnp.exp2(dot(stacked, key[:MAIN], NT)).astype(jnp.bfloat16)
+            stacked = jnp.concatenate([query * pair for pair in pairs], 0)
+            main_keys = jnp.concatenate([key[:MAIN] * half for half in halves], 0)
+            main = jnp.exp2(dot(stacked, main_keys, NT)).astype(jnp.bfloat16)
             rest_keys = jnp.concatenate([key[MAIN:] * mask for mask in masks], 0)
             rest = jnp.exp2(dot(query, rest_keys, NT)).astype(jnp.bfloat16)
-            parts = [main[head * CELLS : (head + 1) * CELLS] for head in range(GROUP)] + [rest]
             if shifted:
                 last = jnp.logical_and(
                     (pl.program_id(0) * held + window) % row_windows == row_windows - 1,
                     lax.axis_index("lat") == lax.axis_size("lat") - 1,
                 )
                 allow = jnp.where(last, allow_ref[...], 1.0).astype(jnp.bfloat16)
-                parts = [part * allow[:, :MAIN] for part in parts[:-1]] + [rest * allow[:, MAIN:]]
-            weights = jnp.concatenate(parts, 1)
-            stacked = jnp.concatenate(
-                [value[:MAIN] * mask for mask in masks] + [value[MAIN:] * mask for mask in masks], 0
-            )
-            total = dot(weights, ones_ref[...])
-            attended[window].append((dot(weights, stacked) / total).astype(jnp.bfloat16))
+                rest = rest * allow[:, MAIN:]
+            for part in range(2):
+                lanes = slice(part * MAIN, (part + 1) * MAIN)
+                parts = [main[head * CELLS : (head + 1) * CELLS, lanes] for head in range(PART)]
+                if shifted:
+                    parts = [one * allow[:, :MAIN] for one in parts]
+                own_value = value[:, lanes]
+                none = jnp.zeros((REST, MAIN), jnp.bfloat16)
+                own_rest = [own_value[MAIN:] * mask for mask in narrow]
+                other_rest = [none] * PART
+                stacked = jnp.concatenate(
+                    [own_value[:MAIN] * mask for mask in narrow]
+                    + (own_rest + other_rest if part == 0 else other_rest + own_rest),
+                    0,
+                )
+                both = jnp.concatenate([stacked, ones_ref[:, lanes]], 1)
+                summed = dot(jnp.concatenate(parts + [rest], 1), both)
+                attended[window].append(
+                    (summed[:, :MAIN] / summed[:, MAIN:]).astype(jnp.bfloat16)
+                )
     attended = jnp.concatenate([jnp.concatenate(parts, 1) for parts in attended], 0)
     projected = dot(attended, w_ref[:, 3 * features :])
     middle = tokens.astype(jnp.float32) + layer_norm(projected, gain_ref[...])
@@ -246,8 +275,12 @@
 
 
 def head_columns():
-    rows = np.concatenate([np.repeat(np.arange(GROUP), MAIN), np.repeat(np.arange(GROUP), REST)])
-    return (rows[:, None] == np.arange(WIDE)[None, :] // HEAD).astype(np.float32)
+    halves = []
+    for part in range(2):
+        own = np.arange(part * PART, (part + 1) * PART)
+        rows = np.concatenate([np.repeat(own, MAIN), np.repeat(np.arange(GROUP), REST)])
+        halves.append(rows[:, None] == np.repeat(own, HEAD)[None, :])
+    return np.concatenate(halves, 1).astype(np.float32)
 
 
 def attend(sources, pieces, gain, sharp, row_windows, after=(), held=2):
@@ -365,7 +398,7 @@
     features = behind.shape[-1]
     flat = lambda side: side.reshape(-1, QUARTER, features)[:-1]
     c, r = WLON // 2, WLAT // 2
-    own = jnp.concatenate([strip(flat(side)) for side in sides[:-1]], 0)
+    own = jnp.concatenate([strip(flat(side)) for side in sides], 0)
     tops = jnp.concatenate([strip(low[None]) for low in below], 0)
     first = jnp.concatenate([strip(corner[None]), strip(flat(behind))], 1)
     return jnp.concatenate([first, jnp.concatenate([tops, own], 1)], 0)
@@ -376,7 +409,7 @@
     hidden_size = up_weight.shape[-1]
     row_windows = rows // WLAT
     weights = (qkv_weight, out_weight, up_weight, down_weight)
-    relay = relayed(qkv_weight.shape[1], lax.axis_size("lat"))
+    relay = relayed(qkv_weight.shape[1], lax.axis_size("lon"), lax.axis_size("lat"))
     spread = np.arange(HEADS)[:, None] == np.arange(features)[None, :] // HEAD
     sharp = logit_scale[:, :, None] * jnp.asarray(spread * math.log2(math.e), jnp.float32)[None]
     sharp = jnp.sum(sharp, 1)
@@ -392,25 +425,33 @@
 
     low_edge, high_edge = (0, 0), (row_windows - 1, 1)
     if relay:
-        attend_weights, feed_weights = weights[:2], weights[2:]
-        (own,) = join([], [(0, attend_weights)])
-        column, feed_own, own = join(
-            [along_z(own)], [(0, feed_weights), (1, attend_weights)], (windows,)
+        (own,) = join([], [[(0, weight) for weight in weights[:2]]])
+        later = [(0, weight) for weight in weights[2:]] + [(1, weight) for weight in weights]
+        (later_own,) = join([], [later])
+        attend_width, feed_width = (
+            sum(weight.shape[2] for weight in pair) for pair in (weights[:2], weights[2:])
         )
+        (pair,) = join([[own, across_z(own, 1)]], (), (windows,))
+        column = along_z(pair)
         pieces = whole_pieces(column, to_neighbours(column))
-        feed_column, column, last_own = join(
-            [along_z(feed_own), along_z(own)], [(1, feed_weights)]
+        feed_pair, last_pair = join(
+            [[later_own, across_z(later_own, 1)]], widths=(feed_width, attend_width + feed_width)
         )
+        feed_column = along_z(feed_pair)
         feed_received = to_neighbours(feed_column)
+        last_pair = tied(last_pair, feed_column)
+        last_other = across_z(last_pair, 2)
         middle = attention(0, [windows], pieces, (feed_column,))
-        feed_pieces = whole_pieces(feed_column, feed_received, middle)
-        received = to_neighbours(tied(column, middle))
-        left_0, right_0, low_0 = forward(0, middle, 0, feed_pieces, low_edge)
-        left_1, right_1, low_1 = forward(0, middle, 1, feed_pieces, low_edge, (low_0,))
-        pieces = whole_pieces(column, received, low_1)
-        (last_column,) = join([along_z(last_own)], (), (low_1,))
-        received = to_neighbours(last_column)
-        after = (last_column,)
+        feed_pieces = whole_pieces(feed_column, feed_received, (middle, last_other))
+        column, last_column = join(
+            [[last_pair, last_other]], (), tuple(feed_pieces[4:]), (attend_width, feed_width)
+        )
+        received = to_neighbours(column)
+        left_0, right_0, low_0 = forward(0, middle, 0, feed_pieces, low_edge, (column,))
+        (joined,) = join([[column] + [tied(part, low_0) for part in received]])
+        pieces = [joined, send(joined, swap)]
+        last_received = to_neighbours(tied(last_column, joined))
+        left_1, right_1, low_1 = forward(0, middle, 1, feed_pieces, low_edge, (joined,))
     else:
         gathered = []
         for block in range(2):
@@ -421,22 +462,22 @@
         middle = attention(0, [windows], first_pieces)
         left_0, right_0, low_0 = forward(0, middle, 0, feed_pieces, low_edge)
         left_1, right_1, low_1 = forward(0, middle, 1, feed_pieces, low_edge)
-        after = ()
     ahead = shift_from(left_0, 1, 0)
     low = jnp.concatenate([low_0, low_1], 0)
     ahead_low = shift_from(low_0, 1, 1)
     below = shift_from(low, 0, 1)
     sources = [left_0, right_0, left_1, right_1, ahead, below, ahead_low]
-    middle = attention(1, sources, pieces, after)
+    middle = attention(1, sources, pieces)
     if relay:
-        last_pieces = whole_pieces(last_column, received, middle)
+        last_pieces = whole_pieces(last_column, last_received, middle)
     left_1, right_1, high_1 = forward(1, middle, 1, last_pieces, high_edge)
     behind = shift_from(right_1, -1, 0)
     corner = shift_from(high_1, -1, -1)
     left_0, right_0, high_0 = forward(1, middle, 0, last_pieces, high_edge, (high_1,))
     above = shift_from(jnp.concatenate([high_0, high_1], 0), 0, -1)
+    sides, above, corner = tied(((left_0, right_0, left_1), above, corner), behind)
     return back_in_place(
-        (left_0, right_0, left_1, right_1), behind, (above[0], above[1], above[2]), corner[1]
+        sides, behind, (above[0], above[1], above[2]), corner[1]
     )
 
 

time: 151 us -> 145 us (0.960)
  starting transfers between devices: 45.5 us -> 31.2 us
  waiting for transfers between devices: 47.4 us -> 58.2 us
  Pallas kernels: 49.1 us -> 46.2 us
    ppermute x40 -> x30, waiting for transfers between devices: 31.3 us -> 48.4 us  [send(): return lax.ppermute(block, ('lon', 'lat'), pairs)]
    ppermute x40 -> x30, starting transfers between devices: 40.4 us -> 23.8 us  [send(): return lax.ppermute(block, ('lon', 'lat'), pairs)]
    ppermute x6, waiting for transfers between devices: 16.1 us -> 9.8 us  [shift_from(): return lax.ppermute(block, ('lon', 'lat'), pairs)]
    pallas_call x2, Pallas kernels: 29.6 us -> 26.7 us  [attend(): pl.pallas_call(functools.partial(attend_kernel, shifted, row_windows, len...]
    ppermute x6, starting transfers between devices: 5.08 us -> 7.4 us  [shift_from(): return lax.ppermute(block, ('lon', 'lat'), pairs)]
  transfers between devices with their start and end apart: 46 -> 36, of which waited for: 18 -> 17; matrix products, arithmetic and copies ran while one was open for 3% -> 2% of each run, Pallas kernels for 26% -> 28%
where the time goes in v7:
time: 145 us
  waiting for transfers between devices  58.2 us (40%)
  Pallas kernels  46.2 us (32%)
  starting transfers between devices  31.2 us (22%)
  local copies, waits for them, and re-layouts  5.9 us (4%)
  other arithmetic  3.03 us (2%)
    ppermute x30, waiting for transfers between devices, send(): return lax.ppermute(block, ('lon', 'lat'), pairs)  48.4 us
    pallas_call x2, Pallas kernels, attend(): pl.pallas_call(functools.partial(attend_kernel, shifted, row_windows, len...  26.7 us
    ppermute x30, starting transfers between devices, send(): return lax.ppermute(block, ('lon', 'lat'), pairs)  23.8 us
    pallas_call x4, Pallas kernels, feed(): pl.pallas_call(functools.partial(feed_kernel, len(pieces), hidden_size, 5...  19.3 us
    ppermute x6, waiting for transfers between devices, shift_from(): return lax.ppermute(block, ('lon', 'lat'), pairs)  9.8 us
    ppermute x6, starting transfers between devices, shift_from(): return lax.ppermute(block, ('lon', 'lat'), pairs)  7.4 us
  transfers between devices with their start and end apart: 36, of which 17 were waited for; matrix products, arithmetic and copies ran while one was open for 2% of the time, Pallas kernels for 28%

profile of v7, /device:TPU:0, one launch (start us, length us, event | category | flops | bytes accessed | tf_op | source)
XLA Modules:
  0.0 144.9 jit_solution(18317492058217962292)
XLA Ops:
  0.0 0.9 copy-done.2
  0.9 0.8 copy-done.4
  1.8 3.0 %collective-permute-start = (bf16[1,16,2048]{2,1,0:T(8,128)(2,1)S(1)}, bf16[1,16,2048]{2,1,0:T(8,128)(2,1)S(1)}, u32[]{:S(2)}, u32[]{:S(2)}) collective-permute-start(bf16[1,16,2048]{2,1,0:T(8,128)(2,1)S(1)} %shard_map.109.refs_0_), channel_id=1, source_target_pairs={{0,8},{1,9},{2,10},{3,11},{4,12},{5,13},{6,14},{7,15},{8,0},{9,1},... | collective-permute-start | bytes 196616 | tf_op jit(solution)/shard_map/ppermute | solution.py:95
  4.8 2.1 %copy.23 = bf16[2,2,6,4,2,3,2,512]{7,6,5,2,4,1,3,0:T(2,128)(2,1)S(1)} copy(bf16[2,2,6,4,2,3,2,512]{7,6,5,4,3,2,1,0:T(2,128)(2,1)} %bitcast.32) | data formatting | bytes 2359296 | tf_op jit(solution)/shard_map/reshape | solution.py:385
  6.9 0.5 reshape.45.refs_2_.refs_0_
  7.5 2.7 %collective-permute-start.1 = (bf16[2,16,2048]{2,1,0:T(8,128)(2,1)S(1)}, bf16[2,16,2048]{2,1,0:T(8,128)(2,1)S(1)}, u32[]{:S(2)}, u32[]{:S(2)}) collective-permute-start(bf16[2,16,2048]{2,1,0:T(8,128)(2,1)S(1)} %shard_map.110.refs_0_), channel_id=1, source_target_pairs={{0,16},{1,17},{2,18},{3,19},{4,20},{5,21},{6,22},{7,23},{8,24},{9,... | collective-permute-start | bytes 393224 | tf_op jit(solution)/shard_map/ppermute | solution.py:95
  10.3 1.6 %collective-permute-start.9 = (bf16[1,16,10240]{2,1,0:T(8,128)(2,1)S(1)}, bf16[1,16,10240]{2,1,0:T(8,128)(2,1)S(1)}, u32[]{:S(2)}, u32[]{:S(2)}) collective-permute-start(bf16[1,16,10240]{2,1,0:T(8,128)(2,1)S(1)} %shard_map.112.refs_0_), channel_id=1, source_target_pairs={{0,8},{1,9},{2,10},{3,11},{4,12},{5,13},{6,14},{7,15},{8,0},{9,1},... | collective-permute-start | bytes 983048 | tf_op jit(solution)/shard_map/ppermute | solution.py:95
  11.9 4.4 %collective-permute-done.1.refs_1_ = bf16[2,16,2048]{2,1,0:T(8,128)(2,1)S(1)} collective-permute-done((bf16[2,16,2048]{2,1,0:T(8,128)(2,1)S(1)}, bf16[2,16,2048]{2,1,0:T(8,128)(2,1)S(1)}, u32[]{:S(2)}, u32[]{:S(2)}) %collective-permute-start.1) | collective-permute-done | bytes 131104 | tf_op jit(solution)/shard_map/ppermute | solution.py:95
  16.3 1.6 %collective-permute-start.2 = (bf16[4,16,2048]{2,1,0:T(8,128)(2,1)S(1)}, bf16[4,16,2048]{2,1,0:T(8,128)(2,1)S(1)}, u32[]{:S(2)}, u32[]{:S(2)}) collective-permute-start(bf16[4,16,2048]{2,1,0:T(8,128)(2,1)S(1)} %shard_map.111.refs_1_), channel_id=1, source_target_pairs={{0,2},{1,3},{2,0},{3,1},{4,6},{5,7},{6,4},{7,5},{8,10},{9,11},{10,... | collective-permute-start | bytes 786440 | tf_op jit(solution)/shard_map/ppermute | solution.py:95
  17.8 1.5 %collective-permute-start.3 = (bf16[4,16,2048]{2,1,0:T(8,128)(2,1)S(1)}, bf16[4,16,2048]{2,1,0:T(8,128)(2,1)S(1)}, u32[]{:S(2)}, u32[]{:S(2)}) collective-permute-start(bf16[4,16,2048]{2,1,0:T(8,128)(2,1)S(1)} %shard_map.111.refs_1_), channel_id=1, source_target_pairs={{0,4},{1,5},{2,6},{3,7},{4,0},{5,1},{6,2},{7,3},{8,12},{9,13},{10,... | collective-permute-start | bytes 786440 | tf_op jit(solution)/shard_map/ppermute | solution.py:95
  19.4 0.5 collective-permute-start.4
  19.8 0.1 multiply_reduce_fusion
  19.9 0.1 collective-permute-start.5
  20.0 1.7 %collective-permute-done.9.refs_1_ = bf16[1,16,10240]{2,1,0:T(8,128)(2,1)S(1)} collective-permute-done((bf16[1,16,10240]{2,1,0:T(8,128)(2,1)S(1)}, bf16[1,16,10240]{2,1,0:T(8,128)(2,1)S(1)}, u32[]{:S(2)}, u32[]{:S(2)}) %collective-permute-start.9) | collective-permute-done | bytes 327712 | tf_op jit(solution)/shard_map/ppermute | solution.py:95
  21.7 0.1 collective-permute-start.10
  21.9 3.7 %collective-permute-done.2.refs_2_ = bf16[4,16,2048]{2,1,0:T(8,128)(2,1)S(1)} collective-permute-done((bf16[4,16,2048]{2,1,0:T(8,128)(2,1)S(1)}, bf16[4,16,2048]{2,1,0:T(8,128)(2,1)S(1)}, u32[]{:S(2)}, u32[]{:S(2)}) %collective-permute-start.2) | collective-permute-done | bytes 262176 | tf_op jit(solution)/shard_map/ppermute | solution.py:95
  25.6 5.6 %collective-permute-done.3.refs_3_ = bf16[4,16,2048]{2,1,0:T(8,128)(2,1)S(1)} collective-permute-done((bf16[4,16,2048]{2,1,0:T(8,128)(2,1)S(1)}, bf16[4,16,2048]{2,1,0:T(8,128)(2,1)S(1)}, u32[]{:S(2)}, u32[]{:S(2)}) %collective-permute-start.3) | collective-permute-done | bytes 262176 | tf_op jit(solution)/shard_map/ppermute | solution.py:95
  31.2 0.5 collective-permute-start.8
  31.7 3.8 %collective-permute-done.10.refs_1_ = bf16[2,16,4096]{2,1,0:T(8,128)(2,1)S(1)} collective-permute-done((bf16[2,16,4096]{2,1,0:T(8,128)(2,1)S(1)}, bf16[2,16,4096]{2,1,0:T(8,128)(2,1)S(1)}, u32[]{:S(2)}, u32[]{:S(2)}) %collective-permute-start.10) | collective-permute-done | bytes 262176 | tf_op jit(solution)/shard_map/ppermute | solution.py:95
  35.5 1.6 %collective-permute-start.11 = (bf16[4,16,4096]{2,1,0:T(8,128)(2,1)S(1)}, bf16[4,16,4096]{2,1,0:T(8,128)(2,1)S(1)}, u32[]{:S(2)}, u32[]{:S(2)}) collective-permute-start(bf16[4,16,4096]{2,1,0:T(8,128)(2,1)S(1)} %shard_map.114.refs_12_.refs_1_), channel_id=1, source_target_pairs={{0,2},{1,3},{2,0},{3,1},{4,6},{5,7},{6,4},{7,5},{8,10},{9,11},{10,... | collective-permute-start | bytes 1572872 | tf_op jit(solution)/shard_map/ppermute | solution.py:95
  37.1 1.5 %collective-permute-start.12 = (bf16[4,16,4096]{2,1,0:T(8,128)(2,1)S(1)}, bf16[4,16,4096]{2,1,0:T(8,128)(2,1)S(1)}, u32[]{:S(2)}, u32[]{:S(2)}) collective-permute-start(bf16[4,16,4096]{2,1,0:T(8,128)(2,1)S(1)} %shard_map.114.refs_12_.refs_1_), channel_id=1, source_target_pairs={{0,4},{1,5},{2,6},{3,7},{4,0},{5,1},{6,2},{7,3},{8,12},{9,13},{10,... | collective-permute-start | bytes 1572872 | tf_op jit(solution)/shard_map/ppermute | solution.py:95
  38.6 0.5 collective-permute-start.13
  39.1 0.1 collective-permute-start.15
  39.2 13.4 %shard_map.115.refs_0_ = bf16[8,144,512]{2,1,0:T(8,128)(2,1)S(1)} custom-call(bf16[8,144,512]{2,1,0:T(8,128)(2,1)S(1)} %reshape.45.refs_2_.refs_0_, bf16[4,16,2048]{2,1,0:T(8,128)(2,1)S(1)} %shard_map.111.refs_1_, bf16[4,16,2048]{2,1,0:T(8,128)(2,1)S(1)} %collective-permute-done.2.refs_2_, bf16[4,16,2048]{2,1,0:T(8,128)(2,1)S(1)} %collective-permute-done.3.refs_3_, ...), custom_call_target="tpu_custom_call" | custom-call | flops 16000000000 | bytes 6000000 | tf_op jit(solution)/shard_map/pallas_call | solution.py:294
  52.6 6.7 %collective-permute-done.15.refs_1_ = bf16[2,16,6144]{2,1,0:T(8,128)(2,1)S(1)} collective-permute-done((bf16[2,16,6144]{2,1,0:T(8,128)(2,1)S(1)}, bf16[2,16,6144]{2,1,0:T(8,128)(2,1)S(1)}, u32[]{:S(2)}, u32[]{:S(2)}) %collective-permute-start.15) | collective-permute-done | bytes 393248 | tf_op jit(solution)/shard_map/ppermute | solution.py:95
  59.4 2.5 %collective-permute-done.12.refs_3_ = bf16[4,16,4096]{2,1,0:T(8,128)(2,1)S(1)} collective-permute-done((bf16[4,16,4096]{2,1,0:T(8,128)(2,1)S(1)}, bf16[4,16,4096]{2,1,0:T(8,128)(2,1)S(1)}, u32[]{:S(2)}, u32[]{:S(2)}) %collective-permute-start.12) | collective-permute-done | bytes 524320 | tf_op jit(solution)/shard_map/ppermute | solution.py:95
  61.9 0.5 collective-permute-start.18
  62.4 1.4 collective-permute-done.17.refs_4_.refs_7_
  63.8 0.7 collective-permute-done.18.refs_5_.refs_8_
  64.6 0.5 collective-permute-start.19
  65.2 1.6 %collective-permute-start.20 = (bf16[4,16,2048]{2,1,0:T(8,128)(2,1)S(1)}, bf16[4,16,2048]{2,1,0:T(8,128)(2,1)S(1)}, u32[]{:S(2)}, u32[]{:S(2)}) collective-permute-start(bf16[4,16,2048]{2,1,0:T(8,128)(2,1)S(1)} %get-tuple-element.43.refs_10_.refs_0_), channel_id=1, source_target_pairs={{0,4},{1,5},{2,6},{3,7},{4,0},{5,1},{6,2},{7,3},{8,12},{9,13},{10,... | collective-permute-start | bytes 786440 | tf_op jit(solution)/shard_map/ppermute | solution.py:95
  66.7 1.4 collective-permute-start.21
  68.2 4.8 %shard_map.117 = (bf16[4,2,36,512]{3,2,1,0:T(8,128)(2,1)S(1)}, bf16[4,2,36,512]{3,2,1,0:T(8,128)(2,1)S(1)}, bf16[2,36,512]{2,1,0:T(8,128)(2,1)S(1)}) custom-call(bf16[8,144,512]{2,1,0:T(8,128)(2,1)S(1)} %shard_map.115.refs_0_, bf16[4,16,4096]{2,1,0:T(8,128)(2,1)S(1)} %shard_map.114.refs_12_.refs_1_, ...), custom_call_target="tpu_custom_call" | custom-call | flops 4831838208 | bytes 8000000 | tf_op jit(solution)/shard_map/pallas_call | solution.py:352
  73.0 0.8 collective-permute-done.19.refs_1_
  73.8 4.1 %collective-permute-done.20.refs_2_ = bf16[4,16,2048]{2,1,0:T(8,128)(2,1)S(1)} collective-permute-done((bf16[4,16,2048]{2,1,0:T(8,128)(2,1)S(1)}, bf16[4,16,2048]{2,1,0:T(8,128)(2,1)S(1)}, u32[]{:S(2)}, u32[]{:S(2)}) %collective-permute-start.20) | collective-permute-done | bytes 262176 | tf_op jit(solution)/shard_map/ppermute | solution.py:95
  78.0 1.6 %collective-permute-done.21.refs_3_ = bf16[4,16,2048]{2,1,0:T(8,128)(2,1)S(1)} collective-permute-done((bf16[4,16,2048]{2,1,0:T(8,128)(2,1)S(1)}, bf16[4,16,2048]{2,1,0:T(8,128)(2,1)S(1)}, u32[]{:S(2)}, u32[]{:S(2)}) %collective-permute-start.21) | collective-permute-done | bytes 262176 | tf_op jit(solution)/shard_map/ppermute | solution.py:95
  79.8 3.3 %collective-permute-start.22 = (bf16[4,2,36,512]{3,2,1,0:T(8,128)(2,1)S(1)}, bf16[4,2,36,512]{3,2,1,0:T(8,128)(2,1)S(1)}, u32[]{:S(2)}, u32[]{:S(2)}) collective-permute-start(bf16[4,2,36,512]{3,2,1,0:T(8,128)(2,1)S(1)} %get-tuple-element.44.refs_0_), channel_id=1, source_target_pairs={{2,0},{3,1},{4,2},{5,3},{6,4},{7,5},{8,6},{9,7},{10,8},{11,9},{12,... | collective-permute-start | bytes 884744 | tf_op jit(solution)/shard_map/ppermute | solution.py:379
  83.1 4.8 %shard_map.119 = (bf16[4,2,36,512]{3,2,1,0:T(8,128)(2,1)S(1)}, bf16[4,2,36,512]{3,2,1,0:T(8,128)(2,1)S(1)}, bf16[2,36,512]{2,1,0:T(8,128)(2,1)S(1)}) custom-call(bf16[8,144,512]{2,1,0:T(8,128)(2,1)S(1)} %shard_map.115.refs_0_, bf16[4,16,4096]{2,1,0:T(8,128)(2,1)S(1)} %shard_map.114.refs_12_.refs_1_, ...), custom_call_target="tpu_custom_call" | custom-call | flops 4831838208 | bytes 8000000 | tf_op jit(solution)/shard_map/pallas_call | solution.py:352
  87.9 0.2 collective-permute-start.23
  88.2 0.5 collective-permute-start.24
  88.6 0.2 collective-permute-start.29
  88.9 3.7 %collective-permute-done.24.refs_6_ = bf16[2,36,512]{2,1,0:T(8,128)(2,1)S(1)} collective-permute-done((bf16[2,36,512]{2,1,0:T(8,128)(2,1)S(1)}, bf16[2,36,512]{2,1,0:T(8,128)(2,1)S(1)}, u32[]{:S(2)}, u32[]{:S(2)}) %collective-permute-start.24) | collective-permute-done | bytes 73760 | tf_op jit(solution)/shard_map/ppermute | solution.py:379
  92.6 0.3 collective-permute-start.26
  92.9 2.4 %collective-permute-start.27 = (bf16[4,16,4096]{2,1,0:T(8,128)(2,1)S(1)}, bf16[4,16,4096]{2,1,0:T(8,128)(2,1)S(1)}, u32[]{:S(2)}, u32[]{:S(2)}) collective-permute-start(bf16[4,16,4096]{2,1,0:T(8,128)(2,1)S(1)} %get-tuple-element.54.refs_1_), channel_id=1, source_target_pairs={{0,4},{1,5},{2,6},{3,7},{4,0},{5,1},{6,2},{7,3},{8,12},{9,13},{10,... | collective-permute-start | bytes 1572872 | tf_op jit(solution)/shard_map/ppermute | solution.py:95
  95.3 0.8 collective-permute-start.28
  96.1 13.3 %shard_map.120.refs_0_ = bf16[8,144,512]{2,1,0:T(8,128)(2,1)S(1)} custom-call(bf16[4,2,36,512]{3,2,1,0:T(8,128)(2,1)S(1)} %get-tuple-element.44.refs_0_, bf16[4,2,36,512]{3,2,1,0:T(8,128)(2,1)S(1)} %get-tuple-element.45.refs_1_, bf16[4,2,36,512]{3,2,1,0:T(8,128)(2,1)S(1)} %get-tuple-element.50.refs_2_, ...), custom_call_target="tpu_custom_call" | custom-call | flops 16000000000 | bytes 6000000 | tf_op jit(solution)/shard_map/pallas_call | solution.py:294
  109.5 9.2 %collective-permute-done.27.refs_3_ = bf16[4,16,4096]{2,1,0:T(8,128)(2,1)S(1)} collective-permute-done((bf16[4,16,4096]{2,1,0:T(8,128)(2,1)S(1)}, bf16[4,16,4096]{2,1,0:T(8,128)(2,1)S(1)}, u32[]{:S(2)}, u32[]{:S(2)}) %collective-permute-start.27) | collective-permute-done | bytes 524320 | tf_op jit(solution)/shard_map/ppermute | solution.py:95
  118.6 0.5 collective-permute-start.32
  119.2 1.4 collective-permute-done.31.refs_7_
  120.5 0.7 collective-permute-done.32.refs_8_
  121.3 4.8 %shard_map.121 = (bf16[4,2,36,512]{3,2,1,0:T(8,128)(2,1)S(1)}, bf16[4,2,36,512]{3,2,1,0:T(8,128)(2,1)S(1)}, bf16[2,36,512]{2,1,0:T(8,128)(2,1)S(1)}) custom-call(bf16[8,144,512]{2,1,0:T(8,128)(2,1)S(1)} %shard_map.120.refs_0_, bf16[4,16,4096]{2,1,0:T(8,128)(2,1)S(1)} %get-tuple-element.54.refs_1_, bf16[4,16,4096]{2,1,0:T(8,128)(2,1)S(1)} %collective-permute-done.26.refs_2_, ...), custom_call_target="tpu_custom_call" | custom-call | flops 4831838208 | bytes 8000000 | tf_op jit(solution)/shard_map/pallas_call | solution.py:352
  126.1 0.8 collective-permute-start.35
  126.9 4.8 %shard_map.122 = (bf16[4,2,36,512]{3,2,1,0:T(8,128)(2,1)S(1)}, bf16[4,2,36,512]{3,2,1,0:T(8,128)(2,1)S(1)}, bf16[2,36,512]{2,1,0:T(8,128)(2,1)S(1)}) custom-call(bf16[8,144,512]{2,1,0:T(8,128)(2,1)S(1)} %shard_map.120.refs_0_, bf16[4,16,4096]{2,1,0:T(8,128)(2,1)S(1)} %get-tuple-element.54.refs_1_, bf16[4,16,4096]{2,1,0:T(8,128)(2,1)S(1)} %collective-permute-done.26.refs_2_, ...), custom_call_target="tpu_custom_call" | custom-call | flops 4831838208 | bytes 8000000 | tf_op jit(solution)/shard_map/pallas_call | solution.py:352
  131.8 2.6 %collective-permute-start.34 = (bf16[2,36,512]{2,1,0:T(8,128)(2,1)S(1)}, bf16[2,36,512]{2,1,0:T(8,128)(2,1)S(1)}, u32[]{:S(2)}, u32[]{:S(2)}) collective-permute-start(bf16[2,36,512]{2,1,0:T(8,128)(2,1)S(1)} %get-tuple-element.58.refs_10_), channel_id=1, source_target_pairs={{31,0},{30,1},{1,2},{0,3},{3,4},{2,5},{5,6},{4,7},{7,8},{6,9},{9,1... | collective-permute-start | bytes 221192 | tf_op jit(solution)/shard_map/ppermute | solution.py:379
  134.4 6.1 %collective-permute-done.34 = bf16[2,36,512]{2,1,0:T(8,128)(2,1)S(1)} collective-permute-done((bf16[2,36,512]{2,1,0:T(8,128)(2,1)S(1)}, bf16[2,36,512]{2,1,0:T(8,128)(2,1)S(1)}, u32[]{:S(2)}, u32[]{:S(2)}) %collective-permute-start.34) | collective-permute-done | bytes 73760 | tf_op jit(solution)/shard_map/ppermute | solution.py:379
  140.5 0.1 reshape.56
  140.6 0.2 copy.21
  140.8 0.1 reshape.53
  141.0 0.2 copy.20
  141.2 0.1 reshape.50
  141.3 0.2 copy.19
  141.7 0.1 reshape.47
  141.8 0.2 copy.18
  142.0 2.9 %maximum_maximum_fusion = bf16[24,24,2,512]{3,2,1,0:T(2,128)(2,1)} fusion(bf16[6,21,2,512]{3,2,1,0:T(2,128)(2,1)S(1)} %bitcast.33, bf16[6,21,2,512]{3,2,1,0:T(2,128)(2,1)S(1)} %bitcast.34, bf16[6,21,2,512]{3,2,1,0:T(2,128)(2,1)S(1)} %bitcast.35, bf16[6,3,2,512]{3,2,1,0:T(2,128)(2,1)S(1)} %reshape_transpose_reshape_broadcast_in_dim_squeeze.15, ...), kind=kLoop, calls=%fused_computation | loop fusion | flops 4128768 | bytes 2359296 | tf_op jit(solution)/shard_map/concatenate | solution.py:404
  (70 shorter events, 0.9 us)
Async XLA Ops:
  0.0 0.9 copy-start.2
  0.9 0.8 copy-start.4
  1.8 5.7 %collective-permute-start = (bf16[1,16,2048]{2,1,0:T(8,128)(2,1)S(1)}, bf16[1,16,2048]{2,1,0:T(8,128)(2,1)S(1)}, u32[]{:S(2)}, u32[]{:S(2)}) collective-permute-start(bf16[1,16,2048]{2,1,0:T(8,128)(2,1)S(1)} %shard_map.109.refs_0_), channel_id=1, source_target_pairs={{0,8},{1,9},{2,10},{3,11},{4,12},{5,13},{6,14},{7,15},{8,0},{9,1},... | collective-permute-start | bytes 196616 | tf_op jit(solution)/shard_map/ppermute | solution.py:95
  7.4 2.8 %copy-start = (bf16[2,32,2048]{2,1,0:T(8,128)(2,1)S(1)}, bf16[2,32,2048]{2,1,0:T(8,128)(2,1)}, u32[]{:S(2)}) copy-start(bf16[2,32,2048]{2,1,0:T(8,128)(2,1)} %refs_4_.1) | copy-start | bytes 786436
  7.4 2.8 %copy-start.1 = (bf16[2,32,2048]{2,1,0:T(8,128)(2,1)S(1)}, bf16[2,32,2048]{2,1,0:T(8,128)(2,1)}, u32[]{:S(2)}) copy-start(bf16[2,32,2048]{2,1,0:T(8,128)(2,1)} %refs_5_.1) | copy-start | bytes 786436
  7.4 2.8 %copy-start.3 = (bf16[2,32,1536]{2,1,0:T(8,128)(2,1)S(1)}, bf16[2,32,1536]{2,1,0:T(8,128)(2,1)}, u32[]{:S(2)}) copy-start(bf16[2,32,1536]{2,1,0:T(8,128)(2,1)} %refs_2_.1) | copy-start | bytes 589828
  7.4 2.8 %copy-start.5 = (bf16[2,32,512]{2,1,0:T(8,128)(2,1)S(1)}, bf16[2,32,512]{2,1,0:T(8,128)(2,1)}, u32[]{:S(2)}) copy-start(bf16[2,32,512]{2,1,0:T(8,128)(2,1)} %refs_3_.1) | copy-start | bytes 196612
  7.5 12.4 %copy-start.8 = (f32[16,512]{1,0:T(8,128)S(1)}, f32[16,512]{1,0:T(8,128)}, u32[]{:S(2)}) copy-start(f32[16,512]{1,0:T(8,128)} %constant.8.clone) | copy-start | bytes 98308
  7.5 12.4 %copy-start.10 = (f32[2,16]{1,0:T(2,128)S(1)}, f32[2,16]{1,0:T(2,128)}, u32[]{:S(2)}) copy-start(f32[2,16]{1,0:T(2,128)} %param.17) | copy-start | bytes 388
  7.5 24.2 %copy-start.9 = (f32[2,2,512]{2,1,0:T(2,128)S(1)}, f32[2,2,512]{2,1,0:T(2,128)}, u32[]{:S(2)}) copy-start(f32[2,2,512]{2,1,0:T(2,128)} %param.16) | copy-start | bytes 24580
  7.5 8.8 %collective-permute-start.1 = (bf16[2,16,2048]{2,1,0:T(8,128)(2,1)S(1)}, bf16[2,16,2048]{2,1,0:T(8,128)(2,1)S(1)}, u32[]{:S(2)}, u32[]{:S(2)}) collective-permute-start(bf16[2,16,2048]{2,1,0:T(8,128)(2,1)S(1)} %shard_map.110.refs_0_), channel_id=1, source_target_pairs={{0,16},{1,17},{2,18},{3,19},{4,20},{5,21},{6,22},{7,23},{8,24},{9,... | collective-permute-start | bytes 393224 | tf_op jit(solution)/shard_map/ppermute | solution.py:95
  10.2 29.0 %copy-start.6 = (bf16[640,256]{1,0:T(8,128)(2,1)S(1)}, bf16[640,256]{1,0:T(8,128)(2,1)}, u32[]{:S(2)}) copy-start(bf16[640,256]{1,0:T(8,128)(2,1)} %constant.9.clone.refs_11_) | copy-start | bytes 983044
  10.3 11.4 %collective-permute-start.9 = (bf16[1,16,10240]{2,1,0:T(8,128)(2,1)S(1)}, bf16[1,16,10240]{2,1,0:T(8,128)(2,1)S(1)}, u32[]{:S(2)}, u32[]{:S(2)}) collective-permute-start(bf16[1,16,10240]{2,1,0:T(8,128)(2,1)S(1)} %shard_map.112.refs_0_), channel_id=1, source_target_pairs={{0,8},{1,9},{2,10},{3,11},{4,12},{5,13},{6,14},{7,15},{8,0},{9,1},... | collective-permute-start | bytes 983048 | tf_op jit(solution)/shard_map/ppermute | solution.py:95
  16.3 9.3 %collective-permute-start.2 = (bf16[4,16,2048]{2,1,0:T(8,128)(2,1)S(1)}, bf16[4,16,2048]{2,1,0:T(8,128)(2,1)S(1)}, u32[]{:S(2)}, u32[]{:S(2)}) collective-permute-start(bf16[4,16,2048]{2,1,0:T(8,128)(2,1)S(1)} %shard_map.111.refs_1_), channel_id=1, source_target_pairs={{0,2},{1,3},{2,0},{3,1},{4,6},{5,7},{6,4},{7,5},{8,10},{9,11},{10,... | collective-permute-start | bytes 786440 | tf_op jit(solution)/shard_map/ppermute | solution.py:95
  17.8 13.3 %collective-permute-start.3 = (bf16[4,16,2048]{2,1,0:T(8,128)(2,1)S(1)}, bf16[4,16,2048]{2,1,0:T(8,128)(2,1)S(1)}, u32[]{:S(2)}, u32[]{:S(2)}) collective-permute-start(bf16[4,16,2048]{2,1,0:T(8,128)(2,1)S(1)} %shard_map.111.refs_1_), channel_id=1, source_target_pairs={{0,4},{1,5},{2,6},{3,7},{4,0},{5,1},{6,2},{7,3},{8,12},{9,13},{10,... | collective-permute-start | bytes 786440 | tf_op jit(solution)/shard_map/ppermute | solution.py:95
  19.4 11.8 %collective-permute-start.4 = (bf16[4,16,2048]{2,1,0:T(8,128)(2,1)S(1)}, bf16[4,16,2048]{2,1,0:T(8,128)(2,1)S(1)}, u32[]{:S(2)}, u32[]{:S(2)}) collective-permute-start(bf16[4,16,2048]{2,1,0:T(8,128)(2,1)S(1)} %shard_map.111.refs_1_), channel_id=1, source_target_pairs={{0,6},{1,7},{2,4},{3,5},{4,2},{5,3},{6,0},{7,1},{8,14},{9,15},{10,... | collective-permute-start | bytes 786440 | tf_op jit(solution)/shard_map/ppermute | solution.py:95
  19.9 17.2 %collective-permute-start.5 = (bf16[4,16,2048]{2,1,0:T(8,128)(2,1)S(1)}, bf16[4,16,2048]{2,1,0:T(8,128)(2,1)S(1)}, u32[]{:S(2)}, u32[]{:S(2)}) collective-permute-start(bf16[4,16,2048]{2,1,0:T(8,128)(2,1)S(1)} %shard_map.111.refs_1_), channel_id=1, source_target_pairs={{0,1},{1,0},{2,3},{3,2},{4,5},{5,4},{6,7},{7,6},{8,9},{9,8},{10,11... | collective-permute-start | bytes 786440 | tf_op jit(solution)/shard_map/ppermute | solution.py:95
  21.7 13.8 %collective-permute-start.10 = (bf16[2,16,4096]{2,1,0:T(8,128)(2,1)S(1)}, bf16[2,16,4096]{2,1,0:T(8,128)(2,1)S(1)}, u32[]{:S(2)}, u32[]{:S(2)}) collective-permute-start(bf16[2,16,4096]{2,1,0:T(8,128)(2,1)S(1)} %get-tuple-element.37.refs_0_), channel_id=1, source_target_pairs={{0,16},{1,17},{2,18},{3,19},{4,20},{5,21},{6,22},{7,23},{8,24},{9,... | collective-permute-start | bytes 786440 | tf_op jit(solution)/shard_map/ppermute | solution.py:95
  25.6 13.1 %collective-permute-start.6 = (bf16[4,16,2048]{2,1,0:T(8,128)(2,1)S(1)}, bf16[4,16,2048]{2,1,0:T(8,128)(2,1)S(1)}, u32[]{:S(2)}, u32[]{:S(2)}) collective-permute-start(bf16[4,16,2048]{2,1,0:T(8,128)(2,1)S(1)} %collective-permute-done.2.refs_2_), channel_id=1, source_target_pairs={{0,1},{1,0},{2,3},{3,2},{4,5},{5,4},{6,7},{7,6},{8,9},{9,8},{10,11... | collective-permute-start | bytes 786440 | tf_op jit(solution)/shard_map/ppermute | solution.py:95
  31.2 7.9 %collective-permute-start.7 = (bf16[4,16,2048]{2,1,0:T(8,128)(2,1)S(1)}, bf16[4,16,2048]{2,1,0:T(8,128)(2,1)S(1)}, u32[]{:S(2)}, u32[]{:S(2)}) collective-permute-start(bf16[4,16,2048]{2,1,0:T(8,128)(2,1)S(1)} %collective-permute-done.3.refs_3_), channel_id=1, source_target_pairs={{0,1},{1,0},{2,3},{3,2},{4,5},{5,4},{6,7},{7,6},{8,9},{9,8},{10,11... | collective-permute-start | bytes 786440 | tf_op jit(solution)/shard_map/ppermute | solution.py:95
  31.2 7.9 %collective-permute-start.8 = (bf16[4,16,2048]{2,1,0:T(8,128)(2,1)S(1)}, bf16[4,16,2048]{2,1,0:T(8,128)(2,1)S(1)}, u32[]{:S(2)}, u32[]{:S(2)}) collective-permute-start(bf16[4,16,2048]{2,1,0:T(8,128)(2,1)S(1)} %collective-permute-done.4.refs_4_), channel_id=1, source_target_pairs={{0,1},{1,0},{2,3},{3,2},{4,5},{5,4},{6,7},{7,6},{8,9},{9,8},{10,11... | collective-permute-start | bytes 786440 | tf_op jit(solution)/shard_map/ppermute | solution.py:95
  35.5 23.8 %collective-permute-start.11 = (bf16[4,16,4096]{2,1,0:T(8,128)(2,1)S(1)}, bf16[4,16,4096]{2,1,0:T(8,128)(2,1)S(1)}, u32[]{:S(2)}, u32[]{:S(2)}) collective-permute-start(bf16[4,16,4096]{2,1,0:T(8,128)(2,1)S(1)} %shard_map.114.refs_12_.refs_1_), channel_id=1, source_target_pairs={{0,2},{1,3},{2,0},{3,1},{4,6},{5,7},{6,4},{7,5},{8,10},{9,11},{10,... | collective-permute-start | bytes 1572872 | tf_op jit(solution)/shard_map/ppermute | solution.py:95
  37.1 24.8 %collective-permute-start.12 = (bf16[4,16,4096]{2,1,0:T(8,128)(2,1)S(1)}, bf16[4,16,4096]{2,1,0:T(8,128)(2,1)S(1)}, u32[]{:S(2)}, u32[]{:S(2)}) collective-permute-start(bf16[4,16,4096]{2,1,0:T(8,128)(2,1)S(1)} %shard_map.114.refs_12_.refs_1_), channel_id=1, source_target_pairs={{0,4},{1,5},{2,6},{3,7},{4,0},{5,1},{6,2},{7,3},{8,12},{9,13},{10,... | collective-permute-start | bytes 1572872 | tf_op jit(solution)/shard_map/ppermute | solution.py:95
  38.6 23.3 %collective-permute-start.13 = (bf16[4,16,4096]{2,1,0:T(8,128)(2,1)S(1)}, bf16[4,16,4096]{2,1,0:T(8,128)(2,1)S(1)}, u32[]{:S(2)}, u32[]{:S(2)}) collective-permute-start(bf16[4,16,4096]{2,1,0:T(8,128)(2,1)S(1)} %shard_map.114.refs_12_.refs_1_), channel_id=1, source_target_pairs={{0,6},{1,7},{2,4},{3,5},{4,2},{5,3},{6,0},{7,1},{8,14},{9,15},{10,... | collective-permute-start | bytes 1572872 | tf_op jit(solution)/shard_map/ppermute | solution.py:95
  39.1 23.3 %collective-permute-start.14 = (bf16[4,16,4096]{2,1,0:T(8,128)(2,1)S(1)}, bf16[4,16,4096]{2,1,0:T(8,128)(2,1)S(1)}, u32[]{:S(2)}, u32[]{:S(2)}) collective-permute-start(bf16[4,16,4096]{2,1,0:T(8,128)(2,1)S(1)} %shard_map.114.refs_12_.refs_1_), channel_id=1, source_target_pairs={{0,1},{1,0},{2,3},{3,2},{4,5},{5,4},{6,7},{7,6},{8,9},{9,8},{10,11... | collective-permute-start | bytes 1572872 | tf_op jit(solution)/shard_map/ppermute | solution.py:95
  39.1 20.2 %collective-permute-start.15 = (bf16[2,16,6144]{2,1,0:T(8,128)(2,1)S(1)}, bf16[2,16,6144]{2,1,0:T(8,128)(2,1)S(1)}, u32[]{:S(2)}, u32[]{:S(2)}) collective-permute-start(bf16[2,16,6144]{2,1,0:T(8,128)(2,1)S(1)} %get-tuple-element.39.refs_0_), channel_id=1, source_target_pairs={{0,16},{1,17},{2,18},{3,19},{4,20},{5,21},{6,22},{7,23},{8,24},{9,... | collective-permute-start | bytes 1179656 | tf_op jit(solution)/shard_map/ppermute | solution.py:95
  59.3 3.1 %collective-permute-start.16 = (bf16[4,16,4096]{2,1,0:T(8,128)(2,1)S(1)}, bf16[4,16,4096]{2,1,0:T(8,128)(2,1)S(1)}, u32[]{:S(2)}, u32[]{:S(2)}) collective-permute-start(bf16[4,16,4096]{2,1,0:T(8,128)(2,1)S(1)} %collective-permute-done.11.refs_2_), channel_id=1, source_target_pairs={{0,1},{1,0},{2,3},{3,2},{4,5},{5,4},{6,7},{7,6},{8,9},{9,8},{10,11... | collective-permute-start | bytes 1572872 | tf_op jit(solution)/shard_map/ppermute | solution.py:95
  61.9 1.9 %collective-permute-start.17 = (bf16[4,16,4096]{2,1,0:T(8,128)(2,1)S(1)}, bf16[4,16,4096]{2,1,0:T(8,128)(2,1)S(1)}, u32[]{:S(2)}, u32[]{:S(2)}) collective-permute-start(bf16[4,16,4096]{2,1,0:T(8,128)(2,1)S(1)} %collective-permute-done.12.refs_3_), channel_id=1, source_target_pairs={{0,1},{1,0},{2,3},{3,2},{4,5},{5,4},{6,7},{7,6},{8,9},{9,8},{10,11... | collective-permute-start | bytes 1572872 | tf_op jit(solution)/shard_map/ppermute | solution.py:95
  61.9 2.7 %collective-permute-start.18 = (bf16[4,16,4096]{2,1,0:T(8,128)(2,1)S(1)}, bf16[4,16,4096]{2,1,0:T(8,128)(2,1)S(1)}, u32[]{:S(2)}, u32[]{:S(2)}) collective-permute-start(bf16[4,16,4096]{2,1,0:T(8,128)(2,1)S(1)} %collective-permute-done.13.refs_4_), channel_id=1, source_target_pairs={{0,1},{1,0},{2,3},{3,2},{4,5},{5,4},{6,7},{7,6},{8,9},{9,8},{10,11... | collective-permute-start | bytes 1572872 | tf_op jit(solution)/shard_map/ppermute | solution.py:95
  64.6 9.2 %collective-permute-start.19 = (bf16[4,16,2048]{2,1,0:T(8,128)(2,1)S(1)}, bf16[4,16,2048]{2,1,0:T(8,128)(2,1)S(1)}, u32[]{:S(2)}, u32[]{:S(2)}) collective-permute-start(bf16[4,16,2048]{2,1,0:T(8,128)(2,1)S(1)} %get-tuple-element.43.refs_10_.refs_0_), channel_id=1, source_target_pairs={{0,2},{1,3},{2,0},{3,1},{4,6},{5,7},{6,4},{7,5},{8,10},{9,11},{10,... | collective-permute-start | bytes 786440 | tf_op jit(solution)/shard_map/ppermute | solution.py:95
  65.2 12.8 %collective-permute-start.20 = (bf16[4,16,2048]{2,1,0:T(8,128)(2,1)S(1)}, bf16[4,16,2048]{2,1,0:T(8,128)(2,1)S(1)}, u32[]{:S(2)}, u32[]{:S(2)}) collective-permute-start(bf16[4,16,2048]{2,1,0:T(8,128)(2,1)S(1)} %get-tuple-element.43.refs_10_.refs_0_), channel_id=1, source_target_pairs={{0,4},{1,5},{2,6},{3,7},{4,0},{5,1},{6,2},{7,3},{8,12},{9,13},{10,... | collective-permute-start | bytes 786440 | tf_op jit(solution)/shard_map/ppermute | solution.py:95
  66.7 12.9 %collective-permute-start.21 = (bf16[4,16,2048]{2,1,0:T(8,128)(2,1)S(1)}, bf16[4,16,2048]{2,1,0:T(8,128)(2,1)S(1)}, u32[]{:S(2)}, u32[]{:S(2)}) collective-permute-start(bf16[4,16,2048]{2,1,0:T(8,128)(2,1)S(1)} %get-tuple-element.43.refs_10_.refs_0_), channel_id=1, source_target_pairs={{0,6},{1,7},{2,4},{3,5},{4,2},{5,3},{6,0},{7,1},{8,14},{9,15},{10,... | collective-permute-start | bytes 786440 | tf_op jit(solution)/shard_map/ppermute | solution.py:95
  79.7 16.4 %collective-permute-start.25 = (bf16[16,16,2048]{2,1,0:T(8,128)(2,1)S(1)}, bf16[16,16,2048]{2,1,0:T(8,128)(2,1)S(1)}, u32[]{:S(2)}, u32[]{:S(2)}) collective-permute-start(bf16[16,16,2048]{2,1,0:T(8,128)(2,1)S(1)} %shard_map.118.refs_10_.refs_7_), channel_id=1, source_target_pairs={{0,1},{1,0},{2,3},{3,2},{4,5},{5,4},{6,7},{7,6},{8,9},{9,8},{10,11... | collective-permute-start | bytes 3145736 | tf_op jit(solution)/shard_map/ppermute | solution.py:95
  79.8 16.3 %copy-start.7 = (f32[144,256]{1,0:T(8,128)S(1)}, f32[144,256]{1,0:T(8,128)}, u32[]{:S(2)}) copy-start(f32[144,256]{1,0:T(8,128)} %constant.10.clone.refs_12_) | copy-start | bytes 442372
  79.8 13.1 %collective-permute-start.22 = (bf16[4,2,36,512]{3,2,1,0:T(8,128)(2,1)S(1)}, bf16[4,2,36,512]{3,2,1,0:T(8,128)(2,1)S(1)}, u32[]{:S(2)}, u32[]{:S(2)}) collective-permute-start(bf16[4,2,36,512]{3,2,1,0:T(8,128)(2,1)S(1)} %get-tuple-element.44.refs_0_), channel_id=1, source_target_pairs={{2,0},{3,1},{4,2},{5,3},{6,4},{7,5},{8,6},{9,7},{10,8},{11,9},{12,... | collective-permute-start | bytes 884744 | tf_op jit(solution)/shard_map/ppermute | solution.py:379
  87.9 7.4 %collective-permute-start.23 = (bf16[4,36,512]{2,1,0:T(8,128)(2,1)S(1)}, bf16[4,36,512]{2,1,0:T(8,128)(2,1)S(1)}, u32[]{:S(2)}, u32[]{:S(2)}) collective-permute-start(bf16[4,36,512]{2,1,0:T(8,128)(2,1)S(1)} %pad_maximum_fusion), channel_id=1, source_target_pairs={{1,0},{0,1},{3,2},{2,3},{5,4},{4,5},{7,6},{6,7},{9,8},{8,9},{11,10... | collective-permute-start | bytes 442376 | tf_op jit(solution)/shard_map/ppermute | solution.py:379
  88.2 4.5 %collective-permute-start.24 = (bf16[2,36,512]{2,1,0:T(8,128)(2,1)S(1)}, bf16[2,36,512]{2,1,0:T(8,128)(2,1)S(1)}, u32[]{:S(2)}, u32[]{:S(2)}) collective-permute-start(bf16[2,36,512]{2,1,0:T(8,128)(2,1)S(1)} %get-tuple-element.46), channel_id=1, source_target_pairs={{3,0},{2,1},{5,2},{4,3},{7,4},{6,5},{9,6},{8,7},{11,8},{10,9},{13,... | collective-permute-start | bytes 221192 | tf_op jit(solution)/shard_map/ppermute | solution.py:379
  88.6 30.5 %collective-permute-start.29 = (bf16[4,16,4096]{2,1,0:T(8,128)(2,1)S(1)}, bf16[4,16,4096]{2,1,0:T(8,128)(2,1)S(1)}, u32[]{:S(2)}, u32[]{:S(2)}) collective-permute-start(bf16[4,16,4096]{2,1,0:T(8,128)(2,1)S(1)} %get-tuple-element.54.refs_1_), channel_id=1, source_target_pairs={{0,1},{1,0},{2,3},{3,2},{4,5},{5,4},{6,7},{7,6},{8,9},{9,8},{10,11... | collective-permute-start | bytes 1572872 | tf_op jit(solution)/shard_map/ppermute | solution.py:95
  92.6 16.8 %collective-permute-start.26 = (bf16[4,16,4096]{2,1,0:T(8,128)(2,1)S(1)}, bf16[4,16,4096]{2,1,0:T(8,128)(2,1)S(1)}, u32[]{:S(2)}, u32[]{:S(2)}) collective-permute-start(bf16[4,16,4096]{2,1,0:T(8,128)(2,1)S(1)} %get-tuple-element.54.refs_1_), channel_id=1, source_target_pairs={{0,2},{1,3},{2,0},{3,1},{4,6},{5,7},{6,4},{7,5},{8,10},{9,11},{10,... | collective-permute-start | bytes 1572872 | tf_op jit(solution)/shard_map/ppermute | solution.py:95
  92.9 25.7 %collective-permute-start.27 = (bf16[4,16,4096]{2,1,0:T(8,128)(2,1)S(1)}, bf16[4,16,4096]{2,1,0:T(8,128)(2,1)S(1)}, u32[]{:S(2)}, u32[]{:S(2)}) collective-permute-start(bf16[4,16,4096]{2,1,0:T(8,128)(2,1)S(1)} %get-tuple-element.54.refs_1_), channel_id=1, source_target_pairs={{0,4},{1,5},{2,6},{3,7},{4,0},{5,1},{6,2},{7,3},{8,12},{9,13},{10,... | collective-permute-start | bytes 1572872 | tf_op jit(solution)/shard_map/ppermute | solution.py:95
  95.3 23.3 %collective-permute-start.28 = (bf16[4,16,4096]{2,1,0:T(8,128)(2,1)S(1)}, bf16[4,16,4096]{2,1,0:T(8,128)(2,1)S(1)}, u32[]{:S(2)}, u32[]{:S(2)}) collective-permute-start(bf16[4,16,4096]{2,1,0:T(8,128)(2,1)S(1)} %get-tuple-element.54.refs_1_), channel_id=1, source_target_pairs={{0,6},{1,7},{2,4},{3,5},{4,2},{5,3},{6,0},{7,1},{8,14},{9,15},{10,... | collective-permute-start | bytes 1572872 | tf_op jit(solution)/shard_map/ppermute | solution.py:95
  109.4 9.8 %collective-permute-start.30 = (bf16[4,16,4096]{2,1,0:T(8,128)(2,1)S(1)}, bf16[4,16,4096]{2,1,0:T(8,128)(2,1)S(1)}, u32[]{:S(2)}, u32[]{:S(2)}) collective-permute-start(bf16[4,16,4096]{2,1,0:T(8,128)(2,1)S(1)} %collective-permute-done.26.refs_2_), channel_id=1, source_target_pairs={{0,1},{1,0},{2,3},{3,2},{4,5},{5,4},{6,7},{7,6},{8,9},{9,8},{10,11... | collective-permute-start | bytes 1572872 | tf_op jit(solution)/shard_map/ppermute | solution.py:95
  118.6 1.9 %collective-permute-start.31 = (bf16[4,16,4096]{2,1,0:T(8,128)(2,1)S(1)}, bf16[4,16,4096]{2,1,0:T(8,128)(2,1)S(1)}, u32[]{:S(2)}, u32[]{:S(2)}) collective-permute-start(bf16[4,16,4096]{2,1,0:T(8,128)(2,1)S(1)} %collective-permute-done.27.refs_3_), channel_id=1, source_target_pairs={{0,1},{1,0},{2,3},{3,2},{4,5},{5,4},{6,7},{7,6},{8,9},{9,8},{10,11... | collective-permute-start | bytes 1572872 | tf_op jit(solution)/shard_map/ppermute | solution.py:95
  118.6 2.7 %collective-permute-start.32 = (bf16[4,16,4096]{2,1,0:T(8,128)(2,1)S(1)}, bf16[4,16,4096]{2,1,0:T(8,128)(2,1)S(1)}, u32[]{:S(2)}, u32[]{:S(2)}) collective-permute-start(bf16[4,16,4096]{2,1,0:T(8,128)(2,1)S(1)} %collective-permute-done.28.refs_4_), channel_id=1, source_target_pairs={{0,1},{1,0},{2,3},{3,2},{4,5},{5,4},{6,7},{7,6},{8,9},{9,8},{10,11... | collective-permute-start | bytes 1572872 | tf_op jit(solution)/shard_map/ppermute | solution.py:95
  126.1 14.3 %collective-permute-start.35 = (bf16[4,2,36,512]{3,2,1,0:T(8,128)(2,1)S(1)}, bf16[4,2,36,512]{3,2,1,0:T(8,128)(2,1)S(1)}, u32[]{:S(2)}, u32[]{:S(2)}) collective-permute-start(bf16[4,2,36,512]{3,2,1,0:T(8,128)(2,1)S(1)} %get-tuple-element.63), channel_id=1, source_target_pairs={{30,0},{31,1},{0,2},{1,3},{2,4},{3,5},{4,6},{5,7},{6,8},{7,9},{8,1... | collective-permute-start | bytes 884744 | tf_op jit(solution)/shard_map/ppermute | solution.py:379
  131.7 8.7 %collective-permute-start.33 = (bf16[4,36,512]{2,1,0:T(8,128)(2,1)S(1)}, bf16[4,36,512]{2,1,0:T(8,128)(2,1)S(1)}, u32[]{:S(2)}, u32[]{:S(2)}) collective-permute-start(bf16[4,36,512]{2,1,0:T(8,128)(2,1)S(1)} %pad_maximum_fusion.1), channel_id=1, source_target_pairs={{1,0},{0,1},{3,2},{2,3},{5,4},{4,5},{7,6},{6,7},{9,8},{8,9},{11,10... | collective-permute-start | bytes 442376 | tf_op jit(solution)/shard_map/ppermute | solution.py:379
  131.8 8.6 %collective-permute-start.34 = (bf16[2,36,512]{2,1,0:T(8,128)(2,1)S(1)}, bf16[2,36,512]{2,1,0:T(8,128)(2,1)S(1)}, u32[]{:S(2)}, u32[]{:S(2)}) collective-permute-start(bf16[2,36,512]{2,1,0:T(8,128)(2,1)S(1)} %get-tuple-element.58.refs_10_), channel_id=1, source_target_pairs={{31,0},{30,1},{1,2},{0,3},{3,4},{2,5},{5,6},{4,7},{7,8},{6,9},{9,1... | collective-permute-start | bytes 221192 | tf_op jit(solution)/shard_map/ppermute | solution.py:379

commit v8 on v7

--- a/solution.py
+++ b/solution.py
@@ -115,12 +115,16 @@
     return lax.optimization_barrier((array, after))[0]
 
 
-def to_neighbours(column):
-    return [
-        send(column, lambda z, y, x, c: (z, y, 1 - x, c)),
-        send(column, lambda z, y, x, c: (z, 1 - y, x, c)),
-        send(column, lambda z, y, x, c: (z, 1 - y, 1 - x, c)),
-    ]
+def beside(z, y, x, c):
+    return (z, y, 1 - x, c) if c == 0 else (z, 1 - y, x, c)
+
+
+def across(z, y, x, c):
+    return (z, 1 - y, x, c) if c == 0 else (z, y, 1 - x, c)
+
+
+def corner(z, y, x, c):
+    return z, 1 - y, 1 - x, c
 
 
 def whole_pieces(column, received, after=None):
@@ -144,10 +148,16 @@
         copy.start()
     lon, lat = lax.axis_index("lon"), lax.axis_index("lat")
     z, y, x = lon // 4, lon // 2 % 2, lon % 2
-    squares = (y * 2 + x, y * 2 + 1 - x, (1 - y) * 2 + x, (1 - y) * 2 + 1 - x)
+    by_x, by_y = y * 2 + 1 - x, (1 - y) * 2 + x
     joined = len(pieces) == 2
     for index, copy in enumerate(copies):
         core = lat if index < len(pieces) // 2 else 1 - lat
+        squares = (
+            y * 2 + x,
+            jnp.where(core == 0, by_x, by_y),
+            jnp.where(core == 0, by_y, by_x),
+            (1 - y) * 2 + 1 - x,
+        )
         copy.wait()
         for column in range(4) if joined else (index % 4,):
             for step in range(lon_size // 4):
@@ -394,13 +404,13 @@
     return arranged.reshape(c, -1, LEVELS, features)
 
 
-def back_in_place(sides, behind, below, corner):
+def back_in_place(sides, behind, above, high):
     features = behind.shape[-1]
     flat = lambda side: side.reshape(-1, QUARTER, features)[:-1]
     c, r = WLON // 2, WLAT // 2
     own = jnp.concatenate([strip(flat(side)) for side in sides], 0)
-    tops = jnp.concatenate([strip(low[None]) for low in below], 0)
-    first = jnp.concatenate([strip(corner[None]), strip(flat(behind))], 1)
+    tops = jnp.concatenate([strip(low[None]) for low in above], 0)
+    first = jnp.concatenate([strip(high[None]), strip(flat(behind))], 1)
     return jnp.concatenate([first, jnp.concatenate([tops, own], 1)], 0)
 
 
@@ -433,25 +443,29 @@
         )
         (pair,) = join([[own, across_z(own, 1)]], (), (windows,))
         column = along_z(pair)
-        pieces = whole_pieces(column, to_neighbours(column))
+        pieces = whole_pieces(column, [send(column, way) for way in (beside, across, corner)])
         feed_pair, last_pair = join(
             [[later_own, across_z(later_own, 1)]], widths=(feed_width, attend_width + feed_width)
         )
         feed_column = along_z(feed_pair)
-        feed_received = to_neighbours(feed_column)
+        received = [send(feed_column, way) for way in (beside, across)]
         last_pair = tied(last_pair, feed_column)
         last_other = across_z(last_pair, 2)
         middle = attention(0, [windows], pieces, (feed_column,))
-        feed_pieces = whole_pieces(feed_column, feed_received, (middle, last_other))
+        received.append(send(tied(received[0], (middle, last_other)), across))
+        feed_pieces = whole_pieces(feed_column, received, middle)
         column, last_column = join(
-            [[last_pair, last_other]], (), tuple(feed_pieces[4:]), (attend_width, feed_width)
-        )
-        received = to_neighbours(column)
+            [[last_pair, last_other]], (), (received[2],), (attend_width, feed_width)
+        )
+        received = [send(column, way) for way in (beside, across)]
         left_0, right_0, low_0 = forward(0, middle, 0, feed_pieces, low_edge, (column,))
-        (joined,) = join([[column] + [tied(part, low_0) for part in received]])
+        received.append(send(tied(received[0], low_0), across))
+        last_column = tied(last_column, (low_0, received[1]))
+        last_received = [send(last_column, way) for way in (beside, across, corner)]
+        ahead, ahead_low = shift_from(left_0, 1, 0), shift_from(low_0, 1, 1)
+        left_1, right_1, low_1 = forward(0, middle, 1, feed_pieces, low_edge, (low_0, received[1]))
+        (joined,) = join([[column] + [tied(part, (low_1, ahead, ahead_low)) for part in received]])
         pieces = [joined, send(joined, swap)]
-        last_received = to_neighbours(tied(last_column, joined))
-        left_1, right_1, low_1 = forward(0, middle, 1, feed_pieces, low_edge, (joined,))
     else:
         gathered = []
         for block in range(2):
@@ -462,23 +476,19 @@
         middle = attention(0, [windows], first_pieces)
         left_0, right_0, low_0 = forward(0, middle, 0, feed_pieces, low_edge)
         left_1, right_1, low_1 = forward(0, middle, 1, feed_pieces, low_edge)
-    ahead = shift_from(left_0, 1, 0)
-    low = jnp.concatenate([low_0, low_1], 0)
-    ahead_low = shift_from(low_0, 1, 1)
-    below = shift_from(low, 0, 1)
+        ahead, ahead_low = shift_from(left_0, 1, 0), shift_from(low_0, 1, 1)
+    below = shift_from(tied(jnp.concatenate([low_0, low_1], 0), ahead_low), 0, 1)
     sources = [left_0, right_0, left_1, right_1, ahead, below, ahead_low]
     middle = attention(1, sources, pieces)
     if relay:
         last_pieces = whole_pieces(last_column, last_received, middle)
     left_1, right_1, high_1 = forward(1, middle, 1, last_pieces, high_edge)
     behind = shift_from(right_1, -1, 0)
-    corner = shift_from(high_1, -1, -1)
+    behind_high = shift_from(high_1, -1, -1)
     left_0, right_0, high_0 = forward(1, middle, 0, last_pieces, high_edge, (high_1,))
-    above = shift_from(jnp.concatenate([high_0, high_1], 0), 0, -1)
-    sides, above, corner = tied(((left_0, right_0, left_1), above, corner), behind)
-    return back_in_place(
-        sides, behind, (above[0], above[1], above[2]), corner[1]
-    )
+    above = shift_from(tied(jnp.concatenate([high_0, high_1], 0), behind_high), 0, -1)
+    sides, above, behind_high = tied(((left_0, right_0, left_1), above, behind_high), behind)
+    return back_in_place(sides, behind, (above[0], above[1], above[2]), behind_high[1])
 
 
 def solution(mesh):

time: 145 us -> 143 us (0.986)
  waiting for transfers between devices: 58.2 us -> 56.7 us
    ppermute x30, waiting for transfers between devices: 48.4 us -> 44.7 us  [send(): return lax.ppermute(block, ('lon', 'lat'), pairs)]
    ppermute x6, waiting for transfers between devices: 9.8 us -> 12 us  [shift_from(): return lax.ppermute(block, ('lon', 'lat'), pairs)]
    ppermute x6, starting transfers between devices: 7.4 us -> 5.63 us  [shift_from(): return lax.ppermute(block, ('lon', 'lat'), pairs)]
  transfers between devices with their start and end apart: 36 -> 36, of which waited for: 17 -> 14; matrix products, arithmetic and copies ran while one was open for 2% -> 2% of each run, Pallas kernels for 28% -> 29%
where the time goes in v8:
time: 143 us; the launch traced here: 142 us
  waiting for transfers between devices  56.7 us (40%)
  Pallas kernels  46.2 us (32%)
  starting transfers between devices  30 us (21%)
  local copies, waits for them, and re-layouts  5.9 us (4%)
  other arithmetic  3.03 us (2%)
    ppermute x30, waiting for transfers between devices, send(): return lax.ppermute(block, ('lon', 'lat'), pairs)  44.7 us
    pallas_call x2, Pallas kernels, attend(): pl.pallas_call(functools.partial(attend_kernel, shifted, row_windows, len...  26.7 us
    ppermute x30, starting transfers between devices, send(): return lax.ppermute(block, ('lon', 'lat'), pairs)  24.4 us
    pallas_call x4, Pallas kernels, feed(): pl.pallas_call(functools.partial(feed_kernel, len(pieces), hidden_size, 5...  19.3 us
    ppermute x6, waiting for transfers between devices, shift_from(): return lax.ppermute(block, ('lon', 'lat'), pairs)  12 us
    ppermute x6, starting transfers between devices, shift_from(): return lax.ppermute(block, ('lon', 'lat'), pairs)  5.63 us
    concatenate x1, other arithmetic, back_in_place(): return jnp.concatenate([first, jnp.concatenate([tops, own], 1)], 0)  2.9 us
  transfers between devices with their start and end apart: 36, of which 14 were waited for; matrix products, arithmetic and copies ran while one was open for 2% of the time, Pallas kernels for 29%

profile of v8, /device:TPU:0, one launch (start us, length us, event | category | flops | bytes accessed | tf_op | source)
XLA Modules:
  0.0 142.3 jit_solution(6512082242222435603)
XLA Ops:
  0.0 0.9 copy-done.2
  0.9 0.8 copy-done.4
  1.8 3.0 %collective-permute-start = (bf16[1,16,2048]{2,1,0:T(8,128)(2,1)S(1)}, bf16[1,16,2048]{2,1,0:T(8,128)(2,1)S(1)}, u32[]{:S(2)}, u32[]{:S(2)}) collective-permute-start(bf16[1,16,2048]{2,1,0:T(8,128)(2,1)S(1)} %shard_map.109.refs_0_), channel_id=1, source_target_pairs={{0,8},{1,9},{2,10},{3,11},{4,12},{5,13},{6,14},{7,15},{8,0},{9,1},... | collective-permute-start | bytes 196616 | tf_op jit(solution)/shard_map/ppermute | solution.py:95
  4.8 2.1 %copy.23 = bf16[2,2,6,4,2,3,2,512]{7,6,5,2,4,1,3,0:T(2,128)(2,1)S(1)} copy(bf16[2,2,6,4,2,3,2,512]{7,6,5,4,3,2,1,0:T(2,128)(2,1)} %bitcast.32) | data formatting | bytes 2359296 | tf_op jit(solution)/shard_map/reshape | solution.py:395
  6.9 0.5 reshape.45.refs_2_.refs_0_
  7.4 0.0 copy-start
  7.5 0.0 copy-start.8
  7.5 2.7 %collective-permute-start.1 = (bf16[2,16,2048]{2,1,0:T(8,128)(2,1)S(1)}, bf16[2,16,2048]{2,1,0:T(8,128)(2,1)S(1)}, u32[]{:S(2)}, u32[]{:S(2)}) collective-permute-start(bf16[2,16,2048]{2,1,0:T(8,128)(2,1)S(1)} %shard_map.110.refs_0_), channel_id=1, source_target_pairs={{0,16},{1,17},{2,18},{3,19},{4,20},{5,21},{6,22},{7,23},{8,24},{9,... | collective-permute-start | bytes 393224 | tf_op jit(solution)/shard_map/ppermute | solution.py:95
  10.2 0.0 copy-start.6
  10.3 1.6 %collective-permute-start.9 = (bf16[1,16,10240]{2,1,0:T(8,128)(2,1)S(1)}, bf16[1,16,10240]{2,1,0:T(8,128)(2,1)S(1)}, u32[]{:S(2)}, u32[]{:S(2)}) collective-permute-start(bf16[1,16,10240]{2,1,0:T(8,128)(2,1)S(1)} %shard_map.112.refs_0_), channel_id=1, source_target_pairs={{0,8},{1,9},{2,10},{3,11},{4,12},{5,13},{6,14},{7,15},{8,0},{9,1},... | collective-permute-start | bytes 983048 | tf_op jit(solution)/shard_map/ppermute | solution.py:95
  11.9 4.4 %collective-permute-done.1.refs_1_ = bf16[2,16,2048]{2,1,0:T(8,128)(2,1)S(1)} collective-permute-done((bf16[2,16,2048]{2,1,0:T(8,128)(2,1)S(1)}, bf16[2,16,2048]{2,1,0:T(8,128)(2,1)S(1)}, u32[]{:S(2)}, u32[]{:S(2)}) %collective-permute-start.1) | collective-permute-done | bytes 131104 | tf_op jit(solution)/shard_map/ppermute | solution.py:95
  16.3 1.6 %collective-permute-start.2 = (bf16[4,16,2048]{2,1,0:T(8,128)(2,1)S(1)}, bf16[4,16,2048]{2,1,0:T(8,128)(2,1)S(1)}, u32[]{:S(2)}, u32[]{:S(2)}) collective-permute-start(bf16[4,16,2048]{2,1,0:T(8,128)(2,1)S(1)} %shard_map.111.refs_1_), channel_id=1, source_target_pairs={{0,2},{1,5},{2,0},{3,7},{4,6},{5,1},{6,4},{7,3},{8,10},{9,13},{10,... | collective-permute-start | bytes 786440 | tf_op jit(solution)/shard_map/ppermute | solution.py:95
  17.8 1.5 %collective-permute-start.3 = (bf16[4,16,2048]{2,1,0:T(8,128)(2,1)S(1)}, bf16[4,16,2048]{2,1,0:T(8,128)(2,1)S(1)}, u32[]{:S(2)}, u32[]{:S(2)}) collective-permute-start(bf16[4,16,2048]{2,1,0:T(8,128)(2,1)S(1)} %shard_map.111.refs_1_), channel_id=1, source_target_pairs={{0,4},{1,3},{2,6},{3,1},{4,0},{5,7},{6,2},{7,5},{8,12},{9,11},{10,... | collective-permute-start | bytes 786440 | tf_op jit(solution)/shard_map/ppermute | solution.py:95
  19.4 0.5 collective-permute-start.4
  19.8 0.1 multiply_reduce_fusion
  19.9 0.1 collective-permute-start.5
  20.0 1.7 %collective-permute-done.9.refs_1_ = bf16[1,16,10240]{2,1,0:T(8,128)(2,1)S(1)} collective-permute-done((bf16[1,16,10240]{2,1,0:T(8,128)(2,1)S(1)}, bf16[1,16,10240]{2,1,0:T(8,128)(2,1)S(1)}, u32[]{:S(2)}, u32[]{:S(2)}) %collective-permute-start.9) | collective-permute-done | bytes 327712 | tf_op jit(solution)/shard_map/ppermute | solution.py:95
  21.7 0.1 collective-permute-start.10
  21.9 3.6 %collective-permute-done.2.refs_2_ = bf16[4,16,2048]{2,1,0:T(8,128)(2,1)S(1)} collective-permute-done((bf16[4,16,2048]{2,1,0:T(8,128)(2,1)S(1)}, bf16[4,16,2048]{2,1,0:T(8,128)(2,1)S(1)}, u32[]{:S(2)}, u32[]{:S(2)}) %collective-permute-start.2) | collective-permute-done | bytes 262176 | tf_op jit(solution)/shard_map/ppermute | solution.py:95
  25.5 0.5 collective-permute-start.7
  26.0 5.2 %collective-permute-done.4.refs_4_ = bf16[4,16,2048]{2,1,0:T(8,128)(2,1)S(1)} collective-permute-done((bf16[4,16,2048]{2,1,0:T(8,128)(2,1)S(1)}, bf16[4,16,2048]{2,1,0:T(8,128)(2,1)S(1)}, u32[]{:S(2)}, u32[]{:S(2)}) %collective-permute-start.4) | collective-permute-done | bytes 262176 | tf_op jit(solution)/shard_map/ppermute | solution.py:95
  31.2 4.3 %collective-permute-done.10.refs_1_ = bf16[2,16,4096]{2,1,0:T(8,128)(2,1)S(1)} collective-permute-done((bf16[2,16,4096]{2,1,0:T(8,128)(2,1)S(1)}, bf16[2,16,4096]{2,1,0:T(8,128)(2,1)S(1)}, u32[]{:S(2)}, u32[]{:S(2)}) %collective-permute-start.10) | collective-permute-done | bytes 262176 | tf_op jit(solution)/shard_map/ppermute | solution.py:95
  35.5 1.6 %collective-permute-start.11 = (bf16[4,16,4096]{2,1,0:T(8,128)(2,1)S(1)}, bf16[4,16,4096]{2,1,0:T(8,128)(2,1)S(1)}, u32[]{:S(2)}, u32[]{:S(2)}) collective-permute-start(bf16[4,16,4096]{2,1,0:T(8,128)(2,1)S(1)} %shard_map.114.refs_12_.refs_1_), channel_id=1, source_target_pairs={{0,2},{1,5},{2,0},{3,7},{4,6},{5,1},{6,4},{7,3},{8,10},{9,13},{10,... | collective-permute-start | bytes 1572872 | tf_op jit(solution)/shard_map/ppermute | solution.py:95
  37.1 1.5 %collective-permute-start.12 = (bf16[4,16,4096]{2,1,0:T(8,128)(2,1)S(1)}, bf16[4,16,4096]{2,1,0:T(8,128)(2,1)S(1)}, u32[]{:S(2)}, u32[]{:S(2)}) collective-permute-start(bf16[4,16,4096]{2,1,0:T(8,128)(2,1)S(1)} %shard_map.114.refs_12_.refs_1_), channel_id=1, source_target_pairs={{0,4},{1,3},{2,6},{3,1},{4,0},{5,7},{6,2},{7,5},{8,12},{9,11},{10,... | collective-permute-start | bytes 1572872 | tf_op jit(solution)/shard_map/ppermute | solution.py:95
  38.7 13.4 %shard_map.115.refs_0_ = bf16[8,144,512]{2,1,0:T(8,128)(2,1)S(1)} custom-call(bf16[8,144,512]{2,1,0:T(8,128)(2,1)S(1)} %reshape.45.refs_2_.refs_0_, bf16[4,16,2048]{2,1,0:T(8,128)(2,1)S(1)} %shard_map.111.refs_1_, bf16[4,16,2048]{2,1,0:T(8,128)(2,1)S(1)} %collective-permute-done.2.refs_2_, bf16[4,16,2048]{2,1,0:T(8,128)(2,1)S(1)} %collective-permute-done.3.refs_3_, ...), custom_call_target="tpu_custom_call" | custom-call | flops 16000000000 | bytes 6000000 | tf_op jit(solution)/shard_map/pallas_call | solution.py:304
  52.1 5.8 %collective-permute-done.13.refs_1_ = bf16[2,16,6144]{2,1,0:T(8,128)(2,1)S(1)} collective-permute-done((bf16[2,16,6144]{2,1,0:T(8,128)(2,1)S(1)}, bf16[2,16,6144]{2,1,0:T(8,128)(2,1)S(1)}, u32[]{:S(2)}, u32[]{:S(2)}) %collective-permute-start.13) | collective-permute-done | bytes 393248 | tf_op jit(solution)/shard_map/ppermute | solution.py:95
  57.8 0.5 collective-permute-start.14
  58.3 0.5 collective-permute-start.16
  58.9 8.2 %collective-permute-done.14.refs_2_.refs_4_ = bf16[4,16,4096]{2,1,0:T(8,128)(2,1)S(1)} collective-permute-done((bf16[4,16,4096]{2,1,0:T(8,128)(2,1)S(1)}, bf16[4,16,4096]{2,1,0:T(8,128)(2,1)S(1)}, u32[]{:S(2)}, u32[]{:S(2)}) %collective-permute-start.14) | collective-permute-done | bytes 524320 | tf_op jit(solution)/shard_map/ppermute | solution.py:95
  67.0 0.1 shard_map.116
  67.1 0.6 collective-permute-start.19
  67.6 0.5 collective-permute-start.23
  68.2 0.7 collective-permute-done.18.refs_8_
  68.9 4.8 %shard_map.117 = (bf16[4,2,36,512]{3,2,1,0:T(8,128)(2,1)S(1)}, bf16[4,2,36,512]{3,2,1,0:T(8,128)(2,1)S(1)}, bf16[2,36,512]{2,1,0:T(8,128)(2,1)S(1)}) custom-call(bf16[8,144,512]{2,1,0:T(8,128)(2,1)S(1)} %shard_map.115.refs_0_, bf16[4,16,4096]{2,1,0:T(8,128)(2,1)S(1)} %shard_map.114.refs_12_.refs_1_, ...), custom_call_target="tpu_custom_call" | custom-call | flops 4831838208 | bytes 8000000 | tf_op jit(solution)/shard_map/pallas_call | solution.py:362
  73.7 3.0 %collective-permute-start.20 = (bf16[4,2,36,512]{3,2,1,0:T(8,128)(2,1)S(1)}, bf16[4,2,36,512]{3,2,1,0:T(8,128)(2,1)S(1)}, u32[]{:S(2)}, u32[]{:S(2)}) collective-permute-start(bf16[4,2,36,512]{3,2,1,0:T(8,128)(2,1)S(1)} %get-tuple-element.49.refs_0_), channel_id=1, source_target_pairs={{2,0},{3,1},{4,2},{5,3},{6,4},{7,5},{8,6},{9,7},{10,8},{11,9},{12,... | collective-permute-start | bytes 884744 | tf_op jit(solution)/shard_map/ppermute | solution.py:389
  76.8 4.9 %shard_map.118 = (bf16[4,2,36,512]{3,2,1,0:T(8,128)(2,1)S(1)}, bf16[4,2,36,512]{3,2,1,0:T(8,128)(2,1)S(1)}, bf16[2,36,512]{2,1,0:T(8,128)(2,1)S(1)}) custom-call(bf16[8,144,512]{2,1,0:T(8,128)(2,1)S(1)} %shard_map.115.refs_0_, bf16[4,16,4096]{2,1,0:T(8,128)(2,1)S(1)} %shard_map.114.refs_12_.refs_1_, ...), custom_call_target="tpu_custom_call" | custom-call | flops 4831838208 | bytes 8000000 | tf_op jit(solution)/shard_map/pallas_call | solution.py:362
  81.7 3.9 %collective-permute-done.21.refs_6_ = bf16[2,36,512]{2,1,0:T(8,128)(2,1)S(1)} collective-permute-done((bf16[2,36,512]{2,1,0:T(8,128)(2,1)S(1)}, bf16[2,36,512]{2,1,0:T(8,128)(2,1)S(1)}, u32[]{:S(2)}, u32[]{:S(2)}) %collective-permute-start.21) | collective-permute-done | bytes 73760 | tf_op jit(solution)/shard_map/ppermute | solution.py:389
  85.6 0.1 shard_map.119.refs_7_
  85.7 2.7 %collective-permute-start.25 = (bf16[16,16,2048]{2,1,0:T(8,128)(2,1)S(1)}, bf16[16,16,2048]{2,1,0:T(8,128)(2,1)S(1)}, u32[]{:S(2)}, u32[]{:S(2)}) collective-permute-start(bf16[16,16,2048]{2,1,0:T(8,128)(2,1)S(1)} %shard_map.119.refs_7_), channel_id=1, source_target_pairs={{0,1},{1,0},{2,3},{3,2},{4,5},{5,4},{6,7},{7,6},{8,9},{9,8},{10,11... | collective-permute-start | bytes 3145736 | tf_op jit(solution)/shard_map/ppermute | solution.py:95
  88.4 0.1 collective-permute-start.22
  88.5 2.2 %collective-permute-start.26 = (bf16[4,16,4096]{2,1,0:T(8,128)(2,1)S(1)}, bf16[4,16,4096]{2,1,0:T(8,128)(2,1)S(1)}, u32[]{:S(2)}, u32[]{:S(2)}) collective-permute-start(bf16[4,16,4096]{2,1,0:T(8,128)(2,1)S(1)} %get-tuple-element.61.refs_1_), channel_id=1, source_target_pairs={{0,2},{1,5},{2,0},{3,7},{4,6},{5,1},{6,4},{7,3},{8,10},{9,13},{10,... | collective-permute-start | bytes 1572872 | tf_op jit(solution)/shard_map/ppermute | solution.py:95
  90.7 2.1 %collective-permute-start.27 = (bf16[4,16,4096]{2,1,0:T(8,128)(2,1)S(1)}, bf16[4,16,4096]{2,1,0:T(8,128)(2,1)S(1)}, u32[]{:S(2)}, u32[]{:S(2)}) collective-permute-start(bf16[4,16,4096]{2,1,0:T(8,128)(2,1)S(1)} %get-tuple-element.61.refs_1_), channel_id=1, source_target_pairs={{0,4},{1,3},{2,6},{3,1},{4,0},{5,7},{6,2},{7,5},{8,12},{9,11},{10,... | collective-permute-start | bytes 1572872 | tf_op jit(solution)/shard_map/ppermute | solution.py:95
  92.8 13.3 %shard_map.120.refs_0_ = bf16[8,144,512]{2,1,0:T(8,128)(2,1)S(1)} custom-call(bf16[4,2,36,512]{3,2,1,0:T(8,128)(2,1)S(1)} %get-tuple-element.49.refs_0_, bf16[4,2,36,512]{3,2,1,0:T(8,128)(2,1)S(1)} %get-tuple-element.50.refs_1_, bf16[4,2,36,512]{3,2,1,0:T(8,128)(2,1)S(1)} %get-tuple-element.52.refs_2_, ...), custom_call_target="tpu_custom_call" | custom-call | flops 16000000000 | bytes 6000000 | tf_op jit(solution)/shard_map/pallas_call | solution.py:304
  106.1 0.5 collective-permute-start.30
  106.6 0.1 collective-permute-start.31
  106.7 9.0 %collective-permute-done.28.refs_4_ = bf16[4,16,4096]{2,1,0:T(8,128)(2,1)S(1)} collective-permute-done((bf16[4,16,4096]{2,1,0:T(8,128)(2,1)S(1)}, bf16[4,16,4096]{2,1,0:T(8,128)(2,1)S(1)}, u32[]{:S(2)}, u32[]{:S(2)}) %collective-permute-start.28) | collective-permute-done | bytes 524320 | tf_op jit(solution)/shard_map/ppermute | solution.py:95
  115.7 1.9 %collective-permute-done.32.refs_8_ = bf16[4,16,4096]{2,1,0:T(8,128)(2,1)S(1)} collective-permute-done((bf16[4,16,4096]{2,1,0:T(8,128)(2,1)S(1)}, bf16[4,16,4096]{2,1,0:T(8,128)(2,1)S(1)}, u32[]{:S(2)}, u32[]{:S(2)}) %collective-permute-start.32) | collective-permute-done | bytes 524320 | tf_op jit(solution)/shard_map/ppermute | solution.py:95
  117.6 4.8 %shard_map.121 = (bf16[4,2,36,512]{3,2,1,0:T(8,128)(2,1)S(1)}, bf16[4,2,36,512]{3,2,1,0:T(8,128)(2,1)S(1)}, bf16[2,36,512]{2,1,0:T(8,128)(2,1)S(1)}) custom-call(bf16[8,144,512]{2,1,0:T(8,128)(2,1)S(1)} %shard_map.120.refs_0_, bf16[4,16,4096]{2,1,0:T(8,128)(2,1)S(1)} %get-tuple-element.61.refs_1_, bf16[4,16,4096]{2,1,0:T(8,128)(2,1)S(1)} %collective-permute-done.26.refs_2_, ...), custom_call_target="tpu_custom_call" | custom-call | flops 4831838208 | bytes 8000000 | tf_op jit(solution)/shard_map/pallas_call | solution.py:362
  122.4 1.5 %collective-permute-start.33 = (bf16[2,36,512]{2,1,0:T(8,128)(2,1)S(1)}, bf16[2,36,512]{2,1,0:T(8,128)(2,1)S(1)}, u32[]{:S(2)}, u32[]{:S(2)}) collective-permute-start(bf16[2,36,512]{2,1,0:T(8,128)(2,1)S(1)} %get-tuple-element.65.refs_10_), channel_id=1, source_target_pairs={{31,0},{30,1},{1,2},{0,3},{3,4},{2,5},{5,6},{4,7},{7,8},{6,9},{9,1... | collective-permute-start | bytes 221192 | tf_op jit(solution)/shard_map/ppermute | solution.py:389
  123.9 0.6 collective-permute-start.35
  124.5 4.8 %shard_map.122 = (bf16[4,2,36,512]{3,2,1,0:T(8,128)(2,1)S(1)}, bf16[4,2,36,512]{3,2,1,0:T(8,128)(2,1)S(1)}, bf16[2,36,512]{2,1,0:T(8,128)(2,1)S(1)}) custom-call(bf16[8,144,512]{2,1,0:T(8,128)(2,1)S(1)} %shard_map.120.refs_0_, bf16[4,16,4096]{2,1,0:T(8,128)(2,1)S(1)} %get-tuple-element.61.refs_1_, bf16[4,16,4096]{2,1,0:T(8,128)(2,1)S(1)} %collective-permute-done.26.refs_2_, ...), custom_call_target="tpu_custom_call" | custom-call | flops 4831838208 | bytes 8000000 | tf_op jit(solution)/shard_map/pallas_call | solution.py:362
  129.3 1.1 collective-permute-done.33
  130.5 0.4 collective-permute-start.34
  130.9 1.0 collective-permute-done.34
  131.9 5.9 %collective-permute-done.35 = bf16[4,2,36,512]{3,2,1,0:T(8,128)(2,1)S(1)} collective-permute-done((bf16[4,2,36,512]{3,2,1,0:T(8,128)(2,1)S(1)}, bf16[4,2,36,512]{3,2,1,0:T(8,128)(2,1)S(1)}, u32[]{:S(2)}, u32[]{:S(2)}) %collective-permute-start.35) | collective-permute-done | bytes 294944 | tf_op jit(solution)/shard_map/ppermute | solution.py:389
  137.8 0.1 reshape.56
  138.0 0.2 copy.21
  138.2 0.1 reshape.53
  138.4 0.2 copy.20
  138.6 0.1 reshape.50
  138.7 0.2 copy.19
  139.0 0.1 reshape.47
  139.2 0.2 copy.18
  139.4 2.9 %maximum_maximum_fusion = bf16[24,24,2,512]{3,2,1,0:T(2,128)(2,1)} fusion(bf16[6,21,2,512]{3,2,1,0:T(2,128)(2,1)S(1)} %bitcast.33, bf16[6,21,2,512]{3,2,1,0:T(2,128)(2,1)S(1)} %bitcast.34, bf16[6,21,2,512]{3,2,1,0:T(2,128)(2,1)S(1)} %bitcast.35, bf16[6,3,2,512]{3,2,1,0:T(2,128)(2,1)S(1)} %reshape_transpose_reshape_broadcast_in_dim_squeeze.15, ...), kind=kLoop, calls=%fused_computation | loop fusion | flops 4128768 | bytes 2359296 | tf_op jit(solution)/shard_map/concatenate | solution.py:414
  (70 shorter events, 0.5 us)
Async XLA Ops:
  0.0 0.9 copy-start.2
  0.9 0.8 copy-start.4
  1.8 5.7 %collective-permute-start = (bf16[1,16,2048]{2,1,0:T(8,128)(2,1)S(1)}, bf16[1,16,2048]{2,1,0:T(8,128)(2,1)S(1)}, u32[]{:S(2)}, u32[]{:S(2)}) collective-permute-start(bf16[1,16,2048]{2,1,0:T(8,128)(2,1)S(1)} %shard_map.109.refs_0_), channel_id=1, source_target_pairs={{0,8},{1,9},{2,10},{3,11},{4,12},{5,13},{6,14},{7,15},{8,0},{9,1},... | collective-permute-start | bytes 196616 | tf_op jit(solution)/shard_map/ppermute | solution.py:95
  7.4 2.8 %copy-start = (bf16[2,32,2048]{2,1,0:T(8,128)(2,1)S(1)}, bf16[2,32,2048]{2,1,0:T(8,128)(2,1)}, u32[]{:S(2)}) copy-start(bf16[2,32,2048]{2,1,0:T(8,128)(2,1)} %refs_4_.1) | copy-start | bytes 786436
  7.4 2.8 %copy-start.1 = (bf16[2,32,2048]{2,1,0:T(8,128)(2,1)S(1)}, bf16[2,32,2048]{2,1,0:T(8,128)(2,1)}, u32[]{:S(2)}) copy-start(bf16[2,32,2048]{2,1,0:T(8,128)(2,1)} %refs_5_.1) | copy-start | bytes 786436
  7.4 2.8 %copy-start.3 = (bf16[2,32,1536]{2,1,0:T(8,128)(2,1)S(1)}, bf16[2,32,1536]{2,1,0:T(8,128)(2,1)}, u32[]{:S(2)}) copy-start(bf16[2,32,1536]{2,1,0:T(8,128)(2,1)} %refs_2_.1) | copy-start | bytes 589828
  7.4 2.8 %copy-start.5 = (bf16[2,32,512]{2,1,0:T(8,128)(2,1)S(1)}, bf16[2,32,512]{2,1,0:T(8,128)(2,1)}, u32[]{:S(2)}) copy-start(bf16[2,32,512]{2,1,0:T(8,128)(2,1)} %refs_3_.1) | copy-start | bytes 196612
  7.5 12.4 %copy-start.8 = (f32[16,512]{1,0:T(8,128)S(1)}, f32[16,512]{1,0:T(8,128)}, u32[]{:S(2)}) copy-start(f32[16,512]{1,0:T(8,128)} %constant.8.clone) | copy-start | bytes 98308
  7.5 12.4 %copy-start.10 = (f32[2,16]{1,0:T(2,128)S(1)}, f32[2,16]{1,0:T(2,128)}, u32[]{:S(2)}) copy-start(f32[2,16]{1,0:T(2,128)} %param.17) | copy-start | bytes 388
  7.5 23.7 %copy-start.9 = (f32[2,2,512]{2,1,0:T(2,128)S(1)}, f32[2,2,512]{2,1,0:T(2,128)}, u32[]{:S(2)}) copy-start(f32[2,2,512]{2,1,0:T(2,128)} %param.16) | copy-start | bytes 24580
  7.5 8.8 %collective-permute-start.1 = (bf16[2,16,2048]{2,1,0:T(8,128)(2,1)S(1)}, bf16[2,16,2048]{2,1,0:T(8,128)(2,1)S(1)}, u32[]{:S(2)}, u32[]{:S(2)}) collective-permute-start(bf16[2,16,2048]{2,1,0:T(8,128)(2,1)S(1)} %shard_map.110.refs_0_), channel_id=1, source_target_pairs={{0,16},{1,17},{2,18},{3,19},{4,20},{5,21},{6,22},{7,23},{8,24},{9,... | collective-permute-start | bytes 393224 | tf_op jit(solution)/shard_map/ppermute | solution.py:95
  10.2 28.4 %copy-start.6 = (bf16[640,256]{1,0:T(8,128)(2,1)S(1)}, bf16[640,256]{1,0:T(8,128)(2,1)}, u32[]{:S(2)}) copy-start(bf16[640,256]{1,0:T(8,128)(2,1)} %constant.9.clone.refs_11_) | copy-start | bytes 983044
  10.3 11.4 %collective-permute-start.9 = (bf16[1,16,10240]{2,1,0:T(8,128)(2,1)S(1)}, bf16[1,16,10240]{2,1,0:T(8,128)(2,1)S(1)}, u32[]{:S(2)}, u32[]{:S(2)}) collective-permute-start(bf16[1,16,10240]{2,1,0:T(8,128)(2,1)S(1)} %shard_map.112.refs_0_), channel_id=1, source_target_pairs={{0,8},{1,9},{2,10},{3,11},{4,12},{5,13},{6,14},{7,15},{8,0},{9,1},... | collective-permute-start | bytes 983048 | tf_op jit(solution)/shard_map/ppermute | solution.py:95
  16.3 9.2 %collective-permute-start.2 = (bf16[4,16,2048]{2,1,0:T(8,128)(2,1)S(1)}, bf16[4,16,2048]{2,1,0:T(8,128)(2,1)S(1)}, u32[]{:S(2)}, u32[]{:S(2)}) collective-permute-start(bf16[4,16,2048]{2,1,0:T(8,128)(2,1)S(1)} %shard_map.111.refs_1_), channel_id=1, source_target_pairs={{0,2},{1,5},{2,0},{3,7},{4,6},{5,1},{6,4},{7,3},{8,10},{9,13},{10,... | collective-permute-start | bytes 786440 | tf_op jit(solution)/shard_map/ppermute | solution.py:95
  17.8 7.6 %collective-permute-start.3 = (bf16[4,16,2048]{2,1,0:T(8,128)(2,1)S(1)}, bf16[4,16,2048]{2,1,0:T(8,128)(2,1)S(1)}, u32[]{:S(2)}, u32[]{:S(2)}) collective-permute-start(bf16[4,16,2048]{2,1,0:T(8,128)(2,1)S(1)} %shard_map.111.refs_1_), channel_id=1, source_target_pairs={{0,4},{1,3},{2,6},{3,1},{4,0},{5,7},{6,2},{7,5},{8,12},{9,11},{10,... | collective-permute-start | bytes 786440 | tf_op jit(solution)/shard_map/ppermute | solution.py:95
  19.4 11.8 %collective-permute-start.4 = (bf16[4,16,2048]{2,1,0:T(8,128)(2,1)S(1)}, bf16[4,16,2048]{2,1,0:T(8,128)(2,1)S(1)}, u32[]{:S(2)}, u32[]{:S(2)}) collective-permute-start(bf16[4,16,2048]{2,1,0:T(8,128)(2,1)S(1)} %shard_map.111.refs_1_), channel_id=1, source_target_pairs={{0,6},{1,7},{2,4},{3,5},{4,2},{5,3},{6,0},{7,1},{8,14},{9,15},{10,... | collective-permute-start | bytes 786440 | tf_op jit(solution)/shard_map/ppermute | solution.py:95
  19.9 17.2 %collective-permute-start.5 = (bf16[4,16,2048]{2,1,0:T(8,128)(2,1)S(1)}, bf16[4,16,2048]{2,1,0:T(8,128)(2,1)S(1)}, u32[]{:S(2)}, u32[]{:S(2)}) collective-permute-start(bf16[4,16,2048]{2,1,0:T(8,128)(2,1)S(1)} %shard_map.111.refs_1_), channel_id=1, source_target_pairs={{0,1},{1,0},{2,3},{3,2},{4,5},{5,4},{6,7},{7,6},{8,9},{9,8},{10,11... | collective-permute-start | bytes 786440 | tf_op jit(solution)/shard_map/ppermute | solution.py:95
  21.7 13.8 %collective-permute-start.10 = (bf16[2,16,4096]{2,1,0:T(8,128)(2,1)S(1)}, bf16[2,16,4096]{2,1,0:T(8,128)(2,1)S(1)}, u32[]{:S(2)}, u32[]{:S(2)}) collective-permute-start(bf16[2,16,4096]{2,1,0:T(8,128)(2,1)S(1)} %get-tuple-element.41.refs_0_), channel_id=1, source_target_pairs={{0,16},{1,17},{2,18},{3,19},{4,20},{5,21},{6,22},{7,23},{8,24},{9,... | collective-permute-start | bytes 786440 | tf_op jit(solution)/shard_map/ppermute | solution.py:95
  25.5 13.2 %collective-permute-start.6 = (bf16[4,16,2048]{2,1,0:T(8,128)(2,1)S(1)}, bf16[4,16,2048]{2,1,0:T(8,128)(2,1)S(1)}, u32[]{:S(2)}, u32[]{:S(2)}) collective-permute-start(bf16[4,16,2048]{2,1,0:T(8,128)(2,1)S(1)} %collective-permute-done.2.refs_2_), channel_id=1, source_target_pairs={{0,1},{1,0},{2,3},{3,2},{4,5},{5,4},{6,7},{7,6},{8,9},{9,8},{10,11... | collective-permute-start | bytes 786440 | tf_op jit(solution)/shard_map/ppermute | solution.py:95
  25.5 13.2 %collective-permute-start.7 = (bf16[4,16,2048]{2,1,0:T(8,128)(2,1)S(1)}, bf16[4,16,2048]{2,1,0:T(8,128)(2,1)S(1)}, u32[]{:S(2)}, u32[]{:S(2)}) collective-permute-start(bf16[4,16,2048]{2,1,0:T(8,128)(2,1)S(1)} %collective-permute-done.3.refs_3_), channel_id=1, source_target_pairs={{0,1},{1,0},{2,3},{3,2},{4,5},{5,4},{6,7},{7,6},{8,9},{9,8},{10,11... | collective-permute-start | bytes 786440 | tf_op jit(solution)/shard_map/ppermute | solution.py:95
  31.2 7.5 %collective-permute-start.8 = (bf16[4,16,2048]{2,1,0:T(8,128)(2,1)S(1)}, bf16[4,16,2048]{2,1,0:T(8,128)(2,1)S(1)}, u32[]{:S(2)}, u32[]{:S(2)}) collective-permute-start(bf16[4,16,2048]{2,1,0:T(8,128)(2,1)S(1)} %collective-permute-done.4.refs_4_), channel_id=1, source_target_pairs={{0,1},{1,0},{2,3},{3,2},{4,5},{5,4},{6,7},{7,6},{8,9},{9,8},{10,11... | collective-permute-start | bytes 786440 | tf_op jit(solution)/shard_map/ppermute | solution.py:95
  35.5 22.3 %collective-permute-start.11 = (bf16[4,16,4096]{2,1,0:T(8,128)(2,1)S(1)}, bf16[4,16,4096]{2,1,0:T(8,128)(2,1)S(1)}, u32[]{:S(2)}, u32[]{:S(2)}) collective-permute-start(bf16[4,16,4096]{2,1,0:T(8,128)(2,1)S(1)} %shard_map.114.refs_12_.refs_1_), channel_id=1, source_target_pairs={{0,2},{1,5},{2,0},{3,7},{4,6},{5,1},{6,4},{7,3},{8,10},{9,13},{10,... | collective-permute-start | bytes 1572872 | tf_op jit(solution)/shard_map/ppermute | solution.py:95
  37.1 21.7 %collective-permute-start.12 = (bf16[4,16,4096]{2,1,0:T(8,128)(2,1)S(1)}, bf16[4,16,4096]{2,1,0:T(8,128)(2,1)S(1)}, u32[]{:S(2)}, u32[]{:S(2)}) collective-permute-start(bf16[4,16,4096]{2,1,0:T(8,128)(2,1)S(1)} %shard_map.114.refs_12_.refs_1_), channel_id=1, source_target_pairs={{0,4},{1,3},{2,6},{3,1},{4,0},{5,7},{6,2},{7,5},{8,12},{9,11},{10,... | collective-permute-start | bytes 1572872 | tf_op jit(solution)/shard_map/ppermute | solution.py:95
  38.6 19.2 %collective-permute-start.13 = (bf16[2,16,6144]{2,1,0:T(8,128)(2,1)S(1)}, bf16[2,16,6144]{2,1,0:T(8,128)(2,1)S(1)}, u32[]{:S(2)}, u32[]{:S(2)}) collective-permute-start(bf16[2,16,6144]{2,1,0:T(8,128)(2,1)S(1)} %get-tuple-element.43.refs_0_), channel_id=1, source_target_pairs={{0,16},{1,17},{2,18},{3,19},{4,20},{5,21},{6,22},{7,23},{8,24},{9,... | collective-permute-start | bytes 1179656 | tf_op jit(solution)/shard_map/ppermute | solution.py:95
  57.8 9.2 %collective-permute-start.14 = (bf16[4,16,4096]{2,1,0:T(8,128)(2,1)S(1)}, bf16[4,16,4096]{2,1,0:T(8,128)(2,1)S(1)}, u32[]{:S(2)}, u32[]{:S(2)}) collective-permute-start(bf16[4,16,4096]{2,1,0:T(8,128)(2,1)S(1)} %collective-permute-done.11.refs_2_), channel_id=1, source_target_pairs={{0,4},{1,3},{2,6},{3,1},{4,0},{5,7},{6,2},{7,5},{8,12},{9,11},{10,... | collective-permute-start | bytes 1572872 | tf_op jit(solution)/shard_map/ppermute | solution.py:95
  58.3 9.3 %collective-permute-start.15 = (bf16[4,16,4096]{2,1,0:T(8,128)(2,1)S(1)}, bf16[4,16,4096]{2,1,0:T(8,128)(2,1)S(1)}, u32[]{:S(2)}, u32[]{:S(2)}) collective-permute-start(bf16[4,16,4096]{2,1,0:T(8,128)(2,1)S(1)} %shard_map.114.refs_12_.refs_1_), channel_id=1, source_target_pairs={{0,1},{1,0},{2,3},{3,2},{4,5},{5,4},{6,7},{7,6},{8,9},{9,8},{10,11... | collective-permute-start | bytes 1572872 | tf_op jit(solution)/shard_map/ppermute | solution.py:95
  58.3 9.8 %collective-permute-start.16 = (bf16[4,16,4096]{2,1,0:T(8,128)(2,1)S(1)}, bf16[4,16,4096]{2,1,0:T(8,128)(2,1)S(1)}, u32[]{:S(2)}, u32[]{:S(2)}) collective-permute-start(bf16[4,16,4096]{2,1,0:T(8,128)(2,1)S(1)} %collective-permute-done.11.refs_2_), channel_id=1, source_target_pairs={{0,1},{1,0},{2,3},{3,2},{4,5},{5,4},{6,7},{7,6},{8,9},{9,8},{10,11... | collective-permute-start | bytes 1572872 | tf_op jit(solution)/shard_map/ppermute | solution.py:95
  58.9 9.3 %collective-permute-start.17 = (bf16[4,16,4096]{2,1,0:T(8,128)(2,1)S(1)}, bf16[4,16,4096]{2,1,0:T(8,128)(2,1)S(1)}, u32[]{:S(2)}, u32[]{:S(2)}) collective-permute-start(bf16[4,16,4096]{2,1,0:T(8,128)(2,1)S(1)} %collective-permute-done.12.refs_3_), channel_id=1, source_target_pairs={{0,1},{1,0},{2,3},{3,2},{4,5},{5,4},{6,7},{7,6},{8,9},{9,8},{10,11... | collective-permute-start | bytes 1572872 | tf_op jit(solution)/shard_map/ppermute | solution.py:95
  67.0 1.9 %collective-permute-start.18 = (bf16[4,16,4096]{2,1,0:T(8,128)(2,1)S(1)}, bf16[4,16,4096]{2,1,0:T(8,128)(2,1)S(1)}, u32[]{:S(2)}, u32[]{:S(2)}) collective-permute-start(bf16[4,16,4096]{2,1,0:T(8,128)(2,1)S(1)} %collective-permute-done.14.refs_2_.refs_4_), channel_id=1, source_target_pairs={{0,1},{1,0},{2,3},{3,2},{4,5},{5,4},{6,7},{7,6},{8,9},{9,8},{10,11... | collective-permute-start | bytes 1572872 | tf_op jit(solution)/shard_map/ppermute | solution.py:95
  67.1 9.7 %collective-permute-start.19 = (bf16[4,16,2048]{2,1,0:T(8,128)(2,1)S(1)}, bf16[4,16,2048]{2,1,0:T(8,128)(2,1)S(1)}, u32[]{:S(2)}, u32[]{:S(2)}) collective-permute-start(bf16[4,16,2048]{2,1,0:T(8,128)(2,1)S(1)} %get-tuple-element.48.refs_10_.refs_0_), channel_id=1, source_target_pairs={{0,4},{1,3},{2,6},{3,1},{4,0},{5,7},{6,2},{7,5},{8,12},{9,11},{10,... | collective-permute-start | bytes 786440 | tf_op jit(solution)/shard_map/ppermute | solution.py:95
  67.6 9.1 %collective-permute-start.23 = (bf16[4,16,2048]{2,1,0:T(8,128)(2,1)S(1)}, bf16[4,16,2048]{2,1,0:T(8,128)(2,1)S(1)}, u32[]{:S(2)}, u32[]{:S(2)}) collective-permute-start(bf16[4,16,2048]{2,1,0:T(8,128)(2,1)S(1)} %get-tuple-element.48.refs_10_.refs_0_), channel_id=1, source_target_pairs={{0,2},{1,5},{2,0},{3,7},{4,6},{5,1},{6,4},{7,3},{8,10},{9,13},{10,... | collective-permute-start | bytes 786440 | tf_op jit(solution)/shard_map/ppermute | solution.py:95
  73.7 11.9 %collective-permute-start.20 = (bf16[4,2,36,512]{3,2,1,0:T(8,128)(2,1)S(1)}, bf16[4,2,36,512]{3,2,1,0:T(8,128)(2,1)S(1)}, u32[]{:S(2)}, u32[]{:S(2)}) collective-permute-start(bf16[4,2,36,512]{3,2,1,0:T(8,128)(2,1)S(1)} %get-tuple-element.49.refs_0_), channel_id=1, source_target_pairs={{2,0},{3,1},{4,2},{5,3},{6,4},{7,5},{8,6},{9,7},{10,8},{11,9},{12,... | collective-permute-start | bytes 884744 | tf_op jit(solution)/shard_map/ppermute | solution.py:389
  76.8 8.8 %collective-permute-start.21 = (bf16[2,36,512]{2,1,0:T(8,128)(2,1)S(1)}, bf16[2,36,512]{2,1,0:T(8,128)(2,1)S(1)}, u32[]{:S(2)}, u32[]{:S(2)}) collective-permute-start(bf16[2,36,512]{2,1,0:T(8,128)(2,1)S(1)} %get-tuple-element.51.refs_10_), channel_id=1, source_target_pairs={{3,0},{2,1},{5,2},{4,3},{7,4},{6,5},{9,6},{8,7},{11,8},{10,9},{13,... | collective-permute-start | bytes 221192 | tf_op jit(solution)/shard_map/ppermute | solution.py:389
  76.8 8.8 %collective-permute-start.24 = (bf16[4,16,2048]{2,1,0:T(8,128)(2,1)S(1)}, bf16[4,16,2048]{2,1,0:T(8,128)(2,1)S(1)}, u32[]{:S(2)}, u32[]{:S(2)}) collective-permute-start(bf16[4,16,2048]{2,1,0:T(8,128)(2,1)S(1)} %collective-permute-done.23.refs_1_), channel_id=1, source_target_pairs={{0,4},{1,3},{2,6},{3,1},{4,0},{5,7},{6,2},{7,5},{8,12},{9,11},{10,... | collective-permute-start | bytes 786440 | tf_op jit(solution)/shard_map/ppermute | solution.py:95
  85.6 7.2 %copy-start.7 = (f32[144,256]{1,0:T(8,128)S(1)}, f32[144,256]{1,0:T(8,128)}, u32[]{:S(2)}) copy-start(f32[144,256]{1,0:T(8,128)} %constant.10.clone.refs_12_) | copy-start | bytes 442372
  85.7 7.1 %collective-permute-start.25 = (bf16[16,16,2048]{2,1,0:T(8,128)(2,1)S(1)}, bf16[16,16,2048]{2,1,0:T(8,128)(2,1)S(1)}, u32[]{:S(2)}, u32[]{:S(2)}) collective-permute-start(bf16[16,16,2048]{2,1,0:T(8,128)(2,1)S(1)} %shard_map.119.refs_7_), channel_id=1, source_target_pairs={{0,1},{1,0},{2,3},{3,2},{4,5},{5,4},{6,7},{7,6},{8,9},{9,8},{10,11... | collective-permute-start | bytes 3145736 | tf_op jit(solution)/shard_map/ppermute | solution.py:95
  88.4 4.4 %collective-permute-start.22 = (bf16[4,36,512]{2,1,0:T(8,128)(2,1)S(1)}, bf16[4,36,512]{2,1,0:T(8,128)(2,1)S(1)}, u32[]{:S(2)}, u32[]{:S(2)}) collective-permute-start(bf16[4,36,512]{2,1,0:T(8,128)(2,1)S(1)} %pad_maximum_fusion), channel_id=1, source_target_pairs={{1,0},{0,1},{3,2},{2,3},{5,4},{4,5},{7,6},{6,7},{9,8},{8,9},{11,10... | collective-permute-start | bytes 442376 | tf_op jit(solution)/shard_map/ppermute | solution.py:389
  88.5 17.7 %collective-permute-start.26 = (bf16[4,16,4096]{2,1,0:T(8,128)(2,1)S(1)}, bf16[4,16,4096]{2,1,0:T(8,128)(2,1)S(1)}, u32[]{:S(2)}, u32[]{:S(2)}) collective-permute-start(bf16[4,16,4096]{2,1,0:T(8,128)(2,1)S(1)} %get-tuple-element.61.refs_1_), channel_id=1, source_target_pairs={{0,2},{1,5},{2,0},{3,7},{4,6},{5,1},{6,4},{7,3},{8,10},{9,13},{10,... | collective-permute-start | bytes 1572872 | tf_op jit(solution)/shard_map/ppermute | solution.py:95
  90.7 15.9 %collective-permute-start.27 = (bf16[4,16,4096]{2,1,0:T(8,128)(2,1)S(1)}, bf16[4,16,4096]{2,1,0:T(8,128)(2,1)S(1)}, u32[]{:S(2)}, u32[]{:S(2)}) collective-permute-start(bf16[4,16,4096]{2,1,0:T(8,128)(2,1)S(1)} %get-tuple-element.61.refs_1_), channel_id=1, source_target_pairs={{0,4},{1,3},{2,6},{3,1},{4,0},{5,7},{6,2},{7,5},{8,12},{9,11},{10,... | collective-permute-start | bytes 1572872 | tf_op jit(solution)/shard_map/ppermute | solution.py:95
  92.8 22.9 %collective-permute-start.28 = (bf16[4,16,4096]{2,1,0:T(8,128)(2,1)S(1)}, bf16[4,16,4096]{2,1,0:T(8,128)(2,1)S(1)}, u32[]{:S(2)}, u32[]{:S(2)}) collective-permute-start(bf16[4,16,4096]{2,1,0:T(8,128)(2,1)S(1)} %get-tuple-element.61.refs_1_), channel_id=1, source_target_pairs={{0,6},{1,7},{2,4},{3,5},{4,2},{5,3},{6,0},{7,1},{8,14},{9,15},{10,... | collective-permute-start | bytes 1572872 | tf_op jit(solution)/shard_map/ppermute | solution.py:95
  92.8 22.9 %collective-permute-start.29 = (bf16[4,16,4096]{2,1,0:T(8,128)(2,1)S(1)}, bf16[4,16,4096]{2,1,0:T(8,128)(2,1)S(1)}, u32[]{:S(2)}, u32[]{:S(2)}) collective-permute-start(bf16[4,16,4096]{2,1,0:T(8,128)(2,1)S(1)} %get-tuple-element.61.refs_1_), channel_id=1, source_target_pairs={{0,1},{1,0},{2,3},{3,2},{4,5},{5,4},{6,7},{7,6},{8,9},{9,8},{10,11... | collective-permute-start | bytes 1572872 | tf_op jit(solution)/shard_map/ppermute | solution.py:95
  106.1 9.6 %collective-permute-start.30 = (bf16[4,16,4096]{2,1,0:T(8,128)(2,1)S(1)}, bf16[4,16,4096]{2,1,0:T(8,128)(2,1)S(1)}, u32[]{:S(2)}, u32[]{:S(2)}) collective-permute-start(bf16[4,16,4096]{2,1,0:T(8,128)(2,1)S(1)} %collective-permute-done.26.refs_2_), channel_id=1, source_target_pairs={{0,1},{1,0},{2,3},{3,2},{4,5},{5,4},{6,7},{7,6},{8,9},{9,8},{10,11... | collective-permute-start | bytes 1572872 | tf_op jit(solution)/shard_map/ppermute | solution.py:95
  106.6 9.1 %collective-permute-start.31 = (bf16[4,16,4096]{2,1,0:T(8,128)(2,1)S(1)}, bf16[4,16,4096]{2,1,0:T(8,128)(2,1)S(1)}, u32[]{:S(2)}, u32[]{:S(2)}) collective-permute-start(bf16[4,16,4096]{2,1,0:T(8,128)(2,1)S(1)} %collective-permute-done.27.refs_3_), channel_id=1, source_target_pairs={{0,1},{1,0},{2,3},{3,2},{4,5},{5,4},{6,7},{7,6},{8,9},{9,8},{10,11... | collective-permute-start | bytes 1572872 | tf_op jit(solution)/shard_map/ppermute | solution.py:95
  115.7 1.9 %collective-permute-start.32 = (bf16[4,16,4096]{2,1,0:T(8,128)(2,1)S(1)}, bf16[4,16,4096]{2,1,0:T(8,128)(2,1)S(1)}, u32[]{:S(2)}, u32[]{:S(2)}) collective-permute-start(bf16[4,16,4096]{2,1,0:T(8,128)(2,1)S(1)} %collective-permute-done.28.refs_4_), channel_id=1, source_target_pairs={{0,1},{1,0},{2,3},{3,2},{4,5},{5,4},{6,7},{7,6},{8,9},{9,8},{10,11... | collective-permute-start | bytes 1572872 | tf_op jit(solution)/shard_map/ppermute | solution.py:95
  122.4 8.1 %collective-permute-start.33 = (bf16[2,36,512]{2,1,0:T(8,128)(2,1)S(1)}, bf16[2,36,512]{2,1,0:T(8,128)(2,1)S(1)}, u32[]{:S(2)}, u32[]{:S(2)}) collective-permute-start(bf16[2,36,512]{2,1,0:T(8,128)(2,1)S(1)} %get-tuple-element.65.refs_10_), channel_id=1, source_target_pairs={{31,0},{30,1},{1,2},{0,3},{3,4},{2,5},{5,6},{4,7},{7,8},{6,9},{9,1... | collective-permute-start | bytes 221192 | tf_op jit(solution)/shard_map/ppermute | solution.py:389
  123.9 13.9 %collective-permute-start.35 = (bf16[4,2,36,512]{3,2,1,0:T(8,128)(2,1)S(1)}, bf16[4,2,36,512]{3,2,1,0:T(8,128)(2,1)S(1)}, u32[]{:S(2)}, u32[]{:S(2)}) collective-permute-start(bf16[4,2,36,512]{3,2,1,0:T(8,128)(2,1)S(1)} %get-tuple-element.71), channel_id=1, source_target_pairs={{30,0},{31,1},{0,2},{1,3},{2,4},{3,5},{4,6},{5,7},{6,8},{7,9},{8,1... | collective-permute-start | bytes 884744 | tf_op jit(solution)/shard_map/ppermute | solution.py:389
  130.5 1.4 %collective-permute-start.34 = (bf16[4,36,512]{2,1,0:T(8,128)(2,1)S(1)}, bf16[4,36,512]{2,1,0:T(8,128)(2,1)S(1)}, u32[]{:S(2)}, u32[]{:S(2)}) collective-permute-start(bf16[4,36,512]{2,1,0:T(8,128)(2,1)S(1)} %pad_maximum_fusion.1), channel_id=1, source_target_pairs={{1,0},{0,1},{3,2},{2,3},{5,4},{4,5},{7,6},{6,7},{9,8},{8,9},{11,10... | collective-permute-start | bytes 442376 | tf_op jit(solution)/shard_map/ppermute | solution.py:389

commit v9 on v8

--- a/solution.py
+++ b/solution.py
@@ -22,6 +22,7 @@
 GROUP = 8
 PART = 4
 WIDE = GROUP * HEAD
+Z_ORDER = (0, 2, 1, 3)
 ANY = pl.BlockSpec(memory_space=pl.ANY)
 NT = (((1,), (1,)), ((), ()))
 
@@ -99,14 +100,6 @@
     return send(block, lambda z, y, x, c: (z ^ bit, y, x, c))
 
 
-def along_z(block, after=()):
-    bit = 2
-    while bit < lax.axis_size("lon") // 4:
-        (block,) = join([[block, across_z(block, bit)]], (), after)
-        bit *= 2
-    return block
-
-
 def swap(z, y, x, c):
     return z, y, x, 1 - c
 
@@ -139,7 +132,6 @@
         copy.wait()
         return
     half = pieces[0].shape[-2]
-    lon_size = lax.axis_size("lon")
     copies = [
         pltpu.make_async_copy(piece, stage_ref.at[index], sem.at[index])
         for index, piece in enumerate(pieces)
@@ -160,10 +152,10 @@
         )
         copy.wait()
         for column in range(4) if joined else (index % 4,):
-            for step in range(lon_size // 4):
-                shard = (z ^ step) * 4 + squares[column]
+            for step in range(len(Z_ORDER)):
+                shard = (z ^ Z_ORDER[step]) * 4 + squares[column]
                 row = pl.multiple_of((shard * 2 + core) * half, 16)
-                place = column * (lon_size // 4) + step if joined else step
+                place = column * len(Z_ORDER) + step if joined else step
                 w_ref[pl.ds(row, half), :] = stage_ref[index, place]
 
 
@@ -436,34 +428,28 @@
     low_edge, high_edge = (0, 0), (row_windows - 1, 1)
     if relay:
         (own,) = join([], [[(0, weight) for weight in weights[:2]]])
-        later = [(0, weight) for weight in weights[2:]] + [(1, weight) for weight in weights]
-        (later_own,) = join([], [later])
-        attend_width, feed_width = (
-            sum(weight.shape[2] for weight in pair) for pair in (weights[:2], weights[2:])
+        feed_own, last_own = join(
+            [], [[(0, weight) for weight in weights[2:]], [(1, weight) for weight in weights]]
         )
-        (pair,) = join([[own, across_z(own, 1)]], (), (windows,))
-        column = along_z(pair)
+        widths = tuple(sum(weight.shape[2] for weight in pair) for pair in (weights[:2], weights[2:]))
+        (pair,) = join([[own, across_z(own, 2)]], (), (windows,))
+        (feed_pair,) = join([[feed_own, across_z(feed_own, 2)]])
+        (column,) = join([[pair, across_z(pair, 1)]], (), (feed_pair,))
         pieces = whole_pieces(column, [send(column, way) for way in (beside, across, corner)])
-        feed_pair, last_pair = join(
-            [[later_own, across_z(later_own, 1)]], widths=(feed_width, attend_width + feed_width)
-        )
-        feed_column = along_z(feed_pair)
-        received = [send(feed_column, way) for way in (beside, across)]
+        (last_pair,) = join([[last_own, across_z(last_own, 2)]])
+        (feed_column,) = join([[feed_pair, across_z(feed_pair, 1)]], (), (last_pair,))
+        received = [send(feed_column, way) for way in (beside, across, corner)]
         last_pair = tied(last_pair, feed_column)
-        last_other = across_z(last_pair, 2)
+        last_other = across_z(last_pair, 1)
         middle = attention(0, [windows], pieces, (feed_column,))
-        received.append(send(tied(received[0], (middle, last_other)), across))
-        feed_pieces = whole_pieces(feed_column, received, middle)
-        column, last_column = join(
-            [[last_pair, last_other]], (), (received[2],), (attend_width, feed_width)
-        )
-        received = [send(column, way) for way in (beside, across)]
+        feed_pieces = whole_pieces(feed_column, received, (middle, last_other))
+        column, last_column = join([[last_pair, last_other]], (), (middle,), widths)
+        received = [send(column, way) for way in (beside, across, corner)]
         left_0, right_0, low_0 = forward(0, middle, 0, feed_pieces, low_edge, (column,))
-        received.append(send(tied(received[0], low_0), across))
-        last_column = tied(last_column, (low_0, received[1]))
+        last_column = tied(last_column, low_0)
         last_received = [send(last_column, way) for way in (beside, across, corner)]
         ahead, ahead_low = shift_from(left_0, 1, 0), shift_from(low_0, 1, 1)
-        left_1, right_1, low_1 = forward(0, middle, 1, feed_pieces, low_edge, (low_0, received[1]))
+        left_1, right_1, low_1 = forward(0, middle, 1, feed_pieces, low_edge, (low_0,))
         (joined,) = join([[column] + [tied(part, (low_1, ahead, ahead_low)) for part in received]])
         pieces = [joined, send(joined, swap)]
     else:

time: 143 us -> 136 us (0.951)
  waiting for transfers between devices: 56.7 us -> 40.5 us
  starting transfers between devices: 30 us -> 37.7 us
  local copies, waits for them, and re-layouts: 5.9 us -> 7.67 us
    ppermute x30 -> x31, waiting for transfers between devices: 44.7 us -> 27.4 us  [send(): return lax.ppermute(block, ('lon', 'lat'), pairs)]
    ppermute x30 -> x31, starting transfers between devices: 24.4 us -> 29.3 us  [send(): return lax.ppermute(block, ('lon', 'lat'), pairs)]
    unnamed x22 -> x20, local copies, waits for them, and re-layouts: 1.82 us -> 4.86 us
    ppermute x6, starting transfers between devices: 5.63 us -> 8.42 us  [shift_from(): return lax.ppermute(block, ('lon', 'lat'), pairs)]
  transfers between devices with their start and end apart: 36 -> 37, of which waited for: 14 -> 12; matrix products, arithmetic and copies ran while one was open for 2% -> 1% of each run, Pallas kernels for 29% -> 30%
where the time goes in v9:
time: 136 us
  Pallas kernels  46.2 us (34%)
  waiting for transfers between devices  40.5 us (30%)
  starting transfers between devices  37.7 us (28%)
  local copies, waits for them, and re-layouts  7.67 us (6%)
  other arithmetic  3.03 us (2%)
    ppermute x31, starting transfers between devices, send(): return lax.ppermute(block, ('lon', 'lat'), pairs)  29.3 us
    ppermute x31, waiting for transfers between devices, send(): return lax.ppermute(block, ('lon', 'lat'), pairs)  27.4 us
    pallas_call x2, Pallas kernels, attend(): pl.pallas_call(functools.partial(attend_kernel, shifted, row_windows, len...  26.7 us
    pallas_call x4, Pallas kernels, feed(): pl.pallas_call(functools.partial(feed_kernel, len(pieces), hidden_size, 5...  19.3 us
    ppermute x6, waiting for transfers between devices, shift_from(): return lax.ppermute(block, ('lon', 'lat'), pairs)  13.1 us
    ppermute x6, starting transfers between devices, shift_from(): return lax.ppermute(block, ('lon', 'lat'), pairs)  8.42 us
    unnamed x20, local copies, waits for them, and re-layouts  4.86 us
    concatenate x1, other arithmetic, back_in_place(): return jnp.concatenate([first, jnp.concatenate([tops, own], 1)], 0)  2.9 us
  transfers between devices with their start and end apart: 37, of which 12 were waited for; matrix products, arithmetic and copies ran while one was open for 1% of the time, Pallas kernels for 30%

profile of v9, /device:TPU:0, one launch (start us, length us, event | category | flops | bytes accessed | tf_op | source)
XLA Modules:
  0.0 135.6 jit_solution(1444929310229712437)
XLA Ops:
  0.0 0.9 copy-done.2
  0.9 0.8 copy-done.3
  1.8 4.0 %collective-permute-start = (bf16[1,16,2048]{2,1,0:T(8,128)(2,1)S(1)}, bf16[1,16,2048]{2,1,0:T(8,128)(2,1)S(1)}, u32[]{:S(2)}, u32[]{:S(2)}) collective-permute-start(bf16[1,16,2048]{2,1,0:T(8,128)(2,1)S(1)} %shard_map.109.refs_0_), channel_id=1, source_target_pairs={{0,16},{1,17},{2,18},{3,19},{4,20},{5,21},{6,22},{7,23},{8,24},{9,... | collective-permute-start | bytes 196616 | tf_op jit(solution)/shard_map/ppermute | solution.py:96
  5.8 0.9 copy-done
  6.8 0.9 copy-done.1
  7.7 0.1 collective-permute-start.2
  7.8 1.2 copy-done.6
  9.0 0.8 copy.23
  9.8 0.5 reshape.45.refs_2_.refs_0_
  10.4 3.0 %collective-permute-start.1 = (bf16[2,16,2048]{2,1,0:T(8,128)(2,1)S(1)}, bf16[2,16,2048]{2,1,0:T(8,128)(2,1)S(1)}, u32[]{:S(2)}, u32[]{:S(2)}) collective-permute-start(bf16[2,16,2048]{2,1,0:T(8,128)(2,1)S(1)} %shard_map.110.refs_0_), channel_id=1, source_target_pairs={{0,8},{1,9},{2,10},{3,11},{4,12},{5,13},{6,14},{7,15},{8,0},{9,1},... | collective-permute-start | bytes 393224 | tf_op jit(solution)/shard_map/ppermute | solution.py:96
  13.4 3.2 %collective-permute-done.2.refs_1_ = bf16[1,16,4096]{2,1,0:T(8,128)(2,1)S(1)} collective-permute-done((bf16[1,16,4096]{2,1,0:T(8,128)(2,1)S(1)}, bf16[1,16,4096]{2,1,0:T(8,128)(2,1)S(1)}, u32[]{:S(2)}, u32[]{:S(2)}) %collective-permute-start.2) | collective-permute-done | bytes 131104 | tf_op jit(solution)/shard_map/ppermute | solution.py:96
  16.6 1.3 collective-permute-done.1.refs_1_
  17.9 1.6 %collective-permute-start.3 = (bf16[4,16,2048]{2,1,0:T(8,128)(2,1)S(1)}, bf16[4,16,2048]{2,1,0:T(8,128)(2,1)S(1)}, u32[]{:S(2)}, u32[]{:S(2)}) collective-permute-start(bf16[4,16,2048]{2,1,0:T(8,128)(2,1)S(1)} %shard_map.113.refs_1_), channel_id=1, source_target_pairs={{0,2},{1,5},{2,0},{3,7},{4,6},{5,1},{6,4},{7,3},{8,10},{9,13},{10,... | collective-permute-start | bytes 786440 | tf_op jit(solution)/shard_map/ppermute | solution.py:96
  19.5 1.5 %collective-permute-start.4 = (bf16[4,16,2048]{2,1,0:T(8,128)(2,1)S(1)}, bf16[4,16,2048]{2,1,0:T(8,128)(2,1)S(1)}, u32[]{:S(2)}, u32[]{:S(2)}) collective-permute-start(bf16[4,16,2048]{2,1,0:T(8,128)(2,1)S(1)} %shard_map.113.refs_1_), channel_id=1, source_target_pairs={{0,4},{1,3},{2,6},{3,1},{4,0},{5,7},{6,2},{7,5},{8,12},{9,11},{10,... | collective-permute-start | bytes 786440 | tf_op jit(solution)/shard_map/ppermute | solution.py:96
  21.0 0.5 collective-permute-start.5
  21.5 1.8 %collective-permute-start.11 = (bf16[1,16,6144]{2,1,0:T(8,128)(2,1)S(1)}, bf16[1,16,6144]{2,1,0:T(8,128)(2,1)S(1)}, u32[]{:S(2)}, u32[]{:S(2)}) collective-permute-start(bf16[1,16,6144]{2,1,0:T(8,128)(2,1)S(1)} %get-tuple-element.40.refs_0_), channel_id=1, source_target_pairs={{0,16},{1,17},{2,18},{3,19},{4,20},{5,21},{6,22},{7,23},{8,24},{9,... | collective-permute-start | bytes 589832 | tf_op jit(solution)/shard_map/ppermute | solution.py:96
  23.3 0.1 multiply_reduce_fusion
  23.4 2.2 %collective-permute-start.10 = (bf16[2,16,4096]{2,1,0:T(8,128)(2,1)S(1)}, bf16[2,16,4096]{2,1,0:T(8,128)(2,1)S(1)}, u32[]{:S(2)}, u32[]{:S(2)}) collective-permute-start(bf16[2,16,4096]{2,1,0:T(8,128)(2,1)S(1)} %shard_map.112.refs_2_.refs_0_), channel_id=1, source_target_pairs={{0,8},{1,9},{2,10},{3,11},{4,12},{5,13},{6,14},{7,15},{8,0},{9,1},... | collective-permute-start | bytes 786440 | tf_op jit(solution)/shard_map/ppermute | solution.py:96
  25.6 4.0 %collective-permute-done.11.refs_1_ = bf16[1,16,6144]{2,1,0:T(8,128)(2,1)S(1)} collective-permute-done((bf16[1,16,6144]{2,1,0:T(8,128)(2,1)S(1)}, bf16[1,16,6144]{2,1,0:T(8,128)(2,1)S(1)}, u32[]{:S(2)}, u32[]{:S(2)}) %collective-permute-start.11) | collective-permute-done | bytes 196640 | tf_op jit(solution)/shard_map/ppermute | solution.py:96
  29.6 0.5 collective-permute-start.7
  30.1 0.7 collective-permute-done.4.refs_3_
  30.8 0.5 collective-permute-start.9
  31.4 0.5 collective-permute-done.10.refs_1_
  31.9 1.6 %collective-permute-start.12 = (bf16[4,16,4096]{2,1,0:T(8,128)(2,1)S(1)}, bf16[4,16,4096]{2,1,0:T(8,128)(2,1)S(1)}, u32[]{:S(2)}, u32[]{:S(2)}) collective-permute-start(bf16[4,16,4096]{2,1,0:T(8,128)(2,1)S(1)} %shard_map.115.refs_12_.refs_1_), channel_id=1, source_target_pairs={{0,2},{1,5},{2,0},{3,7},{4,6},{5,1},{6,4},{7,3},{8,10},{9,13},{10,... | collective-permute-start | bytes 1572872 | tf_op jit(solution)/shard_map/ppermute | solution.py:96
  33.5 1.5 %collective-permute-start.13 = (bf16[4,16,4096]{2,1,0:T(8,128)(2,1)S(1)}, bf16[4,16,4096]{2,1,0:T(8,128)(2,1)S(1)}, u32[]{:S(2)}, u32[]{:S(2)}) collective-permute-start(bf16[4,16,4096]{2,1,0:T(8,128)(2,1)S(1)} %shard_map.115.refs_12_.refs_1_), channel_id=1, source_target_pairs={{0,4},{1,3},{2,6},{3,1},{4,0},{5,7},{6,2},{7,5},{8,12},{9,11},{10,... | collective-permute-start | bytes 1572872 | tf_op jit(solution)/shard_map/ppermute | solution.py:96
  35.0 0.5 collective-permute-start.14
  35.5 1.7 %collective-permute-start.16 = (bf16[2,16,6144]{2,1,0:T(8,128)(2,1)S(1)}, bf16[2,16,6144]{2,1,0:T(8,128)(2,1)S(1)}, u32[]{:S(2)}, u32[]{:S(2)}) collective-permute-start(bf16[2,16,6144]{2,1,0:T(8,128)(2,1)S(1)} %shard_map.114.refs_2_.refs_0_), channel_id=1, source_target_pairs={{0,8},{1,9},{2,10},{3,11},{4,12},{5,13},{6,14},{7,15},{8,0},{9,1},... | collective-permute-start | bytes 1179656 | tf_op jit(solution)/shard_map/ppermute | solution.py:96
  37.2 13.4 %shard_map.116.refs_2_.refs_0_ = bf16[8,144,512]{2,1,0:T(8,128)(2,1)S(1)} custom-call(bf16[8,144,512]{2,1,0:T(8,128)(2,1)S(1)} %reshape.45.refs_2_.refs_0_, bf16[4,16,2048]{2,1,0:T(8,128)(2,1)S(1)} %shard_map.113.refs_1_, bf16[4,16,2048]{2,1,0:T(8,128)(2,1)S(1)} %collective-permute-done.3.refs_2_, bf16[4,16,2048]{2,1,0:T(8,128)(2,1)S(1)} %collective-permute-done.4.refs_3_, ...), custom_call_target="tpu_custom_call" | custom-call | flops 16000000000 | bytes 6000000 | tf_op jit(solution)/shard_map/pallas_call | solution.py:296
  50.6 0.2 collective-permute-start.17
  50.9 0.3 collective-permute-start.18
  51.2 6.9 %collective-permute-done.14.refs_4_ = bf16[4,16,4096]{2,1,0:T(8,128)(2,1)S(1)} collective-permute-done((bf16[4,16,4096]{2,1,0:T(8,128)(2,1)S(1)}, bf16[4,16,4096]{2,1,0:T(8,128)(2,1)S(1)}, u32[]{:S(2)}, u32[]{:S(2)}) %collective-permute-start.14) | collective-permute-done | bytes 524320 | tf_op jit(solution)/shard_map/ppermute | solution.py:96
  58.2 0.9 collective-permute-start.23
  59.1 1.5 %collective-permute-start.24 = (bf16[4,16,2048]{2,1,0:T(8,128)(2,1)S(1)}, bf16[4,16,2048]{2,1,0:T(8,128)(2,1)S(1)}, u32[]{:S(2)}, u32[]{:S(2)}) collective-permute-start(bf16[4,16,2048]{2,1,0:T(8,128)(2,1)S(1)} %get-tuple-element.45.refs_10_.refs_0_), channel_id=1, source_target_pairs={{0,4},{1,3},{2,6},{3,1},{4,0},{5,7},{6,2},{7,5},{8,12},{9,11},{10,... | collective-permute-start | bytes 786440 | tf_op jit(solution)/shard_map/ppermute | solution.py:96
  60.6 1.1 collective-permute-start.25
  61.8 4.8 %shard_map.118 = (bf16[4,2,36,512]{3,2,1,0:T(8,128)(2,1)S(1)}, bf16[4,2,36,512]{3,2,1,0:T(8,128)(2,1)S(1)}, bf16[2,36,512]{2,1,0:T(8,128)(2,1)S(1)}) custom-call(bf16[8,144,512]{2,1,0:T(8,128)(2,1)S(1)} %shard_map.116.refs_2_.refs_0_, bf16[4,16,4096]{2,1,0:T(8,128)(2,1)S(1)} %shard_map.115.refs_12_.refs_1_, ...), custom_call_target="tpu_custom_call" | custom-call | flops 4831838208 | bytes 8000000 | tf_op jit(solution)/shard_map/pallas_call | solution.py:354
  66.6 5.1 %collective-permute-start.20 = (bf16[4,2,36,512]{3,2,1,0:T(8,128)(2,1)S(1)}, bf16[4,2,36,512]{3,2,1,0:T(8,128)(2,1)S(1)}, u32[]{:S(2)}, u32[]{:S(2)}) collective-permute-start(bf16[4,2,36,512]{3,2,1,0:T(8,128)(2,1)S(1)} %get-tuple-element.46.refs_0_), channel_id=1, source_target_pairs={{2,0},{3,1},{4,2},{5,3},{6,4},{7,5},{8,6},{9,7},{10,8},{11,9},{12,... | collective-permute-start | bytes 884744 | tf_op jit(solution)/shard_map/ppermute | solution.py:381
  71.7 4.8 %shard_map.119 = (bf16[4,2,36,512]{3,2,1,0:T(8,128)(2,1)S(1)}, bf16[4,2,36,512]{3,2,1,0:T(8,128)(2,1)S(1)}, bf16[2,36,512]{2,1,0:T(8,128)(2,1)S(1)}) custom-call(bf16[8,144,512]{2,1,0:T(8,128)(2,1)S(1)} %shard_map.116.refs_2_.refs_0_, bf16[4,16,4096]{2,1,0:T(8,128)(2,1)S(1)} %shard_map.115.refs_12_.refs_1_, ...), custom_call_target="tpu_custom_call" | custom-call | flops 4831838208 | bytes 8000000 | tf_op jit(solution)/shard_map/pallas_call | solution.py:354
  76.5 5.3 %collective-permute-done.21.refs_6_ = bf16[2,36,512]{2,1,0:T(8,128)(2,1)S(1)} collective-permute-done((bf16[2,36,512]{2,1,0:T(8,128)(2,1)S(1)}, bf16[2,36,512]{2,1,0:T(8,128)(2,1)S(1)}, u32[]{:S(2)}, u32[]{:S(2)}) %collective-permute-start.21) | collective-permute-done | bytes 73760 | tf_op jit(solution)/shard_map/ppermute | solution.py:381
  82.0 0.6 collective-permute-start.22
  82.6 1.4 %collective-permute-start.27 = (bf16[4,16,4096]{2,1,0:T(8,128)(2,1)S(1)}, bf16[4,16,4096]{2,1,0:T(8,128)(2,1)S(1)}, u32[]{:S(2)}, u32[]{:S(2)}) collective-permute-start(bf16[4,16,4096]{2,1,0:T(8,128)(2,1)S(1)} %get-tuple-element.57.refs_1_), channel_id=1, source_target_pairs={{0,2},{1,5},{2,0},{3,7},{4,6},{5,1},{6,4},{7,3},{8,10},{9,13},{10,... | collective-permute-start | bytes 1572872 | tf_op jit(solution)/shard_map/ppermute | solution.py:96
  84.0 0.3 collective-permute-start.28
  84.3 1.8 %collective-permute-start.29 = (bf16[4,16,4096]{2,1,0:T(8,128)(2,1)S(1)}, bf16[4,16,4096]{2,1,0:T(8,128)(2,1)S(1)}, u32[]{:S(2)}, u32[]{:S(2)}) collective-permute-start(bf16[4,16,4096]{2,1,0:T(8,128)(2,1)S(1)} %get-tuple-element.57.refs_1_), channel_id=1, source_target_pairs={{0,6},{1,7},{2,4},{3,5},{4,2},{5,3},{6,0},{7,1},{8,14},{9,15},{10,... | collective-permute-start | bytes 1572872 | tf_op jit(solution)/shard_map/ppermute | solution.py:96
  86.1 13.3 %shard_map.121.refs_0_ = bf16[8,144,512]{2,1,0:T(8,128)(2,1)S(1)} custom-call(bf16[4,2,36,512]{3,2,1,0:T(8,128)(2,1)S(1)} %get-tuple-element.46.refs_0_, bf16[4,2,36,512]{3,2,1,0:T(8,128)(2,1)S(1)} %get-tuple-element.47.refs_1_, bf16[4,2,36,512]{3,2,1,0:T(8,128)(2,1)S(1)} %get-tuple-element.49.refs_2_, ...), custom_call_target="tpu_custom_call" | custom-call | flops 16000000000 | bytes 6000000 | tf_op jit(solution)/shard_map/pallas_call | solution.py:296
  99.4 0.5 collective-permute-start.31
  100.0 0.1 collective-permute-start.32
  100.0 8.9 %collective-permute-done.29.refs_4_ = bf16[4,16,4096]{2,1,0:T(8,128)(2,1)S(1)} collective-permute-done((bf16[4,16,4096]{2,1,0:T(8,128)(2,1)S(1)}, bf16[4,16,4096]{2,1,0:T(8,128)(2,1)S(1)}, u32[]{:S(2)}, u32[]{:S(2)}) %collective-permute-start.29) | collective-permute-done | bytes 524320 | tf_op jit(solution)/shard_map/ppermute | solution.py:96
  108.9 1.9 %collective-permute-done.33.refs_8_ = bf16[4,16,4096]{2,1,0:T(8,128)(2,1)S(1)} collective-permute-done((bf16[4,16,4096]{2,1,0:T(8,128)(2,1)S(1)}, bf16[4,16,4096]{2,1,0:T(8,128)(2,1)S(1)}, u32[]{:S(2)}, u32[]{:S(2)}) %collective-permute-start.33) | collective-permute-done | bytes 524320 | tf_op jit(solution)/shard_map/ppermute | solution.py:96
  110.8 4.8 %shard_map.122 = (bf16[4,2,36,512]{3,2,1,0:T(8,128)(2,1)S(1)}, bf16[4,2,36,512]{3,2,1,0:T(8,128)(2,1)S(1)}, bf16[2,36,512]{2,1,0:T(8,128)(2,1)S(1)}) custom-call(bf16[8,144,512]{2,1,0:T(8,128)(2,1)S(1)} %shard_map.121.refs_0_, bf16[4,16,4096]{2,1,0:T(8,128)(2,1)S(1)} %get-tuple-element.57.refs_1_, bf16[4,16,4096]{2,1,0:T(8,128)(2,1)S(1)} %collective-permute-done.27.refs_2_, ...), custom_call_target="tpu_custom_call" | custom-call | flops 4831838208 | bytes 8000000 | tf_op jit(solution)/shard_map/pallas_call | solution.py:354
  115.6 0.3 collective-permute-start.34
  116.0 2.1 %collective-permute-start.36 = (bf16[4,2,36,512]{3,2,1,0:T(8,128)(2,1)S(1)}, bf16[4,2,36,512]{3,2,1,0:T(8,128)(2,1)S(1)}, u32[]{:S(2)}, u32[]{:S(2)}) collective-permute-start(bf16[4,2,36,512]{3,2,1,0:T(8,128)(2,1)S(1)} %get-tuple-element.67), channel_id=1, source_target_pairs={{30,0},{31,1},{0,2},{1,3},{2,4},{3,5},{4,6},{5,7},{6,8},{7,9},{8,1... | collective-permute-start | bytes 884744 | tf_op jit(solution)/shard_map/ppermute | solution.py:381
  118.1 4.8 %shard_map.123 = (bf16[4,2,36,512]{3,2,1,0:T(8,128)(2,1)S(1)}, bf16[4,2,36,512]{3,2,1,0:T(8,128)(2,1)S(1)}, bf16[2,36,512]{2,1,0:T(8,128)(2,1)S(1)}) custom-call(bf16[8,144,512]{2,1,0:T(8,128)(2,1)S(1)} %shard_map.121.refs_0_, bf16[4,16,4096]{2,1,0:T(8,128)(2,1)S(1)} %get-tuple-element.57.refs_1_, bf16[4,16,4096]{2,1,0:T(8,128)(2,1)S(1)} %collective-permute-done.27.refs_2_, ...), custom_call_target="tpu_custom_call" | custom-call | flops 4831838208 | bytes 8000000 | tf_op jit(solution)/shard_map/pallas_call | solution.py:354
  122.9 0.9 collective-permute-done.34
  123.8 0.3 collective-permute-start.35
  124.1 1.1 collective-permute-done.35
  125.2 5.9 %collective-permute-done.36 = bf16[4,2,36,512]{3,2,1,0:T(8,128)(2,1)S(1)} collective-permute-done((bf16[4,2,36,512]{3,2,1,0:T(8,128)(2,1)S(1)}, bf16[4,2,36,512]{3,2,1,0:T(8,128)(2,1)S(1)}, u32[]{:S(2)}, u32[]{:S(2)}) %collective-permute-start.36) | collective-permute-done | bytes 294944 | tf_op jit(solution)/shard_map/ppermute | solution.py:381
  131.1 0.1 reshape.56
  131.2 0.2 copy.21
  131.4 0.1 reshape.53
  131.6 0.2 copy.20
  131.8 0.1 reshape.50
  132.0 0.2 copy.19
  132.3 0.1 reshape.47
  132.4 0.2 copy.18
  132.7 2.9 %maximum_maximum_fusion = bf16[24,24,2,512]{3,2,1,0:T(2,128)(2,1)} fusion(bf16[6,21,2,512]{3,2,1,0:T(2,128)(2,1)S(1)} %bitcast.33, bf16[6,21,2,512]{3,2,1,0:T(2,128)(2,1)S(1)} %bitcast.34, bf16[6,21,2,512]{3,2,1,0:T(2,128)(2,1)S(1)} %bitcast.35, bf16[6,3,2,512]{3,2,1,0:T(2,128)(2,1)S(1)} %reshape_transpose_reshape_broadcast_in_dim_squeeze.15, ...), kind=kLoop, calls=%fused_computation | loop fusion | flops 4128768 | bytes 2359296 | tf_op jit(solution)/shard_map/concatenate | solution.py:406
  (71 shorter events, 0.7 us)
Async XLA Ops:
  0.0 0.9 copy-start.2
  0.9 0.8 copy-start.3
  1.8 8.6 %collective-permute-start = (bf16[1,16,2048]{2,1,0:T(8,128)(2,1)S(1)}, bf16[1,16,2048]{2,1,0:T(8,128)(2,1)S(1)}, u32[]{:S(2)}, u32[]{:S(2)}) collective-permute-start(bf16[1,16,2048]{2,1,0:T(8,128)(2,1)S(1)} %shard_map.109.refs_0_), channel_id=1, source_target_pairs={{0,16},{1,17},{2,18},{3,19},{4,20},{5,21},{6,22},{7,23},{8,24},{9,... | collective-permute-start | bytes 196616 | tf_op jit(solution)/shard_map/ppermute | solution.py:96
  5.8 0.9 copy-start
  6.8 0.9 copy-start.1
  7.7 1.3 copy-start.6
  7.7 8.8 %collective-permute-start.2 = (bf16[1,16,4096]{2,1,0:T(8,128)(2,1)S(1)}, bf16[1,16,4096]{2,1,0:T(8,128)(2,1)S(1)}, u32[]{:S(2)}, u32[]{:S(2)}) collective-permute-start(bf16[1,16,4096]{2,1,0:T(8,128)(2,1)S(1)} %get-tuple-element.39.refs_0_), channel_id=1, source_target_pairs={{0,16},{1,17},{2,18},{3,19},{4,20},{5,21},{6,22},{7,23},{8,24},{9,... | collective-permute-start | bytes 393224 | tf_op jit(solution)/shard_map/ppermute | solution.py:96
  10.3 13.0 %copy-start.7 = (f32[16,512]{1,0:T(8,128)S(1)}, f32[16,512]{1,0:T(8,128)}, u32[]{:S(2)}) copy-start(f32[16,512]{1,0:T(8,128)} %constant.8.clone) | copy-start | bytes 98308
  10.3 13.0 %copy-start.9 = (f32[2,16]{1,0:T(2,128)S(1)}, f32[2,16]{1,0:T(2,128)}, u32[]{:S(2)}) copy-start(f32[2,16]{1,0:T(2,128)} %param.17) | copy-start | bytes 388
  10.3 21.0 %copy-start.8 = (f32[2,2,512]{2,1,0:T(2,128)S(1)}, f32[2,2,512]{2,1,0:T(2,128)}, u32[]{:S(2)}) copy-start(f32[2,2,512]{2,1,0:T(2,128)} %param.16) | copy-start | bytes 24580
  10.4 7.5 %collective-permute-start.1 = (bf16[2,16,2048]{2,1,0:T(8,128)(2,1)S(1)}, bf16[2,16,2048]{2,1,0:T(8,128)(2,1)S(1)}, u32[]{:S(2)}, u32[]{:S(2)}) collective-permute-start(bf16[2,16,2048]{2,1,0:T(8,128)(2,1)S(1)} %shard_map.110.refs_0_), channel_id=1, source_target_pairs={{0,8},{1,9},{2,10},{3,11},{4,12},{5,13},{6,14},{7,15},{8,0},{9,1},... | collective-permute-start | bytes 393224 | tf_op jit(solution)/shard_map/ppermute | solution.py:96
  17.9 19.3 %copy-start.4 = (bf16[640,256]{1,0:T(8,128)(2,1)S(1)}, bf16[640,256]{1,0:T(8,128)(2,1)}, u32[]{:S(2)}) copy-start(bf16[640,256]{1,0:T(8,128)(2,1)} %constant.9.clone.refs_11_) | copy-start | bytes 983044
  17.9 11.7 %collective-permute-start.3 = (bf16[4,16,2048]{2,1,0:T(8,128)(2,1)S(1)}, bf16[4,16,2048]{2,1,0:T(8,128)(2,1)S(1)}, u32[]{:S(2)}, u32[]{:S(2)}) collective-permute-start(bf16[4,16,2048]{2,1,0:T(8,128)(2,1)S(1)} %shard_map.113.refs_1_), channel_id=1, source_target_pairs={{0,2},{1,5},{2,0},{3,7},{4,6},{5,1},{6,4},{7,3},{8,10},{9,13},{10,... | collective-permute-start | bytes 786440 | tf_op jit(solution)/shard_map/ppermute | solution.py:96
  19.5 11.3 %collective-permute-start.4 = (bf16[4,16,2048]{2,1,0:T(8,128)(2,1)S(1)}, bf16[4,16,2048]{2,1,0:T(8,128)(2,1)S(1)}, u32[]{:S(2)}, u32[]{:S(2)}) collective-permute-start(bf16[4,16,2048]{2,1,0:T(8,128)(2,1)S(1)} %shard_map.113.refs_1_), channel_id=1, source_target_pairs={{0,4},{1,3},{2,6},{3,1},{4,0},{5,7},{6,2},{7,5},{8,12},{9,11},{10,... | collective-permute-start | bytes 786440 | tf_op jit(solution)/shard_map/ppermute | solution.py:96
  21.0 9.8 %collective-permute-start.5 = (bf16[4,16,2048]{2,1,0:T(8,128)(2,1)S(1)}, bf16[4,16,2048]{2,1,0:T(8,128)(2,1)S(1)}, u32[]{:S(2)}, u32[]{:S(2)}) collective-permute-start(bf16[4,16,2048]{2,1,0:T(8,128)(2,1)S(1)} %shard_map.113.refs_1_), channel_id=1, source_target_pairs={{0,6},{1,7},{2,4},{3,5},{4,2},{5,3},{6,0},{7,1},{8,14},{9,15},{10,... | collective-permute-start | bytes 786440 | tf_op jit(solution)/shard_map/ppermute | solution.py:96
  21.5 8.1 %collective-permute-start.11 = (bf16[1,16,6144]{2,1,0:T(8,128)(2,1)S(1)}, bf16[1,16,6144]{2,1,0:T(8,128)(2,1)S(1)}, u32[]{:S(2)}, u32[]{:S(2)}) collective-permute-start(bf16[1,16,6144]{2,1,0:T(8,128)(2,1)S(1)} %get-tuple-element.40.refs_0_), channel_id=1, source_target_pairs={{0,16},{1,17},{2,18},{3,19},{4,20},{5,21},{6,22},{7,23},{8,24},{9,... | collective-permute-start | bytes 589832 | tf_op jit(solution)/shard_map/ppermute | solution.py:96
  23.4 8.5 %collective-permute-start.10 = (bf16[2,16,4096]{2,1,0:T(8,128)(2,1)S(1)}, bf16[2,16,4096]{2,1,0:T(8,128)(2,1)S(1)}, u32[]{:S(2)}, u32[]{:S(2)}) collective-permute-start(bf16[2,16,4096]{2,1,0:T(8,128)(2,1)S(1)} %shard_map.112.refs_2_.refs_0_), channel_id=1, source_target_pairs={{0,8},{1,9},{2,10},{3,11},{4,12},{5,13},{6,14},{7,15},{8,0},{9,1},... | collective-permute-start | bytes 786440 | tf_op jit(solution)/shard_map/ppermute | solution.py:96
  29.6 3.9 %collective-permute-start.6 = (bf16[4,16,2048]{2,1,0:T(8,128)(2,1)S(1)}, bf16[4,16,2048]{2,1,0:T(8,128)(2,1)S(1)}, u32[]{:S(2)}, u32[]{:S(2)}) collective-permute-start(bf16[4,16,2048]{2,1,0:T(8,128)(2,1)S(1)} %shard_map.113.refs_1_), channel_id=1, source_target_pairs={{0,1},{1,0},{2,3},{3,2},{4,5},{5,4},{6,7},{7,6},{8,9},{9,8},{10,11... | collective-permute-start | bytes 786440 | tf_op jit(solution)/shard_map/ppermute | solution.py:96
  29.6 5.4 %collective-permute-start.7 = (bf16[4,16,2048]{2,1,0:T(8,128)(2,1)S(1)}, bf16[4,16,2048]{2,1,0:T(8,128)(2,1)S(1)}, u32[]{:S(2)}, u32[]{:S(2)}) collective-permute-start(bf16[4,16,2048]{2,1,0:T(8,128)(2,1)S(1)} %collective-permute-done.3.refs_2_), channel_id=1, source_target_pairs={{0,1},{1,0},{2,3},{3,2},{4,5},{5,4},{6,7},{7,6},{8,9},{9,8},{10,11... | collective-permute-start | bytes 786440 | tf_op jit(solution)/shard_map/ppermute | solution.py:96
  30.8 4.7 %collective-permute-start.8 = (bf16[4,16,2048]{2,1,0:T(8,128)(2,1)S(1)}, bf16[4,16,2048]{2,1,0:T(8,128)(2,1)S(1)}, u32[]{:S(2)}, u32[]{:S(2)}) collective-permute-start(bf16[4,16,2048]{2,1,0:T(8,128)(2,1)S(1)} %collective-permute-done.4.refs_3_), channel_id=1, source_target_pairs={{0,1},{1,0},{2,3},{3,2},{4,5},{5,4},{6,7},{7,6},{8,9},{9,8},{10,11... | collective-permute-start | bytes 786440 | tf_op jit(solution)/shard_map/ppermute | solution.py:96
  30.8 4.7 %collective-permute-start.9 = (bf16[4,16,2048]{2,1,0:T(8,128)(2,1)S(1)}, bf16[4,16,2048]{2,1,0:T(8,128)(2,1)S(1)}, u32[]{:S(2)}, u32[]{:S(2)}) collective-permute-start(bf16[4,16,2048]{2,1,0:T(8,128)(2,1)S(1)} %collective-permute-done.5.refs_4_), channel_id=1, source_target_pairs={{0,1},{1,0},{2,3},{3,2},{4,5},{5,4},{6,7},{7,6},{8,9},{9,8},{10,11... | collective-permute-start | bytes 786440 | tf_op jit(solution)/shard_map/ppermute | solution.py:96
  31.9 18.7 %collective-permute-start.12 = (bf16[4,16,4096]{2,1,0:T(8,128)(2,1)S(1)}, bf16[4,16,4096]{2,1,0:T(8,128)(2,1)S(1)}, u32[]{:S(2)}, u32[]{:S(2)}) collective-permute-start(bf16[4,16,4096]{2,1,0:T(8,128)(2,1)S(1)} %shard_map.115.refs_12_.refs_1_), channel_id=1, source_target_pairs={{0,2},{1,5},{2,0},{3,7},{4,6},{5,1},{6,4},{7,3},{8,10},{9,13},{10,... | collective-permute-start | bytes 1572872 | tf_op jit(solution)/shard_map/ppermute | solution.py:96
  33.5 17.4 %collective-permute-start.13 = (bf16[4,16,4096]{2,1,0:T(8,128)(2,1)S(1)}, bf16[4,16,4096]{2,1,0:T(8,128)(2,1)S(1)}, u32[]{:S(2)}, u32[]{:S(2)}) collective-permute-start(bf16[4,16,4096]{2,1,0:T(8,128)(2,1)S(1)} %shard_map.115.refs_12_.refs_1_), channel_id=1, source_target_pairs={{0,4},{1,3},{2,6},{3,1},{4,0},{5,7},{6,2},{7,5},{8,12},{9,11},{10,... | collective-permute-start | bytes 1572872 | tf_op jit(solution)/shard_map/ppermute | solution.py:96
  35.0 23.1 %collective-permute-start.14 = (bf16[4,16,4096]{2,1,0:T(8,128)(2,1)S(1)}, bf16[4,16,4096]{2,1,0:T(8,128)(2,1)S(1)}, u32[]{:S(2)}, u32[]{:S(2)}) collective-permute-start(bf16[4,16,4096]{2,1,0:T(8,128)(2,1)S(1)} %shard_map.115.refs_12_.refs_1_), channel_id=1, source_target_pairs={{0,6},{1,7},{2,4},{3,5},{4,2},{5,3},{6,0},{7,1},{8,14},{9,15},{10,... | collective-permute-start | bytes 1572872 | tf_op jit(solution)/shard_map/ppermute | solution.py:96
  35.5 23.6 %collective-permute-start.15 = (bf16[4,16,4096]{2,1,0:T(8,128)(2,1)S(1)}, bf16[4,16,4096]{2,1,0:T(8,128)(2,1)S(1)}, u32[]{:S(2)}, u32[]{:S(2)}) collective-permute-start(bf16[4,16,4096]{2,1,0:T(8,128)(2,1)S(1)} %shard_map.115.refs_12_.refs_1_), channel_id=1, source_target_pairs={{0,1},{1,0},{2,3},{3,2},{4,5},{5,4},{6,7},{7,6},{8,9},{9,8},{10,11... | collective-permute-start | bytes 1572872 | tf_op jit(solution)/shard_map/ppermute | solution.py:96
  35.5 15.1 %collective-permute-start.16 = (bf16[2,16,6144]{2,1,0:T(8,128)(2,1)S(1)}, bf16[2,16,6144]{2,1,0:T(8,128)(2,1)S(1)}, u32[]{:S(2)}, u32[]{:S(2)}) collective-permute-start(bf16[2,16,6144]{2,1,0:T(8,128)(2,1)S(1)} %shard_map.114.refs_2_.refs_0_), channel_id=1, source_target_pairs={{0,8},{1,9},{2,10},{3,11},{4,12},{5,13},{6,14},{7,15},{8,0},{9,1},... | collective-permute-start | bytes 1179656 | tf_op jit(solution)/shard_map/ppermute | solution.py:96
  50.6 10.0 %collective-permute-start.17 = (bf16[4,16,4096]{2,1,0:T(8,128)(2,1)S(1)}, bf16[4,16,4096]{2,1,0:T(8,128)(2,1)S(1)}, u32[]{:S(2)}, u32[]{:S(2)}) collective-permute-start(bf16[4,16,4096]{2,1,0:T(8,128)(2,1)S(1)} %collective-permute-done.12.refs_2_), channel_id=1, source_target_pairs={{0,1},{1,0},{2,3},{3,2},{4,5},{5,4},{6,7},{7,6},{8,9},{9,8},{10,11... | collective-permute-start | bytes 1572872 | tf_op jit(solution)/shard_map/ppermute | solution.py:96
  50.9 10.9 %collective-permute-start.18 = (bf16[4,16,4096]{2,1,0:T(8,128)(2,1)S(1)}, bf16[4,16,4096]{2,1,0:T(8,128)(2,1)S(1)}, u32[]{:S(2)}, u32[]{:S(2)}) collective-permute-start(bf16[4,16,4096]{2,1,0:T(8,128)(2,1)S(1)} %collective-permute-done.13.refs_3_), channel_id=1, source_target_pairs={{0,1},{1,0},{2,3},{3,2},{4,5},{5,4},{6,7},{7,6},{8,9},{9,8},{10,11... | collective-permute-start | bytes 1572872 | tf_op jit(solution)/shard_map/ppermute | solution.py:96
  58.1 3.6 %collective-permute-start.19 = (bf16[4,16,4096]{2,1,0:T(8,128)(2,1)S(1)}, bf16[4,16,4096]{2,1,0:T(8,128)(2,1)S(1)}, u32[]{:S(2)}, u32[]{:S(2)}) collective-permute-start(bf16[4,16,4096]{2,1,0:T(8,128)(2,1)S(1)} %collective-permute-done.14.refs_4_), channel_id=1, source_target_pairs={{0,1},{1,0},{2,3},{3,2},{4,5},{5,4},{6,7},{7,6},{8,9},{9,8},{10,11... | collective-permute-start | bytes 1572872 | tf_op jit(solution)/shard_map/ppermute | solution.py:96
  58.2 18.3 %collective-permute-start.23 = (bf16[4,16,2048]{2,1,0:T(8,128)(2,1)S(1)}, bf16[4,16,2048]{2,1,0:T(8,128)(2,1)S(1)}, u32[]{:S(2)}, u32[]{:S(2)}) collective-permute-start(bf16[4,16,2048]{2,1,0:T(8,128)(2,1)S(1)} %get-tuple-element.45.refs_10_.refs_0_), channel_id=1, source_target_pairs={{0,2},{1,5},{2,0},{3,7},{4,6},{5,1},{6,4},{7,3},{8,10},{9,13},{10,... | collective-permute-start | bytes 786440 | tf_op jit(solution)/shard_map/ppermute | solution.py:96
  59.1 22.7 %collective-permute-start.24 = (bf16[4,16,2048]{2,1,0:T(8,128)(2,1)S(1)}, bf16[4,16,2048]{2,1,0:T(8,128)(2,1)S(1)}, u32[]{:S(2)}, u32[]{:S(2)}) collective-permute-start(bf16[4,16,2048]{2,1,0:T(8,128)(2,1)S(1)} %get-tuple-element.45.refs_10_.refs_0_), channel_id=1, source_target_pairs={{0,4},{1,3},{2,6},{3,1},{4,0},{5,7},{6,2},{7,5},{8,12},{9,11},{10,... | collective-permute-start | bytes 786440 | tf_op jit(solution)/shard_map/ppermute | solution.py:96
  60.6 21.2 %collective-permute-start.25 = (bf16[4,16,2048]{2,1,0:T(8,128)(2,1)S(1)}, bf16[4,16,2048]{2,1,0:T(8,128)(2,1)S(1)}, u32[]{:S(2)}, u32[]{:S(2)}) collective-permute-start(bf16[4,16,2048]{2,1,0:T(8,128)(2,1)S(1)} %get-tuple-element.45.refs_10_.refs_0_), channel_id=1, source_target_pairs={{0,6},{1,7},{2,4},{3,5},{4,2},{5,3},{6,0},{7,1},{8,14},{9,15},{10,... | collective-permute-start | bytes 786440 | tf_op jit(solution)/shard_map/ppermute | solution.py:96
  66.6 15.2 %collective-permute-start.20 = (bf16[4,2,36,512]{3,2,1,0:T(8,128)(2,1)S(1)}, bf16[4,2,36,512]{3,2,1,0:T(8,128)(2,1)S(1)}, u32[]{:S(2)}, u32[]{:S(2)}) collective-permute-start(bf16[4,2,36,512]{3,2,1,0:T(8,128)(2,1)S(1)} %get-tuple-element.46.refs_0_), channel_id=1, source_target_pairs={{2,0},{3,1},{4,2},{5,3},{6,4},{7,5},{8,6},{9,7},{10,8},{11,9},{12,... | collective-permute-start | bytes 884744 | tf_op jit(solution)/shard_map/ppermute | solution.py:381
  71.7 10.1 %collective-permute-start.21 = (bf16[2,36,512]{2,1,0:T(8,128)(2,1)S(1)}, bf16[2,36,512]{2,1,0:T(8,128)(2,1)S(1)}, u32[]{:S(2)}, u32[]{:S(2)}) collective-permute-start(bf16[2,36,512]{2,1,0:T(8,128)(2,1)S(1)} %get-tuple-element.48.refs_10_), channel_id=1, source_target_pairs={{3,0},{2,1},{5,2},{4,3},{7,4},{6,5},{9,6},{8,7},{11,8},{10,9},{13,... | collective-permute-start | bytes 221192 | tf_op jit(solution)/shard_map/ppermute | solution.py:381
  81.8 4.3 %copy-start.5 = (f32[144,256]{1,0:T(8,128)S(1)}, f32[144,256]{1,0:T(8,128)}, u32[]{:S(2)}) copy-start(f32[144,256]{1,0:T(8,128)} %constant.10.clone.refs_12_) | copy-start | bytes 442372
  81.9 4.2 %collective-permute-start.26 = (bf16[16,16,2048]{2,1,0:T(8,128)(2,1)S(1)}, bf16[16,16,2048]{2,1,0:T(8,128)(2,1)S(1)}, u32[]{:S(2)}, u32[]{:S(2)}) collective-permute-start(bf16[16,16,2048]{2,1,0:T(8,128)(2,1)S(1)} %shard_map.120.refs_7_), channel_id=1, source_target_pairs={{0,1},{1,0},{2,3},{3,2},{4,5},{5,4},{6,7},{7,6},{8,9},{9,8},{10,11... | collective-permute-start | bytes 3145736 | tf_op jit(solution)/shard_map/ppermute | solution.py:96
  82.0 4.0 %collective-permute-start.22 = (bf16[4,36,512]{2,1,0:T(8,128)(2,1)S(1)}, bf16[4,36,512]{2,1,0:T(8,128)(2,1)S(1)}, u32[]{:S(2)}, u32[]{:S(2)}) collective-permute-start(bf16[4,36,512]{2,1,0:T(8,128)(2,1)S(1)} %pad_maximum_fusion), channel_id=1, source_target_pairs={{1,0},{0,1},{3,2},{2,3},{5,4},{4,5},{7,6},{6,7},{9,8},{8,9},{11,10... | collective-permute-start | bytes 442376 | tf_op jit(solution)/shard_map/ppermute | solution.py:381
  82.6 16.8 %collective-permute-start.27 = (bf16[4,16,4096]{2,1,0:T(8,128)(2,1)S(1)}, bf16[4,16,4096]{2,1,0:T(8,128)(2,1)S(1)}, u32[]{:S(2)}, u32[]{:S(2)}) collective-permute-start(bf16[4,16,4096]{2,1,0:T(8,128)(2,1)S(1)} %get-tuple-element.57.refs_1_), channel_id=1, source_target_pairs={{0,2},{1,5},{2,0},{3,7},{4,6},{5,1},{6,4},{7,3},{8,10},{9,13},{10,... | collective-permute-start | bytes 1572872 | tf_op jit(solution)/shard_map/ppermute | solution.py:96
  84.0 16.0 %collective-permute-start.28 = (bf16[4,16,4096]{2,1,0:T(8,128)(2,1)S(1)}, bf16[4,16,4096]{2,1,0:T(8,128)(2,1)S(1)}, u32[]{:S(2)}, u32[]{:S(2)}) collective-permute-start(bf16[4,16,4096]{2,1,0:T(8,128)(2,1)S(1)} %get-tuple-element.57.refs_1_), channel_id=1, source_target_pairs={{0,4},{1,3},{2,6},{3,1},{4,0},{5,7},{6,2},{7,5},{8,12},{9,11},{10,... | collective-permute-start | bytes 1572872 | tf_op jit(solution)/shard_map/ppermute | solution.py:96
  84.3 24.6 %collective-permute-start.29 = (bf16[4,16,4096]{2,1,0:T(8,128)(2,1)S(1)}, bf16[4,16,4096]{2,1,0:T(8,128)(2,1)S(1)}, u32[]{:S(2)}, u32[]{:S(2)}) collective-permute-start(bf16[4,16,4096]{2,1,0:T(8,128)(2,1)S(1)} %get-tuple-element.57.refs_1_), channel_id=1, source_target_pairs={{0,6},{1,7},{2,4},{3,5},{4,2},{5,3},{6,0},{7,1},{8,14},{9,15},{10,... | collective-permute-start | bytes 1572872 | tf_op jit(solution)/shard_map/ppermute | solution.py:96
  86.1 22.8 %collective-permute-start.30 = (bf16[4,16,4096]{2,1,0:T(8,128)(2,1)S(1)}, bf16[4,16,4096]{2,1,0:T(8,128)(2,1)S(1)}, u32[]{:S(2)}, u32[]{:S(2)}) collective-permute-start(bf16[4,16,4096]{2,1,0:T(8,128)(2,1)S(1)} %get-tuple-element.57.refs_1_), channel_id=1, source_target_pairs={{0,1},{1,0},{2,3},{3,2},{4,5},{5,4},{6,7},{7,6},{8,9},{9,8},{10,11... | collective-permute-start | bytes 1572872 | tf_op jit(solution)/shard_map/ppermute | solution.py:96
  99.4 9.5 %collective-permute-start.31 = (bf16[4,16,4096]{2,1,0:T(8,128)(2,1)S(1)}, bf16[4,16,4096]{2,1,0:T(8,128)(2,1)S(1)}, u32[]{:S(2)}, u32[]{:S(2)}) collective-permute-start(bf16[4,16,4096]{2,1,0:T(8,128)(2,1)S(1)} %collective-permute-done.27.refs_2_), channel_id=1, source_target_pairs={{0,1},{1,0},{2,3},{3,2},{4,5},{5,4},{6,7},{7,6},{8,9},{9,8},{10,11... | collective-permute-start | bytes 1572872 | tf_op jit(solution)/shard_map/ppermute | solution.py:96
  100.0 9.0 %collective-permute-start.32 = (bf16[4,16,4096]{2,1,0:T(8,128)(2,1)S(1)}, bf16[4,16,4096]{2,1,0:T(8,128)(2,1)S(1)}, u32[]{:S(2)}, u32[]{:S(2)}) collective-permute-start(bf16[4,16,4096]{2,1,0:T(8,128)(2,1)S(1)} %collective-permute-done.28.refs_3_), channel_id=1, source_target_pairs={{0,1},{1,0},{2,3},{3,2},{4,5},{5,4},{6,7},{7,6},{8,9},{9,8},{10,11... | collective-permute-start | bytes 1572872 | tf_op jit(solution)/shard_map/ppermute | solution.py:96
  108.9 1.9 %collective-permute-start.33 = (bf16[4,16,4096]{2,1,0:T(8,128)(2,1)S(1)}, bf16[4,16,4096]{2,1,0:T(8,128)(2,1)S(1)}, u32[]{:S(2)}, u32[]{:S(2)}) collective-permute-start(bf16[4,16,4096]{2,1,0:T(8,128)(2,1)S(1)} %collective-permute-done.29.refs_4_), channel_id=1, source_target_pairs={{0,1},{1,0},{2,3},{3,2},{4,5},{5,4},{6,7},{7,6},{8,9},{9,8},{10,11... | collective-permute-start | bytes 1572872 | tf_op jit(solution)/shard_map/ppermute | solution.py:96
  115.6 8.1 %collective-permute-start.34 = (bf16[2,36,512]{2,1,0:T(8,128)(2,1)S(1)}, bf16[2,36,512]{2,1,0:T(8,128)(2,1)S(1)}, u32[]{:S(2)}, u32[]{:S(2)}) collective-permute-start(bf16[2,36,512]{2,1,0:T(8,128)(2,1)S(1)} %get-tuple-element.61.refs_10_), channel_id=1, source_target_pairs={{31,0},{30,1},{1,2},{0,3},{3,4},{2,5},{5,6},{4,7},{7,8},{6,9},{9,1... | collective-permute-start | bytes 221192 | tf_op jit(solution)/shard_map/ppermute | solution.py:381
  116.0 15.1 %collective-permute-start.36 = (bf16[4,2,36,512]{3,2,1,0:T(8,128)(2,1)S(1)}, bf16[4,2,36,512]{3,2,1,0:T(8,128)(2,1)S(1)}, u32[]{:S(2)}, u32[]{:S(2)}) collective-permute-start(bf16[4,2,36,512]{3,2,1,0:T(8,128)(2,1)S(1)} %get-tuple-element.67), channel_id=1, source_target_pairs={{30,0},{31,1},{0,2},{1,3},{2,4},{3,5},{4,6},{5,7},{6,8},{7,9},{8,1... | collective-permute-start | bytes 884744 | tf_op jit(solution)/shard_map/ppermute | solution.py:381
  123.8 1.4 %collective-permute-start.35 = (bf16[4,36,512]{2,1,0:T(8,128)(2,1)S(1)}, bf16[4,36,512]{2,1,0:T(8,128)(2,1)S(1)}, u32[]{:S(2)}, u32[]{:S(2)}) collective-permute-start(bf16[4,36,512]{2,1,0:T(8,128)(2,1)S(1)} %pad_maximum_fusion.1), channel_id=1, source_target_pairs={{1,0},{0,1},{3,2},{2,3},{5,4},{4,5},{7,6},{6,7},{9,8},{8,9},{11,10... | collective-permute-start | bytes 442376 | tf_op jit(solution)/shard_map/ppermute | solution.py:381

commit v10 on v9

--- a/solution.py
+++ b/solution.py
@@ -120,9 +120,8 @@
     return z, 1 - y, 1 - x, c
 
 
-def whole_pieces(column, received, after=None):
-    sent = received if after is None else [tied(part, after) for part in received]
-    return [column] + received + [send(part, swap) for part in [column] + sent]
+def whole_pieces(column, received):
+    return [column] + received + [send(part, swap) for part in [column] + received]
 
 
 def load_pieces(pieces, w_ref, stage_ref, sem):
@@ -141,22 +140,21 @@
     lon, lat = lax.axis_index("lon"), lax.axis_index("lat")
     z, y, x = lon // 4, lon // 2 % 2, lon % 2
     by_x, by_y = y * 2 + 1 - x, (1 - y) * 2 + x
-    joined = len(pieces) == 2
+    parts = len(pieces) // 2
     for index, copy in enumerate(copies):
-        core = lat if index < len(pieces) // 2 else 1 - lat
+        core = lat if index < parts else 1 - lat
         squares = (
             y * 2 + x,
             jnp.where(core == 0, by_x, by_y),
             jnp.where(core == 0, by_y, by_x),
             (1 - y) * 2 + 1 - x,
         )
+        held = squares[index % 4 : index % 4 + 1] if parts == 4 else squares[index % 2 * 2 :][:2]
         copy.wait()
-        for column in range(4) if joined else (index % 4,):
-            for step in range(len(Z_ORDER)):
-                shard = (z ^ Z_ORDER[step]) * 4 + squares[column]
-                row = pl.multiple_of((shard * 2 + core) * half, 16)
-                place = column * len(Z_ORDER) + step if joined else step
-                w_ref[pl.ds(row, half), :] = stage_ref[index, place]
+        for step in range(pieces[0].shape[0]):
+            shard = (z ^ Z_ORDER[step // len(held)]) * 4 + held[step % len(held)]
+            row = pl.multiple_of((shard * 2 + core) * half, 16)
+            w_ref[pl.ds(row, half), :] = stage_ref[index, step]
 
 
 def load_scratch(pieces, rows, width):
@@ -285,19 +283,21 @@
     return np.concatenate(halves, 1).astype(np.float32)
 
 
-def attend(sources, pieces, gain, sharp, row_windows, after=(), held=2):
+def attend(sources, columns, pieces, gain, sharp, row_windows, after=(), held=2):
     shifted = len(sources) > 1
     features = sources[0].shape[-1]
-    count = 2 * row_windows
+    count = len(columns) * row_windows
+    skipped = columns[0] * row_windows // held
     whole = lambda shape: pl.BlockSpec(shape, lambda i: (0,) * len(shape))
     block = pl.BlockSpec((held, CELLS, features), lambda i: (i, 0, 0))
+    x_block = pl.BlockSpec((held, CELLS, features), lambda i: (i + skipped, 0, 0))
     ones = jnp.asarray(head_columns(), jnp.bfloat16)
     extra = (jnp.asarray(allowed_pairs()),) if shifted else ()
     return pl.pallas_call(
         functools.partial(attend_kernel, shifted, row_windows, len(pieces)),
         grid=(count // held,),
         out_shape=jax.ShapeDtypeStruct((count, CELLS, features), jnp.bfloat16),
-        in_specs=([whole(source.shape) for source in sources] if shifted else [block])
+        in_specs=([whole(source.shape) for source in sources] if shifted else [x_block])
         + [ANY] * len(pieces)
         + [whole((1, features))] * 2
         + [whole(ones.shape)]
@@ -346,9 +346,8 @@
                         edge_ref[side] = quarter
 
 
-def feed(windows, column, pieces, gain, hidden_size, edge, after=(), held=2):
-    count, cells, features = windows.shape
-    count = count // 2
+def feed(windows, column, count, pieces, gain, hidden_size, edge, after=(), held=2):
+    _, cells, features = windows.shape
     block = pl.BlockSpec((held, cells, features), lambda i: (i + column * count // held, 0, 0))
     side = pl.BlockSpec((held, 2, QUARTER, features), lambda i: (i, 0, 0, 0))
     return pl.pallas_call(
@@ -417,13 +416,13 @@
     sharp = jnp.sum(sharp, 1)
     windows = to_windows(tokens)
 
-    def attention(block, sources, pieces, after=()):
-        return attend(
-            sources, pieces, norm_gain[block, :1], sharp[block : block + 1], row_windows, after
-        )
+    def attention(block, sources, columns, pieces, after=()):
+        gain, scale = norm_gain[block, :1], sharp[block : block + 1]
+        return attend(sources, columns, pieces, gain, scale, row_windows, after)
 
     def forward(block, middle, column, pieces, edge, after=()):
-        return feed(middle, column, pieces, norm_gain[block, 1:], hidden_size, edge, after)
+        gain = norm_gain[block, 1:]
+        return feed(middle, column, row_windows, pieces, gain, hidden_size, edge, after)
 
     low_edge, high_edge = (0, 0), (row_windows - 1, 1)
     if relay:
@@ -434,24 +433,25 @@
         widths = tuple(sum(weight.shape[2] for weight in pair) for pair in (weights[:2], weights[2:]))
         (pair,) = join([[own, across_z(own, 2)]], (), (windows,))
         (feed_pair,) = join([[feed_own, across_z(feed_own, 2)]])
-        (column,) = join([[pair, across_z(pair, 1)]], (), (feed_pair,))
+        (last_pair,) = join([[last_own, send(last_own, beside)]])
+        (column,) = join([[pair, across_z(pair, 1)]], (), (feed_pair, last_pair))
         pieces = whole_pieces(column, [send(column, way) for way in (beside, across, corner)])
-        (last_pair,) = join([[last_own, across_z(last_own, 2)]])
-        (feed_column,) = join([[feed_pair, across_z(feed_pair, 1)]], (), (last_pair,))
-        received = [send(feed_column, way) for way in (beside, across, corner)]
-        last_pair = tied(last_pair, feed_column)
-        last_other = across_z(last_pair, 1)
-        middle = attention(0, [windows], pieces, (feed_column,))
-        feed_pieces = whole_pieces(feed_column, received, (middle, last_other))
-        column, last_column = join([[last_pair, last_other]], (), (middle,), widths)
-        received = [send(column, way) for way in (beside, across, corner)]
+        (last_four,) = join([[last_pair, across_z(last_pair, 2)]])
+        (feed_column,) = join([[feed_pair, across_z(feed_pair, 1)]])
+        received = [send(feed_column, way) for way in (beside, across)]
+        last_other = across_z(last_four, 1)
+        middle = attention(0, [windows], (0, 1), pieces, (feed_column, last_four))
+        received.append(send(tied(received[0], middle), across))
+        sent = [feed_column] + tied(received[:2], (middle, last_other)) + [tied(received[2], middle)]
+        feed_pieces = [feed_column] + received + [send(part, swap) for part in sent]
+        column, last_column = join([[last_four, last_other]], (), (middle,), widths)
+        received = send(column, across)
         left_0, right_0, low_0 = forward(0, middle, 0, feed_pieces, low_edge, (column,))
-        last_column = tied(last_column, low_0)
-        last_received = [send(last_column, way) for way in (beside, across, corner)]
         ahead, ahead_low = shift_from(left_0, 1, 0), shift_from(low_0, 1, 1)
-        left_1, right_1, low_1 = forward(0, middle, 1, feed_pieces, low_edge, (low_0,))
-        (joined,) = join([[column] + [tied(part, (low_1, ahead, ahead_low)) for part in received]])
-        pieces = [joined, send(joined, swap)]
+        left_1, right_1, low_1 = forward(0, middle, 1, feed_pieces, low_edge, (low_0, received))
+        pieces = [column, received]
+        pieces += [send(column, swap), send(tied(received, low_1), swap)]
+        last_received = send(tied(last_column, received), across)
     else:
         gathered = []
         for block in range(2):
@@ -459,15 +459,16 @@
                 chunk = jnp.concatenate([weight[block] for weight in pair], 1)
                 gathered.append([lax.all_gather(chunk, "lon", axis=0, tiled=True)])
         first_pieces, feed_pieces, pieces, last_pieces = gathered
-        middle = attention(0, [windows], first_pieces)
+        middle = attention(0, [windows], (0, 1), first_pieces)
         left_0, right_0, low_0 = forward(0, middle, 0, feed_pieces, low_edge)
         left_1, right_1, low_1 = forward(0, middle, 1, feed_pieces, low_edge)
         ahead, ahead_low = shift_from(left_0, 1, 0), shift_from(low_0, 1, 1)
-    below = shift_from(tied(jnp.concatenate([low_0, low_1], 0), ahead_low), 0, 1)
+    below = shift_from(tied(jnp.concatenate([low_0, low_1], 0), (ahead, ahead_low)), 0, 1)
     sources = [left_0, right_0, left_1, right_1, ahead, below, ahead_low]
-    middle = attention(1, sources, pieces)
+    middle = attention(1, sources, (0, 1), pieces)
     if relay:
-        last_pieces = whole_pieces(last_column, last_received, middle)
+        last_pieces = [last_column, last_received]
+        last_pieces += [send(last_column, swap), send(tied(last_received, middle), swap)]
     left_1, right_1, high_1 = forward(1, middle, 1, last_pieces, high_edge)
     behind = shift_from(right_1, -1, 0)
     behind_high = shift_from(high_1, -1, -1)

time: 136 us -> 139 us (1.022)
  waiting for transfers between devices: 40.5 us -> 51.7 us
  starting transfers between devices: 37.7 us -> 30.7 us
    ppermute x31 -> x27, waiting for transfers between devices: 27.4 us -> 35.9 us  [send(): return lax.ppermute(block, ('lon', 'lat'), pairs)]
    ppermute x31 -> x27, starting transfers between devices: 29.3 us -> 22.6 us  [send(): return lax.ppermute(block, ('lon', 'lat'), pairs)]
    ppermute x6, waiting for transfers between devices: 13.1 us -> 15.8 us  [shift_from(): return lax.ppermute(block, ('lon', 'lat'), pairs)]
  transfers between devices with their start and end apart: 37 -> 33, of which waited for: 12 -> 15; matrix products, arithmetic and copies ran while one was open for 1% -> 1% of each run, Pallas kernels for 30% -> 30%
where the time goes in v10:
time: 139 us
  waiting for transfers between devices  51.7 us (37%)
  Pallas kernels  46.2 us (33%)
  starting transfers between devices  30.7 us (22%)
  local copies, waits for them, and re-layouts  6.51 us (5%)
  other arithmetic  3.03 us (2%)
    ppermute x27, waiting for transfers between devices, send(): return lax.ppermute(block, ('lon', 'lat'), pairs)  35.9 us
    pallas_call x2, Pallas kernels, attend(): pl.pallas_call(functools.partial(attend_kernel, shifted, row_windows, len...  26.7 us
    ppermute x27, starting transfers between devices, send(): return lax.ppermute(block, ('lon', 'lat'), pairs)  22.6 us
    pallas_call x4, Pallas kernels, feed(): pl.pallas_call(functools.partial(feed_kernel, len(pieces), hidden_size, 5...  19.2 us
    ppermute x6, waiting for transfers between devices, shift_from(): return lax.ppermute(block, ('lon', 'lat'), pairs)  15.8 us
    ppermute x6, starting transfers between devices, shift_from(): return lax.ppermute(block, ('lon', 'lat'), pairs)  8.05 us
    unnamed x20, local copies, waits for them, and re-layouts  3.7 us
    concatenate x1, other arithmetic, back_in_place(): return jnp.concatenate([first, jnp.concatenate([tops, own], 1)], 0)  2.9 us
  transfers between devices with their start and end apart: 33, of which 15 were waited for; matrix products, arithmetic and copies ran while one was open for 1% of the time, Pallas kernels for 30%

profile of v10, /device:TPU:0, one launch (start us, length us, event | category | flops | bytes accessed | tf_op | source)
XLA Modules:
  0.0 138.5 jit_solution(10437526053377637830)
XLA Ops:
  0.0 0.9 copy-done.2
  0.9 0.8 copy-done.3
  1.8 4.0 %collective-permute-start = (bf16[1,16,2048]{2,1,0:T(8,128)(2,1)S(1)}, bf16[1,16,2048]{2,1,0:T(8,128)(2,1)S(1)}, u32[]{:S(2)}, u32[]{:S(2)}) collective-permute-start(bf16[1,16,2048]{2,1,0:T(8,128)(2,1)S(1)} %shard_map.109.refs_0_), channel_id=1, source_target_pairs={{0,16},{1,17},{2,18},{3,19},{4,20},{5,21},{6,22},{7,23},{8,24},{9,... | collective-permute-start | bytes 196616 | tf_op jit(solution)/shard_map/ppermute | solution.py:96
  5.8 0.9 copy-done
  6.8 0.9 copy-done.1
  7.7 1.6 %collective-permute-start.3 = (bf16[1,16,6144]{2,1,0:T(8,128)(2,1)S(1)}, bf16[1,16,6144]{2,1,0:T(8,128)(2,1)S(1)}, u32[]{:S(2)}, u32[]{:S(2)}) collective-permute-start(bf16[1,16,6144]{2,1,0:T(8,128)(2,1)S(1)} %get-tuple-element.36.refs_0_), channel_id=1, source_target_pairs={{0,2},{1,5},{2,0},{3,7},{4,6},{5,1},{6,4},{7,3},{8,10},{9,13},{10,... | collective-permute-start | bytes 589832 | tf_op jit(solution)/shard_map/ppermute | solution.py:96
  9.3 0.3 collective-permute-start.2
  9.6 0.8 copy.23
  10.5 0.5 reshape.45.refs_2_.refs_0_
  11.0 1.6 %collective-permute-start.1 = (bf16[2,16,2048]{2,1,0:T(8,128)(2,1)S(1)}, bf16[2,16,2048]{2,1,0:T(8,128)(2,1)S(1)}, u32[]{:S(2)}, u32[]{:S(2)}) collective-permute-start(bf16[2,16,2048]{2,1,0:T(8,128)(2,1)S(1)} %shard_map.110.refs_0_), channel_id=1, source_target_pairs={{0,8},{1,9},{2,10},{3,11},{4,12},{5,13},{6,14},{7,15},{8,0},{9,1},... | collective-permute-start | bytes 393224 | tf_op jit(solution)/shard_map/ppermute | solution.py:96
  12.7 5.0 %collective-permute-done.2.refs_1_ = bf16[1,16,4096]{2,1,0:T(8,128)(2,1)S(1)} collective-permute-done((bf16[1,16,4096]{2,1,0:T(8,128)(2,1)S(1)}, bf16[1,16,4096]{2,1,0:T(8,128)(2,1)S(1)}, u32[]{:S(2)}, u32[]{:S(2)}) %collective-permute-start.2) | collective-permute-done | bytes 131104 | tf_op jit(solution)/shard_map/ppermute | solution.py:96
  17.7 0.5 collective-permute-start.11
  18.3 1.2 collective-permute-start.4
  19.5 1.3 collective-permute-start.5
  20.8 1.0 collective-permute-start.6
  21.8 0.1 multiply_reduce_fusion
  21.9 0.1 collective-permute-start.7
  22.0 2.2 %collective-permute-done.11.refs_1_ = bf16[2,16,4096]{2,1,0:T(8,128)(2,1)S(1)} collective-permute-done((bf16[2,16,4096]{2,1,0:T(8,128)(2,1)S(1)}, bf16[2,16,4096]{2,1,0:T(8,128)(2,1)S(1)}, u32[]{:S(2)}, u32[]{:S(2)}) %collective-permute-start.11) | collective-permute-done | bytes 262176 | tf_op jit(solution)/shard_map/ppermute | solution.py:96
  24.2 1.8 %collective-permute-start.12 = (bf16[2,16,6144]{2,1,0:T(8,128)(2,1)S(1)}, bf16[2,16,6144]{2,1,0:T(8,128)(2,1)S(1)}, u32[]{:S(2)}, u32[]{:S(2)}) collective-permute-start(bf16[2,16,6144]{2,1,0:T(8,128)(2,1)S(1)} %shard_map.113.refs_3_.refs_0_), channel_id=1, source_target_pairs={{0,16},{1,17},{2,18},{3,19},{4,20},{5,21},{6,22},{7,23},{8,24},{9,... | collective-permute-start | bytes 1179656 | tf_op jit(solution)/shard_map/ppermute | solution.py:96
  26.0 1.6 %collective-permute-done.4.refs_2_ = bf16[4,16,2048]{2,1,0:T(8,128)(2,1)S(1)} collective-permute-done((bf16[4,16,2048]{2,1,0:T(8,128)(2,1)S(1)}, bf16[4,16,2048]{2,1,0:T(8,128)(2,1)S(1)}, u32[]{:S(2)}, u32[]{:S(2)}) %collective-permute-start.4) | collective-permute-done | bytes 262176 | tf_op jit(solution)/shard_map/ppermute | solution.py:96
  27.6 0.5 collective-permute-start.9
  28.1 4.1 %collective-permute-done.6.refs_4_ = bf16[4,16,2048]{2,1,0:T(8,128)(2,1)S(1)} collective-permute-done((bf16[4,16,2048]{2,1,0:T(8,128)(2,1)S(1)}, bf16[4,16,2048]{2,1,0:T(8,128)(2,1)S(1)}, u32[]{:S(2)}, u32[]{:S(2)}) %collective-permute-start.6) | collective-permute-done | bytes 262176 | tf_op jit(solution)/shard_map/ppermute | solution.py:96
  32.3 10.6 %collective-permute-done.12.refs_1_ = bf16[2,16,6144]{2,1,0:T(8,128)(2,1)S(1)} collective-permute-done((bf16[2,16,6144]{2,1,0:T(8,128)(2,1)S(1)}, bf16[2,16,6144]{2,1,0:T(8,128)(2,1)S(1)}, u32[]{:S(2)}, u32[]{:S(2)}) %collective-permute-start.12) | collective-permute-done | bytes 393248 | tf_op jit(solution)/shard_map/ppermute | solution.py:96
  42.9 2.9 %collective-permute-start.13 = (bf16[4,16,4096]{2,1,0:T(8,128)(2,1)S(1)}, bf16[4,16,4096]{2,1,0:T(8,128)(2,1)S(1)}, u32[]{:S(2)}, u32[]{:S(2)}) collective-permute-start(bf16[4,16,4096]{2,1,0:T(8,128)(2,1)S(1)} %shard_map.115.refs_12_.refs_1_), channel_id=1, source_target_pairs={{0,2},{1,5},{2,0},{3,7},{4,6},{5,1},{6,4},{7,3},{8,10},{9,13},{10,... | collective-permute-start | bytes 1572872 | tf_op jit(solution)/shard_map/ppermute | solution.py:96
  45.8 0.1 shard_map.116.refs_13_.refs_0_
  45.9 0.1 collective-permute-start.14
  46.0 0.1 collective-permute-start.17
  46.1 13.4 %shard_map.117.refs_2_.refs_0_ = bf16[8,144,512]{2,1,0:T(8,128)(2,1)S(1)} custom-call(bf16[8,144,512]{2,1,0:T(8,128)(2,1)S(1)} %reshape.45.refs_2_.refs_0_, bf16[4,16,2048]{2,1,0:T(8,128)(2,1)S(1)} %shard_map.114.refs_1_, bf16[4,16,2048]{2,1,0:T(8,128)(2,1)S(1)} %collective-permute-done.4.refs_2_, bf16[4,16,2048]{2,1,0:T(8,128)(2,1)S(1)} %collective-permute-done.5.refs_3_, ...), custom_call_target="tpu_custom_call" | custom-call | flops 16000000000 | bytes 6000000 | tf_op jit(solution)/shard_map/pallas_call | solution.py:296
  59.5 2.0 %collective-permute-start.15 = (bf16[4,16,4096]{2,1,0:T(8,128)(2,1)S(1)}, bf16[4,16,4096]{2,1,0:T(8,128)(2,1)S(1)}, u32[]{:S(2)}, u32[]{:S(2)}) collective-permute-start(bf16[4,16,4096]{2,1,0:T(8,128)(2,1)S(1)} %collective-permute-done.13.refs_2_), channel_id=1, source_target_pairs={{0,4},{1,3},{2,6},{3,1},{4,0},{5,7},{6,2},{7,5},{8,12},{9,11},{10,... | collective-permute-start | bytes 1572872 | tf_op jit(solution)/shard_map/ppermute | solution.py:96
  61.5 3.6 %collective-permute-done.17.refs_1_ = bf16[4,16,6144]{2,1,0:T(8,128)(2,1)S(1)} collective-permute-done((bf16[4,16,6144]{2,1,0:T(8,128)(2,1)S(1)}, bf16[4,16,6144]{2,1,0:T(8,128)(2,1)S(1)}, u32[]{:S(2)}, u32[]{:S(2)}) %collective-permute-start.17) | collective-permute-done | bytes 786464 | tf_op jit(solution)/shard_map/ppermute | solution.py:96
  65.1 0.5 collective-permute-start.19
  65.6 3.1 %collective-permute-done.15.refs_4_ = bf16[4,16,4096]{2,1,0:T(8,128)(2,1)S(1)} collective-permute-done((bf16[4,16,4096]{2,1,0:T(8,128)(2,1)S(1)}, bf16[4,16,4096]{2,1,0:T(8,128)(2,1)S(1)}, u32[]{:S(2)}, u32[]{:S(2)}) %collective-permute-start.15) | collective-permute-done | bytes 524320 | tf_op jit(solution)/shard_map/ppermute | solution.py:96
  68.8 0.1 shard_map.118
  68.9 2.0 %collective-permute-start.21 = (bf16[8,16,2048]{2,1,0:T(8,128)(2,1)S(1)}, bf16[8,16,2048]{2,1,0:T(8,128)(2,1)S(1)}, u32[]{:S(2)}, u32[]{:S(2)}) collective-permute-start(bf16[8,16,2048]{2,1,0:T(8,128)(2,1)S(1)} %get-tuple-element.41.refs_10_.refs_7_), channel_id=1, source_target_pairs={{0,4},{1,3},{2,6},{3,1},{4,0},{5,7},{6,2},{7,5},{8,12},{9,11},{10,... | collective-permute-start | bytes 1572872 | tf_op jit(solution)/shard_map/ppermute | solution.py:96
  70.9 4.9 %shard_map.119 = (bf16[4,2,36,512]{3,2,1,0:T(8,128)(2,1)S(1)}, bf16[4,2,36,512]{3,2,1,0:T(8,128)(2,1)S(1)}, bf16[2,36,512]{2,1,0:T(8,128)(2,1)S(1)}) custom-call(bf16[8,144,512]{2,1,0:T(8,128)(2,1)S(1)} %shard_map.117.refs_2_.refs_0_, bf16[4,16,4096]{2,1,0:T(8,128)(2,1)S(1)} %shard_map.115.refs_12_.refs_1_, ...), custom_call_target="tpu_custom_call" | custom-call | flops 4831838208 | bytes 8000000 | tf_op jit(solution)/shard_map/pallas_call | solution.py:353
  75.8 2.3 %collective-permute-done.21.refs_11_.refs_8_ = bf16[8,16,2048]{2,1,0:T(8,128)(2,1)S(1)} collective-permute-done((bf16[8,16,2048]{2,1,0:T(8,128)(2,1)S(1)}, bf16[8,16,2048]{2,1,0:T(8,128)(2,1)S(1)}, u32[]{:S(2)}, u32[]{:S(2)}) %collective-permute-start.21) | collective-permute-done | bytes 524320 | tf_op jit(solution)/shard_map/ppermute | solution.py:96
  78.1 4.8 %shard_map.120 = (bf16[4,2,36,512]{3,2,1,0:T(8,128)(2,1)S(1)}, bf16[4,2,36,512]{3,2,1,0:T(8,128)(2,1)S(1)}, bf16[2,36,512]{2,1,0:T(8,128)(2,1)S(1)}) custom-call(bf16[8,144,512]{2,1,0:T(8,128)(2,1)S(1)} %shard_map.117.refs_2_.refs_0_, bf16[4,16,4096]{2,1,0:T(8,128)(2,1)S(1)} %shard_map.115.refs_12_.refs_1_, ...), custom_call_target="tpu_custom_call" | custom-call | flops 4831838208 | bytes 8000000 | tf_op jit(solution)/shard_map/pallas_call | solution.py:353
  82.9 0.1 collective-permute-start.26
  83.0 3.5 %collective-permute-start.22 = (bf16[4,2,36,512]{3,2,1,0:T(8,128)(2,1)S(1)}, bf16[4,2,36,512]{3,2,1,0:T(8,128)(2,1)S(1)}, u32[]{:S(2)}, u32[]{:S(2)}) collective-permute-start(bf16[4,2,36,512]{3,2,1,0:T(8,128)(2,1)S(1)} %get-tuple-element.42.refs_0_), channel_id=1, source_target_pairs={{2,0},{3,1},{4,2},{5,3},{6,4},{7,5},{8,6},{9,7},{10,8},{11,9},{12,... | collective-permute-start | bytes 884744 | tf_op jit(solution)/shard_map/ppermute | solution.py:380
  86.5 1.7 %collective-permute-start.23 = (bf16[2,36,512]{2,1,0:T(8,128)(2,1)S(1)}, bf16[2,36,512]{2,1,0:T(8,128)(2,1)S(1)}, u32[]{:S(2)}, u32[]{:S(2)}) collective-permute-start(bf16[2,36,512]{2,1,0:T(8,128)(2,1)S(1)} %get-tuple-element.44.refs_10_), channel_id=1, source_target_pairs={{3,0},{2,1},{5,2},{4,3},{7,4},{6,5},{9,6},{8,7},{11,8},{10,9},{13,... | collective-permute-start | bytes 221192 | tf_op jit(solution)/shard_map/ppermute | solution.py:380
  88.2 7.6 %collective-permute-done.23.refs_6_ = bf16[2,36,512]{2,1,0:T(8,128)(2,1)S(1)} collective-permute-done((bf16[2,36,512]{2,1,0:T(8,128)(2,1)S(1)}, bf16[2,36,512]{2,1,0:T(8,128)(2,1)S(1)}, u32[]{:S(2)}, u32[]{:S(2)}) %collective-permute-start.23) | collective-permute-done | bytes 73760 | tf_op jit(solution)/shard_map/ppermute | solution.py:380
  95.9 0.5 collective-permute-start.28
  96.4 0.5 collective-permute-start.27
  96.9 0.4 collective-permute-done.24.refs_5_
  97.3 13.3 %shard_map.121.refs_0_ = bf16[8,144,512]{2,1,0:T(8,128)(2,1)S(1)} custom-call(bf16[4,2,36,512]{3,2,1,0:T(8,128)(2,1)S(1)} %get-tuple-element.42.refs_0_, bf16[4,2,36,512]{3,2,1,0:T(8,128)(2,1)S(1)} %get-tuple-element.43.refs_1_, bf16[4,2,36,512]{3,2,1,0:T(8,128)(2,1)S(1)} %get-tuple-element.45.refs_2_, ...), custom_call_target="tpu_custom_call" | custom-call | flops 16000000000 | bytes 6000000 | tf_op jit(solution)/shard_map/pallas_call | solution.py:296
  110.6 0.6 collective-permute-done.27.refs_2_
  111.2 2.7 %collective-permute-done.29.refs_4_ = bf16[8,16,4096]{2,1,0:T(8,128)(2,1)S(1)} collective-permute-done((bf16[8,16,4096]{2,1,0:T(8,128)(2,1)S(1)}, bf16[8,16,4096]{2,1,0:T(8,128)(2,1)S(1)}, u32[]{:S(2)}, u32[]{:S(2)}) %collective-permute-start.29) | collective-permute-done | bytes 1048608 | tf_op jit(solution)/shard_map/ppermute | solution.py:96
  113.8 4.7 %shard_map.122 = (bf16[4,2,36,512]{3,2,1,0:T(8,128)(2,1)S(1)}, bf16[4,2,36,512]{3,2,1,0:T(8,128)(2,1)S(1)}, bf16[2,36,512]{2,1,0:T(8,128)(2,1)S(1)}) custom-call(bf16[8,144,512]{2,1,0:T(8,128)(2,1)S(1)} %shard_map.121.refs_0_, bf16[8,16,4096]{2,1,0:T(8,128)(2,1)S(1)} %get-tuple-element.51.refs_1_, bf16[8,16,4096]{2,1,0:T(8,128)(2,1)S(1)} %collective-permute-done.27.refs_2_, ...), custom_call_target="tpu_custom_call" | custom-call | flops 4831838208 | bytes 8000000 | tf_op jit(solution)/shard_map/pallas_call | solution.py:353
  118.6 0.7 collective-permute-start.30
  119.3 1.3 collective-permute-start.32
  120.6 4.7 %shard_map.123 = (bf16[4,2,36,512]{3,2,1,0:T(8,128)(2,1)S(1)}, bf16[4,2,36,512]{3,2,1,0:T(8,128)(2,1)S(1)}, bf16[2,36,512]{2,1,0:T(8,128)(2,1)S(1)}) custom-call(bf16[8,144,512]{2,1,0:T(8,128)(2,1)S(1)} %shard_map.121.refs_0_, bf16[8,16,4096]{2,1,0:T(8,128)(2,1)S(1)} %get-tuple-element.51.refs_1_, bf16[8,16,4096]{2,1,0:T(8,128)(2,1)S(1)} %collective-permute-done.27.refs_2_, ...), custom_call_target="tpu_custom_call" | custom-call | flops 4831838208 | bytes 8000000 | tf_op jit(solution)/shard_map/pallas_call | solution.py:353
  125.4 1.1 collective-permute-done.30
  126.5 0.8 collective-permute-start.31
  127.3 1.0 collective-permute-done.31
  128.3 5.7 %collective-permute-done.32 = bf16[4,2,36,512]{3,2,1,0:T(8,128)(2,1)S(1)} collective-permute-done((bf16[4,2,36,512]{3,2,1,0:T(8,128)(2,1)S(1)}, bf16[4,2,36,512]{3,2,1,0:T(8,128)(2,1)S(1)}, u32[]{:S(2)}, u32[]{:S(2)}) %collective-permute-start.32) | collective-permute-done | bytes 294944 | tf_op jit(solution)/shard_map/ppermute | solution.py:380
  134.0 0.1 reshape.56
  134.2 0.2 copy.21
  134.4 0.1 reshape.53
  134.5 0.2 copy.20
  134.8 0.1 reshape.50
  134.9 0.2 copy.19
  135.2 0.1 reshape.47
  135.4 0.2 copy.18
  135.6 2.9 %maximum_maximum_fusion = bf16[24,24,2,512]{3,2,1,0:T(2,128)(2,1)} fusion(bf16[6,21,2,512]{3,2,1,0:T(2,128)(2,1)S(1)} %bitcast.33, bf16[6,21,2,512]{3,2,1,0:T(2,128)(2,1)S(1)} %bitcast.34, bf16[6,21,2,512]{3,2,1,0:T(2,128)(2,1)S(1)} %bitcast.35, bf16[6,3,2,512]{3,2,1,0:T(2,128)(2,1)S(1)} %reshape_transpose_reshape_broadcast_in_dim_squeeze.15, ...), kind=kLoop, calls=%fused_computation | loop fusion | flops 4128768 | bytes 2359296 | tf_op jit(solution)/shard_map/concatenate | solution.py:405
  (63 shorter events, 0.5 us)
Async XLA Ops:
  0.0 0.9 copy-start.2
  0.9 0.8 copy-start.3
  1.8 9.2 %collective-permute-start = (bf16[1,16,2048]{2,1,0:T(8,128)(2,1)S(1)}, bf16[1,16,2048]{2,1,0:T(8,128)(2,1)S(1)}, u32[]{:S(2)}, u32[]{:S(2)}) collective-permute-start(bf16[1,16,2048]{2,1,0:T(8,128)(2,1)S(1)} %shard_map.109.refs_0_), channel_id=1, source_target_pairs={{0,16},{1,17},{2,18},{3,19},{4,20},{5,21},{6,22},{7,23},{8,24},{9,... | collective-permute-start | bytes 196616 | tf_op jit(solution)/shard_map/ppermute | solution.py:96
  5.8 0.9 copy-start
  6.8 0.9 copy-start.1
  7.7 1.9 %copy-start.6 = (bf16[24,24,2,512]{3,2,1,0:T(2,128)(2,1)S(1)}, bf16[24,24,2,512]{3,2,1,0:T(2,128)(2,1)}, u32[]{:S(2)}) copy-start(bf16[24,24,2,512]{3,2,1,0:T(2,128)(2,1)} %param.11) | copy-start | bytes 3538948
  7.7 10.5 %collective-permute-start.3 = (bf16[1,16,6144]{2,1,0:T(8,128)(2,1)S(1)}, bf16[1,16,6144]{2,1,0:T(8,128)(2,1)S(1)}, u32[]{:S(2)}, u32[]{:S(2)}) collective-permute-start(bf16[1,16,6144]{2,1,0:T(8,128)(2,1)S(1)} %get-tuple-element.36.refs_0_), channel_id=1, source_target_pairs={{0,2},{1,5},{2,0},{3,7},{4,6},{5,1},{6,4},{7,3},{8,10},{9,13},{10,... | collective-permute-start | bytes 589832 | tf_op jit(solution)/shard_map/ppermute | solution.py:96
  9.3 8.4 %collective-permute-start.2 = (bf16[1,16,4096]{2,1,0:T(8,128)(2,1)S(1)}, bf16[1,16,4096]{2,1,0:T(8,128)(2,1)S(1)}, u32[]{:S(2)}, u32[]{:S(2)}) collective-permute-start(bf16[1,16,4096]{2,1,0:T(8,128)(2,1)S(1)} %get-tuple-element.35.refs_0_), channel_id=1, source_target_pairs={{0,16},{1,17},{2,18},{3,19},{4,20},{5,21},{6,22},{7,23},{8,24},{9,... | collective-permute-start | bytes 393224 | tf_op jit(solution)/shard_map/ppermute | solution.py:96
  11.0 10.8 %copy-start.7 = (f32[16,512]{1,0:T(8,128)S(1)}, f32[16,512]{1,0:T(8,128)}, u32[]{:S(2)}) copy-start(f32[16,512]{1,0:T(8,128)} %constant.8.clone) | copy-start | bytes 98308
  11.0 10.8 %copy-start.9 = (f32[2,16]{1,0:T(2,128)S(1)}, f32[2,16]{1,0:T(2,128)}, u32[]{:S(2)}) copy-start(f32[2,16]{1,0:T(2,128)} %param.17) | copy-start | bytes 388
  11.0 21.2 %copy-start.8 = (f32[2,2,512]{2,1,0:T(2,128)S(1)}, f32[2,2,512]{2,1,0:T(2,128)}, u32[]{:S(2)}) copy-start(f32[2,2,512]{2,1,0:T(2,128)} %param.16) | copy-start | bytes 24580
  11.0 7.2 %collective-permute-start.1 = (bf16[2,16,2048]{2,1,0:T(8,128)(2,1)S(1)}, bf16[2,16,2048]{2,1,0:T(8,128)(2,1)S(1)}, u32[]{:S(2)}, u32[]{:S(2)}) collective-permute-start(bf16[2,16,2048]{2,1,0:T(8,128)(2,1)S(1)} %shard_map.110.refs_0_), channel_id=1, source_target_pairs={{0,8},{1,9},{2,10},{3,11},{4,12},{5,13},{6,14},{7,15},{8,0},{9,1},... | collective-permute-start | bytes 393224 | tf_op jit(solution)/shard_map/ppermute | solution.py:96
  17.7 6.4 %collective-permute-start.11 = (bf16[2,16,4096]{2,1,0:T(8,128)(2,1)S(1)}, bf16[2,16,4096]{2,1,0:T(8,128)(2,1)S(1)}, u32[]{:S(2)}, u32[]{:S(2)}) collective-permute-start(bf16[2,16,4096]{2,1,0:T(8,128)(2,1)S(1)} %shard_map.112.refs_2_.refs_0_), channel_id=1, source_target_pairs={{0,8},{1,9},{2,10},{3,11},{4,12},{5,13},{6,14},{7,15},{8,0},{9,1},... | collective-permute-start | bytes 786440 | tf_op jit(solution)/shard_map/ppermute | solution.py:96
  18.3 9.3 %collective-permute-start.4 = (bf16[4,16,2048]{2,1,0:T(8,128)(2,1)S(1)}, bf16[4,16,2048]{2,1,0:T(8,128)(2,1)S(1)}, u32[]{:S(2)}, u32[]{:S(2)}) collective-permute-start(bf16[4,16,2048]{2,1,0:T(8,128)(2,1)S(1)} %shard_map.114.refs_1_), channel_id=1, source_target_pairs={{0,2},{1,5},{2,0},{3,7},{4,6},{5,1},{6,4},{7,3},{8,10},{9,13},{10,... | collective-permute-start | bytes 786440 | tf_op jit(solution)/shard_map/ppermute | solution.py:96
  19.5 8.1 %collective-permute-start.5 = (bf16[4,16,2048]{2,1,0:T(8,128)(2,1)S(1)}, bf16[4,16,2048]{2,1,0:T(8,128)(2,1)S(1)}, u32[]{:S(2)}, u32[]{:S(2)}) collective-permute-start(bf16[4,16,2048]{2,1,0:T(8,128)(2,1)S(1)} %shard_map.114.refs_1_), channel_id=1, source_target_pairs={{0,4},{1,3},{2,6},{3,1},{4,0},{5,7},{6,2},{7,5},{8,12},{9,11},{10,... | collective-permute-start | bytes 786440 | tf_op jit(solution)/shard_map/ppermute | solution.py:96
  20.8 11.4 %collective-permute-start.6 = (bf16[4,16,2048]{2,1,0:T(8,128)(2,1)S(1)}, bf16[4,16,2048]{2,1,0:T(8,128)(2,1)S(1)}, u32[]{:S(2)}, u32[]{:S(2)}) collective-permute-start(bf16[4,16,2048]{2,1,0:T(8,128)(2,1)S(1)} %shard_map.114.refs_1_), channel_id=1, source_target_pairs={{0,6},{1,7},{2,4},{3,5},{4,2},{5,3},{6,0},{7,1},{8,14},{9,15},{10,... | collective-permute-start | bytes 786440 | tf_op jit(solution)/shard_map/ppermute | solution.py:96
  21.9 24.0 %collective-permute-start.7 = (bf16[4,16,2048]{2,1,0:T(8,128)(2,1)S(1)}, bf16[4,16,2048]{2,1,0:T(8,128)(2,1)S(1)}, u32[]{:S(2)}, u32[]{:S(2)}) collective-permute-start(bf16[4,16,2048]{2,1,0:T(8,128)(2,1)S(1)} %shard_map.114.refs_1_), channel_id=1, source_target_pairs={{0,1},{1,0},{2,3},{3,2},{4,5},{5,4},{6,7},{7,6},{8,9},{9,8},{10,11... | collective-permute-start | bytes 786440 | tf_op jit(solution)/shard_map/ppermute | solution.py:96
  24.2 18.7 %collective-permute-start.12 = (bf16[2,16,6144]{2,1,0:T(8,128)(2,1)S(1)}, bf16[2,16,6144]{2,1,0:T(8,128)(2,1)S(1)}, u32[]{:S(2)}, u32[]{:S(2)}) collective-permute-start(bf16[2,16,6144]{2,1,0:T(8,128)(2,1)S(1)} %shard_map.113.refs_3_.refs_0_), channel_id=1, source_target_pairs={{0,16},{1,17},{2,18},{3,19},{4,20},{5,21},{6,22},{7,23},{8,24},{9,... | collective-permute-start | bytes 1179656 | tf_op jit(solution)/shard_map/ppermute | solution.py:96
  27.6 18.4 %collective-permute-start.8 = (bf16[4,16,2048]{2,1,0:T(8,128)(2,1)S(1)}, bf16[4,16,2048]{2,1,0:T(8,128)(2,1)S(1)}, u32[]{:S(2)}, u32[]{:S(2)}) collective-permute-start(bf16[4,16,2048]{2,1,0:T(8,128)(2,1)S(1)} %collective-permute-done.4.refs_2_), channel_id=1, source_target_pairs={{0,1},{1,0},{2,3},{3,2},{4,5},{5,4},{6,7},{7,6},{8,9},{9,8},{10,11... | collective-permute-start | bytes 786440 | tf_op jit(solution)/shard_map/ppermute | solution.py:96
  27.6 18.5 %collective-permute-start.9 = (bf16[4,16,2048]{2,1,0:T(8,128)(2,1)S(1)}, bf16[4,16,2048]{2,1,0:T(8,128)(2,1)S(1)}, u32[]{:S(2)}, u32[]{:S(2)}) collective-permute-start(bf16[4,16,2048]{2,1,0:T(8,128)(2,1)S(1)} %collective-permute-done.5.refs_3_), channel_id=1, source_target_pairs={{0,1},{1,0},{2,3},{3,2},{4,5},{5,4},{6,7},{7,6},{8,9},{9,8},{10,11... | collective-permute-start | bytes 786440 | tf_op jit(solution)/shard_map/ppermute | solution.py:96
  32.2 13.9 %collective-permute-start.10 = (bf16[4,16,2048]{2,1,0:T(8,128)(2,1)S(1)}, bf16[4,16,2048]{2,1,0:T(8,128)(2,1)S(1)}, u32[]{:S(2)}, u32[]{:S(2)}) collective-permute-start(bf16[4,16,2048]{2,1,0:T(8,128)(2,1)S(1)} %collective-permute-done.6.refs_4_), channel_id=1, source_target_pairs={{0,1},{1,0},{2,3},{3,2},{4,5},{5,4},{6,7},{7,6},{8,9},{9,8},{10,11... | collective-permute-start | bytes 786440 | tf_op jit(solution)/shard_map/ppermute | solution.py:96
  32.2 13.9 %copy-start.4 = (bf16[640,256]{1,0:T(8,128)(2,1)S(1)}, bf16[640,256]{1,0:T(8,128)(2,1)}, u32[]{:S(2)}) copy-start(bf16[640,256]{1,0:T(8,128)(2,1)} %constant.9.clone.refs_11_.refs_13_) | copy-start | bytes 983044
  42.9 16.6 %collective-permute-start.13 = (bf16[4,16,4096]{2,1,0:T(8,128)(2,1)S(1)}, bf16[4,16,4096]{2,1,0:T(8,128)(2,1)S(1)}, u32[]{:S(2)}, u32[]{:S(2)}) collective-permute-start(bf16[4,16,4096]{2,1,0:T(8,128)(2,1)S(1)} %shard_map.115.refs_12_.refs_1_), channel_id=1, source_target_pairs={{0,2},{1,5},{2,0},{3,7},{4,6},{5,1},{6,4},{7,3},{8,10},{9,13},{10,... | collective-permute-start | bytes 1572872 | tf_op jit(solution)/shard_map/ppermute | solution.py:96
  45.9 15.6 %collective-permute-start.14 = (bf16[4,16,4096]{2,1,0:T(8,128)(2,1)S(1)}, bf16[4,16,4096]{2,1,0:T(8,128)(2,1)S(1)}, u32[]{:S(2)}, u32[]{:S(2)}) collective-permute-start(bf16[4,16,4096]{2,1,0:T(8,128)(2,1)S(1)} %shard_map.115.refs_12_.refs_1_), channel_id=1, source_target_pairs={{0,4},{1,3},{2,6},{3,1},{4,0},{5,7},{6,2},{7,5},{8,12},{9,11},{10,... | collective-permute-start | bytes 1572872 | tf_op jit(solution)/shard_map/ppermute | solution.py:96
  46.0 19.1 %collective-permute-start.17 = (bf16[4,16,6144]{2,1,0:T(8,128)(2,1)S(1)}, bf16[4,16,6144]{2,1,0:T(8,128)(2,1)S(1)}, u32[]{:S(2)}, u32[]{:S(2)}) collective-permute-start(bf16[4,16,6144]{2,1,0:T(8,128)(2,1)S(1)} %shard_map.116.refs_13_.refs_0_), channel_id=1, source_target_pairs={{0,8},{1,9},{2,10},{3,11},{4,12},{5,13},{6,14},{7,15},{8,0},{9,1},... | collective-permute-start | bytes 2359304 | tf_op jit(solution)/shard_map/ppermute | solution.py:96
  59.5 9.2 %collective-permute-start.15 = (bf16[4,16,4096]{2,1,0:T(8,128)(2,1)S(1)}, bf16[4,16,4096]{2,1,0:T(8,128)(2,1)S(1)}, u32[]{:S(2)}, u32[]{:S(2)}) collective-permute-start(bf16[4,16,4096]{2,1,0:T(8,128)(2,1)S(1)} %collective-permute-done.13.refs_2_), channel_id=1, source_target_pairs={{0,4},{1,3},{2,6},{3,1},{4,0},{5,7},{6,2},{7,5},{8,12},{9,11},{10,... | collective-permute-start | bytes 1572872 | tf_op jit(solution)/shard_map/ppermute | solution.py:96
  61.5 9.4 %collective-permute-start.16 = (bf16[4,16,4096]{2,1,0:T(8,128)(2,1)S(1)}, bf16[4,16,4096]{2,1,0:T(8,128)(2,1)S(1)}, u32[]{:S(2)}, u32[]{:S(2)}) collective-permute-start(bf16[4,16,4096]{2,1,0:T(8,128)(2,1)S(1)} %shard_map.115.refs_12_.refs_1_), channel_id=1, source_target_pairs={{0,1},{1,0},{2,3},{3,2},{4,5},{5,4},{6,7},{7,6},{8,9},{9,8},{10,11... | collective-permute-start | bytes 1572872 | tf_op jit(solution)/shard_map/ppermute | solution.py:96
  65.1 5.8 %collective-permute-start.18 = (bf16[4,16,4096]{2,1,0:T(8,128)(2,1)S(1)}, bf16[4,16,4096]{2,1,0:T(8,128)(2,1)S(1)}, u32[]{:S(2)}, u32[]{:S(2)}) collective-permute-start(bf16[4,16,4096]{2,1,0:T(8,128)(2,1)S(1)} %collective-permute-done.13.refs_2_), channel_id=1, source_target_pairs={{0,1},{1,0},{2,3},{3,2},{4,5},{5,4},{6,7},{7,6},{8,9},{9,8},{10,11... | collective-permute-start | bytes 1572872 | tf_op jit(solution)/shard_map/ppermute | solution.py:96
  65.1 5.8 %collective-permute-start.19 = (bf16[4,16,4096]{2,1,0:T(8,128)(2,1)S(1)}, bf16[4,16,4096]{2,1,0:T(8,128)(2,1)S(1)}, u32[]{:S(2)}, u32[]{:S(2)}) collective-permute-start(bf16[4,16,4096]{2,1,0:T(8,128)(2,1)S(1)} %collective-permute-done.14.refs_3_), channel_id=1, source_target_pairs={{0,1},{1,0},{2,3},{3,2},{4,5},{5,4},{6,7},{7,6},{8,9},{9,8},{10,11... | collective-permute-start | bytes 1572872 | tf_op jit(solution)/shard_map/ppermute | solution.py:96
  68.8 2.1 %collective-permute-start.20 = (bf16[4,16,4096]{2,1,0:T(8,128)(2,1)S(1)}, bf16[4,16,4096]{2,1,0:T(8,128)(2,1)S(1)}, u32[]{:S(2)}, u32[]{:S(2)}) collective-permute-start(bf16[4,16,4096]{2,1,0:T(8,128)(2,1)S(1)} %collective-permute-done.15.refs_4_), channel_id=1, source_target_pairs={{0,1},{1,0},{2,3},{3,2},{4,5},{5,4},{6,7},{7,6},{8,9},{9,8},{10,11... | collective-permute-start | bytes 1572872 | tf_op jit(solution)/shard_map/ppermute | solution.py:96
  68.9 9.2 %collective-permute-start.21 = (bf16[8,16,2048]{2,1,0:T(8,128)(2,1)S(1)}, bf16[8,16,2048]{2,1,0:T(8,128)(2,1)S(1)}, u32[]{:S(2)}, u32[]{:S(2)}) collective-permute-start(bf16[8,16,2048]{2,1,0:T(8,128)(2,1)S(1)} %get-tuple-element.41.refs_10_.refs_7_), channel_id=1, source_target_pairs={{0,4},{1,3},{2,6},{3,1},{4,0},{5,7},{6,2},{7,5},{8,12},{9,11},{10,... | collective-permute-start | bytes 1572872 | tf_op jit(solution)/shard_map/ppermute | solution.py:96
  70.9 26.0 %collective-permute-start.25 = (bf16[8,16,2048]{2,1,0:T(8,128)(2,1)S(1)}, bf16[8,16,2048]{2,1,0:T(8,128)(2,1)S(1)}, u32[]{:S(2)}, u32[]{:S(2)}) collective-permute-start(bf16[8,16,2048]{2,1,0:T(8,128)(2,1)S(1)} %get-tuple-element.41.refs_10_.refs_7_), channel_id=1, source_target_pairs={{0,1},{1,0},{2,3},{3,2},{4,5},{5,4},{6,7},{7,6},{8,9},{9,8},{10,11... | collective-permute-start | bytes 1572872 | tf_op jit(solution)/shard_map/ppermute | solution.py:96
  78.1 19.1 %copy-start.5 = (f32[144,256]{1,0:T(8,128)S(1)}, f32[144,256]{1,0:T(8,128)}, u32[]{:S(2)}) copy-start(f32[144,256]{1,0:T(8,128)} %constant.10.clone.refs_14_) | copy-start | bytes 442372
  82.9 14.3 %collective-permute-start.26 = (bf16[8,16,2048]{2,1,0:T(8,128)(2,1)S(1)}, bf16[8,16,2048]{2,1,0:T(8,128)(2,1)S(1)}, u32[]{:S(2)}, u32[]{:S(2)}) collective-permute-start(bf16[8,16,2048]{2,1,0:T(8,128)(2,1)S(1)} %collective-permute-done.21.refs_11_.refs_8_), channel_id=1, source_target_pairs={{0,1},{1,0},{2,3},{3,2},{4,5},{5,4},{6,7},{7,6},{8,9},{9,8},{10,11... | collective-permute-start | bytes 1572872 | tf_op jit(solution)/shard_map/ppermute | solution.py:96
  83.0 12.8 %collective-permute-start.22 = (bf16[4,2,36,512]{3,2,1,0:T(8,128)(2,1)S(1)}, bf16[4,2,36,512]{3,2,1,0:T(8,128)(2,1)S(1)}, u32[]{:S(2)}, u32[]{:S(2)}) collective-permute-start(bf16[4,2,36,512]{3,2,1,0:T(8,128)(2,1)S(1)} %get-tuple-element.42.refs_0_), channel_id=1, source_target_pairs={{2,0},{3,1},{4,2},{5,3},{6,4},{7,5},{8,6},{9,7},{10,8},{11,9},{12,... | collective-permute-start | bytes 884744 | tf_op jit(solution)/shard_map/ppermute | solution.py:380
  86.5 9.3 %collective-permute-start.23 = (bf16[2,36,512]{2,1,0:T(8,128)(2,1)S(1)}, bf16[2,36,512]{2,1,0:T(8,128)(2,1)S(1)}, u32[]{:S(2)}, u32[]{:S(2)}) collective-permute-start(bf16[2,36,512]{2,1,0:T(8,128)(2,1)S(1)} %get-tuple-element.44.refs_10_), channel_id=1, source_target_pairs={{3,0},{2,1},{5,2},{4,3},{7,4},{6,5},{9,6},{8,7},{11,8},{10,9},{13,... | collective-permute-start | bytes 221192 | tf_op jit(solution)/shard_map/ppermute | solution.py:380
  95.9 1.4 %collective-permute-start.24 = (bf16[4,36,512]{2,1,0:T(8,128)(2,1)S(1)}, bf16[4,36,512]{2,1,0:T(8,128)(2,1)S(1)}, u32[]{:S(2)}, u32[]{:S(2)}) collective-permute-start(bf16[4,36,512]{2,1,0:T(8,128)(2,1)S(1)} %pad_maximum_fusion), channel_id=1, source_target_pairs={{1,0},{0,1},{3,2},{2,3},{5,4},{4,5},{7,6},{6,7},{9,8},{8,9},{11,10... | collective-permute-start | bytes 442376 | tf_op jit(solution)/shard_map/ppermute | solution.py:380
  95.9 15.3 %collective-permute-start.28 = (bf16[8,16,4096]{2,1,0:T(8,128)(2,1)S(1)}, bf16[8,16,4096]{2,1,0:T(8,128)(2,1)S(1)}, u32[]{:S(2)}, u32[]{:S(2)}) collective-permute-start(bf16[8,16,4096]{2,1,0:T(8,128)(2,1)S(1)} %get-tuple-element.51.refs_1_), channel_id=1, source_target_pairs={{0,1},{1,0},{2,3},{3,2},{4,5},{5,4},{6,7},{7,6},{8,9},{9,8},{10,11... | collective-permute-start | bytes 3145736 | tf_op jit(solution)/shard_map/ppermute | solution.py:96
  96.4 14.8 %collective-permute-start.27 = (bf16[8,16,4096]{2,1,0:T(8,128)(2,1)S(1)}, bf16[8,16,4096]{2,1,0:T(8,128)(2,1)S(1)}, u32[]{:S(2)}, u32[]{:S(2)}) collective-permute-start(bf16[8,16,4096]{2,1,0:T(8,128)(2,1)S(1)} %get-tuple-element.51.refs_1_), channel_id=1, source_target_pairs={{0,4},{1,3},{2,6},{3,1},{4,0},{5,7},{6,2},{7,5},{8,12},{9,11},{10,... | collective-permute-start | bytes 3145736 | tf_op jit(solution)/shard_map/ppermute | solution.py:96
  111.2 2.7 %collective-permute-start.29 = (bf16[8,16,4096]{2,1,0:T(8,128)(2,1)S(1)}, bf16[8,16,4096]{2,1,0:T(8,128)(2,1)S(1)}, u32[]{:S(2)}, u32[]{:S(2)}) collective-permute-start(bf16[8,16,4096]{2,1,0:T(8,128)(2,1)S(1)} %collective-permute-done.27.refs_2_), channel_id=1, source_target_pairs={{0,1},{1,0},{2,3},{3,2},{4,5},{5,4},{6,7},{7,6},{8,9},{9,8},{10,11... | collective-permute-start | bytes 3145736 | tf_op jit(solution)/shard_map/ppermute | solution.py:96
  118.6 7.9 %collective-permute-start.30 = (bf16[2,36,512]{2,1,0:T(8,128)(2,1)S(1)}, bf16[2,36,512]{2,1,0:T(8,128)(2,1)S(1)}, u32[]{:S(2)}, u32[]{:S(2)}) collective-permute-start(bf16[2,36,512]{2,1,0:T(8,128)(2,1)S(1)} %get-tuple-element.53.refs_6_), channel_id=1, source_target_pairs={{31,0},{30,1},{1,2},{0,3},{3,4},{2,5},{5,6},{4,7},{7,8},{6,9},{9,1... | collective-permute-start | bytes 221192 | tf_op jit(solution)/shard_map/ppermute | solution.py:380
  119.3 14.7 %collective-permute-start.32 = (bf16[4,2,36,512]{3,2,1,0:T(8,128)(2,1)S(1)}, bf16[4,2,36,512]{3,2,1,0:T(8,128)(2,1)S(1)}, u32[]{:S(2)}, u32[]{:S(2)}) collective-permute-start(bf16[4,2,36,512]{3,2,1,0:T(8,128)(2,1)S(1)} %get-tuple-element.59), channel_id=1, source_target_pairs={{30,0},{31,1},{0,2},{1,3},{2,4},{3,5},{4,6},{5,7},{6,8},{7,9},{8,1... | collective-permute-start | bytes 884744 | tf_op jit(solution)/shard_map/ppermute | solution.py:380
  126.5 1.8 %collective-permute-start.31 = (bf16[4,36,512]{2,1,0:T(8,128)(2,1)S(1)}, bf16[4,36,512]{2,1,0:T(8,128)(2,1)S(1)}, u32[]{:S(2)}, u32[]{:S(2)}) collective-permute-start(bf16[4,36,512]{2,1,0:T(8,128)(2,1)S(1)} %pad_maximum_fusion.1), channel_id=1, source_target_pairs={{1,0},{0,1},{3,2},{2,3},{5,4},{4,5},{7,6},{6,7},{9,8},{8,9},{11,10... | collective-permute-start | bytes 442376 | tf_op jit(solution)/shard_map/ppermute | solution.py:380

commit v11 on v10

--- a/solution.py
+++ b/solution.py
@@ -183,7 +183,7 @@
     return jnp.concatenate(quarters, 0).astype(jnp.bfloat16)
 
 
-def attend_kernel(shifted, row_windows, count, *refs):
+def attend_kernel(shifted, row_windows, skipped, count, *refs):
     sources = 7 if shifted else 1
     x_refs, pieces = refs[:sources], refs[sources : sources + count]
     gain_ref, sharp_ref, ones_ref = refs[sources + count : sources + count + 3]
@@ -199,7 +199,9 @@
         sides = (x_refs[0:2], x_refs[2:4])
         tokens = jnp.concatenate(
             [
-                rolled_window(pl.program_id(0) * held + window, row_windows, sides, *x_refs[4:])
+                rolled_window(
+                    (pl.program_id(0) + skipped) * held + window, row_windows, sides, *x_refs[4:]
+                )
                 for window in range(held)
             ],
             0,
@@ -238,7 +240,7 @@
             rest = jnp.exp2(dot(query, rest_keys, NT)).astype(jnp.bfloat16)
             if shifted:
                 last = jnp.logical_and(
-                    (pl.program_id(0) * held + window) % row_windows == row_windows - 1,
+                    ((pl.program_id(0) + skipped) * held + window) % row_windows == row_windows - 1,
                     lax.axis_index("lat") == lax.axis_size("lat") - 1,
                 )
                 allow = jnp.where(last, allow_ref[...], 1.0).astype(jnp.bfloat16)
@@ -294,7 +296,7 @@
     ones = jnp.asarray(head_columns(), jnp.bfloat16)
     extra = (jnp.asarray(allowed_pairs()),) if shifted else ()
     return pl.pallas_call(
-        functools.partial(attend_kernel, shifted, row_windows, len(pieces)),
+        functools.partial(attend_kernel, shifted, row_windows, skipped, len(pieces)),
         grid=(count // held,),
         out_shape=jax.ShapeDtypeStruct((count, CELLS, features), jnp.bfloat16),
         in_specs=([whole(source.shape) for source in sources] if shifted else [x_block])
@@ -433,46 +435,56 @@
         widths = tuple(sum(weight.shape[2] for weight in pair) for pair in (weights[:2], weights[2:]))
         (pair,) = join([[own, across_z(own, 2)]], (), (windows,))
         (feed_pair,) = join([[feed_own, across_z(feed_own, 2)]])
-        (last_pair,) = join([[last_own, send(last_own, beside)]])
+        last_pair, final_pair = join([[last_own, send(last_own, beside)]], widths=widths)
         (column,) = join([[pair, across_z(pair, 1)]], (), (feed_pair, last_pair))
-        pieces = whole_pieces(column, [send(column, way) for way in (beside, across, corner)])
-        (last_four,) = join([[last_pair, across_z(last_pair, 2)]])
+        received = [send(column, way) for way in (beside, across, corner)]
+        sent = [tied(column, received[0])] + received
+        pieces = [column] + received + [send(part, swap) for part in sent]
         (feed_column,) = join([[feed_pair, across_z(feed_pair, 1)]])
         received = [send(feed_column, way) for way in (beside, across)]
-        last_other = across_z(last_four, 1)
-        middle = attention(0, [windows], (0, 1), pieces, (feed_column, last_four))
-        received.append(send(tied(received[0], middle), across))
-        sent = [feed_column] + tied(received[:2], (middle, last_other)) + [tied(received[2], middle)]
-        feed_pieces = [feed_column] + received + [send(part, swap) for part in sent]
-        column, last_column = join([[last_four, last_other]], (), (middle,), widths)
-        received = send(column, across)
-        left_0, right_0, low_0 = forward(0, middle, 0, feed_pieces, low_edge, (column,))
+        (last_four,) = join([[last_pair, across_z(last_pair, 2)]])
+        (last_column,) = join([[last_four, across_z(last_four, 1)]])
+        last_received = send(tied(last_column, feed_column), across)
+        final_pair = tied(final_pair, last_four)
+        final_other = across_z(final_pair, 2)
+        middle = attention(0, [windows], (0, 1), pieces, (feed_column, last_column))
+        received.append(send(tied(received[0], (middle, final_other, last_received)), across))
+        swapped = [send(part, swap) for part in [feed_column] + tied(received[:2], middle)]
+        swapped.append(send(tied(received[2], tuple(swapped)), swap))
+        feed_pieces = [feed_column] + received + swapped
+        (final_four,) = join([[final_pair, final_other]], (), (middle,))
+        last_pieces = [last_column, last_received]
+        last_pieces += [send(part, swap) for part in tied(last_pieces, middle)]
+        left_0, right_0, low_0 = forward(0, middle, 0, feed_pieces, low_edge, (final_four,))
         ahead, ahead_low = shift_from(left_0, 1, 0), shift_from(low_0, 1, 1)
-        left_1, right_1, low_1 = forward(0, middle, 1, feed_pieces, low_edge, (low_0, received))
-        pieces = [column, received]
-        pieces += [send(column, swap), send(tied(received, low_1), swap)]
-        last_received = send(tied(last_column, received), across)
+        left_1, right_1, low_1 = forward(0, middle, 1, feed_pieces, low_edge, (low_0, *last_pieces))
+        (final_column,) = join([[final_four, across_z(final_four, 1)]], (), (low_1,))
+        final_received = send(final_column, across)
+        after = (final_column,)
     else:
         gathered = []
         for block in range(2):
             for pair in (weights[:2], weights[2:]):
                 chunk = jnp.concatenate([weight[block] for weight in pair], 1)
                 gathered.append([lax.all_gather(chunk, "lon", axis=0, tiled=True)])
-        first_pieces, feed_pieces, pieces, last_pieces = gathered
+        first_pieces, feed_pieces, last_pieces, final_pieces = gathered
+        after = ()
         middle = attention(0, [windows], (0, 1), first_pieces)
         left_0, right_0, low_0 = forward(0, middle, 0, feed_pieces, low_edge)
         left_1, right_1, low_1 = forward(0, middle, 1, feed_pieces, low_edge)
         ahead, ahead_low = shift_from(left_0, 1, 0), shift_from(low_0, 1, 1)
     below = shift_from(tied(jnp.concatenate([low_0, low_1], 0), (ahead, ahead_low)), 0, 1)
-    sources = [left_0, right_0, left_1, right_1, ahead, below, ahead_low]
-    middle = attention(1, sources, (0, 1), pieces)
+    sides = [left_0, right_0, left_1, right_1]
+    unused = [left_1, below, below]
+    middle_0 = attention(1, sides + unused, (0,), last_pieces, after)
+    middle_1 = attention(1, sides + [ahead, below, ahead_low], (1,), last_pieces, (middle_0,))
     if relay:
-        last_pieces = [last_column, last_received]
-        last_pieces += [send(last_column, swap), send(tied(last_received, middle), swap)]
-    left_1, right_1, high_1 = forward(1, middle, 1, last_pieces, high_edge)
+        final_pieces = [final_column, final_received]
+        final_pieces += [send(final_column, swap), send(tied(final_received, middle_1), swap)]
+    left_1, right_1, high_1 = forward(1, middle_1, 0, final_pieces, high_edge)
     behind = shift_from(right_1, -1, 0)
     behind_high = shift_from(high_1, -1, -1)
-    left_0, right_0, high_0 = forward(1, middle, 0, last_pieces, high_edge, (high_1,))
+    left_0, right_0, high_0 = forward(1, middle_0, 0, final_pieces, high_edge, (high_1,))
     above = shift_from(tied(jnp.concatenate([high_0, high_1], 0), behind_high), 0, -1)
     sides, above, behind_high = tied(((left_0, right_0, left_1), above, behind_high), behind)
     return back_in_place(sides, behind, (above[0], above[1], above[2]), behind_high[1])

time: 139 us -> 132 us (0.950)
  waiting for transfers between devices: 51.7 us -> 37 us
  starting transfers between devices: 30.7 us -> 38.2 us
    ppermute x27 -> x29, waiting for transfers between devices: 35.9 us -> 23.6 us  [send(): return lax.ppermute(block, ('lon', 'lat'), pairs)]
    ppermute x27 -> x29, starting transfers between devices: 22.6 us -> 29.3 us  [send(): return lax.ppermute(block, ('lon', 'lat'), pairs)]
    ppermute x6, waiting for transfers between devices: 15.8 us -> 13.4 us  [shift_from(): return lax.ppermute(block, ('lon', 'lat'), pairs)]
    pallas_call x2 -> x3, Pallas kernels: 26.7 us -> 27 us  [attend(): pl.pallas_call(functools.partial(attend_kernel, shifted, row_windows, ski...]
  transfers between devices with their start and end apart: 33 -> 35, of which waited for: 15 -> 12; matrix products, arithmetic and copies ran while one was open for 1% -> 1% of each run, Pallas kernels for 30% -> 32%
where the time goes in v11:
time: 132 us
  Pallas kernels  46.5 us (35%)
  starting transfers between devices  38.2 us (29%)
  waiting for transfers between devices  37 us (28%)
  local copies, waits for them, and re-layouts  6.51 us (5%)
  other arithmetic  3.03 us (2%)
    ppermute x29, starting transfers between devices, send(): return lax.ppermute(block, ('lon', 'lat'), pairs)  29.3 us
    pallas_call x3, Pallas kernels, attend(): pl.pallas_call(functools.partial(attend_kernel, shifted, row_windows, ski...  27 us
    ppermute x29, waiting for transfers between devices, send(): return lax.ppermute(block, ('lon', 'lat'), pairs)  23.6 us
    pallas_call x4, Pallas kernels, feed(): pl.pallas_call(functools.partial(feed_kernel, len(pieces), hidden_size, 5...  19.2 us
    ppermute x6, waiting for transfers between devices, shift_from(): return lax.ppermute(block, ('lon', 'lat'), pairs)  13.4 us
    ppermute x6, starting transfers between devices, shift_from(): return lax.ppermute(block, ('lon', 'lat'), pairs)  8.91 us
    unnamed x20, local copies, waits for them, and re-layouts  3.7 us
    concatenate x1, other arithmetic, back_in_place(): return jnp.concatenate([first, jnp.concatenate([tops, own], 1)], 0)  2.9 us
  transfers between devices with their start and end apart: 35, of which 12 were waited for; matrix products, arithmetic and copies ran while one was open for 1% of the time, Pallas kernels for 32%

profile of v11, /device:TPU:0, one launch (start us, length us, event | category | flops | bytes accessed | tf_op | source)
XLA Modules:
  0.0 131.7 jit_solution(11859127011946178423)
XLA Ops:
  0.0 0.9 copy-done.2
  0.9 0.8 copy-done.3
  1.8 4.0 %collective-permute-start = (bf16[1,16,2048]{2,1,0:T(8,128)(2,1)S(1)}, bf16[1,16,2048]{2,1,0:T(8,128)(2,1)S(1)}, u32[]{:S(2)}, u32[]{:S(2)}) collective-permute-start(bf16[1,16,2048]{2,1,0:T(8,128)(2,1)S(1)} %shard_map.127.refs_0_), channel_id=1, source_target_pairs={{0,16},{1,17},{2,18},{3,19},{4,20},{5,21},{6,22},{7,23},{8,24},{9,... | collective-permute-start | bytes 196616 | tf_op jit(solution)/shard_map/ppermute | solution.py:96
  5.8 0.9 copy-done
  6.8 0.9 copy-done.1
  7.7 1.6 %collective-permute-start.3 = (bf16[1,16,6144]{2,1,0:T(8,128)(2,1)S(1)}, bf16[1,16,6144]{2,1,0:T(8,128)(2,1)S(1)}, u32[]{:S(2)}, u32[]{:S(2)}) collective-permute-start(bf16[1,16,6144]{2,1,0:T(8,128)(2,1)S(1)} %get-tuple-element.39.refs_0_), channel_id=1, source_target_pairs={{0,2},{1,5},{2,0},{3,7},{4,6},{5,1},{6,4},{7,3},{8,10},{9,13},{10,... | collective-permute-start | bytes 589832 | tf_op jit(solution)/shard_map/ppermute | solution.py:96
  9.3 0.3 collective-permute-start.2
  9.6 0.8 copy.25
  10.5 0.5 reshape.45.refs_2_.refs_0_
  11.0 1.6 %collective-permute-start.1 = (bf16[2,16,2048]{2,1,0:T(8,128)(2,1)S(1)}, bf16[2,16,2048]{2,1,0:T(8,128)(2,1)S(1)}, u32[]{:S(2)}, u32[]{:S(2)}) collective-permute-start(bf16[2,16,2048]{2,1,0:T(8,128)(2,1)S(1)} %shard_map.128.refs_0_), channel_id=1, source_target_pairs={{0,8},{1,9},{2,10},{3,11},{4,12},{5,13},{6,14},{7,15},{8,0},{9,1},... | collective-permute-start | bytes 393224 | tf_op jit(solution)/shard_map/ppermute | solution.py:96
  12.7 5.0 %collective-permute-done.2.refs_1_ = bf16[1,16,4096]{2,1,0:T(8,128)(2,1)S(1)} collective-permute-done((bf16[1,16,4096]{2,1,0:T(8,128)(2,1)S(1)}, bf16[1,16,4096]{2,1,0:T(8,128)(2,1)S(1)}, u32[]{:S(2)}, u32[]{:S(2)}) %collective-permute-start.2) | collective-permute-done | bytes 131104 | tf_op jit(solution)/shard_map/ppermute | solution.py:96
  17.8 1.6 %collective-permute-start.4 = (bf16[4,16,2048]{2,1,0:T(8,128)(2,1)S(1)}, bf16[4,16,2048]{2,1,0:T(8,128)(2,1)S(1)}, u32[]{:S(2)}, u32[]{:S(2)}) collective-permute-start(bf16[4,16,2048]{2,1,0:T(8,128)(2,1)S(1)} %shard_map.132.refs_1_), channel_id=1, source_target_pairs={{0,2},{1,5},{2,0},{3,7},{4,6},{5,1},{6,4},{7,3},{8,10},{9,13},{10,... | collective-permute-start | bytes 786440 | tf_op jit(solution)/shard_map/ppermute | solution.py:96
  19.4 1.9 %collective-permute-start.5 = (bf16[4,16,2048]{2,1,0:T(8,128)(2,1)S(1)}, bf16[4,16,2048]{2,1,0:T(8,128)(2,1)S(1)}, u32[]{:S(2)}, u32[]{:S(2)}) collective-permute-start(bf16[4,16,2048]{2,1,0:T(8,128)(2,1)S(1)} %shard_map.132.refs_1_), channel_id=1, source_target_pairs={{0,4},{1,3},{2,6},{3,1},{4,0},{5,7},{6,2},{7,5},{8,12},{9,11},{10,... | collective-permute-start | bytes 786440 | tf_op jit(solution)/shard_map/ppermute | solution.py:96
  21.3 0.4 collective-permute-start.6
  21.8 3.9 %collective-permute-start.12 = (bf16[2,16,2048]{2,1,0:T(8,128)(2,1)S(1)}, bf16[2,16,2048]{2,1,0:T(8,128)(2,1)S(1)}, u32[]{:S(2)}, u32[]{:S(2)}) collective-permute-start(bf16[2,16,2048]{2,1,0:T(8,128)(2,1)S(1)} %get-tuple-element.40.refs_3_.refs_0_), channel_id=1, source_target_pairs={{0,16},{1,17},{2,18},{3,19},{4,20},{5,21},{6,22},{7,23},{8,24},{9,... | collective-permute-start | bytes 393224 | tf_op jit(solution)/shard_map/ppermute | solution.py:96
  25.7 0.1 multiply_reduce_fusion
  25.8 4.2 %collective-permute-done.12.refs_1_ = bf16[2,16,2048]{2,1,0:T(8,128)(2,1)S(1)} collective-permute-done((bf16[2,16,2048]{2,1,0:T(8,128)(2,1)S(1)}, bf16[2,16,2048]{2,1,0:T(8,128)(2,1)S(1)}, u32[]{:S(2)}, u32[]{:S(2)}) %collective-permute-start.12) | collective-permute-done | bytes 131104 | tf_op jit(solution)/shard_map/ppermute | solution.py:96
  30.0 2.3 %collective-permute-start.13 = (bf16[4,16,2048]{2,1,0:T(8,128)(2,1)S(1)}, bf16[4,16,2048]{2,1,0:T(8,128)(2,1)S(1)}, u32[]{:S(2)}, u32[]{:S(2)}) collective-permute-start(bf16[4,16,2048]{2,1,0:T(8,128)(2,1)S(1)} %shard_map.134.refs_0_), channel_id=1, source_target_pairs={{0,8},{1,9},{2,10},{3,11},{4,12},{5,13},{6,14},{7,15},{8,0},{9,1},... | collective-permute-start | bytes 786440 | tf_op jit(solution)/shard_map/ppermute | solution.py:96
  32.3 0.5 collective-permute-start.8
  32.9 0.4 collective-permute-start.10
  33.4 3.8 %collective-permute-done.13.refs_1_ = bf16[4,16,2048]{2,1,0:T(8,128)(2,1)S(1)} collective-permute-done((bf16[4,16,2048]{2,1,0:T(8,128)(2,1)S(1)}, bf16[4,16,2048]{2,1,0:T(8,128)(2,1)S(1)}, u32[]{:S(2)}, u32[]{:S(2)}) %collective-permute-start.13) | collective-permute-done | bytes 262176 | tf_op jit(solution)/shard_map/ppermute | solution.py:96
  37.2 1.3 collective-permute-start.16
  38.5 1.8 %collective-permute-start.14 = (bf16[4,16,4096]{2,1,0:T(8,128)(2,1)S(1)}, bf16[4,16,4096]{2,1,0:T(8,128)(2,1)S(1)}, u32[]{:S(2)}, u32[]{:S(2)}) collective-permute-start(bf16[4,16,4096]{2,1,0:T(8,128)(2,1)S(1)} %shard_map.133.refs_12_.refs_1_), channel_id=1, source_target_pairs={{0,2},{1,5},{2,0},{3,7},{4,6},{5,1},{6,4},{7,3},{8,10},{9,13},{10,... | collective-permute-start | bytes 1572872 | tf_op jit(solution)/shard_map/ppermute | solution.py:96
  40.3 1.2 collective-permute-start.15
  41.5 0.9 collective-permute-start.17
  42.4 13.3 %shard_map.136.refs_2_.refs_0_ = bf16[8,144,512]{2,1,0:T(8,128)(2,1)S(1)} custom-call(bf16[8,144,512]{2,1,0:T(8,128)(2,1)S(1)} %reshape.45.refs_2_.refs_0_, bf16[4,16,2048]{2,1,0:T(8,128)(2,1)S(1)} %shard_map.132.refs_1_, bf16[4,16,2048]{2,1,0:T(8,128)(2,1)S(1)} %collective-permute-done.4.refs_2_, bf16[4,16,2048]{2,1,0:T(8,128)(2,1)S(1)} %collective-permute-done.5.refs_3_, ...), custom_call_target="tpu_custom_call" | custom-call | flops 16000000000 | bytes 6000000 | tf_op jit(solution)/shard_map/pallas_call | solution.py:298
  55.8 0.1 collective-permute-start.20
  55.9 0.5 collective-permute-start.21
  56.4 1.2 collective-permute-start.18
  57.5 0.2 collective-permute-done.20.refs_6_
  57.8 0.7 collective-permute-done.21.refs_7_
  58.5 7.0 %collective-permute-done.18.refs_4_ = bf16[4,16,4096]{2,1,0:T(8,128)(2,1)S(1)} collective-permute-done((bf16[4,16,4096]{2,1,0:T(8,128)(2,1)S(1)}, bf16[4,16,4096]{2,1,0:T(8,128)(2,1)S(1)}, u32[]{:S(2)}, u32[]{:S(2)}) %collective-permute-start.18) | collective-permute-done | bytes 524320 | tf_op jit(solution)/shard_map/ppermute | solution.py:96
  65.5 0.5 collective-permute-start.22
  66.1 0.5 collective-permute-start.24
  66.5 1.8 %collective-permute-start.28 = (bf16[4,16,4096]{2,1,0:T(8,128)(2,1)S(1)}, bf16[4,16,4096]{2,1,0:T(8,128)(2,1)S(1)}, u32[]{:S(2)}, u32[]{:S(2)}) collective-permute-start(bf16[4,16,4096]{2,1,0:T(8,128)(2,1)S(1)} %shard_map.137.refs_10_.refs_0_), channel_id=1, source_target_pairs={{0,8},{1,9},{2,10},{3,11},{4,12},{5,13},{6,14},{7,15},{8,0},{9,1},... | collective-permute-start | bytes 1572872 | tf_op jit(solution)/shard_map/ppermute | solution.py:96
  68.3 4.8 %shard_map.138 = (bf16[4,2,36,512]{3,2,1,0:T(8,128)(2,1)S(1)}, bf16[4,2,36,512]{3,2,1,0:T(8,128)(2,1)S(1)}, bf16[2,36,512]{2,1,0:T(8,128)(2,1)S(1)}) custom-call(bf16[8,144,512]{2,1,0:T(8,128)(2,1)S(1)} %shard_map.136.refs_2_.refs_0_, bf16[4,16,4096]{2,1,0:T(8,128)(2,1)S(1)} %shard_map.133.refs_12_.refs_1_, ...), custom_call_target="tpu_custom_call" | custom-call | flops 4831838208 | bytes 8000000 | tf_op jit(solution)/shard_map/pallas_call | solution.py:355
  73.2 5.4 %collective-permute-start.25 = (bf16[4,2,36,512]{3,2,1,0:T(8,128)(2,1)S(1)}, bf16[4,2,36,512]{3,2,1,0:T(8,128)(2,1)S(1)}, u32[]{:S(2)}, u32[]{:S(2)}) collective-permute-start(bf16[4,2,36,512]{3,2,1,0:T(8,128)(2,1)S(1)} %get-tuple-element.49.refs_0_), channel_id=1, source_target_pairs={{2,0},{3,1},{4,2},{5,3},{6,4},{7,5},{8,6},{9,7},{10,8},{11,9},{12,... | collective-permute-start | bytes 884744 | tf_op jit(solution)/shard_map/ppermute | solution.py:382
  78.6 4.9 %shard_map.139 = (bf16[4,2,36,512]{3,2,1,0:T(8,128)(2,1)S(1)}, bf16[4,2,36,512]{3,2,1,0:T(8,128)(2,1)S(1)}, bf16[2,36,512]{2,1,0:T(8,128)(2,1)S(1)}) custom-call(bf16[8,144,512]{2,1,0:T(8,128)(2,1)S(1)} %shard_map.136.refs_2_.refs_0_, bf16[4,16,4096]{2,1,0:T(8,128)(2,1)S(1)} %shard_map.133.refs_12_.refs_1_, ...), custom_call_target="tpu_custom_call" | custom-call | flops 4831838208 | bytes 8000000 | tf_op jit(solution)/shard_map/pallas_call | solution.py:355
  83.5 5.3 %collective-permute-done.26.refs_6_ = bf16[2,36,512]{2,1,0:T(8,128)(2,1)S(1)} collective-permute-done((bf16[2,36,512]{2,1,0:T(8,128)(2,1)S(1)}, bf16[2,36,512]{2,1,0:T(8,128)(2,1)S(1)}, u32[]{:S(2)}, u32[]{:S(2)}) %collective-permute-start.26) | collective-permute-done | bytes 73760 | tf_op jit(solution)/shard_map/ppermute | solution.py:382
  88.8 0.1 shard_map.140.refs_15_.refs_1_
  88.9 0.1 collective-permute-start.29
  89.0 0.6 collective-permute-start.30
  89.6 0.7 collective-permute-done.27.refs_5_.refs_6_
  90.2 6.8 %shard_map.141.refs_15_.refs_0_ = bf16[4,144,512]{2,1,0:T(8,128)(2,1)S(1)} custom-call(bf16[4,2,36,512]{3,2,1,0:T(8,128)(2,1)S(1)} %get-tuple-element.49.refs_0_, bf16[4,2,36,512]{3,2,1,0:T(8,128)(2,1)S(1)} %get-tuple-element.50.refs_1_, bf16[4,2,36,512]{3,2,1,0:T(8,128)(2,1)S(1)} %get-tuple-element.54.refs_2_.refs_4_, ...), custom_call_target="tpu_custom_call" | custom-call | flops 8000000000 | bytes 6000000 | tf_op jit(solution)/shard_map/pallas_call | solution.py:298
  97.0 6.9 %shard_map.142.refs_0_ = bf16[4,144,512]{2,1,0:T(8,128)(2,1)S(1)} custom-call(bf16[4,2,36,512]{3,2,1,0:T(8,128)(2,1)S(1)} %get-tuple-element.49.refs_0_, bf16[4,2,36,512]{3,2,1,0:T(8,128)(2,1)S(1)} %get-tuple-element.50.refs_1_, bf16[4,2,36,512]{3,2,1,0:T(8,128)(2,1)S(1)} %get-tuple-element.54.refs_2_.refs_4_, ...), custom_call_target="tpu_custom_call" | custom-call | flops 8000000000 | bytes 6000000 | tf_op jit(solution)/shard_map/pallas_call | solution.py:298
  103.9 0.2 collective-permute-start.31
  104.1 2.5 %collective-permute-done.31.refs_4_ = bf16[8,16,4096]{2,1,0:T(8,128)(2,1)S(1)} collective-permute-done((bf16[8,16,4096]{2,1,0:T(8,128)(2,1)S(1)}, bf16[8,16,4096]{2,1,0:T(8,128)(2,1)S(1)}, u32[]{:S(2)}, u32[]{:S(2)}) %collective-permute-start.31) | collective-permute-done | bytes 1048608 | tf_op jit(solution)/shard_map/ppermute | solution.py:96
  106.7 4.7 %shard_map.143 = (bf16[4,2,36,512]{3,2,1,0:T(8,128)(2,1)S(1)}, bf16[4,2,36,512]{3,2,1,0:T(8,128)(2,1)S(1)}, bf16[2,36,512]{2,1,0:T(8,128)(2,1)S(1)}) custom-call(bf16[4,144,512]{2,1,0:T(8,128)(2,1)S(1)} %shard_map.142.refs_0_, bf16[8,16,4096]{2,1,0:T(8,128)(2,1)S(1)} %shard_map.140.refs_15_.refs_1_, ...), custom_call_target="tpu_custom_call" | custom-call | flops 4831838208 | bytes 8000000 | tf_op jit(solution)/shard_map/pallas_call | solution.py:355
  111.4 2.4 %collective-permute-start.32 = (bf16[2,36,512]{2,1,0:T(8,128)(2,1)S(1)}, bf16[2,36,512]{2,1,0:T(8,128)(2,1)S(1)}, u32[]{:S(2)}, u32[]{:S(2)}) collective-permute-start(bf16[2,36,512]{2,1,0:T(8,128)(2,1)S(1)} %get-tuple-element.59.refs_6_), channel_id=1, source_target_pairs={{31,0},{30,1},{1,2},{0,3},{3,4},{2,5},{5,6},{4,7},{7,8},{6,9},{9,1... | collective-permute-start | bytes 221192 | tf_op jit(solution)/shard_map/ppermute | solution.py:382
  113.8 0.9 collective-permute-start.34
  114.7 4.7 %shard_map.144 = (bf16[4,2,36,512]{3,2,1,0:T(8,128)(2,1)S(1)}, bf16[4,2,36,512]{3,2,1,0:T(8,128)(2,1)S(1)}, bf16[2,36,512]{2,1,0:T(8,128)(2,1)S(1)}) custom-call(bf16[4,144,512]{2,1,0:T(8,128)(2,1)S(1)} %shard_map.141.refs_15_.refs_0_, bf16[8,16,4096]{2,1,0:T(8,128)(2,1)S(1)} %shard_map.140.refs_15_.refs_1_, ...), custom_call_target="tpu_custom_call" | custom-call | flops 4831838208 | bytes 8000000 | tf_op jit(solution)/shard_map/pallas_call | solution.py:355
  119.5 0.2 collective-permute-done.32
  119.7 0.2 collective-permute-start.33
  119.9 1.2 collective-permute-done.33
  121.1 6.1 %collective-permute-done.34 = bf16[4,2,36,512]{3,2,1,0:T(8,128)(2,1)S(1)} collective-permute-done((bf16[4,2,36,512]{3,2,1,0:T(8,128)(2,1)S(1)}, bf16[4,2,36,512]{3,2,1,0:T(8,128)(2,1)S(1)}, u32[]{:S(2)}, u32[]{:S(2)}) %collective-permute-start.34) | collective-permute-done | bytes 294944 | tf_op jit(solution)/shard_map/ppermute | solution.py:382
  127.2 0.1 reshape.56
  127.3 0.2 copy.23
  127.6 0.1 reshape.53
  127.7 0.2 copy.22
  127.9 0.1 reshape.50
  128.1 0.2 copy.21
  128.4 0.1 reshape.47
  128.5 0.2 copy.20
  128.8 2.9 %maximum_maximum_fusion = bf16[24,24,2,512]{3,2,1,0:T(2,128)(2,1)} fusion(bf16[6,21,2,512]{3,2,1,0:T(2,128)(2,1)S(1)} %bitcast.33, bf16[6,21,2,512]{3,2,1,0:T(2,128)(2,1)S(1)} %bitcast.34, bf16[6,21,2,512]{3,2,1,0:T(2,128)(2,1)S(1)} %bitcast.35, bf16[6,3,2,512]{3,2,1,0:T(2,128)(2,1)S(1)} %reshape_transpose_reshape_broadcast_in_dim_squeeze.15, ...), kind=kLoop, calls=%fused_computation | loop fusion | flops 4128768 | bytes 2359296 | tf_op jit(solution)/shard_map/concatenate | solution.py:407
  (70 shorter events, 0.7 us)
Async XLA Ops:
  0.0 0.9 copy-start.2
  0.9 0.8 copy-start.3
  1.8 9.2 %collective-permute-start = (bf16[1,16,2048]{2,1,0:T(8,128)(2,1)S(1)}, bf16[1,16,2048]{2,1,0:T(8,128)(2,1)S(1)}, u32[]{:S(2)}, u32[]{:S(2)}) collective-permute-start(bf16[1,16,2048]{2,1,0:T(8,128)(2,1)S(1)} %shard_map.127.refs_0_), channel_id=1, source_target_pairs={{0,16},{1,17},{2,18},{3,19},{4,20},{5,21},{6,22},{7,23},{8,24},{9,... | collective-permute-start | bytes 196616 | tf_op jit(solution)/shard_map/ppermute | solution.py:96
  5.8 0.9 copy-start
  6.8 0.9 copy-start.1
  7.7 1.9 %copy-start.6 = (bf16[24,24,2,512]{3,2,1,0:T(2,128)(2,1)S(1)}, bf16[24,24,2,512]{3,2,1,0:T(2,128)(2,1)}, u32[]{:S(2)}) copy-start(bf16[24,24,2,512]{3,2,1,0:T(2,128)(2,1)} %param.13) | copy-start | bytes 3538948
  7.7 10.0 %collective-permute-start.3 = (bf16[1,16,6144]{2,1,0:T(8,128)(2,1)S(1)}, bf16[1,16,6144]{2,1,0:T(8,128)(2,1)S(1)}, u32[]{:S(2)}, u32[]{:S(2)}) collective-permute-start(bf16[1,16,6144]{2,1,0:T(8,128)(2,1)S(1)} %get-tuple-element.39.refs_0_), channel_id=1, source_target_pairs={{0,2},{1,5},{2,0},{3,7},{4,6},{5,1},{6,4},{7,3},{8,10},{9,13},{10,... | collective-permute-start | bytes 589832 | tf_op jit(solution)/shard_map/ppermute | solution.py:96
  9.3 8.4 %collective-permute-start.2 = (bf16[1,16,4096]{2,1,0:T(8,128)(2,1)S(1)}, bf16[1,16,4096]{2,1,0:T(8,128)(2,1)S(1)}, u32[]{:S(2)}, u32[]{:S(2)}) collective-permute-start(bf16[1,16,4096]{2,1,0:T(8,128)(2,1)S(1)} %get-tuple-element.38.refs_0_), channel_id=1, source_target_pairs={{0,16},{1,17},{2,18},{3,19},{4,20},{5,21},{6,22},{7,23},{8,24},{9,... | collective-permute-start | bytes 393224 | tf_op jit(solution)/shard_map/ppermute | solution.py:96
  11.0 14.7 %copy-start.7 = (f32[16,512]{1,0:T(8,128)S(1)}, f32[16,512]{1,0:T(8,128)}, u32[]{:S(2)}) copy-start(f32[16,512]{1,0:T(8,128)} %constant.8.clone) | copy-start | bytes 98308
  11.0 14.7 %copy-start.9 = (f32[2,16]{1,0:T(2,128)S(1)}, f32[2,16]{1,0:T(2,128)}, u32[]{:S(2)}) copy-start(f32[2,16]{1,0:T(2,128)} %param.19) | copy-start | bytes 388
  11.0 22.3 %copy-start.8 = (f32[2,2,512]{2,1,0:T(2,128)S(1)}, f32[2,2,512]{2,1,0:T(2,128)}, u32[]{:S(2)}) copy-start(f32[2,2,512]{2,1,0:T(2,128)} %param.18) | copy-start | bytes 24580
  11.0 6.8 %collective-permute-start.1 = (bf16[2,16,2048]{2,1,0:T(8,128)(2,1)S(1)}, bf16[2,16,2048]{2,1,0:T(8,128)(2,1)S(1)}, u32[]{:S(2)}, u32[]{:S(2)}) collective-permute-start(bf16[2,16,2048]{2,1,0:T(8,128)(2,1)S(1)} %shard_map.128.refs_0_), channel_id=1, source_target_pairs={{0,8},{1,9},{2,10},{3,11},{4,12},{5,13},{6,14},{7,15},{8,0},{9,1},... | collective-permute-start | bytes 393224 | tf_op jit(solution)/shard_map/ppermute | solution.py:96
  17.8 14.5 %collective-permute-start.4 = (bf16[4,16,2048]{2,1,0:T(8,128)(2,1)S(1)}, bf16[4,16,2048]{2,1,0:T(8,128)(2,1)S(1)}, u32[]{:S(2)}, u32[]{:S(2)}) collective-permute-start(bf16[4,16,2048]{2,1,0:T(8,128)(2,1)S(1)} %shard_map.132.refs_1_), channel_id=1, source_target_pairs={{0,2},{1,5},{2,0},{3,7},{4,6},{5,1},{6,4},{7,3},{8,10},{9,13},{10,... | collective-permute-start | bytes 786440 | tf_op jit(solution)/shard_map/ppermute | solution.py:96
  19.4 12.9 %collective-permute-start.11 = (bf16[2,16,4096]{2,1,0:T(8,128)(2,1)S(1)}, bf16[2,16,4096]{2,1,0:T(8,128)(2,1)S(1)}, u32[]{:S(2)}, u32[]{:S(2)}) collective-permute-start(bf16[2,16,4096]{2,1,0:T(8,128)(2,1)S(1)} %shard_map.130.refs_2_.refs_0_), channel_id=1, source_target_pairs={{0,8},{1,9},{2,10},{3,11},{4,12},{5,13},{6,14},{7,15},{8,0},{9,1},... | collective-permute-start | bytes 786440 | tf_op jit(solution)/shard_map/ppermute | solution.py:96
  19.4 13.4 %collective-permute-start.5 = (bf16[4,16,2048]{2,1,0:T(8,128)(2,1)S(1)}, bf16[4,16,2048]{2,1,0:T(8,128)(2,1)S(1)}, u32[]{:S(2)}, u32[]{:S(2)}) collective-permute-start(bf16[4,16,2048]{2,1,0:T(8,128)(2,1)S(1)} %shard_map.132.refs_1_), channel_id=1, source_target_pairs={{0,4},{1,3},{2,6},{3,1},{4,0},{5,7},{6,2},{7,5},{8,12},{9,11},{10,... | collective-permute-start | bytes 786440 | tf_op jit(solution)/shard_map/ppermute | solution.py:96
  21.3 11.6 %collective-permute-start.6 = (bf16[4,16,2048]{2,1,0:T(8,128)(2,1)S(1)}, bf16[4,16,2048]{2,1,0:T(8,128)(2,1)S(1)}, u32[]{:S(2)}, u32[]{:S(2)}) collective-permute-start(bf16[4,16,2048]{2,1,0:T(8,128)(2,1)S(1)} %shard_map.132.refs_1_), channel_id=1, source_target_pairs={{0,6},{1,7},{2,4},{3,5},{4,2},{5,3},{6,0},{7,1},{8,14},{9,15},{10,... | collective-permute-start | bytes 786440 | tf_op jit(solution)/shard_map/ppermute | solution.py:96
  21.8 8.2 %collective-permute-start.12 = (bf16[2,16,2048]{2,1,0:T(8,128)(2,1)S(1)}, bf16[2,16,2048]{2,1,0:T(8,128)(2,1)S(1)}, u32[]{:S(2)}, u32[]{:S(2)}) collective-permute-start(bf16[2,16,2048]{2,1,0:T(8,128)(2,1)S(1)} %get-tuple-element.40.refs_3_.refs_0_), channel_id=1, source_target_pairs={{0,16},{1,17},{2,18},{3,19},{4,20},{5,21},{6,22},{7,23},{8,24},{9,... | collective-permute-start | bytes 393224 | tf_op jit(solution)/shard_map/ppermute | solution.py:96
  30.0 12.4 %copy-start.4 = (bf16[640,256]{1,0:T(8,128)(2,1)S(1)}, bf16[640,256]{1,0:T(8,128)(2,1)}, u32[]{:S(2)}) copy-start(bf16[640,256]{1,0:T(8,128)(2,1)} %constant.9.clone.refs_11_.refs_13_) | copy-start | bytes 983044
  30.0 7.1 %collective-permute-start.13 = (bf16[4,16,2048]{2,1,0:T(8,128)(2,1)S(1)}, bf16[4,16,2048]{2,1,0:T(8,128)(2,1)S(1)}, u32[]{:S(2)}, u32[]{:S(2)}) collective-permute-start(bf16[4,16,2048]{2,1,0:T(8,128)(2,1)S(1)} %shard_map.134.refs_0_), channel_id=1, source_target_pairs={{0,8},{1,9},{2,10},{3,11},{4,12},{5,13},{6,14},{7,15},{8,0},{9,1},... | collective-permute-start | bytes 786440 | tf_op jit(solution)/shard_map/ppermute | solution.py:96
  32.3 6.2 %collective-permute-start.7 = (bf16[4,16,2048]{2,1,0:T(8,128)(2,1)S(1)}, bf16[4,16,2048]{2,1,0:T(8,128)(2,1)S(1)}, u32[]{:S(2)}, u32[]{:S(2)}) collective-permute-start(bf16[4,16,2048]{2,1,0:T(8,128)(2,1)S(1)} %shard_map.132.refs_1_), channel_id=1, source_target_pairs={{0,1},{1,0},{2,3},{3,2},{4,5},{5,4},{6,7},{7,6},{8,9},{9,8},{10,11... | collective-permute-start | bytes 786440 | tf_op jit(solution)/shard_map/ppermute | solution.py:96
  32.3 8.0 %collective-permute-start.8 = (bf16[4,16,2048]{2,1,0:T(8,128)(2,1)S(1)}, bf16[4,16,2048]{2,1,0:T(8,128)(2,1)S(1)}, u32[]{:S(2)}, u32[]{:S(2)}) collective-permute-start(bf16[4,16,2048]{2,1,0:T(8,128)(2,1)S(1)} %collective-permute-done.4.refs_2_), channel_id=1, source_target_pairs={{0,1},{1,0},{2,3},{3,2},{4,5},{5,4},{6,7},{7,6},{8,9},{9,8},{10,11... | collective-permute-start | bytes 786440 | tf_op jit(solution)/shard_map/ppermute | solution.py:96
  32.8 8.6 %collective-permute-start.9 = (bf16[4,16,2048]{2,1,0:T(8,128)(2,1)S(1)}, bf16[4,16,2048]{2,1,0:T(8,128)(2,1)S(1)}, u32[]{:S(2)}, u32[]{:S(2)}) collective-permute-start(bf16[4,16,2048]{2,1,0:T(8,128)(2,1)S(1)} %collective-permute-done.5.refs_3_), channel_id=1, source_target_pairs={{0,1},{1,0},{2,3},{3,2},{4,5},{5,4},{6,7},{7,6},{8,9},{9,8},{10,11... | collective-permute-start | bytes 786440 | tf_op jit(solution)/shard_map/ppermute | solution.py:96
  32.9 8.6 %collective-permute-start.10 = (bf16[4,16,2048]{2,1,0:T(8,128)(2,1)S(1)}, bf16[4,16,2048]{2,1,0:T(8,128)(2,1)S(1)}, u32[]{:S(2)}, u32[]{:S(2)}) collective-permute-start(bf16[4,16,2048]{2,1,0:T(8,128)(2,1)S(1)} %collective-permute-done.6.refs_4_), channel_id=1, source_target_pairs={{0,1},{1,0},{2,3},{3,2},{4,5},{5,4},{6,7},{7,6},{8,9},{9,8},{10,11... | collective-permute-start | bytes 786440 | tf_op jit(solution)/shard_map/ppermute | solution.py:96
  37.2 19.2 %collective-permute-start.16 = (bf16[2,16,4096]{2,1,0:T(8,128)(2,1)S(1)}, bf16[2,16,4096]{2,1,0:T(8,128)(2,1)S(1)}, u32[]{:S(2)}, u32[]{:S(2)}) collective-permute-start(bf16[2,16,4096]{2,1,0:T(8,128)(2,1)S(1)} %get-tuple-element.43.refs_0_), channel_id=1, source_target_pairs={{0,16},{1,17},{2,18},{3,19},{4,20},{5,21},{6,22},{7,23},{8,24},{9,... | collective-permute-start | bytes 786440 | tf_op jit(solution)/shard_map/ppermute | solution.py:96
  38.5 17.3 %collective-permute-start.14 = (bf16[4,16,4096]{2,1,0:T(8,128)(2,1)S(1)}, bf16[4,16,4096]{2,1,0:T(8,128)(2,1)S(1)}, u32[]{:S(2)}, u32[]{:S(2)}) collective-permute-start(bf16[4,16,4096]{2,1,0:T(8,128)(2,1)S(1)} %shard_map.133.refs_12_.refs_1_), channel_id=1, source_target_pairs={{0,2},{1,5},{2,0},{3,7},{4,6},{5,1},{6,4},{7,3},{8,10},{9,13},{10,... | collective-permute-start | bytes 1572872 | tf_op jit(solution)/shard_map/ppermute | solution.py:96
  40.3 15.5 %collective-permute-start.15 = (bf16[4,16,4096]{2,1,0:T(8,128)(2,1)S(1)}, bf16[4,16,4096]{2,1,0:T(8,128)(2,1)S(1)}, u32[]{:S(2)}, u32[]{:S(2)}) collective-permute-start(bf16[4,16,4096]{2,1,0:T(8,128)(2,1)S(1)} %shard_map.133.refs_12_.refs_1_), channel_id=1, source_target_pairs={{0,4},{1,3},{2,6},{3,1},{4,0},{5,7},{6,2},{7,5},{8,12},{9,11},{10,... | collective-permute-start | bytes 1572872 | tf_op jit(solution)/shard_map/ppermute | solution.py:96
  41.5 16.1 %collective-permute-start.19 = (bf16[4,16,4096]{2,1,0:T(8,128)(2,1)S(1)}, bf16[4,16,4096]{2,1,0:T(8,128)(2,1)S(1)}, u32[]{:S(2)}, u32[]{:S(2)}) collective-permute-start(bf16[4,16,4096]{2,1,0:T(8,128)(2,1)S(1)} %shard_map.133.refs_12_.refs_1_), channel_id=1, source_target_pairs={{0,1},{1,0},{2,3},{3,2},{4,5},{5,4},{6,7},{7,6},{8,9},{9,8},{10,11... | collective-permute-start | bytes 1572872 | tf_op jit(solution)/shard_map/ppermute | solution.py:96
  41.5 14.9 %collective-permute-start.17 = (bf16[8,16,2048]{2,1,0:T(8,128)(2,1)S(1)}, bf16[8,16,2048]{2,1,0:T(8,128)(2,1)S(1)}, u32[]{:S(2)}, u32[]{:S(2)}) collective-permute-start(bf16[8,16,2048]{2,1,0:T(8,128)(2,1)S(1)} %shard_map.135.refs_13_.refs_11_.refs_7_), channel_id=1, source_target_pairs={{0,4},{1,3},{2,6},{3,1},{4,0},{5,7},{6,2},{7,5},{8,12},{9,11},{10,... | collective-permute-start | bytes 1572872 | tf_op jit(solution)/shard_map/ppermute | solution.py:96
  55.8 2.0 %collective-permute-start.20 = (bf16[4,16,4096]{2,1,0:T(8,128)(2,1)S(1)}, bf16[4,16,4096]{2,1,0:T(8,128)(2,1)S(1)}, u32[]{:S(2)}, u32[]{:S(2)}) collective-permute-start(bf16[4,16,4096]{2,1,0:T(8,128)(2,1)S(1)} %collective-permute-done.14.refs_2_), channel_id=1, source_target_pairs={{0,1},{1,0},{2,3},{3,2},{4,5},{5,4},{6,7},{7,6},{8,9},{9,8},{10,11... | collective-permute-start | bytes 1572872 | tf_op jit(solution)/shard_map/ppermute | solution.py:96
  55.9 2.6 %collective-permute-start.21 = (bf16[4,16,4096]{2,1,0:T(8,128)(2,1)S(1)}, bf16[4,16,4096]{2,1,0:T(8,128)(2,1)S(1)}, u32[]{:S(2)}, u32[]{:S(2)}) collective-permute-start(bf16[4,16,4096]{2,1,0:T(8,128)(2,1)S(1)} %collective-permute-done.15.refs_3_), channel_id=1, source_target_pairs={{0,1},{1,0},{2,3},{3,2},{4,5},{5,4},{6,7},{7,6},{8,9},{9,8},{10,11... | collective-permute-start | bytes 1572872 | tf_op jit(solution)/shard_map/ppermute | solution.py:96
  56.4 9.2 %collective-permute-start.18 = (bf16[4,16,4096]{2,1,0:T(8,128)(2,1)S(1)}, bf16[4,16,4096]{2,1,0:T(8,128)(2,1)S(1)}, u32[]{:S(2)}, u32[]{:S(2)}) collective-permute-start(bf16[4,16,4096]{2,1,0:T(8,128)(2,1)S(1)} %collective-permute-done.14.refs_2_), channel_id=1, source_target_pairs={{0,4},{1,3},{2,6},{3,1},{4,0},{5,7},{6,2},{7,5},{8,12},{9,11},{10,... | collective-permute-start | bytes 1572872 | tf_op jit(solution)/shard_map/ppermute | solution.py:96
  65.5 2.8 %collective-permute-start.22 = (bf16[4,16,4096]{2,1,0:T(8,128)(2,1)S(1)}, bf16[4,16,4096]{2,1,0:T(8,128)(2,1)S(1)}, u32[]{:S(2)}, u32[]{:S(2)}) collective-permute-start(bf16[4,16,4096]{2,1,0:T(8,128)(2,1)S(1)} %collective-permute-done.18.refs_4_), channel_id=1, source_target_pairs={{0,1},{1,0},{2,3},{3,2},{4,5},{5,4},{6,7},{7,6},{8,9},{9,8},{10,11... | collective-permute-start | bytes 1572872 | tf_op jit(solution)/shard_map/ppermute | solution.py:96
  66.0 12.6 %collective-permute-start.23 = (bf16[8,16,2048]{2,1,0:T(8,128)(2,1)S(1)}, bf16[8,16,2048]{2,1,0:T(8,128)(2,1)S(1)}, u32[]{:S(2)}, u32[]{:S(2)}) collective-permute-start(bf16[8,16,2048]{2,1,0:T(8,128)(2,1)S(1)} %shard_map.135.refs_13_.refs_11_.refs_7_), channel_id=1, source_target_pairs={{0,1},{1,0},{2,3},{3,2},{4,5},{5,4},{6,7},{7,6},{8,9},{9,8},{10,11... | collective-permute-start | bytes 1572872 | tf_op jit(solution)/shard_map/ppermute | solution.py:96
  66.1 12.5 %collective-permute-start.24 = (bf16[8,16,2048]{2,1,0:T(8,128)(2,1)S(1)}, bf16[8,16,2048]{2,1,0:T(8,128)(2,1)S(1)}, u32[]{:S(2)}, u32[]{:S(2)}) collective-permute-start(bf16[8,16,2048]{2,1,0:T(8,128)(2,1)S(1)} %collective-permute-done.17.refs_12_.refs_8_), channel_id=1, source_target_pairs={{0,1},{1,0},{2,3},{3,2},{4,5},{5,4},{6,7},{7,6},{8,9},{9,8},{10,11... | collective-permute-start | bytes 1572872 | tf_op jit(solution)/shard_map/ppermute | solution.py:96
  66.5 22.3 %collective-permute-start.28 = (bf16[4,16,4096]{2,1,0:T(8,128)(2,1)S(1)}, bf16[4,16,4096]{2,1,0:T(8,128)(2,1)S(1)}, u32[]{:S(2)}, u32[]{:S(2)}) collective-permute-start(bf16[4,16,4096]{2,1,0:T(8,128)(2,1)S(1)} %shard_map.137.refs_10_.refs_0_), channel_id=1, source_target_pairs={{0,8},{1,9},{2,10},{3,11},{4,12},{5,13},{6,14},{7,15},{8,0},{9,1},... | collective-permute-start | bytes 1572872 | tf_op jit(solution)/shard_map/ppermute | solution.py:96
  73.2 15.6 %collective-permute-start.25 = (bf16[4,2,36,512]{3,2,1,0:T(8,128)(2,1)S(1)}, bf16[4,2,36,512]{3,2,1,0:T(8,128)(2,1)S(1)}, u32[]{:S(2)}, u32[]{:S(2)}) collective-permute-start(bf16[4,2,36,512]{3,2,1,0:T(8,128)(2,1)S(1)} %get-tuple-element.49.refs_0_), channel_id=1, source_target_pairs={{2,0},{3,1},{4,2},{5,3},{6,4},{7,5},{8,6},{9,7},{10,8},{11,9},{12,... | collective-permute-start | bytes 884744 | tf_op jit(solution)/shard_map/ppermute | solution.py:382
  78.5 10.3 %collective-permute-start.26 = (bf16[2,36,512]{2,1,0:T(8,128)(2,1)S(1)}, bf16[2,36,512]{2,1,0:T(8,128)(2,1)S(1)}, u32[]{:S(2)}, u32[]{:S(2)}) collective-permute-start(bf16[2,36,512]{2,1,0:T(8,128)(2,1)S(1)} %get-tuple-element.51.refs_10_), channel_id=1, source_target_pairs={{3,0},{2,1},{5,2},{4,3},{7,4},{6,5},{9,6},{8,7},{11,8},{10,9},{13,... | collective-permute-start | bytes 221192 | tf_op jit(solution)/shard_map/ppermute | solution.py:382
  83.4 6.8 %copy-start.5 = (f32[144,256]{1,0:T(8,128)S(1)}, f32[144,256]{1,0:T(8,128)}, u32[]{:S(2)}) copy-start(f32[144,256]{1,0:T(8,128)} %constant.10.clone.refs_14_) | copy-start | bytes 442372
  88.8 1.4 %collective-permute-start.27 = (bf16[4,36,512]{2,1,0:T(8,128)(2,1)S(1)}, bf16[4,36,512]{2,1,0:T(8,128)(2,1)S(1)}, u32[]{:S(2)}, u32[]{:S(2)}) collective-permute-start(bf16[4,36,512]{2,1,0:T(8,128)(2,1)S(1)} %pad_maximum_fusion), channel_id=1, source_target_pairs={{1,0},{0,1},{3,2},{2,3},{5,4},{4,5},{7,6},{6,7},{9,8},{8,9},{11,10... | collective-permute-start | bytes 442376 | tf_op jit(solution)/shard_map/ppermute | solution.py:382
  88.9 15.0 %collective-permute-start.29 = (bf16[8,16,4096]{2,1,0:T(8,128)(2,1)S(1)}, bf16[8,16,4096]{2,1,0:T(8,128)(2,1)S(1)}, u32[]{:S(2)}, u32[]{:S(2)}) collective-permute-start(bf16[8,16,4096]{2,1,0:T(8,128)(2,1)S(1)} %shard_map.140.refs_15_.refs_1_), channel_id=1, source_target_pairs={{0,4},{1,3},{2,6},{3,1},{4,0},{5,7},{6,2},{7,5},{8,12},{9,11},{10,... | collective-permute-start | bytes 3145736 | tf_op jit(solution)/shard_map/ppermute | solution.py:96
  89.0 15.2 %collective-permute-start.30 = (bf16[8,16,4096]{2,1,0:T(8,128)(2,1)S(1)}, bf16[8,16,4096]{2,1,0:T(8,128)(2,1)S(1)}, u32[]{:S(2)}, u32[]{:S(2)}) collective-permute-start(bf16[8,16,4096]{2,1,0:T(8,128)(2,1)S(1)} %shard_map.140.refs_15_.refs_1_), channel_id=1, source_target_pairs={{0,1},{1,0},{2,3},{3,2},{4,5},{5,4},{6,7},{7,6},{8,9},{9,8},{10,11... | collective-permute-start | bytes 3145736 | tf_op jit(solution)/shard_map/ppermute | solution.py:96
  103.9 2.7 %collective-permute-start.31 = (bf16[8,16,4096]{2,1,0:T(8,128)(2,1)S(1)}, bf16[8,16,4096]{2,1,0:T(8,128)(2,1)S(1)}, u32[]{:S(2)}, u32[]{:S(2)}) collective-permute-start(bf16[8,16,4096]{2,1,0:T(8,128)(2,1)S(1)} %collective-permute-done.29.refs_2_), channel_id=1, source_target_pairs={{0,1},{1,0},{2,3},{3,2},{4,5},{5,4},{6,7},{7,6},{8,9},{9,8},{10,11... | collective-permute-start | bytes 3145736 | tf_op jit(solution)/shard_map/ppermute | solution.py:96
  111.4 8.3 %collective-permute-start.32 = (bf16[2,36,512]{2,1,0:T(8,128)(2,1)S(1)}, bf16[2,36,512]{2,1,0:T(8,128)(2,1)S(1)}, u32[]{:S(2)}, u32[]{:S(2)}) collective-permute-start(bf16[2,36,512]{2,1,0:T(8,128)(2,1)S(1)} %get-tuple-element.59.refs_6_), channel_id=1, source_target_pairs={{31,0},{30,1},{1,2},{0,3},{3,4},{2,5},{5,6},{4,7},{7,8},{6,9},{9,1... | collective-permute-start | bytes 221192 | tf_op jit(solution)/shard_map/ppermute | solution.py:382
  113.8 13.4 %collective-permute-start.34 = (bf16[4,2,36,512]{3,2,1,0:T(8,128)(2,1)S(1)}, bf16[4,2,36,512]{3,2,1,0:T(8,128)(2,1)S(1)}, u32[]{:S(2)}, u32[]{:S(2)}) collective-permute-start(bf16[4,2,36,512]{3,2,1,0:T(8,128)(2,1)S(1)} %get-tuple-element.65), channel_id=1, source_target_pairs={{30,0},{31,1},{0,2},{1,3},{2,4},{3,5},{4,6},{5,7},{6,8},{7,9},{8,1... | collective-permute-start | bytes 884744 | tf_op jit(solution)/shard_map/ppermute | solution.py:382
  119.7 1.4 %collective-permute-start.33 = (bf16[4,36,512]{2,1,0:T(8,128)(2,1)S(1)}, bf16[4,36,512]{2,1,0:T(8,128)(2,1)S(1)}, u32[]{:S(2)}, u32[]{:S(2)}) collective-permute-start(bf16[4,36,512]{2,1,0:T(8,128)(2,1)S(1)} %pad_maximum_fusion.1), channel_id=1, source_target_pairs={{1,0},{0,1},{3,2},{2,3},{5,4},{4,5},{7,6},{6,7},{9,8},{8,9},{11,10... | collective-permute-start | bytes 442376 | tf_op jit(solution)/shard_map/ppermute | solution.py:382

commit v12 on v10

--- a/solution.py
+++ b/solution.py
@@ -22,6 +22,7 @@
 GROUP = 8
 PART = 4
 WIDE = GROUP * HEAD
+FEED_FLOPS, FEED_BYTES = 1_000_000, 100_000
 Z_ORDER = (0, 2, 1, 3)
 ANY = pl.BlockSpec(memory_space=pl.ANY)
 NT = (((1,), (1,)), ((), ()))
@@ -166,25 +167,8 @@
     ]
 
 
-def rolled_window(place, row_windows, sides, ahead_ref, low_ref, ahead_low_ref):
-    (left_0, right_0), (left_1, right_1) = sides
-    first = place < row_windows
-    row = place % row_windows
-    following = jnp.minimum(row + 1, row_windows - 1)
-    wide = lambda quarter: quarter.astype(jnp.float32)
-    pick = lambda a, b: jnp.where(first, wide(a), wide(b))
-    low = lambda quarter, value: jnp.where(row == row_windows - 1, quarter, value)
-    quarters = [
-        pick(right_0[row, 1], right_1[row, 1]),
-        low(pick(low_ref[1], low_ref[3]), pick(right_0[following, 0], right_1[following, 0])),
-        pick(left_1[row, 1], ahead_ref[row, 1]),
-        low(pick(low_ref[2], ahead_low_ref[0]), pick(left_1[following, 0], ahead_ref[following, 0])),
-    ]
-    return jnp.concatenate(quarters, 0).astype(jnp.bfloat16)
-
-
 def attend_kernel(shifted, row_windows, count, *refs):
-    sources = 7 if shifted else 1
+    sources = 2 if shifted else 1
     x_refs, pieces = refs[:sources], refs[sources : sources + count]
     gain_ref, sharp_ref, ones_ref = refs[sources + count : sources + count + 3]
     allow_ref = refs[sources + count + 3] if shifted else None
@@ -196,14 +180,11 @@
         load_pieces(pieces, w_ref, stage_ref, sem)
 
     if shifted:
-        sides = (x_refs[0:2], x_refs[2:4])
-        tokens = jnp.concatenate(
-            [
-                rolled_window(pl.program_id(0) * held + window, row_windows, sides, *x_refs[4:])
-                for window in range(held)
-            ],
-            0,
-        )
+        quarters = []
+        for window in range(held):
+            for strip_ref in x_refs:
+                quarters += [strip_ref[2 * window + half].astype(jnp.float32) for half in range(2)]
+        tokens = jnp.concatenate(quarters, 0).astype(jnp.bfloat16)
     else:
         tokens = x_refs[0][...].reshape(held * CELLS, features)
     channel = lax.broadcasted_iota(jnp.int32, (WIDE, WIDE), 0) // HEAD
@@ -290,6 +271,7 @@
     skipped = columns[0] * row_windows // held
     whole = lambda shape: pl.BlockSpec(shape, lambda i: (0,) * len(shape))
     block = pl.BlockSpec((held, CELLS, features), lambda i: (i, 0, 0))
+    strip_block = pl.BlockSpec((2 * held, QUARTER, features), lambda i: (i, 0, 0))
     x_block = pl.BlockSpec((held, CELLS, features), lambda i: (i + skipped, 0, 0))
     ones = jnp.asarray(head_columns(), jnp.bfloat16)
     extra = (jnp.asarray(allowed_pairs()),) if shifted else ()
@@ -297,7 +279,7 @@
         functools.partial(attend_kernel, shifted, row_windows, len(pieces)),
         grid=(count // held,),
         out_shape=jax.ShapeDtypeStruct((count, CELLS, features), jnp.bfloat16),
-        in_specs=([whole(source.shape) for source in sources] if shifted else [x_block])
+        in_specs=([strip_block] * 2 if shifted else [x_block])
         + [ANY] * len(pieces)
         + [whole((1, features))] * 2
         + [whole(ones.shape)]
@@ -338,7 +320,7 @@
             for half in range(2):
                 start = window * CELLS + (side * 2 + half) * QUARTER
                 quarter = result[start : start + QUARTER].astype(jnp.bfloat16)
-                target[window, half] = quarter
+                target[2 * window + half] = quarter
                 if half == edge_half and window == edge_window % held:
 
                     @pl.when(pl.program_id(0) == edge_window // held)
@@ -349,11 +331,11 @@
 def feed(windows, column, count, pieces, gain, hidden_size, edge, after=(), held=2):
     _, cells, features = windows.shape
     block = pl.BlockSpec((held, cells, features), lambda i: (i + column * count // held, 0, 0))
-    side = pl.BlockSpec((held, 2, QUARTER, features), lambda i: (i, 0, 0, 0))
+    side = pl.BlockSpec((2 * held, QUARTER, features), lambda i: (i, 0, 0))
     return pl.pallas_call(
         functools.partial(feed_kernel, len(pieces), hidden_size, 512, edge),
         grid=(count // held,),
-        out_shape=[jax.ShapeDtypeStruct((count, 2, QUARTER, features), jnp.bfloat16)] * 2
+        out_shape=[jax.ShapeDtypeStruct((2 * count, QUARTER, features), jnp.bfloat16)] * 2
         + [jax.ShapeDtypeStruct((2, QUARTER, features), jnp.bfloat16)],
         in_specs=[block]
         + [ANY] * len(pieces)
@@ -363,8 +345,8 @@
         scratch_shapes=load_scratch(pieces, features, 2 * hidden_size),
         compiler_params=pltpu.CompilerParams(vmem_limit_bytes=24 * 2**20),
         cost_estimate=pl.CostEstimate(
-            flops=8 * count * cells * features * hidden_size,
-            bytes_accessed=8_000_000,
+            flops=FEED_FLOPS,
+            bytes_accessed=FEED_BYTES,
             transcendentals=0,
         ),
     )(windows, *pieces, gain, *after)
@@ -388,21 +370,34 @@
     return arranged.reshape(-1, CELLS, features)
 
 
-def strip(quarters):
+def strips_kernel(picks, *refs):
+    sources, outs = refs[: len(refs) - len(picks)], refs[len(refs) - len(picks) :]
+    for pick, target in zip(picks, outs):
+        place = 0
+        for source, first, count in pick:
+            target[place : place + count] = sources[source][first : first + count]
+            place += count
+
+
+def strips(sources, picks):
+    shape = sources[0].shape[1:]
+    held = pl.BlockSpec(memory_space=pltpu.VMEM)
+    return pl.pallas_call(
+        functools.partial(strips_kernel, picks),
+        out_shape=[
+            jax.ShapeDtypeStruct((sum(count for _, _, count in pick),) + shape, jnp.bfloat16)
+            for pick in picks
+        ],
+        in_specs=[held] * len(sources),
+        compiler_params=pltpu.CompilerParams(vmem_limit_bytes=10 * 2**20),
+    )(*sources)
+
+
+def from_strips(quarters, cols, rows):
     features = quarters.shape[-1]
     c, r = WLON // 2, WLAT // 2
-    arranged = quarters.reshape(-1, c, r, LEVELS, features).transpose(1, 0, 2, 3, 4)
-    return arranged.reshape(c, -1, LEVELS, features)
-
-
-def back_in_place(sides, behind, above, high):
-    features = behind.shape[-1]
-    flat = lambda side: side.reshape(-1, QUARTER, features)[:-1]
-    c, r = WLON // 2, WLAT // 2
-    own = jnp.concatenate([strip(flat(side)) for side in sides], 0)
-    tops = jnp.concatenate([strip(low[None]) for low in above], 0)
-    first = jnp.concatenate([strip(high[None]), strip(flat(behind))], 1)
-    return jnp.concatenate([first, jnp.concatenate([tops, own], 1)], 0)
+    arranged = quarters.reshape(cols // c, rows // r, c, r, LEVELS, features)
+    return arranged.transpose(0, 2, 1, 3, 4, 5).reshape(cols, rows, LEVELS, features)
 
 
 def per_device(tokens, qkv_weight, out_weight, up_weight, down_weight, norm_gain, logit_scale):
@@ -435,47 +430,69 @@
         (feed_pair,) = join([[feed_own, across_z(feed_own, 2)]])
         (last_pair,) = join([[last_own, send(last_own, beside)]])
         (column,) = join([[pair, across_z(pair, 1)]], (), (feed_pair, last_pair))
-        pieces = whole_pieces(column, [send(column, way) for way in (beside, across, corner)])
-        (last_four,) = join([[last_pair, across_z(last_pair, 2)]])
+        received = [send(column, way) for way in (beside, across, corner)]
+        sent = [tied(column, received[0])] + received
+        pieces = [column] + received + [send(part, swap) for part in sent]
         (feed_column,) = join([[feed_pair, across_z(feed_pair, 1)]])
         received = [send(feed_column, way) for way in (beside, across)]
+        last_other = across_z(last_pair, 2)
+        middle_0 = attention(0, [windows], (0,), pieces, (feed_column,))
+        received.append(send(tied(received[0], (middle_0, last_other)), across))
+        (last_four,) = join([[last_pair, last_other]], (), (middle_0,))
         last_other = across_z(last_four, 1)
-        middle = attention(0, [windows], (0, 1), pieces, (feed_column, last_four))
-        received.append(send(tied(received[0], middle), across))
-        sent = [feed_column] + tied(received[:2], (middle, last_other)) + [tied(received[2], middle)]
-        feed_pieces = [feed_column] + received + [send(part, swap) for part in sent]
-        column, last_column = join([[last_four, last_other]], (), (middle,), widths)
-        received = send(column, across)
-        left_0, right_0, low_0 = forward(0, middle, 0, feed_pieces, low_edge, (column,))
-        ahead, ahead_low = shift_from(left_0, 1, 0), shift_from(low_0, 1, 1)
-        left_1, right_1, low_1 = forward(0, middle, 1, feed_pieces, low_edge, (low_0, received))
-        pieces = [column, received]
-        pieces += [send(column, swap), send(tied(received, low_1), swap)]
-        last_received = send(tied(last_column, received), across)
+        middle_1 = attention(0, [windows], (1,), pieces, (middle_0, last_four))
+        swapped = [send(part, swap) for part in [feed_column] + tied(received[:2], middle_0)]
+        swapped.append(send(tied(received[2], (middle_1, *swapped)), swap))
+        feed_pieces = [feed_column] + received + swapped
     else:
         gathered = []
         for block in range(2):
             for pair in (weights[:2], weights[2:]):
                 chunk = jnp.concatenate([weight[block] for weight in pair], 1)
                 gathered.append([lax.all_gather(chunk, "lon", axis=0, tiled=True)])
-        first_pieces, feed_pieces, pieces, last_pieces = gathered
-        middle = attention(0, [windows], (0, 1), first_pieces)
-        left_0, right_0, low_0 = forward(0, middle, 0, feed_pieces, low_edge)
-        left_1, right_1, low_1 = forward(0, middle, 1, feed_pieces, low_edge)
-        ahead, ahead_low = shift_from(left_0, 1, 0), shift_from(low_0, 1, 1)
-    below = shift_from(tied(jnp.concatenate([low_0, low_1], 0), (ahead, ahead_low)), 0, 1)
-    sources = [left_0, right_0, left_1, right_1, ahead, below, ahead_low]
-    middle = attention(1, sources, (0, 1), pieces)
+        pieces, feed_pieces, last_pieces, final_pieces = gathered
+        middle_0 = attention(0, [windows], (0,), pieces)
+        middle_1 = attention(0, [windows], (1,), pieces)
+    left_0, right_0, low_0 = forward(0, middle_0, 0, feed_pieces, low_edge)
+    below_0 = shift_from(low_0, 0, 1)
+    size = left_0.shape[0]
+    (ahead,) = strips([left_0, below_0], [[(0, 1, size - 1), (1, 0, 1)]])
+    ahead = shift_from(ahead, 1, 0)
+    after = (below_0,)
     if relay:
-        last_pieces = [last_column, last_received]
-        last_pieces += [send(last_column, swap), send(tied(last_received, middle), swap)]
-    left_1, right_1, high_1 = forward(1, middle, 1, last_pieces, high_edge)
-    behind = shift_from(right_1, -1, 0)
-    behind_high = shift_from(high_1, -1, -1)
-    left_0, right_0, high_0 = forward(1, middle, 0, last_pieces, high_edge, (high_1,))
-    above = shift_from(tied(jnp.concatenate([high_0, high_1], 0), behind_high), 0, -1)
-    sides, above, behind_high = tied(((left_0, right_0, left_1), above, behind_high), behind)
-    return back_in_place(sides, behind, (above[0], above[1], above[2]), behind_high[1])
+        last_column, final_column = join([[last_four, last_other]], (), (low_0,), widths)
+        last_received = send(last_column, across)
+        after += (last_column,)
+    left_1, right_1, low_1 = forward(0, middle_1, 0, feed_pieces, low_edge, after)
+    below_1 = shift_from(low_1, 0, 1)
+    if relay:
+        last_pieces = [last_column, last_received, send(last_column, swap)]
+        last_pieces.append(send(tied(last_received, low_1), swap))
+        final_received = send(tied(final_column, last_received), across)
+    lefts = strips(
+        [right_0, left_1, right_1, below_0, below_1],
+        [
+            [(0, 1, size - 1), (3, 1, 1)],
+            [(1, 1, size - 1), (4, 0, 1)],
+            [(2, 1, size - 1), (4, 1, 1)],
+        ],
+    )
+    middle_0 = attention(1, lefts[:2], (0,), last_pieces)
+    middle_1 = attention(1, [lefts[2], ahead], (1,), last_pieces, (middle_0,))
+    if relay:
+        final_pieces = [final_column, final_received, send(final_column, swap)]
+        final_pieces.append(send(tied(final_received, middle_1), swap))
+    left_1, right_1, high_1 = forward(1, middle_1, 0, final_pieces, high_edge)
+    above_1 = shift_from(high_1, 0, -1)
+    (behind,) = strips([above_1, right_1], [[(0, 1, 1), (1, 0, size - 1)]])
+    behind = shift_from(behind, -1, 0)
+    left_0, right_0, high_0 = forward(1, middle_0, 0, final_pieces, high_edge, (above_1,))
+    above_0 = shift_from(high_0, 0, -1)
+    picks = [(0, 0, size)]
+    for place, (low, quarter) in enumerate(((4, 0), (4, 1), (5, 0))):
+        picks += [(low, quarter, 1), (place + 1, 0, size - 1)]
+    (mixed,) = strips([behind, left_0, right_0, left_1, above_0, above_1], [picks])
+    return from_strips(mixed, cols, rows)
 
 
 def solution(mesh):

time: 139 us -> 131 us (0.942)
  waiting for transfers between devices: 51.7 us -> 43.6 us
  other arithmetic: 3.03 us -> 0.09 us
    ppermute x6, waiting for transfers between devices: 15.8 us -> 10.4 us  [shift_from(): return lax.ppermute(block, ('lon', 'lat'), pairs)]
    concatenate x3 -> x0, other arithmetic: 2.94 us -> none  [the longest x1 2.9 us: back_in_place(): return jnp.concatenate([first, jnp.concatenate([tops, own], 1)], 0)]
    ppermute x27, waiting for transfers between devices: 35.9 us -> 33.2 us  [send(): return lax.ppermute(block, ('lon', 'lat'), pairs)]
    transpose x0 -> x1, local copies, waits for them, and re-layouts: none -> 2.23 us  [from_strips(): arranged.transpose(0, 2, 1, 3, 4, 5).reshape(cols, rows, LEVELS, features)]
    pallas_call x2 -> x4, Pallas kernels: 26.7 us -> 27.5 us  [attend(): pl.pallas_call(functools.partial(attend_kernel, shifted, row_windows, len...]
  transfers between devices with their start and end apart: 33 -> 33, of which waited for: 15 -> 15; matrix products, arithmetic and copies ran while one was open for 1% -> 1% of each run, Pallas kernels for 30% -> 32%
where the time goes in v12:
time: 131 us
  Pallas kernels  47.2 us (36%)
  waiting for transfers between devices  43.6 us (33%)
  starting transfers between devices  31.9 us (24%)
  local copies, waits for them, and re-layouts  7.6 us (6%)
    ppermute x27, waiting for transfers between devices, send(): return lax.ppermute(block, ('lon', 'lat'), pairs)  33.2 us
    pallas_call x4, Pallas kernels, attend(): pl.pallas_call(functools.partial(attend_kernel, shifted, row_windows, len...  27.5 us
    ppermute x27, starting transfers between devices, send(): return lax.ppermute(block, ('lon', 'lat'), pairs)  23.3 us
    pallas_call x4, Pallas kernels, feed(): pl.pallas_call(functools.partial(feed_kernel, len(pieces), hidden_size, 5...  19.2 us
    ppermute x6, waiting for transfers between devices, shift_from(): return lax.ppermute(block, ('lon', 'lat'), pairs)  10.4 us
    ppermute x6, starting transfers between devices, shift_from(): return lax.ppermute(block, ('lon', 'lat'), pairs)  8.59 us
    unnamed x20, local copies, waits for them, and re-layouts  3.7 us
  transfers between devices with their start and end apart: 33, of which 15 were waited for; matrix products, arithmetic and copies ran while one was open for 1% of the time, Pallas kernels for 32%

profile of v12, /device:TPU:0, one launch (start us, length us, event | category | flops | bytes accessed | tf_op | source)
XLA Modules:
  0.0 130.7 jit_solution(12515560708866535215)
XLA Ops:
  0.0 0.9 copy-done.2
  0.9 0.8 copy-done.3
  1.8 4.0 %collective-permute-start = (bf16[1,16,2048]{2,1,0:T(8,128)(2,1)S(1)}, bf16[1,16,2048]{2,1,0:T(8,128)(2,1)S(1)}, u32[]{:S(2)}, u32[]{:S(2)}) collective-permute-start(bf16[1,16,2048]{2,1,0:T(8,128)(2,1)S(1)} %shard_map.136.refs_0_), channel_id=1, source_target_pairs={{0,16},{1,17},{2,18},{3,19},{4,20},{5,21},{6,22},{7,23},{8,24},{9,... | collective-permute-start | bytes 196616 | tf_op jit(solution)/shard_map/ppermute | solution.py:97
  5.8 0.9 copy-done
  6.8 0.9 copy-done.1
  7.7 1.6 %collective-permute-start.3 = (bf16[1,16,6144]{2,1,0:T(8,128)(2,1)S(1)}, bf16[1,16,6144]{2,1,0:T(8,128)(2,1)S(1)}, u32[]{:S(2)}, u32[]{:S(2)}) collective-permute-start(bf16[1,16,6144]{2,1,0:T(8,128)(2,1)S(1)} %get-tuple-element.33.refs_0_), channel_id=1, source_target_pairs={{0,2},{1,5},{2,0},{3,7},{4,6},{5,1},{6,4},{7,3},{8,10},{9,13},{10,... | collective-permute-start | bytes 589832 | tf_op jit(solution)/shard_map/ppermute | solution.py:97
  9.3 0.3 collective-permute-start.2
  9.6 0.8 copy.26
  10.5 0.5 reshape.15.refs_2_.refs_0_
  11.0 0.0 copy-start.7
  11.0 1.6 %collective-permute-start.1 = (bf16[2,16,2048]{2,1,0:T(8,128)(2,1)S(1)}, bf16[2,16,2048]{2,1,0:T(8,128)(2,1)S(1)}, u32[]{:S(2)}, u32[]{:S(2)}) collective-permute-start(bf16[2,16,2048]{2,1,0:T(8,128)(2,1)S(1)} %shard_map.137.refs_0_), channel_id=1, source_target_pairs={{0,8},{1,9},{2,10},{3,11},{4,12},{5,13},{6,14},{7,15},{8,0},{9,1},... | collective-permute-start | bytes 393224 | tf_op jit(solution)/shard_map/ppermute | solution.py:97
  12.7 5.0 %collective-permute-done.2.refs_1_ = bf16[1,16,4096]{2,1,0:T(8,128)(2,1)S(1)} collective-permute-done((bf16[1,16,4096]{2,1,0:T(8,128)(2,1)S(1)}, bf16[1,16,4096]{2,1,0:T(8,128)(2,1)S(1)}, u32[]{:S(2)}, u32[]{:S(2)}) %collective-permute-start.2) | collective-permute-done | bytes 131104 | tf_op jit(solution)/shard_map/ppermute | solution.py:97
  17.8 0.0 copy-start.4
  17.8 1.6 %collective-permute-start.4 = (bf16[4,16,2048]{2,1,0:T(8,128)(2,1)S(1)}, bf16[4,16,2048]{2,1,0:T(8,128)(2,1)S(1)}, u32[]{:S(2)}, u32[]{:S(2)}) collective-permute-start(bf16[4,16,2048]{2,1,0:T(8,128)(2,1)S(1)} %shard_map.141.refs_1_), channel_id=1, source_target_pairs={{0,2},{1,5},{2,0},{3,7},{4,6},{5,1},{6,4},{7,3},{8,10},{9,13},{10,... | collective-permute-start | bytes 786440 | tf_op jit(solution)/shard_map/ppermute | solution.py:97
  19.4 0.9 collective-permute-start.6
  20.3 1.1 collective-permute-start.5
  21.4 0.1 multiply_reduce_fusion
  21.5 0.5 collective-permute-start.11
  21.9 5.2 %collective-permute-done.4.refs_2_ = bf16[4,16,2048]{2,1,0:T(8,128)(2,1)S(1)} collective-permute-done((bf16[4,16,2048]{2,1,0:T(8,128)(2,1)S(1)}, bf16[4,16,2048]{2,1,0:T(8,128)(2,1)S(1)}, u32[]{:S(2)}, u32[]{:S(2)}) %collective-permute-start.4) | collective-permute-done | bytes 262176 | tf_op jit(solution)/shard_map/ppermute | solution.py:97
  27.1 0.5 collective-permute-start.8
  27.6 4.5 %collective-permute-done.6.refs_4_ = bf16[4,16,2048]{2,1,0:T(8,128)(2,1)S(1)} collective-permute-done((bf16[4,16,2048]{2,1,0:T(8,128)(2,1)S(1)}, bf16[4,16,2048]{2,1,0:T(8,128)(2,1)S(1)}, u32[]{:S(2)}, u32[]{:S(2)}) %collective-permute-start.6) | collective-permute-done | bytes 262176 | tf_op jit(solution)/shard_map/ppermute | solution.py:97
  32.1 0.5 collective-permute-start.9
  32.6 3.1 %collective-permute-start.14 = (bf16[2,16,6144]{2,1,0:T(8,128)(2,1)S(1)}, bf16[2,16,6144]{2,1,0:T(8,128)(2,1)S(1)}, u32[]{:S(2)}, u32[]{:S(2)}) collective-permute-start(bf16[2,16,6144]{2,1,0:T(8,128)(2,1)S(1)} %shard_map.140.refs_3_.refs_0_), channel_id=1, source_target_pairs={{0,16},{1,17},{2,18},{3,19},{4,20},{5,21},{6,22},{7,23},{8,24},{9,... | collective-permute-start | bytes 1179656 | tf_op jit(solution)/shard_map/ppermute | solution.py:97
  35.8 0.1 collective-permute-start.16
  35.9 0.8 collective-permute-start.13
  36.8 1.5 %collective-permute-start.12 = (bf16[4,16,4096]{2,1,0:T(8,128)(2,1)S(1)}, bf16[4,16,4096]{2,1,0:T(8,128)(2,1)S(1)}, u32[]{:S(2)}, u32[]{:S(2)}) collective-permute-start(bf16[4,16,4096]{2,1,0:T(8,128)(2,1)S(1)} %shard_map.142.refs_12_.refs_1_), channel_id=1, source_target_pairs={{0,2},{1,5},{2,0},{3,7},{4,6},{5,1},{6,4},{7,3},{8,10},{9,13},{10,... | collective-permute-start | bytes 1572872 | tf_op jit(solution)/shard_map/ppermute | solution.py:97
  38.3 6.9 %shard_map.143.refs_2_.refs_12_.refs_0_ = bf16[4,144,512]{2,1,0:T(8,128)(2,1)S(1)} custom-call(bf16[8,144,512]{2,1,0:T(8,128)(2,1)S(1)} %reshape.15.refs_2_.refs_0_, bf16[4,16,2048]{2,1,0:T(8,128)(2,1)S(1)} %shard_map.141.refs_1_, bf16[4,16,2048]{2,1,0:T(8,128)(2,1)S(1)} %collective-permute-done.4.refs_2_, ...), custom_call_target="tpu_custom_call" | custom-call | flops 8000000000 | bytes 6000000 | tf_op jit(solution)/shard_map/pallas_call | solution.py:278
  45.2 8.3 %collective-permute-done.14.refs_1_ = bf16[2,16,6144]{2,1,0:T(8,128)(2,1)S(1)} collective-permute-done((bf16[2,16,6144]{2,1,0:T(8,128)(2,1)S(1)}, bf16[2,16,6144]{2,1,0:T(8,128)(2,1)S(1)}, u32[]{:S(2)}, u32[]{:S(2)}) %collective-permute-start.14) | collective-permute-done | bytes 393248 | tf_op jit(solution)/shard_map/ppermute | solution.py:97
  53.5 0.1 shard_map.144.refs_13_.refs_0_
  53.6 0.8 collective-permute-start.21
  54.4 0.8 collective-permute-start.15
  55.1 0.5 collective-permute-start.18
  55.6 6.9 %shard_map.145.refs_0_ = bf16[4,144,512]{2,1,0:T(8,128)(2,1)S(1)} custom-call(bf16[8,144,512]{2,1,0:T(8,128)(2,1)S(1)} %reshape.15.refs_2_.refs_0_, bf16[4,16,2048]{2,1,0:T(8,128)(2,1)S(1)} %shard_map.141.refs_1_, bf16[4,16,2048]{2,1,0:T(8,128)(2,1)S(1)} %collective-permute-done.4.refs_2_, bf16[4,16,2048]{2,1,0:T(8,128)(2,1)S(1)} %collective-permute-done.5.refs_3_, ...), custom_call_target="tpu_custom_call" | custom-call | flops 8000000000 | bytes 6000000 | tf_op jit(solution)/shard_map/pallas_call | solution.py:278
  62.6 1.0 collective-permute-done.15.refs_4_
  63.6 1.9 %collective-permute-done.19.refs_8_ = bf16[4,16,4096]{2,1,0:T(8,128)(2,1)S(1)} collective-permute-done((bf16[4,16,4096]{2,1,0:T(8,128)(2,1)S(1)}, bf16[4,16,4096]{2,1,0:T(8,128)(2,1)S(1)}, u32[]{:S(2)}, u32[]{:S(2)}) %collective-permute-start.19) | collective-permute-done | bytes 524320 | tf_op jit(solution)/shard_map/ppermute | solution.py:97
  65.5 4.8 %shard_map.146 = (bf16[8,36,512]{2,1,0:T(8,128)(2,1)S(1)}, bf16[8,36,512]{2,1,0:T(8,128)(2,1)S(1)}, bf16[2,36,512]{2,1,0:T(8,128)(2,1)S(1)}) custom-call(bf16[4,144,512]{2,1,0:T(8,128)(2,1)S(1)} %shard_map.143.refs_2_.refs_12_.refs_0_, bf16[4,16,4096]{2,1,0:T(8,128)(2,1)S(1)} %shard_map.142.refs_12_.refs_1_, ...), custom_call_target="tpu_custom_call" | custom-call | flops 1000000 | bytes 100000 | tf_op jit(solution)/shard_map/pallas_call | solution.py:335
  70.3 2.3 %collective-permute-done.21.refs_1_ = bf16[4,16,6144]{2,1,0:T(8,128)(2,1)S(1)} collective-permute-done((bf16[4,16,6144]{2,1,0:T(8,128)(2,1)S(1)}, bf16[4,16,6144]{2,1,0:T(8,128)(2,1)S(1)}, u32[]{:S(2)}, u32[]{:S(2)}) %collective-permute-start.21) | collective-permute-done | bytes 786464 | tf_op jit(solution)/shard_map/ppermute | solution.py:97
  72.6 0.1 shard_map.147
  72.7 0.8 collective-permute-start.24
  73.5 0.5 collective-permute-start.25
  74.0 0.8 collective-permute-done.20.refs_10_.refs_3_.refs_1_
  74.8 4.8 %shard_map.148 = (bf16[8,36,512]{2,1,0:T(8,128)(2,1)S(1)}, bf16[8,36,512]{2,1,0:T(8,128)(2,1)S(1)}, bf16[2,36,512]{2,1,0:T(8,128)(2,1)S(1)}) custom-call(bf16[4,144,512]{2,1,0:T(8,128)(2,1)S(1)} %shard_map.145.refs_0_, bf16[4,16,4096]{2,1,0:T(8,128)(2,1)S(1)} %shard_map.142.refs_12_.refs_1_, bf16[4,16,4096]{2,1,0:T(8,128)(2,1)S(1)} %collective-permute-done.12.refs_2_, ...), custom_call_target="tpu_custom_call" | custom-call | flops 1000000 | bytes 100000 | tf_op jit(solution)/shard_map/pallas_call | solution.py:335
  79.7 2.3 %collective-permute-done.24.refs_3_ = bf16[8,16,2048]{2,1,0:T(8,128)(2,1)S(1)} collective-permute-done((bf16[8,16,2048]{2,1,0:T(8,128)(2,1)S(1)}, bf16[8,16,2048]{2,1,0:T(8,128)(2,1)S(1)}, u32[]{:S(2)}, u32[]{:S(2)}) %collective-permute-start.24) | collective-permute-done | bytes 524320 | tf_op jit(solution)/shard_map/ppermute | solution.py:97
  81.9 0.5 collective-permute-start.22
  82.5 5.3 %collective-permute-start.23 = (bf16[8,36,512]{2,1,0:T(8,128)(2,1)S(1)}, bf16[8,36,512]{2,1,0:T(8,128)(2,1)S(1)}, u32[]{:S(2)}, u32[]{:S(2)}) collective-permute-start(bf16[8,36,512]{2,1,0:T(8,128)(2,1)S(1)} %shard_map.150), channel_id=1, source_target_pairs={{2,0},{3,1},{4,2},{5,3},{6,4},{7,5},{8,6},{9,7},{10,8},{11,9},{12,... | collective-permute-start | bytes 884744 | tf_op jit(solution)/shard_map/ppermute | solution.py:362
  87.7 0.1 shard_map.149
  87.8 0.1 collective-permute-start.27
  87.9 6.9 %shard_map.151.refs_10_.refs_0_ = bf16[4,144,512]{2,1,0:T(8,128)(2,1)S(1)} custom-call(bf16[8,36,512]{2,1,0:T(8,128)(2,1)S(1)} %get-tuple-element.48.refs_0_, bf16[8,36,512]{2,1,0:T(8,128)(2,1)S(1)} %get-tuple-element.49.refs_1_, bf16[8,16,2048]{2,1,0:T(8,128)(2,1)S(1)} %get-tuple-element.41.refs_11_.refs_2_, ...), custom_call_target="tpu_custom_call" | custom-call | flops 8000000000 | bytes 6000000 | tf_op jit(solution)/shard_map/pallas_call | solution.py:278
  94.8 0.6 collective-permute-done.23.refs_1_
  95.4 6.8 %shard_map.152.refs_0_ = bf16[4,144,512]{2,1,0:T(8,128)(2,1)S(1)} custom-call(bf16[8,36,512]{2,1,0:T(8,128)(2,1)S(1)} %get-tuple-element.45.refs_0_, bf16[8,36,512]{2,1,0:T(8,128)(2,1)S(1)} %collective-permute-done.23.refs_1_, bf16[8,16,2048]{2,1,0:T(8,128)(2,1)S(1)} %get-tuple-element.41.refs_11_.refs_2_, ...), custom_call_target="tpu_custom_call" | custom-call | flops 8000000000 | bytes 6000000 | tf_op jit(solution)/shard_map/pallas_call | solution.py:278
  102.2 0.5 collective-permute-done.27.refs_2_
  102.7 1.7 %collective-permute-start.29 = (bf16[8,16,4096]{2,1,0:T(8,128)(2,1)S(1)}, bf16[8,16,4096]{2,1,0:T(8,128)(2,1)S(1)}, u32[]{:S(2)}, u32[]{:S(2)}) collective-permute-start(bf16[8,16,4096]{2,1,0:T(8,128)(2,1)S(1)} %collective-permute-done.27.refs_2_), channel_id=1, source_target_pairs={{0,1},{1,0},{2,3},{3,2},{4,5},{5,4},{6,7},{7,6},{8,9},{9,8},{10,11... | collective-permute-start | bytes 3145736 | tf_op jit(solution)/shard_map/ppermute | solution.py:97
  104.3 2.3 %collective-permute-done.29.refs_4_ = bf16[8,16,4096]{2,1,0:T(8,128)(2,1)S(1)} collective-permute-done((bf16[8,16,4096]{2,1,0:T(8,128)(2,1)S(1)}, bf16[8,16,4096]{2,1,0:T(8,128)(2,1)S(1)}, u32[]{:S(2)}, u32[]{:S(2)}) %collective-permute-start.29) | collective-permute-done | bytes 1048608 | tf_op jit(solution)/shard_map/ppermute | solution.py:97
  106.6 4.7 %shard_map.153 = (bf16[8,36,512]{2,1,0:T(8,128)(2,1)S(1)}, bf16[8,36,512]{2,1,0:T(8,128)(2,1)S(1)}, bf16[2,36,512]{2,1,0:T(8,128)(2,1)S(1)}) custom-call(bf16[4,144,512]{2,1,0:T(8,128)(2,1)S(1)} %shard_map.152.refs_0_, bf16[8,16,4096]{2,1,0:T(8,128)(2,1)S(1)} %get-tuple-element.51.refs_1_, bf16[8,16,4096]{2,1,0:T(8,128)(2,1)S(1)} %collective-permute-done.27.refs_2_, ...), custom_call_target="tpu_custom_call" | custom-call | flops 1000000 | bytes 100000 | tf_op jit(solution)/shard_map/pallas_call | solution.py:335
  111.4 0.4 collective-permute-start.30
  111.8 0.9 collective-permute-done.30.refs_0_.refs_6_.refs_5_
  112.8 2.2 %collective-permute-start.31 = (bf16[8,36,512]{2,1,0:T(8,128)(2,1)S(1)}, bf16[8,36,512]{2,1,0:T(8,128)(2,1)S(1)}, u32[]{:S(2)}, u32[]{:S(2)}) collective-permute-start(bf16[8,36,512]{2,1,0:T(8,128)(2,1)S(1)} %shard_map.154), channel_id=1, source_target_pairs={{30,0},{31,1},{0,2},{1,3},{2,4},{3,5},{4,6},{5,7},{6,8},{7,9},{8,1... | collective-permute-start | bytes 884744 | tf_op jit(solution)/shard_map/ppermute | solution.py:362
  115.0 4.8 %shard_map.155 = (bf16[8,36,512]{2,1,0:T(8,128)(2,1)S(1)}, bf16[8,36,512]{2,1,0:T(8,128)(2,1)S(1)}, bf16[2,36,512]{2,1,0:T(8,128)(2,1)S(1)}) custom-call(bf16[4,144,512]{2,1,0:T(8,128)(2,1)S(1)} %shard_map.151.refs_10_.refs_0_, bf16[8,16,4096]{2,1,0:T(8,128)(2,1)S(1)} %get-tuple-element.51.refs_1_, bf16[8,16,4096]{2,1,0:T(8,128)(2,1)S(1)} %collective-permute-done.27.refs_2_, ...), custom_call_target="tpu_custom_call" | custom-call | flops 1000000 | bytes 100000 | tf_op jit(solution)/shard_map/pallas_call | solution.py:335
  119.8 0.1 collective-permute-start.32
  119.9 1.2 collective-permute-done.32.refs_4_
  121.1 6.9 %collective-permute-done.31.refs_0_ = bf16[8,36,512]{2,1,0:T(8,128)(2,1)S(1)} collective-permute-done((bf16[8,36,512]{2,1,0:T(8,128)(2,1)S(1)}, bf16[8,36,512]{2,1,0:T(8,128)(2,1)S(1)}, u32[]{:S(2)}, u32[]{:S(2)}) %collective-permute-start.31) | collective-permute-done | bytes 294944 | tf_op jit(solution)/shard_map/ppermute | solution.py:362
  128.0 0.1 shard_map.156
  128.1 0.4 copy.23
  128.4 2.2 %copy.24 = bf16[4,6,8,3,2,512]{5,4,3,2,1,0:T(2,128)(2,1)} copy(bf16[4,6,8,3,2,512]{5,2,0,4,3,1:T(8,128)(2,1)S(1)} %bitcast.16) | data formatting | bytes 2359296 | tf_op jit(solution)/shard_map/transpose | solution.py:400
  (50 shorter events, 0.3 us)
Async XLA Ops:
  0.0 0.9 copy-start.2
  0.9 0.8 copy-start.3
  1.8 9.2 %collective-permute-start = (bf16[1,16,2048]{2,1,0:T(8,128)(2,1)S(1)}, bf16[1,16,2048]{2,1,0:T(8,128)(2,1)S(1)}, u32[]{:S(2)}, u32[]{:S(2)}) collective-permute-start(bf16[1,16,2048]{2,1,0:T(8,128)(2,1)S(1)} %shard_map.136.refs_0_), channel_id=1, source_target_pairs={{0,16},{1,17},{2,18},{3,19},{4,20},{5,21},{6,22},{7,23},{8,24},{9,... | collective-permute-start | bytes 196616 | tf_op jit(solution)/shard_map/ppermute | solution.py:97
  5.8 0.9 copy-start
  6.8 0.9 copy-start.1
  7.7 1.9 %copy-start.6 = (bf16[24,24,2,512]{3,2,1,0:T(2,128)(2,1)S(1)}, bf16[24,24,2,512]{3,2,1,0:T(2,128)(2,1)}, u32[]{:S(2)}) copy-start(bf16[24,24,2,512]{3,2,1,0:T(2,128)(2,1)} %param.14) | copy-start | bytes 3538948
  7.7 10.0 %collective-permute-start.3 = (bf16[1,16,6144]{2,1,0:T(8,128)(2,1)S(1)}, bf16[1,16,6144]{2,1,0:T(8,128)(2,1)S(1)}, u32[]{:S(2)}, u32[]{:S(2)}) collective-permute-start(bf16[1,16,6144]{2,1,0:T(8,128)(2,1)S(1)} %get-tuple-element.33.refs_0_), channel_id=1, source_target_pairs={{0,2},{1,5},{2,0},{3,7},{4,6},{5,1},{6,4},{7,3},{8,10},{9,13},{10,... | collective-permute-start | bytes 589832 | tf_op jit(solution)/shard_map/ppermute | solution.py:97
  9.3 8.4 %collective-permute-start.2 = (bf16[1,16,4096]{2,1,0:T(8,128)(2,1)S(1)}, bf16[1,16,4096]{2,1,0:T(8,128)(2,1)S(1)}, u32[]{:S(2)}, u32[]{:S(2)}) collective-permute-start(bf16[1,16,4096]{2,1,0:T(8,128)(2,1)S(1)} %get-tuple-element.32.refs_0_), channel_id=1, source_target_pairs={{0,16},{1,17},{2,18},{3,19},{4,20},{5,21},{6,22},{7,23},{8,24},{9,... | collective-permute-start | bytes 393224 | tf_op jit(solution)/shard_map/ppermute | solution.py:97
  11.0 10.4 %copy-start.7 = (f32[16,512]{1,0:T(8,128)S(1)}, f32[16,512]{1,0:T(8,128)}, u32[]{:S(2)}) copy-start(f32[16,512]{1,0:T(8,128)} %constant.8.clone) | copy-start | bytes 98308
  11.0 10.4 %copy-start.9 = (f32[2,16]{1,0:T(2,128)S(1)}, f32[2,16]{1,0:T(2,128)}, u32[]{:S(2)}) copy-start(f32[2,16]{1,0:T(2,128)} %param.20) | copy-start | bytes 388
  11.0 21.6 %copy-start.8 = (f32[2,2,512]{2,1,0:T(2,128)S(1)}, f32[2,2,512]{2,1,0:T(2,128)}, u32[]{:S(2)}) copy-start(f32[2,2,512]{2,1,0:T(2,128)} %param.19) | copy-start | bytes 24580
  11.0 6.8 %collective-permute-start.1 = (bf16[2,16,2048]{2,1,0:T(8,128)(2,1)S(1)}, bf16[2,16,2048]{2,1,0:T(8,128)(2,1)S(1)}, u32[]{:S(2)}, u32[]{:S(2)}) collective-permute-start(bf16[2,16,2048]{2,1,0:T(8,128)(2,1)S(1)} %shard_map.137.refs_0_), channel_id=1, source_target_pairs={{0,8},{1,9},{2,10},{3,11},{4,12},{5,13},{6,14},{7,15},{8,0},{9,1},... | collective-permute-start | bytes 393224 | tf_op jit(solution)/shard_map/ppermute | solution.py:97
  17.8 20.5 %copy-start.4 = (bf16[640,256]{1,0:T(8,128)(2,1)S(1)}, bf16[640,256]{1,0:T(8,128)(2,1)}, u32[]{:S(2)}) copy-start(bf16[640,256]{1,0:T(8,128)(2,1)} %constant.9.clone.refs_11_.refs_8_) | copy-start | bytes 983044
  17.8 9.3 %collective-permute-start.4 = (bf16[4,16,2048]{2,1,0:T(8,128)(2,1)S(1)}, bf16[4,16,2048]{2,1,0:T(8,128)(2,1)S(1)}, u32[]{:S(2)}, u32[]{:S(2)}) collective-permute-start(bf16[4,16,2048]{2,1,0:T(8,128)(2,1)S(1)} %shard_map.141.refs_1_), channel_id=1, source_target_pairs={{0,2},{1,5},{2,0},{3,7},{4,6},{5,1},{6,4},{7,3},{8,10},{9,13},{10,... | collective-permute-start | bytes 786440 | tf_op jit(solution)/shard_map/ppermute | solution.py:97
  19.4 12.7 %collective-permute-start.6 = (bf16[4,16,2048]{2,1,0:T(8,128)(2,1)S(1)}, bf16[4,16,2048]{2,1,0:T(8,128)(2,1)S(1)}, u32[]{:S(2)}, u32[]{:S(2)}) collective-permute-start(bf16[4,16,2048]{2,1,0:T(8,128)(2,1)S(1)} %shard_map.141.refs_1_), channel_id=1, source_target_pairs={{0,6},{1,7},{2,4},{3,5},{4,2},{5,3},{6,0},{7,1},{8,14},{9,15},{10,... | collective-permute-start | bytes 786440 | tf_op jit(solution)/shard_map/ppermute | solution.py:97
  20.3 11.8 %collective-permute-start.5 = (bf16[4,16,2048]{2,1,0:T(8,128)(2,1)S(1)}, bf16[4,16,2048]{2,1,0:T(8,128)(2,1)S(1)}, u32[]{:S(2)}, u32[]{:S(2)}) collective-permute-start(bf16[4,16,2048]{2,1,0:T(8,128)(2,1)S(1)} %shard_map.141.refs_1_), channel_id=1, source_target_pairs={{0,4},{1,3},{2,6},{3,1},{4,0},{5,7},{6,2},{7,5},{8,12},{9,11},{10,... | collective-permute-start | bytes 786440 | tf_op jit(solution)/shard_map/ppermute | solution.py:97
  21.5 11.2 %collective-permute-start.11 = (bf16[2,16,4096]{2,1,0:T(8,128)(2,1)S(1)}, bf16[2,16,4096]{2,1,0:T(8,128)(2,1)S(1)}, u32[]{:S(2)}, u32[]{:S(2)}) collective-permute-start(bf16[2,16,4096]{2,1,0:T(8,128)(2,1)S(1)} %shard_map.139.refs_2_.refs_0_), channel_id=1, source_target_pairs={{0,8},{1,9},{2,10},{3,11},{4,12},{5,13},{6,14},{7,15},{8,0},{9,1},... | collective-permute-start | bytes 786440 | tf_op jit(solution)/shard_map/ppermute | solution.py:97
  27.1 9.6 %collective-permute-start.7 = (bf16[4,16,2048]{2,1,0:T(8,128)(2,1)S(1)}, bf16[4,16,2048]{2,1,0:T(8,128)(2,1)S(1)}, u32[]{:S(2)}, u32[]{:S(2)}) collective-permute-start(bf16[4,16,2048]{2,1,0:T(8,128)(2,1)S(1)} %shard_map.141.refs_1_), channel_id=1, source_target_pairs={{0,1},{1,0},{2,3},{3,2},{4,5},{5,4},{6,7},{7,6},{8,9},{9,8},{10,11... | collective-permute-start | bytes 786440 | tf_op jit(solution)/shard_map/ppermute | solution.py:97
  27.1 11.1 %collective-permute-start.8 = (bf16[4,16,2048]{2,1,0:T(8,128)(2,1)S(1)}, bf16[4,16,2048]{2,1,0:T(8,128)(2,1)S(1)}, u32[]{:S(2)}, u32[]{:S(2)}) collective-permute-start(bf16[4,16,2048]{2,1,0:T(8,128)(2,1)S(1)} %collective-permute-done.4.refs_2_), channel_id=1, source_target_pairs={{0,1},{1,0},{2,3},{3,2},{4,5},{5,4},{6,7},{7,6},{8,9},{9,8},{10,11... | collective-permute-start | bytes 786440 | tf_op jit(solution)/shard_map/ppermute | solution.py:97
  32.1 3.7 %collective-permute-start.10 = (bf16[4,16,2048]{2,1,0:T(8,128)(2,1)S(1)}, bf16[4,16,2048]{2,1,0:T(8,128)(2,1)S(1)}, u32[]{:S(2)}, u32[]{:S(2)}) collective-permute-start(bf16[4,16,2048]{2,1,0:T(8,128)(2,1)S(1)} %collective-permute-done.6.refs_4_), channel_id=1, source_target_pairs={{0,1},{1,0},{2,3},{3,2},{4,5},{5,4},{6,7},{7,6},{8,9},{9,8},{10,11... | collective-permute-start | bytes 786440 | tf_op jit(solution)/shard_map/ppermute | solution.py:97
  32.1 3.8 %collective-permute-start.9 = (bf16[4,16,2048]{2,1,0:T(8,128)(2,1)S(1)}, bf16[4,16,2048]{2,1,0:T(8,128)(2,1)S(1)}, u32[]{:S(2)}, u32[]{:S(2)}) collective-permute-start(bf16[4,16,2048]{2,1,0:T(8,128)(2,1)S(1)} %collective-permute-done.5.refs_3_), channel_id=1, source_target_pairs={{0,1},{1,0},{2,3},{3,2},{4,5},{5,4},{6,7},{7,6},{8,9},{9,8},{10,11... | collective-permute-start | bytes 786440 | tf_op jit(solution)/shard_map/ppermute | solution.py:97
  32.6 20.9 %collective-permute-start.14 = (bf16[2,16,6144]{2,1,0:T(8,128)(2,1)S(1)}, bf16[2,16,6144]{2,1,0:T(8,128)(2,1)S(1)}, u32[]{:S(2)}, u32[]{:S(2)}) collective-permute-start(bf16[2,16,6144]{2,1,0:T(8,128)(2,1)S(1)} %shard_map.140.refs_3_.refs_0_), channel_id=1, source_target_pairs={{0,16},{1,17},{2,18},{3,19},{4,20},{5,21},{6,22},{7,23},{8,24},{9,... | collective-permute-start | bytes 1179656 | tf_op jit(solution)/shard_map/ppermute | solution.py:97
  35.8 26.7 %collective-permute-start.16 = (bf16[4,16,4096]{2,1,0:T(8,128)(2,1)S(1)}, bf16[4,16,4096]{2,1,0:T(8,128)(2,1)S(1)}, u32[]{:S(2)}, u32[]{:S(2)}) collective-permute-start(bf16[4,16,4096]{2,1,0:T(8,128)(2,1)S(1)} %shard_map.142.refs_12_.refs_1_), channel_id=1, source_target_pairs={{0,1},{1,0},{2,3},{3,2},{4,5},{5,4},{6,7},{7,6},{8,9},{9,8},{10,11... | collective-permute-start | bytes 1572872 | tf_op jit(solution)/shard_map/ppermute | solution.py:97
  35.9 18.4 %collective-permute-start.13 = (bf16[4,16,4096]{2,1,0:T(8,128)(2,1)S(1)}, bf16[4,16,4096]{2,1,0:T(8,128)(2,1)S(1)}, u32[]{:S(2)}, u32[]{:S(2)}) collective-permute-start(bf16[4,16,4096]{2,1,0:T(8,128)(2,1)S(1)} %shard_map.142.refs_12_.refs_1_), channel_id=1, source_target_pairs={{0,4},{1,3},{2,6},{3,1},{4,0},{5,7},{6,2},{7,5},{8,12},{9,11},{10,... | collective-permute-start | bytes 1572872 | tf_op jit(solution)/shard_map/ppermute | solution.py:97
  36.8 17.6 %collective-permute-start.12 = (bf16[4,16,4096]{2,1,0:T(8,128)(2,1)S(1)}, bf16[4,16,4096]{2,1,0:T(8,128)(2,1)S(1)}, u32[]{:S(2)}, u32[]{:S(2)}) collective-permute-start(bf16[4,16,4096]{2,1,0:T(8,128)(2,1)S(1)} %shard_map.142.refs_12_.refs_1_), channel_id=1, source_target_pairs={{0,2},{1,5},{2,0},{3,7},{4,6},{5,1},{6,4},{7,3},{8,10},{9,13},{10,... | collective-permute-start | bytes 1572872 | tf_op jit(solution)/shard_map/ppermute | solution.py:97
  53.6 19.0 %collective-permute-start.21 = (bf16[4,16,6144]{2,1,0:T(8,128)(2,1)S(1)}, bf16[4,16,6144]{2,1,0:T(8,128)(2,1)S(1)}, u32[]{:S(2)}, u32[]{:S(2)}) collective-permute-start(bf16[4,16,6144]{2,1,0:T(8,128)(2,1)S(1)} %shard_map.144.refs_13_.refs_0_), channel_id=1, source_target_pairs={{0,8},{1,9},{2,10},{3,11},{4,12},{5,13},{6,14},{7,15},{8,0},{9,1},... | collective-permute-start | bytes 2359304 | tf_op jit(solution)/shard_map/ppermute | solution.py:97
  54.4 9.2 %collective-permute-start.15 = (bf16[4,16,4096]{2,1,0:T(8,128)(2,1)S(1)}, bf16[4,16,4096]{2,1,0:T(8,128)(2,1)S(1)}, u32[]{:S(2)}, u32[]{:S(2)}) collective-permute-start(bf16[4,16,4096]{2,1,0:T(8,128)(2,1)S(1)} %collective-permute-done.12.refs_2_), channel_id=1, source_target_pairs={{0,4},{1,3},{2,6},{3,1},{4,0},{5,7},{6,2},{7,5},{8,12},{9,11},{10,... | collective-permute-start | bytes 1572872 | tf_op jit(solution)/shard_map/ppermute | solution.py:97
  55.1 8.4 %collective-permute-start.17 = (bf16[4,16,4096]{2,1,0:T(8,128)(2,1)S(1)}, bf16[4,16,4096]{2,1,0:T(8,128)(2,1)S(1)}, u32[]{:S(2)}, u32[]{:S(2)}) collective-permute-start(bf16[4,16,4096]{2,1,0:T(8,128)(2,1)S(1)} %collective-permute-done.12.refs_2_), channel_id=1, source_target_pairs={{0,1},{1,0},{2,3},{3,2},{4,5},{5,4},{6,7},{7,6},{8,9},{9,8},{10,11... | collective-permute-start | bytes 1572872 | tf_op jit(solution)/shard_map/ppermute | solution.py:97
  55.1 8.4 %collective-permute-start.18 = (bf16[4,16,4096]{2,1,0:T(8,128)(2,1)S(1)}, bf16[4,16,4096]{2,1,0:T(8,128)(2,1)S(1)}, u32[]{:S(2)}, u32[]{:S(2)}) collective-permute-start(bf16[4,16,4096]{2,1,0:T(8,128)(2,1)S(1)} %collective-permute-done.13.refs_3_), channel_id=1, source_target_pairs={{0,1},{1,0},{2,3},{3,2},{4,5},{5,4},{6,7},{7,6},{8,9},{9,8},{10,11... | collective-permute-start | bytes 1572872 | tf_op jit(solution)/shard_map/ppermute | solution.py:97
  63.5 1.9 %collective-permute-start.19 = (bf16[4,16,4096]{2,1,0:T(8,128)(2,1)S(1)}, bf16[4,16,4096]{2,1,0:T(8,128)(2,1)S(1)}, u32[]{:S(2)}, u32[]{:S(2)}) collective-permute-start(bf16[4,16,4096]{2,1,0:T(8,128)(2,1)S(1)} %collective-permute-done.15.refs_4_), channel_id=1, source_target_pairs={{0,1},{1,0},{2,3},{3,2},{4,5},{5,4},{6,7},{7,6},{8,9},{9,8},{10,11... | collective-permute-start | bytes 1572872 | tf_op jit(solution)/shard_map/ppermute | solution.py:97
  72.7 9.2 %collective-permute-start.24 = (bf16[8,16,2048]{2,1,0:T(8,128)(2,1)S(1)}, bf16[8,16,2048]{2,1,0:T(8,128)(2,1)S(1)}, u32[]{:S(2)}, u32[]{:S(2)}) collective-permute-start(bf16[8,16,2048]{2,1,0:T(8,128)(2,1)S(1)} %get-tuple-element.41.refs_11_.refs_2_), channel_id=1, source_target_pairs={{0,4},{1,3},{2,6},{3,1},{4,0},{5,7},{6,2},{7,5},{8,12},{9,11},{10,... | collective-permute-start | bytes 1572872 | tf_op jit(solution)/shard_map/ppermute | solution.py:97
  73.5 1.3 collective-permute-start.20
  73.5 14.4 %collective-permute-start.25 = (bf16[8,16,2048]{2,1,0:T(8,128)(2,1)S(1)}, bf16[8,16,2048]{2,1,0:T(8,128)(2,1)S(1)}, u32[]{:S(2)}, u32[]{:S(2)}) collective-permute-start(bf16[8,16,2048]{2,1,0:T(8,128)(2,1)S(1)} %get-tuple-element.41.refs_11_.refs_2_), channel_id=1, source_target_pairs={{0,1},{1,0},{2,3},{3,2},{4,5},{5,4},{6,7},{7,6},{8,9},{9,8},{10,11... | collective-permute-start | bytes 1572872 | tf_op jit(solution)/shard_map/ppermute | solution.py:97
  79.6 8.3 %copy-start.5 = (f32[144,256]{1,0:T(8,128)S(1)}, f32[144,256]{1,0:T(8,128)}, u32[]{:S(2)}) copy-start(f32[144,256]{1,0:T(8,128)} %constant.10.clone.refs_9_) | copy-start | bytes 442372
  81.9 6.0 %collective-permute-start.26 = (bf16[8,16,2048]{2,1,0:T(8,128)(2,1)S(1)}, bf16[8,16,2048]{2,1,0:T(8,128)(2,1)S(1)}, u32[]{:S(2)}, u32[]{:S(2)}) collective-permute-start(bf16[8,16,2048]{2,1,0:T(8,128)(2,1)S(1)} %collective-permute-done.24.refs_3_), channel_id=1, source_target_pairs={{0,1},{1,0},{2,3},{3,2},{4,5},{5,4},{6,7},{7,6},{8,9},{9,8},{10,11... | collective-permute-start | bytes 1572872 | tf_op jit(solution)/shard_map/ppermute | solution.py:97
  81.9 5.8 %collective-permute-start.22 = (bf16[2,36,512]{2,1,0:T(8,128)(2,1)S(1)}, bf16[2,36,512]{2,1,0:T(8,128)(2,1)S(1)}, u32[]{:S(2)}, u32[]{:S(2)}) collective-permute-start(bf16[2,36,512]{2,1,0:T(8,128)(2,1)S(1)} %get-tuple-element.44), channel_id=1, source_target_pairs={{1,0},{0,1},{3,2},{2,3},{5,4},{4,5},{7,6},{6,7},{9,8},{8,9},{11,10... | collective-permute-start | bytes 221192 | tf_op jit(solution)/shard_map/ppermute | solution.py:362
  82.4 21.9 %collective-permute-start.28 = (bf16[8,16,4096]{2,1,0:T(8,128)(2,1)S(1)}, bf16[8,16,4096]{2,1,0:T(8,128)(2,1)S(1)}, u32[]{:S(2)}, u32[]{:S(2)}) collective-permute-start(bf16[8,16,4096]{2,1,0:T(8,128)(2,1)S(1)} %get-tuple-element.51.refs_1_), channel_id=1, source_target_pairs={{0,1},{1,0},{2,3},{3,2},{4,5},{5,4},{6,7},{7,6},{8,9},{9,8},{10,11... | collective-permute-start | bytes 3145736 | tf_op jit(solution)/shard_map/ppermute | solution.py:97
  82.5 12.9 %collective-permute-start.23 = (bf16[8,36,512]{2,1,0:T(8,128)(2,1)S(1)}, bf16[8,36,512]{2,1,0:T(8,128)(2,1)S(1)}, u32[]{:S(2)}, u32[]{:S(2)}) collective-permute-start(bf16[8,36,512]{2,1,0:T(8,128)(2,1)S(1)} %shard_map.150), channel_id=1, source_target_pairs={{2,0},{3,1},{4,2},{5,3},{6,4},{7,5},{8,6},{9,7},{10,8},{11,9},{12,... | collective-permute-start | bytes 884744 | tf_op jit(solution)/shard_map/ppermute | solution.py:362
  87.8 14.9 %collective-permute-start.27 = (bf16[8,16,4096]{2,1,0:T(8,128)(2,1)S(1)}, bf16[8,16,4096]{2,1,0:T(8,128)(2,1)S(1)}, u32[]{:S(2)}, u32[]{:S(2)}) collective-permute-start(bf16[8,16,4096]{2,1,0:T(8,128)(2,1)S(1)} %get-tuple-element.51.refs_1_), channel_id=1, source_target_pairs={{0,4},{1,3},{2,6},{3,1},{4,0},{5,7},{6,2},{7,5},{8,12},{9,11},{10,... | collective-permute-start | bytes 3145736 | tf_op jit(solution)/shard_map/ppermute | solution.py:97
  102.7 4.0 %collective-permute-start.29 = (bf16[8,16,4096]{2,1,0:T(8,128)(2,1)S(1)}, bf16[8,16,4096]{2,1,0:T(8,128)(2,1)S(1)}, u32[]{:S(2)}, u32[]{:S(2)}) collective-permute-start(bf16[8,16,4096]{2,1,0:T(8,128)(2,1)S(1)} %collective-permute-done.27.refs_2_), channel_id=1, source_target_pairs={{0,1},{1,0},{2,3},{3,2},{4,5},{5,4},{6,7},{7,6},{8,9},{9,8},{10,11... | collective-permute-start | bytes 3145736 | tf_op jit(solution)/shard_map/ppermute | solution.py:97
  111.4 1.4 %collective-permute-start.30 = (bf16[2,36,512]{2,1,0:T(8,128)(2,1)S(1)}, bf16[2,36,512]{2,1,0:T(8,128)(2,1)S(1)}, u32[]{:S(2)}, u32[]{:S(2)}) collective-permute-start(bf16[2,36,512]{2,1,0:T(8,128)(2,1)S(1)} %get-tuple-element.53), channel_id=1, source_target_pairs={{1,0},{0,1},{3,2},{2,3},{5,4},{4,5},{7,6},{6,7},{9,8},{8,9},{11,10... | collective-permute-start | bytes 221192 | tf_op jit(solution)/shard_map/ppermute | solution.py:362
  112.8 15.2 %collective-permute-start.31 = (bf16[8,36,512]{2,1,0:T(8,128)(2,1)S(1)}, bf16[8,36,512]{2,1,0:T(8,128)(2,1)S(1)}, u32[]{:S(2)}, u32[]{:S(2)}) collective-permute-start(bf16[8,36,512]{2,1,0:T(8,128)(2,1)S(1)} %shard_map.154), channel_id=1, source_target_pairs={{30,0},{31,1},{0,2},{1,3},{2,4},{3,5},{4,6},{5,7},{6,8},{7,9},{8,1... | collective-permute-start | bytes 884744 | tf_op jit(solution)/shard_map/ppermute | solution.py:362
  119.8 1.3 %collective-permute-start.32 = (bf16[2,36,512]{2,1,0:T(8,128)(2,1)S(1)}, bf16[2,36,512]{2,1,0:T(8,128)(2,1)S(1)}, u32[]{:S(2)}, u32[]{:S(2)}) collective-permute-start(bf16[2,36,512]{2,1,0:T(8,128)(2,1)S(1)} %get-tuple-element.58), channel_id=1, source_target_pairs={{1,0},{0,1},{3,2},{2,3},{5,4},{4,5},{7,6},{6,7},{9,8},{8,9},{11,10... | collective-permute-start | bytes 221192 | tf_op jit(solution)/shard_map/ppermute | solution.py:362

commit v13 on v12

--- a/solution.py
+++ b/solution.py
@@ -150,11 +150,14 @@
             jnp.where(core == 0, by_y, by_x),
             (1 - y) * 2 + 1 - x,
         )
-        held = squares[index % 4 : index % 4 + 1] if parts == 4 else squares[index % 2 * 2 :][:2]
         copy.wait()
         for step in range(pieces[0].shape[0]):
-            shard = (z ^ Z_ORDER[step // len(held)]) * 4 + held[step % len(held)]
-            row = pl.multiple_of((shard * 2 + core) * half, 16)
+            if parts == 4:
+                square, along = squares[index % 4], Z_ORDER[step]
+            else:
+                square = squares[index % 2 * 2 + step // 2 % 2]
+                along = Z_ORDER[step // 4 * 2 + step % 2]
+            row = pl.multiple_of((((z ^ along) * 4 + square) * 2 + core) * half, 16)
             w_ref[pl.ds(row, half), :] = stage_ref[index, step]
 
 
@@ -428,19 +431,19 @@
         widths = tuple(sum(weight.shape[2] for weight in pair) for pair in (weights[:2], weights[2:]))
         (pair,) = join([[own, across_z(own, 2)]], (), (windows,))
         (feed_pair,) = join([[feed_own, across_z(feed_own, 2)]])
-        (last_pair,) = join([[last_own, send(last_own, beside)]])
+        (last_pair,) = join([[last_own, across_z(last_own, 2)]])
         (column,) = join([[pair, across_z(pair, 1)]], (), (feed_pair, last_pair))
         received = [send(column, way) for way in (beside, across, corner)]
         sent = [tied(column, received[0])] + received
         pieces = [column] + received + [send(part, swap) for part in sent]
-        (feed_column,) = join([[feed_pair, across_z(feed_pair, 1)]])
+        (last_four,) = join([[last_pair, send(last_pair, beside)]])
+        (feed_column,) = join([[feed_pair, across_z(feed_pair, 1)]], (), (last_four,))
         received = [send(feed_column, way) for way in (beside, across)]
-        last_other = across_z(last_pair, 2)
+        last_other = across_z(last_four, 1)
         middle_0 = attention(0, [windows], (0,), pieces, (feed_column,))
-        received.append(send(tied(received[0], (middle_0, last_other)), across))
-        (last_four,) = join([[last_pair, last_other]], (), (middle_0,))
-        last_other = across_z(last_four, 1)
-        middle_1 = attention(0, [windows], (1,), pieces, (middle_0, last_four))
+        received.append(send(tied(received[0], middle_0), across))
+        last_column, final_column = join([[last_four, last_other]], (), (middle_0,), widths)
+        middle_1 = attention(0, [windows], (1,), pieces, (middle_0, last_column))
         swapped = [send(part, swap) for part in [feed_column] + tied(received[:2], middle_0)]
         swapped.append(send(tied(received[2], (middle_1, *swapped)), swap))
         feed_pieces = [feed_column] + received + swapped
@@ -458,17 +461,14 @@
     size = left_0.shape[0]
     (ahead,) = strips([left_0, below_0], [[(0, 1, size - 1), (1, 0, 1)]])
     ahead = shift_from(ahead, 1, 0)
-    after = (below_0,)
     if relay:
-        last_column, final_column = join([[last_four, last_other]], (), (low_0,), widths)
-        last_received = send(last_column, across)
-        after += (last_column,)
-    left_1, right_1, low_1 = forward(0, middle_1, 0, feed_pieces, low_edge, after)
-    below_1 = shift_from(low_1, 0, 1)
+        last_received = send(tied(last_column, middle_1), across)
+    left_1, right_1, low_1 = forward(0, middle_1, 0, feed_pieces, low_edge, (below_0,))
+    below_1 = shift_from(tied(low_1, ahead), 0, 1)
     if relay:
         last_pieces = [last_column, last_received, send(last_column, swap)]
         last_pieces.append(send(tied(last_received, low_1), swap))
-        final_received = send(tied(final_column, last_received), across)
+        final_received = send(tied(final_column, (last_received, ahead)), across)
     lefts = strips(
         [right_0, left_1, right_1, below_0, below_1],
         [
@@ -477,8 +477,7 @@
             [(2, 1, size - 1), (4, 1, 1)],
         ],
     )
-    middle_0 = attention(1, lefts[:2], (0,), last_pieces)
-    middle_1 = attention(1, [lefts[2], ahead], (1,), last_pieces, (middle_0,))
+    middle_1 = attention(1, [lefts[2], ahead], (1,), last_pieces)
     if relay:
         final_pieces = [final_column, final_received, send(final_column, swap)]
         final_pieces.append(send(tied(final_received, middle_1), swap))
@@ -486,7 +485,8 @@
     above_1 = shift_from(high_1, 0, -1)
     (behind,) = strips([above_1, right_1], [[(0, 1, 1), (1, 0, size - 1)]])
     behind = shift_from(behind, -1, 0)
-    left_0, right_0, high_0 = forward(1, middle_0, 0, final_pieces, high_edge, (above_1,))
+    middle_0 = attention(1, lefts[:2], (0,), last_pieces, (above_1,))
+    left_0, right_0, high_0 = forward(1, middle_0, 0, final_pieces, high_edge)
     above_0 = shift_from(high_0, 0, -1)
     picks = [(0, 0, size)]
     for place, (low, quarter) in enumerate(((4, 0), (4, 1), (5, 0))):

time: 131 us -> 132 us (level)
  waiting for transfers between devices: 43.6 us -> 50.6 us
  starting transfers between devices: 31.9 us -> 26.3 us
    ppermute x27, waiting for transfers between devices: 33.2 us -> 44.4 us  [send(): return lax.ppermute(block, ('lon', 'lat'), pairs)]
    ppermute x6, waiting for transfers between devices: 10.4 us -> 6.17 us  [shift_from(): return lax.ppermute(block, ('lon', 'lat'), pairs)]
    ppermute x27, starting transfers between devices: 23.3 us -> 20.1 us  [send(): return lax.ppermute(block, ('lon', 'lat'), pairs)]
    ppermute x6, starting transfers between devices: 8.59 us -> 6.22 us  [shift_from(): return lax.ppermute(block, ('lon', 'lat'), pairs)]
  transfers between devices with their start and end apart: 33 -> 33, of which waited for: 15 -> 14; matrix products, arithmetic and copies ran while one was open for 1% -> 1% of each run, Pallas kernels for 32% -> 32%
where the time goes in v13:
time: 132 us
  waiting for transfers between devices  50.6 us (38%)
  Pallas kernels  47.2 us (36%)
  starting transfers between devices  26.3 us (20%)
  local copies, waits for them, and re-layouts  7.6 us (6%)
    ppermute x27, waiting for transfers between devices, send(): return lax.ppermute(block, ('lon', 'lat'), pairs)  44.4 us
    pallas_call x4, Pallas kernels, attend(): pl.pallas_call(functools.partial(attend_kernel, shifted, row_windows, len...  27.6 us
    ppermute x27, starting transfers between devices, send(): return lax.ppermute(block, ('lon', 'lat'), pairs)  20.1 us
    pallas_call x4, Pallas kernels, feed(): pl.pallas_call(functools.partial(feed_kernel, len(pieces), hidden_size, 5...  19.2 us
    ppermute x6, starting transfers between devices, shift_from(): return lax.ppermute(block, ('lon', 'lat'), pairs)  6.22 us
    ppermute x6, waiting for transfers between devices, shift_from(): return lax.ppermute(block, ('lon', 'lat'), pairs)  6.17 us
    unnamed x20, local copies, waits for them, and re-layouts  3.7 us
  transfers between devices with their start and end apart: 33, of which 14 were waited for; matrix products, arithmetic and copies ran while one was open for 1% of the time, Pallas kernels for 32%

profile of v13, /device:TPU:0, one launch (start us, length us, event | category | flops | bytes accessed | tf_op | source)
XLA Modules:
  0.0 132.1 jit_solution(6798550911767831700)
XLA Ops:
  0.0 0.9 copy-done
  1.0 0.9 copy-done.1
  1.9 0.9 copy-done.2
  2.8 0.8 copy-done.3
  3.7 4.1 %collective-permute-start.3 = (bf16[1,16,6144]{2,1,0:T(8,128)(2,1)S(1)}, bf16[1,16,6144]{2,1,0:T(8,128)(2,1)S(1)}, u32[]{:S(2)}, u32[]{:S(2)}) collective-permute-start(bf16[1,16,6144]{2,1,0:T(8,128)(2,1)S(1)} %get-tuple-element.35.refs_0_), channel_id=1, source_target_pairs={{0,16},{1,17},{2,18},{3,19},{4,20},{5,21},{6,22},{7,23},{8,24},{9,... | collective-permute-start | bytes 589832 | tf_op jit(solution)/shard_map/ppermute | solution.py:97
  7.8 0.1 collective-permute-start
  7.9 2.8 %collective-permute-start.2 = (bf16[1,16,4096]{2,1,0:T(8,128)(2,1)S(1)}, bf16[1,16,4096]{2,1,0:T(8,128)(2,1)S(1)}, u32[]{:S(2)}, u32[]{:S(2)}) collective-permute-start(bf16[1,16,4096]{2,1,0:T(8,128)(2,1)S(1)} %get-tuple-element.34.refs_0_), channel_id=1, source_target_pairs={{0,16},{1,17},{2,18},{3,19},{4,20},{5,21},{6,22},{7,23},{8,24},{9,... | collective-permute-start | bytes 393224 | tf_op jit(solution)/shard_map/ppermute | solution.py:97
  10.7 0.8 copy.26
  11.6 0.5 reshape.15.refs_2_.refs_0_
  12.1 11.3 %collective-permute-done.refs_1_ = bf16[1,16,2048]{2,1,0:T(8,128)(2,1)S(1)} collective-permute-done((bf16[1,16,2048]{2,1,0:T(8,128)(2,1)S(1)}, bf16[1,16,2048]{2,1,0:T(8,128)(2,1)S(1)}, u32[]{:S(2)}, u32[]{:S(2)}) %collective-permute-start) | collective-permute-done | bytes 65568 | tf_op jit(solution)/shard_map/ppermute | solution.py:97
  23.4 0.0 copy-start.7
  23.4 0.1 collective-permute-start.1
  23.5 1.9 %collective-permute-start.12 = (bf16[2,16,6144]{2,1,0:T(8,128)(2,1)S(1)}, bf16[2,16,6144]{2,1,0:T(8,128)(2,1)S(1)}, u32[]{:S(2)}, u32[]{:S(2)}) collective-permute-start(bf16[2,16,6144]{2,1,0:T(8,128)(2,1)S(1)} %shard_map.140.refs_3_.refs_0_), channel_id=1, source_target_pairs={{0,2},{1,5},{2,0},{3,7},{4,6},{5,1},{6,4},{7,3},{8,10},{9,13},{10,... | collective-permute-start | bytes 1179656 | tf_op jit(solution)/shard_map/ppermute | solution.py:97
  25.5 3.0 %collective-permute-done.1.refs_1_ = bf16[2,16,2048]{2,1,0:T(8,128)(2,1)S(1)} collective-permute-done((bf16[2,16,2048]{2,1,0:T(8,128)(2,1)S(1)}, bf16[2,16,2048]{2,1,0:T(8,128)(2,1)S(1)}, u32[]{:S(2)}, u32[]{:S(2)}) %collective-permute-start.1) | collective-permute-done | bytes 131104 | tf_op jit(solution)/shard_map/ppermute | solution.py:97
  28.5 1.9 %collective-permute-start.4 = (bf16[4,16,2048]{2,1,0:T(8,128)(2,1)S(1)}, bf16[4,16,2048]{2,1,0:T(8,128)(2,1)S(1)}, u32[]{:S(2)}, u32[]{:S(2)}) collective-permute-start(bf16[4,16,2048]{2,1,0:T(8,128)(2,1)S(1)} %shard_map.141.refs_1_), channel_id=1, source_target_pairs={{0,2},{1,5},{2,0},{3,7},{4,6},{5,1},{6,4},{7,3},{8,10},{9,13},{10,... | collective-permute-start | bytes 786440 | tf_op jit(solution)/shard_map/ppermute | solution.py:97
  30.4 1.5 %collective-permute-start.6 = (bf16[4,16,2048]{2,1,0:T(8,128)(2,1)S(1)}, bf16[4,16,2048]{2,1,0:T(8,128)(2,1)S(1)}, u32[]{:S(2)}, u32[]{:S(2)}) collective-permute-start(bf16[4,16,2048]{2,1,0:T(8,128)(2,1)S(1)} %shard_map.141.refs_1_), channel_id=1, source_target_pairs={{0,6},{1,7},{2,4},{3,5},{4,2},{5,3},{6,0},{7,1},{8,14},{9,15},{10,... | collective-permute-start | bytes 786440 | tf_op jit(solution)/shard_map/ppermute | solution.py:97
  31.9 0.2 collective-permute-start.5
  32.0 0.3 collective-permute-start.11
  32.4 5.5 %collective-permute-done.4.refs_2_ = bf16[4,16,2048]{2,1,0:T(8,128)(2,1)S(1)} collective-permute-done((bf16[4,16,2048]{2,1,0:T(8,128)(2,1)S(1)}, bf16[4,16,2048]{2,1,0:T(8,128)(2,1)S(1)}, u32[]{:S(2)}, u32[]{:S(2)}) %collective-permute-start.4) | collective-permute-done | bytes 262176 | tf_op jit(solution)/shard_map/ppermute | solution.py:97
  37.9 6.0 %collective-permute-done.6.refs_4_ = bf16[4,16,2048]{2,1,0:T(8,128)(2,1)S(1)} collective-permute-done((bf16[4,16,2048]{2,1,0:T(8,128)(2,1)S(1)}, bf16[4,16,2048]{2,1,0:T(8,128)(2,1)S(1)}, u32[]{:S(2)}, u32[]{:S(2)}) %collective-permute-start.6) | collective-permute-done | bytes 262176 | tf_op jit(solution)/shard_map/ppermute | solution.py:97
  43.9 0.5 collective-permute-start.10
  44.4 0.1 collective-permute-start.9
  44.5 0.1 multiply_reduce_fusion
  44.6 0.1 shard_map.142.refs_2_.refs_0_
  44.7 0.0 copy-start.4
  44.7 2.1 %collective-permute-start.19 = (bf16[4,16,6144]{2,1,0:T(8,128)(2,1)S(1)}, bf16[4,16,6144]{2,1,0:T(8,128)(2,1)S(1)}, u32[]{:S(2)}, u32[]{:S(2)}) collective-permute-start(bf16[4,16,6144]{2,1,0:T(8,128)(2,1)S(1)} %shard_map.142.refs_2_.refs_0_), channel_id=1, source_target_pairs={{0,8},{1,9},{2,10},{3,11},{4,12},{5,13},{6,14},{7,15},{8,0},{9,1},... | collective-permute-start | bytes 2359304 | tf_op jit(solution)/shard_map/ppermute | solution.py:97
  46.8 0.2 collective-permute-start.16
  47.0 0.2 collective-permute-start.14
  47.2 1.8 %collective-permute-start.13 = (bf16[4,16,4096]{2,1,0:T(8,128)(2,1)S(1)}, bf16[4,16,4096]{2,1,0:T(8,128)(2,1)S(1)}, u32[]{:S(2)}, u32[]{:S(2)}) collective-permute-start(bf16[4,16,4096]{2,1,0:T(8,128)(2,1)S(1)} %shard_map.143.refs_12_.refs_1_), channel_id=1, source_target_pairs={{0,2},{1,5},{2,0},{3,7},{4,6},{5,1},{6,4},{7,3},{8,10},{9,13},{10,... | collective-permute-start | bytes 1572872 | tf_op jit(solution)/shard_map/ppermute | solution.py:97
  49.0 6.9 %shard_map.144.refs_2_.refs_12_.refs_0_ = bf16[4,144,512]{2,1,0:T(8,128)(2,1)S(1)} custom-call(bf16[8,144,512]{2,1,0:T(8,128)(2,1)S(1)} %reshape.15.refs_2_.refs_0_, bf16[4,16,2048]{2,1,0:T(8,128)(2,1)S(1)} %shard_map.141.refs_1_, bf16[4,16,2048]{2,1,0:T(8,128)(2,1)S(1)} %collective-permute-done.4.refs_2_, ...), custom_call_target="tpu_custom_call" | custom-call | flops 8000000000 | bytes 6000000 | tf_op jit(solution)/shard_map/pallas_call | solution.py:281
  55.9 5.3 %collective-permute-done.14.refs_3_ = bf16[4,16,4096]{2,1,0:T(8,128)(2,1)S(1)} collective-permute-done((bf16[4,16,4096]{2,1,0:T(8,128)(2,1)S(1)}, bf16[4,16,4096]{2,1,0:T(8,128)(2,1)S(1)}, u32[]{:S(2)}, u32[]{:S(2)}) %collective-permute-start.14) | collective-permute-done | bytes 524320 | tf_op jit(solution)/shard_map/ppermute | solution.py:97
  61.3 0.2 collective-permute-start.15
  61.5 1.1 collective-permute-start.17
  62.5 2.4 %collective-permute-done.19.refs_1_ = bf16[4,16,6144]{2,1,0:T(8,128)(2,1)S(1)} collective-permute-done((bf16[4,16,6144]{2,1,0:T(8,128)(2,1)S(1)}, bf16[4,16,6144]{2,1,0:T(8,128)(2,1)S(1)}, u32[]{:S(2)}, u32[]{:S(2)}) %collective-permute-start.19) | collective-permute-done | bytes 786464 | tf_op jit(solution)/shard_map/ppermute | solution.py:97
  64.9 0.1 shard_map.145
  65.0 6.9 %shard_map.146.refs_0_ = bf16[4,144,512]{2,1,0:T(8,128)(2,1)S(1)} custom-call(bf16[8,144,512]{2,1,0:T(8,128)(2,1)S(1)} %reshape.15.refs_2_.refs_0_, bf16[4,16,2048]{2,1,0:T(8,128)(2,1)S(1)} %shard_map.141.refs_1_, bf16[4,16,2048]{2,1,0:T(8,128)(2,1)S(1)} %collective-permute-done.4.refs_2_, bf16[4,16,2048]{2,1,0:T(8,128)(2,1)S(1)} %collective-permute-done.5.refs_3_, ...), custom_call_target="tpu_custom_call" | custom-call | flops 8000000000 | bytes 6000000 | tf_op jit(solution)/shard_map/pallas_call | solution.py:281
  72.0 0.1 collective-permute-start.20
  72.1 0.2 collective-permute-start.24
  72.3 1.7 %collective-permute-done.20.refs_8_ = bf16[4,16,4096]{2,1,0:T(8,128)(2,1)S(1)} collective-permute-done((bf16[4,16,4096]{2,1,0:T(8,128)(2,1)S(1)}, bf16[4,16,4096]{2,1,0:T(8,128)(2,1)S(1)}, u32[]{:S(2)}, u32[]{:S(2)}) %collective-permute-start.20) | collective-permute-done | bytes 524320 | tf_op jit(solution)/shard_map/ppermute | solution.py:97
  74.0 4.8 %shard_map.147 = (bf16[8,36,512]{2,1,0:T(8,128)(2,1)S(1)}, bf16[8,36,512]{2,1,0:T(8,128)(2,1)S(1)}, bf16[2,36,512]{2,1,0:T(8,128)(2,1)S(1)}) custom-call(bf16[4,144,512]{2,1,0:T(8,128)(2,1)S(1)} %shard_map.144.refs_2_.refs_12_.refs_0_, bf16[4,16,4096]{2,1,0:T(8,128)(2,1)S(1)} %shard_map.143.refs_12_.refs_1_, ...), custom_call_target="tpu_custom_call" | custom-call | flops 1000000 | bytes 100000 | tf_op jit(solution)/shard_map/pallas_call | solution.py:338
  78.8 0.2 collective-permute-start.21
  79.0 1.1 collective-permute-done.21.refs_10_.refs_1_.refs_3_
  80.2 3.8 %collective-permute-start.22 = (bf16[8,36,512]{2,1,0:T(8,128)(2,1)S(1)}, bf16[8,36,512]{2,1,0:T(8,128)(2,1)S(1)}, u32[]{:S(2)}, u32[]{:S(2)}) collective-permute-start(bf16[8,36,512]{2,1,0:T(8,128)(2,1)S(1)} %shard_map.149), channel_id=1, source_target_pairs={{2,0},{3,1},{4,2},{5,3},{6,4},{7,5},{8,6},{9,7},{10,8},{11,9},{12,... | collective-permute-start | bytes 884744 | tf_op jit(solution)/shard_map/ppermute | solution.py:365
  84.0 4.8 %shard_map.148 = (bf16[8,36,512]{2,1,0:T(8,128)(2,1)S(1)}, bf16[8,36,512]{2,1,0:T(8,128)(2,1)S(1)}, bf16[2,36,512]{2,1,0:T(8,128)(2,1)S(1)}) custom-call(bf16[4,144,512]{2,1,0:T(8,128)(2,1)S(1)} %shard_map.146.refs_0_, bf16[4,16,4096]{2,1,0:T(8,128)(2,1)S(1)} %shard_map.143.refs_12_.refs_1_, bf16[4,16,4096]{2,1,0:T(8,128)(2,1)S(1)} %collective-permute-done.13.refs_2_, ...), custom_call_target="tpu_custom_call" | custom-call | flops 1000000 | bytes 100000 | tf_op jit(solution)/shard_map/pallas_call | solution.py:338
  88.9 0.6 collective-permute-start.26
  89.5 1.9 %collective-permute-done.22.refs_1_ = bf16[8,36,512]{2,1,0:T(8,128)(2,1)S(1)} collective-permute-done((bf16[8,36,512]{2,1,0:T(8,128)(2,1)S(1)}, bf16[8,36,512]{2,1,0:T(8,128)(2,1)S(1)}, u32[]{:S(2)}, u32[]{:S(2)}) %collective-permute-start.22) | collective-permute-done | bytes 294944 | tf_op jit(solution)/shard_map/ppermute | solution.py:365
  91.3 0.3 collective-permute-start.23
  91.7 0.2 collective-permute-start.28
  91.8 0.8 collective-permute-done.23.refs_4_
  92.6 0.1 shard_map.150
  92.7 6.9 %shard_map.151.refs_0_ = bf16[4,144,512]{2,1,0:T(8,128)(2,1)S(1)} custom-call(bf16[8,36,512]{2,1,0:T(8,128)(2,1)S(1)} %get-tuple-element.49.refs_0_, bf16[8,36,512]{2,1,0:T(8,128)(2,1)S(1)} %collective-permute-done.22.refs_1_, bf16[8,16,2048]{2,1,0:T(8,128)(2,1)S(1)} %get-tuple-element.50.refs_13_.refs_2_, ...), custom_call_target="tpu_custom_call" | custom-call | flops 8000000000 | bytes 6000000 | tf_op jit(solution)/shard_map/pallas_call | solution.py:281
  99.6 6.5 %collective-permute-done.27.refs_2_ = bf16[8,16,4096]{2,1,0:T(8,128)(2,1)S(1)} collective-permute-done((bf16[8,16,4096]{2,1,0:T(8,128)(2,1)S(1)}, bf16[8,16,4096]{2,1,0:T(8,128)(2,1)S(1)}, u32[]{:S(2)}, u32[]{:S(2)}) %collective-permute-start.27) | collective-permute-done | bytes 1048608 | tf_op jit(solution)/shard_map/ppermute | solution.py:97
  106.1 2.7 %collective-permute-done.29.refs_4_ = bf16[8,16,4096]{2,1,0:T(8,128)(2,1)S(1)} collective-permute-done((bf16[8,16,4096]{2,1,0:T(8,128)(2,1)S(1)}, bf16[8,16,4096]{2,1,0:T(8,128)(2,1)S(1)}, u32[]{:S(2)}, u32[]{:S(2)}) %collective-permute-start.29) | collective-permute-done | bytes 1048608 | tf_op jit(solution)/shard_map/ppermute | solution.py:97
  108.8 4.8 %shard_map.152 = (bf16[8,36,512]{2,1,0:T(8,128)(2,1)S(1)}, bf16[8,36,512]{2,1,0:T(8,128)(2,1)S(1)}, bf16[2,36,512]{2,1,0:T(8,128)(2,1)S(1)}) custom-call(bf16[4,144,512]{2,1,0:T(8,128)(2,1)S(1)} %shard_map.151.refs_0_, bf16[8,16,4096]{2,1,0:T(8,128)(2,1)S(1)} %get-tuple-element.53.refs_1_, bf16[8,16,4096]{2,1,0:T(8,128)(2,1)S(1)} %collective-permute-done.27.refs_2_, ...), custom_call_target="tpu_custom_call" | custom-call | flops 1000000 | bytes 100000 | tf_op jit(solution)/shard_map/pallas_call | solution.py:338
  113.5 0.2 collective-permute-start.30
  113.7 1.2 collective-permute-done.30.refs_0_.refs_10_.refs_5_
  114.9 1.6 %collective-permute-start.31 = (bf16[8,36,512]{2,1,0:T(8,128)(2,1)S(1)}, bf16[8,36,512]{2,1,0:T(8,128)(2,1)S(1)}, u32[]{:S(2)}, u32[]{:S(2)}) collective-permute-start(bf16[8,36,512]{2,1,0:T(8,128)(2,1)S(1)} %shard_map.153), channel_id=1, source_target_pairs={{30,0},{31,1},{0,2},{1,3},{2,4},{3,5},{4,6},{5,7},{6,8},{7,9},{8,1... | collective-permute-start | bytes 884744 | tf_op jit(solution)/shard_map/ppermute | solution.py:365
  116.5 6.8 %shard_map.154.refs_0_ = bf16[4,144,512]{2,1,0:T(8,128)(2,1)S(1)} custom-call(bf16[8,36,512]{2,1,0:T(8,128)(2,1)S(1)} %get-tuple-element.57.refs_0_, bf16[8,36,512]{2,1,0:T(8,128)(2,1)S(1)} %get-tuple-element.58.refs_1_, bf16[8,16,2048]{2,1,0:T(8,128)(2,1)S(1)} %get-tuple-element.50.refs_13_.refs_2_, ...), custom_call_target="tpu_custom_call" | custom-call | flops 8000000000 | bytes 6000000 | tf_op jit(solution)/shard_map/pallas_call | solution.py:281
  123.3 4.8 %shard_map.155 = (bf16[8,36,512]{2,1,0:T(8,128)(2,1)S(1)}, bf16[8,36,512]{2,1,0:T(8,128)(2,1)S(1)}, bf16[2,36,512]{2,1,0:T(8,128)(2,1)S(1)}) custom-call(bf16[4,144,512]{2,1,0:T(8,128)(2,1)S(1)} %shard_map.154.refs_0_, bf16[8,16,4096]{2,1,0:T(8,128)(2,1)S(1)} %get-tuple-element.53.refs_1_, bf16[8,16,4096]{2,1,0:T(8,128)(2,1)S(1)} %collective-permute-done.27.refs_2_, ...), custom_call_target="tpu_custom_call" | custom-call | flops 1000000 | bytes 100000 | tf_op jit(solution)/shard_map/pallas_call | solution.py:338
  128.1 0.1 collective-permute-start.32
  128.2 1.3 collective-permute-done.32.refs_4_
  129.5 0.1 shard_map.156
  129.6 0.4 copy.23
  129.9 2.2 %copy.24 = bf16[4,6,8,3,2,512]{5,4,3,2,1,0:T(2,128)(2,1)} copy(bf16[4,6,8,3,2,512]{5,2,0,4,3,1:T(8,128)(2,1)S(1)} %bitcast.16) | data formatting | bytes 2359296 | tf_op jit(solution)/shard_map/transpose | solution.py:403
  (50 shorter events, 0.3 us)
Async XLA Ops:
  0.0 0.9 copy-start
  1.0 0.9 copy-start.1
  1.9 0.9 copy-start.2
  2.8 0.8 copy-start.3
  3.7 7.1 %copy-start.6 = (bf16[24,24,2,512]{3,2,1,0:T(2,128)(2,1)S(1)}, bf16[24,24,2,512]{3,2,1,0:T(2,128)(2,1)}, u32[]{:S(2)}) copy-start(bf16[24,24,2,512]{3,2,1,0:T(2,128)(2,1)} %param.14) | copy-start | bytes 3538948
  3.7 19.8 %collective-permute-start.3 = (bf16[1,16,6144]{2,1,0:T(8,128)(2,1)S(1)}, bf16[1,16,6144]{2,1,0:T(8,128)(2,1)S(1)}, u32[]{:S(2)}, u32[]{:S(2)}) collective-permute-start(bf16[1,16,6144]{2,1,0:T(8,128)(2,1)S(1)} %get-tuple-element.35.refs_0_), channel_id=1, source_target_pairs={{0,16},{1,17},{2,18},{3,19},{4,20},{5,21},{6,22},{7,23},{8,24},{9,... | collective-permute-start | bytes 589832 | tf_op jit(solution)/shard_map/ppermute | solution.py:97
  7.8 15.6 %collective-permute-start = (bf16[1,16,2048]{2,1,0:T(8,128)(2,1)S(1)}, bf16[1,16,2048]{2,1,0:T(8,128)(2,1)S(1)}, u32[]{:S(2)}, u32[]{:S(2)}) collective-permute-start(bf16[1,16,2048]{2,1,0:T(8,128)(2,1)S(1)} %shard_map.136.refs_0_), channel_id=1, source_target_pairs={{0,16},{1,17},{2,18},{3,19},{4,20},{5,21},{6,22},{7,23},{8,24},{9,... | collective-permute-start | bytes 196616 | tf_op jit(solution)/shard_map/ppermute | solution.py:97
  7.9 17.5 %collective-permute-start.2 = (bf16[1,16,4096]{2,1,0:T(8,128)(2,1)S(1)}, bf16[1,16,4096]{2,1,0:T(8,128)(2,1)S(1)}, u32[]{:S(2)}, u32[]{:S(2)}) collective-permute-start(bf16[1,16,4096]{2,1,0:T(8,128)(2,1)S(1)} %get-tuple-element.34.refs_0_), channel_id=1, source_target_pairs={{0,16},{1,17},{2,18},{3,19},{4,20},{5,21},{6,22},{7,23},{8,24},{9,... | collective-permute-start | bytes 393224 | tf_op jit(solution)/shard_map/ppermute | solution.py:97
  23.4 9.0 %copy-start.8 = (f32[2,2,512]{2,1,0:T(2,128)S(1)}, f32[2,2,512]{2,1,0:T(2,128)}, u32[]{:S(2)}) copy-start(f32[2,2,512]{2,1,0:T(2,128)} %param.19) | copy-start | bytes 24580
  23.4 21.1 %copy-start.7 = (f32[16,512]{1,0:T(8,128)S(1)}, f32[16,512]{1,0:T(8,128)}, u32[]{:S(2)}) copy-start(f32[16,512]{1,0:T(8,128)} %constant.8.clone) | copy-start | bytes 98308
  23.4 21.1 %copy-start.9 = (f32[2,16]{1,0:T(2,128)S(1)}, f32[2,16]{1,0:T(2,128)}, u32[]{:S(2)}) copy-start(f32[2,16]{1,0:T(2,128)} %param.20) | copy-start | bytes 388
  23.4 5.0 %collective-permute-start.1 = (bf16[2,16,2048]{2,1,0:T(8,128)(2,1)S(1)}, bf16[2,16,2048]{2,1,0:T(8,128)(2,1)S(1)}, u32[]{:S(2)}, u32[]{:S(2)}) collective-permute-start(bf16[2,16,2048]{2,1,0:T(8,128)(2,1)S(1)} %shard_map.137.refs_0_), channel_id=1, source_target_pairs={{0,8},{1,9},{2,10},{3,11},{4,12},{5,13},{6,14},{7,15},{8,0},{9,1},... | collective-permute-start | bytes 393224 | tf_op jit(solution)/shard_map/ppermute | solution.py:97
  23.5 20.9 %collective-permute-start.12 = (bf16[2,16,6144]{2,1,0:T(8,128)(2,1)S(1)}, bf16[2,16,6144]{2,1,0:T(8,128)(2,1)S(1)}, u32[]{:S(2)}, u32[]{:S(2)}) collective-permute-start(bf16[2,16,6144]{2,1,0:T(8,128)(2,1)S(1)} %shard_map.140.refs_3_.refs_0_), channel_id=1, source_target_pairs={{0,2},{1,5},{2,0},{3,7},{4,6},{5,1},{6,4},{7,3},{8,10},{9,13},{10,... | collective-permute-start | bytes 1179656 | tf_op jit(solution)/shard_map/ppermute | solution.py:97
  28.5 9.4 %collective-permute-start.4 = (bf16[4,16,2048]{2,1,0:T(8,128)(2,1)S(1)}, bf16[4,16,2048]{2,1,0:T(8,128)(2,1)S(1)}, u32[]{:S(2)}, u32[]{:S(2)}) collective-permute-start(bf16[4,16,2048]{2,1,0:T(8,128)(2,1)S(1)} %shard_map.141.refs_1_), channel_id=1, source_target_pairs={{0,2},{1,5},{2,0},{3,7},{4,6},{5,1},{6,4},{7,3},{8,10},{9,13},{10,... | collective-permute-start | bytes 786440 | tf_op jit(solution)/shard_map/ppermute | solution.py:97
  30.4 13.5 %collective-permute-start.6 = (bf16[4,16,2048]{2,1,0:T(8,128)(2,1)S(1)}, bf16[4,16,2048]{2,1,0:T(8,128)(2,1)S(1)}, u32[]{:S(2)}, u32[]{:S(2)}) collective-permute-start(bf16[4,16,2048]{2,1,0:T(8,128)(2,1)S(1)} %shard_map.141.refs_1_), channel_id=1, source_target_pairs={{0,6},{1,7},{2,4},{3,5},{4,2},{5,3},{6,0},{7,1},{8,14},{9,15},{10,... | collective-permute-start | bytes 786440 | tf_op jit(solution)/shard_map/ppermute | solution.py:97
  31.9 12.1 %collective-permute-start.5 = (bf16[4,16,2048]{2,1,0:T(8,128)(2,1)S(1)}, bf16[4,16,2048]{2,1,0:T(8,128)(2,1)S(1)}, u32[]{:S(2)}, u32[]{:S(2)}) collective-permute-start(bf16[4,16,2048]{2,1,0:T(8,128)(2,1)S(1)} %shard_map.141.refs_1_), channel_id=1, source_target_pairs={{0,4},{1,3},{2,6},{3,1},{4,0},{5,7},{6,2},{7,5},{8,12},{9,11},{10,... | collective-permute-start | bytes 786440 | tf_op jit(solution)/shard_map/ppermute | solution.py:97
  32.0 12.7 %collective-permute-start.11 = (bf16[2,16,4096]{2,1,0:T(8,128)(2,1)S(1)}, bf16[2,16,4096]{2,1,0:T(8,128)(2,1)S(1)}, u32[]{:S(2)}, u32[]{:S(2)}) collective-permute-start(bf16[2,16,4096]{2,1,0:T(8,128)(2,1)S(1)} %shard_map.139.refs_2_.refs_0_), channel_id=1, source_target_pairs={{0,8},{1,9},{2,10},{3,11},{4,12},{5,13},{6,14},{7,15},{8,0},{9,1},... | collective-permute-start | bytes 786440 | tf_op jit(solution)/shard_map/ppermute | solution.py:97
  37.9 9.3 %collective-permute-start.7 = (bf16[4,16,2048]{2,1,0:T(8,128)(2,1)S(1)}, bf16[4,16,2048]{2,1,0:T(8,128)(2,1)S(1)}, u32[]{:S(2)}, u32[]{:S(2)}) collective-permute-start(bf16[4,16,2048]{2,1,0:T(8,128)(2,1)S(1)} %shard_map.141.refs_1_), channel_id=1, source_target_pairs={{0,1},{1,0},{2,3},{3,2},{4,5},{5,4},{6,7},{7,6},{8,9},{9,8},{10,11... | collective-permute-start | bytes 786440 | tf_op jit(solution)/shard_map/ppermute | solution.py:97
  43.9 5.1 %collective-permute-start.8 = (bf16[4,16,2048]{2,1,0:T(8,128)(2,1)S(1)}, bf16[4,16,2048]{2,1,0:T(8,128)(2,1)S(1)}, u32[]{:S(2)}, u32[]{:S(2)}) collective-permute-start(bf16[4,16,2048]{2,1,0:T(8,128)(2,1)S(1)} %collective-permute-done.4.refs_2_), channel_id=1, source_target_pairs={{0,1},{1,0},{2,3},{3,2},{4,5},{5,4},{6,7},{7,6},{8,9},{9,8},{10,11... | collective-permute-start | bytes 786440 | tf_op jit(solution)/shard_map/ppermute | solution.py:97
  43.9 2.9 %collective-permute-start.10 = (bf16[4,16,2048]{2,1,0:T(8,128)(2,1)S(1)}, bf16[4,16,2048]{2,1,0:T(8,128)(2,1)S(1)}, u32[]{:S(2)}, u32[]{:S(2)}) collective-permute-start(bf16[4,16,2048]{2,1,0:T(8,128)(2,1)S(1)} %collective-permute-done.6.refs_4_), channel_id=1, source_target_pairs={{0,1},{1,0},{2,3},{3,2},{4,5},{5,4},{6,7},{7,6},{8,9},{9,8},{10,11... | collective-permute-start | bytes 786440 | tf_op jit(solution)/shard_map/ppermute | solution.py:97
  44.4 2.6 %collective-permute-start.9 = (bf16[4,16,2048]{2,1,0:T(8,128)(2,1)S(1)}, bf16[4,16,2048]{2,1,0:T(8,128)(2,1)S(1)}, u32[]{:S(2)}, u32[]{:S(2)}) collective-permute-start(bf16[4,16,2048]{2,1,0:T(8,128)(2,1)S(1)} %collective-permute-done.5.refs_3_), channel_id=1, source_target_pairs={{0,1},{1,0},{2,3},{3,2},{4,5},{5,4},{6,7},{7,6},{8,9},{9,8},{10,11... | collective-permute-start | bytes 786440 | tf_op jit(solution)/shard_map/ppermute | solution.py:97
  44.7 4.4 %copy-start.4 = (bf16[640,256]{1,0:T(8,128)(2,1)S(1)}, bf16[640,256]{1,0:T(8,128)(2,1)}, u32[]{:S(2)}) copy-start(bf16[640,256]{1,0:T(8,128)(2,1)} %constant.9.clone.refs_11_.refs_8_) | copy-start | bytes 983044
  44.7 20.2 %collective-permute-start.19 = (bf16[4,16,6144]{2,1,0:T(8,128)(2,1)S(1)}, bf16[4,16,6144]{2,1,0:T(8,128)(2,1)S(1)}, u32[]{:S(2)}, u32[]{:S(2)}) collective-permute-start(bf16[4,16,6144]{2,1,0:T(8,128)(2,1)S(1)} %shard_map.142.refs_2_.refs_0_), channel_id=1, source_target_pairs={{0,8},{1,9},{2,10},{3,11},{4,12},{5,13},{6,14},{7,15},{8,0},{9,1},... | collective-permute-start | bytes 2359304 | tf_op jit(solution)/shard_map/ppermute | solution.py:97
  46.8 25.1 %collective-permute-start.16 = (bf16[4,16,4096]{2,1,0:T(8,128)(2,1)S(1)}, bf16[4,16,4096]{2,1,0:T(8,128)(2,1)S(1)}, u32[]{:S(2)}, u32[]{:S(2)}) collective-permute-start(bf16[4,16,4096]{2,1,0:T(8,128)(2,1)S(1)} %shard_map.143.refs_12_.refs_1_), channel_id=1, source_target_pairs={{0,1},{1,0},{2,3},{3,2},{4,5},{5,4},{6,7},{7,6},{8,9},{9,8},{10,11... | collective-permute-start | bytes 1572872 | tf_op jit(solution)/shard_map/ppermute | solution.py:97
  47.0 14.3 %collective-permute-start.14 = (bf16[4,16,4096]{2,1,0:T(8,128)(2,1)S(1)}, bf16[4,16,4096]{2,1,0:T(8,128)(2,1)S(1)}, u32[]{:S(2)}, u32[]{:S(2)}) collective-permute-start(bf16[4,16,4096]{2,1,0:T(8,128)(2,1)S(1)} %shard_map.143.refs_12_.refs_1_), channel_id=1, source_target_pairs={{0,4},{1,3},{2,6},{3,1},{4,0},{5,7},{6,2},{7,5},{8,12},{9,11},{10,... | collective-permute-start | bytes 1572872 | tf_op jit(solution)/shard_map/ppermute | solution.py:97
  47.2 14.1 %collective-permute-start.13 = (bf16[4,16,4096]{2,1,0:T(8,128)(2,1)S(1)}, bf16[4,16,4096]{2,1,0:T(8,128)(2,1)S(1)}, u32[]{:S(2)}, u32[]{:S(2)}) collective-permute-start(bf16[4,16,4096]{2,1,0:T(8,128)(2,1)S(1)} %shard_map.143.refs_12_.refs_1_), channel_id=1, source_target_pairs={{0,2},{1,5},{2,0},{3,7},{4,6},{5,1},{6,4},{7,3},{8,10},{9,13},{10,... | collective-permute-start | bytes 1572872 | tf_op jit(solution)/shard_map/ppermute | solution.py:97
  61.3 10.7 %collective-permute-start.15 = (bf16[4,16,4096]{2,1,0:T(8,128)(2,1)S(1)}, bf16[4,16,4096]{2,1,0:T(8,128)(2,1)S(1)}, u32[]{:S(2)}, u32[]{:S(2)}) collective-permute-start(bf16[4,16,4096]{2,1,0:T(8,128)(2,1)S(1)} %collective-permute-done.13.refs_2_), channel_id=1, source_target_pairs={{0,4},{1,3},{2,6},{3,1},{4,0},{5,7},{6,2},{7,5},{8,12},{9,11},{10,... | collective-permute-start | bytes 1572872 | tf_op jit(solution)/shard_map/ppermute | solution.py:97
  61.5 10.5 %collective-permute-start.17 = (bf16[4,16,4096]{2,1,0:T(8,128)(2,1)S(1)}, bf16[4,16,4096]{2,1,0:T(8,128)(2,1)S(1)}, u32[]{:S(2)}, u32[]{:S(2)}) collective-permute-start(bf16[4,16,4096]{2,1,0:T(8,128)(2,1)S(1)} %collective-permute-done.13.refs_2_), channel_id=1, source_target_pairs={{0,1},{1,0},{2,3},{3,2},{4,5},{5,4},{6,7},{7,6},{8,9},{9,8},{10,11... | collective-permute-start | bytes 1572872 | tf_op jit(solution)/shard_map/ppermute | solution.py:97
  62.5 9.5 %collective-permute-start.18 = (bf16[4,16,4096]{2,1,0:T(8,128)(2,1)S(1)}, bf16[4,16,4096]{2,1,0:T(8,128)(2,1)S(1)}, u32[]{:S(2)}, u32[]{:S(2)}) collective-permute-start(bf16[4,16,4096]{2,1,0:T(8,128)(2,1)S(1)} %collective-permute-done.14.refs_3_), channel_id=1, source_target_pairs={{0,1},{1,0},{2,3},{3,2},{4,5},{5,4},{6,7},{7,6},{8,9},{9,8},{10,11... | collective-permute-start | bytes 1572872 | tf_op jit(solution)/shard_map/ppermute | solution.py:97
  72.0 2.0 %collective-permute-start.20 = (bf16[4,16,4096]{2,1,0:T(8,128)(2,1)S(1)}, bf16[4,16,4096]{2,1,0:T(8,128)(2,1)S(1)}, u32[]{:S(2)}, u32[]{:S(2)}) collective-permute-start(bf16[4,16,4096]{2,1,0:T(8,128)(2,1)S(1)} %collective-permute-done.15.refs_4_), channel_id=1, source_target_pairs={{0,1},{1,0},{2,3},{3,2},{4,5},{5,4},{6,7},{7,6},{8,9},{9,8},{10,11... | collective-permute-start | bytes 1572872 | tf_op jit(solution)/shard_map/ppermute | solution.py:97
  72.1 16.8 %collective-permute-start.24 = (bf16[8,16,2048]{2,1,0:T(8,128)(2,1)S(1)}, bf16[8,16,2048]{2,1,0:T(8,128)(2,1)S(1)}, u32[]{:S(2)}, u32[]{:S(2)}) collective-permute-start(bf16[8,16,2048]{2,1,0:T(8,128)(2,1)S(1)} %get-tuple-element.50.refs_13_.refs_2_), channel_id=1, source_target_pairs={{0,4},{1,3},{2,6},{3,1},{4,0},{5,7},{6,2},{7,5},{8,12},{9,11},{10,... | collective-permute-start | bytes 1572872 | tf_op jit(solution)/shard_map/ppermute | solution.py:97
  78.8 1.3 %collective-permute-start.21 = (bf16[2,36,512]{2,1,0:T(8,128)(2,1)S(1)}, bf16[2,36,512]{2,1,0:T(8,128)(2,1)S(1)}, u32[]{:S(2)}, u32[]{:S(2)}) collective-permute-start(bf16[2,36,512]{2,1,0:T(8,128)(2,1)S(1)} %get-tuple-element.43), channel_id=1, source_target_pairs={{1,0},{0,1},{3,2},{2,3},{5,4},{4,5},{7,6},{6,7},{9,8},{8,9},{11,10... | collective-permute-start | bytes 221192 | tf_op jit(solution)/shard_map/ppermute | solution.py:365
  80.2 12.5 %copy-start.5 = (f32[144,256]{1,0:T(8,128)S(1)}, f32[144,256]{1,0:T(8,128)}, u32[]{:S(2)}) copy-start(f32[144,256]{1,0:T(8,128)} %constant.10.clone.refs_9_) | copy-start | bytes 442372
  80.2 11.1 %collective-permute-start.22 = (bf16[8,36,512]{2,1,0:T(8,128)(2,1)S(1)}, bf16[8,36,512]{2,1,0:T(8,128)(2,1)S(1)}, u32[]{:S(2)}, u32[]{:S(2)}) collective-permute-start(bf16[8,36,512]{2,1,0:T(8,128)(2,1)S(1)} %shard_map.149), channel_id=1, source_target_pairs={{2,0},{3,1},{4,2},{5,3},{6,4},{7,5},{8,6},{9,7},{10,8},{11,9},{12,... | collective-permute-start | bytes 884744 | tf_op jit(solution)/shard_map/ppermute | solution.py:365
  84.0 8.6 %collective-permute-start.25 = (bf16[8,16,2048]{2,1,0:T(8,128)(2,1)S(1)}, bf16[8,16,2048]{2,1,0:T(8,128)(2,1)S(1)}, u32[]{:S(2)}, u32[]{:S(2)}) collective-permute-start(bf16[8,16,2048]{2,1,0:T(8,128)(2,1)S(1)} %get-tuple-element.50.refs_13_.refs_2_), channel_id=1, source_target_pairs={{0,1},{1,0},{2,3},{3,2},{4,5},{5,4},{6,7},{7,6},{8,9},{9,8},{10,11... | collective-permute-start | bytes 1572872 | tf_op jit(solution)/shard_map/ppermute | solution.py:97
  88.9 3.8 %collective-permute-start.26 = (bf16[8,16,2048]{2,1,0:T(8,128)(2,1)S(1)}, bf16[8,16,2048]{2,1,0:T(8,128)(2,1)S(1)}, u32[]{:S(2)}, u32[]{:S(2)}) collective-permute-start(bf16[8,16,2048]{2,1,0:T(8,128)(2,1)S(1)} %collective-permute-done.24.refs_3_), channel_id=1, source_target_pairs={{0,1},{1,0},{2,3},{3,2},{4,5},{5,4},{6,7},{7,6},{8,9},{9,8},{10,11... | collective-permute-start | bytes 1572872 | tf_op jit(solution)/shard_map/ppermute | solution.py:97
  91.3 14.8 %collective-permute-start.27 = (bf16[8,16,4096]{2,1,0:T(8,128)(2,1)S(1)}, bf16[8,16,4096]{2,1,0:T(8,128)(2,1)S(1)}, u32[]{:S(2)}, u32[]{:S(2)}) collective-permute-start(bf16[8,16,4096]{2,1,0:T(8,128)(2,1)S(1)} %get-tuple-element.53.refs_1_), channel_id=1, source_target_pairs={{0,4},{1,3},{2,6},{3,1},{4,0},{5,7},{6,2},{7,5},{8,12},{9,11},{10,... | collective-permute-start | bytes 3145736 | tf_op jit(solution)/shard_map/ppermute | solution.py:97
  91.3 1.3 collective-permute-start.23
  91.7 14.5 %collective-permute-start.28 = (bf16[8,16,4096]{2,1,0:T(8,128)(2,1)S(1)}, bf16[8,16,4096]{2,1,0:T(8,128)(2,1)S(1)}, u32[]{:S(2)}, u32[]{:S(2)}) collective-permute-start(bf16[8,16,4096]{2,1,0:T(8,128)(2,1)S(1)} %get-tuple-element.53.refs_1_), channel_id=1, source_target_pairs={{0,1},{1,0},{2,3},{3,2},{4,5},{5,4},{6,7},{7,6},{8,9},{9,8},{10,11... | collective-permute-start | bytes 3145736 | tf_op jit(solution)/shard_map/ppermute | solution.py:97
  106.1 2.7 %collective-permute-start.29 = (bf16[8,16,4096]{2,1,0:T(8,128)(2,1)S(1)}, bf16[8,16,4096]{2,1,0:T(8,128)(2,1)S(1)}, u32[]{:S(2)}, u32[]{:S(2)}) collective-permute-start(bf16[8,16,4096]{2,1,0:T(8,128)(2,1)S(1)} %collective-permute-done.27.refs_2_), channel_id=1, source_target_pairs={{0,1},{1,0},{2,3},{3,2},{4,5},{5,4},{6,7},{7,6},{8,9},{9,8},{10,11... | collective-permute-start | bytes 3145736 | tf_op jit(solution)/shard_map/ppermute | solution.py:97
  113.5 1.3 %collective-permute-start.30 = (bf16[2,36,512]{2,1,0:T(8,128)(2,1)S(1)}, bf16[2,36,512]{2,1,0:T(8,128)(2,1)S(1)}, u32[]{:S(2)}, u32[]{:S(2)}) collective-permute-start(bf16[2,36,512]{2,1,0:T(8,128)(2,1)S(1)} %get-tuple-element.55), channel_id=1, source_target_pairs={{1,0},{0,1},{3,2},{2,3},{5,4},{4,5},{7,6},{6,7},{9,8},{8,9},{11,10... | collective-permute-start | bytes 221192 | tf_op jit(solution)/shard_map/ppermute | solution.py:365
  114.9 14.6 %collective-permute-start.31 = (bf16[8,36,512]{2,1,0:T(8,128)(2,1)S(1)}, bf16[8,36,512]{2,1,0:T(8,128)(2,1)S(1)}, u32[]{:S(2)}, u32[]{:S(2)}) collective-permute-start(bf16[8,36,512]{2,1,0:T(8,128)(2,1)S(1)} %shard_map.153), channel_id=1, source_target_pairs={{30,0},{31,1},{0,2},{1,3},{2,4},{3,5},{4,6},{5,7},{6,8},{7,9},{8,1... | collective-permute-start | bytes 884744 | tf_op jit(solution)/shard_map/ppermute | solution.py:365
  128.1 1.3 %collective-permute-start.32 = (bf16[2,36,512]{2,1,0:T(8,128)(2,1)S(1)}, bf16[2,36,512]{2,1,0:T(8,128)(2,1)S(1)}, u32[]{:S(2)}, u32[]{:S(2)}) collective-permute-start(bf16[2,36,512]{2,1,0:T(8,128)(2,1)S(1)} %get-tuple-element.62), channel_id=1, source_target_pairs={{1,0},{0,1},{3,2},{2,3},{5,4},{4,5},{7,6},{6,7},{9,8},{8,9},{11,10... | collective-permute-start | bytes 221192 | tf_op jit(solution)/shard_map/ppermute | solution.py:365

commit v14 on v13

--- a/solution.py
+++ b/solution.py
@@ -88,6 +88,30 @@
     )(*pieces, *sources, *after)
 
 
+def halves_kernel(widths, here_ref, there_ref, *outs):
+    start = 0
+    for index, width in enumerate(widths):
+        for half in range(2):
+            rows, lanes = slice(2 * half, 2 * half + 2), slice(start, start + width)
+            outs[2 * index + half][:2] = here_ref[rows, :, lanes]
+            outs[2 * index + half][2:] = there_ref[rows, :, lanes]
+        start += width
+
+
+def halves(here, there, widths, after):
+    held = pl.BlockSpec(memory_space=pltpu.VMEM)
+    return pl.pallas_call(
+        lambda *refs: halves_kernel(widths, refs[0], refs[1], *refs[2 + len(after) :]),
+        out_shape=[
+            jax.ShapeDtypeStruct((4, here.shape[1], width), jnp.bfloat16)
+            for width in widths
+            for _ in range(2)
+        ],
+        in_specs=[held] * 2 + [ANY] * len(after),
+        compiler_params=pltpu.CompilerParams(vmem_limit_bytes=10 * 2**20),
+    )(here, there, *after)
+
+
 def send(block, move):
     pairs = []
     for lon in range(lax.axis_size("lon")):
@@ -125,38 +149,32 @@
     return [column] + received + [send(part, swap) for part in [column] + received]
 
 
-def load_pieces(pieces, w_ref, stage_ref, sem):
-    if len(pieces) == 1:
-        copy = pltpu.make_async_copy(pieces[0], w_ref, sem.at[0])
-        copy.start()
-        copy.wait()
-        return
-    half = pieces[0].shape[-2]
+def load_pieces(kind, pieces, w_ref, stage_ref, sem):
     copies = [
-        pltpu.make_async_copy(piece, stage_ref.at[index], sem.at[index])
+        pltpu.make_async_copy(piece, w_ref if kind == "rows" else stage_ref.at[index], sem.at[index])
         for index, piece in enumerate(pieces)
     ]
     for copy in copies:
         copy.start()
+    if kind == "rows":
+        copies[0].wait()
+        return
+    half = pieces[0].shape[-2]
     lon, lat = lax.axis_index("lon"), lax.axis_index("lat")
     z, y, x = lon // 4, lon // 2 % 2, lon % 2
     by_x, by_y = y * 2 + 1 - x, (1 - y) * 2 + x
-    parts = len(pieces) // 2
     for index, copy in enumerate(copies):
-        core = lat if index < parts else 1 - lat
-        squares = (
-            y * 2 + x,
-            jnp.where(core == 0, by_x, by_y),
-            jnp.where(core == 0, by_y, by_x),
-            (1 - y) * 2 + 1 - x,
-        )
+        core = lat if index < 4 else 1 - lat
+        own, opposite = y * 2 + x, (1 - y) * 2 + 1 - x
+        one = jnp.where(core == 0, by_x, by_y)
+        other = jnp.where(core == 0, by_y, by_x)
         copy.wait()
-        for step in range(pieces[0].shape[0]):
-            if parts == 4:
-                square, along = squares[index % 4], Z_ORDER[step]
+        for step in range(4):
+            if kind == "columns":
+                square, along = (own, one, other, opposite)[index % 4], Z_ORDER[step]
             else:
-                square = squares[index % 2 * 2 + step // 2 % 2]
-                along = Z_ORDER[step // 4 * 2 + step % 2]
+                pairs = ((own, one), (own, other), (other, opposite), (one, opposite))
+                square, along = pairs[index % 4][step % 2], index % 2 * 2 + step // 2
             row = pl.multiple_of((((z ^ along) * 4 + square) * 2 + core) * half, 16)
             w_ref[pl.ds(row, half), :] = stage_ref[index, step]
 
@@ -170,7 +188,7 @@
     ]
 
 
-def attend_kernel(shifted, row_windows, count, *refs):
+def attend_kernel(shifted, row_windows, kind, count, *refs):
     sources = 2 if shifted else 1
     x_refs, pieces = refs[:sources], refs[sources : sources + count]
     gain_ref, sharp_ref, ones_ref = refs[sources + count : sources + count + 3]
@@ -180,7 +198,7 @@
 
     @pl.when(pl.program_id(0) == 0)
     def _():
-        load_pieces(pieces, w_ref, stage_ref, sem)
+        load_pieces(kind, pieces, w_ref, stage_ref, sem)
 
     if shifted:
         quarters = []
@@ -269,6 +287,7 @@
 
 def attend(sources, columns, pieces, gain, sharp, row_windows, after=(), held=2):
     shifted = len(sources) > 1
+    kind, pieces = pieces
     features = sources[0].shape[-1]
     count = len(columns) * row_windows
     skipped = columns[0] * row_windows // held
@@ -279,7 +298,7 @@
     ones = jnp.asarray(head_columns(), jnp.bfloat16)
     extra = (jnp.asarray(allowed_pairs()),) if shifted else ()
     return pl.pallas_call(
-        functools.partial(attend_kernel, shifted, row_windows, len(pieces)),
+        functools.partial(attend_kernel, shifted, row_windows, kind, len(pieces)),
         grid=(count // held,),
         out_shape=jax.ShapeDtypeStruct((count, CELLS, features), jnp.bfloat16),
         in_specs=([strip_block] * 2 if shifted else [x_block])
@@ -297,14 +316,14 @@
     )(*sources, *pieces, gain, sharp, ones, *extra, *after)
 
 
-def feed_kernel(count, hidden_size, chunk, edge, *refs):
+def feed_kernel(kind, count, hidden_size, chunk, edge, *refs):
     x_ref, pieces, gain_ref = refs[0], refs[1 : 1 + count], refs[1 + count]
     left_ref, right_ref, edge_ref, w_ref, stage_ref, sem = refs[-6:]
     held, _, features = x_ref.shape
 
     @pl.when(pl.program_id(0) == 0)
     def _():
-        load_pieces(pieces, w_ref, stage_ref, sem)
+        load_pieces(kind, pieces, w_ref, stage_ref, sem)
 
     tokens = x_ref[...].reshape(held * CELLS, features)
     total = jnp.zeros(tokens.shape, jnp.float32)
@@ -333,10 +352,11 @@
 
 def feed(windows, column, count, pieces, gain, hidden_size, edge, after=(), held=2):
     _, cells, features = windows.shape
+    kind, pieces = pieces
     block = pl.BlockSpec((held, cells, features), lambda i: (i + column * count // held, 0, 0))
     side = pl.BlockSpec((2 * held, QUARTER, features), lambda i: (i, 0, 0))
     return pl.pallas_call(
-        functools.partial(feed_kernel, len(pieces), hidden_size, 512, edge),
+        functools.partial(feed_kernel, kind, len(pieces), hidden_size, 512, edge),
         grid=(count // held,),
         out_shape=[jax.ShapeDtypeStruct((2 * count, QUARTER, features), jnp.bfloat16)] * 2
         + [jax.ShapeDtypeStruct((2, QUARTER, features), jnp.bfloat16)],
@@ -426,34 +446,40 @@
     if relay:
         (own,) = join([], [[(0, weight) for weight in weights[:2]]])
         feed_own, last_own = join(
-            [], [[(0, weight) for weight in weights[2:]], [(1, weight) for weight in weights]]
+            [],
+            [[(0, weight) for weight in weights[2:]], [(1, weight) for weight in weights]],
+            (own,),
         )
         widths = tuple(sum(weight.shape[2] for weight in pair) for pair in (weights[:2], weights[2:]))
         (pair,) = join([[own, across_z(own, 2)]], (), (windows,))
         (feed_pair,) = join([[feed_own, across_z(feed_own, 2)]])
-        (last_pair,) = join([[last_own, across_z(last_own, 2)]])
-        (column,) = join([[pair, across_z(pair, 1)]], (), (feed_pair, last_pair))
+        (column,) = join([[pair, across_z(pair, 1)]], (), (feed_pair,))
         received = [send(column, way) for way in (beside, across, corner)]
         sent = [tied(column, received[0])] + received
-        pieces = [column] + received + [send(part, swap) for part in sent]
-        (last_four,) = join([[last_pair, send(last_pair, beside)]])
+        pieces = "columns", [column] + received + [send(part, swap) for part in sent]
+        last_own = tied(last_own, pair)
+        last_other = across_z(last_own, 2)
+        (last_four,) = join(
+            [[last_own, send(last_own, beside), last_other, send(last_other, across)]]
+        )
         (feed_column,) = join([[feed_pair, across_z(feed_pair, 1)]], (), (last_four,))
         received = [send(feed_column, way) for way in (beside, across)]
         last_other = across_z(last_four, 1)
         middle_0 = attention(0, [windows], (0,), pieces, (feed_column,))
-        received.append(send(tied(received[0], middle_0), across))
-        last_column, final_column = join([[last_four, last_other]], (), (middle_0,), widths)
-        middle_1 = attention(0, [windows], (1,), pieces, (middle_0, last_column))
-        swapped = [send(part, swap) for part in [feed_column] + tied(received[:2], middle_0)]
-        swapped.append(send(tied(received[2], (middle_1, *swapped)), swap))
-        feed_pieces = [feed_column] + received + swapped
+        first, second = tied((received[0][:2], received[1][2:]), middle_0)
+        corners = [send(first, across), send(second, beside)]
+        *last_columns, final_one, final_other = halves(last_four, last_other, widths, (middle_0,))
+        middle_1 = attention(0, [windows], (1,), pieces, (middle_0, last_columns[0]))
+        swapped = [send(part, swap) for part in [feed_column] + tied(received, middle_0)]
+        received += join([tied(corners, (middle_1, *swapped))])
+        feed_pieces = "columns", [feed_column] + received + swapped + [send(received[2], swap)]
     else:
         gathered = []
         for block in range(2):
             for pair in (weights[:2], weights[2:]):
                 chunk = jnp.concatenate([weight[block] for weight in pair], 1)
-                gathered.append([lax.all_gather(chunk, "lon", axis=0, tiled=True)])
-        pieces, feed_pieces, last_pieces, final_pieces = gathered
+                gathered.append(lax.all_gather(chunk, "lon", axis=0, tiled=True))
+        pieces, feed_pieces, last_pieces, final_pieces = (("rows", [rows]) for rows in gathered)
         middle_0 = attention(0, [windows], (0,), pieces)
         middle_1 = attention(0, [windows], (1,), pieces)
     left_0, right_0, low_0 = forward(0, middle_0, 0, feed_pieces, low_edge)
@@ -462,13 +488,20 @@
     (ahead,) = strips([left_0, below_0], [[(0, 1, size - 1), (1, 0, 1)]])
     ahead = shift_from(ahead, 1, 0)
     if relay:
-        last_received = send(tied(last_column, middle_1), across)
+        last_received = [
+            send(part, way) for part, way in zip(tied(last_columns, middle_1), (across, beside))
+        ]
     left_1, right_1, low_1 = forward(0, middle_1, 0, feed_pieces, low_edge, (below_0,))
     below_1 = shift_from(tied(low_1, ahead), 0, 1)
     if relay:
-        last_pieces = [last_column, last_received, send(last_column, swap)]
-        last_pieces.append(send(tied(last_received, low_1), swap))
-        final_received = send(tied(final_column, (last_received, ahead)), across)
+        last_pieces = last_columns + last_received
+        last_pieces += [send(part, swap) for part in last_columns + tied(last_received, low_1)]
+        last_pieces = "halves", last_pieces
+        final_columns = [final_one, final_other]
+        final_received = [
+            send(part, way)
+            for part, way in zip(tied(final_columns, (last_received, ahead)), (across, beside))
+        ]
     lefts = strips(
         [right_0, left_1, right_1, below_0, below_1],
         [
@@ -479,8 +512,9 @@
     )
     middle_1 = attention(1, [lefts[2], ahead], (1,), last_pieces)
     if relay:
-        final_pieces = [final_column, final_received, send(final_column, swap)]
-        final_pieces.append(send(tied(final_received, middle_1), swap))
+        final_pieces = final_columns + final_received
+        final_pieces += [send(part, swap) for part in final_columns + tied(final_received, middle_1)]
+        final_pieces = "halves", final_pieces
     left_1, right_1, high_1 = forward(1, middle_1, 0, final_pieces, high_edge)
     above_1 = shift_from(high_1, 0, -1)
     (behind,) = strips([above_1, right_1], [[(0, 1, 1), (1, 0, size - 1)]])

time: 132 us -> 128 us (0.970)
  waiting for transfers between devices: 50.6 us -> 35 us
  starting transfers between devices: 26.3 us -> 35.5 us
    ppermute x27 -> x35, waiting for transfers between devices: 44.4 us -> 28.7 us  [send(): return lax.ppermute(block, ('lon', 'lat'), pairs)]
    ppermute x27 -> x35, starting transfers between devices: 20.1 us -> 30.5 us  [send(): return lax.ppermute(block, ('lon', 'lat'), pairs)]
    pallas_call x8 -> x9, Pallas kernels: 46.8 us -> 47.2 us  [the longest x4 27.7 us: attend(): pl.pallas_call(functools.partial(attend_kernel, shifted, row_windows, kin...]
  transfers between devices with their start and end apart: 33 -> 41, of which waited for: 14 -> 14; matrix products, arithmetic and copies ran while one was open for 1% -> 1% of each run, Pallas kernels for 32% -> 33%
where the time goes in v14:
time: 128 us; the launch traced here: 127 us
  Pallas kernels  47.6 us (37%)
  starting transfers between devices  35.5 us (28%)
  waiting for transfers between devices  35 us (27%)
  local copies, waits for them, and re-layouts  8.8 us (7%)
    ppermute x35, starting transfers between devices, send(): return lax.ppermute(block, ('lon', 'lat'), pairs)  30.5 us
    ppermute x35, waiting for transfers between devices, send(): return lax.ppermute(block, ('lon', 'lat'), pairs)  28.7 us
    pallas_call x4, Pallas kernels, attend(): pl.pallas_call(functools.partial(attend_kernel, shifted, row_windows, kin...  27.7 us
    pallas_call x4, Pallas kernels, feed(): pl.pallas_call(functools.partial(feed_kernel, kind, len(pieces), hidden_s...  19.3 us
    ppermute x6, waiting for transfers between devices, shift_from(): return lax.ppermute(block, ('lon', 'lat'), pairs)  6.3 us
    ppermute x6, starting transfers between devices, shift_from(): return lax.ppermute(block, ('lon', 'lat'), pairs)  4.97 us
    unnamed x20, local copies, waits for them, and re-layouts  4.86 us
  transfers between devices with their start and end apart: 41, of which 14 were waited for; matrix products, arithmetic and copies ran while one was open for 1% of the time, Pallas kernels for 33%

profile of v14, /device:TPU:0, one launch (start us, length us, event | category | flops | bytes accessed | tf_op | source)
XLA Modules:
  0.0 127.3 jit_solution(10713528828458887146)
XLA Ops:
  0.0 0.9 copy-done.2
  0.9 0.8 copy-done.3
  1.8 4.0 %collective-permute-start = (bf16[1,16,2048]{2,1,0:T(8,128)(2,1)S(1)}, bf16[1,16,2048]{2,1,0:T(8,128)(2,1)S(1)}, u32[]{:S(2)}, u32[]{:S(2)}) collective-permute-start(bf16[1,16,2048]{2,1,0:T(8,128)(2,1)S(1)} %shard_map.136.refs_0_.refs_6_), channel_id=1, source_target_pairs={{0,16},{1,17},{2,18},{3,19},{4,20},{5,21},{6,22},{7,23},{8,24},{9,... | collective-permute-start | bytes 196616 | tf_op jit(solution)/shard_map/ppermute | solution.py:121
  5.8 0.9 copy-done
  6.8 0.9 copy-done.1
  7.8 1.2 copy-done.6
  9.0 0.8 copy.26
  9.8 0.5 reshape.15.refs_2_.refs_0_
  10.4 3.0 %collective-permute-start.1 = (bf16[2,16,2048]{2,1,0:T(8,128)(2,1)S(1)}, bf16[2,16,2048]{2,1,0:T(8,128)(2,1)S(1)}, u32[]{:S(2)}, u32[]{:S(2)}) collective-permute-start(bf16[2,16,2048]{2,1,0:T(8,128)(2,1)S(1)} %shard_map.137.refs_0_), channel_id=1, source_target_pairs={{0,8},{1,9},{2,10},{3,11},{4,12},{5,13},{6,14},{7,15},{8,0},{9,1},... | collective-permute-start | bytes 393224 | tf_op jit(solution)/shard_map/ppermute | solution.py:121
  13.4 3.2 %collective-permute-done.2.refs_1_ = bf16[1,16,4096]{2,1,0:T(8,128)(2,1)S(1)} collective-permute-done((bf16[1,16,4096]{2,1,0:T(8,128)(2,1)S(1)}, bf16[1,16,4096]{2,1,0:T(8,128)(2,1)S(1)}, u32[]{:S(2)}, u32[]{:S(2)}) %collective-permute-start.2) | collective-permute-done | bytes 131104 | tf_op jit(solution)/shard_map/ppermute | solution.py:121
  16.6 1.3 %collective-permute-done.1.refs_1_ = bf16[2,16,2048]{2,1,0:T(8,128)(2,1)S(1)} collective-permute-done((bf16[2,16,2048]{2,1,0:T(8,128)(2,1)S(1)}, bf16[2,16,2048]{2,1,0:T(8,128)(2,1)S(1)}, u32[]{:S(2)}, u32[]{:S(2)}) %collective-permute-start.1) | collective-permute-done | bytes 131104 | tf_op jit(solution)/shard_map/ppermute | solution.py:121
  17.9 1.6 %collective-permute-start.3 = (bf16[4,16,2048]{2,1,0:T(8,128)(2,1)S(1)}, bf16[4,16,2048]{2,1,0:T(8,128)(2,1)S(1)}, u32[]{:S(2)}, u32[]{:S(2)}) collective-permute-start(bf16[4,16,2048]{2,1,0:T(8,128)(2,1)S(1)} %shard_map.140.refs_1_), channel_id=1, source_target_pairs={{0,2},{1,5},{2,0},{3,7},{4,6},{5,1},{6,4},{7,3},{8,10},{9,13},{10,... | collective-permute-start | bytes 786440 | tf_op jit(solution)/shard_map/ppermute | solution.py:121
  19.5 1.8 %collective-permute-start.12 = (bf16[1,16,6144]{2,1,0:T(8,128)(2,1)S(1)}, bf16[1,16,6144]{2,1,0:T(8,128)(2,1)S(1)}, u32[]{:S(2)}, u32[]{:S(2)}) collective-permute-start(bf16[1,16,6144]{2,1,0:T(8,128)(2,1)S(1)} %get-tuple-element.46.refs_0_), channel_id=1, source_target_pairs={{0,16},{1,17},{2,18},{3,19},{4,20},{5,21},{6,22},{7,23},{8,24},{9,... | collective-permute-start | bytes 589832 | tf_op jit(solution)/shard_map/ppermute | solution.py:121
  21.3 1.5 %collective-permute-start.4 = (bf16[4,16,2048]{2,1,0:T(8,128)(2,1)S(1)}, bf16[4,16,2048]{2,1,0:T(8,128)(2,1)S(1)}, u32[]{:S(2)}, u32[]{:S(2)}) collective-permute-start(bf16[4,16,2048]{2,1,0:T(8,128)(2,1)S(1)} %shard_map.140.refs_1_), channel_id=1, source_target_pairs={{0,4},{1,3},{2,6},{3,1},{4,0},{5,7},{6,2},{7,5},{8,12},{9,11},{10,... | collective-permute-start | bytes 786440 | tf_op jit(solution)/shard_map/ppermute | solution.py:121
  22.8 0.5 collective-permute-start.5
  23.3 1.5 %collective-permute-start.11 = (bf16[1,16,6144]{2,1,0:T(8,128)(2,1)S(1)}, bf16[1,16,6144]{2,1,0:T(8,128)(2,1)S(1)}, u32[]{:S(2)}, u32[]{:S(2)}) collective-permute-start(bf16[1,16,6144]{2,1,0:T(8,128)(2,1)S(1)} %get-tuple-element.46.refs_0_), channel_id=1, source_target_pairs={{0,2},{1,5},{2,0},{3,7},{4,6},{5,1},{6,4},{7,3},{8,10},{9,13},{10,... | collective-permute-start | bytes 589832 | tf_op jit(solution)/shard_map/ppermute | solution.py:121
  24.8 3.9 %collective-permute-done.12.refs_2_ = bf16[1,16,6144]{2,1,0:T(8,128)(2,1)S(1)} collective-permute-done((bf16[1,16,6144]{2,1,0:T(8,128)(2,1)S(1)}, bf16[1,16,6144]{2,1,0:T(8,128)(2,1)S(1)}, u32[]{:S(2)}, u32[]{:S(2)}) %collective-permute-start.12) | collective-permute-done | bytes 196640 | tf_op jit(solution)/shard_map/ppermute | solution.py:121
  28.7 0.7 collective-permute-start.10
  29.4 0.5 collective-permute-start.13
  29.9 6.9 %collective-permute-done.11.refs_1_ = bf16[1,16,6144]{2,1,0:T(8,128)(2,1)S(1)} collective-permute-done((bf16[1,16,6144]{2,1,0:T(8,128)(2,1)S(1)}, bf16[1,16,6144]{2,1,0:T(8,128)(2,1)S(1)}, u32[]{:S(2)}, u32[]{:S(2)}) %collective-permute-start.11) | collective-permute-done | bytes 196640 | tf_op jit(solution)/shard_map/ppermute | solution.py:121
  36.8 0.5 collective-permute-start.7
  37.4 0.4 collective-permute-start.9
  37.9 0.1 multiply_reduce_fusion
  38.0 0.7 collective-permute-start.18
  38.8 1.5 %collective-permute-start.14 = (bf16[4,16,4096]{2,1,0:T(8,128)(2,1)S(1)}, bf16[4,16,4096]{2,1,0:T(8,128)(2,1)S(1)}, u32[]{:S(2)}, u32[]{:S(2)}) collective-permute-start(bf16[4,16,4096]{2,1,0:T(8,128)(2,1)S(1)} %shard_map.142.refs_12_.refs_1_), channel_id=1, source_target_pairs={{0,2},{1,5},{2,0},{3,7},{4,6},{5,1},{6,4},{7,3},{8,10},{9,13},{10,... | collective-permute-start | bytes 1572872 | tf_op jit(solution)/shard_map/ppermute | solution.py:121
  40.3 1.5 %collective-permute-start.15 = (bf16[4,16,4096]{2,1,0:T(8,128)(2,1)S(1)}, bf16[4,16,4096]{2,1,0:T(8,128)(2,1)S(1)}, u32[]{:S(2)}, u32[]{:S(2)}) collective-permute-start(bf16[4,16,4096]{2,1,0:T(8,128)(2,1)S(1)} %shard_map.142.refs_12_.refs_1_), channel_id=1, source_target_pairs={{0,4},{1,3},{2,6},{3,1},{4,0},{5,7},{6,2},{7,5},{8,12},{9,11},{10,... | collective-permute-start | bytes 1572872 | tf_op jit(solution)/shard_map/ppermute | solution.py:121
  41.9 6.9 %shard_map.143.refs_2_.refs_12_.refs_0_ = bf16[4,144,512]{2,1,0:T(8,128)(2,1)S(1)} custom-call(bf16[8,144,512]{2,1,0:T(8,128)(2,1)S(1)} %reshape.15.refs_2_.refs_0_, bf16[4,16,2048]{2,1,0:T(8,128)(2,1)S(1)} %shard_map.140.refs_1_, bf16[4,16,2048]{2,1,0:T(8,128)(2,1)S(1)} %collective-permute-done.3.refs_2_, ...), custom_call_target="tpu_custom_call" | custom-call | flops 8000000000 | bytes 6000000 | tf_op jit(solution)/shard_map/pallas_call | solution.py:300
  48.8 4.6 %collective-permute-done.14.refs_2_ = bf16[4,16,4096]{2,1,0:T(8,128)(2,1)S(1)} collective-permute-done((bf16[4,16,4096]{2,1,0:T(8,128)(2,1)S(1)}, bf16[4,16,4096]{2,1,0:T(8,128)(2,1)S(1)}, u32[]{:S(2)}, u32[]{:S(2)}) %collective-permute-start.14) | collective-permute-done | bytes 524320 | tf_op jit(solution)/shard_map/ppermute | solution.py:121
  53.4 1.2 collective-permute-start.16
  54.6 1.5 %collective-permute-start.17 = (bf16[2,16,4096]{2,1,0:T(8,128)(2,1)S(1)}, bf16[2,16,4096]{2,1,0:T(8,128)(2,1)S(1)}, u32[]{:S(2)}, u32[]{:S(2)}) collective-permute-start(bf16[2,16,4096]{2,1,0:T(8,128)(2,1)S(1)} %slice.40), channel_id=1, source_target_pairs={{0,2},{1,5},{2,0},{3,7},{4,6},{5,1},{6,4},{7,3},{8,10},{9,13},{10,... | collective-permute-start | bytes 786440 | tf_op jit(solution)/shard_map/ppermute | solution.py:121
  56.1 1.5 %collective-permute-done.18.refs_1_ = bf16[4,16,6144]{2,1,0:T(8,128)(2,1)S(1)} collective-permute-done((bf16[4,16,6144]{2,1,0:T(8,128)(2,1)S(1)}, bf16[4,16,6144]{2,1,0:T(8,128)(2,1)S(1)}, u32[]{:S(2)}, u32[]{:S(2)}) %collective-permute-start.18) | collective-permute-done | bytes 786464 | tf_op jit(solution)/shard_map/ppermute | solution.py:121
  57.6 0.1 shard_map.144
  57.7 6.9 %shard_map.145.refs_0_ = bf16[4,144,512]{2,1,0:T(8,128)(2,1)S(1)} custom-call(bf16[8,144,512]{2,1,0:T(8,128)(2,1)S(1)} %reshape.15.refs_2_.refs_0_, bf16[4,16,2048]{2,1,0:T(8,128)(2,1)S(1)} %shard_map.140.refs_1_, bf16[4,16,2048]{2,1,0:T(8,128)(2,1)S(1)} %collective-permute-done.3.refs_2_, bf16[4,16,2048]{2,1,0:T(8,128)(2,1)S(1)} %collective-permute-done.4.refs_3_, ...), custom_call_target="tpu_custom_call" | custom-call | flops 8000000000 | bytes 6000000 | tf_op jit(solution)/shard_map/pallas_call | solution.py:300
  64.8 0.6 collective-permute-start.22
  65.4 0.9 collective-permute-start.26
  66.2 1.5 %collective-permute-start.27 = (bf16[4,16,2048]{2,1,0:T(8,128)(2,1)S(1)}, bf16[4,16,2048]{2,1,0:T(8,128)(2,1)S(1)}, u32[]{:S(2)}, u32[]{:S(2)}) collective-permute-start(bf16[4,16,2048]{2,1,0:T(8,128)(2,1)S(1)} %get-tuple-element.64.refs_3_), channel_id=1, source_target_pairs={{0,2},{1,5},{2,0},{3,7},{4,6},{5,1},{6,4},{7,3},{8,10},{9,13},{10,... | collective-permute-start | bytes 786440 | tf_op jit(solution)/shard_map/ppermute | solution.py:121
  67.7 4.8 %shard_map.147 = (bf16[8,36,512]{2,1,0:T(8,128)(2,1)S(1)}, bf16[8,36,512]{2,1,0:T(8,128)(2,1)S(1)}, bf16[2,36,512]{2,1,0:T(8,128)(2,1)S(1)}) custom-call(bf16[4,144,512]{2,1,0:T(8,128)(2,1)S(1)} %shard_map.143.refs_2_.refs_12_.refs_0_, bf16[4,16,4096]{2,1,0:T(8,128)(2,1)S(1)} %shard_map.142.refs_12_.refs_1_, ...), custom_call_target="tpu_custom_call" | custom-call | flops 1000000 | bytes 100000 | tf_op jit(solution)/shard_map/pallas_call | solution.py:358
  72.6 1.3 collective-permute-done.23.refs_10_.refs_1_.refs_3_
  73.9 3.4 %collective-permute-start.24 = (bf16[8,36,512]{2,1,0:T(8,128)(2,1)S(1)}, bf16[8,36,512]{2,1,0:T(8,128)(2,1)S(1)}, u32[]{:S(2)}, u32[]{:S(2)}) collective-permute-start(bf16[8,36,512]{2,1,0:T(8,128)(2,1)S(1)} %shard_map.149), channel_id=1, source_target_pairs={{2,0},{3,1},{4,2},{5,3},{6,4},{7,5},{8,6},{9,7},{10,8},{11,9},{12,... | collective-permute-start | bytes 884744 | tf_op jit(solution)/shard_map/ppermute | solution.py:385
  77.4 0.5 collective-permute-start.29
  77.9 4.8 %shard_map.148 = (bf16[8,36,512]{2,1,0:T(8,128)(2,1)S(1)}, bf16[8,36,512]{2,1,0:T(8,128)(2,1)S(1)}, bf16[2,36,512]{2,1,0:T(8,128)(2,1)S(1)}) custom-call(bf16[4,144,512]{2,1,0:T(8,128)(2,1)S(1)} %shard_map.145.refs_0_, bf16[4,16,4096]{2,1,0:T(8,128)(2,1)S(1)} %shard_map.142.refs_12_.refs_1_, bf16[4,16,4096]{2,1,0:T(8,128)(2,1)S(1)} %collective-permute-done.14.refs_2_, ...), custom_call_target="tpu_custom_call" | custom-call | flops 1000000 | bytes 100000 | tf_op jit(solution)/shard_map/pallas_call | solution.py:358
  82.8 0.5 collective-permute-start.31
  83.3 1.3 %collective-permute-done.24.refs_1_ = bf16[8,36,512]{2,1,0:T(8,128)(2,1)S(1)} collective-permute-done((bf16[8,36,512]{2,1,0:T(8,128)(2,1)S(1)}, bf16[8,36,512]{2,1,0:T(8,128)(2,1)S(1)}, u32[]{:S(2)}, u32[]{:S(2)}) %collective-permute-start.24) | collective-permute-done | bytes 294944 | tf_op jit(solution)/shard_map/ppermute | solution.py:385
  84.7 1.3 %collective-permute-done.25.refs_4_ = bf16[2,36,512]{2,1,0:T(8,128)(2,1)S(1)} collective-permute-done((bf16[2,36,512]{2,1,0:T(8,128)(2,1)S(1)}, bf16[2,36,512]{2,1,0:T(8,128)(2,1)S(1)}, u32[]{:S(2)}, u32[]{:S(2)}) %collective-permute-start.25) | collective-permute-done | bytes 73760 | tf_op jit(solution)/shard_map/ppermute | solution.py:385
  85.9 0.2 collective-permute-start.34
  86.2 0.4 collective-permute-start.35
  86.6 0.4 collective-permute-start.32
  87.0 2.4 %collective-permute-start.33 = (bf16[4,16,4096]{2,1,0:T(8,128)(2,1)S(1)}, bf16[4,16,4096]{2,1,0:T(8,128)(2,1)S(1)}, u32[]{:S(2)}, u32[]{:S(2)}) collective-permute-start(bf16[4,16,4096]{2,1,0:T(8,128)(2,1)S(1)} %get-tuple-element.70.refs_2_), channel_id=1, source_target_pairs={{0,2},{1,5},{2,0},{3,7},{4,6},{5,1},{6,4},{7,3},{8,10},{9,13},{10,... | collective-permute-start | bytes 1572872 | tf_op jit(solution)/shard_map/ppermute | solution.py:121
  89.4 6.9 %shard_map.151.refs_0_ = bf16[4,144,512]{2,1,0:T(8,128)(2,1)S(1)} custom-call(bf16[8,36,512]{2,1,0:T(8,128)(2,1)S(1)} %get-tuple-element.61.refs_0_, bf16[8,36,512]{2,1,0:T(8,128)(2,1)S(1)} %collective-permute-done.24.refs_1_, bf16[4,16,2048]{2,1,0:T(8,128)(2,1)S(1)} %get-tuple-element.63.refs_13_.refs_2_, ...), custom_call_target="tpu_custom_call" | custom-call | flops 8000000000 | bytes 6000000 | tf_op jit(solution)/shard_map/pallas_call | solution.py:300
  96.3 5.0 %collective-permute-done.32.refs_3_ = bf16[4,16,4096]{2,1,0:T(8,128)(2,1)S(1)} collective-permute-done((bf16[4,16,4096]{2,1,0:T(8,128)(2,1)S(1)}, bf16[4,16,4096]{2,1,0:T(8,128)(2,1)S(1)}, u32[]{:S(2)}, u32[]{:S(2)}) %collective-permute-start.32) | collective-permute-done | bytes 524320 | tf_op jit(solution)/shard_map/ppermute | solution.py:121
  101.4 0.1 collective-permute-start.36
  101.5 0.4 collective-permute-start.37
  101.9 1.4 %collective-permute-done.36.refs_7_ = bf16[4,16,4096]{2,1,0:T(8,128)(2,1)S(1)} collective-permute-done((bf16[4,16,4096]{2,1,0:T(8,128)(2,1)S(1)}, bf16[4,16,4096]{2,1,0:T(8,128)(2,1)S(1)}, u32[]{:S(2)}, u32[]{:S(2)}) %collective-permute-start.36) | collective-permute-done | bytes 524320 | tf_op jit(solution)/shard_map/ppermute | solution.py:121
  103.3 0.7 collective-permute-done.37.refs_8_
  104.0 4.8 %shard_map.152 = (bf16[8,36,512]{2,1,0:T(8,128)(2,1)S(1)}, bf16[8,36,512]{2,1,0:T(8,128)(2,1)S(1)}, bf16[2,36,512]{2,1,0:T(8,128)(2,1)S(1)}) custom-call(bf16[4,144,512]{2,1,0:T(8,128)(2,1)S(1)} %shard_map.151.refs_0_, bf16[4,16,4096]{2,1,0:T(8,128)(2,1)S(1)} %get-tuple-element.69.refs_1_, bf16[4,16,4096]{2,1,0:T(8,128)(2,1)S(1)} %get-tuple-element.70.refs_2_, ...), custom_call_target="tpu_custom_call" | custom-call | flops 1000000 | bytes 100000 | tf_op jit(solution)/shard_map/pallas_call | solution.py:358
  108.9 0.2 collective-permute-start.38
  109.1 1.1 collective-permute-done.38.refs_0_.refs_14_.refs_5_
  110.2 1.2 collective-permute-start.39
  111.5 6.9 %shard_map.154.refs_0_ = bf16[4,144,512]{2,1,0:T(8,128)(2,1)S(1)} custom-call(bf16[8,36,512]{2,1,0:T(8,128)(2,1)S(1)} %get-tuple-element.75.refs_0_, bf16[8,36,512]{2,1,0:T(8,128)(2,1)S(1)} %get-tuple-element.76.refs_1_, bf16[4,16,2048]{2,1,0:T(8,128)(2,1)S(1)} %get-tuple-element.63.refs_13_.refs_2_, bf16[4,16,2048]{2,1,0:T(8,128)(2,1)S(1)} %get-tuple-element.64.refs_3_, ...), custom_call_target="tpu_custom_call" | custom-call | flops 8000000000 | bytes 6000000 | tf_op jit(solution)/shard_map/pallas_call | solution.py:300
  118.4 4.9 %shard_map.155 = (bf16[8,36,512]{2,1,0:T(8,128)(2,1)S(1)}, bf16[8,36,512]{2,1,0:T(8,128)(2,1)S(1)}, bf16[2,36,512]{2,1,0:T(8,128)(2,1)S(1)}) custom-call(bf16[4,144,512]{2,1,0:T(8,128)(2,1)S(1)} %shard_map.154.refs_0_, bf16[4,16,4096]{2,1,0:T(8,128)(2,1)S(1)} %get-tuple-element.69.refs_1_, bf16[4,16,4096]{2,1,0:T(8,128)(2,1)S(1)} %get-tuple-element.70.refs_2_, ...), custom_call_target="tpu_custom_call" | custom-call | flops 1000000 | bytes 100000 | tf_op jit(solution)/shard_map/pallas_call | solution.py:358
  123.3 1.3 collective-permute-done.40.refs_4_
  124.6 0.1 shard_map.156
  124.7 0.4 copy.23
  125.1 2.2 %copy.24 = bf16[4,6,8,3,2,512]{5,4,3,2,1,0:T(2,128)(2,1)} copy(bf16[4,6,8,3,2,512]{5,2,0,4,3,1:T(8,128)(2,1)S(1)} %bitcast.16) | data formatting | bytes 2359296 | tf_op jit(solution)/shard_map/transpose | solution.py:423
  (68 shorter events, 0.9 us)
Async XLA Ops:
  0.0 0.9 copy-start.2
  0.9 0.8 copy-start.3
  1.8 8.6 %collective-permute-start = (bf16[1,16,2048]{2,1,0:T(8,128)(2,1)S(1)}, bf16[1,16,2048]{2,1,0:T(8,128)(2,1)S(1)}, u32[]{:S(2)}, u32[]{:S(2)}) collective-permute-start(bf16[1,16,2048]{2,1,0:T(8,128)(2,1)S(1)} %shard_map.136.refs_0_.refs_6_), channel_id=1, source_target_pairs={{0,16},{1,17},{2,18},{3,19},{4,20},{5,21},{6,22},{7,23},{8,24},{9,... | collective-permute-start | bytes 196616 | tf_op jit(solution)/shard_map/ppermute | solution.py:121
  5.8 0.9 copy-start
  6.8 0.9 copy-start.1
  7.7 1.3 copy-start.6
  7.7 8.8 %collective-permute-start.2 = (bf16[1,16,4096]{2,1,0:T(8,128)(2,1)S(1)}, bf16[1,16,4096]{2,1,0:T(8,128)(2,1)S(1)}, u32[]{:S(2)}, u32[]{:S(2)}) collective-permute-start(bf16[1,16,4096]{2,1,0:T(8,128)(2,1)S(1)} %get-tuple-element.43.refs_0_), channel_id=1, source_target_pairs={{0,16},{1,17},{2,18},{3,19},{4,20},{5,21},{6,22},{7,23},{8,24},{9,... | collective-permute-start | bytes 393224 | tf_op jit(solution)/shard_map/ppermute | solution.py:121
  10.3 19.6 %copy-start.8 = (f32[2,2,512]{2,1,0:T(2,128)S(1)}, f32[2,2,512]{2,1,0:T(2,128)}, u32[]{:S(2)}) copy-start(f32[2,2,512]{2,1,0:T(2,128)} %param.19) | copy-start | bytes 24580
  10.3 27.6 %copy-start.7 = (f32[16,512]{1,0:T(8,128)S(1)}, f32[16,512]{1,0:T(8,128)}, u32[]{:S(2)}) copy-start(f32[16,512]{1,0:T(8,128)} %constant.8.clone) | copy-start | bytes 98308
  10.3 27.5 %copy-start.9 = (f32[2,16]{1,0:T(2,128)S(1)}, f32[2,16]{1,0:T(2,128)}, u32[]{:S(2)}) copy-start(f32[2,16]{1,0:T(2,128)} %param.20) | copy-start | bytes 388
  10.4 7.5 %collective-permute-start.1 = (bf16[2,16,2048]{2,1,0:T(8,128)(2,1)S(1)}, bf16[2,16,2048]{2,1,0:T(8,128)(2,1)S(1)}, u32[]{:S(2)}, u32[]{:S(2)}) collective-permute-start(bf16[2,16,2048]{2,1,0:T(8,128)(2,1)S(1)} %shard_map.137.refs_0_), channel_id=1, source_target_pairs={{0,8},{1,9},{2,10},{3,11},{4,12},{5,13},{6,14},{7,15},{8,0},{9,1},... | collective-permute-start | bytes 393224 | tf_op jit(solution)/shard_map/ppermute | solution.py:121
  17.9 11.5 %collective-permute-start.3 = (bf16[4,16,2048]{2,1,0:T(8,128)(2,1)S(1)}, bf16[4,16,2048]{2,1,0:T(8,128)(2,1)S(1)}, u32[]{:S(2)}, u32[]{:S(2)}) collective-permute-start(bf16[4,16,2048]{2,1,0:T(8,128)(2,1)S(1)} %shard_map.140.refs_1_), channel_id=1, source_target_pairs={{0,2},{1,5},{2,0},{3,7},{4,6},{5,1},{6,4},{7,3},{8,10},{9,13},{10,... | collective-permute-start | bytes 786440 | tf_op jit(solution)/shard_map/ppermute | solution.py:121
  19.5 9.2 %collective-permute-start.12 = (bf16[1,16,6144]{2,1,0:T(8,128)(2,1)S(1)}, bf16[1,16,6144]{2,1,0:T(8,128)(2,1)S(1)}, u32[]{:S(2)}, u32[]{:S(2)}) collective-permute-start(bf16[1,16,6144]{2,1,0:T(8,128)(2,1)S(1)} %get-tuple-element.46.refs_0_), channel_id=1, source_target_pairs={{0,16},{1,17},{2,18},{3,19},{4,20},{5,21},{6,22},{7,23},{8,24},{9,... | collective-permute-start | bytes 589832 | tf_op jit(solution)/shard_map/ppermute | solution.py:121
  21.3 15.6 %collective-permute-start.4 = (bf16[4,16,2048]{2,1,0:T(8,128)(2,1)S(1)}, bf16[4,16,2048]{2,1,0:T(8,128)(2,1)S(1)}, u32[]{:S(2)}, u32[]{:S(2)}) collective-permute-start(bf16[4,16,2048]{2,1,0:T(8,128)(2,1)S(1)} %shard_map.140.refs_1_), channel_id=1, source_target_pairs={{0,4},{1,3},{2,6},{3,1},{4,0},{5,7},{6,2},{7,5},{8,12},{9,11},{10,... | collective-permute-start | bytes 786440 | tf_op jit(solution)/shard_map/ppermute | solution.py:121
  22.8 14.6 %collective-permute-start.5 = (bf16[4,16,2048]{2,1,0:T(8,128)(2,1)S(1)}, bf16[4,16,2048]{2,1,0:T(8,128)(2,1)S(1)}, u32[]{:S(2)}, u32[]{:S(2)}) collective-permute-start(bf16[4,16,2048]{2,1,0:T(8,128)(2,1)S(1)} %shard_map.140.refs_1_), channel_id=1, source_target_pairs={{0,6},{1,7},{2,4},{3,5},{4,2},{5,3},{6,0},{7,1},{8,14},{9,15},{10,... | collective-permute-start | bytes 786440 | tf_op jit(solution)/shard_map/ppermute | solution.py:121
  23.3 13.6 %collective-permute-start.11 = (bf16[1,16,6144]{2,1,0:T(8,128)(2,1)S(1)}, bf16[1,16,6144]{2,1,0:T(8,128)(2,1)S(1)}, u32[]{:S(2)}, u32[]{:S(2)}) collective-permute-start(bf16[1,16,6144]{2,1,0:T(8,128)(2,1)S(1)} %get-tuple-element.46.refs_0_), channel_id=1, source_target_pairs={{0,2},{1,5},{2,0},{3,7},{4,6},{5,1},{6,4},{7,3},{8,10},{9,13},{10,... | collective-permute-start | bytes 589832 | tf_op jit(solution)/shard_map/ppermute | solution.py:121
  28.7 9.3 %collective-permute-start.10 = (bf16[2,16,4096]{2,1,0:T(8,128)(2,1)S(1)}, bf16[2,16,4096]{2,1,0:T(8,128)(2,1)S(1)}, u32[]{:S(2)}, u32[]{:S(2)}) collective-permute-start(bf16[2,16,4096]{2,1,0:T(8,128)(2,1)S(1)} %shard_map.139.refs_2_.refs_0_), channel_id=1, source_target_pairs={{0,8},{1,9},{2,10},{3,11},{4,12},{5,13},{6,14},{7,15},{8,0},{9,1},... | collective-permute-start | bytes 786440 | tf_op jit(solution)/shard_map/ppermute | solution.py:121
  29.4 8.0 %collective-permute-start.13 = (bf16[1,16,6144]{2,1,0:T(8,128)(2,1)S(1)}, bf16[1,16,6144]{2,1,0:T(8,128)(2,1)S(1)}, u32[]{:S(2)}, u32[]{:S(2)}) collective-permute-start(bf16[1,16,6144]{2,1,0:T(8,128)(2,1)S(1)} %collective-permute-done.12.refs_2_), channel_id=1, source_target_pairs={{0,4},{1,3},{2,6},{3,1},{4,0},{5,7},{6,2},{7,5},{8,12},{9,11},{10,... | collective-permute-start | bytes 589832 | tf_op jit(solution)/shard_map/ppermute | solution.py:121
  36.8 2.0 %collective-permute-start.6 = (bf16[4,16,2048]{2,1,0:T(8,128)(2,1)S(1)}, bf16[4,16,2048]{2,1,0:T(8,128)(2,1)S(1)}, u32[]{:S(2)}, u32[]{:S(2)}) collective-permute-start(bf16[4,16,2048]{2,1,0:T(8,128)(2,1)S(1)} %shard_map.140.refs_1_), channel_id=1, source_target_pairs={{0,1},{1,0},{2,3},{3,2},{4,5},{5,4},{6,7},{7,6},{8,9},{9,8},{10,11... | collective-permute-start | bytes 786440 | tf_op jit(solution)/shard_map/ppermute | solution.py:121
  36.8 3.5 %collective-permute-start.7 = (bf16[4,16,2048]{2,1,0:T(8,128)(2,1)S(1)}, bf16[4,16,2048]{2,1,0:T(8,128)(2,1)S(1)}, u32[]{:S(2)}, u32[]{:S(2)}) collective-permute-start(bf16[4,16,2048]{2,1,0:T(8,128)(2,1)S(1)} %collective-permute-done.3.refs_2_), channel_id=1, source_target_pairs={{0,1},{1,0},{2,3},{3,2},{4,5},{5,4},{6,7},{7,6},{8,9},{9,8},{10,11... | collective-permute-start | bytes 786440 | tf_op jit(solution)/shard_map/ppermute | solution.py:121
  37.4 4.5 %collective-permute-start.8 = (bf16[4,16,2048]{2,1,0:T(8,128)(2,1)S(1)}, bf16[4,16,2048]{2,1,0:T(8,128)(2,1)S(1)}, u32[]{:S(2)}, u32[]{:S(2)}) collective-permute-start(bf16[4,16,2048]{2,1,0:T(8,128)(2,1)S(1)} %collective-permute-done.4.refs_3_), channel_id=1, source_target_pairs={{0,1},{1,0},{2,3},{3,2},{4,5},{5,4},{6,7},{7,6},{8,9},{9,8},{10,11... | collective-permute-start | bytes 786440 | tf_op jit(solution)/shard_map/ppermute | solution.py:121
  37.4 4.4 %collective-permute-start.9 = (bf16[4,16,2048]{2,1,0:T(8,128)(2,1)S(1)}, bf16[4,16,2048]{2,1,0:T(8,128)(2,1)S(1)}, u32[]{:S(2)}, u32[]{:S(2)}) collective-permute-start(bf16[4,16,2048]{2,1,0:T(8,128)(2,1)S(1)} %collective-permute-done.5.refs_4_), channel_id=1, source_target_pairs={{0,1},{1,0},{2,3},{3,2},{4,5},{5,4},{6,7},{7,6},{8,9},{9,8},{10,11... | collective-permute-start | bytes 786440 | tf_op jit(solution)/shard_map/ppermute | solution.py:121
  38.0 3.8 %copy-start.4 = (bf16[640,256]{1,0:T(8,128)(2,1)S(1)}, bf16[640,256]{1,0:T(8,128)(2,1)}, u32[]{:S(2)}) copy-start(bf16[640,256]{1,0:T(8,128)(2,1)} %constant.9.clone.refs_11_.refs_12_) | copy-start | bytes 983044
  38.0 19.6 %collective-permute-start.18 = (bf16[4,16,6144]{2,1,0:T(8,128)(2,1)S(1)}, bf16[4,16,6144]{2,1,0:T(8,128)(2,1)S(1)}, u32[]{:S(2)}, u32[]{:S(2)}) collective-permute-start(bf16[4,16,6144]{2,1,0:T(8,128)(2,1)S(1)} %shard_map.141.refs_2_.refs_0_), channel_id=1, source_target_pairs={{0,8},{1,9},{2,10},{3,11},{4,12},{5,13},{6,14},{7,15},{8,0},{9,1},... | collective-permute-start | bytes 2359304 | tf_op jit(solution)/shard_map/ppermute | solution.py:121
  38.8 14.6 %collective-permute-start.14 = (bf16[4,16,4096]{2,1,0:T(8,128)(2,1)S(1)}, bf16[4,16,4096]{2,1,0:T(8,128)(2,1)S(1)}, u32[]{:S(2)}, u32[]{:S(2)}) collective-permute-start(bf16[4,16,4096]{2,1,0:T(8,128)(2,1)S(1)} %shard_map.142.refs_12_.refs_1_), channel_id=1, source_target_pairs={{0,2},{1,5},{2,0},{3,7},{4,6},{5,1},{6,4},{7,3},{8,10},{9,13},{10,... | collective-permute-start | bytes 1572872 | tf_op jit(solution)/shard_map/ppermute | solution.py:121
  40.3 13.1 %collective-permute-start.15 = (bf16[4,16,4096]{2,1,0:T(8,128)(2,1)S(1)}, bf16[4,16,4096]{2,1,0:T(8,128)(2,1)S(1)}, u32[]{:S(2)}, u32[]{:S(2)}) collective-permute-start(bf16[4,16,4096]{2,1,0:T(8,128)(2,1)S(1)} %shard_map.142.refs_12_.refs_1_), channel_id=1, source_target_pairs={{0,4},{1,3},{2,6},{3,1},{4,0},{5,7},{6,2},{7,5},{8,12},{9,11},{10,... | collective-permute-start | bytes 1572872 | tf_op jit(solution)/shard_map/ppermute | solution.py:121
  41.8 22.9 %collective-permute-start.19 = (bf16[4,16,4096]{2,1,0:T(8,128)(2,1)S(1)}, bf16[4,16,4096]{2,1,0:T(8,128)(2,1)S(1)}, u32[]{:S(2)}, u32[]{:S(2)}) collective-permute-start(bf16[4,16,4096]{2,1,0:T(8,128)(2,1)S(1)} %shard_map.142.refs_12_.refs_1_), channel_id=1, source_target_pairs={{0,1},{1,0},{2,3},{3,2},{4,5},{5,4},{6,7},{7,6},{8,9},{9,8},{10,11... | collective-permute-start | bytes 1572872 | tf_op jit(solution)/shard_map/ppermute | solution.py:121
  53.4 11.3 %collective-permute-start.16 = (bf16[2,16,4096]{2,1,0:T(8,128)(2,1)S(1)}, bf16[2,16,4096]{2,1,0:T(8,128)(2,1)S(1)}, u32[]{:S(2)}, u32[]{:S(2)}) collective-permute-start(bf16[2,16,4096]{2,1,0:T(8,128)(2,1)S(1)} %slice.39), channel_id=1, source_target_pairs={{0,4},{1,3},{2,6},{3,1},{4,0},{5,7},{6,2},{7,5},{8,12},{9,11},{10,... | collective-permute-start | bytes 786440 | tf_op jit(solution)/shard_map/ppermute | solution.py:121
  54.6 10.1 %collective-permute-start.17 = (bf16[2,16,4096]{2,1,0:T(8,128)(2,1)S(1)}, bf16[2,16,4096]{2,1,0:T(8,128)(2,1)S(1)}, u32[]{:S(2)}, u32[]{:S(2)}) collective-permute-start(bf16[2,16,4096]{2,1,0:T(8,128)(2,1)S(1)} %slice.40), channel_id=1, source_target_pairs={{0,2},{1,5},{2,0},{3,7},{4,6},{5,1},{6,4},{7,3},{8,10},{9,13},{10,... | collective-permute-start | bytes 786440 | tf_op jit(solution)/shard_map/ppermute | solution.py:121
  56.1 8.6 %collective-permute-start.20 = (bf16[4,16,4096]{2,1,0:T(8,128)(2,1)S(1)}, bf16[4,16,4096]{2,1,0:T(8,128)(2,1)S(1)}, u32[]{:S(2)}, u32[]{:S(2)}) collective-permute-start(bf16[4,16,4096]{2,1,0:T(8,128)(2,1)S(1)} %collective-permute-done.14.refs_2_), channel_id=1, source_target_pairs={{0,1},{1,0},{2,3},{3,2},{4,5},{5,4},{6,7},{7,6},{8,9},{9,8},{10,11... | collective-permute-start | bytes 1572872 | tf_op jit(solution)/shard_map/ppermute | solution.py:121
  57.6 7.1 %collective-permute-start.21 = (bf16[4,16,4096]{2,1,0:T(8,128)(2,1)S(1)}, bf16[4,16,4096]{2,1,0:T(8,128)(2,1)S(1)}, u32[]{:S(2)}, u32[]{:S(2)}) collective-permute-start(bf16[4,16,4096]{2,1,0:T(8,128)(2,1)S(1)} %collective-permute-done.15.refs_3_), channel_id=1, source_target_pairs={{0,1},{1,0},{2,3},{3,2},{4,5},{5,4},{6,7},{7,6},{8,9},{9,8},{10,11... | collective-permute-start | bytes 1572872 | tf_op jit(solution)/shard_map/ppermute | solution.py:121
  64.8 2.9 %collective-permute-start.22 = (bf16[4,16,4096]{2,1,0:T(8,128)(2,1)S(1)}, bf16[4,16,4096]{2,1,0:T(8,128)(2,1)S(1)}, u32[]{:S(2)}, u32[]{:S(2)}) collective-permute-start(bf16[4,16,4096]{2,1,0:T(8,128)(2,1)S(1)} %shard_map.146.refs_4_), channel_id=1, source_target_pairs={{0,1},{1,0},{2,3},{3,2},{4,5},{5,4},{6,7},{7,6},{8,9},{9,8},{10,11... | collective-permute-start | bytes 1572872 | tf_op jit(solution)/shard_map/ppermute | solution.py:121
  65.4 17.4 %collective-permute-start.26 = (bf16[4,16,2048]{2,1,0:T(8,128)(2,1)S(1)}, bf16[4,16,2048]{2,1,0:T(8,128)(2,1)S(1)}, u32[]{:S(2)}, u32[]{:S(2)}) collective-permute-start(bf16[4,16,2048]{2,1,0:T(8,128)(2,1)S(1)} %get-tuple-element.63.refs_13_.refs_2_), channel_id=1, source_target_pairs={{0,4},{1,3},{2,6},{3,1},{4,0},{5,7},{6,2},{7,5},{8,12},{9,11},{10,... | collective-permute-start | bytes 786440 | tf_op jit(solution)/shard_map/ppermute | solution.py:121
  66.2 16.5 %collective-permute-start.27 = (bf16[4,16,2048]{2,1,0:T(8,128)(2,1)S(1)}, bf16[4,16,2048]{2,1,0:T(8,128)(2,1)S(1)}, u32[]{:S(2)}, u32[]{:S(2)}) collective-permute-start(bf16[4,16,2048]{2,1,0:T(8,128)(2,1)S(1)} %get-tuple-element.64.refs_3_), channel_id=1, source_target_pairs={{0,2},{1,5},{2,0},{3,7},{4,6},{5,1},{6,4},{7,3},{8,10},{9,13},{10,... | collective-permute-start | bytes 786440 | tf_op jit(solution)/shard_map/ppermute | solution.py:121
  72.6 1.3 %collective-permute-start.23 = (bf16[2,36,512]{2,1,0:T(8,128)(2,1)S(1)}, bf16[2,36,512]{2,1,0:T(8,128)(2,1)S(1)}, u32[]{:S(2)}, u32[]{:S(2)}) collective-permute-start(bf16[2,36,512]{2,1,0:T(8,128)(2,1)S(1)} %get-tuple-element.55), channel_id=1, source_target_pairs={{1,0},{0,1},{3,2},{2,3},{5,4},{4,5},{7,6},{6,7},{9,8},{8,9},{11,10... | collective-permute-start | bytes 221192 | tf_op jit(solution)/shard_map/ppermute | solution.py:385
  73.9 15.5 %copy-start.5 = (f32[144,256]{1,0:T(8,128)S(1)}, f32[144,256]{1,0:T(8,128)}, u32[]{:S(2)}) copy-start(f32[144,256]{1,0:T(8,128)} %constant.10.clone.refs_13_) | copy-start | bytes 442372
  73.9 10.7 %collective-permute-start.24 = (bf16[8,36,512]{2,1,0:T(8,128)(2,1)S(1)}, bf16[8,36,512]{2,1,0:T(8,128)(2,1)S(1)}, u32[]{:S(2)}, u32[]{:S(2)}) collective-permute-start(bf16[8,36,512]{2,1,0:T(8,128)(2,1)S(1)} %shard_map.149), channel_id=1, source_target_pairs={{2,0},{3,1},{4,2},{5,3},{6,4},{7,5},{8,6},{9,7},{10,8},{11,9},{12,... | collective-permute-start | bytes 884744 | tf_op jit(solution)/shard_map/ppermute | solution.py:385
  77.4 8.8 %collective-permute-start.28 = (bf16[4,16,2048]{2,1,0:T(8,128)(2,1)S(1)}, bf16[4,16,2048]{2,1,0:T(8,128)(2,1)S(1)}, u32[]{:S(2)}, u32[]{:S(2)}) collective-permute-start(bf16[4,16,2048]{2,1,0:T(8,128)(2,1)S(1)} %get-tuple-element.63.refs_13_.refs_2_), channel_id=1, source_target_pairs={{0,1},{1,0},{2,3},{3,2},{4,5},{5,4},{6,7},{7,6},{8,9},{9,8},{10,11... | collective-permute-start | bytes 786440 | tf_op jit(solution)/shard_map/ppermute | solution.py:121
  77.4 9.2 %collective-permute-start.29 = (bf16[4,16,2048]{2,1,0:T(8,128)(2,1)S(1)}, bf16[4,16,2048]{2,1,0:T(8,128)(2,1)S(1)}, u32[]{:S(2)}, u32[]{:S(2)}) collective-permute-start(bf16[4,16,2048]{2,1,0:T(8,128)(2,1)S(1)} %get-tuple-element.64.refs_3_), channel_id=1, source_target_pairs={{0,1},{1,0},{2,3},{3,2},{4,5},{5,4},{6,7},{7,6},{8,9},{9,8},{10,11... | collective-permute-start | bytes 786440 | tf_op jit(solution)/shard_map/ppermute | solution.py:121
  82.7 4.3 %collective-permute-start.30 = (bf16[4,16,2048]{2,1,0:T(8,128)(2,1)S(1)}, bf16[4,16,2048]{2,1,0:T(8,128)(2,1)S(1)}, u32[]{:S(2)}, u32[]{:S(2)}) collective-permute-start(bf16[4,16,2048]{2,1,0:T(8,128)(2,1)S(1)} %collective-permute-done.26.refs_4_), channel_id=1, source_target_pairs={{0,1},{1,0},{2,3},{3,2},{4,5},{5,4},{6,7},{7,6},{8,9},{9,8},{10,11... | collective-permute-start | bytes 786440 | tf_op jit(solution)/shard_map/ppermute | solution.py:121
  82.8 6.6 %collective-permute-start.31 = (bf16[4,16,2048]{2,1,0:T(8,128)(2,1)S(1)}, bf16[4,16,2048]{2,1,0:T(8,128)(2,1)S(1)}, u32[]{:S(2)}, u32[]{:S(2)}) collective-permute-start(bf16[4,16,2048]{2,1,0:T(8,128)(2,1)S(1)} %collective-permute-done.27.refs_5_), channel_id=1, source_target_pairs={{0,1},{1,0},{2,3},{3,2},{4,5},{5,4},{6,7},{7,6},{8,9},{9,8},{10,11... | collective-permute-start | bytes 786440 | tf_op jit(solution)/shard_map/ppermute | solution.py:121
  84.7 1.3 %collective-permute-start.25 = (bf16[2,36,512]{2,1,0:T(8,128)(2,1)S(1)}, bf16[2,36,512]{2,1,0:T(8,128)(2,1)S(1)}, u32[]{:S(2)}, u32[]{:S(2)}) collective-permute-start(bf16[2,36,512]{2,1,0:T(8,128)(2,1)S(1)} %get-tuple-element.60), channel_id=1, source_target_pairs={{1,0},{0,1},{3,2},{2,3},{5,4},{4,5},{7,6},{6,7},{9,8},{8,9},{11,10... | collective-permute-start | bytes 221192 | tf_op jit(solution)/shard_map/ppermute | solution.py:385
  85.9 16.0 %collective-permute-start.34 = (bf16[4,16,4096]{2,1,0:T(8,128)(2,1)S(1)}, bf16[4,16,4096]{2,1,0:T(8,128)(2,1)S(1)}, u32[]{:S(2)}, u32[]{:S(2)}) collective-permute-start(bf16[4,16,4096]{2,1,0:T(8,128)(2,1)S(1)} %get-tuple-element.69.refs_1_), channel_id=1, source_target_pairs={{0,1},{1,0},{2,3},{3,2},{4,5},{5,4},{6,7},{7,6},{8,9},{9,8},{10,11... | collective-permute-start | bytes 1572872 | tf_op jit(solution)/shard_map/ppermute | solution.py:121
  86.2 15.7 %collective-permute-start.35 = (bf16[4,16,4096]{2,1,0:T(8,128)(2,1)S(1)}, bf16[4,16,4096]{2,1,0:T(8,128)(2,1)S(1)}, u32[]{:S(2)}, u32[]{:S(2)}) collective-permute-start(bf16[4,16,4096]{2,1,0:T(8,128)(2,1)S(1)} %get-tuple-element.70.refs_2_), channel_id=1, source_target_pairs={{0,1},{1,0},{2,3},{3,2},{4,5},{5,4},{6,7},{7,6},{8,9},{9,8},{10,11... | collective-permute-start | bytes 1572872 | tf_op jit(solution)/shard_map/ppermute | solution.py:121
  86.6 14.8 %collective-permute-start.32 = (bf16[4,16,4096]{2,1,0:T(8,128)(2,1)S(1)}, bf16[4,16,4096]{2,1,0:T(8,128)(2,1)S(1)}, u32[]{:S(2)}, u32[]{:S(2)}) collective-permute-start(bf16[4,16,4096]{2,1,0:T(8,128)(2,1)S(1)} %get-tuple-element.69.refs_1_), channel_id=1, source_target_pairs={{0,4},{1,3},{2,6},{3,1},{4,0},{5,7},{6,2},{7,5},{8,12},{9,11},{10,... | collective-permute-start | bytes 1572872 | tf_op jit(solution)/shard_map/ppermute | solution.py:121
  87.0 14.3 %collective-permute-start.33 = (bf16[4,16,4096]{2,1,0:T(8,128)(2,1)S(1)}, bf16[4,16,4096]{2,1,0:T(8,128)(2,1)S(1)}, u32[]{:S(2)}, u32[]{:S(2)}) collective-permute-start(bf16[4,16,4096]{2,1,0:T(8,128)(2,1)S(1)} %get-tuple-element.70.refs_2_), channel_id=1, source_target_pairs={{0,2},{1,5},{2,0},{3,7},{4,6},{5,1},{6,4},{7,3},{8,10},{9,13},{10,... | collective-permute-start | bytes 1572872 | tf_op jit(solution)/shard_map/ppermute | solution.py:121
  101.4 1.9 %collective-permute-start.36 = (bf16[4,16,4096]{2,1,0:T(8,128)(2,1)S(1)}, bf16[4,16,4096]{2,1,0:T(8,128)(2,1)S(1)}, u32[]{:S(2)}, u32[]{:S(2)}) collective-permute-start(bf16[4,16,4096]{2,1,0:T(8,128)(2,1)S(1)} %collective-permute-done.32.refs_3_), channel_id=1, source_target_pairs={{0,1},{1,0},{2,3},{3,2},{4,5},{5,4},{6,7},{7,6},{8,9},{9,8},{10,11... | collective-permute-start | bytes 1572872 | tf_op jit(solution)/shard_map/ppermute | solution.py:121
  101.5 2.5 %collective-permute-start.37 = (bf16[4,16,4096]{2,1,0:T(8,128)(2,1)S(1)}, bf16[4,16,4096]{2,1,0:T(8,128)(2,1)S(1)}, u32[]{:S(2)}, u32[]{:S(2)}) collective-permute-start(bf16[4,16,4096]{2,1,0:T(8,128)(2,1)S(1)} %collective-permute-done.33.refs_4_), channel_id=1, source_target_pairs={{0,1},{1,0},{2,3},{3,2},{4,5},{5,4},{6,7},{7,6},{8,9},{9,8},{10,11... | collective-permute-start | bytes 1572872 | tf_op jit(solution)/shard_map/ppermute | solution.py:121
  108.9 1.3 %collective-permute-start.38 = (bf16[2,36,512]{2,1,0:T(8,128)(2,1)S(1)}, bf16[2,36,512]{2,1,0:T(8,128)(2,1)S(1)}, u32[]{:S(2)}, u32[]{:S(2)}) collective-permute-start(bf16[2,36,512]{2,1,0:T(8,128)(2,1)S(1)} %get-tuple-element.73), channel_id=1, source_target_pairs={{1,0},{0,1},{3,2},{2,3},{5,4},{4,5},{7,6},{6,7},{9,8},{8,9},{11,10... | collective-permute-start | bytes 221192 | tf_op jit(solution)/shard_map/ppermute | solution.py:385
  110.2 14.4 %collective-permute-start.39 = (bf16[8,36,512]{2,1,0:T(8,128)(2,1)S(1)}, bf16[8,36,512]{2,1,0:T(8,128)(2,1)S(1)}, u32[]{:S(2)}, u32[]{:S(2)}) collective-permute-start(bf16[8,36,512]{2,1,0:T(8,128)(2,1)S(1)} %shard_map.153), channel_id=1, source_target_pairs={{30,0},{31,1},{0,2},{1,3},{2,4},{3,5},{4,6},{5,7},{6,8},{7,9},{8,1... | collective-permute-start | bytes 884744 | tf_op jit(solution)/shard_map/ppermute | solution.py:385
  123.3 1.3 %collective-permute-start.40 = (bf16[2,36,512]{2,1,0:T(8,128)(2,1)S(1)}, bf16[2,36,512]{2,1,0:T(8,128)(2,1)S(1)}, u32[]{:S(2)}, u32[]{:S(2)}) collective-permute-start(bf16[2,36,512]{2,1,0:T(8,128)(2,1)S(1)} %get-tuple-element.80), channel_id=1, source_target_pairs={{1,0},{0,1},{3,2},{2,3},{5,4},{4,5},{7,6},{6,7},{9,8},{8,9},{11,10... | collective-permute-start | bytes 221192 | tf_op jit(solution)/shard_map/ppermute | solution.py:385

commit v15 on v14

--- a/solution.py
+++ b/solution.py
@@ -453,16 +453,14 @@
         widths = tuple(sum(weight.shape[2] for weight in pair) for pair in (weights[:2], weights[2:]))
         (pair,) = join([[own, across_z(own, 2)]], (), (windows,))
         (feed_pair,) = join([[feed_own, across_z(feed_own, 2)]])
-        (column,) = join([[pair, across_z(pair, 1)]], (), (feed_pair,))
+        last_beside = send(last_own, beside)
+        (column,) = join([[pair, across_z(pair, 1)]], (), (feed_pair, last_beside))
         received = [send(column, way) for way in (beside, across, corner)]
         sent = [tied(column, received[0])] + received
         pieces = "columns", [column] + received + [send(part, swap) for part in sent]
-        last_own = tied(last_own, pair)
-        last_other = across_z(last_own, 2)
-        (last_four,) = join(
-            [[last_own, send(last_own, beside), last_other, send(last_other, across)]]
-        )
-        (feed_column,) = join([[feed_pair, across_z(feed_pair, 1)]], (), (last_four,))
+        last_other = across_z(tied(last_own, feed_pair), 2)
+        (last_four,) = join([[last_own, last_beside, last_other, send(last_other, across)]])
+        (feed_column,) = join([[feed_pair, across_z(feed_pair, 1)]])
         received = [send(feed_column, way) for way in (beside, across)]
         last_other = across_z(last_four, 1)
         middle_0 = attention(0, [windows], (0,), pieces, (feed_column,))
@@ -500,7 +498,7 @@
         final_columns = [final_one, final_other]
         final_received = [
             send(part, way)
-            for part, way in zip(tied(final_columns, (last_received, ahead)), (across, beside))
+            for part, way in zip(tied(final_columns, last_received), (across, beside))
         ]
     lefts = strips(
         [right_0, left_1, right_1, below_0, below_1],

time: 128 us -> 135 us (1.055)
  waiting for transfers between devices: 35 us -> 46.7 us
  starting transfers between devices: 35.5 us -> 32.5 us
    ppermute x35, waiting for transfers between devices: 28.7 us -> 39.5 us  [send(): return lax.ppermute(block, ('lon', 'lat'), pairs)]
    ppermute x35, starting transfers between devices: 30.5 us -> 26.3 us  [send(): return lax.ppermute(block, ('lon', 'lat'), pairs)]
  transfers between devices with their start and end apart: 41 -> 41, of which waited for: 14 -> 15; matrix products, arithmetic and copies ran while one was open for 1% -> 1% of each run, Pallas kernels for 33% -> 32%
where the time goes in v15:
time: 135 us
  Pallas kernels  47.6 us (35%)
  waiting for transfers between devices  46.7 us (35%)
  starting transfers between devices  32.5 us (24%)
  local copies, waits for them, and re-layouts  7.64 us (6%)
    ppermute x35, waiting for transfers between devices, send(): return lax.ppermute(block, ('lon', 'lat'), pairs)  39.5 us
    pallas_call x4, Pallas kernels, attend(): pl.pallas_call(functools.partial(attend_kernel, shifted, row_windows, kin...  27.7 us
    ppermute x35, starting transfers between devices, send(): return lax.ppermute(block, ('lon', 'lat'), pairs)  26.3 us
    pallas_call x4, Pallas kernels, feed(): pl.pallas_call(functools.partial(feed_kernel, kind, len(pieces), hidden_s...  19.3 us
    ppermute x6, waiting for transfers between devices, shift_from(): return lax.ppermute(block, ('lon', 'lat'), pairs)  7.23 us
    ppermute x6, starting transfers between devices, shift_from(): return lax.ppermute(block, ('lon', 'lat'), pairs)  6.26 us
    unnamed x20, local copies, waits for them, and re-layouts  3.7 us
  transfers between devices with their start and end apart: 41, of which 15 were waited for; matrix products, arithmetic and copies ran while one was open for 1% of the time, Pallas kernels for 32%

profile of v15, /device:TPU:0, one launch (start us, length us, event | category | flops | bytes accessed | tf_op | source)
XLA Modules:
  0.0 135.0 jit_solution(1859537542300760020)
XLA Ops:
  0.0 0.9 copy-done.2
  0.9 0.8 copy-done.3
  1.8 0.9 copy-done
  2.7 0.9 copy-done.1
  3.7 4.1 %collective-permute-start.2 = (bf16[1,16,4096]{2,1,0:T(8,128)(2,1)S(1)}, bf16[1,16,4096]{2,1,0:T(8,128)(2,1)S(1)}, u32[]{:S(2)}, u32[]{:S(2)}) collective-permute-start(bf16[1,16,4096]{2,1,0:T(8,128)(2,1)S(1)} %get-tuple-element.43.refs_0_), channel_id=1, source_target_pairs={{0,16},{1,17},{2,18},{3,19},{4,20},{5,21},{6,22},{7,23},{8,24},{9,... | collective-permute-start | bytes 393224 | tf_op jit(solution)/shard_map/ppermute | solution.py:121
  7.8 0.1 collective-permute-start
  7.9 1.7 %collective-permute-start.3 = (bf16[1,16,6144]{2,1,0:T(8,128)(2,1)S(1)}, bf16[1,16,6144]{2,1,0:T(8,128)(2,1)S(1)}, u32[]{:S(2)}, u32[]{:S(2)}) collective-permute-start(bf16[1,16,6144]{2,1,0:T(8,128)(2,1)S(1)} %get-tuple-element.48.refs_0_), channel_id=1, source_target_pairs={{0,2},{1,5},{2,0},{3,7},{4,6},{5,1},{6,4},{7,3},{8,10},{9,13},{10,... | collective-permute-start | bytes 589832 | tf_op jit(solution)/shard_map/ppermute | solution.py:121
  9.6 6.6 %collective-permute-done.2.refs_1_ = bf16[1,16,4096]{2,1,0:T(8,128)(2,1)S(1)} collective-permute-done((bf16[1,16,4096]{2,1,0:T(8,128)(2,1)S(1)}, bf16[1,16,4096]{2,1,0:T(8,128)(2,1)S(1)}, u32[]{:S(2)}, u32[]{:S(2)}) %collective-permute-start.2) | collective-permute-done | bytes 131104 | tf_op jit(solution)/shard_map/ppermute | solution.py:121
  16.2 0.1 collective-permute-start.16
  16.3 0.8 copy.26
  17.2 0.5 reshape.15.refs_2_.refs_0_
  17.7 4.3 %collective-permute-start.1 = (bf16[2,16,2048]{2,1,0:T(8,128)(2,1)S(1)}, bf16[2,16,2048]{2,1,0:T(8,128)(2,1)S(1)}, u32[]{:S(2)}, u32[]{:S(2)}) collective-permute-start(bf16[2,16,2048]{2,1,0:T(8,128)(2,1)S(1)} %shard_map.137.refs_0_), channel_id=1, source_target_pairs={{0,8},{1,9},{2,10},{3,11},{4,12},{5,13},{6,14},{7,15},{8,0},{9,1},... | collective-permute-start | bytes 393224 | tf_op jit(solution)/shard_map/ppermute | solution.py:121
  22.0 5.9 %collective-permute-done.1.refs_1_ = bf16[2,16,2048]{2,1,0:T(8,128)(2,1)S(1)} collective-permute-done((bf16[2,16,2048]{2,1,0:T(8,128)(2,1)S(1)}, bf16[2,16,2048]{2,1,0:T(8,128)(2,1)S(1)}, u32[]{:S(2)}, u32[]{:S(2)}) %collective-permute-start.1) | collective-permute-done | bytes 131104 | tf_op jit(solution)/shard_map/ppermute | solution.py:121
  28.0 1.3 collective-permute-start.4
  29.3 1.5 %collective-permute-start.5 = (bf16[4,16,2048]{2,1,0:T(8,128)(2,1)S(1)}, bf16[4,16,2048]{2,1,0:T(8,128)(2,1)S(1)}, u32[]{:S(2)}, u32[]{:S(2)}) collective-permute-start(bf16[4,16,2048]{2,1,0:T(8,128)(2,1)S(1)} %shard_map.140.refs_1_), channel_id=1, source_target_pairs={{0,4},{1,3},{2,6},{3,1},{4,0},{5,7},{6,2},{7,5},{8,12},{9,11},{10,... | collective-permute-start | bytes 786440 | tf_op jit(solution)/shard_map/ppermute | solution.py:121
  30.8 0.7 collective-permute-start.6
  31.5 1.3 collective-permute-start.17
  32.8 4.4 %collective-permute-done.4.refs_2_ = bf16[4,16,2048]{2,1,0:T(8,128)(2,1)S(1)} collective-permute-done((bf16[4,16,2048]{2,1,0:T(8,128)(2,1)S(1)}, bf16[4,16,2048]{2,1,0:T(8,128)(2,1)S(1)}, u32[]{:S(2)}, u32[]{:S(2)}) %collective-permute-start.4) | collective-permute-done | bytes 262176 | tf_op jit(solution)/shard_map/ppermute | solution.py:121
  37.2 0.5 collective-permute-start.8
  37.7 5.9 %collective-permute-done.6.refs_4_ = bf16[4,16,2048]{2,1,0:T(8,128)(2,1)S(1)} collective-permute-done((bf16[4,16,2048]{2,1,0:T(8,128)(2,1)S(1)}, bf16[4,16,2048]{2,1,0:T(8,128)(2,1)S(1)}, u32[]{:S(2)}, u32[]{:S(2)}) %collective-permute-start.6) | collective-permute-done | bytes 262176 | tf_op jit(solution)/shard_map/ppermute | solution.py:121
  43.6 0.5 collective-permute-start.10
  44.1 0.1 multiply_reduce_fusion
  44.5 1.6 %collective-permute-start.12 = (bf16[4,16,4096]{2,1,0:T(8,128)(2,1)S(1)}, bf16[4,16,4096]{2,1,0:T(8,128)(2,1)S(1)}, u32[]{:S(2)}, u32[]{:S(2)}) collective-permute-start(bf16[4,16,4096]{2,1,0:T(8,128)(2,1)S(1)} %shard_map.141.refs_12_.refs_1_), channel_id=1, source_target_pairs={{0,2},{1,5},{2,0},{3,7},{4,6},{5,1},{6,4},{7,3},{8,10},{9,13},{10,... | collective-permute-start | bytes 1572872 | tf_op jit(solution)/shard_map/ppermute | solution.py:121
  46.1 0.6 collective-permute-start.13
  46.7 6.9 %shard_map.142.refs_2_.refs_12_.refs_0_ = bf16[4,144,512]{2,1,0:T(8,128)(2,1)S(1)} custom-call(bf16[8,144,512]{2,1,0:T(8,128)(2,1)S(1)} %reshape.15.refs_2_.refs_0_, bf16[4,16,2048]{2,1,0:T(8,128)(2,1)S(1)} %shard_map.140.refs_1_, bf16[4,16,2048]{2,1,0:T(8,128)(2,1)S(1)} %collective-permute-done.4.refs_2_, ...), custom_call_target="tpu_custom_call" | custom-call | flops 8000000000 | bytes 6000000 | tf_op jit(solution)/shard_map/pallas_call | solution.py:300
  53.7 5.6 %collective-permute-done.12.refs_2_ = bf16[4,16,4096]{2,1,0:T(8,128)(2,1)S(1)} collective-permute-done((bf16[4,16,4096]{2,1,0:T(8,128)(2,1)S(1)}, bf16[4,16,4096]{2,1,0:T(8,128)(2,1)S(1)}, u32[]{:S(2)}, u32[]{:S(2)}) %collective-permute-start.12) | collective-permute-done | bytes 524320 | tf_op jit(solution)/shard_map/ppermute | solution.py:121
  59.4 0.9 collective-permute-start.14
  60.3 1.2 collective-permute-start.15
  61.5 2.4 %collective-permute-done.18.refs_1_ = bf16[4,16,6144]{2,1,0:T(8,128)(2,1)S(1)} collective-permute-done((bf16[4,16,6144]{2,1,0:T(8,128)(2,1)S(1)}, bf16[4,16,6144]{2,1,0:T(8,128)(2,1)S(1)}, u32[]{:S(2)}, u32[]{:S(2)}) %collective-permute-start.18) | collective-permute-done | bytes 786464 | tf_op jit(solution)/shard_map/ppermute | solution.py:121
  63.9 0.1 shard_map.144
  64.0 6.9 %shard_map.145.refs_0_ = bf16[4,144,512]{2,1,0:T(8,128)(2,1)S(1)} custom-call(bf16[8,144,512]{2,1,0:T(8,128)(2,1)S(1)} %reshape.15.refs_2_.refs_0_, bf16[4,16,2048]{2,1,0:T(8,128)(2,1)S(1)} %shard_map.140.refs_1_, bf16[4,16,2048]{2,1,0:T(8,128)(2,1)S(1)} %collective-permute-done.4.refs_2_, bf16[4,16,2048]{2,1,0:T(8,128)(2,1)S(1)} %collective-permute-done.5.refs_3_, ...), custom_call_target="tpu_custom_call" | custom-call | flops 8000000000 | bytes 6000000 | tf_op jit(solution)/shard_map/pallas_call | solution.py:300
  71.0 0.6 collective-permute-start.22
  71.6 1.3 collective-permute-start.26
  72.8 1.1 collective-permute-start.27
  73.9 4.8 %shard_map.147 = (bf16[8,36,512]{2,1,0:T(8,128)(2,1)S(1)}, bf16[8,36,512]{2,1,0:T(8,128)(2,1)S(1)}, bf16[2,36,512]{2,1,0:T(8,128)(2,1)S(1)}) custom-call(bf16[4,144,512]{2,1,0:T(8,128)(2,1)S(1)} %shard_map.142.refs_2_.refs_12_.refs_0_, bf16[4,16,4096]{2,1,0:T(8,128)(2,1)S(1)} %shard_map.141.refs_12_.refs_1_, ...), custom_call_target="tpu_custom_call" | custom-call | flops 1000000 | bytes 100000 | tf_op jit(solution)/shard_map/pallas_call | solution.py:358
  78.8 1.3 collective-permute-done.23.refs_10_.refs_1_.refs_3_
  80.1 5.4 %collective-permute-start.24 = (bf16[8,36,512]{2,1,0:T(8,128)(2,1)S(1)}, bf16[8,36,512]{2,1,0:T(8,128)(2,1)S(1)}, u32[]{:S(2)}, u32[]{:S(2)}) collective-permute-start(bf16[8,36,512]{2,1,0:T(8,128)(2,1)S(1)} %shard_map.149), channel_id=1, source_target_pairs={{2,0},{3,1},{4,2},{5,3},{6,4},{7,5},{8,6},{9,7},{10,8},{11,9},{12,... | collective-permute-start | bytes 884744 | tf_op jit(solution)/shard_map/ppermute | solution.py:385
  85.6 0.1 collective-permute-start.28
  85.6 0.4 collective-permute-start.29
  86.1 4.8 %shard_map.148 = (bf16[8,36,512]{2,1,0:T(8,128)(2,1)S(1)}, bf16[8,36,512]{2,1,0:T(8,128)(2,1)S(1)}, bf16[2,36,512]{2,1,0:T(8,128)(2,1)S(1)}) custom-call(bf16[4,144,512]{2,1,0:T(8,128)(2,1)S(1)} %shard_map.145.refs_0_, bf16[4,16,4096]{2,1,0:T(8,128)(2,1)S(1)} %shard_map.141.refs_12_.refs_1_, bf16[4,16,4096]{2,1,0:T(8,128)(2,1)S(1)} %collective-permute-done.12.refs_2_, ...), custom_call_target="tpu_custom_call" | custom-call | flops 1000000 | bytes 100000 | tf_op jit(solution)/shard_map/pallas_call | solution.py:358
  90.9 0.1 collective-permute-start.30
  91.1 0.4 collective-permute-start.31
  91.5 1.5 %collective-permute-done.24.refs_1_ = bf16[8,36,512]{2,1,0:T(8,128)(2,1)S(1)} collective-permute-done((bf16[8,36,512]{2,1,0:T(8,128)(2,1)S(1)}, bf16[8,36,512]{2,1,0:T(8,128)(2,1)S(1)}, u32[]{:S(2)}, u32[]{:S(2)}) %collective-permute-start.24) | collective-permute-done | bytes 294944 | tf_op jit(solution)/shard_map/ppermute | solution.py:385
  93.0 1.3 collective-permute-done.25.refs_4_
  94.3 0.2 collective-permute-start.34
  94.6 0.4 collective-permute-start.35
  95.0 0.6 collective-permute-start.33
  95.6 6.9 %shard_map.151.refs_0_ = bf16[4,144,512]{2,1,0:T(8,128)(2,1)S(1)} custom-call(bf16[8,36,512]{2,1,0:T(8,128)(2,1)S(1)} %get-tuple-element.61.refs_0_, bf16[8,36,512]{2,1,0:T(8,128)(2,1)S(1)} %collective-permute-done.24.refs_1_, bf16[4,16,2048]{2,1,0:T(8,128)(2,1)S(1)} %get-tuple-element.63.refs_13_.refs_2_, ...), custom_call_target="tpu_custom_call" | custom-call | flops 8000000000 | bytes 6000000 | tf_op jit(solution)/shard_map/pallas_call | solution.py:300
  102.5 6.5 %collective-permute-done.32.refs_3_ = bf16[4,16,4096]{2,1,0:T(8,128)(2,1)S(1)} collective-permute-done((bf16[4,16,4096]{2,1,0:T(8,128)(2,1)S(1)}, bf16[4,16,4096]{2,1,0:T(8,128)(2,1)S(1)}, u32[]{:S(2)}, u32[]{:S(2)}) %collective-permute-start.32) | collective-permute-done | bytes 524320 | tf_op jit(solution)/shard_map/ppermute | solution.py:121
  109.0 0.5 collective-permute-start.37
  109.6 1.4 %collective-permute-done.36.refs_7_ = bf16[4,16,4096]{2,1,0:T(8,128)(2,1)S(1)} collective-permute-done((bf16[4,16,4096]{2,1,0:T(8,128)(2,1)S(1)}, bf16[4,16,4096]{2,1,0:T(8,128)(2,1)S(1)}, u32[]{:S(2)}, u32[]{:S(2)}) %collective-permute-start.36) | collective-permute-done | bytes 524320 | tf_op jit(solution)/shard_map/ppermute | solution.py:121
  111.0 0.7 collective-permute-done.37.refs_8_
  111.7 4.8 %shard_map.152 = (bf16[8,36,512]{2,1,0:T(8,128)(2,1)S(1)}, bf16[8,36,512]{2,1,0:T(8,128)(2,1)S(1)}, bf16[2,36,512]{2,1,0:T(8,128)(2,1)S(1)}) custom-call(bf16[4,144,512]{2,1,0:T(8,128)(2,1)S(1)} %shard_map.151.refs_0_, bf16[4,16,4096]{2,1,0:T(8,128)(2,1)S(1)} %get-tuple-element.69.refs_1_, bf16[4,16,4096]{2,1,0:T(8,128)(2,1)S(1)} %get-tuple-element.70.refs_2_, ...), custom_call_target="tpu_custom_call" | custom-call | flops 1000000 | bytes 100000 | tf_op jit(solution)/shard_map/pallas_call | solution.py:358
  116.5 0.2 collective-permute-start.38
  116.7 1.1 collective-permute-done.38.refs_0_.refs_14_.refs_5_
  117.9 0.5 collective-permute-start.39
  118.4 6.9 %shard_map.154.refs_0_ = bf16[4,144,512]{2,1,0:T(8,128)(2,1)S(1)} custom-call(bf16[8,36,512]{2,1,0:T(8,128)(2,1)S(1)} %get-tuple-element.75.refs_0_, bf16[8,36,512]{2,1,0:T(8,128)(2,1)S(1)} %get-tuple-element.76.refs_1_, bf16[4,16,2048]{2,1,0:T(8,128)(2,1)S(1)} %get-tuple-element.63.refs_13_.refs_2_, bf16[4,16,2048]{2,1,0:T(8,128)(2,1)S(1)} %get-tuple-element.64.refs_3_, ...), custom_call_target="tpu_custom_call" | custom-call | flops 8000000000 | bytes 6000000 | tf_op jit(solution)/shard_map/pallas_call | solution.py:300
  125.3 4.9 %shard_map.155 = (bf16[8,36,512]{2,1,0:T(8,128)(2,1)S(1)}, bf16[8,36,512]{2,1,0:T(8,128)(2,1)S(1)}, bf16[2,36,512]{2,1,0:T(8,128)(2,1)S(1)}) custom-call(bf16[4,144,512]{2,1,0:T(8,128)(2,1)S(1)} %shard_map.154.refs_0_, bf16[4,16,4096]{2,1,0:T(8,128)(2,1)S(1)} %get-tuple-element.69.refs_1_, bf16[4,16,4096]{2,1,0:T(8,128)(2,1)S(1)} %get-tuple-element.70.refs_2_, ...), custom_call_target="tpu_custom_call" | custom-call | flops 1000000 | bytes 100000 | tf_op jit(solution)/shard_map/pallas_call | solution.py:358
  130.2 0.1 collective-permute-start.40
  130.3 1.3 collective-permute-done.40.refs_4_
  131.5 0.8 collective-permute-done.39.refs_0_
  132.3 0.1 shard_map.156
  132.4 0.4 copy.23
  132.7 2.2 %copy.24 = bf16[4,6,8,3,2,512]{5,4,3,2,1,0:T(2,128)(2,1)} copy(bf16[4,6,8,3,2,512]{5,2,0,4,3,1:T(8,128)(2,1)S(1)} %bitcast.16) | data formatting | bytes 2359296 | tf_op jit(solution)/shard_map/transpose | solution.py:423
  (68 shorter events, 0.6 us)
Async XLA Ops:
  0.0 0.9 copy-start.2
  0.9 0.8 copy-start.3
  1.8 0.9 copy-start
  2.7 0.9 copy-start.1
  3.7 12.6 %copy-start.6 = (bf16[24,24,2,512]{3,2,1,0:T(2,128)(2,1)S(1)}, bf16[24,24,2,512]{3,2,1,0:T(2,128)(2,1)}, u32[]{:S(2)}) copy-start(bf16[24,24,2,512]{3,2,1,0:T(2,128)(2,1)} %param.14) | copy-start | bytes 3538948
  3.7 12.5 %collective-permute-start.2 = (bf16[1,16,4096]{2,1,0:T(8,128)(2,1)S(1)}, bf16[1,16,4096]{2,1,0:T(8,128)(2,1)S(1)}, u32[]{:S(2)}, u32[]{:S(2)}) collective-permute-start(bf16[1,16,4096]{2,1,0:T(8,128)(2,1)S(1)} %get-tuple-element.43.refs_0_), channel_id=1, source_target_pairs={{0,16},{1,17},{2,18},{3,19},{4,20},{5,21},{6,22},{7,23},{8,24},{9,... | collective-permute-start | bytes 393224 | tf_op jit(solution)/shard_map/ppermute | solution.py:121
  7.8 9.9 %collective-permute-start = (bf16[1,16,2048]{2,1,0:T(8,128)(2,1)S(1)}, bf16[1,16,2048]{2,1,0:T(8,128)(2,1)S(1)}, u32[]{:S(2)}, u32[]{:S(2)}) collective-permute-start(bf16[1,16,2048]{2,1,0:T(8,128)(2,1)S(1)} %shard_map.136.refs_0_.refs_6_), channel_id=1, source_target_pairs={{0,16},{1,17},{2,18},{3,19},{4,20},{5,21},{6,22},{7,23},{8,24},{9,... | collective-permute-start | bytes 196616 | tf_op jit(solution)/shard_map/ppermute | solution.py:121
  7.9 20.1 %collective-permute-start.3 = (bf16[1,16,6144]{2,1,0:T(8,128)(2,1)S(1)}, bf16[1,16,6144]{2,1,0:T(8,128)(2,1)S(1)}, u32[]{:S(2)}, u32[]{:S(2)}) collective-permute-start(bf16[1,16,6144]{2,1,0:T(8,128)(2,1)S(1)} %get-tuple-element.48.refs_0_), channel_id=1, source_target_pairs={{0,2},{1,5},{2,0},{3,7},{4,6},{5,1},{6,4},{7,3},{8,10},{9,13},{10,... | collective-permute-start | bytes 589832 | tf_op jit(solution)/shard_map/ppermute | solution.py:121
  16.2 15.3 %collective-permute-start.16 = (bf16[1,16,6144]{2,1,0:T(8,128)(2,1)S(1)}, bf16[1,16,6144]{2,1,0:T(8,128)(2,1)S(1)}, u32[]{:S(2)}, u32[]{:S(2)}) collective-permute-start(bf16[1,16,6144]{2,1,0:T(8,128)(2,1)S(1)} %get-tuple-element.48.refs_0_), channel_id=1, source_target_pairs={{0,16},{1,17},{2,18},{3,19},{4,20},{5,21},{6,22},{7,23},{8,24},{9,... | collective-permute-start | bytes 589832 | tf_op jit(solution)/shard_map/ppermute | solution.py:121
  17.6 15.2 %copy-start.8 = (f32[2,2,512]{2,1,0:T(2,128)S(1)}, f32[2,2,512]{2,1,0:T(2,128)}, u32[]{:S(2)}) copy-start(f32[2,2,512]{2,1,0:T(2,128)} %param.19) | copy-start | bytes 24580
  17.7 26.5 %copy-start.7 = (f32[16,512]{1,0:T(8,128)S(1)}, f32[16,512]{1,0:T(8,128)}, u32[]{:S(2)}) copy-start(f32[16,512]{1,0:T(8,128)} %constant.8.clone) | copy-start | bytes 98308
  17.7 26.5 %copy-start.9 = (f32[2,16]{1,0:T(2,128)S(1)}, f32[2,16]{1,0:T(2,128)}, u32[]{:S(2)}) copy-start(f32[2,16]{1,0:T(2,128)} %param.20) | copy-start | bytes 388
  17.7 10.2 %collective-permute-start.1 = (bf16[2,16,2048]{2,1,0:T(8,128)(2,1)S(1)}, bf16[2,16,2048]{2,1,0:T(8,128)(2,1)S(1)}, u32[]{:S(2)}, u32[]{:S(2)}) collective-permute-start(bf16[2,16,2048]{2,1,0:T(8,128)(2,1)S(1)} %shard_map.137.refs_0_), channel_id=1, source_target_pairs={{0,8},{1,9},{2,10},{3,11},{4,12},{5,13},{6,14},{7,15},{8,0},{9,1},... | collective-permute-start | bytes 393224 | tf_op jit(solution)/shard_map/ppermute | solution.py:121
  28.0 9.2 %collective-permute-start.4 = (bf16[4,16,2048]{2,1,0:T(8,128)(2,1)S(1)}, bf16[4,16,2048]{2,1,0:T(8,128)(2,1)S(1)}, u32[]{:S(2)}, u32[]{:S(2)}) collective-permute-start(bf16[4,16,2048]{2,1,0:T(8,128)(2,1)S(1)} %shard_map.140.refs_1_), channel_id=1, source_target_pairs={{0,2},{1,5},{2,0},{3,7},{4,6},{5,1},{6,4},{7,3},{8,10},{9,13},{10,... | collective-permute-start | bytes 786440 | tf_op jit(solution)/shard_map/ppermute | solution.py:121
  29.3 7.9 %collective-permute-start.5 = (bf16[4,16,2048]{2,1,0:T(8,128)(2,1)S(1)}, bf16[4,16,2048]{2,1,0:T(8,128)(2,1)S(1)}, u32[]{:S(2)}, u32[]{:S(2)}) collective-permute-start(bf16[4,16,2048]{2,1,0:T(8,128)(2,1)S(1)} %shard_map.140.refs_1_), channel_id=1, source_target_pairs={{0,4},{1,3},{2,6},{3,1},{4,0},{5,7},{6,2},{7,5},{8,12},{9,11},{10,... | collective-permute-start | bytes 786440 | tf_op jit(solution)/shard_map/ppermute | solution.py:121
  30.8 12.8 %collective-permute-start.6 = (bf16[4,16,2048]{2,1,0:T(8,128)(2,1)S(1)}, bf16[4,16,2048]{2,1,0:T(8,128)(2,1)S(1)}, u32[]{:S(2)}, u32[]{:S(2)}) collective-permute-start(bf16[4,16,2048]{2,1,0:T(8,128)(2,1)S(1)} %shard_map.140.refs_1_), channel_id=1, source_target_pairs={{0,6},{1,7},{2,4},{3,5},{4,2},{5,3},{6,0},{7,1},{8,14},{9,15},{10,... | collective-permute-start | bytes 786440 | tf_op jit(solution)/shard_map/ppermute | solution.py:121
  31.5 12.8 %collective-permute-start.11 = (bf16[2,16,4096]{2,1,0:T(8,128)(2,1)S(1)}, bf16[2,16,4096]{2,1,0:T(8,128)(2,1)S(1)}, u32[]{:S(2)}, u32[]{:S(2)}) collective-permute-start(bf16[2,16,4096]{2,1,0:T(8,128)(2,1)S(1)} %shard_map.139.refs_2_.refs_0_), channel_id=1, source_target_pairs={{0,8},{1,9},{2,10},{3,11},{4,12},{5,13},{6,14},{7,15},{8,0},{9,1},... | collective-permute-start | bytes 786440 | tf_op jit(solution)/shard_map/ppermute | solution.py:121
  31.5 12.1 %collective-permute-start.17 = (bf16[1,16,6144]{2,1,0:T(8,128)(2,1)S(1)}, bf16[1,16,6144]{2,1,0:T(8,128)(2,1)S(1)}, u32[]{:S(2)}, u32[]{:S(2)}) collective-permute-start(bf16[1,16,6144]{2,1,0:T(8,128)(2,1)S(1)} %collective-permute-done.16.refs_2_), channel_id=1, source_target_pairs={{0,4},{1,3},{2,6},{3,1},{4,0},{5,7},{6,2},{7,5},{8,12},{9,11},{10,... | collective-permute-start | bytes 589832 | tf_op jit(solution)/shard_map/ppermute | solution.py:121
  37.2 7.3 %collective-permute-start.7 = (bf16[4,16,2048]{2,1,0:T(8,128)(2,1)S(1)}, bf16[4,16,2048]{2,1,0:T(8,128)(2,1)S(1)}, u32[]{:S(2)}, u32[]{:S(2)}) collective-permute-start(bf16[4,16,2048]{2,1,0:T(8,128)(2,1)S(1)} %shard_map.140.refs_1_), channel_id=1, source_target_pairs={{0,1},{1,0},{2,3},{3,2},{4,5},{5,4},{6,7},{7,6},{8,9},{9,8},{10,11... | collective-permute-start | bytes 786440 | tf_op jit(solution)/shard_map/ppermute | solution.py:121
  37.2 8.9 %collective-permute-start.8 = (bf16[4,16,2048]{2,1,0:T(8,128)(2,1)S(1)}, bf16[4,16,2048]{2,1,0:T(8,128)(2,1)S(1)}, u32[]{:S(2)}, u32[]{:S(2)}) collective-permute-start(bf16[4,16,2048]{2,1,0:T(8,128)(2,1)S(1)} %collective-permute-done.4.refs_2_), channel_id=1, source_target_pairs={{0,1},{1,0},{2,3},{3,2},{4,5},{5,4},{6,7},{7,6},{8,9},{9,8},{10,11... | collective-permute-start | bytes 786440 | tf_op jit(solution)/shard_map/ppermute | solution.py:121
  43.6 3.1 %collective-permute-start.9 = (bf16[4,16,2048]{2,1,0:T(8,128)(2,1)S(1)}, bf16[4,16,2048]{2,1,0:T(8,128)(2,1)S(1)}, u32[]{:S(2)}, u32[]{:S(2)}) collective-permute-start(bf16[4,16,2048]{2,1,0:T(8,128)(2,1)S(1)} %collective-permute-done.5.refs_3_), channel_id=1, source_target_pairs={{0,1},{1,0},{2,3},{3,2},{4,5},{5,4},{6,7},{7,6},{8,9},{9,8},{10,11... | collective-permute-start | bytes 786440 | tf_op jit(solution)/shard_map/ppermute | solution.py:121
  43.6 3.1 %collective-permute-start.10 = (bf16[4,16,2048]{2,1,0:T(8,128)(2,1)S(1)}, bf16[4,16,2048]{2,1,0:T(8,128)(2,1)S(1)}, u32[]{:S(2)}, u32[]{:S(2)}) collective-permute-start(bf16[4,16,2048]{2,1,0:T(8,128)(2,1)S(1)} %collective-permute-done.6.refs_4_), channel_id=1, source_target_pairs={{0,1},{1,0},{2,3},{3,2},{4,5},{5,4},{6,7},{7,6},{8,9},{9,8},{10,11... | collective-permute-start | bytes 786440 | tf_op jit(solution)/shard_map/ppermute | solution.py:121
  44.2 2.5 %copy-start.4 = (bf16[640,256]{1,0:T(8,128)(2,1)S(1)}, bf16[640,256]{1,0:T(8,128)(2,1)}, u32[]{:S(2)}) copy-start(bf16[640,256]{1,0:T(8,128)(2,1)} %constant.9.clone.refs_11_.refs_12_) | copy-start | bytes 983044
  44.3 19.5 %collective-permute-start.18 = (bf16[4,16,6144]{2,1,0:T(8,128)(2,1)S(1)}, bf16[4,16,6144]{2,1,0:T(8,128)(2,1)S(1)}, u32[]{:S(2)}, u32[]{:S(2)}) collective-permute-start(bf16[4,16,6144]{2,1,0:T(8,128)(2,1)S(1)} %shard_map.143.refs_0_), channel_id=1, source_target_pairs={{0,8},{1,9},{2,10},{3,11},{4,12},{5,13},{6,14},{7,15},{8,0},{9,1},... | collective-permute-start | bytes 2359304 | tf_op jit(solution)/shard_map/ppermute | solution.py:121
  44.5 14.8 %collective-permute-start.12 = (bf16[4,16,4096]{2,1,0:T(8,128)(2,1)S(1)}, bf16[4,16,4096]{2,1,0:T(8,128)(2,1)S(1)}, u32[]{:S(2)}, u32[]{:S(2)}) collective-permute-start(bf16[4,16,4096]{2,1,0:T(8,128)(2,1)S(1)} %shard_map.141.refs_12_.refs_1_), channel_id=1, source_target_pairs={{0,2},{1,5},{2,0},{3,7},{4,6},{5,1},{6,4},{7,3},{8,10},{9,13},{10,... | collective-permute-start | bytes 1572872 | tf_op jit(solution)/shard_map/ppermute | solution.py:121
  46.1 13.3 %collective-permute-start.13 = (bf16[4,16,4096]{2,1,0:T(8,128)(2,1)S(1)}, bf16[4,16,4096]{2,1,0:T(8,128)(2,1)S(1)}, u32[]{:S(2)}, u32[]{:S(2)}) collective-permute-start(bf16[4,16,4096]{2,1,0:T(8,128)(2,1)S(1)} %shard_map.141.refs_12_.refs_1_), channel_id=1, source_target_pairs={{0,4},{1,3},{2,6},{3,1},{4,0},{5,7},{6,2},{7,5},{8,12},{9,11},{10,... | collective-permute-start | bytes 1572872 | tf_op jit(solution)/shard_map/ppermute | solution.py:121
  46.7 24.2 %collective-permute-start.19 = (bf16[4,16,4096]{2,1,0:T(8,128)(2,1)S(1)}, bf16[4,16,4096]{2,1,0:T(8,128)(2,1)S(1)}, u32[]{:S(2)}, u32[]{:S(2)}) collective-permute-start(bf16[4,16,4096]{2,1,0:T(8,128)(2,1)S(1)} %shard_map.141.refs_12_.refs_1_), channel_id=1, source_target_pairs={{0,1},{1,0},{2,3},{3,2},{4,5},{5,4},{6,7},{7,6},{8,9},{9,8},{10,11... | collective-permute-start | bytes 1572872 | tf_op jit(solution)/shard_map/ppermute | solution.py:121
  59.4 11.6 %collective-permute-start.14 = (bf16[2,16,4096]{2,1,0:T(8,128)(2,1)S(1)}, bf16[2,16,4096]{2,1,0:T(8,128)(2,1)S(1)}, u32[]{:S(2)}, u32[]{:S(2)}) collective-permute-start(bf16[2,16,4096]{2,1,0:T(8,128)(2,1)S(1)} %slice.39), channel_id=1, source_target_pairs={{0,4},{1,3},{2,6},{3,1},{4,0},{5,7},{6,2},{7,5},{8,12},{9,11},{10,... | collective-permute-start | bytes 786440 | tf_op jit(solution)/shard_map/ppermute | solution.py:121
  60.3 10.7 %collective-permute-start.15 = (bf16[2,16,4096]{2,1,0:T(8,128)(2,1)S(1)}, bf16[2,16,4096]{2,1,0:T(8,128)(2,1)S(1)}, u32[]{:S(2)}, u32[]{:S(2)}) collective-permute-start(bf16[2,16,4096]{2,1,0:T(8,128)(2,1)S(1)} %slice.40), channel_id=1, source_target_pairs={{0,2},{1,5},{2,0},{3,7},{4,6},{5,1},{6,4},{7,3},{8,10},{9,13},{10,... | collective-permute-start | bytes 786440 | tf_op jit(solution)/shard_map/ppermute | solution.py:121
  61.5 9.5 %collective-permute-start.20 = (bf16[4,16,4096]{2,1,0:T(8,128)(2,1)S(1)}, bf16[4,16,4096]{2,1,0:T(8,128)(2,1)S(1)}, u32[]{:S(2)}, u32[]{:S(2)}) collective-permute-start(bf16[4,16,4096]{2,1,0:T(8,128)(2,1)S(1)} %collective-permute-done.12.refs_2_), channel_id=1, source_target_pairs={{0,1},{1,0},{2,3},{3,2},{4,5},{5,4},{6,7},{7,6},{8,9},{9,8},{10,11... | collective-permute-start | bytes 1572872 | tf_op jit(solution)/shard_map/ppermute | solution.py:121
  63.8 7.1 %collective-permute-start.21 = (bf16[4,16,4096]{2,1,0:T(8,128)(2,1)S(1)}, bf16[4,16,4096]{2,1,0:T(8,128)(2,1)S(1)}, u32[]{:S(2)}, u32[]{:S(2)}) collective-permute-start(bf16[4,16,4096]{2,1,0:T(8,128)(2,1)S(1)} %collective-permute-done.13.refs_3_), channel_id=1, source_target_pairs={{0,1},{1,0},{2,3},{3,2},{4,5},{5,4},{6,7},{7,6},{8,9},{9,8},{10,11... | collective-permute-start | bytes 1572872 | tf_op jit(solution)/shard_map/ppermute | solution.py:121
  71.0 2.9 %collective-permute-start.22 = (bf16[4,16,4096]{2,1,0:T(8,128)(2,1)S(1)}, bf16[4,16,4096]{2,1,0:T(8,128)(2,1)S(1)}, u32[]{:S(2)}, u32[]{:S(2)}) collective-permute-start(bf16[4,16,4096]{2,1,0:T(8,128)(2,1)S(1)} %shard_map.146.refs_4_), channel_id=1, source_target_pairs={{0,1},{1,0},{2,3},{3,2},{4,5},{5,4},{6,7},{7,6},{8,9},{9,8},{10,11... | collective-permute-start | bytes 1572872 | tf_op jit(solution)/shard_map/ppermute | solution.py:121
  71.6 19.3 %collective-permute-start.26 = (bf16[4,16,2048]{2,1,0:T(8,128)(2,1)S(1)}, bf16[4,16,2048]{2,1,0:T(8,128)(2,1)S(1)}, u32[]{:S(2)}, u32[]{:S(2)}) collective-permute-start(bf16[4,16,2048]{2,1,0:T(8,128)(2,1)S(1)} %get-tuple-element.63.refs_13_.refs_2_), channel_id=1, source_target_pairs={{0,4},{1,3},{2,6},{3,1},{4,0},{5,7},{6,2},{7,5},{8,12},{9,11},{10,... | collective-permute-start | bytes 786440 | tf_op jit(solution)/shard_map/ppermute | solution.py:121
  72.8 18.1 %collective-permute-start.27 = (bf16[4,16,2048]{2,1,0:T(8,128)(2,1)S(1)}, bf16[4,16,2048]{2,1,0:T(8,128)(2,1)S(1)}, u32[]{:S(2)}, u32[]{:S(2)}) collective-permute-start(bf16[4,16,2048]{2,1,0:T(8,128)(2,1)S(1)} %get-tuple-element.64.refs_3_), channel_id=1, source_target_pairs={{0,2},{1,5},{2,0},{3,7},{4,6},{5,1},{6,4},{7,3},{8,10},{9,13},{10,... | collective-permute-start | bytes 786440 | tf_op jit(solution)/shard_map/ppermute | solution.py:121
  78.7 1.3 collective-permute-start.23
  80.1 15.5 %copy-start.5 = (f32[144,256]{1,0:T(8,128)S(1)}, f32[144,256]{1,0:T(8,128)}, u32[]{:S(2)}) copy-start(f32[144,256]{1,0:T(8,128)} %constant.10.clone.refs_13_) | copy-start | bytes 442372
  80.1 12.9 %collective-permute-start.24 = (bf16[8,36,512]{2,1,0:T(8,128)(2,1)S(1)}, bf16[8,36,512]{2,1,0:T(8,128)(2,1)S(1)}, u32[]{:S(2)}, u32[]{:S(2)}) collective-permute-start(bf16[8,36,512]{2,1,0:T(8,128)(2,1)S(1)} %shard_map.149), channel_id=1, source_target_pairs={{2,0},{3,1},{4,2},{5,3},{6,4},{7,5},{8,6},{9,7},{10,8},{11,9},{12,... | collective-permute-start | bytes 884744 | tf_op jit(solution)/shard_map/ppermute | solution.py:385
  85.6 9.0 %collective-permute-start.28 = (bf16[4,16,2048]{2,1,0:T(8,128)(2,1)S(1)}, bf16[4,16,2048]{2,1,0:T(8,128)(2,1)S(1)}, u32[]{:S(2)}, u32[]{:S(2)}) collective-permute-start(bf16[4,16,2048]{2,1,0:T(8,128)(2,1)S(1)} %get-tuple-element.63.refs_13_.refs_2_), channel_id=1, source_target_pairs={{0,1},{1,0},{2,3},{3,2},{4,5},{5,4},{6,7},{7,6},{8,9},{9,8},{10,11... | collective-permute-start | bytes 786440 | tf_op jit(solution)/shard_map/ppermute | solution.py:121
  85.6 9.3 %collective-permute-start.29 = (bf16[4,16,2048]{2,1,0:T(8,128)(2,1)S(1)}, bf16[4,16,2048]{2,1,0:T(8,128)(2,1)S(1)}, u32[]{:S(2)}, u32[]{:S(2)}) collective-permute-start(bf16[4,16,2048]{2,1,0:T(8,128)(2,1)S(1)} %get-tuple-element.64.refs_3_), channel_id=1, source_target_pairs={{0,1},{1,0},{2,3},{3,2},{4,5},{5,4},{6,7},{7,6},{8,9},{9,8},{10,11... | collective-permute-start | bytes 786440 | tf_op jit(solution)/shard_map/ppermute | solution.py:121
  90.9 4.1 %collective-permute-start.30 = (bf16[4,16,2048]{2,1,0:T(8,128)(2,1)S(1)}, bf16[4,16,2048]{2,1,0:T(8,128)(2,1)S(1)}, u32[]{:S(2)}, u32[]{:S(2)}) collective-permute-start(bf16[4,16,2048]{2,1,0:T(8,128)(2,1)S(1)} %collective-permute-done.26.refs_4_), channel_id=1, source_target_pairs={{0,1},{1,0},{2,3},{3,2},{4,5},{5,4},{6,7},{7,6},{8,9},{9,8},{10,11... | collective-permute-start | bytes 786440 | tf_op jit(solution)/shard_map/ppermute | solution.py:121
  91.1 4.5 %collective-permute-start.31 = (bf16[4,16,2048]{2,1,0:T(8,128)(2,1)S(1)}, bf16[4,16,2048]{2,1,0:T(8,128)(2,1)S(1)}, u32[]{:S(2)}, u32[]{:S(2)}) collective-permute-start(bf16[4,16,2048]{2,1,0:T(8,128)(2,1)S(1)} %collective-permute-done.27.refs_5_), channel_id=1, source_target_pairs={{0,1},{1,0},{2,3},{3,2},{4,5},{5,4},{6,7},{7,6},{8,9},{9,8},{10,11... | collective-permute-start | bytes 786440 | tf_op jit(solution)/shard_map/ppermute | solution.py:121
  93.0 1.3 collective-permute-start.25
  94.3 15.2 %collective-permute-start.34 = (bf16[4,16,4096]{2,1,0:T(8,128)(2,1)S(1)}, bf16[4,16,4096]{2,1,0:T(8,128)(2,1)S(1)}, u32[]{:S(2)}, u32[]{:S(2)}) collective-permute-start(bf16[4,16,4096]{2,1,0:T(8,128)(2,1)S(1)} %get-tuple-element.69.refs_1_), channel_id=1, source_target_pairs={{0,1},{1,0},{2,3},{3,2},{4,5},{5,4},{6,7},{7,6},{8,9},{9,8},{10,11... | collective-permute-start | bytes 1572872 | tf_op jit(solution)/shard_map/ppermute | solution.py:121
  94.6 15.0 %collective-permute-start.35 = (bf16[4,16,4096]{2,1,0:T(8,128)(2,1)S(1)}, bf16[4,16,4096]{2,1,0:T(8,128)(2,1)S(1)}, u32[]{:S(2)}, u32[]{:S(2)}) collective-permute-start(bf16[4,16,4096]{2,1,0:T(8,128)(2,1)S(1)} %get-tuple-element.70.refs_2_), channel_id=1, source_target_pairs={{0,1},{1,0},{2,3},{3,2},{4,5},{5,4},{6,7},{7,6},{8,9},{9,8},{10,11... | collective-permute-start | bytes 1572872 | tf_op jit(solution)/shard_map/ppermute | solution.py:121
  95.0 14.1 %collective-permute-start.32 = (bf16[4,16,4096]{2,1,0:T(8,128)(2,1)S(1)}, bf16[4,16,4096]{2,1,0:T(8,128)(2,1)S(1)}, u32[]{:S(2)}, u32[]{:S(2)}) collective-permute-start(bf16[4,16,4096]{2,1,0:T(8,128)(2,1)S(1)} %get-tuple-element.69.refs_1_), channel_id=1, source_target_pairs={{0,4},{1,3},{2,6},{3,1},{4,0},{5,7},{6,2},{7,5},{8,12},{9,11},{10,... | collective-permute-start | bytes 1572872 | tf_op jit(solution)/shard_map/ppermute | solution.py:121
  95.0 14.1 %collective-permute-start.33 = (bf16[4,16,4096]{2,1,0:T(8,128)(2,1)S(1)}, bf16[4,16,4096]{2,1,0:T(8,128)(2,1)S(1)}, u32[]{:S(2)}, u32[]{:S(2)}) collective-permute-start(bf16[4,16,4096]{2,1,0:T(8,128)(2,1)S(1)} %get-tuple-element.70.refs_2_), channel_id=1, source_target_pairs={{0,2},{1,5},{2,0},{3,7},{4,6},{5,1},{6,4},{7,3},{8,10},{9,13},{10,... | collective-permute-start | bytes 1572872 | tf_op jit(solution)/shard_map/ppermute | solution.py:121
  109.0 1.9 %collective-permute-start.36 = (bf16[4,16,4096]{2,1,0:T(8,128)(2,1)S(1)}, bf16[4,16,4096]{2,1,0:T(8,128)(2,1)S(1)}, u32[]{:S(2)}, u32[]{:S(2)}) collective-permute-start(bf16[4,16,4096]{2,1,0:T(8,128)(2,1)S(1)} %collective-permute-done.32.refs_3_), channel_id=1, source_target_pairs={{0,1},{1,0},{2,3},{3,2},{4,5},{5,4},{6,7},{7,6},{8,9},{9,8},{10,11... | collective-permute-start | bytes 1572872 | tf_op jit(solution)/shard_map/ppermute | solution.py:121
  109.0 2.7 %collective-permute-start.37 = (bf16[4,16,4096]{2,1,0:T(8,128)(2,1)S(1)}, bf16[4,16,4096]{2,1,0:T(8,128)(2,1)S(1)}, u32[]{:S(2)}, u32[]{:S(2)}) collective-permute-start(bf16[4,16,4096]{2,1,0:T(8,128)(2,1)S(1)} %collective-permute-done.33.refs_4_), channel_id=1, source_target_pairs={{0,1},{1,0},{2,3},{3,2},{4,5},{5,4},{6,7},{7,6},{8,9},{9,8},{10,11... | collective-permute-start | bytes 1572872 | tf_op jit(solution)/shard_map/ppermute | solution.py:121
  116.5 1.3 collective-permute-start.38
  117.9 14.4 %collective-permute-start.39 = (bf16[8,36,512]{2,1,0:T(8,128)(2,1)S(1)}, bf16[8,36,512]{2,1,0:T(8,128)(2,1)S(1)}, u32[]{:S(2)}, u32[]{:S(2)}) collective-permute-start(bf16[8,36,512]{2,1,0:T(8,128)(2,1)S(1)} %shard_map.153), channel_id=1, source_target_pairs={{30,0},{31,1},{0,2},{1,3},{2,4},{3,5},{4,6},{5,7},{6,8},{7,9},{8,1... | collective-permute-start | bytes 884744 | tf_op jit(solution)/shard_map/ppermute | solution.py:385
  130.2 1.3 collective-permute-start.40

commit v16 on v15

--- a/solution.py
+++ b/solution.py
@@ -458,15 +458,19 @@
         received = [send(column, way) for way in (beside, across, corner)]
         sent = [tied(column, received[0])] + received
         pieces = "columns", [column] + received + [send(part, swap) for part in sent]
-        last_other = across_z(tied(last_own, feed_pair), 2)
-        (last_four,) = join([[last_own, last_beside, last_other, send(last_other, across)]])
+        last_other = across_z(tied(last_own, column), 2)
+        last_across = send(tied(last_other, received[0]), across)
+        last_four, final_four = join(
+            [[last_own, last_beside, last_other, last_across]], widths=widths
+        )
         (feed_column,) = join([[feed_pair, across_z(feed_pair, 1)]])
         received = [send(feed_column, way) for way in (beside, across)]
         last_other = across_z(last_four, 1)
         middle_0 = attention(0, [windows], (0,), pieces, (feed_column,))
         first, second = tied((received[0][:2], received[1][2:]), middle_0)
         corners = [send(first, across), send(second, beside)]
-        *last_columns, final_one, final_other = halves(last_four, last_other, widths, (middle_0,))
+        last_columns = list(halves(last_four, last_other, widths[:1], (middle_0,)))
+        final_other = across_z(tied(final_four, middle_0), 1)
         middle_1 = attention(0, [windows], (1,), pieces, (middle_0, last_columns[0]))
         swapped = [send(part, swap) for part in [feed_column] + tied(received, middle_0)]
         received += join([tied(corners, (middle_1, *swapped))])
@@ -485,17 +489,19 @@
     size = left_0.shape[0]
     (ahead,) = strips([left_0, below_0], [[(0, 1, size - 1), (1, 0, 1)]])
     ahead = shift_from(ahead, 1, 0)
+    after = (below_0,)
     if relay:
         last_received = [
             send(part, way) for part, way in zip(tied(last_columns, middle_1), (across, beside))
         ]
-    left_1, right_1, low_1 = forward(0, middle_1, 0, feed_pieces, low_edge, (below_0,))
+        final_columns = list(halves(final_four, final_other, widths[1:], (low_0,)))
+        after += (final_columns[0],)
+    left_1, right_1, low_1 = forward(0, middle_1, 0, feed_pieces, low_edge, after)
     below_1 = shift_from(tied(low_1, ahead), 0, 1)
     if relay:
         last_pieces = last_columns + last_received
         last_pieces += [send(part, swap) for part in last_columns + tied(last_received, low_1)]
         last_pieces = "halves", last_pieces
-        final_columns = [final_one, final_other]
         final_received = [
             send(part, way)
             for part, way in zip(tied(final_columns, last_received), (across, beside))

time: 135 us -> 128 us (0.948)
  waiting for transfers between devices: 46.7 us -> 29.5 us
  starting transfers between devices: 32.5 us -> 43.1 us
    ppermute x35 -> x36, waiting for transfers between devices: 39.5 us -> 24.4 us  [send(): return lax.ppermute(block, ('lon', 'lat'), pairs)]
    ppermute x35 -> x36, starting transfers between devices: 26.3 us -> 38 us  [send(): return lax.ppermute(block, ('lon', 'lat'), pairs)]
    ppermute x6, waiting for transfers between devices: 7.23 us -> 5.1 us  [shift_from(): return lax.ppermute(block, ('lon', 'lat'), pairs)]
  transfers between devices with their start and end apart: 41 -> 42, of which waited for: 15 -> 16; matrix products, arithmetic and copies ran while one was open for 1% -> 1% of each run, Pallas kernels for 32% -> 33%
where the time goes in v16:
time: 128 us
  Pallas kernels  47.5 us (37%)
  starting transfers between devices  43.1 us (34%)
  waiting for transfers between devices  29.5 us (23%)
  local copies, waits for them, and re-layouts  7.64 us (6%)
    ppermute x36, starting transfers between devices, send(): return lax.ppermute(block, ('lon', 'lat'), pairs)  38 us
    pallas_call x4, Pallas kernels, attend(): pl.pallas_call(functools.partial(attend_kernel, shifted, row_windows, kin...  27.7 us
    ppermute x36, waiting for transfers between devices, send(): return lax.ppermute(block, ('lon', 'lat'), pairs)  24.4 us
    pallas_call x4, Pallas kernels, feed(): pl.pallas_call(functools.partial(feed_kernel, kind, len(pieces), hidden_s...  19.4 us
    ppermute x6, waiting for transfers between devices, shift_from(): return lax.ppermute(block, ('lon', 'lat'), pairs)  5.1 us
    ppermute x6, starting transfers between devices, shift_from(): return lax.ppermute(block, ('lon', 'lat'), pairs)  5.09 us
    unnamed x20, local copies, waits for them, and re-layouts  3.7 us
  transfers between devices with their start and end apart: 42, of which 16 were waited for; matrix products, arithmetic and copies ran while one was open for 1% of the time, Pallas kernels for 33%

profile of v16, /device:TPU:0, one launch (start us, length us, event | category | flops | bytes accessed | tf_op | source)
XLA Modules:
  0.0 128.2 jit_solution(8289675541770878264)
XLA Ops:
  0.0 0.9 copy-done.2
  0.9 0.8 copy-done.3
  1.8 4.0 %collective-permute-start = (bf16[1,16,2048]{2,1,0:T(8,128)(2,1)S(1)}, bf16[1,16,2048]{2,1,0:T(8,128)(2,1)S(1)}, u32[]{:S(2)}, u32[]{:S(2)}) collective-permute-start(bf16[1,16,2048]{2,1,0:T(8,128)(2,1)S(1)} %shard_map.136.refs_0_.refs_6_), channel_id=1, source_target_pairs={{0,16},{1,17},{2,18},{3,19},{4,20},{5,21},{6,22},{7,23},{8,24},{9,... | collective-permute-start | bytes 196616 | tf_op jit(solution)/shard_map/ppermute | solution.py:121
  5.8 0.9 copy-done
  6.8 0.9 copy-done.1
  7.7 1.6 %collective-permute-start.3 = (bf16[1,16,6144]{2,1,0:T(8,128)(2,1)S(1)}, bf16[1,16,6144]{2,1,0:T(8,128)(2,1)S(1)}, u32[]{:S(2)}, u32[]{:S(2)}) collective-permute-start(bf16[1,16,6144]{2,1,0:T(8,128)(2,1)S(1)} %get-tuple-element.52.refs_0_), channel_id=1, source_target_pairs={{0,2},{1,5},{2,0},{3,7},{4,6},{5,1},{6,4},{7,3},{8,10},{9,13},{10,... | collective-permute-start | bytes 589832 | tf_op jit(solution)/shard_map/ppermute | solution.py:121
  9.3 0.3 collective-permute-start.2
  9.6 0.8 copy.26
  10.5 0.5 reshape.15.refs_2_.refs_0_
  11.0 1.6 %collective-permute-start.1 = (bf16[2,16,2048]{2,1,0:T(8,128)(2,1)S(1)}, bf16[2,16,2048]{2,1,0:T(8,128)(2,1)S(1)}, u32[]{:S(2)}, u32[]{:S(2)}) collective-permute-start(bf16[2,16,2048]{2,1,0:T(8,128)(2,1)S(1)} %shard_map.137.refs_0_), channel_id=1, source_target_pairs={{0,8},{1,9},{2,10},{3,11},{4,12},{5,13},{6,14},{7,15},{8,0},{9,1},... | collective-permute-start | bytes 393224 | tf_op jit(solution)/shard_map/ppermute | solution.py:121
  12.7 5.0 %collective-permute-done.2.refs_1_ = bf16[1,16,4096]{2,1,0:T(8,128)(2,1)S(1)} collective-permute-done((bf16[1,16,4096]{2,1,0:T(8,128)(2,1)S(1)}, bf16[1,16,4096]{2,1,0:T(8,128)(2,1)S(1)}, u32[]{:S(2)}, u32[]{:S(2)}) %collective-permute-start.2) | collective-permute-done | bytes 131104 | tf_op jit(solution)/shard_map/ppermute | solution.py:121
  17.8 1.6 %collective-permute-start.4 = (bf16[4,16,2048]{2,1,0:T(8,128)(2,1)S(1)}, bf16[4,16,2048]{2,1,0:T(8,128)(2,1)S(1)}, u32[]{:S(2)}, u32[]{:S(2)}) collective-permute-start(bf16[4,16,2048]{2,1,0:T(8,128)(2,1)S(1)} %shard_map.140.refs_1_), channel_id=1, source_target_pairs={{0,2},{1,5},{2,0},{3,7},{4,6},{5,1},{6,4},{7,3},{8,10},{9,13},{10,... | collective-permute-start | bytes 786440 | tf_op jit(solution)/shard_map/ppermute | solution.py:121
  19.4 1.4 %collective-permute-start.5 = (bf16[4,16,2048]{2,1,0:T(8,128)(2,1)S(1)}, bf16[4,16,2048]{2,1,0:T(8,128)(2,1)S(1)}, u32[]{:S(2)}, u32[]{:S(2)}) collective-permute-start(bf16[4,16,2048]{2,1,0:T(8,128)(2,1)S(1)} %shard_map.140.refs_1_), channel_id=1, source_target_pairs={{0,4},{1,3},{2,6},{3,1},{4,0},{5,7},{6,2},{7,5},{8,12},{9,11},{10,... | collective-permute-start | bytes 786440 | tf_op jit(solution)/shard_map/ppermute | solution.py:121
  20.8 0.6 collective-permute-start.6
  21.3 0.4 collective-permute-start.11
  21.7 4.0 %collective-permute-start.16 = (bf16[1,16,6144]{2,1,0:T(8,128)(2,1)S(1)}, bf16[1,16,6144]{2,1,0:T(8,128)(2,1)S(1)}, u32[]{:S(2)}, u32[]{:S(2)}) collective-permute-start(bf16[1,16,6144]{2,1,0:T(8,128)(2,1)S(1)} %get-tuple-element.52.refs_0_), channel_id=1, source_target_pairs={{0,16},{1,17},{2,18},{3,19},{4,20},{5,21},{6,22},{7,23},{8,24},{9,... | collective-permute-start | bytes 589832 | tf_op jit(solution)/shard_map/ppermute | solution.py:121
  25.7 1.4 %collective-permute-done.4.refs_2_ = bf16[4,16,2048]{2,1,0:T(8,128)(2,1)S(1)} collective-permute-done((bf16[4,16,2048]{2,1,0:T(8,128)(2,1)S(1)}, bf16[4,16,2048]{2,1,0:T(8,128)(2,1)S(1)}, u32[]{:S(2)}, u32[]{:S(2)}) %collective-permute-start.4) | collective-permute-done | bytes 262176 | tf_op jit(solution)/shard_map/ppermute | solution.py:121
  27.1 3.1 %collective-permute-done.16.refs_2_ = bf16[1,16,6144]{2,1,0:T(8,128)(2,1)S(1)} collective-permute-done((bf16[1,16,6144]{2,1,0:T(8,128)(2,1)S(1)}, bf16[1,16,6144]{2,1,0:T(8,128)(2,1)S(1)}, u32[]{:S(2)}, u32[]{:S(2)}) %collective-permute-start.16) | collective-permute-done | bytes 196640 | tf_op jit(solution)/shard_map/ppermute | solution.py:121
  30.2 0.5 collective-permute-start.9
  30.7 1.3 %collective-permute-done.6.refs_4_ = bf16[4,16,2048]{2,1,0:T(8,128)(2,1)S(1)} collective-permute-done((bf16[4,16,2048]{2,1,0:T(8,128)(2,1)S(1)}, bf16[4,16,2048]{2,1,0:T(8,128)(2,1)S(1)}, u32[]{:S(2)}, u32[]{:S(2)}) %collective-permute-start.6) | collective-permute-done | bytes 262176 | tf_op jit(solution)/shard_map/ppermute | solution.py:121
  32.1 0.1 multiply_reduce_fusion
  32.2 1.3 collective-permute-start.17
  33.5 4.4 %collective-permute-done.17.refs_3_ = bf16[1,16,6144]{2,1,0:T(8,128)(2,1)S(1)} collective-permute-done((bf16[1,16,6144]{2,1,0:T(8,128)(2,1)S(1)}, bf16[1,16,6144]{2,1,0:T(8,128)(2,1)S(1)}, u32[]{:S(2)}, u32[]{:S(2)}) %collective-permute-start.17) | collective-permute-done | bytes 196640 | tf_op jit(solution)/shard_map/ppermute | solution.py:121
  37.9 1.7 %collective-permute-start.12 = (bf16[4,16,4096]{2,1,0:T(8,128)(2,1)S(1)}, bf16[4,16,4096]{2,1,0:T(8,128)(2,1)S(1)}, u32[]{:S(2)}, u32[]{:S(2)}) collective-permute-start(bf16[4,16,4096]{2,1,0:T(8,128)(2,1)S(1)} %shard_map.141.refs_12_.refs_1_), channel_id=1, source_target_pairs={{0,2},{1,5},{2,0},{3,7},{4,6},{5,1},{6,4},{7,3},{8,10},{9,13},{10,... | collective-permute-start | bytes 1572872 | tf_op jit(solution)/shard_map/ppermute | solution.py:121
  39.7 0.6 collective-permute-start.13
  40.3 3.9 %collective-permute-start.18 = (bf16[4,16,2048]{2,1,0:T(8,128)(2,1)S(1)}, bf16[4,16,2048]{2,1,0:T(8,128)(2,1)S(1)}, u32[]{:S(2)}, u32[]{:S(2)}) collective-permute-start(bf16[4,16,2048]{2,1,0:T(8,128)(2,1)S(1)} %get-tuple-element.54.refs_0_), channel_id=1, source_target_pairs={{0,8},{1,9},{2,10},{3,11},{4,12},{5,13},{6,14},{7,15},{8,0},{9,1},... | collective-permute-start | bytes 786440 | tf_op jit(solution)/shard_map/ppermute | solution.py:121
  44.3 6.9 %shard_map.142.refs_2_.refs_12_.refs_0_ = bf16[4,144,512]{2,1,0:T(8,128)(2,1)S(1)} custom-call(bf16[8,144,512]{2,1,0:T(8,128)(2,1)S(1)} %reshape.15.refs_2_.refs_0_, bf16[4,16,2048]{2,1,0:T(8,128)(2,1)S(1)} %shard_map.140.refs_1_, bf16[4,16,2048]{2,1,0:T(8,128)(2,1)S(1)} %collective-permute-done.4.refs_2_, ...), custom_call_target="tpu_custom_call" | custom-call | flops 8000000000 | bytes 6000000 | tf_op jit(solution)/shard_map/pallas_call | solution.py:300
  51.2 0.8 collective-permute-done.12.refs_2_
  52.0 1.4 %collective-permute-start.14 = (bf16[2,16,4096]{2,1,0:T(8,128)(2,1)S(1)}, bf16[2,16,4096]{2,1,0:T(8,128)(2,1)S(1)}, u32[]{:S(2)}, u32[]{:S(2)}) collective-permute-start(bf16[2,16,4096]{2,1,0:T(8,128)(2,1)S(1)} %slice.39), channel_id=1, source_target_pairs={{0,4},{1,3},{2,6},{3,1},{4,0},{5,7},{6,2},{7,5},{8,12},{9,11},{10,... | collective-permute-start | bytes 786440 | tf_op jit(solution)/shard_map/ppermute | solution.py:121
  53.4 1.7 %collective-permute-start.15 = (bf16[2,16,4096]{2,1,0:T(8,128)(2,1)S(1)}, bf16[2,16,4096]{2,1,0:T(8,128)(2,1)S(1)}, u32[]{:S(2)}, u32[]{:S(2)}) collective-permute-start(bf16[2,16,4096]{2,1,0:T(8,128)(2,1)S(1)} %slice.40), channel_id=1, source_target_pairs={{0,2},{1,5},{2,0},{3,7},{4,6},{5,1},{6,4},{7,3},{8,10},{9,13},{10,... | collective-permute-start | bytes 786440 | tf_op jit(solution)/shard_map/ppermute | solution.py:121
  55.1 0.5 collective-permute-start.21
  55.7 6.9 %shard_map.145.refs_0_ = bf16[4,144,512]{2,1,0:T(8,128)(2,1)S(1)} custom-call(bf16[8,144,512]{2,1,0:T(8,128)(2,1)S(1)} %reshape.15.refs_2_.refs_0_, bf16[4,16,2048]{2,1,0:T(8,128)(2,1)S(1)} %shard_map.140.refs_1_, bf16[4,16,2048]{2,1,0:T(8,128)(2,1)S(1)} %collective-permute-done.4.refs_2_, bf16[4,16,2048]{2,1,0:T(8,128)(2,1)S(1)} %collective-permute-done.5.refs_3_, ...), custom_call_target="tpu_custom_call" | custom-call | flops 8000000000 | bytes 6000000 | tf_op jit(solution)/shard_map/pallas_call | solution.py:300
  62.8 3.8 %collective-permute-start.24 = (bf16[4,16,4096]{2,1,0:T(8,128)(2,1)S(1)}, bf16[4,16,4096]{2,1,0:T(8,128)(2,1)S(1)}, u32[]{:S(2)}, u32[]{:S(2)}) collective-permute-start(bf16[4,16,4096]{2,1,0:T(8,128)(2,1)S(1)} %get-tuple-element.63.refs_0_), channel_id=1, source_target_pairs={{0,8},{1,9},{2,10},{3,11},{4,12},{5,13},{6,14},{7,15},{8,0},{9,1},... | collective-permute-start | bytes 1572872 | tf_op jit(solution)/shard_map/ppermute | solution.py:121
  66.6 0.6 collective-permute-start.27
  67.2 0.9 collective-permute-start.28
  68.2 4.8 %shard_map.147 = (bf16[8,36,512]{2,1,0:T(8,128)(2,1)S(1)}, bf16[8,36,512]{2,1,0:T(8,128)(2,1)S(1)}, bf16[2,36,512]{2,1,0:T(8,128)(2,1)S(1)}) custom-call(bf16[4,144,512]{2,1,0:T(8,128)(2,1)S(1)} %shard_map.142.refs_2_.refs_12_.refs_0_, bf16[4,16,4096]{2,1,0:T(8,128)(2,1)S(1)} %shard_map.141.refs_12_.refs_1_, ...), custom_call_target="tpu_custom_call" | custom-call | flops 1000000 | bytes 100000 | tf_op jit(solution)/shard_map/pallas_call | solution.py:358
  73.1 1.3 collective-permute-done.23.refs_10_.refs_1_.refs_3_
  74.4 2.5 %collective-permute-start.25 = (bf16[8,36,512]{2,1,0:T(8,128)(2,1)S(1)}, bf16[8,36,512]{2,1,0:T(8,128)(2,1)S(1)}, u32[]{:S(2)}, u32[]{:S(2)}) collective-permute-start(bf16[8,36,512]{2,1,0:T(8,128)(2,1)S(1)} %shard_map.150), channel_id=1, source_target_pairs={{2,0},{3,1},{4,2},{5,3},{6,4},{7,5},{8,6},{9,7},{10,8},{11,9},{12,... | collective-permute-start | bytes 884744 | tf_op jit(solution)/shard_map/ppermute | solution.py:385
  76.9 2.5 %collective-permute-done.24.refs_1_ = bf16[4,16,4096]{2,1,0:T(8,128)(2,1)S(1)} collective-permute-done((bf16[4,16,4096]{2,1,0:T(8,128)(2,1)S(1)}, bf16[4,16,4096]{2,1,0:T(8,128)(2,1)S(1)}, u32[]{:S(2)}, u32[]{:S(2)}) %collective-permute-start.24) | collective-permute-done | bytes 524320 | tf_op jit(solution)/shard_map/ppermute | solution.py:121
  79.4 4.9 %shard_map.149 = (bf16[8,36,512]{2,1,0:T(8,128)(2,1)S(1)}, bf16[8,36,512]{2,1,0:T(8,128)(2,1)S(1)}, bf16[2,36,512]{2,1,0:T(8,128)(2,1)S(1)}) custom-call(bf16[4,144,512]{2,1,0:T(8,128)(2,1)S(1)} %shard_map.145.refs_0_, bf16[4,16,4096]{2,1,0:T(8,128)(2,1)S(1)} %shard_map.141.refs_12_.refs_1_, bf16[4,16,4096]{2,1,0:T(8,128)(2,1)S(1)} %collective-permute-done.12.refs_2_, ...), custom_call_target="tpu_custom_call" | custom-call | flops 1000000 | bytes 100000 | tf_op jit(solution)/shard_map/pallas_call | solution.py:358
  84.3 0.6 collective-permute-start.31
  84.9 0.1 collective-permute-start.32
  85.0 0.4 collective-permute-done.25.refs_1_
  85.4 1.2 collective-permute-done.26.refs_4_
  86.7 0.3 collective-permute-start.35
  87.0 0.3 collective-permute-start.36
  87.3 0.3 collective-permute-start.33
  87.6 3.4 %collective-permute-start.34 = (bf16[4,16,4096]{2,1,0:T(8,128)(2,1)S(1)}, bf16[4,16,4096]{2,1,0:T(8,128)(2,1)S(1)}, u32[]{:S(2)}, u32[]{:S(2)}) collective-permute-start(bf16[4,16,4096]{2,1,0:T(8,128)(2,1)S(1)} %get-tuple-element.78.refs_2_), channel_id=1, source_target_pairs={{0,2},{1,5},{2,0},{3,7},{4,6},{5,1},{6,4},{7,3},{8,10},{9,13},{10,... | collective-permute-start | bytes 1572872 | tf_op jit(solution)/shard_map/ppermute | solution.py:121
  91.0 6.9 %shard_map.152.refs_0_ = bf16[4,144,512]{2,1,0:T(8,128)(2,1)S(1)} custom-call(bf16[8,36,512]{2,1,0:T(8,128)(2,1)S(1)} %get-tuple-element.70.refs_0_, bf16[8,36,512]{2,1,0:T(8,128)(2,1)S(1)} %collective-permute-done.25.refs_1_, bf16[4,16,2048]{2,1,0:T(8,128)(2,1)S(1)} %get-tuple-element.72.refs_13_.refs_2_, ...), custom_call_target="tpu_custom_call" | custom-call | flops 8000000000 | bytes 6000000 | tf_op jit(solution)/shard_map/pallas_call | solution.py:300
  97.9 3.4 %collective-permute-done.33.refs_3_ = bf16[4,16,4096]{2,1,0:T(8,128)(2,1)S(1)} collective-permute-done((bf16[4,16,4096]{2,1,0:T(8,128)(2,1)S(1)}, bf16[4,16,4096]{2,1,0:T(8,128)(2,1)S(1)}, u32[]{:S(2)}, u32[]{:S(2)}) %collective-permute-start.33) | collective-permute-done | bytes 524320 | tf_op jit(solution)/shard_map/ppermute | solution.py:121
  101.3 0.1 collective-permute-done.34.refs_4_
  101.4 0.5 collective-permute-start.37
  102.0 1.5 %collective-permute-done.37.refs_7_ = bf16[4,16,4096]{2,1,0:T(8,128)(2,1)S(1)} collective-permute-done((bf16[4,16,4096]{2,1,0:T(8,128)(2,1)S(1)}, bf16[4,16,4096]{2,1,0:T(8,128)(2,1)S(1)}, u32[]{:S(2)}, u32[]{:S(2)}) %collective-permute-start.37) | collective-permute-done | bytes 524320 | tf_op jit(solution)/shard_map/ppermute | solution.py:121
  103.5 0.7 collective-permute-done.38.refs_8_
  104.2 4.8 %shard_map.153 = (bf16[8,36,512]{2,1,0:T(8,128)(2,1)S(1)}, bf16[8,36,512]{2,1,0:T(8,128)(2,1)S(1)}, bf16[2,36,512]{2,1,0:T(8,128)(2,1)S(1)}) custom-call(bf16[4,144,512]{2,1,0:T(8,128)(2,1)S(1)} %shard_map.152.refs_0_, bf16[4,16,4096]{2,1,0:T(8,128)(2,1)S(1)} %get-tuple-element.77.refs_11_.refs_1_, bf16[4,16,4096]{2,1,0:T(8,128)(2,1)S(1)} %get-tuple-element.78.refs_2_, ...), custom_call_target="tpu_custom_call" | custom-call | flops 1000000 | bytes 100000 | tf_op jit(solution)/shard_map/pallas_call | solution.py:358
  109.1 0.4 collective-permute-start.39
  109.5 0.9 collective-permute-done.39.refs_0_.refs_14_.refs_5_
  110.4 2.0 %collective-permute-start.40 = (bf16[8,36,512]{2,1,0:T(8,128)(2,1)S(1)}, bf16[8,36,512]{2,1,0:T(8,128)(2,1)S(1)}, u32[]{:S(2)}, u32[]{:S(2)}) collective-permute-start(bf16[8,36,512]{2,1,0:T(8,128)(2,1)S(1)} %shard_map.154), channel_id=1, source_target_pairs={{30,0},{31,1},{0,2},{1,3},{2,4},{3,5},{4,6},{5,7},{6,8},{7,9},{8,1... | collective-permute-start | bytes 884744 | tf_op jit(solution)/shard_map/ppermute | solution.py:385
  112.4 6.9 %shard_map.155.refs_0_ = bf16[4,144,512]{2,1,0:T(8,128)(2,1)S(1)} custom-call(bf16[8,36,512]{2,1,0:T(8,128)(2,1)S(1)} %get-tuple-element.83.refs_0_, bf16[8,36,512]{2,1,0:T(8,128)(2,1)S(1)} %get-tuple-element.84.refs_1_, bf16[4,16,2048]{2,1,0:T(8,128)(2,1)S(1)} %get-tuple-element.72.refs_13_.refs_2_, bf16[4,16,2048]{2,1,0:T(8,128)(2,1)S(1)} %get-tuple-element.73.refs_3_, ...), custom_call_target="tpu_custom_call" | custom-call | flops 8000000000 | bytes 6000000 | tf_op jit(solution)/shard_map/pallas_call | solution.py:300
  119.3 4.9 %shard_map.156 = (bf16[8,36,512]{2,1,0:T(8,128)(2,1)S(1)}, bf16[8,36,512]{2,1,0:T(8,128)(2,1)S(1)}, bf16[2,36,512]{2,1,0:T(8,128)(2,1)S(1)}) custom-call(bf16[4,144,512]{2,1,0:T(8,128)(2,1)S(1)} %shard_map.155.refs_0_, bf16[4,16,4096]{2,1,0:T(8,128)(2,1)S(1)} %get-tuple-element.77.refs_11_.refs_1_, bf16[4,16,4096]{2,1,0:T(8,128)(2,1)S(1)} %get-tuple-element.78.refs_2_, ...), custom_call_target="tpu_custom_call" | custom-call | flops 1000000 | bytes 100000 | tf_op jit(solution)/shard_map/pallas_call | solution.py:358
  124.3 1.3 collective-permute-done.41.refs_4_
  125.6 0.1 shard_map.157
  125.7 0.4 copy.23
  126.0 2.2 %copy.24 = bf16[4,6,8,3,2,512]{5,4,3,2,1,0:T(2,128)(2,1)} copy(bf16[4,6,8,3,2,512]{5,2,0,4,3,1:T(8,128)(2,1)S(1)} %bitcast.16) | data formatting | bytes 2359296 | tf_op jit(solution)/shard_map/transpose | solution.py:423
  (71 shorter events, 0.8 us)
Async XLA Ops:
  0.0 0.9 copy-start.2
  0.9 0.8 copy-start.3
  1.8 9.2 %collective-permute-start = (bf16[1,16,2048]{2,1,0:T(8,128)(2,1)S(1)}, bf16[1,16,2048]{2,1,0:T(8,128)(2,1)S(1)}, u32[]{:S(2)}, u32[]{:S(2)}) collective-permute-start(bf16[1,16,2048]{2,1,0:T(8,128)(2,1)S(1)} %shard_map.136.refs_0_.refs_6_), channel_id=1, source_target_pairs={{0,16},{1,17},{2,18},{3,19},{4,20},{5,21},{6,22},{7,23},{8,24},{9,... | collective-permute-start | bytes 196616 | tf_op jit(solution)/shard_map/ppermute | solution.py:121
  5.8 0.9 copy-start
  6.8 0.9 copy-start.1
  7.7 1.9 %copy-start.6 = (bf16[24,24,2,512]{3,2,1,0:T(2,128)(2,1)S(1)}, bf16[24,24,2,512]{3,2,1,0:T(2,128)(2,1)}, u32[]{:S(2)}) copy-start(bf16[24,24,2,512]{3,2,1,0:T(2,128)(2,1)} %param.14) | copy-start | bytes 3538948
  7.7 10.0 %collective-permute-start.3 = (bf16[1,16,6144]{2,1,0:T(8,128)(2,1)S(1)}, bf16[1,16,6144]{2,1,0:T(8,128)(2,1)S(1)}, u32[]{:S(2)}, u32[]{:S(2)}) collective-permute-start(bf16[1,16,6144]{2,1,0:T(8,128)(2,1)S(1)} %get-tuple-element.52.refs_0_), channel_id=1, source_target_pairs={{0,2},{1,5},{2,0},{3,7},{4,6},{5,1},{6,4},{7,3},{8,10},{9,13},{10,... | collective-permute-start | bytes 589832 | tf_op jit(solution)/shard_map/ppermute | solution.py:121
  9.3 8.4 %collective-permute-start.2 = (bf16[1,16,4096]{2,1,0:T(8,128)(2,1)S(1)}, bf16[1,16,4096]{2,1,0:T(8,128)(2,1)S(1)}, u32[]{:S(2)}, u32[]{:S(2)}) collective-permute-start(bf16[1,16,4096]{2,1,0:T(8,128)(2,1)S(1)} %get-tuple-element.47.refs_0_), channel_id=1, source_target_pairs={{0,16},{1,17},{2,18},{3,19},{4,20},{5,21},{6,22},{7,23},{8,24},{9,... | collective-permute-start | bytes 393224 | tf_op jit(solution)/shard_map/ppermute | solution.py:121
  11.0 14.8 %copy-start.8 = (f32[2,2,512]{2,1,0:T(2,128)S(1)}, f32[2,2,512]{2,1,0:T(2,128)}, u32[]{:S(2)}) copy-start(f32[2,2,512]{2,1,0:T(2,128)} %param.19) | copy-start | bytes 24580
  11.0 21.1 %copy-start.7 = (f32[16,512]{1,0:T(8,128)S(1)}, f32[16,512]{1,0:T(8,128)}, u32[]{:S(2)}) copy-start(f32[16,512]{1,0:T(8,128)} %constant.8.clone) | copy-start | bytes 98308
  11.0 21.1 %copy-start.9 = (f32[2,16]{1,0:T(2,128)S(1)}, f32[2,16]{1,0:T(2,128)}, u32[]{:S(2)}) copy-start(f32[2,16]{1,0:T(2,128)} %param.20) | copy-start | bytes 388
  11.0 6.7 %collective-permute-start.1 = (bf16[2,16,2048]{2,1,0:T(8,128)(2,1)S(1)}, bf16[2,16,2048]{2,1,0:T(8,128)(2,1)S(1)}, u32[]{:S(2)}, u32[]{:S(2)}) collective-permute-start(bf16[2,16,2048]{2,1,0:T(8,128)(2,1)S(1)} %shard_map.137.refs_0_), channel_id=1, source_target_pairs={{0,8},{1,9},{2,10},{3,11},{4,12},{5,13},{6,14},{7,15},{8,0},{9,1},... | collective-permute-start | bytes 393224 | tf_op jit(solution)/shard_map/ppermute | solution.py:121
  17.8 26.5 %copy-start.4 = (bf16[640,256]{1,0:T(8,128)(2,1)S(1)}, bf16[640,256]{1,0:T(8,128)(2,1)}, u32[]{:S(2)}) copy-start(bf16[640,256]{1,0:T(8,128)(2,1)} %constant.9.clone.refs_11_.refs_12_) | copy-start | bytes 983044
  17.8 9.3 %collective-permute-start.4 = (bf16[4,16,2048]{2,1,0:T(8,128)(2,1)S(1)}, bf16[4,16,2048]{2,1,0:T(8,128)(2,1)S(1)}, u32[]{:S(2)}, u32[]{:S(2)}) collective-permute-start(bf16[4,16,2048]{2,1,0:T(8,128)(2,1)S(1)} %shard_map.140.refs_1_), channel_id=1, source_target_pairs={{0,2},{1,5},{2,0},{3,7},{4,6},{5,1},{6,4},{7,3},{8,10},{9,13},{10,... | collective-permute-start | bytes 786440 | tf_op jit(solution)/shard_map/ppermute | solution.py:121
  19.4 10.9 %collective-permute-start.5 = (bf16[4,16,2048]{2,1,0:T(8,128)(2,1)S(1)}, bf16[4,16,2048]{2,1,0:T(8,128)(2,1)S(1)}, u32[]{:S(2)}, u32[]{:S(2)}) collective-permute-start(bf16[4,16,2048]{2,1,0:T(8,128)(2,1)S(1)} %shard_map.140.refs_1_), channel_id=1, source_target_pairs={{0,4},{1,3},{2,6},{3,1},{4,0},{5,7},{6,2},{7,5},{8,12},{9,11},{10,... | collective-permute-start | bytes 786440 | tf_op jit(solution)/shard_map/ppermute | solution.py:121
  20.8 11.3 %collective-permute-start.6 = (bf16[4,16,2048]{2,1,0:T(8,128)(2,1)S(1)}, bf16[4,16,2048]{2,1,0:T(8,128)(2,1)S(1)}, u32[]{:S(2)}, u32[]{:S(2)}) collective-permute-start(bf16[4,16,2048]{2,1,0:T(8,128)(2,1)S(1)} %shard_map.140.refs_1_), channel_id=1, source_target_pairs={{0,6},{1,7},{2,4},{3,5},{4,2},{5,3},{6,0},{7,1},{8,14},{9,15},{10,... | collective-permute-start | bytes 786440 | tf_op jit(solution)/shard_map/ppermute | solution.py:121
  21.3 10.8 %collective-permute-start.11 = (bf16[2,16,4096]{2,1,0:T(8,128)(2,1)S(1)}, bf16[2,16,4096]{2,1,0:T(8,128)(2,1)S(1)}, u32[]{:S(2)}, u32[]{:S(2)}) collective-permute-start(bf16[2,16,4096]{2,1,0:T(8,128)(2,1)S(1)} %shard_map.139.refs_2_.refs_0_), channel_id=1, source_target_pairs={{0,8},{1,9},{2,10},{3,11},{4,12},{5,13},{6,14},{7,15},{8,0},{9,1},... | collective-permute-start | bytes 786440 | tf_op jit(solution)/shard_map/ppermute | solution.py:121
  21.7 8.5 %collective-permute-start.16 = (bf16[1,16,6144]{2,1,0:T(8,128)(2,1)S(1)}, bf16[1,16,6144]{2,1,0:T(8,128)(2,1)S(1)}, u32[]{:S(2)}, u32[]{:S(2)}) collective-permute-start(bf16[1,16,6144]{2,1,0:T(8,128)(2,1)S(1)} %get-tuple-element.52.refs_0_), channel_id=1, source_target_pairs={{0,16},{1,17},{2,18},{3,19},{4,20},{5,21},{6,22},{7,23},{8,24},{9,... | collective-permute-start | bytes 589832 | tf_op jit(solution)/shard_map/ppermute | solution.py:121
  27.1 12.6 %collective-permute-start.7 = (bf16[4,16,2048]{2,1,0:T(8,128)(2,1)S(1)}, bf16[4,16,2048]{2,1,0:T(8,128)(2,1)S(1)}, u32[]{:S(2)}, u32[]{:S(2)}) collective-permute-start(bf16[4,16,2048]{2,1,0:T(8,128)(2,1)S(1)} %shard_map.140.refs_1_), channel_id=1, source_target_pairs={{0,1},{1,0},{2,3},{3,2},{4,5},{5,4},{6,7},{7,6},{8,9},{9,8},{10,11... | collective-permute-start | bytes 786440 | tf_op jit(solution)/shard_map/ppermute | solution.py:121
  30.2 10.1 %collective-permute-start.8 = (bf16[4,16,2048]{2,1,0:T(8,128)(2,1)S(1)}, bf16[4,16,2048]{2,1,0:T(8,128)(2,1)S(1)}, u32[]{:S(2)}, u32[]{:S(2)}) collective-permute-start(bf16[4,16,2048]{2,1,0:T(8,128)(2,1)S(1)} %collective-permute-done.4.refs_2_), channel_id=1, source_target_pairs={{0,1},{1,0},{2,3},{3,2},{4,5},{5,4},{6,7},{7,6},{8,9},{9,8},{10,11... | collective-permute-start | bytes 786440 | tf_op jit(solution)/shard_map/ppermute | solution.py:121
  30.2 10.1 %collective-permute-start.9 = (bf16[4,16,2048]{2,1,0:T(8,128)(2,1)S(1)}, bf16[4,16,2048]{2,1,0:T(8,128)(2,1)S(1)}, u32[]{:S(2)}, u32[]{:S(2)}) collective-permute-start(bf16[4,16,2048]{2,1,0:T(8,128)(2,1)S(1)} %collective-permute-done.5.refs_3_), channel_id=1, source_target_pairs={{0,1},{1,0},{2,3},{3,2},{4,5},{5,4},{6,7},{7,6},{8,9},{9,8},{10,11... | collective-permute-start | bytes 786440 | tf_op jit(solution)/shard_map/ppermute | solution.py:121
  32.1 12.2 %collective-permute-start.10 = (bf16[4,16,2048]{2,1,0:T(8,128)(2,1)S(1)}, bf16[4,16,2048]{2,1,0:T(8,128)(2,1)S(1)}, u32[]{:S(2)}, u32[]{:S(2)}) collective-permute-start(bf16[4,16,2048]{2,1,0:T(8,128)(2,1)S(1)} %collective-permute-done.6.refs_4_), channel_id=1, source_target_pairs={{0,1},{1,0},{2,3},{3,2},{4,5},{5,4},{6,7},{7,6},{8,9},{9,8},{10,11... | collective-permute-start | bytes 786440 | tf_op jit(solution)/shard_map/ppermute | solution.py:121
  32.2 5.7 %collective-permute-start.17 = (bf16[1,16,6144]{2,1,0:T(8,128)(2,1)S(1)}, bf16[1,16,6144]{2,1,0:T(8,128)(2,1)S(1)}, u32[]{:S(2)}, u32[]{:S(2)}) collective-permute-start(bf16[1,16,6144]{2,1,0:T(8,128)(2,1)S(1)} %collective-permute-done.16.refs_2_), channel_id=1, source_target_pairs={{0,4},{1,3},{2,6},{3,1},{4,0},{5,7},{6,2},{7,5},{8,12},{9,11},{10,... | collective-permute-start | bytes 589832 | tf_op jit(solution)/shard_map/ppermute | solution.py:121
  37.9 14.0 %collective-permute-start.12 = (bf16[4,16,4096]{2,1,0:T(8,128)(2,1)S(1)}, bf16[4,16,4096]{2,1,0:T(8,128)(2,1)S(1)}, u32[]{:S(2)}, u32[]{:S(2)}) collective-permute-start(bf16[4,16,4096]{2,1,0:T(8,128)(2,1)S(1)} %shard_map.141.refs_12_.refs_1_), channel_id=1, source_target_pairs={{0,2},{1,5},{2,0},{3,7},{4,6},{5,1},{6,4},{7,3},{8,10},{9,13},{10,... | collective-permute-start | bytes 1572872 | tf_op jit(solution)/shard_map/ppermute | solution.py:121
  39.7 12.2 %collective-permute-start.13 = (bf16[4,16,4096]{2,1,0:T(8,128)(2,1)S(1)}, bf16[4,16,4096]{2,1,0:T(8,128)(2,1)S(1)}, u32[]{:S(2)}, u32[]{:S(2)}) collective-permute-start(bf16[4,16,4096]{2,1,0:T(8,128)(2,1)S(1)} %shard_map.141.refs_12_.refs_1_), channel_id=1, source_target_pairs={{0,4},{1,3},{2,6},{3,1},{4,0},{5,7},{6,2},{7,5},{8,12},{9,11},{10,... | collective-permute-start | bytes 1572872 | tf_op jit(solution)/shard_map/ppermute | solution.py:121
  40.3 22.3 %collective-permute-start.19 = (bf16[4,16,4096]{2,1,0:T(8,128)(2,1)S(1)}, bf16[4,16,4096]{2,1,0:T(8,128)(2,1)S(1)}, u32[]{:S(2)}, u32[]{:S(2)}) collective-permute-start(bf16[4,16,4096]{2,1,0:T(8,128)(2,1)S(1)} %shard_map.141.refs_12_.refs_1_), channel_id=1, source_target_pairs={{0,1},{1,0},{2,3},{3,2},{4,5},{5,4},{6,7},{7,6},{8,9},{9,8},{10,11... | collective-permute-start | bytes 1572872 | tf_op jit(solution)/shard_map/ppermute | solution.py:121
  40.3 14.8 %collective-permute-start.18 = (bf16[4,16,2048]{2,1,0:T(8,128)(2,1)S(1)}, bf16[4,16,2048]{2,1,0:T(8,128)(2,1)S(1)}, u32[]{:S(2)}, u32[]{:S(2)}) collective-permute-start(bf16[4,16,2048]{2,1,0:T(8,128)(2,1)S(1)} %get-tuple-element.54.refs_0_), channel_id=1, source_target_pairs={{0,8},{1,9},{2,10},{3,11},{4,12},{5,13},{6,14},{7,15},{8,0},{9,1},... | collective-permute-start | bytes 786440 | tf_op jit(solution)/shard_map/ppermute | solution.py:121
  52.0 10.6 %collective-permute-start.14 = (bf16[2,16,4096]{2,1,0:T(8,128)(2,1)S(1)}, bf16[2,16,4096]{2,1,0:T(8,128)(2,1)S(1)}, u32[]{:S(2)}, u32[]{:S(2)}) collective-permute-start(bf16[2,16,4096]{2,1,0:T(8,128)(2,1)S(1)} %slice.39), channel_id=1, source_target_pairs={{0,4},{1,3},{2,6},{3,1},{4,0},{5,7},{6,2},{7,5},{8,12},{9,11},{10,... | collective-permute-start | bytes 786440 | tf_op jit(solution)/shard_map/ppermute | solution.py:121
  53.4 9.2 %collective-permute-start.15 = (bf16[2,16,4096]{2,1,0:T(8,128)(2,1)S(1)}, bf16[2,16,4096]{2,1,0:T(8,128)(2,1)S(1)}, u32[]{:S(2)}, u32[]{:S(2)}) collective-permute-start(bf16[2,16,4096]{2,1,0:T(8,128)(2,1)S(1)} %slice.40), channel_id=1, source_target_pairs={{0,2},{1,5},{2,0},{3,7},{4,6},{5,1},{6,4},{7,3},{8,10},{9,13},{10,... | collective-permute-start | bytes 786440 | tf_op jit(solution)/shard_map/ppermute | solution.py:121
  55.1 7.5 %collective-permute-start.20 = (bf16[4,16,4096]{2,1,0:T(8,128)(2,1)S(1)}, bf16[4,16,4096]{2,1,0:T(8,128)(2,1)S(1)}, u32[]{:S(2)}, u32[]{:S(2)}) collective-permute-start(bf16[4,16,4096]{2,1,0:T(8,128)(2,1)S(1)} %collective-permute-done.12.refs_2_), channel_id=1, source_target_pairs={{0,1},{1,0},{2,3},{3,2},{4,5},{5,4},{6,7},{7,6},{8,9},{9,8},{10,11... | collective-permute-start | bytes 1572872 | tf_op jit(solution)/shard_map/ppermute | solution.py:121
  55.1 7.5 %collective-permute-start.21 = (bf16[4,16,4096]{2,1,0:T(8,128)(2,1)S(1)}, bf16[4,16,4096]{2,1,0:T(8,128)(2,1)S(1)}, u32[]{:S(2)}, u32[]{:S(2)}) collective-permute-start(bf16[4,16,4096]{2,1,0:T(8,128)(2,1)S(1)} %collective-permute-done.13.refs_3_), channel_id=1, source_target_pairs={{0,1},{1,0},{2,3},{3,2},{4,5},{5,4},{6,7},{7,6},{8,9},{9,8},{10,11... | collective-permute-start | bytes 1572872 | tf_op jit(solution)/shard_map/ppermute | solution.py:121
  62.7 5.4 %collective-permute-start.22 = (bf16[4,16,4096]{2,1,0:T(8,128)(2,1)S(1)}, bf16[4,16,4096]{2,1,0:T(8,128)(2,1)S(1)}, u32[]{:S(2)}, u32[]{:S(2)}) collective-permute-start(bf16[4,16,4096]{2,1,0:T(8,128)(2,1)S(1)} %shard_map.146.refs_4_), channel_id=1, source_target_pairs={{0,1},{1,0},{2,3},{3,2},{4,5},{5,4},{6,7},{7,6},{8,9},{9,8},{10,11... | collective-permute-start | bytes 1572872 | tf_op jit(solution)/shard_map/ppermute | solution.py:121
  62.8 16.6 %collective-permute-start.24 = (bf16[4,16,4096]{2,1,0:T(8,128)(2,1)S(1)}, bf16[4,16,4096]{2,1,0:T(8,128)(2,1)S(1)}, u32[]{:S(2)}, u32[]{:S(2)}) collective-permute-start(bf16[4,16,4096]{2,1,0:T(8,128)(2,1)S(1)} %get-tuple-element.63.refs_0_), channel_id=1, source_target_pairs={{0,8},{1,9},{2,10},{3,11},{4,12},{5,13},{6,14},{7,15},{8,0},{9,1},... | collective-permute-start | bytes 1572872 | tf_op jit(solution)/shard_map/ppermute | solution.py:121
  66.6 17.7 %collective-permute-start.27 = (bf16[4,16,2048]{2,1,0:T(8,128)(2,1)S(1)}, bf16[4,16,2048]{2,1,0:T(8,128)(2,1)S(1)}, u32[]{:S(2)}, u32[]{:S(2)}) collective-permute-start(bf16[4,16,2048]{2,1,0:T(8,128)(2,1)S(1)} %get-tuple-element.72.refs_13_.refs_2_), channel_id=1, source_target_pairs={{0,4},{1,3},{2,6},{3,1},{4,0},{5,7},{6,2},{7,5},{8,12},{9,11},{10,... | collective-permute-start | bytes 786440 | tf_op jit(solution)/shard_map/ppermute | solution.py:121
  67.2 17.1 %collective-permute-start.28 = (bf16[4,16,2048]{2,1,0:T(8,128)(2,1)S(1)}, bf16[4,16,2048]{2,1,0:T(8,128)(2,1)S(1)}, u32[]{:S(2)}, u32[]{:S(2)}) collective-permute-start(bf16[4,16,2048]{2,1,0:T(8,128)(2,1)S(1)} %get-tuple-element.73.refs_3_), channel_id=1, source_target_pairs={{0,2},{1,5},{2,0},{3,7},{4,6},{5,1},{6,4},{7,3},{8,10},{9,13},{10,... | collective-permute-start | bytes 786440 | tf_op jit(solution)/shard_map/ppermute | solution.py:121
  73.0 1.3 %collective-permute-start.23 = (bf16[2,36,512]{2,1,0:T(8,128)(2,1)S(1)}, bf16[2,36,512]{2,1,0:T(8,128)(2,1)S(1)}, u32[]{:S(2)}, u32[]{:S(2)}) collective-permute-start(bf16[2,36,512]{2,1,0:T(8,128)(2,1)S(1)} %get-tuple-element.61.refs_2_), channel_id=1, source_target_pairs={{1,0},{0,1},{3,2},{2,3},{5,4},{4,5},{7,6},{6,7},{9,8},{8,9},{11,10... | collective-permute-start | bytes 221192 | tf_op jit(solution)/shard_map/ppermute | solution.py:385
  74.4 11.0 %collective-permute-start.25 = (bf16[8,36,512]{2,1,0:T(8,128)(2,1)S(1)}, bf16[8,36,512]{2,1,0:T(8,128)(2,1)S(1)}, u32[]{:S(2)}, u32[]{:S(2)}) collective-permute-start(bf16[8,36,512]{2,1,0:T(8,128)(2,1)S(1)} %shard_map.150), channel_id=1, source_target_pairs={{2,0},{3,1},{4,2},{5,3},{6,4},{7,5},{8,6},{9,7},{10,8},{11,9},{12,... | collective-permute-start | bytes 884744 | tf_op jit(solution)/shard_map/ppermute | solution.py:385
  76.9 10.1 %collective-permute-start.29 = (bf16[4,16,2048]{2,1,0:T(8,128)(2,1)S(1)}, bf16[4,16,2048]{2,1,0:T(8,128)(2,1)S(1)}, u32[]{:S(2)}, u32[]{:S(2)}) collective-permute-start(bf16[4,16,2048]{2,1,0:T(8,128)(2,1)S(1)} %get-tuple-element.72.refs_13_.refs_2_), channel_id=1, source_target_pairs={{0,1},{1,0},{2,3},{3,2},{4,5},{5,4},{6,7},{7,6},{8,9},{9,8},{10,11... | collective-permute-start | bytes 786440 | tf_op jit(solution)/shard_map/ppermute | solution.py:121
  79.3 8.0 %collective-permute-start.30 = (bf16[4,16,2048]{2,1,0:T(8,128)(2,1)S(1)}, bf16[4,16,2048]{2,1,0:T(8,128)(2,1)S(1)}, u32[]{:S(2)}, u32[]{:S(2)}) collective-permute-start(bf16[4,16,2048]{2,1,0:T(8,128)(2,1)S(1)} %get-tuple-element.73.refs_3_), channel_id=1, source_target_pairs={{0,1},{1,0},{2,3},{3,2},{4,5},{5,4},{6,7},{7,6},{8,9},{9,8},{10,11... | collective-permute-start | bytes 786440 | tf_op jit(solution)/shard_map/ppermute | solution.py:121
  79.4 11.6 %copy-start.5 = (f32[144,256]{1,0:T(8,128)S(1)}, f32[144,256]{1,0:T(8,128)}, u32[]{:S(2)}) copy-start(f32[144,256]{1,0:T(8,128)} %constant.10.clone.refs_13_) | copy-start | bytes 442372
  84.3 3.3 %collective-permute-start.31 = (bf16[4,16,2048]{2,1,0:T(8,128)(2,1)S(1)}, bf16[4,16,2048]{2,1,0:T(8,128)(2,1)S(1)}, u32[]{:S(2)}, u32[]{:S(2)}) collective-permute-start(bf16[4,16,2048]{2,1,0:T(8,128)(2,1)S(1)} %collective-permute-done.27.refs_4_), channel_id=1, source_target_pairs={{0,1},{1,0},{2,3},{3,2},{4,5},{5,4},{6,7},{7,6},{8,9},{9,8},{10,11... | collective-permute-start | bytes 786440 | tf_op jit(solution)/shard_map/ppermute | solution.py:121
  84.9 6.1 %collective-permute-start.32 = (bf16[4,16,2048]{2,1,0:T(8,128)(2,1)S(1)}, bf16[4,16,2048]{2,1,0:T(8,128)(2,1)S(1)}, u32[]{:S(2)}, u32[]{:S(2)}) collective-permute-start(bf16[4,16,2048]{2,1,0:T(8,128)(2,1)S(1)} %collective-permute-done.28.refs_5_), channel_id=1, source_target_pairs={{0,1},{1,0},{2,3},{3,2},{4,5},{5,4},{6,7},{7,6},{8,9},{9,8},{10,11... | collective-permute-start | bytes 786440 | tf_op jit(solution)/shard_map/ppermute | solution.py:121
  85.4 1.3 collective-permute-start.26
  86.7 15.3 %collective-permute-start.35 = (bf16[4,16,4096]{2,1,0:T(8,128)(2,1)S(1)}, bf16[4,16,4096]{2,1,0:T(8,128)(2,1)S(1)}, u32[]{:S(2)}, u32[]{:S(2)}) collective-permute-start(bf16[4,16,4096]{2,1,0:T(8,128)(2,1)S(1)} %get-tuple-element.77.refs_11_.refs_1_), channel_id=1, source_target_pairs={{0,1},{1,0},{2,3},{3,2},{4,5},{5,4},{6,7},{7,6},{8,9},{9,8},{10,11... | collective-permute-start | bytes 1572872 | tf_op jit(solution)/shard_map/ppermute | solution.py:121
  87.0 14.9 %collective-permute-start.36 = (bf16[4,16,4096]{2,1,0:T(8,128)(2,1)S(1)}, bf16[4,16,4096]{2,1,0:T(8,128)(2,1)S(1)}, u32[]{:S(2)}, u32[]{:S(2)}) collective-permute-start(bf16[4,16,4096]{2,1,0:T(8,128)(2,1)S(1)} %get-tuple-element.78.refs_2_), channel_id=1, source_target_pairs={{0,1},{1,0},{2,3},{3,2},{4,5},{5,4},{6,7},{7,6},{8,9},{9,8},{10,11... | collective-permute-start | bytes 1572872 | tf_op jit(solution)/shard_map/ppermute | solution.py:121
  87.3 14.0 %collective-permute-start.33 = (bf16[4,16,4096]{2,1,0:T(8,128)(2,1)S(1)}, bf16[4,16,4096]{2,1,0:T(8,128)(2,1)S(1)}, u32[]{:S(2)}, u32[]{:S(2)}) collective-permute-start(bf16[4,16,4096]{2,1,0:T(8,128)(2,1)S(1)} %get-tuple-element.77.refs_11_.refs_1_), channel_id=1, source_target_pairs={{0,4},{1,3},{2,6},{3,1},{4,0},{5,7},{6,2},{7,5},{8,12},{9,11},{10,... | collective-permute-start | bytes 1572872 | tf_op jit(solution)/shard_map/ppermute | solution.py:121
  87.6 13.8 %collective-permute-start.34 = (bf16[4,16,4096]{2,1,0:T(8,128)(2,1)S(1)}, bf16[4,16,4096]{2,1,0:T(8,128)(2,1)S(1)}, u32[]{:S(2)}, u32[]{:S(2)}) collective-permute-start(bf16[4,16,4096]{2,1,0:T(8,128)(2,1)S(1)} %get-tuple-element.78.refs_2_), channel_id=1, source_target_pairs={{0,2},{1,5},{2,0},{3,7},{4,6},{5,1},{6,4},{7,3},{8,10},{9,13},{10,... | collective-permute-start | bytes 1572872 | tf_op jit(solution)/shard_map/ppermute | solution.py:121
  101.4 2.1 %collective-permute-start.37 = (bf16[4,16,4096]{2,1,0:T(8,128)(2,1)S(1)}, bf16[4,16,4096]{2,1,0:T(8,128)(2,1)S(1)}, u32[]{:S(2)}, u32[]{:S(2)}) collective-permute-start(bf16[4,16,4096]{2,1,0:T(8,128)(2,1)S(1)} %collective-permute-done.33.refs_3_), channel_id=1, source_target_pairs={{0,1},{1,0},{2,3},{3,2},{4,5},{5,4},{6,7},{7,6},{8,9},{9,8},{10,11... | collective-permute-start | bytes 1572872 | tf_op jit(solution)/shard_map/ppermute | solution.py:121
  101.9 2.3 %collective-permute-start.38 = (bf16[4,16,4096]{2,1,0:T(8,128)(2,1)S(1)}, bf16[4,16,4096]{2,1,0:T(8,128)(2,1)S(1)}, u32[]{:S(2)}, u32[]{:S(2)}) collective-permute-start(bf16[4,16,4096]{2,1,0:T(8,128)(2,1)S(1)} %collective-permute-done.34.refs_4_), channel_id=1, source_target_pairs={{0,1},{1,0},{2,3},{3,2},{4,5},{5,4},{6,7},{7,6},{8,9},{9,8},{10,11... | collective-permute-start | bytes 1572872 | tf_op jit(solution)/shard_map/ppermute | solution.py:121
  109.1 1.4 %collective-permute-start.39 = (bf16[2,36,512]{2,1,0:T(8,128)(2,1)S(1)}, bf16[2,36,512]{2,1,0:T(8,128)(2,1)S(1)}, u32[]{:S(2)}, u32[]{:S(2)}) collective-permute-start(bf16[2,36,512]{2,1,0:T(8,128)(2,1)S(1)} %get-tuple-element.81), channel_id=1, source_target_pairs={{1,0},{0,1},{3,2},{2,3},{5,4},{4,5},{7,6},{6,7},{9,8},{8,9},{11,10... | collective-permute-start | bytes 221192 | tf_op jit(solution)/shard_map/ppermute | solution.py:385
  110.4 15.1 %collective-permute-start.40 = (bf16[8,36,512]{2,1,0:T(8,128)(2,1)S(1)}, bf16[8,36,512]{2,1,0:T(8,128)(2,1)S(1)}, u32[]{:S(2)}, u32[]{:S(2)}) collective-permute-start(bf16[8,36,512]{2,1,0:T(8,128)(2,1)S(1)} %shard_map.154), channel_id=1, source_target_pairs={{30,0},{31,1},{0,2},{1,3},{2,4},{3,5},{4,6},{5,7},{6,8},{7,9},{8,1... | collective-permute-start | bytes 884744 | tf_op jit(solution)/shard_map/ppermute | solution.py:385
  124.2 1.3 %collective-permute-start.41 = (bf16[2,36,512]{2,1,0:T(8,128)(2,1)S(1)}, bf16[2,36,512]{2,1,0:T(8,128)(2,1)S(1)}, u32[]{:S(2)}, u32[]{:S(2)}) collective-permute-start(bf16[2,36,512]{2,1,0:T(8,128)(2,1)S(1)} %get-tuple-element.88), channel_id=1, source_target_pairs={{1,0},{0,1},{3,2},{2,3},{5,4},{4,5},{7,6},{6,7},{9,8},{8,9},{11,10... | collective-permute-start | bytes 221192 | tf_op jit(solution)/shard_map/ppermute | solution.py:385

commit v17 on v16

--- a/solution.py
+++ b/solution.py
@@ -456,22 +456,18 @@
         last_beside = send(last_own, beside)
         (column,) = join([[pair, across_z(pair, 1)]], (), (feed_pair, last_beside))
         received = [send(column, way) for way in (beside, across, corner)]
-        sent = [tied(column, received[0])] + received
+        last_other = across_z(tied(last_own, column), 2)
+        sent = [tied(column, (received[0], last_other))] + received
         pieces = "columns", [column] + received + [send(part, swap) for part in sent]
-        last_other = across_z(tied(last_own, column), 2)
         last_across = send(tied(last_other, received[0]), across)
-        last_four, final_four = join(
-            [[last_own, last_beside, last_other, last_across]], widths=widths
-        )
         (feed_column,) = join([[feed_pair, across_z(feed_pair, 1)]])
         received = [send(feed_column, way) for way in (beside, across)]
+        middle_0 = attention(0, [windows], (0,), pieces, (feed_column,))
+        first, second = tied((received[0][:2], received[1][2:]), (middle_0, last_across))
+        corners = [send(first, across), send(second, beside)]
+        (last_four,) = join([[last_own, last_beside, last_other, last_across]], (), (middle_0,))
+        middle_1 = attention(0, [windows], (1,), pieces, (middle_0, last_four))
         last_other = across_z(last_four, 1)
-        middle_0 = attention(0, [windows], (0,), pieces, (feed_column,))
-        first, second = tied((received[0][:2], received[1][2:]), middle_0)
-        corners = [send(first, across), send(second, beside)]
-        last_columns = list(halves(last_four, last_other, widths[:1], (middle_0,)))
-        final_other = across_z(tied(final_four, middle_0), 1)
-        middle_1 = attention(0, [windows], (1,), pieces, (middle_0, last_columns[0]))
         swapped = [send(part, swap) for part in [feed_column] + tied(received, middle_0)]
         received += join([tied(corners, (middle_1, *swapped))])
         feed_pieces = "columns", [feed_column] + received + swapped + [send(received[2], swap)]
@@ -491,11 +487,10 @@
     ahead = shift_from(ahead, 1, 0)
     after = (below_0,)
     if relay:
-        last_received = [
-            send(part, way) for part, way in zip(tied(last_columns, middle_1), (across, beside))
-        ]
-        final_columns = list(halves(final_four, final_other, widths[1:], (low_0,)))
-        after += (final_columns[0],)
+        columns = halves(last_four, last_other, widths, (low_0,))
+        last_columns, final_columns = list(columns[:2]), list(columns[2:])
+        last_received = [send(part, way) for part, way in zip(last_columns, (across, beside))]
+        after += (last_columns[0],)
     left_1, right_1, low_1 = forward(0, middle_1, 0, feed_pieces, low_edge, after)
     below_1 = shift_from(tied(low_1, ahead), 0, 1)
     if relay:

time: 128 us -> 129 us (level)
  waiting for transfers between devices: 29.5 us -> 36.2 us
  starting transfers between devices: 43.1 us -> 37 us
    ppermute x36 -> x35, starting transfers between devices: 38 us -> 30.7 us  [send(): return lax.ppermute(block, ('lon', 'lat'), pairs)]
    ppermute x36 -> x35, waiting for transfers between devices: 24.4 us -> 29.9 us  [send(): return lax.ppermute(block, ('lon', 'lat'), pairs)]
  transfers between devices with their start and end apart: 42 -> 41, of which waited for: 16 -> 15; matrix products, arithmetic and copies ran while one was open for 1% -> 1% of each run, Pallas kernels for 33% -> 33%
where the time goes in v17:
time: 129 us
  Pallas kernels  47.5 us (37%)
  starting transfers between devices  37 us (29%)
  waiting for transfers between devices  36.2 us (28%)
  local copies, waits for them, and re-layouts  7.64 us (6%)
    ppermute x35, starting transfers between devices, send(): return lax.ppermute(block, ('lon', 'lat'), pairs)  30.7 us
    ppermute x35, waiting for transfers between devices, send(): return lax.ppermute(block, ('lon', 'lat'), pairs)  29.9 us
    pallas_call x4, Pallas kernels, attend(): pl.pallas_call(functools.partial(attend_kernel, shifted, row_windows, kin...  27.6 us
    pallas_call x4, Pallas kernels, feed(): pl.pallas_call(functools.partial(feed_kernel, kind, len(pieces), hidden_s...  19.3 us
    ppermute x6, starting transfers between devices, shift_from(): return lax.ppermute(block, ('lon', 'lat'), pairs)  6.33 us
    ppermute x6, waiting for transfers between devices, shift_from(): return lax.ppermute(block, ('lon', 'lat'), pairs)  6.29 us
    unnamed x20, local copies, waits for them, and re-layouts  3.7 us
  transfers between devices with their start and end apart: 41, of which 15 were waited for; matrix products, arithmetic and copies ran while one was open for 1% of the time, Pallas kernels for 33%

profile of v17, /device:TPU:0, one launch (start us, length us, event | category | flops | bytes accessed | tf_op | source)
XLA Modules:
  0.0 128.7 jit_solution(1935246529729571186)
XLA Ops:
  0.0 0.9 copy-done.2
  0.9 0.8 copy-done.3
  1.8 4.0 %collective-permute-start = (bf16[1,16,2048]{2,1,0:T(8,128)(2,1)S(1)}, bf16[1,16,2048]{2,1,0:T(8,128)(2,1)S(1)}, u32[]{:S(2)}, u32[]{:S(2)}) collective-permute-start(bf16[1,16,2048]{2,1,0:T(8,128)(2,1)S(1)} %shard_map.136.refs_0_.refs_6_), channel_id=1, source_target_pairs={{0,16},{1,17},{2,18},{3,19},{4,20},{5,21},{6,22},{7,23},{8,24},{9,... | collective-permute-start | bytes 196616 | tf_op jit(solution)/shard_map/ppermute | solution.py:121
  5.8 0.9 copy-done
  6.8 0.9 copy-done.1
  7.7 1.6 %collective-permute-start.3 = (bf16[1,16,6144]{2,1,0:T(8,128)(2,1)S(1)}, bf16[1,16,6144]{2,1,0:T(8,128)(2,1)S(1)}, u32[]{:S(2)}, u32[]{:S(2)}) collective-permute-start(bf16[1,16,6144]{2,1,0:T(8,128)(2,1)S(1)} %get-tuple-element.44.refs_0_), channel_id=1, source_target_pairs={{0,2},{1,5},{2,0},{3,7},{4,6},{5,1},{6,4},{7,3},{8,10},{9,13},{10,... | collective-permute-start | bytes 589832 | tf_op jit(solution)/shard_map/ppermute | solution.py:121
  9.3 0.3 collective-permute-start.2
  9.6 0.8 copy.26
  10.5 0.5 reshape.15.refs_2_.refs_0_
  11.0 1.6 %collective-permute-start.1 = (bf16[2,16,2048]{2,1,0:T(8,128)(2,1)S(1)}, bf16[2,16,2048]{2,1,0:T(8,128)(2,1)S(1)}, u32[]{:S(2)}, u32[]{:S(2)}) collective-permute-start(bf16[2,16,2048]{2,1,0:T(8,128)(2,1)S(1)} %shard_map.137.refs_0_), channel_id=1, source_target_pairs={{0,8},{1,9},{2,10},{3,11},{4,12},{5,13},{6,14},{7,15},{8,0},{9,1},... | collective-permute-start | bytes 393224 | tf_op jit(solution)/shard_map/ppermute | solution.py:121
  12.7 5.0 %collective-permute-done.2.refs_1_ = bf16[1,16,4096]{2,1,0:T(8,128)(2,1)S(1)} collective-permute-done((bf16[1,16,4096]{2,1,0:T(8,128)(2,1)S(1)}, bf16[1,16,4096]{2,1,0:T(8,128)(2,1)S(1)}, u32[]{:S(2)}, u32[]{:S(2)}) %collective-permute-start.2) | collective-permute-done | bytes 131104 | tf_op jit(solution)/shard_map/ppermute | solution.py:121
  17.8 1.6 %collective-permute-start.4 = (bf16[4,16,2048]{2,1,0:T(8,128)(2,1)S(1)}, bf16[4,16,2048]{2,1,0:T(8,128)(2,1)S(1)}, u32[]{:S(2)}, u32[]{:S(2)}) collective-permute-start(bf16[4,16,2048]{2,1,0:T(8,128)(2,1)S(1)} %shard_map.140.refs_1_), channel_id=1, source_target_pairs={{0,2},{1,5},{2,0},{3,7},{4,6},{5,1},{6,4},{7,3},{8,10},{9,13},{10,... | collective-permute-start | bytes 786440 | tf_op jit(solution)/shard_map/ppermute | solution.py:121
  19.4 0.9 collective-permute-start.6
  20.3 1.1 collective-permute-start.5
  21.3 1.9 %collective-permute-start.7 = (bf16[1,16,6144]{2,1,0:T(8,128)(2,1)S(1)}, bf16[1,16,6144]{2,1,0:T(8,128)(2,1)S(1)}, u32[]{:S(2)}, u32[]{:S(2)}) collective-permute-start(bf16[1,16,6144]{2,1,0:T(8,128)(2,1)S(1)} %get-tuple-element.44.refs_0_), channel_id=1, source_target_pairs={{0,16},{1,17},{2,18},{3,19},{4,20},{5,21},{6,22},{7,23},{8,24},{9,... | collective-permute-start | bytes 589832 | tf_op jit(solution)/shard_map/ppermute | solution.py:121
  23.2 0.1 multiply_reduce_fusion
  23.3 2.5 %collective-permute-start.12 = (bf16[2,16,4096]{2,1,0:T(8,128)(2,1)S(1)}, bf16[2,16,4096]{2,1,0:T(8,128)(2,1)S(1)}, u32[]{:S(2)}, u32[]{:S(2)}) collective-permute-start(bf16[2,16,4096]{2,1,0:T(8,128)(2,1)S(1)} %shard_map.139.refs_2_.refs_0_), channel_id=1, source_target_pairs={{0,8},{1,9},{2,10},{3,11},{4,12},{5,13},{6,14},{7,15},{8,0},{9,1},... | collective-permute-start | bytes 786440 | tf_op jit(solution)/shard_map/ppermute | solution.py:121
  25.9 5.9 %collective-permute-done.7.refs_2_ = bf16[1,16,6144]{2,1,0:T(8,128)(2,1)S(1)} collective-permute-done((bf16[1,16,6144]{2,1,0:T(8,128)(2,1)S(1)}, bf16[1,16,6144]{2,1,0:T(8,128)(2,1)S(1)}, u32[]{:S(2)}, u32[]{:S(2)}) %collective-permute-start.7) | collective-permute-done | bytes 196640 | tf_op jit(solution)/shard_map/ppermute | solution.py:121
  31.7 0.5 collective-permute-start.9
  32.3 0.5 collective-permute-start.10
  32.8 0.6 collective-permute-done.12.refs_1_
  33.5 0.5 collective-permute-done.11.refs_8_
  34.0 1.0 collective-permute-start.14
  35.0 1.8 %collective-permute-start.13 = (bf16[4,16,4096]{2,1,0:T(8,128)(2,1)S(1)}, bf16[4,16,4096]{2,1,0:T(8,128)(2,1)S(1)}, u32[]{:S(2)}, u32[]{:S(2)}) collective-permute-start(bf16[4,16,4096]{2,1,0:T(8,128)(2,1)S(1)} %shard_map.141.refs_12_.refs_1_), channel_id=1, source_target_pairs={{0,2},{1,5},{2,0},{3,7},{4,6},{5,1},{6,4},{7,3},{8,10},{9,13},{10,... | collective-permute-start | bytes 1572872 | tf_op jit(solution)/shard_map/ppermute | solution.py:121
  36.8 1.0 collective-permute-start.15
  37.8 6.9 %shard_map.142.refs_4_.refs_12_.refs_0_ = bf16[4,144,512]{2,1,0:T(8,128)(2,1)S(1)} custom-call(bf16[8,144,512]{2,1,0:T(8,128)(2,1)S(1)} %reshape.15.refs_2_.refs_0_, bf16[4,16,2048]{2,1,0:T(8,128)(2,1)S(1)} %shard_map.140.refs_1_, bf16[4,16,2048]{2,1,0:T(8,128)(2,1)S(1)} %collective-permute-done.4.refs_2_, ...), custom_call_target="tpu_custom_call" | custom-call | flops 8000000000 | bytes 6000000 | tf_op jit(solution)/shard_map/pallas_call | solution.py:300
  44.7 6.2 %collective-permute-done.15.refs_3_ = bf16[1,16,6144]{2,1,0:T(8,128)(2,1)S(1)} collective-permute-done((bf16[1,16,6144]{2,1,0:T(8,128)(2,1)S(1)}, bf16[1,16,6144]{2,1,0:T(8,128)(2,1)S(1)}, u32[]{:S(2)}, u32[]{:S(2)}) %collective-permute-start.15) | collective-permute-done | bytes 196640 | tf_op jit(solution)/shard_map/ppermute | solution.py:121
  51.0 1.0 collective-permute-start.23
  52.0 1.2 collective-permute-start.16
  53.3 1.2 collective-permute-start.17
  54.5 0.5 collective-permute-start.20
  55.0 6.9 %shard_map.144.refs_0_ = bf16[4,144,512]{2,1,0:T(8,128)(2,1)S(1)} custom-call(bf16[8,144,512]{2,1,0:T(8,128)(2,1)S(1)} %reshape.15.refs_2_.refs_0_, bf16[4,16,2048]{2,1,0:T(8,128)(2,1)S(1)} %shard_map.140.refs_1_, bf16[4,16,2048]{2,1,0:T(8,128)(2,1)S(1)} %collective-permute-done.4.refs_2_, bf16[4,16,2048]{2,1,0:T(8,128)(2,1)S(1)} %collective-permute-done.5.refs_3_, ...), custom_call_target="tpu_custom_call" | custom-call | flops 8000000000 | bytes 6000000 | tf_op jit(solution)/shard_map/pallas_call | solution.py:300
  62.0 1.9 %collective-permute-done.21.refs_8_ = bf16[4,16,4096]{2,1,0:T(8,128)(2,1)S(1)} collective-permute-done((bf16[4,16,4096]{2,1,0:T(8,128)(2,1)S(1)}, bf16[4,16,4096]{2,1,0:T(8,128)(2,1)S(1)}, u32[]{:S(2)}, u32[]{:S(2)}) %collective-permute-start.21) | collective-permute-done | bytes 524320 | tf_op jit(solution)/shard_map/ppermute | solution.py:121
  63.9 4.8 %shard_map.146 = (bf16[8,36,512]{2,1,0:T(8,128)(2,1)S(1)}, bf16[8,36,512]{2,1,0:T(8,128)(2,1)S(1)}, bf16[2,36,512]{2,1,0:T(8,128)(2,1)S(1)}) custom-call(bf16[4,144,512]{2,1,0:T(8,128)(2,1)S(1)} %shard_map.142.refs_4_.refs_12_.refs_0_, bf16[4,16,4096]{2,1,0:T(8,128)(2,1)S(1)} %shard_map.141.refs_12_.refs_1_, ...), custom_call_target="tpu_custom_call" | custom-call | flops 1000000 | bytes 100000 | tf_op jit(solution)/shard_map/pallas_call | solution.py:358
  68.8 1.0 collective-permute-done.23.refs_1_
  69.8 0.1 shard_map.147
  69.9 1.8 %collective-permute-start.27 = (bf16[4,16,2048]{2,1,0:T(8,128)(2,1)S(1)}, bf16[4,16,2048]{2,1,0:T(8,128)(2,1)S(1)}, u32[]{:S(2)}, u32[]{:S(2)}) collective-permute-start(bf16[4,16,2048]{2,1,0:T(8,128)(2,1)S(1)} %get-tuple-element.62.refs_3_), channel_id=1, source_target_pairs={{0,2},{1,5},{2,0},{3,7},{4,6},{5,1},{6,4},{7,3},{8,10},{9,13},{10,... | collective-permute-start | bytes 786440 | tf_op jit(solution)/shard_map/ppermute | solution.py:121
  71.7 1.0 collective-permute-start.26
  72.7 1.3 collective-permute-done.22.refs_10_.refs_1_.refs_3_
  74.1 4.8 %collective-permute-start.24 = (bf16[8,36,512]{2,1,0:T(8,128)(2,1)S(1)}, bf16[8,36,512]{2,1,0:T(8,128)(2,1)S(1)}, u32[]{:S(2)}, u32[]{:S(2)}) collective-permute-start(bf16[8,36,512]{2,1,0:T(8,128)(2,1)S(1)} %shard_map.149), channel_id=1, source_target_pairs={{2,0},{3,1},{4,2},{5,3},{6,4},{7,5},{8,6},{9,7},{10,8},{11,9},{12,... | collective-permute-start | bytes 884744 | tf_op jit(solution)/shard_map/ppermute | solution.py:385
  78.8 0.5 collective-permute-start.28
  79.3 4.8 %shard_map.148 = (bf16[8,36,512]{2,1,0:T(8,128)(2,1)S(1)}, bf16[8,36,512]{2,1,0:T(8,128)(2,1)S(1)}, bf16[2,36,512]{2,1,0:T(8,128)(2,1)S(1)}) custom-call(bf16[4,144,512]{2,1,0:T(8,128)(2,1)S(1)} %shard_map.144.refs_0_, bf16[4,16,4096]{2,1,0:T(8,128)(2,1)S(1)} %shard_map.141.refs_12_.refs_1_, bf16[4,16,4096]{2,1,0:T(8,128)(2,1)S(1)} %collective-permute-done.13.refs_2_, ...), custom_call_target="tpu_custom_call" | custom-call | flops 1000000 | bytes 100000 | tf_op jit(solution)/shard_map/pallas_call | solution.py:358
  84.3 0.5 collective-permute-start.31
  84.8 1.3 %collective-permute-done.24.refs_1_ = bf16[8,36,512]{2,1,0:T(8,128)(2,1)S(1)} collective-permute-done((bf16[8,36,512]{2,1,0:T(8,128)(2,1)S(1)}, bf16[8,36,512]{2,1,0:T(8,128)(2,1)S(1)}, u32[]{:S(2)}, u32[]{:S(2)}) %collective-permute-start.24) | collective-permute-done | bytes 294944 | tf_op jit(solution)/shard_map/ppermute | solution.py:385
  86.1 1.3 collective-permute-done.25.refs_4_
  87.4 0.2 collective-permute-start.34
  87.6 0.4 collective-permute-start.35
  88.1 1.2 collective-permute-start.33
  89.3 6.9 %shard_map.151.refs_0_ = bf16[4,144,512]{2,1,0:T(8,128)(2,1)S(1)} custom-call(bf16[8,36,512]{2,1,0:T(8,128)(2,1)S(1)} %get-tuple-element.61.refs_0_, bf16[8,36,512]{2,1,0:T(8,128)(2,1)S(1)} %collective-permute-done.24.refs_1_, bf16[4,16,2048]{2,1,0:T(8,128)(2,1)S(1)} %get-tuple-element.55.refs_11_.refs_2_, ...), custom_call_target="tpu_custom_call" | custom-call | flops 8000000000 | bytes 6000000 | tf_op jit(solution)/shard_map/pallas_call | solution.py:300
  96.2 6.6 %collective-permute-done.32.refs_3_ = bf16[4,16,4096]{2,1,0:T(8,128)(2,1)S(1)} collective-permute-done((bf16[4,16,4096]{2,1,0:T(8,128)(2,1)S(1)}, bf16[4,16,4096]{2,1,0:T(8,128)(2,1)S(1)}, u32[]{:S(2)}, u32[]{:S(2)}) %collective-permute-start.32) | collective-permute-done | bytes 524320 | tf_op jit(solution)/shard_map/ppermute | solution.py:121
  102.8 0.1 collective-permute-start.36
  102.9 0.4 collective-permute-start.37
  103.3 1.4 %collective-permute-done.36.refs_7_ = bf16[4,16,4096]{2,1,0:T(8,128)(2,1)S(1)} collective-permute-done((bf16[4,16,4096]{2,1,0:T(8,128)(2,1)S(1)}, bf16[4,16,4096]{2,1,0:T(8,128)(2,1)S(1)}, u32[]{:S(2)}, u32[]{:S(2)}) %collective-permute-start.36) | collective-permute-done | bytes 524320 | tf_op jit(solution)/shard_map/ppermute | solution.py:121
  104.7 0.7 collective-permute-done.37.refs_8_
  105.5 4.8 %shard_map.152 = (bf16[8,36,512]{2,1,0:T(8,128)(2,1)S(1)}, bf16[8,36,512]{2,1,0:T(8,128)(2,1)S(1)}, bf16[2,36,512]{2,1,0:T(8,128)(2,1)S(1)}) custom-call(bf16[4,144,512]{2,1,0:T(8,128)(2,1)S(1)} %shard_map.151.refs_0_, bf16[4,16,4096]{2,1,0:T(8,128)(2,1)S(1)} %get-tuple-element.67.refs_1_, bf16[4,16,4096]{2,1,0:T(8,128)(2,1)S(1)} %get-tuple-element.68.refs_2_, ...), custom_call_target="tpu_custom_call" | custom-call | flops 1000000 | bytes 100000 | tf_op jit(solution)/shard_map/pallas_call | solution.py:358
  110.3 0.2 collective-permute-start.38
  110.5 1.1 collective-permute-done.38.refs_0_.refs_14_.refs_5_
  111.6 1.3 collective-permute-start.39
  112.9 6.9 %shard_map.154.refs_0_ = bf16[4,144,512]{2,1,0:T(8,128)(2,1)S(1)} custom-call(bf16[8,36,512]{2,1,0:T(8,128)(2,1)S(1)} %get-tuple-element.73.refs_0_, bf16[8,36,512]{2,1,0:T(8,128)(2,1)S(1)} %get-tuple-element.74.refs_1_, bf16[4,16,2048]{2,1,0:T(8,128)(2,1)S(1)} %get-tuple-element.55.refs_11_.refs_2_, bf16[4,16,2048]{2,1,0:T(8,128)(2,1)S(1)} %get-tuple-element.62.refs_3_, ...), custom_call_target="tpu_custom_call" | custom-call | flops 8000000000 | bytes 6000000 | tf_op jit(solution)/shard_map/pallas_call | solution.py:300
  119.8 4.9 %shard_map.155 = (bf16[8,36,512]{2,1,0:T(8,128)(2,1)S(1)}, bf16[8,36,512]{2,1,0:T(8,128)(2,1)S(1)}, bf16[2,36,512]{2,1,0:T(8,128)(2,1)S(1)}) custom-call(bf16[4,144,512]{2,1,0:T(8,128)(2,1)S(1)} %shard_map.154.refs_0_, bf16[4,16,4096]{2,1,0:T(8,128)(2,1)S(1)} %get-tuple-element.67.refs_1_, bf16[4,16,4096]{2,1,0:T(8,128)(2,1)S(1)} %get-tuple-element.68.refs_2_, ...), custom_call_target="tpu_custom_call" | custom-call | flops 1000000 | bytes 100000 | tf_op jit(solution)/shard_map/pallas_call | solution.py:358
  124.8 1.3 collective-permute-done.40.refs_4_
  126.1 0.1 shard_map.156
  126.2 0.4 copy.23
  126.5 2.2 %copy.24 = bf16[4,6,8,3,2,512]{5,4,3,2,1,0:T(2,128)(2,1)} copy(bf16[4,6,8,3,2,512]{5,2,0,4,3,1:T(8,128)(2,1)S(1)} %bitcast.16) | data formatting | bytes 2359296 | tf_op jit(solution)/shard_map/transpose | solution.py:423
  (68 shorter events, 0.8 us)
Async XLA Ops:
  0.0 0.9 copy-start.2
  0.9 0.8 copy-start.3
  1.8 9.2 %collective-permute-start = (bf16[1,16,2048]{2,1,0:T(8,128)(2,1)S(1)}, bf16[1,16,2048]{2,1,0:T(8,128)(2,1)S(1)}, u32[]{:S(2)}, u32[]{:S(2)}) collective-permute-start(bf16[1,16,2048]{2,1,0:T(8,128)(2,1)S(1)} %shard_map.136.refs_0_.refs_6_), channel_id=1, source_target_pairs={{0,16},{1,17},{2,18},{3,19},{4,20},{5,21},{6,22},{7,23},{8,24},{9,... | collective-permute-start | bytes 196616 | tf_op jit(solution)/shard_map/ppermute | solution.py:121
  5.8 0.9 copy-start
  6.8 0.9 copy-start.1
  7.7 1.9 %copy-start.6 = (bf16[24,24,2,512]{3,2,1,0:T(2,128)(2,1)S(1)}, bf16[24,24,2,512]{3,2,1,0:T(2,128)(2,1)}, u32[]{:S(2)}) copy-start(bf16[24,24,2,512]{3,2,1,0:T(2,128)(2,1)} %param.14) | copy-start | bytes 3538948
  7.7 10.0 %collective-permute-start.3 = (bf16[1,16,6144]{2,1,0:T(8,128)(2,1)S(1)}, bf16[1,16,6144]{2,1,0:T(8,128)(2,1)S(1)}, u32[]{:S(2)}, u32[]{:S(2)}) collective-permute-start(bf16[1,16,6144]{2,1,0:T(8,128)(2,1)S(1)} %get-tuple-element.44.refs_0_), channel_id=1, source_target_pairs={{0,2},{1,5},{2,0},{3,7},{4,6},{5,1},{6,4},{7,3},{8,10},{9,13},{10,... | collective-permute-start | bytes 589832 | tf_op jit(solution)/shard_map/ppermute | solution.py:121
  9.3 8.4 %collective-permute-start.2 = (bf16[1,16,4096]{2,1,0:T(8,128)(2,1)S(1)}, bf16[1,16,4096]{2,1,0:T(8,128)(2,1)S(1)}, u32[]{:S(2)}, u32[]{:S(2)}) collective-permute-start(bf16[1,16,4096]{2,1,0:T(8,128)(2,1)S(1)} %get-tuple-element.42.refs_0_), channel_id=1, source_target_pairs={{0,16},{1,17},{2,18},{3,19},{4,20},{5,21},{6,22},{7,23},{8,24},{9,... | collective-permute-start | bytes 393224 | tf_op jit(solution)/shard_map/ppermute | solution.py:121
  11.0 12.3 %copy-start.7 = (f32[16,512]{1,0:T(8,128)S(1)}, f32[16,512]{1,0:T(8,128)}, u32[]{:S(2)}) copy-start(f32[16,512]{1,0:T(8,128)} %constant.8.clone) | copy-start | bytes 98308
  11.0 12.3 %copy-start.9 = (f32[2,16]{1,0:T(2,128)S(1)}, f32[2,16]{1,0:T(2,128)}, u32[]{:S(2)}) copy-start(f32[2,16]{1,0:T(2,128)} %param.20) | copy-start | bytes 388
  11.0 21.8 %copy-start.8 = (f32[2,2,512]{2,1,0:T(2,128)S(1)}, f32[2,2,512]{2,1,0:T(2,128)}, u32[]{:S(2)}) copy-start(f32[2,2,512]{2,1,0:T(2,128)} %param.19) | copy-start | bytes 24580
  11.0 6.7 %collective-permute-start.1 = (bf16[2,16,2048]{2,1,0:T(8,128)(2,1)S(1)}, bf16[2,16,2048]{2,1,0:T(8,128)(2,1)S(1)}, u32[]{:S(2)}, u32[]{:S(2)}) collective-permute-start(bf16[2,16,2048]{2,1,0:T(8,128)(2,1)S(1)} %shard_map.137.refs_0_), channel_id=1, source_target_pairs={{0,8},{1,9},{2,10},{3,11},{4,12},{5,13},{6,14},{7,15},{8,0},{9,1},... | collective-permute-start | bytes 393224 | tf_op jit(solution)/shard_map/ppermute | solution.py:121
  17.7 20.1 %copy-start.4 = (bf16[640,256]{1,0:T(8,128)(2,1)S(1)}, bf16[640,256]{1,0:T(8,128)(2,1)}, u32[]{:S(2)}) copy-start(bf16[640,256]{1,0:T(8,128)(2,1)} %constant.9.clone.refs_11_.refs_12_) | copy-start | bytes 983044
  17.8 13.9 %collective-permute-start.4 = (bf16[4,16,2048]{2,1,0:T(8,128)(2,1)S(1)}, bf16[4,16,2048]{2,1,0:T(8,128)(2,1)S(1)}, u32[]{:S(2)}, u32[]{:S(2)}) collective-permute-start(bf16[4,16,2048]{2,1,0:T(8,128)(2,1)S(1)} %shard_map.140.refs_1_), channel_id=1, source_target_pairs={{0,2},{1,5},{2,0},{3,7},{4,6},{5,1},{6,4},{7,3},{8,10},{9,13},{10,... | collective-permute-start | bytes 786440 | tf_op jit(solution)/shard_map/ppermute | solution.py:121
  19.4 12.9 %collective-permute-start.6 = (bf16[4,16,2048]{2,1,0:T(8,128)(2,1)S(1)}, bf16[4,16,2048]{2,1,0:T(8,128)(2,1)S(1)}, u32[]{:S(2)}, u32[]{:S(2)}) collective-permute-start(bf16[4,16,2048]{2,1,0:T(8,128)(2,1)S(1)} %shard_map.140.refs_1_), channel_id=1, source_target_pairs={{0,6},{1,7},{2,4},{3,5},{4,2},{5,3},{6,0},{7,1},{8,14},{9,15},{10,... | collective-permute-start | bytes 786440 | tf_op jit(solution)/shard_map/ppermute | solution.py:121
  20.3 12.0 %collective-permute-start.5 = (bf16[4,16,2048]{2,1,0:T(8,128)(2,1)S(1)}, bf16[4,16,2048]{2,1,0:T(8,128)(2,1)S(1)}, u32[]{:S(2)}, u32[]{:S(2)}) collective-permute-start(bf16[4,16,2048]{2,1,0:T(8,128)(2,1)S(1)} %shard_map.140.refs_1_), channel_id=1, source_target_pairs={{0,4},{1,3},{2,6},{3,1},{4,0},{5,7},{6,2},{7,5},{8,12},{9,11},{10,... | collective-permute-start | bytes 786440 | tf_op jit(solution)/shard_map/ppermute | solution.py:121
  21.3 10.4 %collective-permute-start.7 = (bf16[1,16,6144]{2,1,0:T(8,128)(2,1)S(1)}, bf16[1,16,6144]{2,1,0:T(8,128)(2,1)S(1)}, u32[]{:S(2)}, u32[]{:S(2)}) collective-permute-start(bf16[1,16,6144]{2,1,0:T(8,128)(2,1)S(1)} %get-tuple-element.44.refs_0_), channel_id=1, source_target_pairs={{0,16},{1,17},{2,18},{3,19},{4,20},{5,21},{6,22},{7,23},{8,24},{9,... | collective-permute-start | bytes 589832 | tf_op jit(solution)/shard_map/ppermute | solution.py:121
  23.3 10.1 %collective-permute-start.12 = (bf16[2,16,4096]{2,1,0:T(8,128)(2,1)S(1)}, bf16[2,16,4096]{2,1,0:T(8,128)(2,1)S(1)}, u32[]{:S(2)}, u32[]{:S(2)}) collective-permute-start(bf16[2,16,4096]{2,1,0:T(8,128)(2,1)S(1)} %shard_map.139.refs_2_.refs_0_), channel_id=1, source_target_pairs={{0,8},{1,9},{2,10},{3,11},{4,12},{5,13},{6,14},{7,15},{8,0},{9,1},... | collective-permute-start | bytes 786440 | tf_op jit(solution)/shard_map/ppermute | solution.py:121
  31.7 5.1 %collective-permute-start.8 = (bf16[4,16,2048]{2,1,0:T(8,128)(2,1)S(1)}, bf16[4,16,2048]{2,1,0:T(8,128)(2,1)S(1)}, u32[]{:S(2)}, u32[]{:S(2)}) collective-permute-start(bf16[4,16,2048]{2,1,0:T(8,128)(2,1)S(1)} %shard_map.140.refs_1_), channel_id=1, source_target_pairs={{0,1},{1,0},{2,3},{3,2},{4,5},{5,4},{6,7},{7,6},{8,9},{9,8},{10,11... | collective-permute-start | bytes 786440 | tf_op jit(solution)/shard_map/ppermute | solution.py:121
  31.7 6.1 %collective-permute-start.9 = (bf16[4,16,2048]{2,1,0:T(8,128)(2,1)S(1)}, bf16[4,16,2048]{2,1,0:T(8,128)(2,1)S(1)}, u32[]{:S(2)}, u32[]{:S(2)}) collective-permute-start(bf16[4,16,2048]{2,1,0:T(8,128)(2,1)S(1)} %collective-permute-done.4.refs_2_), channel_id=1, source_target_pairs={{0,1},{1,0},{2,3},{3,2},{4,5},{5,4},{6,7},{7,6},{8,9},{9,8},{10,11... | collective-permute-start | bytes 786440 | tf_op jit(solution)/shard_map/ppermute | solution.py:121
  32.2 1.8 %collective-permute-start.11 = (bf16[4,16,2048]{2,1,0:T(8,128)(2,1)S(1)}, bf16[4,16,2048]{2,1,0:T(8,128)(2,1)S(1)}, u32[]{:S(2)}, u32[]{:S(2)}) collective-permute-start(bf16[4,16,2048]{2,1,0:T(8,128)(2,1)S(1)} %collective-permute-done.6.refs_4_), channel_id=1, source_target_pairs={{0,1},{1,0},{2,3},{3,2},{4,5},{5,4},{6,7},{7,6},{8,9},{9,8},{10,11... | collective-permute-start | bytes 786440 | tf_op jit(solution)/shard_map/ppermute | solution.py:121
  32.3 2.8 %collective-permute-start.10 = (bf16[4,16,2048]{2,1,0:T(8,128)(2,1)S(1)}, bf16[4,16,2048]{2,1,0:T(8,128)(2,1)S(1)}, u32[]{:S(2)}, u32[]{:S(2)}) collective-permute-start(bf16[4,16,2048]{2,1,0:T(8,128)(2,1)S(1)} %collective-permute-done.5.refs_3_), channel_id=1, source_target_pairs={{0,1},{1,0},{2,3},{3,2},{4,5},{5,4},{6,7},{7,6},{8,9},{9,8},{10,11... | collective-permute-start | bytes 786440 | tf_op jit(solution)/shard_map/ppermute | solution.py:121
  33.4 21.1 %collective-permute-start.18 = (bf16[4,16,4096]{2,1,0:T(8,128)(2,1)S(1)}, bf16[4,16,4096]{2,1,0:T(8,128)(2,1)S(1)}, u32[]{:S(2)}, u32[]{:S(2)}) collective-permute-start(bf16[4,16,4096]{2,1,0:T(8,128)(2,1)S(1)} %shard_map.141.refs_12_.refs_1_), channel_id=1, source_target_pairs={{0,1},{1,0},{2,3},{3,2},{4,5},{5,4},{6,7},{7,6},{8,9},{9,8},{10,11... | collective-permute-start | bytes 1572872 | tf_op jit(solution)/shard_map/ppermute | solution.py:121
  34.0 18.0 %collective-permute-start.14 = (bf16[4,16,4096]{2,1,0:T(8,128)(2,1)S(1)}, bf16[4,16,4096]{2,1,0:T(8,128)(2,1)S(1)}, u32[]{:S(2)}, u32[]{:S(2)}) collective-permute-start(bf16[4,16,4096]{2,1,0:T(8,128)(2,1)S(1)} %shard_map.141.refs_12_.refs_1_), channel_id=1, source_target_pairs={{0,4},{1,3},{2,6},{3,1},{4,0},{5,7},{6,2},{7,5},{8,12},{9,11},{10,... | collective-permute-start | bytes 1572872 | tf_op jit(solution)/shard_map/ppermute | solution.py:121
  35.0 17.0 %collective-permute-start.13 = (bf16[4,16,4096]{2,1,0:T(8,128)(2,1)S(1)}, bf16[4,16,4096]{2,1,0:T(8,128)(2,1)S(1)}, u32[]{:S(2)}, u32[]{:S(2)}) collective-permute-start(bf16[4,16,4096]{2,1,0:T(8,128)(2,1)S(1)} %shard_map.141.refs_12_.refs_1_), channel_id=1, source_target_pairs={{0,2},{1,5},{2,0},{3,7},{4,6},{5,1},{6,4},{7,3},{8,10},{9,13},{10,... | collective-permute-start | bytes 1572872 | tf_op jit(solution)/shard_map/ppermute | solution.py:121
  36.8 14.1 %collective-permute-start.15 = (bf16[1,16,6144]{2,1,0:T(8,128)(2,1)S(1)}, bf16[1,16,6144]{2,1,0:T(8,128)(2,1)S(1)}, u32[]{:S(2)}, u32[]{:S(2)}) collective-permute-start(bf16[1,16,6144]{2,1,0:T(8,128)(2,1)S(1)} %collective-permute-done.7.refs_2_), channel_id=1, source_target_pairs={{0,4},{1,3},{2,6},{3,1},{4,0},{5,7},{6,2},{7,5},{8,12},{9,11},{10,... | collective-permute-start | bytes 589832 | tf_op jit(solution)/shard_map/ppermute | solution.py:121
  51.0 18.8 %collective-permute-start.23 = (bf16[4,16,6144]{2,1,0:T(8,128)(2,1)S(1)}, bf16[4,16,6144]{2,1,0:T(8,128)(2,1)S(1)}, u32[]{:S(2)}, u32[]{:S(2)}) collective-permute-start(bf16[4,16,6144]{2,1,0:T(8,128)(2,1)S(1)} %shard_map.143.refs_13_.refs_0_), channel_id=1, source_target_pairs={{0,8},{1,9},{2,10},{3,11},{4,12},{5,13},{6,14},{7,15},{8,0},{9,1},... | collective-permute-start | bytes 2359304 | tf_op jit(solution)/shard_map/ppermute | solution.py:121
  52.0 9.8 %collective-permute-start.16 = (bf16[2,16,4096]{2,1,0:T(8,128)(2,1)S(1)}, bf16[2,16,4096]{2,1,0:T(8,128)(2,1)S(1)}, u32[]{:S(2)}, u32[]{:S(2)}) collective-permute-start(bf16[2,16,4096]{2,1,0:T(8,128)(2,1)S(1)} %slice.39), channel_id=1, source_target_pairs={{0,4},{1,3},{2,6},{3,1},{4,0},{5,7},{6,2},{7,5},{8,12},{9,11},{10,... | collective-permute-start | bytes 786440 | tf_op jit(solution)/shard_map/ppermute | solution.py:121
  53.3 8.6 %collective-permute-start.17 = (bf16[2,16,4096]{2,1,0:T(8,128)(2,1)S(1)}, bf16[2,16,4096]{2,1,0:T(8,128)(2,1)S(1)}, u32[]{:S(2)}, u32[]{:S(2)}) collective-permute-start(bf16[2,16,4096]{2,1,0:T(8,128)(2,1)S(1)} %slice.40), channel_id=1, source_target_pairs={{0,2},{1,5},{2,0},{3,7},{4,6},{5,1},{6,4},{7,3},{8,10},{9,13},{10,... | collective-permute-start | bytes 786440 | tf_op jit(solution)/shard_map/ppermute | solution.py:121
  54.5 7.4 %collective-permute-start.19 = (bf16[4,16,4096]{2,1,0:T(8,128)(2,1)S(1)}, bf16[4,16,4096]{2,1,0:T(8,128)(2,1)S(1)}, u32[]{:S(2)}, u32[]{:S(2)}) collective-permute-start(bf16[4,16,4096]{2,1,0:T(8,128)(2,1)S(1)} %collective-permute-done.13.refs_2_), channel_id=1, source_target_pairs={{0,1},{1,0},{2,3},{3,2},{4,5},{5,4},{6,7},{7,6},{8,9},{9,8},{10,11... | collective-permute-start | bytes 1572872 | tf_op jit(solution)/shard_map/ppermute | solution.py:121
  54.5 7.4 %collective-permute-start.20 = (bf16[4,16,4096]{2,1,0:T(8,128)(2,1)S(1)}, bf16[4,16,4096]{2,1,0:T(8,128)(2,1)S(1)}, u32[]{:S(2)}, u32[]{:S(2)}) collective-permute-start(bf16[4,16,4096]{2,1,0:T(8,128)(2,1)S(1)} %collective-permute-done.14.refs_3_), channel_id=1, source_target_pairs={{0,1},{1,0},{2,3},{3,2},{4,5},{5,4},{6,7},{7,6},{8,9},{9,8},{10,11... | collective-permute-start | bytes 1572872 | tf_op jit(solution)/shard_map/ppermute | solution.py:121
  62.0 2.0 %collective-permute-start.21 = (bf16[4,16,4096]{2,1,0:T(8,128)(2,1)S(1)}, bf16[4,16,4096]{2,1,0:T(8,128)(2,1)S(1)}, u32[]{:S(2)}, u32[]{:S(2)}) collective-permute-start(bf16[4,16,4096]{2,1,0:T(8,128)(2,1)S(1)} %shard_map.145.refs_4_), channel_id=1, source_target_pairs={{0,1},{1,0},{2,3},{3,2},{4,5},{5,4},{6,7},{7,6},{8,9},{9,8},{10,11... | collective-permute-start | bytes 1572872 | tf_op jit(solution)/shard_map/ppermute | solution.py:121
  69.9 14.3 %collective-permute-start.27 = (bf16[4,16,2048]{2,1,0:T(8,128)(2,1)S(1)}, bf16[4,16,2048]{2,1,0:T(8,128)(2,1)S(1)}, u32[]{:S(2)}, u32[]{:S(2)}) collective-permute-start(bf16[4,16,2048]{2,1,0:T(8,128)(2,1)S(1)} %get-tuple-element.62.refs_3_), channel_id=1, source_target_pairs={{0,2},{1,5},{2,0},{3,7},{4,6},{5,1},{6,4},{7,3},{8,10},{9,13},{10,... | collective-permute-start | bytes 786440 | tf_op jit(solution)/shard_map/ppermute | solution.py:121
  71.7 12.5 %collective-permute-start.26 = (bf16[4,16,2048]{2,1,0:T(8,128)(2,1)S(1)}, bf16[4,16,2048]{2,1,0:T(8,128)(2,1)S(1)}, u32[]{:S(2)}, u32[]{:S(2)}) collective-permute-start(bf16[4,16,2048]{2,1,0:T(8,128)(2,1)S(1)} %get-tuple-element.55.refs_11_.refs_2_), channel_id=1, source_target_pairs={{0,4},{1,3},{2,6},{3,1},{4,0},{5,7},{6,2},{7,5},{8,12},{9,11},{10,... | collective-permute-start | bytes 786440 | tf_op jit(solution)/shard_map/ppermute | solution.py:121
  72.7 1.3 collective-permute-start.22
  74.0 15.3 %copy-start.5 = (f32[144,256]{1,0:T(8,128)S(1)}, f32[144,256]{1,0:T(8,128)}, u32[]{:S(2)}) copy-start(f32[144,256]{1,0:T(8,128)} %constant.10.clone.refs_13_) | copy-start | bytes 442372
  74.1 12.1 %collective-permute-start.24 = (bf16[8,36,512]{2,1,0:T(8,128)(2,1)S(1)}, bf16[8,36,512]{2,1,0:T(8,128)(2,1)S(1)}, u32[]{:S(2)}, u32[]{:S(2)}) collective-permute-start(bf16[8,36,512]{2,1,0:T(8,128)(2,1)S(1)} %shard_map.149), channel_id=1, source_target_pairs={{2,0},{3,1},{4,2},{5,3},{6,4},{7,5},{8,6},{9,7},{10,8},{11,9},{12,... | collective-permute-start | bytes 884744 | tf_op jit(solution)/shard_map/ppermute | solution.py:385
  78.8 8.8 %collective-permute-start.29 = (bf16[4,16,2048]{2,1,0:T(8,128)(2,1)S(1)}, bf16[4,16,2048]{2,1,0:T(8,128)(2,1)S(1)}, u32[]{:S(2)}, u32[]{:S(2)}) collective-permute-start(bf16[4,16,2048]{2,1,0:T(8,128)(2,1)S(1)} %get-tuple-element.62.refs_3_), channel_id=1, source_target_pairs={{0,1},{1,0},{2,3},{3,2},{4,5},{5,4},{6,7},{7,6},{8,9},{9,8},{10,11... | collective-permute-start | bytes 786440 | tf_op jit(solution)/shard_map/ppermute | solution.py:121
  78.8 9.2 %collective-permute-start.28 = (bf16[4,16,2048]{2,1,0:T(8,128)(2,1)S(1)}, bf16[4,16,2048]{2,1,0:T(8,128)(2,1)S(1)}, u32[]{:S(2)}, u32[]{:S(2)}) collective-permute-start(bf16[4,16,2048]{2,1,0:T(8,128)(2,1)S(1)} %get-tuple-element.55.refs_11_.refs_2_), channel_id=1, source_target_pairs={{0,1},{1,0},{2,3},{3,2},{4,5},{5,4},{6,7},{7,6},{8,9},{9,8},{10,11... | collective-permute-start | bytes 786440 | tf_op jit(solution)/shard_map/ppermute | solution.py:121
  84.2 3.9 %collective-permute-start.30 = (bf16[4,16,2048]{2,1,0:T(8,128)(2,1)S(1)}, bf16[4,16,2048]{2,1,0:T(8,128)(2,1)S(1)}, u32[]{:S(2)}, u32[]{:S(2)}) collective-permute-start(bf16[4,16,2048]{2,1,0:T(8,128)(2,1)S(1)} %collective-permute-done.26.refs_4_), channel_id=1, source_target_pairs={{0,1},{1,0},{2,3},{3,2},{4,5},{5,4},{6,7},{7,6},{8,9},{9,8},{10,11... | collective-permute-start | bytes 786440 | tf_op jit(solution)/shard_map/ppermute | solution.py:121
  84.3 5.0 %collective-permute-start.31 = (bf16[4,16,2048]{2,1,0:T(8,128)(2,1)S(1)}, bf16[4,16,2048]{2,1,0:T(8,128)(2,1)S(1)}, u32[]{:S(2)}, u32[]{:S(2)}) collective-permute-start(bf16[4,16,2048]{2,1,0:T(8,128)(2,1)S(1)} %collective-permute-done.27.refs_5_), channel_id=1, source_target_pairs={{0,1},{1,0},{2,3},{3,2},{4,5},{5,4},{6,7},{7,6},{8,9},{9,8},{10,11... | collective-permute-start | bytes 786440 | tf_op jit(solution)/shard_map/ppermute | solution.py:121
  86.1 1.3 collective-permute-start.25
  87.4 15.9 %collective-permute-start.34 = (bf16[4,16,4096]{2,1,0:T(8,128)(2,1)S(1)}, bf16[4,16,4096]{2,1,0:T(8,128)(2,1)S(1)}, u32[]{:S(2)}, u32[]{:S(2)}) collective-permute-start(bf16[4,16,4096]{2,1,0:T(8,128)(2,1)S(1)} %get-tuple-element.67.refs_1_), channel_id=1, source_target_pairs={{0,1},{1,0},{2,3},{3,2},{4,5},{5,4},{6,7},{7,6},{8,9},{9,8},{10,11... | collective-permute-start | bytes 1572872 | tf_op jit(solution)/shard_map/ppermute | solution.py:121
  87.6 15.7 %collective-permute-start.35 = (bf16[4,16,4096]{2,1,0:T(8,128)(2,1)S(1)}, bf16[4,16,4096]{2,1,0:T(8,128)(2,1)S(1)}, u32[]{:S(2)}, u32[]{:S(2)}) collective-permute-start(bf16[4,16,4096]{2,1,0:T(8,128)(2,1)S(1)} %get-tuple-element.68.refs_2_), channel_id=1, source_target_pairs={{0,1},{1,0},{2,3},{3,2},{4,5},{5,4},{6,7},{7,6},{8,9},{9,8},{10,11... | collective-permute-start | bytes 1572872 | tf_op jit(solution)/shard_map/ppermute | solution.py:121
  88.1 14.7 %collective-permute-start.32 = (bf16[4,16,4096]{2,1,0:T(8,128)(2,1)S(1)}, bf16[4,16,4096]{2,1,0:T(8,128)(2,1)S(1)}, u32[]{:S(2)}, u32[]{:S(2)}) collective-permute-start(bf16[4,16,4096]{2,1,0:T(8,128)(2,1)S(1)} %get-tuple-element.67.refs_1_), channel_id=1, source_target_pairs={{0,4},{1,3},{2,6},{3,1},{4,0},{5,7},{6,2},{7,5},{8,12},{9,11},{10,... | collective-permute-start | bytes 1572872 | tf_op jit(solution)/shard_map/ppermute | solution.py:121
  88.1 14.7 %collective-permute-start.33 = (bf16[4,16,4096]{2,1,0:T(8,128)(2,1)S(1)}, bf16[4,16,4096]{2,1,0:T(8,128)(2,1)S(1)}, u32[]{:S(2)}, u32[]{:S(2)}) collective-permute-start(bf16[4,16,4096]{2,1,0:T(8,128)(2,1)S(1)} %get-tuple-element.68.refs_2_), channel_id=1, source_target_pairs={{0,2},{1,5},{2,0},{3,7},{4,6},{5,1},{6,4},{7,3},{8,10},{9,13},{10,... | collective-permute-start | bytes 1572872 | tf_op jit(solution)/shard_map/ppermute | solution.py:121
  102.8 1.9 %collective-permute-start.36 = (bf16[4,16,4096]{2,1,0:T(8,128)(2,1)S(1)}, bf16[4,16,4096]{2,1,0:T(8,128)(2,1)S(1)}, u32[]{:S(2)}, u32[]{:S(2)}) collective-permute-start(bf16[4,16,4096]{2,1,0:T(8,128)(2,1)S(1)} %collective-permute-done.32.refs_3_), channel_id=1, source_target_pairs={{0,1},{1,0},{2,3},{3,2},{4,5},{5,4},{6,7},{7,6},{8,9},{9,8},{10,11... | collective-permute-start | bytes 1572872 | tf_op jit(solution)/shard_map/ppermute | solution.py:121
  102.9 2.5 %collective-permute-start.37 = (bf16[4,16,4096]{2,1,0:T(8,128)(2,1)S(1)}, bf16[4,16,4096]{2,1,0:T(8,128)(2,1)S(1)}, u32[]{:S(2)}, u32[]{:S(2)}) collective-permute-start(bf16[4,16,4096]{2,1,0:T(8,128)(2,1)S(1)} %collective-permute-done.33.refs_4_), channel_id=1, source_target_pairs={{0,1},{1,0},{2,3},{3,2},{4,5},{5,4},{6,7},{7,6},{8,9},{9,8},{10,11... | collective-permute-start | bytes 1572872 | tf_op jit(solution)/shard_map/ppermute | solution.py:121
  110.3 1.3 %collective-permute-start.38 = (bf16[2,36,512]{2,1,0:T(8,128)(2,1)S(1)}, bf16[2,36,512]{2,1,0:T(8,128)(2,1)S(1)}, u32[]{:S(2)}, u32[]{:S(2)}) collective-permute-start(bf16[2,36,512]{2,1,0:T(8,128)(2,1)S(1)} %get-tuple-element.71), channel_id=1, source_target_pairs={{1,0},{0,1},{3,2},{2,3},{5,4},{4,5},{7,6},{6,7},{9,8},{8,9},{11,10... | collective-permute-start | bytes 221192 | tf_op jit(solution)/shard_map/ppermute | solution.py:385
  111.6 14.4 %collective-permute-start.39 = (bf16[8,36,512]{2,1,0:T(8,128)(2,1)S(1)}, bf16[8,36,512]{2,1,0:T(8,128)(2,1)S(1)}, u32[]{:S(2)}, u32[]{:S(2)}) collective-permute-start(bf16[8,36,512]{2,1,0:T(8,128)(2,1)S(1)} %shard_map.153), channel_id=1, source_target_pairs={{30,0},{31,1},{0,2},{1,3},{2,4},{3,5},{4,6},{5,7},{6,8},{7,9},{8,1... | collective-permute-start | bytes 884744 | tf_op jit(solution)/shard_map/ppermute | solution.py:385
  124.7 1.3 %collective-permute-start.40 = (bf16[2,36,512]{2,1,0:T(8,128)(2,1)S(1)}, bf16[2,36,512]{2,1,0:T(8,128)(2,1)S(1)}, u32[]{:S(2)}, u32[]{:S(2)}) collective-permute-start(bf16[2,36,512]{2,1,0:T(8,128)(2,1)S(1)} %get-tuple-element.78), channel_id=1, source_target_pairs={{1,0},{0,1},{3,2},{2,3},{5,4},{4,5},{7,6},{6,7},{9,8},{8,9},{11,10... | collective-permute-start | bytes 221192 | tf_op jit(solution)/shard_map/ppermute | solution.py:385

commit v18 on v17

--- a/solution.py
+++ b/solution.py
@@ -149,7 +149,9 @@
     return [column] + received + [send(part, swap) for part in [column] + received]
 
 
-def load_pieces(kind, pieces, w_ref, stage_ref, sem):
+def load_pieces(kind, first, pieces, w_ref, stage_ref, sem):
+    if kind == "halves":
+        pieces = [piece.at[:, :, pl.ds(first, w_ref.shape[1])] for piece in pieces]
     copies = [
         pltpu.make_async_copy(piece, w_ref if kind == "rows" else stage_ref.at[index], sem.at[index])
         for index, piece in enumerate(pieces)
@@ -180,7 +182,7 @@
 
 
 def load_scratch(pieces, rows, width):
-    stage = (len(pieces),) + pieces[0].shape if len(pieces) > 1 else (1, 1, 16, 128)
+    stage = (len(pieces),) + pieces[0].shape[:2] + (width,) if len(pieces) > 1 else (1, 1, 16, 128)
     return [
         pltpu.VMEM((rows, width), jnp.bfloat16),
         pltpu.VMEM(stage, jnp.bfloat16),
@@ -198,7 +200,7 @@
 
     @pl.when(pl.program_id(0) == 0)
     def _():
-        load_pieces(kind, pieces, w_ref, stage_ref, sem)
+        load_pieces(kind, 0, pieces, w_ref, stage_ref, sem)
 
     if shifted:
         quarters = []
@@ -311,7 +313,7 @@
         scratch_shapes=load_scratch(pieces, features, 4 * features),
         compiler_params=pltpu.CompilerParams(vmem_limit_bytes=24 * 2**20),
         cost_estimate=pl.CostEstimate(
-            flops=count * 2_000_000_000, bytes_accessed=6_000_000, transcendentals=0
+            flops=count * 300_000_000, bytes_accessed=1_000_000, transcendentals=0
         ),
     )(*sources, *pieces, gain, sharp, ones, *extra, *after)
 
@@ -323,7 +325,7 @@
 
     @pl.when(pl.program_id(0) == 0)
     def _():
-        load_pieces(kind, pieces, w_ref, stage_ref, sem)
+        load_pieces(kind, 4 * x_ref.shape[-1], pieces, w_ref, stage_ref, sem)
 
     tokens = x_ref[...].reshape(held * CELLS, features)
     total = jnp.zeros(tokens.shape, jnp.float32)
@@ -450,22 +452,21 @@
             [[(0, weight) for weight in weights[2:]], [(1, weight) for weight in weights]],
             (own,),
         )
-        widths = tuple(sum(weight.shape[2] for weight in pair) for pair in (weights[:2], weights[2:]))
         (pair,) = join([[own, across_z(own, 2)]], (), (windows,))
         (feed_pair,) = join([[feed_own, across_z(feed_own, 2)]])
-        last_beside = send(last_own, beside)
-        (column,) = join([[pair, across_z(pair, 1)]], (), (feed_pair, last_beside))
+        last_beside, last_across = send(last_own, beside), send(last_own, across)
+        (last_pair,) = join([[last_own, last_across]])
+        (column,) = join([[pair, across_z(pair, 1)]], (), (feed_pair, last_beside, last_pair))
         received = [send(column, way) for way in (beside, across, corner)]
-        last_other = across_z(tied(last_own, column), 2)
+        last_other = across_z(tied(last_pair, column), 2)
         sent = [tied(column, (received[0], last_other))] + received
         pieces = "columns", [column] + received + [send(part, swap) for part in sent]
-        last_across = send(tied(last_other, received[0]), across)
         (feed_column,) = join([[feed_pair, across_z(feed_pair, 1)]])
+        (last_four,) = join([[last_own, last_beside, last_other]])
         received = [send(feed_column, way) for way in (beside, across)]
         middle_0 = attention(0, [windows], (0,), pieces, (feed_column,))
-        first, second = tied((received[0][:2], received[1][2:]), (middle_0, last_across))
+        first, second = tied((received[0][:2], received[1][2:]), middle_0)
         corners = [send(first, across), send(second, beside)]
-        (last_four,) = join([[last_own, last_beside, last_other, last_across]], (), (middle_0,))
         middle_1 = attention(0, [windows], (1,), pieces, (middle_0, last_four))
         last_other = across_z(last_four, 1)
         swapped = [send(part, swap) for part in [feed_column] + tied(received, middle_0)]
@@ -485,22 +486,18 @@
     size = left_0.shape[0]
     (ahead,) = strips([left_0, below_0], [[(0, 1, size - 1), (1, 0, 1)]])
     ahead = shift_from(ahead, 1, 0)
-    after = (below_0,)
     if relay:
-        columns = halves(last_four, last_other, widths, (low_0,))
-        last_columns, final_columns = list(columns[:2]), list(columns[2:])
+        last_columns = list(halves(last_four, last_other, (last_four.shape[2],), (low_0,)))
         last_received = [send(part, way) for part, way in zip(last_columns, (across, beside))]
-        after += (last_columns[0],)
-    left_1, right_1, low_1 = forward(0, middle_1, 0, feed_pieces, low_edge, after)
+    left_1, right_1, low_1 = forward(0, middle_1, 0, feed_pieces, low_edge, (below_0,))
     below_1 = shift_from(tied(low_1, ahead), 0, 1)
     if relay:
         last_pieces = last_columns + last_received
-        last_pieces += [send(part, swap) for part in last_columns + tied(last_received, low_1)]
-        last_pieces = "halves", last_pieces
-        final_received = [
-            send(part, way)
-            for part, way in zip(tied(final_columns, last_received), (across, beside))
-        ]
+        swapped = [send(tied(last_columns[0], low_0), swap)]
+        swapped.append(send(tied(last_columns[1], swapped[0]), swap))
+        last_received = tied(last_received, (low_1, ahead, *swapped))
+        last_pieces += swapped + [send(part, swap) for part in last_received]
+        last_pieces = final_pieces = "halves", last_pieces
     lefts = strips(
         [right_0, left_1, right_1, below_0, below_1],
         [
@@ -510,10 +507,6 @@
         ],
     )
     middle_1 = attention(1, [lefts[2], ahead], (1,), last_pieces)
-    if relay:
-        final_pieces = final_columns + final_received
-        final_pieces += [send(part, swap) for part in final_columns + tied(final_received, middle_1)]
-        final_pieces = "halves", final_pieces
     left_1, right_1, high_1 = forward(1, middle_1, 0, final_pieces, high_edge)
     above_1 = shift_from(high_1, 0, -1)
     (behind,) = strips([above_1, right_1], [[(0, 1, 1), (1, 0, size - 1)]])

time: 129 us -> 135 us (1.047)
  waiting for transfers between devices: 36.2 us -> 44.6 us
  starting transfers between devices: 37 us -> 34.5 us
    ppermute x6, waiting for transfers between devices: 6.29 us -> 20.4 us  [shift_from(): return lax.ppermute(block, ('lon', 'lat'), pairs)]
    ppermute x35 -> x29, waiting for transfers between devices: 29.9 us -> 24.2 us  [send(): return lax.ppermute(block, ('lon', 'lat'), pairs)]
    ppermute x35 -> x29, starting transfers between devices: 30.7 us -> 27.5 us  [send(): return lax.ppermute(block, ('lon', 'lat'), pairs)]
  transfers between devices with their start and end apart: 41 -> 35, of which waited for: 15 -> 14; matrix products, arithmetic and copies ran while one was open for 1% -> 1% of each run, Pallas kernels for 33% -> 26%
where the time goes in v18:
time: 135 us
  Pallas kernels  47.6 us (35%)
  waiting for transfers between devices  44.6 us (33%)
  starting transfers between devices  34.5 us (26%)
  local copies, waits for them, and re-layouts  7.64 us (6%)
    pallas_call x4, Pallas kernels, attend(): pl.pallas_call(functools.partial(attend_kernel, shifted, row_windows, kin...  27.7 us
    ppermute x29, starting transfers between devices, send(): return lax.ppermute(block, ('lon', 'lat'), pairs)  27.5 us
    ppermute x29, waiting for transfers between devices, send(): return lax.ppermute(block, ('lon', 'lat'), pairs)  24.2 us
    ppermute x6, waiting for transfers between devices, shift_from(): return lax.ppermute(block, ('lon', 'lat'), pairs)  20.4 us
    pallas_call x4, Pallas kernels, feed(): pl.pallas_call(functools.partial(feed_kernel, kind, len(pieces), hidden_s...  19.3 us
    ppermute x6, starting transfers between devices, shift_from(): return lax.ppermute(block, ('lon', 'lat'), pairs)  7.06 us
    unnamed x20, local copies, waits for them, and re-layouts  3.7 us
  transfers between devices with their start and end apart: 35, of which 14 were waited for; matrix products, arithmetic and copies ran while one was open for 1% of the time, Pallas kernels for 26%

profile of v18, /device:TPU:0, one launch (start us, length us, event | category | flops | bytes accessed | tf_op | source)
XLA Modules:
  0.0 134.8 jit_solution(12765943472469130694)
XLA Ops:
  0.0 0.9 copy-done.3
  0.9 0.8 copy-done.5
  1.8 4.0 %collective-permute-start = (bf16[1,16,2048]{2,1,0:T(8,128)(2,1)S(1)}, bf16[1,16,2048]{2,1,0:T(8,128)(2,1)S(1)}, u32[]{:S(2)}, u32[]{:S(2)}) collective-permute-start(bf16[1,16,2048]{2,1,0:T(8,128)(2,1)S(1)} %shard_map.136.refs_0_.refs_6_), channel_id=1, source_target_pairs={{0,16},{1,17},{2,18},{3,19},{4,20},{5,21},{6,22},{7,23},{8,24},{9,... | collective-permute-start | bytes 196616 | tf_op jit(solution)/shard_map/ppermute | solution.py:121
  5.8 0.9 copy-done.1
  6.8 0.9 copy-done.2
  7.7 1.6 %collective-permute-start.4 = (bf16[1,16,6144]{2,1,0:T(8,128)(2,1)S(1)}, bf16[1,16,6144]{2,1,0:T(8,128)(2,1)S(1)}, u32[]{:S(2)}, u32[]{:S(2)}) collective-permute-start(bf16[1,16,6144]{2,1,0:T(8,128)(2,1)S(1)} %get-tuple-element.38.refs_0_), channel_id=1, source_target_pairs={{0,4},{1,3},{2,6},{3,1},{4,0},{5,7},{6,2},{7,5},{8,12},{9,11},{10,... | collective-permute-start | bytes 589832 | tf_op jit(solution)/shard_map/ppermute | solution.py:121
  9.3 1.5 %collective-permute-start.3 = (bf16[1,16,6144]{2,1,0:T(8,128)(2,1)S(1)}, bf16[1,16,6144]{2,1,0:T(8,128)(2,1)S(1)}, u32[]{:S(2)}, u32[]{:S(2)}) collective-permute-start(bf16[1,16,6144]{2,1,0:T(8,128)(2,1)S(1)} %get-tuple-element.38.refs_0_), channel_id=1, source_target_pairs={{0,2},{1,5},{2,0},{3,7},{4,6},{5,1},{6,4},{7,3},{8,10},{9,13},{10,... | collective-permute-start | bytes 589832 | tf_op jit(solution)/shard_map/ppermute | solution.py:121
  10.8 0.3 collective-permute-start.2
  11.2 0.8 copy.26
  12.0 0.5 reshape.15.refs_2_.refs_0_
  12.5 1.6 %collective-permute-start.1 = (bf16[2,16,2048]{2,1,0:T(8,128)(2,1)S(1)}, bf16[2,16,2048]{2,1,0:T(8,128)(2,1)S(1)}, u32[]{:S(2)}, u32[]{:S(2)}) collective-permute-start(bf16[2,16,2048]{2,1,0:T(8,128)(2,1)S(1)} %shard_map.137.refs_0_), channel_id=1, source_target_pairs={{0,8},{1,9},{2,10},{3,11},{4,12},{5,13},{6,14},{7,15},{8,0},{9,1},... | collective-permute-start | bytes 393224 | tf_op jit(solution)/shard_map/ppermute | solution.py:121
  14.1 4.8 %collective-permute-done.2.refs_1_ = bf16[1,16,4096]{2,1,0:T(8,128)(2,1)S(1)} collective-permute-done((bf16[1,16,4096]{2,1,0:T(8,128)(2,1)S(1)}, bf16[1,16,4096]{2,1,0:T(8,128)(2,1)S(1)}, u32[]{:S(2)}, u32[]{:S(2)}) %collective-permute-start.2) | collective-permute-done | bytes 131104 | tf_op jit(solution)/shard_map/ppermute | solution.py:121
  19.1 0.6 collective-permute-start.7
  19.7 0.3 collective-permute-start.13
  20.0 1.5 %collective-permute-start.6 = (bf16[4,16,2048]{2,1,0:T(8,128)(2,1)S(1)}, bf16[4,16,2048]{2,1,0:T(8,128)(2,1)S(1)}, u32[]{:S(2)}, u32[]{:S(2)}) collective-permute-start(bf16[4,16,2048]{2,1,0:T(8,128)(2,1)S(1)} %shard_map.141.refs_1_), channel_id=1, source_target_pairs={{0,4},{1,3},{2,6},{3,1},{4,0},{5,7},{6,2},{7,5},{8,12},{9,11},{10,... | collective-permute-start | bytes 786440 | tf_op jit(solution)/shard_map/ppermute | solution.py:121
  21.5 1.5 %collective-permute-start.5 = (bf16[4,16,2048]{2,1,0:T(8,128)(2,1)S(1)}, bf16[4,16,2048]{2,1,0:T(8,128)(2,1)S(1)}, u32[]{:S(2)}, u32[]{:S(2)}) collective-permute-start(bf16[4,16,2048]{2,1,0:T(8,128)(2,1)S(1)} %shard_map.141.refs_1_), channel_id=1, source_target_pairs={{0,2},{1,5},{2,0},{3,7},{4,6},{5,1},{6,4},{7,3},{8,10},{9,13},{10,... | collective-permute-start | bytes 786440 | tf_op jit(solution)/shard_map/ppermute | solution.py:121
  23.0 3.5 %collective-permute-start.8 = (bf16[2,16,6144]{2,1,0:T(8,128)(2,1)S(1)}, bf16[2,16,6144]{2,1,0:T(8,128)(2,1)S(1)}, u32[]{:S(2)}, u32[]{:S(2)}) collective-permute-start(bf16[2,16,6144]{2,1,0:T(8,128)(2,1)S(1)} %shard_map.140.refs_4_), channel_id=1, source_target_pairs={{0,16},{1,17},{2,18},{3,19},{4,20},{5,21},{6,22},{7,23},{8,24},{9,... | collective-permute-start | bytes 1179656 | tf_op jit(solution)/shard_map/ppermute | solution.py:121
  26.5 2.2 %collective-permute-done.7.refs_4_ = bf16[4,16,2048]{2,1,0:T(8,128)(2,1)S(1)} collective-permute-done((bf16[4,16,2048]{2,1,0:T(8,128)(2,1)S(1)}, bf16[4,16,2048]{2,1,0:T(8,128)(2,1)S(1)}, u32[]{:S(2)}, u32[]{:S(2)}) %collective-permute-start.7) | collective-permute-done | bytes 262176 | tf_op jit(solution)/shard_map/ppermute | solution.py:121
  28.8 2.4 %collective-permute-start.15 = (bf16[4,16,4096]{2,1,0:T(8,128)(2,1)S(1)}, bf16[4,16,4096]{2,1,0:T(8,128)(2,1)S(1)}, u32[]{:S(2)}, u32[]{:S(2)}) collective-permute-start(bf16[4,16,4096]{2,1,0:T(8,128)(2,1)S(1)} %shard_map.142.refs_12_.refs_1_), channel_id=1, source_target_pairs={{0,4},{1,3},{2,6},{3,1},{4,0},{5,7},{6,2},{7,5},{8,12},{9,11},{10,... | collective-permute-start | bytes 1572872 | tf_op jit(solution)/shard_map/ppermute | solution.py:121
  31.1 0.3 collective-permute-done.6.refs_3_
  31.4 2.4 %collective-permute-start.14 = (bf16[4,16,4096]{2,1,0:T(8,128)(2,1)S(1)}, bf16[4,16,4096]{2,1,0:T(8,128)(2,1)S(1)}, u32[]{:S(2)}, u32[]{:S(2)}) collective-permute-start(bf16[4,16,4096]{2,1,0:T(8,128)(2,1)S(1)} %shard_map.142.refs_12_.refs_1_), channel_id=1, source_target_pairs={{0,2},{1,5},{2,0},{3,7},{4,6},{5,1},{6,4},{7,3},{8,10},{9,13},{10,... | collective-permute-start | bytes 1572872 | tf_op jit(solution)/shard_map/ppermute | solution.py:121
  33.9 8.6 %collective-permute-done.8.refs_2_ = bf16[2,16,6144]{2,1,0:T(8,128)(2,1)S(1)} collective-permute-done((bf16[2,16,6144]{2,1,0:T(8,128)(2,1)S(1)}, bf16[2,16,6144]{2,1,0:T(8,128)(2,1)S(1)}, u32[]{:S(2)}, u32[]{:S(2)}) %collective-permute-start.8) | collective-permute-done | bytes 393248 | tf_op jit(solution)/shard_map/ppermute | solution.py:121
  42.5 0.5 collective-permute-start.9
  43.0 0.1 multiply_reduce_fusion
  43.1 0.1 collective-permute-start.18
  43.2 0.8 collective-permute-done.10.refs_6_
  44.0 0.4 collective-permute-done.9.refs_5_
  44.4 6.9 %shard_map.143.refs_12_.refs_0_ = bf16[4,144,512]{2,1,0:T(8,128)(2,1)S(1)} custom-call(bf16[8,144,512]{2,1,0:T(8,128)(2,1)S(1)} %reshape.15.refs_2_.refs_0_, bf16[4,16,2048]{2,1,0:T(8,128)(2,1)S(1)} %shard_map.141.refs_1_, bf16[4,16,2048]{2,1,0:T(8,128)(2,1)S(1)} %collective-permute-done.5.refs_2_, bf16[4,16,2048]{2,1,0:T(8,128)(2,1)S(1)} %collective-permute-done.6.refs_3_, ...), custom_call_target="tpu_custom_call" | custom-call | flops 1200000000 | bytes 1000000 | tf_op jit(solution)/shard_map/pallas_call | solution.py:302
  51.3 0.2 collective-permute-start.19
  51.5 0.4 collective-permute-start.20
  52.0 0.6 collective-permute-start.16
  52.6 0.7 collective-permute-start.17
  53.4 0.1 collective-permute-start.25
  53.5 6.9 %shard_map.145.refs_0_ = bf16[4,144,512]{2,1,0:T(8,128)(2,1)S(1)} custom-call(bf16[8,144,512]{2,1,0:T(8,128)(2,1)S(1)} %reshape.15.refs_2_.refs_0_, bf16[4,16,2048]{2,1,0:T(8,128)(2,1)S(1)} %shard_map.141.refs_1_, bf16[4,16,2048]{2,1,0:T(8,128)(2,1)S(1)} %collective-permute-done.5.refs_2_, bf16[4,16,2048]{2,1,0:T(8,128)(2,1)S(1)} %collective-permute-done.6.refs_3_, ...), custom_call_target="tpu_custom_call" | custom-call | flops 1200000000 | bytes 1000000 | tf_op jit(solution)/shard_map/pallas_call | solution.py:302
  60.4 0.3 collective-permute-done.16.refs_0_
  60.7 0.1 collective-permute-start.21
  60.8 1.9 %collective-permute-done.21.refs_8_ = bf16[4,16,4096]{2,1,0:T(8,128)(2,1)S(1)} collective-permute-done((bf16[4,16,4096]{2,1,0:T(8,128)(2,1)S(1)}, bf16[4,16,4096]{2,1,0:T(8,128)(2,1)S(1)}, u32[]{:S(2)}, u32[]{:S(2)}) %collective-permute-start.21) | collective-permute-done | bytes 524320 | tf_op jit(solution)/shard_map/ppermute | solution.py:121
  62.7 4.8 %shard_map.147 = (bf16[8,36,512]{2,1,0:T(8,128)(2,1)S(1)}, bf16[8,36,512]{2,1,0:T(8,128)(2,1)S(1)}, bf16[2,36,512]{2,1,0:T(8,128)(2,1)S(1)}) custom-call(bf16[4,144,512]{2,1,0:T(8,128)(2,1)S(1)} %shard_map.143.refs_12_.refs_0_, bf16[4,16,4096]{2,1,0:T(8,128)(2,1)S(1)} %shard_map.142.refs_12_.refs_1_, ...), custom_call_target="tpu_custom_call" | custom-call | flops 1000000 | bytes 100000 | tf_op jit(solution)/shard_map/pallas_call | solution.py:360
  67.6 4.9 %collective-permute-done.25.refs_1_ = bf16[4,16,6144]{2,1,0:T(8,128)(2,1)S(1)} collective-permute-done((bf16[4,16,6144]{2,1,0:T(8,128)(2,1)S(1)}, bf16[4,16,6144]{2,1,0:T(8,128)(2,1)S(1)}, u32[]{:S(2)}, u32[]{:S(2)}) %collective-permute-start.25) | collective-permute-done | bytes 786464 | tf_op jit(solution)/shard_map/ppermute | solution.py:121
  72.5 0.1 shard_map.151
  72.6 0.1 collective-permute-start.28
  72.7 1.4 %collective-permute-start.26 = (bf16[4,16,6144]{2,1,0:T(8,128)(2,1)S(1)}, bf16[4,16,6144]{2,1,0:T(8,128)(2,1)S(1)}, u32[]{:S(2)}, u32[]{:S(2)}) collective-permute-start(bf16[4,16,6144]{2,1,0:T(8,128)(2,1)S(1)} %get-tuple-element.57.refs_2_.refs_1_), channel_id=1, source_target_pairs={{0,4},{1,3},{2,6},{3,1},{4,0},{5,7},{6,2},{7,5},{8,12},{9,11},{10,... | collective-permute-start | bytes 2359304 | tf_op jit(solution)/shard_map/ppermute | solution.py:121
  74.1 1.4 %collective-permute-start.27 = (bf16[4,16,6144]{2,1,0:T(8,128)(2,1)S(1)}, bf16[4,16,6144]{2,1,0:T(8,128)(2,1)S(1)}, u32[]{:S(2)}, u32[]{:S(2)}) collective-permute-start(bf16[4,16,6144]{2,1,0:T(8,128)(2,1)S(1)} %get-tuple-element.58.refs_3_.refs_2_), channel_id=1, source_target_pairs={{0,2},{1,5},{2,0},{3,7},{4,6},{5,1},{6,4},{7,3},{8,10},{9,13},{10,... | collective-permute-start | bytes 2359304 | tf_op jit(solution)/shard_map/ppermute | solution.py:121
  75.5 0.5 collective-permute-start.22
  76.0 1.9 %collective-permute-done.22.refs_10_.refs_1_.refs_3_ = bf16[2,36,512]{2,1,0:T(8,128)(2,1)S(1)} collective-permute-done((bf16[2,36,512]{2,1,0:T(8,128)(2,1)S(1)}, bf16[2,36,512]{2,1,0:T(8,128)(2,1)S(1)}, u32[]{:S(2)}, u32[]{:S(2)}) %collective-permute-start.22) | collective-permute-done | bytes 73760 | tf_op jit(solution)/shard_map/ppermute | solution.py:387
  77.9 3.7 %collective-permute-start.23 = (bf16[8,36,512]{2,1,0:T(8,128)(2,1)S(1)}, bf16[8,36,512]{2,1,0:T(8,128)(2,1)S(1)}, u32[]{:S(2)}, u32[]{:S(2)}) collective-permute-start(bf16[8,36,512]{2,1,0:T(8,128)(2,1)S(1)} %shard_map.149), channel_id=1, source_target_pairs={{2,0},{3,1},{4,2},{5,3},{6,4},{7,5},{8,6},{9,7},{10,8},{11,9},{12,... | collective-permute-start | bytes 884744 | tf_op jit(solution)/shard_map/ppermute | solution.py:387
  81.6 4.8 %shard_map.148 = (bf16[8,36,512]{2,1,0:T(8,128)(2,1)S(1)}, bf16[8,36,512]{2,1,0:T(8,128)(2,1)S(1)}, bf16[2,36,512]{2,1,0:T(8,128)(2,1)S(1)}) custom-call(bf16[4,144,512]{2,1,0:T(8,128)(2,1)S(1)} %shard_map.145.refs_0_, bf16[4,16,4096]{2,1,0:T(8,128)(2,1)S(1)} %shard_map.142.refs_12_.refs_1_, bf16[4,16,4096]{2,1,0:T(8,128)(2,1)S(1)} %collective-permute-done.14.refs_2_, ...), custom_call_target="tpu_custom_call" | custom-call | flops 1000000 | bytes 100000 | tf_op jit(solution)/shard_map/pallas_call | solution.py:360
  86.5 13.1 %collective-permute-done.23.refs_1_ = bf16[8,36,512]{2,1,0:T(8,128)(2,1)S(1)} collective-permute-done((bf16[8,36,512]{2,1,0:T(8,128)(2,1)S(1)}, bf16[8,36,512]{2,1,0:T(8,128)(2,1)S(1)}, u32[]{:S(2)}, u32[]{:S(2)}) %collective-permute-start.23) | collective-permute-done | bytes 294944 | tf_op jit(solution)/shard_map/ppermute | solution.py:387
  99.6 0.1 collective-permute-start.30
  99.7 0.5 collective-permute-start.31
  100.2 0.1 collective-permute-start.24
  100.3 2.9 %collective-permute-done.24.refs_4_ = bf16[2,36,512]{2,1,0:T(8,128)(2,1)S(1)} collective-permute-done((bf16[2,36,512]{2,1,0:T(8,128)(2,1)S(1)}, bf16[2,36,512]{2,1,0:T(8,128)(2,1)S(1)}, u32[]{:S(2)}, u32[]{:S(2)}) %collective-permute-start.24) | collective-permute-done | bytes 73760 | tf_op jit(solution)/shard_map/ppermute | solution.py:387
  103.3 6.9 %shard_map.152.refs_0_ = bf16[4,144,512]{2,1,0:T(8,128)(2,1)S(1)} custom-call(bf16[8,36,512]{2,1,0:T(8,128)(2,1)S(1)} %get-tuple-element.54.refs_0_, bf16[8,36,512]{2,1,0:T(8,128)(2,1)S(1)} %collective-permute-done.23.refs_1_, bf16[4,16,6144]{2,1,0:T(8,128)(2,1)S(1)} %get-tuple-element.57.refs_2_.refs_1_, ...), custom_call_target="tpu_custom_call" | custom-call | flops 1200000000 | bytes 1000000 | tf_op jit(solution)/shard_map/pallas_call | solution.py:302
  110.3 4.8 %shard_map.153 = (bf16[8,36,512]{2,1,0:T(8,128)(2,1)S(1)}, bf16[8,36,512]{2,1,0:T(8,128)(2,1)S(1)}, bf16[2,36,512]{2,1,0:T(8,128)(2,1)S(1)}) custom-call(bf16[4,144,512]{2,1,0:T(8,128)(2,1)S(1)} %shard_map.152.refs_0_, bf16[4,16,6144]{2,1,0:T(8,128)(2,1)S(1)} %get-tuple-element.57.refs_2_.refs_1_, ...), custom_call_target="tpu_custom_call" | custom-call | flops 1000000 | bytes 100000 | tf_op jit(solution)/shard_map/pallas_call | solution.py:360
  115.1 0.2 collective-permute-start.32
  115.3 1.1 collective-permute-done.32.refs_0_.refs_14_.refs_5_
  116.5 2.5 %collective-permute-start.33 = (bf16[8,36,512]{2,1,0:T(8,128)(2,1)S(1)}, bf16[8,36,512]{2,1,0:T(8,128)(2,1)S(1)}, u32[]{:S(2)}, u32[]{:S(2)}) collective-permute-start(bf16[8,36,512]{2,1,0:T(8,128)(2,1)S(1)} %shard_map.154), channel_id=1, source_target_pairs={{30,0},{31,1},{0,2},{1,3},{2,4},{3,5},{4,6},{5,7},{6,8},{7,9},{8,1... | collective-permute-start | bytes 884744 | tf_op jit(solution)/shard_map/ppermute | solution.py:387
  119.0 6.9 %shard_map.155.refs_0_ = bf16[4,144,512]{2,1,0:T(8,128)(2,1)S(1)} custom-call(bf16[8,36,512]{2,1,0:T(8,128)(2,1)S(1)} %get-tuple-element.63.refs_0_, bf16[8,36,512]{2,1,0:T(8,128)(2,1)S(1)} %get-tuple-element.64.refs_1_, bf16[4,16,6144]{2,1,0:T(8,128)(2,1)S(1)} %get-tuple-element.57.refs_2_.refs_1_, ...), custom_call_target="tpu_custom_call" | custom-call | flops 1200000000 | bytes 1000000 | tf_op jit(solution)/shard_map/pallas_call | solution.py:302
  125.9 4.9 %shard_map.156 = (bf16[8,36,512]{2,1,0:T(8,128)(2,1)S(1)}, bf16[8,36,512]{2,1,0:T(8,128)(2,1)S(1)}, bf16[2,36,512]{2,1,0:T(8,128)(2,1)S(1)}) custom-call(bf16[4,144,512]{2,1,0:T(8,128)(2,1)S(1)} %shard_map.155.refs_0_, bf16[4,16,6144]{2,1,0:T(8,128)(2,1)S(1)} %get-tuple-element.57.refs_2_.refs_1_, ...), custom_call_target="tpu_custom_call" | custom-call | flops 1000000 | bytes 100000 | tf_op jit(solution)/shard_map/pallas_call | solution.py:360
  130.7 0.1 collective-permute-start.34
  130.8 1.3 collective-permute-done.34.refs_4_
  132.1 0.1 shard_map.157
  132.2 0.4 copy.23
  132.6 2.2 %copy.24 = bf16[4,6,8,3,2,512]{5,4,3,2,1,0:T(2,128)(2,1)} copy(bf16[4,6,8,3,2,512]{5,2,0,4,3,1:T(8,128)(2,1)S(1)} %bitcast.16) | data formatting | bytes 2359296 | tf_op jit(solution)/shard_map/transpose | solution.py:425
  (57 shorter events, 0.5 us)
Async XLA Ops:
  0.0 0.9 copy-start.3
  0.9 0.8 copy-start.5
  1.8 10.7 %collective-permute-start = (bf16[1,16,2048]{2,1,0:T(8,128)(2,1)S(1)}, bf16[1,16,2048]{2,1,0:T(8,128)(2,1)S(1)}, u32[]{:S(2)}, u32[]{:S(2)}) collective-permute-start(bf16[1,16,2048]{2,1,0:T(8,128)(2,1)S(1)} %shard_map.136.refs_0_.refs_6_), channel_id=1, source_target_pairs={{0,16},{1,17},{2,18},{3,19},{4,20},{5,21},{6,22},{7,23},{8,24},{9,... | collective-permute-start | bytes 196616 | tf_op jit(solution)/shard_map/ppermute | solution.py:121
  5.8 0.9 copy-start.1
  6.8 0.9 copy-start.2
  7.7 3.4 %copy-start.6 = (bf16[24,24,2,512]{3,2,1,0:T(2,128)(2,1)S(1)}, bf16[24,24,2,512]{3,2,1,0:T(2,128)(2,1)}, u32[]{:S(2)}) copy-start(bf16[24,24,2,512]{3,2,1,0:T(2,128)(2,1)} %param.14) | copy-start | bytes 3538948
  7.7 11.2 %collective-permute-start.4 = (bf16[1,16,6144]{2,1,0:T(8,128)(2,1)S(1)}, bf16[1,16,6144]{2,1,0:T(8,128)(2,1)S(1)}, u32[]{:S(2)}, u32[]{:S(2)}) collective-permute-start(bf16[1,16,6144]{2,1,0:T(8,128)(2,1)S(1)} %get-tuple-element.38.refs_0_), channel_id=1, source_target_pairs={{0,4},{1,3},{2,6},{3,1},{4,0},{5,7},{6,2},{7,5},{8,12},{9,11},{10,... | collective-permute-start | bytes 589832 | tf_op jit(solution)/shard_map/ppermute | solution.py:121
  9.3 9.7 %collective-permute-start.3 = (bf16[1,16,6144]{2,1,0:T(8,128)(2,1)S(1)}, bf16[1,16,6144]{2,1,0:T(8,128)(2,1)S(1)}, u32[]{:S(2)}, u32[]{:S(2)}) collective-permute-start(bf16[1,16,6144]{2,1,0:T(8,128)(2,1)S(1)} %get-tuple-element.38.refs_0_), channel_id=1, source_target_pairs={{0,2},{1,5},{2,0},{3,7},{4,6},{5,1},{6,4},{7,3},{8,10},{9,13},{10,... | collective-permute-start | bytes 589832 | tf_op jit(solution)/shard_map/ppermute | solution.py:121
  10.8 8.1 %collective-permute-start.2 = (bf16[1,16,4096]{2,1,0:T(8,128)(2,1)S(1)}, bf16[1,16,4096]{2,1,0:T(8,128)(2,1)S(1)}, u32[]{:S(2)}, u32[]{:S(2)}) collective-permute-start(bf16[1,16,4096]{2,1,0:T(8,128)(2,1)S(1)} %get-tuple-element.37.refs_0_), channel_id=1, source_target_pairs={{0,16},{1,17},{2,18},{3,19},{4,20},{5,21},{6,22},{7,23},{8,24},{9,... | collective-permute-start | bytes 393224 | tf_op jit(solution)/shard_map/ppermute | solution.py:121
  12.5 6.5 %collective-permute-start.1 = (bf16[2,16,2048]{2,1,0:T(8,128)(2,1)S(1)}, bf16[2,16,2048]{2,1,0:T(8,128)(2,1)S(1)}, u32[]{:S(2)}, u32[]{:S(2)}) collective-permute-start(bf16[2,16,2048]{2,1,0:T(8,128)(2,1)S(1)} %shard_map.137.refs_0_), channel_id=1, source_target_pairs={{0,8},{1,9},{2,10},{3,11},{4,12},{5,13},{6,14},{7,15},{8,0},{9,1},... | collective-permute-start | bytes 393224 | tf_op jit(solution)/shard_map/ppermute | solution.py:121
  19.0 14.9 %copy-start.8 = (f32[2,2,512]{2,1,0:T(2,128)S(1)}, f32[2,2,512]{2,1,0:T(2,128)}, u32[]{:S(2)}) copy-start(f32[2,2,512]{2,1,0:T(2,128)} %param.19) | copy-start | bytes 24580
  19.0 24.0 %copy-start.7 = (f32[16,512]{1,0:T(8,128)S(1)}, f32[16,512]{1,0:T(8,128)}, u32[]{:S(2)}) copy-start(f32[16,512]{1,0:T(8,128)} %constant.8.clone) | copy-start | bytes 98308
  19.0 24.0 %copy-start.9 = (f32[2,16]{1,0:T(2,128)S(1)}, f32[2,16]{1,0:T(2,128)}, u32[]{:S(2)}) copy-start(f32[2,16]{1,0:T(2,128)} %param.20) | copy-start | bytes 388
  19.0 25.4 %copy-start = (bf16[640,256]{1,0:T(8,128)(2,1)S(1)}, bf16[640,256]{1,0:T(8,128)(2,1)}, u32[]{:S(2)}) copy-start(bf16[640,256]{1,0:T(8,128)(2,1)} %constant.9.clone.refs_11_.refs_12_) | copy-start | bytes 983044
  19.1 9.6 %collective-permute-start.7 = (bf16[4,16,2048]{2,1,0:T(8,128)(2,1)S(1)}, bf16[4,16,2048]{2,1,0:T(8,128)(2,1)S(1)}, u32[]{:S(2)}, u32[]{:S(2)}) collective-permute-start(bf16[4,16,2048]{2,1,0:T(8,128)(2,1)S(1)} %shard_map.141.refs_1_), channel_id=1, source_target_pairs={{0,6},{1,7},{2,4},{3,5},{4,2},{5,3},{6,0},{7,1},{8,14},{9,15},{10,... | collective-permute-start | bytes 786440 | tf_op jit(solution)/shard_map/ppermute | solution.py:121
  19.7 9.1 %collective-permute-start.13 = (bf16[2,16,4096]{2,1,0:T(8,128)(2,1)S(1)}, bf16[2,16,4096]{2,1,0:T(8,128)(2,1)S(1)}, u32[]{:S(2)}, u32[]{:S(2)}) collective-permute-start(bf16[2,16,4096]{2,1,0:T(8,128)(2,1)S(1)} %shard_map.139.refs_2_.refs_0_), channel_id=1, source_target_pairs={{0,8},{1,9},{2,10},{3,11},{4,12},{5,13},{6,14},{7,15},{8,0},{9,1},... | collective-permute-start | bytes 786440 | tf_op jit(solution)/shard_map/ppermute | solution.py:121
  20.0 11.4 %collective-permute-start.6 = (bf16[4,16,2048]{2,1,0:T(8,128)(2,1)S(1)}, bf16[4,16,2048]{2,1,0:T(8,128)(2,1)S(1)}, u32[]{:S(2)}, u32[]{:S(2)}) collective-permute-start(bf16[4,16,2048]{2,1,0:T(8,128)(2,1)S(1)} %shard_map.141.refs_1_), channel_id=1, source_target_pairs={{0,4},{1,3},{2,6},{3,1},{4,0},{5,7},{6,2},{7,5},{8,12},{9,11},{10,... | collective-permute-start | bytes 786440 | tf_op jit(solution)/shard_map/ppermute | solution.py:121
  21.5 12.3 %collective-permute-start.5 = (bf16[4,16,2048]{2,1,0:T(8,128)(2,1)S(1)}, bf16[4,16,2048]{2,1,0:T(8,128)(2,1)S(1)}, u32[]{:S(2)}, u32[]{:S(2)}) collective-permute-start(bf16[4,16,2048]{2,1,0:T(8,128)(2,1)S(1)} %shard_map.141.refs_1_), channel_id=1, source_target_pairs={{0,2},{1,5},{2,0},{3,7},{4,6},{5,1},{6,4},{7,3},{8,10},{9,13},{10,... | collective-permute-start | bytes 786440 | tf_op jit(solution)/shard_map/ppermute | solution.py:121
  23.0 19.5 %collective-permute-start.8 = (bf16[2,16,6144]{2,1,0:T(8,128)(2,1)S(1)}, bf16[2,16,6144]{2,1,0:T(8,128)(2,1)S(1)}, u32[]{:S(2)}, u32[]{:S(2)}) collective-permute-start(bf16[2,16,6144]{2,1,0:T(8,128)(2,1)S(1)} %shard_map.140.refs_4_), channel_id=1, source_target_pairs={{0,16},{1,17},{2,18},{3,19},{4,20},{5,21},{6,22},{7,23},{8,24},{9,... | collective-permute-start | bytes 1179656 | tf_op jit(solution)/shard_map/ppermute | solution.py:121
  28.7 13.8 %collective-permute-start.12 = (bf16[4,16,2048]{2,1,0:T(8,128)(2,1)S(1)}, bf16[4,16,2048]{2,1,0:T(8,128)(2,1)S(1)}, u32[]{:S(2)}, u32[]{:S(2)}) collective-permute-start(bf16[4,16,2048]{2,1,0:T(8,128)(2,1)S(1)} %collective-permute-done.7.refs_4_), channel_id=1, source_target_pairs={{0,1},{1,0},{2,3},{3,2},{4,5},{5,4},{6,7},{7,6},{8,9},{9,8},{10,11... | collective-permute-start | bytes 786440 | tf_op jit(solution)/shard_map/ppermute | solution.py:121
  28.8 22.6 %collective-permute-start.15 = (bf16[4,16,4096]{2,1,0:T(8,128)(2,1)S(1)}, bf16[4,16,4096]{2,1,0:T(8,128)(2,1)S(1)}, u32[]{:S(2)}, u32[]{:S(2)}) collective-permute-start(bf16[4,16,4096]{2,1,0:T(8,128)(2,1)S(1)} %shard_map.142.refs_12_.refs_1_), channel_id=1, source_target_pairs={{0,4},{1,3},{2,6},{3,1},{4,0},{5,7},{6,2},{7,5},{8,12},{9,11},{10,... | collective-permute-start | bytes 1572872 | tf_op jit(solution)/shard_map/ppermute | solution.py:121
  31.4 19.9 %collective-permute-start.14 = (bf16[4,16,4096]{2,1,0:T(8,128)(2,1)S(1)}, bf16[4,16,4096]{2,1,0:T(8,128)(2,1)S(1)}, u32[]{:S(2)}, u32[]{:S(2)}) collective-permute-start(bf16[4,16,4096]{2,1,0:T(8,128)(2,1)S(1)} %shard_map.142.refs_12_.refs_1_), channel_id=1, source_target_pairs={{0,2},{1,5},{2,0},{3,7},{4,6},{5,1},{6,4},{7,3},{8,10},{9,13},{10,... | collective-permute-start | bytes 1572872 | tf_op jit(solution)/shard_map/ppermute | solution.py:121
  33.8 9.3 %collective-permute-start.11 = (bf16[4,16,2048]{2,1,0:T(8,128)(2,1)S(1)}, bf16[4,16,2048]{2,1,0:T(8,128)(2,1)S(1)}, u32[]{:S(2)}, u32[]{:S(2)}) collective-permute-start(bf16[4,16,2048]{2,1,0:T(8,128)(2,1)S(1)} %collective-permute-done.6.refs_3_), channel_id=1, source_target_pairs={{0,1},{1,0},{2,3},{3,2},{4,5},{5,4},{6,7},{7,6},{8,9},{9,8},{10,11... | collective-permute-start | bytes 786440 | tf_op jit(solution)/shard_map/ppermute | solution.py:121
  42.5 1.5 %collective-permute-start.10 = (bf16[4,16,2048]{2,1,0:T(8,128)(2,1)S(1)}, bf16[4,16,2048]{2,1,0:T(8,128)(2,1)S(1)}, u32[]{:S(2)}, u32[]{:S(2)}) collective-permute-start(bf16[4,16,2048]{2,1,0:T(8,128)(2,1)S(1)} %collective-permute-done.5.refs_2_), channel_id=1, source_target_pairs={{0,1},{1,0},{2,3},{3,2},{4,5},{5,4},{6,7},{7,6},{8,9},{9,8},{10,11... | collective-permute-start | bytes 786440 | tf_op jit(solution)/shard_map/ppermute | solution.py:121
  42.5 1.9 %collective-permute-start.9 = (bf16[4,16,2048]{2,1,0:T(8,128)(2,1)S(1)}, bf16[4,16,2048]{2,1,0:T(8,128)(2,1)S(1)}, u32[]{:S(2)}, u32[]{:S(2)}) collective-permute-start(bf16[4,16,2048]{2,1,0:T(8,128)(2,1)S(1)} %shard_map.141.refs_1_), channel_id=1, source_target_pairs={{0,1},{1,0},{2,3},{3,2},{4,5},{5,4},{6,7},{7,6},{8,9},{9,8},{10,11... | collective-permute-start | bytes 786440 | tf_op jit(solution)/shard_map/ppermute | solution.py:121
  43.1 10.3 %collective-permute-start.18 = (bf16[4,16,4096]{2,1,0:T(8,128)(2,1)S(1)}, bf16[4,16,4096]{2,1,0:T(8,128)(2,1)S(1)}, u32[]{:S(2)}, u32[]{:S(2)}) collective-permute-start(bf16[4,16,4096]{2,1,0:T(8,128)(2,1)S(1)} %shard_map.142.refs_12_.refs_1_), channel_id=1, source_target_pairs={{0,1},{1,0},{2,3},{3,2},{4,5},{5,4},{6,7},{7,6},{8,9},{9,8},{10,11... | collective-permute-start | bytes 1572872 | tf_op jit(solution)/shard_map/ppermute | solution.py:121
  51.3 9.4 %collective-permute-start.19 = (bf16[4,16,4096]{2,1,0:T(8,128)(2,1)S(1)}, bf16[4,16,4096]{2,1,0:T(8,128)(2,1)S(1)}, u32[]{:S(2)}, u32[]{:S(2)}) collective-permute-start(bf16[4,16,4096]{2,1,0:T(8,128)(2,1)S(1)} %collective-permute-done.14.refs_2_), channel_id=1, source_target_pairs={{0,1},{1,0},{2,3},{3,2},{4,5},{5,4},{6,7},{7,6},{8,9},{9,8},{10,11... | collective-permute-start | bytes 1572872 | tf_op jit(solution)/shard_map/ppermute | solution.py:121
  51.5 9.2 %collective-permute-start.20 = (bf16[4,16,4096]{2,1,0:T(8,128)(2,1)S(1)}, bf16[4,16,4096]{2,1,0:T(8,128)(2,1)S(1)}, u32[]{:S(2)}, u32[]{:S(2)}) collective-permute-start(bf16[4,16,4096]{2,1,0:T(8,128)(2,1)S(1)} %collective-permute-done.15.refs_3_), channel_id=1, source_target_pairs={{0,1},{1,0},{2,3},{3,2},{4,5},{5,4},{6,7},{7,6},{8,9},{9,8},{10,11... | collective-permute-start | bytes 1572872 | tf_op jit(solution)/shard_map/ppermute | solution.py:121
  52.0 8.7 %collective-permute-start.16 = (bf16[2,16,4096]{2,1,0:T(8,128)(2,1)S(1)}, bf16[2,16,4096]{2,1,0:T(8,128)(2,1)S(1)}, u32[]{:S(2)}, u32[]{:S(2)}) collective-permute-start(bf16[2,16,4096]{2,1,0:T(8,128)(2,1)S(1)} %slice.39), channel_id=1, source_target_pairs={{0,4},{1,3},{2,6},{3,1},{4,0},{5,7},{6,2},{7,5},{8,12},{9,11},{10,... | collective-permute-start | bytes 786440 | tf_op jit(solution)/shard_map/ppermute | solution.py:121
  52.6 8.1 %collective-permute-start.17 = (bf16[2,16,4096]{2,1,0:T(8,128)(2,1)S(1)}, bf16[2,16,4096]{2,1,0:T(8,128)(2,1)S(1)}, u32[]{:S(2)}, u32[]{:S(2)}) collective-permute-start(bf16[2,16,4096]{2,1,0:T(8,128)(2,1)S(1)} %slice.40), channel_id=1, source_target_pairs={{0,2},{1,5},{2,0},{3,7},{4,6},{5,1},{6,4},{7,3},{8,10},{9,13},{10,... | collective-permute-start | bytes 786440 | tf_op jit(solution)/shard_map/ppermute | solution.py:121
  53.4 19.1 %collective-permute-start.25 = (bf16[4,16,6144]{2,1,0:T(8,128)(2,1)S(1)}, bf16[4,16,6144]{2,1,0:T(8,128)(2,1)S(1)}, u32[]{:S(2)}, u32[]{:S(2)}) collective-permute-start(bf16[4,16,6144]{2,1,0:T(8,128)(2,1)S(1)} %shard_map.144.refs_13_.refs_0_), channel_id=1, source_target_pairs={{0,8},{1,9},{2,10},{3,11},{4,12},{5,13},{6,14},{7,15},{8,0},{9,1},... | collective-permute-start | bytes 2359304 | tf_op jit(solution)/shard_map/ppermute | solution.py:121
  60.7 2.0 %collective-permute-start.21 = (bf16[4,16,4096]{2,1,0:T(8,128)(2,1)S(1)}, bf16[4,16,4096]{2,1,0:T(8,128)(2,1)S(1)}, u32[]{:S(2)}, u32[]{:S(2)}) collective-permute-start(bf16[4,16,4096]{2,1,0:T(8,128)(2,1)S(1)} %shard_map.146.refs_4_), channel_id=1, source_target_pairs={{0,1},{1,0},{2,3},{3,2},{4,5},{5,4},{6,7},{7,6},{8,9},{9,8},{10,11... | collective-permute-start | bytes 1572872 | tf_op jit(solution)/shard_map/ppermute | solution.py:121
  72.6 2.9 %collective-permute-start.28 = (bf16[4,16,6144]{2,1,0:T(8,128)(2,1)S(1)}, bf16[4,16,6144]{2,1,0:T(8,128)(2,1)S(1)}, u32[]{:S(2)}, u32[]{:S(2)}) collective-permute-start(bf16[4,16,6144]{2,1,0:T(8,128)(2,1)S(1)} %get-tuple-element.57.refs_2_.refs_1_), channel_id=1, source_target_pairs={{0,1},{1,0},{2,3},{3,2},{4,5},{5,4},{6,7},{7,6},{8,9},{9,8},{10,11... | collective-permute-start | bytes 2359304 | tf_op jit(solution)/shard_map/ppermute | solution.py:121
  72.7 27.0 %collective-permute-start.26 = (bf16[4,16,6144]{2,1,0:T(8,128)(2,1)S(1)}, bf16[4,16,6144]{2,1,0:T(8,128)(2,1)S(1)}, u32[]{:S(2)}, u32[]{:S(2)}) collective-permute-start(bf16[4,16,6144]{2,1,0:T(8,128)(2,1)S(1)} %get-tuple-element.57.refs_2_.refs_1_), channel_id=1, source_target_pairs={{0,4},{1,3},{2,6},{3,1},{4,0},{5,7},{6,2},{7,5},{8,12},{9,11},{10,... | collective-permute-start | bytes 2359304 | tf_op jit(solution)/shard_map/ppermute | solution.py:121
  74.1 25.6 %collective-permute-start.27 = (bf16[4,16,6144]{2,1,0:T(8,128)(2,1)S(1)}, bf16[4,16,6144]{2,1,0:T(8,128)(2,1)S(1)}, u32[]{:S(2)}, u32[]{:S(2)}) collective-permute-start(bf16[4,16,6144]{2,1,0:T(8,128)(2,1)S(1)} %get-tuple-element.58.refs_3_.refs_2_), channel_id=1, source_target_pairs={{0,2},{1,5},{2,0},{3,7},{4,6},{5,1},{6,4},{7,3},{8,10},{9,13},{10,... | collective-permute-start | bytes 2359304 | tf_op jit(solution)/shard_map/ppermute | solution.py:121
  75.5 24.1 %collective-permute-start.29 = (bf16[4,16,6144]{2,1,0:T(8,128)(2,1)S(1)}, bf16[4,16,6144]{2,1,0:T(8,128)(2,1)S(1)}, u32[]{:S(2)}, u32[]{:S(2)}) collective-permute-start(bf16[4,16,6144]{2,1,0:T(8,128)(2,1)S(1)} %get-tuple-element.58.refs_3_.refs_2_), channel_id=1, source_target_pairs={{0,1},{1,0},{2,3},{3,2},{4,5},{5,4},{6,7},{7,6},{8,9},{9,8},{10,11... | collective-permute-start | bytes 2359304 | tf_op jit(solution)/shard_map/ppermute | solution.py:121
  75.5 2.4 %collective-permute-start.22 = (bf16[2,36,512]{2,1,0:T(8,128)(2,1)S(1)}, bf16[2,36,512]{2,1,0:T(8,128)(2,1)S(1)}, u32[]{:S(2)}, u32[]{:S(2)}) collective-permute-start(bf16[2,36,512]{2,1,0:T(8,128)(2,1)S(1)} %get-tuple-element.48.refs_2_), channel_id=1, source_target_pairs={{1,0},{0,1},{3,2},{2,3},{5,4},{4,5},{7,6},{6,7},{9,8},{8,9},{11,10... | collective-permute-start | bytes 221192 | tf_op jit(solution)/shard_map/ppermute | solution.py:387
  77.9 21.7 %collective-permute-start.23 = (bf16[8,36,512]{2,1,0:T(8,128)(2,1)S(1)}, bf16[8,36,512]{2,1,0:T(8,128)(2,1)S(1)}, u32[]{:S(2)}, u32[]{:S(2)}) collective-permute-start(bf16[8,36,512]{2,1,0:T(8,128)(2,1)S(1)} %shard_map.149), channel_id=1, source_target_pairs={{2,0},{3,1},{4,2},{5,3},{6,4},{7,5},{8,6},{9,7},{10,8},{11,9},{12,... | collective-permute-start | bytes 884744 | tf_op jit(solution)/shard_map/ppermute | solution.py:387
  86.5 16.8 %copy-start.4 = (f32[144,256]{1,0:T(8,128)S(1)}, f32[144,256]{1,0:T(8,128)}, u32[]{:S(2)}) copy-start(f32[144,256]{1,0:T(8,128)} %constant.10.clone.refs_13_) | copy-start | bytes 442372
  99.6 3.7 %collective-permute-start.30 = (bf16[4,16,6144]{2,1,0:T(8,128)(2,1)S(1)}, bf16[4,16,6144]{2,1,0:T(8,128)(2,1)S(1)}, u32[]{:S(2)}, u32[]{:S(2)}) collective-permute-start(bf16[4,16,6144]{2,1,0:T(8,128)(2,1)S(1)} %collective-permute-done.26.refs_4_.refs_3_), channel_id=1, source_target_pairs={{0,1},{1,0},{2,3},{3,2},{4,5},{5,4},{6,7},{7,6},{8,9},{9,8},{10,11... | collective-permute-start | bytes 2359304 | tf_op jit(solution)/shard_map/ppermute | solution.py:121
  99.7 3.6 %collective-permute-start.31 = (bf16[4,16,6144]{2,1,0:T(8,128)(2,1)S(1)}, bf16[4,16,6144]{2,1,0:T(8,128)(2,1)S(1)}, u32[]{:S(2)}, u32[]{:S(2)}) collective-permute-start(bf16[4,16,6144]{2,1,0:T(8,128)(2,1)S(1)} %collective-permute-done.27.refs_5_.refs_4_), channel_id=1, source_target_pairs={{0,1},{1,0},{2,3},{3,2},{4,5},{5,4},{6,7},{7,6},{8,9},{9,8},{10,11... | collective-permute-start | bytes 2359304 | tf_op jit(solution)/shard_map/ppermute | solution.py:121
  100.2 3.0 %collective-permute-start.24 = (bf16[2,36,512]{2,1,0:T(8,128)(2,1)S(1)}, bf16[2,36,512]{2,1,0:T(8,128)(2,1)S(1)}, u32[]{:S(2)}, u32[]{:S(2)}) collective-permute-start(bf16[2,36,512]{2,1,0:T(8,128)(2,1)S(1)} %get-tuple-element.53), channel_id=1, source_target_pairs={{1,0},{0,1},{3,2},{2,3},{5,4},{4,5},{7,6},{6,7},{9,8},{8,9},{11,10... | collective-permute-start | bytes 221192 | tf_op jit(solution)/shard_map/ppermute | solution.py:387
  115.1 1.3 collective-permute-start.32
  116.5 15.6 %collective-permute-start.33 = (bf16[8,36,512]{2,1,0:T(8,128)(2,1)S(1)}, bf16[8,36,512]{2,1,0:T(8,128)(2,1)S(1)}, u32[]{:S(2)}, u32[]{:S(2)}) collective-permute-start(bf16[8,36,512]{2,1,0:T(8,128)(2,1)S(1)} %shard_map.154), channel_id=1, source_target_pairs={{30,0},{31,1},{0,2},{1,3},{2,4},{3,5},{4,6},{5,7},{6,8},{7,9},{8,1... | collective-permute-start | bytes 884744 | tf_op jit(solution)/shard_map/ppermute | solution.py:387
  130.7 1.3 collective-permute-start.34

commit v19 on v17

--- a/solution.py
+++ b/solution.py
@@ -465,11 +465,15 @@
         middle_0 = attention(0, [windows], (0,), pieces, (feed_column,))
         first, second = tied((received[0][:2], received[1][2:]), (middle_0, last_across))
         corners = [send(first, across), send(second, beside)]
-        (last_four,) = join([[last_own, last_beside, last_other, last_across]], (), (middle_0,))
+        last_four, final_four = join(
+            [[last_own, last_beside, last_other, last_across]], (), (middle_0,), widths
+        )
         middle_1 = attention(0, [windows], (1,), pieces, (middle_0, last_four))
-        last_other = across_z(last_four, 1)
+        last_other, final_other = across_z(last_four, 1), across_z(final_four, 1)
+        last_columns = list(halves(last_four, last_other, widths[:1], (middle_1,)))
+        last_received = [send(part, way) for part, way in zip(last_columns, (across, beside))]
         swapped = [send(part, swap) for part in [feed_column] + tied(received, middle_0)]
-        received += join([tied(corners, (middle_1, *swapped))])
+        received += join([tied(corners, (middle_1, last_other, *swapped))])
         feed_pieces = "columns", [feed_column] + received + swapped + [send(received[2], swap)]
     else:
         gathered = []
@@ -478,19 +482,17 @@
                 chunk = jnp.concatenate([weight[block] for weight in pair], 1)
                 gathered.append(lax.all_gather(chunk, "lon", axis=0, tiled=True))
         pieces, feed_pieces, last_pieces, final_pieces = (("rows", [rows]) for rows in gathered)
+        last_columns = ()
         middle_0 = attention(0, [windows], (0,), pieces)
         middle_1 = attention(0, [windows], (1,), pieces)
-    left_0, right_0, low_0 = forward(0, middle_0, 0, feed_pieces, low_edge)
+    left_0, right_0, low_0 = forward(0, middle_0, 0, feed_pieces, low_edge, last_columns)
     below_0 = shift_from(low_0, 0, 1)
     size = left_0.shape[0]
     (ahead,) = strips([left_0, below_0], [[(0, 1, size - 1), (1, 0, 1)]])
     ahead = shift_from(ahead, 1, 0)
     after = (below_0,)
     if relay:
-        columns = halves(last_four, last_other, widths, (low_0,))
-        last_columns, final_columns = list(columns[:2]), list(columns[2:])
-        last_received = [send(part, way) for part, way in zip(last_columns, (across, beside))]
-        after += (last_columns[0],)
+        final_columns = list(halves(final_four, final_other, widths[1:], (low_0,)))
     left_1, right_1, low_1 = forward(0, middle_1, 0, feed_pieces, low_edge, after)
     below_1 = shift_from(tied(low_1, ahead), 0, 1)
     if relay:
@@ -499,7 +501,7 @@
         last_pieces = "halves", last_pieces
         final_received = [
             send(part, way)
-            for part, way in zip(tied(final_columns, last_received), (across, beside))
+            for part, way in zip(tied(final_columns, ahead), (across, beside))
         ]
     lefts = strips(
         [right_0, left_1, right_1, below_0, below_1],

time: 129 us -> 131 us (1.016)
  starting transfers between devices: 37 us -> 41.2 us
  waiting for transfers between devices: 36.2 us -> 33.4 us
    ppermute x35 -> x36, waiting for transfers between devices: 29.9 us -> 27.1 us  [send(): return lax.ppermute(block, ('lon', 'lat'), pairs)]
    ppermute x6, starting transfers between devices: 6.33 us -> 8.94 us  [shift_from(): return lax.ppermute(block, ('lon', 'lat'), pairs)]
    ppermute x35 -> x36, starting transfers between devices: 30.7 us -> 32.2 us  [send(): return lax.ppermute(block, ('lon', 'lat'), pairs)]
  transfers between devices with their start and end apart: 41 -> 42, of which waited for: 15 -> 15; matrix products, arithmetic and copies ran while one was open for 1% -> 1% of each run, Pallas kernels for 33% -> 29%
where the time goes in v19:
time: 131 us; the launch traced here: 130 us
  Pallas kernels  47.5 us (36%)
  starting transfers between devices  41.2 us (31%)
  waiting for transfers between devices  33.4 us (25%)
  local copies, waits for them, and re-layouts  7.64 us (6%)
    ppermute x36, starting transfers between devices, send(): return lax.ppermute(block, ('lon', 'lat'), pairs)  32.2 us
    pallas_call x4, Pallas kernels, attend(): pl.pallas_call(functools.partial(attend_kernel, shifted, row_windows, kin...  27.6 us
    ppermute x36, waiting for transfers between devices, send(): return lax.ppermute(block, ('lon', 'lat'), pairs)  27.1 us
    pallas_call x4, Pallas kernels, feed(): pl.pallas_call(functools.partial(feed_kernel, kind, len(pieces), hidden_s...  19.4 us
    ppermute x6, starting transfers between devices, shift_from(): return lax.ppermute(block, ('lon', 'lat'), pairs)  8.94 us
    ppermute x6, waiting for transfers between devices, shift_from(): return lax.ppermute(block, ('lon', 'lat'), pairs)  6.36 us
    unnamed x20, local copies, waits for them, and re-layouts  3.7 us
  transfers between devices with their start and end apart: 42, of which 15 were waited for; matrix products, arithmetic and copies ran while one was open for 1% of the time, Pallas kernels for 29%

profile of v19, /device:TPU:0, one launch (start us, length us, event | category | flops | bytes accessed | tf_op | source)
XLA Modules:
  0.0 130.1 jit_solution(5807372531689446954)
XLA Ops:
  0.0 0.9 copy-done.2
  0.9 0.8 copy-done.3
  1.8 4.0 %collective-permute-start = (bf16[1,16,2048]{2,1,0:T(8,128)(2,1)S(1)}, bf16[1,16,2048]{2,1,0:T(8,128)(2,1)S(1)}, u32[]{:S(2)}, u32[]{:S(2)}) collective-permute-start(bf16[1,16,2048]{2,1,0:T(8,128)(2,1)S(1)} %shard_map.136.refs_0_.refs_6_), channel_id=1, source_target_pairs={{0,16},{1,17},{2,18},{3,19},{4,20},{5,21},{6,22},{7,23},{8,24},{9,... | collective-permute-start | bytes 196616 | tf_op jit(solution)/shard_map/ppermute | solution.py:121
  5.8 0.9 copy-done
  6.8 0.9 copy-done.1
  7.7 1.6 %collective-permute-start.3 = (bf16[1,16,6144]{2,1,0:T(8,128)(2,1)S(1)}, bf16[1,16,6144]{2,1,0:T(8,128)(2,1)S(1)}, u32[]{:S(2)}, u32[]{:S(2)}) collective-permute-start(bf16[1,16,6144]{2,1,0:T(8,128)(2,1)S(1)} %get-tuple-element.46.refs_0_), channel_id=1, source_target_pairs={{0,2},{1,5},{2,0},{3,7},{4,6},{5,1},{6,4},{7,3},{8,10},{9,13},{10,... | collective-permute-start | bytes 589832 | tf_op jit(solution)/shard_map/ppermute | solution.py:121
  9.3 0.3 collective-permute-start.2
  9.6 0.8 copy.26
  10.5 0.5 reshape.15.refs_2_.refs_0_
  11.0 1.6 %collective-permute-start.1 = (bf16[2,16,2048]{2,1,0:T(8,128)(2,1)S(1)}, bf16[2,16,2048]{2,1,0:T(8,128)(2,1)S(1)}, u32[]{:S(2)}, u32[]{:S(2)}) collective-permute-start(bf16[2,16,2048]{2,1,0:T(8,128)(2,1)S(1)} %shard_map.137.refs_0_), channel_id=1, source_target_pairs={{0,8},{1,9},{2,10},{3,11},{4,12},{5,13},{6,14},{7,15},{8,0},{9,1},... | collective-permute-start | bytes 393224 | tf_op jit(solution)/shard_map/ppermute | solution.py:121
  12.7 5.0 %collective-permute-done.2.refs_1_ = bf16[1,16,4096]{2,1,0:T(8,128)(2,1)S(1)} collective-permute-done((bf16[1,16,4096]{2,1,0:T(8,128)(2,1)S(1)}, bf16[1,16,4096]{2,1,0:T(8,128)(2,1)S(1)}, u32[]{:S(2)}, u32[]{:S(2)}) %collective-permute-start.2) | collective-permute-done | bytes 131104 | tf_op jit(solution)/shard_map/ppermute | solution.py:121
  17.8 1.6 %collective-permute-start.4 = (bf16[4,16,2048]{2,1,0:T(8,128)(2,1)S(1)}, bf16[4,16,2048]{2,1,0:T(8,128)(2,1)S(1)}, u32[]{:S(2)}, u32[]{:S(2)}) collective-permute-start(bf16[4,16,2048]{2,1,0:T(8,128)(2,1)S(1)} %shard_map.140.refs_1_), channel_id=1, source_target_pairs={{0,2},{1,5},{2,0},{3,7},{4,6},{5,1},{6,4},{7,3},{8,10},{9,13},{10,... | collective-permute-start | bytes 786440 | tf_op jit(solution)/shard_map/ppermute | solution.py:121
  19.4 1.4 %collective-permute-start.5 = (bf16[4,16,2048]{2,1,0:T(8,128)(2,1)S(1)}, bf16[4,16,2048]{2,1,0:T(8,128)(2,1)S(1)}, u32[]{:S(2)}, u32[]{:S(2)}) collective-permute-start(bf16[4,16,2048]{2,1,0:T(8,128)(2,1)S(1)} %shard_map.140.refs_1_), channel_id=1, source_target_pairs={{0,4},{1,3},{2,6},{3,1},{4,0},{5,7},{6,2},{7,5},{8,12},{9,11},{10,... | collective-permute-start | bytes 786440 | tf_op jit(solution)/shard_map/ppermute | solution.py:121
  20.7 0.6 collective-permute-start.6
  21.3 1.9 %collective-permute-start.7 = (bf16[1,16,6144]{2,1,0:T(8,128)(2,1)S(1)}, bf16[1,16,6144]{2,1,0:T(8,128)(2,1)S(1)}, u32[]{:S(2)}, u32[]{:S(2)}) collective-permute-start(bf16[1,16,6144]{2,1,0:T(8,128)(2,1)S(1)} %get-tuple-element.46.refs_0_), channel_id=1, source_target_pairs={{0,16},{1,17},{2,18},{3,19},{4,20},{5,21},{6,22},{7,23},{8,24},{9,... | collective-permute-start | bytes 589832 | tf_op jit(solution)/shard_map/ppermute | solution.py:121
  23.2 0.1 multiply_reduce_fusion
  23.3 2.5 %collective-permute-start.12 = (bf16[2,16,4096]{2,1,0:T(8,128)(2,1)S(1)}, bf16[2,16,4096]{2,1,0:T(8,128)(2,1)S(1)}, u32[]{:S(2)}, u32[]{:S(2)}) collective-permute-start(bf16[2,16,4096]{2,1,0:T(8,128)(2,1)S(1)} %shard_map.139.refs_2_.refs_0_), channel_id=1, source_target_pairs={{0,8},{1,9},{2,10},{3,11},{4,12},{5,13},{6,14},{7,15},{8,0},{9,1},... | collective-permute-start | bytes 786440 | tf_op jit(solution)/shard_map/ppermute | solution.py:121
  25.9 5.9 %collective-permute-done.7.refs_2_ = bf16[1,16,6144]{2,1,0:T(8,128)(2,1)S(1)} collective-permute-done((bf16[1,16,6144]{2,1,0:T(8,128)(2,1)S(1)}, bf16[1,16,6144]{2,1,0:T(8,128)(2,1)S(1)}, u32[]{:S(2)}, u32[]{:S(2)}) %collective-permute-start.7) | collective-permute-done | bytes 196640 | tf_op jit(solution)/shard_map/ppermute | solution.py:121
  31.7 0.5 collective-permute-start.9
  32.3 0.5 collective-permute-start.11
  32.8 0.6 collective-permute-done.12.refs_1_
  33.4 1.8 %collective-permute-start.13 = (bf16[4,16,4096]{2,1,0:T(8,128)(2,1)S(1)}, bf16[4,16,4096]{2,1,0:T(8,128)(2,1)S(1)}, u32[]{:S(2)}, u32[]{:S(2)}) collective-permute-start(bf16[4,16,4096]{2,1,0:T(8,128)(2,1)S(1)} %shard_map.141.refs_12_.refs_1_), channel_id=1, source_target_pairs={{0,2},{1,5},{2,0},{3,7},{4,6},{5,1},{6,4},{7,3},{8,10},{9,13},{10,... | collective-permute-start | bytes 1572872 | tf_op jit(solution)/shard_map/ppermute | solution.py:121
  35.2 0.4 collective-permute-start.14
  35.6 1.7 %collective-permute-start.15 = (bf16[1,16,6144]{2,1,0:T(8,128)(2,1)S(1)}, bf16[1,16,6144]{2,1,0:T(8,128)(2,1)S(1)}, u32[]{:S(2)}, u32[]{:S(2)}) collective-permute-start(bf16[1,16,6144]{2,1,0:T(8,128)(2,1)S(1)} %collective-permute-done.7.refs_2_), channel_id=1, source_target_pairs={{0,4},{1,3},{2,6},{3,1},{4,0},{5,7},{6,2},{7,5},{8,12},{9,11},{10,... | collective-permute-start | bytes 589832 | tf_op jit(solution)/shard_map/ppermute | solution.py:121
  37.3 6.9 %shard_map.142.refs_4_.refs_12_.refs_0_ = bf16[4,144,512]{2,1,0:T(8,128)(2,1)S(1)} custom-call(bf16[8,144,512]{2,1,0:T(8,128)(2,1)S(1)} %reshape.15.refs_2_.refs_0_, bf16[4,16,2048]{2,1,0:T(8,128)(2,1)S(1)} %shard_map.140.refs_1_, bf16[4,16,2048]{2,1,0:T(8,128)(2,1)S(1)} %collective-permute-done.4.refs_2_, ...), custom_call_target="tpu_custom_call" | custom-call | flops 8000000000 | bytes 6000000 | tf_op jit(solution)/shard_map/pallas_call | solution.py:300
  44.2 4.7 %collective-permute-done.15.refs_3_ = bf16[1,16,6144]{2,1,0:T(8,128)(2,1)S(1)} collective-permute-done((bf16[1,16,6144]{2,1,0:T(8,128)(2,1)S(1)}, bf16[1,16,6144]{2,1,0:T(8,128)(2,1)S(1)}, u32[]{:S(2)}, u32[]{:S(2)}) %collective-permute-start.15) | collective-permute-done | bytes 196640 | tf_op jit(solution)/shard_map/ppermute | solution.py:121
  49.0 0.7 collective-permute-start.18
  49.8 1.0 collective-permute-start.16
  50.8 1.1 collective-permute-start.17
  51.9 0.4 collective-permute-start.20
  52.3 0.1 collective-permute-start.21
  52.4 6.9 %shard_map.144.refs_2_.refs_0_ = bf16[4,144,512]{2,1,0:T(8,128)(2,1)S(1)} custom-call(bf16[8,144,512]{2,1,0:T(8,128)(2,1)S(1)} %reshape.15.refs_2_.refs_0_, bf16[4,16,2048]{2,1,0:T(8,128)(2,1)S(1)} %shard_map.140.refs_1_, bf16[4,16,2048]{2,1,0:T(8,128)(2,1)S(1)} %collective-permute-done.4.refs_2_, bf16[4,16,2048]{2,1,0:T(8,128)(2,1)S(1)} %collective-permute-done.5.refs_3_, ...), custom_call_target="tpu_custom_call" | custom-call | flops 8000000000 | bytes 6000000 | tf_op jit(solution)/shard_map/pallas_call | solution.py:300
  59.4 0.5 collective-permute-start.22
  59.9 1.5 %collective-permute-done.22.refs_8_ = bf16[4,16,4096]{2,1,0:T(8,128)(2,1)S(1)} collective-permute-done((bf16[4,16,4096]{2,1,0:T(8,128)(2,1)S(1)}, bf16[4,16,4096]{2,1,0:T(8,128)(2,1)S(1)}, u32[]{:S(2)}, u32[]{:S(2)}) %collective-permute-start.22) | collective-permute-done | bytes 524320 | tf_op jit(solution)/shard_map/ppermute | solution.py:121
  61.4 4.8 %shard_map.147 = (bf16[8,36,512]{2,1,0:T(8,128)(2,1)S(1)}, bf16[8,36,512]{2,1,0:T(8,128)(2,1)S(1)}, bf16[2,36,512]{2,1,0:T(8,128)(2,1)S(1)}) custom-call(bf16[4,144,512]{2,1,0:T(8,128)(2,1)S(1)} %shard_map.142.refs_4_.refs_12_.refs_0_, bf16[4,16,4096]{2,1,0:T(8,128)(2,1)S(1)} %shard_map.141.refs_12_.refs_1_, ...), custom_call_target="tpu_custom_call" | custom-call | flops 1000000 | bytes 100000 | tf_op jit(solution)/shard_map/pallas_call | solution.py:358
  66.2 0.4 collective-permute-start.23
  66.7 1.4 %collective-permute-start.32 = (bf16[4,16,4096]{2,1,0:T(8,128)(2,1)S(1)}, bf16[4,16,4096]{2,1,0:T(8,128)(2,1)S(1)}, u32[]{:S(2)}, u32[]{:S(2)}) collective-permute-start(bf16[4,16,4096]{2,1,0:T(8,128)(2,1)S(1)} %get-tuple-element.68.refs_0_), channel_id=1, source_target_pairs={{0,8},{1,9},{2,10},{3,11},{4,12},{5,13},{6,14},{7,15},{8,0},{9,1},... | collective-permute-start | bytes 1572872 | tf_op jit(solution)/shard_map/ppermute | solution.py:121
  68.1 5.1 %collective-permute-start.24 = (bf16[8,36,512]{2,1,0:T(8,128)(2,1)S(1)}, bf16[8,36,512]{2,1,0:T(8,128)(2,1)S(1)}, u32[]{:S(2)}, u32[]{:S(2)}) collective-permute-start(bf16[8,36,512]{2,1,0:T(8,128)(2,1)S(1)} %shard_map.149), channel_id=1, source_target_pairs={{2,0},{3,1},{4,2},{5,3},{6,4},{7,5},{8,6},{9,7},{10,8},{11,9},{12,... | collective-permute-start | bytes 884744 | tf_op jit(solution)/shard_map/ppermute | solution.py:385
  73.2 4.9 %shard_map.148 = (bf16[8,36,512]{2,1,0:T(8,128)(2,1)S(1)}, bf16[8,36,512]{2,1,0:T(8,128)(2,1)S(1)}, bf16[2,36,512]{2,1,0:T(8,128)(2,1)S(1)}) custom-call(bf16[4,144,512]{2,1,0:T(8,128)(2,1)S(1)} %shard_map.144.refs_2_.refs_0_, bf16[4,16,4096]{2,1,0:T(8,128)(2,1)S(1)} %shard_map.141.refs_12_.refs_1_, ...), custom_call_target="tpu_custom_call" | custom-call | flops 1000000 | bytes 100000 | tf_op jit(solution)/shard_map/pallas_call | solution.py:358
  78.1 3.1 %collective-permute-done.26.refs_4_ = bf16[4,16,2048]{2,1,0:T(8,128)(2,1)S(1)} collective-permute-done((bf16[4,16,2048]{2,1,0:T(8,128)(2,1)S(1)}, bf16[4,16,2048]{2,1,0:T(8,128)(2,1)S(1)}, u32[]{:S(2)}, u32[]{:S(2)}) %collective-permute-start.26) | collective-permute-done | bytes 262176 | tf_op jit(solution)/shard_map/ppermute | solution.py:121
  81.2 1.3 collective-permute-start.29
  82.5 1.0 collective-permute-done.27.refs_5_
  83.5 3.1 %collective-permute-done.24.refs_1_ = bf16[8,36,512]{2,1,0:T(8,128)(2,1)S(1)} collective-permute-done((bf16[8,36,512]{2,1,0:T(8,128)(2,1)S(1)}, bf16[8,36,512]{2,1,0:T(8,128)(2,1)S(1)}, u32[]{:S(2)}, u32[]{:S(2)}) %collective-permute-start.24) | collective-permute-done | bytes 294944 | tf_op jit(solution)/shard_map/ppermute | solution.py:385
  86.6 0.5 collective-permute-start.25
  87.1 1.1 collective-permute-done.25.refs_4_
  88.2 0.1 collective-permute-start.35
  88.4 0.4 collective-permute-start.36
  88.9 4.0 %collective-permute-start.34 = (bf16[4,16,4096]{2,1,0:T(8,128)(2,1)S(1)}, bf16[4,16,4096]{2,1,0:T(8,128)(2,1)S(1)}, u32[]{:S(2)}, u32[]{:S(2)}) collective-permute-start(bf16[4,16,4096]{2,1,0:T(8,128)(2,1)S(1)} %get-tuple-element.72.refs_2_), channel_id=1, source_target_pairs={{0,2},{1,5},{2,0},{3,7},{4,6},{5,1},{6,4},{7,3},{8,10},{9,13},{10,... | collective-permute-start | bytes 1572872 | tf_op jit(solution)/shard_map/ppermute | solution.py:121
  92.9 6.9 %shard_map.151.refs_0_ = bf16[4,144,512]{2,1,0:T(8,128)(2,1)S(1)} custom-call(bf16[8,36,512]{2,1,0:T(8,128)(2,1)S(1)} %get-tuple-element.65.refs_0_, bf16[8,36,512]{2,1,0:T(8,128)(2,1)S(1)} %collective-permute-done.24.refs_1_, bf16[4,16,2048]{2,1,0:T(8,128)(2,1)S(1)} %get-tuple-element.56.refs_10_.refs_2_, ...), custom_call_target="tpu_custom_call" | custom-call | flops 8000000000 | bytes 6000000 | tf_op jit(solution)/shard_map/pallas_call | solution.py:300
  99.8 2.6 %collective-permute-done.33.refs_3_ = bf16[4,16,4096]{2,1,0:T(8,128)(2,1)S(1)} collective-permute-done((bf16[4,16,4096]{2,1,0:T(8,128)(2,1)S(1)}, bf16[4,16,4096]{2,1,0:T(8,128)(2,1)S(1)}, u32[]{:S(2)}, u32[]{:S(2)}) %collective-permute-start.33) | collective-permute-done | bytes 524320 | tf_op jit(solution)/shard_map/ppermute | solution.py:121
  102.5 0.4 collective-permute-done.34.refs_4_
  102.8 0.7 collective-permute-start.37
  103.5 1.5 %collective-permute-done.37.refs_7_ = bf16[4,16,4096]{2,1,0:T(8,128)(2,1)S(1)} collective-permute-done((bf16[4,16,4096]{2,1,0:T(8,128)(2,1)S(1)}, bf16[4,16,4096]{2,1,0:T(8,128)(2,1)S(1)}, u32[]{:S(2)}, u32[]{:S(2)}) %collective-permute-start.37) | collective-permute-done | bytes 524320 | tf_op jit(solution)/shard_map/ppermute | solution.py:121
  105.0 0.7 collective-permute-done.38.refs_8_
  105.8 4.8 %shard_map.153 = (bf16[8,36,512]{2,1,0:T(8,128)(2,1)S(1)}, bf16[8,36,512]{2,1,0:T(8,128)(2,1)S(1)}, bf16[2,36,512]{2,1,0:T(8,128)(2,1)S(1)}) custom-call(bf16[4,144,512]{2,1,0:T(8,128)(2,1)S(1)} %shard_map.151.refs_0_, bf16[4,16,4096]{2,1,0:T(8,128)(2,1)S(1)} %get-tuple-element.71.refs_1_, bf16[4,16,4096]{2,1,0:T(8,128)(2,1)S(1)} %get-tuple-element.72.refs_2_, ...), custom_call_target="tpu_custom_call" | custom-call | flops 1000000 | bytes 100000 | tf_op jit(solution)/shard_map/pallas_call | solution.py:358
  110.6 0.4 collective-permute-start.39
  111.0 0.9 collective-permute-done.39.refs_0_.refs_14_.refs_5_
  112.0 2.4 %collective-permute-start.40 = (bf16[8,36,512]{2,1,0:T(8,128)(2,1)S(1)}, bf16[8,36,512]{2,1,0:T(8,128)(2,1)S(1)}, u32[]{:S(2)}, u32[]{:S(2)}) collective-permute-start(bf16[8,36,512]{2,1,0:T(8,128)(2,1)S(1)} %shard_map.154), channel_id=1, source_target_pairs={{30,0},{31,1},{0,2},{1,3},{2,4},{3,5},{4,6},{5,7},{6,8},{7,9},{8,1... | collective-permute-start | bytes 884744 | tf_op jit(solution)/shard_map/ppermute | solution.py:385
  114.3 6.9 %shard_map.155.refs_0_ = bf16[4,144,512]{2,1,0:T(8,128)(2,1)S(1)} custom-call(bf16[8,36,512]{2,1,0:T(8,128)(2,1)S(1)} %get-tuple-element.77.refs_0_, bf16[8,36,512]{2,1,0:T(8,128)(2,1)S(1)} %get-tuple-element.78.refs_1_, bf16[4,16,2048]{2,1,0:T(8,128)(2,1)S(1)} %get-tuple-element.56.refs_10_.refs_2_, ...), custom_call_target="tpu_custom_call" | custom-call | flops 8000000000 | bytes 6000000 | tf_op jit(solution)/shard_map/pallas_call | solution.py:300
  121.2 4.9 %shard_map.156 = (bf16[8,36,512]{2,1,0:T(8,128)(2,1)S(1)}, bf16[8,36,512]{2,1,0:T(8,128)(2,1)S(1)}, bf16[2,36,512]{2,1,0:T(8,128)(2,1)S(1)}) custom-call(bf16[4,144,512]{2,1,0:T(8,128)(2,1)S(1)} %shard_map.155.refs_0_, bf16[4,16,4096]{2,1,0:T(8,128)(2,1)S(1)} %get-tuple-element.71.refs_1_, bf16[4,16,4096]{2,1,0:T(8,128)(2,1)S(1)} %get-tuple-element.72.refs_2_, ...), custom_call_target="tpu_custom_call" | custom-call | flops 1000000 | bytes 100000 | tf_op jit(solution)/shard_map/pallas_call | solution.py:358
  126.2 1.3 collective-permute-done.41.refs_4_
  127.5 0.1 shard_map.157
  127.5 0.4 copy.23
  127.9 2.2 %copy.24 = bf16[4,6,8,3,2,512]{5,4,3,2,1,0:T(2,128)(2,1)} copy(bf16[4,6,8,3,2,512]{5,2,0,4,3,1:T(8,128)(2,1)S(1)} %bitcast.16) | data formatting | bytes 2359296 | tf_op jit(solution)/shard_map/transpose | solution.py:423
  (71 shorter events, 0.7 us)
Async XLA Ops:
  0.0 0.9 copy-start.2
  0.9 0.8 copy-start.3
  1.8 9.2 %collective-permute-start = (bf16[1,16,2048]{2,1,0:T(8,128)(2,1)S(1)}, bf16[1,16,2048]{2,1,0:T(8,128)(2,1)S(1)}, u32[]{:S(2)}, u32[]{:S(2)}) collective-permute-start(bf16[1,16,2048]{2,1,0:T(8,128)(2,1)S(1)} %shard_map.136.refs_0_.refs_6_), channel_id=1, source_target_pairs={{0,16},{1,17},{2,18},{3,19},{4,20},{5,21},{6,22},{7,23},{8,24},{9,... | collective-permute-start | bytes 196616 | tf_op jit(solution)/shard_map/ppermute | solution.py:121
  5.8 0.9 copy-start
  6.8 0.9 copy-start.1
  7.7 1.9 %copy-start.6 = (bf16[24,24,2,512]{3,2,1,0:T(2,128)(2,1)S(1)}, bf16[24,24,2,512]{3,2,1,0:T(2,128)(2,1)}, u32[]{:S(2)}) copy-start(bf16[24,24,2,512]{3,2,1,0:T(2,128)(2,1)} %param.14) | copy-start | bytes 3538948
  7.7 10.0 %collective-permute-start.3 = (bf16[1,16,6144]{2,1,0:T(8,128)(2,1)S(1)}, bf16[1,16,6144]{2,1,0:T(8,128)(2,1)S(1)}, u32[]{:S(2)}, u32[]{:S(2)}) collective-permute-start(bf16[1,16,6144]{2,1,0:T(8,128)(2,1)S(1)} %get-tuple-element.46.refs_0_), channel_id=1, source_target_pairs={{0,2},{1,5},{2,0},{3,7},{4,6},{5,1},{6,4},{7,3},{8,10},{9,13},{10,... | collective-permute-start | bytes 589832 | tf_op jit(solution)/shard_map/ppermute | solution.py:121
  9.3 8.4 %collective-permute-start.2 = (bf16[1,16,4096]{2,1,0:T(8,128)(2,1)S(1)}, bf16[1,16,4096]{2,1,0:T(8,128)(2,1)S(1)}, u32[]{:S(2)}, u32[]{:S(2)}) collective-permute-start(bf16[1,16,4096]{2,1,0:T(8,128)(2,1)S(1)} %get-tuple-element.44.refs_0_), channel_id=1, source_target_pairs={{0,16},{1,17},{2,18},{3,19},{4,20},{5,21},{6,22},{7,23},{8,24},{9,... | collective-permute-start | bytes 393224 | tf_op jit(solution)/shard_map/ppermute | solution.py:121
  11.0 12.3 %copy-start.7 = (f32[16,512]{1,0:T(8,128)S(1)}, f32[16,512]{1,0:T(8,128)}, u32[]{:S(2)}) copy-start(f32[16,512]{1,0:T(8,128)} %constant.8.clone) | copy-start | bytes 98308
  11.0 12.3 %copy-start.9 = (f32[2,16]{1,0:T(2,128)S(1)}, f32[2,16]{1,0:T(2,128)}, u32[]{:S(2)}) copy-start(f32[2,16]{1,0:T(2,128)} %param.20) | copy-start | bytes 388
  11.0 21.8 %copy-start.8 = (f32[2,2,512]{2,1,0:T(2,128)S(1)}, f32[2,2,512]{2,1,0:T(2,128)}, u32[]{:S(2)}) copy-start(f32[2,2,512]{2,1,0:T(2,128)} %param.19) | copy-start | bytes 24580
  11.0 6.7 %collective-permute-start.1 = (bf16[2,16,2048]{2,1,0:T(8,128)(2,1)S(1)}, bf16[2,16,2048]{2,1,0:T(8,128)(2,1)S(1)}, u32[]{:S(2)}, u32[]{:S(2)}) collective-permute-start(bf16[2,16,2048]{2,1,0:T(8,128)(2,1)S(1)} %shard_map.137.refs_0_), channel_id=1, source_target_pairs={{0,8},{1,9},{2,10},{3,11},{4,12},{5,13},{6,14},{7,15},{8,0},{9,1},... | collective-permute-start | bytes 393224 | tf_op jit(solution)/shard_map/ppermute | solution.py:121
  17.7 19.6 %copy-start.4 = (bf16[640,256]{1,0:T(8,128)(2,1)S(1)}, bf16[640,256]{1,0:T(8,128)(2,1)}, u32[]{:S(2)}) copy-start(bf16[640,256]{1,0:T(8,128)(2,1)} %constant.9.clone.refs_11_.refs_12_) | copy-start | bytes 983044
  17.8 13.9 %collective-permute-start.4 = (bf16[4,16,2048]{2,1,0:T(8,128)(2,1)S(1)}, bf16[4,16,2048]{2,1,0:T(8,128)(2,1)S(1)}, u32[]{:S(2)}, u32[]{:S(2)}) collective-permute-start(bf16[4,16,2048]{2,1,0:T(8,128)(2,1)S(1)} %shard_map.140.refs_1_), channel_id=1, source_target_pairs={{0,2},{1,5},{2,0},{3,7},{4,6},{5,1},{6,4},{7,3},{8,10},{9,13},{10,... | collective-permute-start | bytes 786440 | tf_op jit(solution)/shard_map/ppermute | solution.py:121
  19.4 12.9 %collective-permute-start.5 = (bf16[4,16,2048]{2,1,0:T(8,128)(2,1)S(1)}, bf16[4,16,2048]{2,1,0:T(8,128)(2,1)S(1)}, u32[]{:S(2)}, u32[]{:S(2)}) collective-permute-start(bf16[4,16,2048]{2,1,0:T(8,128)(2,1)S(1)} %shard_map.140.refs_1_), channel_id=1, source_target_pairs={{0,4},{1,3},{2,6},{3,1},{4,0},{5,7},{6,2},{7,5},{8,12},{9,11},{10,... | collective-permute-start | bytes 786440 | tf_op jit(solution)/shard_map/ppermute | solution.py:121
  20.7 11.5 %collective-permute-start.6 = (bf16[4,16,2048]{2,1,0:T(8,128)(2,1)S(1)}, bf16[4,16,2048]{2,1,0:T(8,128)(2,1)S(1)}, u32[]{:S(2)}, u32[]{:S(2)}) collective-permute-start(bf16[4,16,2048]{2,1,0:T(8,128)(2,1)S(1)} %shard_map.140.refs_1_), channel_id=1, source_target_pairs={{0,6},{1,7},{2,4},{3,5},{4,2},{5,3},{6,0},{7,1},{8,14},{9,15},{10,... | collective-permute-start | bytes 786440 | tf_op jit(solution)/shard_map/ppermute | solution.py:121
  21.3 10.4 %collective-permute-start.7 = (bf16[1,16,6144]{2,1,0:T(8,128)(2,1)S(1)}, bf16[1,16,6144]{2,1,0:T(8,128)(2,1)S(1)}, u32[]{:S(2)}, u32[]{:S(2)}) collective-permute-start(bf16[1,16,6144]{2,1,0:T(8,128)(2,1)S(1)} %get-tuple-element.46.refs_0_), channel_id=1, source_target_pairs={{0,16},{1,17},{2,18},{3,19},{4,20},{5,21},{6,22},{7,23},{8,24},{9,... | collective-permute-start | bytes 589832 | tf_op jit(solution)/shard_map/ppermute | solution.py:121
  23.3 10.1 %collective-permute-start.12 = (bf16[2,16,4096]{2,1,0:T(8,128)(2,1)S(1)}, bf16[2,16,4096]{2,1,0:T(8,128)(2,1)S(1)}, u32[]{:S(2)}, u32[]{:S(2)}) collective-permute-start(bf16[2,16,4096]{2,1,0:T(8,128)(2,1)S(1)} %shard_map.139.refs_2_.refs_0_), channel_id=1, source_target_pairs={{0,8},{1,9},{2,10},{3,11},{4,12},{5,13},{6,14},{7,15},{8,0},{9,1},... | collective-permute-start | bytes 786440 | tf_op jit(solution)/shard_map/ppermute | solution.py:121
  31.7 3.5 %collective-permute-start.8 = (bf16[4,16,2048]{2,1,0:T(8,128)(2,1)S(1)}, bf16[4,16,2048]{2,1,0:T(8,128)(2,1)S(1)}, u32[]{:S(2)}, u32[]{:S(2)}) collective-permute-start(bf16[4,16,2048]{2,1,0:T(8,128)(2,1)S(1)} %shard_map.140.refs_1_), channel_id=1, source_target_pairs={{0,1},{1,0},{2,3},{3,2},{4,5},{5,4},{6,7},{7,6},{8,9},{9,8},{10,11... | collective-permute-start | bytes 786440 | tf_op jit(solution)/shard_map/ppermute | solution.py:121
  31.7 3.8 %collective-permute-start.9 = (bf16[4,16,2048]{2,1,0:T(8,128)(2,1)S(1)}, bf16[4,16,2048]{2,1,0:T(8,128)(2,1)S(1)}, u32[]{:S(2)}, u32[]{:S(2)}) collective-permute-start(bf16[4,16,2048]{2,1,0:T(8,128)(2,1)S(1)} %collective-permute-done.4.refs_2_), channel_id=1, source_target_pairs={{0,1},{1,0},{2,3},{3,2},{4,5},{5,4},{6,7},{7,6},{8,9},{9,8},{10,11... | collective-permute-start | bytes 786440 | tf_op jit(solution)/shard_map/ppermute | solution.py:121
  32.2 3.3 %collective-permute-start.10 = (bf16[4,16,2048]{2,1,0:T(8,128)(2,1)S(1)}, bf16[4,16,2048]{2,1,0:T(8,128)(2,1)S(1)}, u32[]{:S(2)}, u32[]{:S(2)}) collective-permute-start(bf16[4,16,2048]{2,1,0:T(8,128)(2,1)S(1)} %collective-permute-done.5.refs_3_), channel_id=1, source_target_pairs={{0,1},{1,0},{2,3},{3,2},{4,5},{5,4},{6,7},{7,6},{8,9},{9,8},{10,11... | collective-permute-start | bytes 786440 | tf_op jit(solution)/shard_map/ppermute | solution.py:121
  32.3 5.1 %collective-permute-start.11 = (bf16[4,16,2048]{2,1,0:T(8,128)(2,1)S(1)}, bf16[4,16,2048]{2,1,0:T(8,128)(2,1)S(1)}, u32[]{:S(2)}, u32[]{:S(2)}) collective-permute-start(bf16[4,16,2048]{2,1,0:T(8,128)(2,1)S(1)} %collective-permute-done.6.refs_4_), channel_id=1, source_target_pairs={{0,1},{1,0},{2,3},{3,2},{4,5},{5,4},{6,7},{7,6},{8,9},{9,8},{10,11... | collective-permute-start | bytes 786440 | tf_op jit(solution)/shard_map/ppermute | solution.py:121
  33.4 16.3 %collective-permute-start.13 = (bf16[4,16,4096]{2,1,0:T(8,128)(2,1)S(1)}, bf16[4,16,4096]{2,1,0:T(8,128)(2,1)S(1)}, u32[]{:S(2)}, u32[]{:S(2)}) collective-permute-start(bf16[4,16,4096]{2,1,0:T(8,128)(2,1)S(1)} %shard_map.141.refs_12_.refs_1_), channel_id=1, source_target_pairs={{0,2},{1,5},{2,0},{3,7},{4,6},{5,1},{6,4},{7,3},{8,10},{9,13},{10,... | collective-permute-start | bytes 1572872 | tf_op jit(solution)/shard_map/ppermute | solution.py:121
  35.2 14.5 %collective-permute-start.14 = (bf16[4,16,4096]{2,1,0:T(8,128)(2,1)S(1)}, bf16[4,16,4096]{2,1,0:T(8,128)(2,1)S(1)}, u32[]{:S(2)}, u32[]{:S(2)}) collective-permute-start(bf16[4,16,4096]{2,1,0:T(8,128)(2,1)S(1)} %shard_map.141.refs_12_.refs_1_), channel_id=1, source_target_pairs={{0,4},{1,3},{2,6},{3,1},{4,0},{5,7},{6,2},{7,5},{8,12},{9,11},{10,... | collective-permute-start | bytes 1572872 | tf_op jit(solution)/shard_map/ppermute | solution.py:121
  35.6 16.7 %collective-permute-start.19 = (bf16[4,16,4096]{2,1,0:T(8,128)(2,1)S(1)}, bf16[4,16,4096]{2,1,0:T(8,128)(2,1)S(1)}, u32[]{:S(2)}, u32[]{:S(2)}) collective-permute-start(bf16[4,16,4096]{2,1,0:T(8,128)(2,1)S(1)} %shard_map.141.refs_12_.refs_1_), channel_id=1, source_target_pairs={{0,1},{1,0},{2,3},{3,2},{4,5},{5,4},{6,7},{7,6},{8,9},{9,8},{10,11... | collective-permute-start | bytes 1572872 | tf_op jit(solution)/shard_map/ppermute | solution.py:121
  35.6 13.3 %collective-permute-start.15 = (bf16[1,16,6144]{2,1,0:T(8,128)(2,1)S(1)}, bf16[1,16,6144]{2,1,0:T(8,128)(2,1)S(1)}, u32[]{:S(2)}, u32[]{:S(2)}) collective-permute-start(bf16[1,16,6144]{2,1,0:T(8,128)(2,1)S(1)} %collective-permute-done.7.refs_2_), channel_id=1, source_target_pairs={{0,4},{1,3},{2,6},{3,1},{4,0},{5,7},{6,2},{7,5},{8,12},{9,11},{10,... | collective-permute-start | bytes 589832 | tf_op jit(solution)/shard_map/ppermute | solution.py:121
  49.0 10.3 %collective-permute-start.18 = (bf16[4,16,2048]{2,1,0:T(8,128)(2,1)S(1)}, bf16[4,16,2048]{2,1,0:T(8,128)(2,1)S(1)}, u32[]{:S(2)}, u32[]{:S(2)}) collective-permute-start(bf16[4,16,2048]{2,1,0:T(8,128)(2,1)S(1)} %get-tuple-element.51.refs_13_.refs_0_), channel_id=1, source_target_pairs={{0,8},{1,9},{2,10},{3,11},{4,12},{5,13},{6,14},{7,15},{8,0},{9,1},... | collective-permute-start | bytes 786440 | tf_op jit(solution)/shard_map/ppermute | solution.py:121
  49.8 9.6 %collective-permute-start.16 = (bf16[2,16,4096]{2,1,0:T(8,128)(2,1)S(1)}, bf16[2,16,4096]{2,1,0:T(8,128)(2,1)S(1)}, u32[]{:S(2)}, u32[]{:S(2)}) collective-permute-start(bf16[2,16,4096]{2,1,0:T(8,128)(2,1)S(1)} %slice.39), channel_id=1, source_target_pairs={{0,4},{1,3},{2,6},{3,1},{4,0},{5,7},{6,2},{7,5},{8,12},{9,11},{10,... | collective-permute-start | bytes 786440 | tf_op jit(solution)/shard_map/ppermute | solution.py:121
  50.8 8.6 %collective-permute-start.17 = (bf16[2,16,4096]{2,1,0:T(8,128)(2,1)S(1)}, bf16[2,16,4096]{2,1,0:T(8,128)(2,1)S(1)}, u32[]{:S(2)}, u32[]{:S(2)}) collective-permute-start(bf16[2,16,4096]{2,1,0:T(8,128)(2,1)S(1)} %slice.40), channel_id=1, source_target_pairs={{0,2},{1,5},{2,0},{3,7},{4,6},{5,1},{6,4},{7,3},{8,10},{9,13},{10,... | collective-permute-start | bytes 786440 | tf_op jit(solution)/shard_map/ppermute | solution.py:121
  51.9 7.5 %collective-permute-start.20 = (bf16[4,16,4096]{2,1,0:T(8,128)(2,1)S(1)}, bf16[4,16,4096]{2,1,0:T(8,128)(2,1)S(1)}, u32[]{:S(2)}, u32[]{:S(2)}) collective-permute-start(bf16[4,16,4096]{2,1,0:T(8,128)(2,1)S(1)} %collective-permute-done.13.refs_2_), channel_id=1, source_target_pairs={{0,1},{1,0},{2,3},{3,2},{4,5},{5,4},{6,7},{7,6},{8,9},{9,8},{10,11... | collective-permute-start | bytes 1572872 | tf_op jit(solution)/shard_map/ppermute | solution.py:121
  52.3 7.0 %collective-permute-start.21 = (bf16[4,16,4096]{2,1,0:T(8,128)(2,1)S(1)}, bf16[4,16,4096]{2,1,0:T(8,128)(2,1)S(1)}, u32[]{:S(2)}, u32[]{:S(2)}) collective-permute-start(bf16[4,16,4096]{2,1,0:T(8,128)(2,1)S(1)} %collective-permute-done.14.refs_3_), channel_id=1, source_target_pairs={{0,1},{1,0},{2,3},{3,2},{4,5},{5,4},{6,7},{7,6},{8,9},{9,8},{10,11... | collective-permute-start | bytes 1572872 | tf_op jit(solution)/shard_map/ppermute | solution.py:121
  59.4 2.0 %collective-permute-start.22 = (bf16[4,16,4096]{2,1,0:T(8,128)(2,1)S(1)}, bf16[4,16,4096]{2,1,0:T(8,128)(2,1)S(1)}, u32[]{:S(2)}, u32[]{:S(2)}) collective-permute-start(bf16[4,16,4096]{2,1,0:T(8,128)(2,1)S(1)} %shard_map.145.refs_4_), channel_id=1, source_target_pairs={{0,1},{1,0},{2,3},{3,2},{4,5},{5,4},{6,7},{7,6},{8,9},{9,8},{10,11... | collective-permute-start | bytes 1572872 | tf_op jit(solution)/shard_map/ppermute | solution.py:121
  66.2 1.8 %collective-permute-start.23 = (bf16[2,36,512]{2,1,0:T(8,128)(2,1)S(1)}, bf16[2,36,512]{2,1,0:T(8,128)(2,1)S(1)}, u32[]{:S(2)}, u32[]{:S(2)}) collective-permute-start(bf16[2,36,512]{2,1,0:T(8,128)(2,1)S(1)} %get-tuple-element.59.refs_2_), channel_id=1, source_target_pairs={{1,0},{0,1},{3,2},{2,3},{5,4},{4,5},{7,6},{6,7},{9,8},{8,9},{11,10... | collective-permute-start | bytes 221192 | tf_op jit(solution)/shard_map/ppermute | solution.py:385
  66.7 19.9 %collective-permute-start.32 = (bf16[4,16,4096]{2,1,0:T(8,128)(2,1)S(1)}, bf16[4,16,4096]{2,1,0:T(8,128)(2,1)S(1)}, u32[]{:S(2)}, u32[]{:S(2)}) collective-permute-start(bf16[4,16,4096]{2,1,0:T(8,128)(2,1)S(1)} %get-tuple-element.68.refs_0_), channel_id=1, source_target_pairs={{0,8},{1,9},{2,10},{3,11},{4,12},{5,13},{6,14},{7,15},{8,0},{9,1},... | collective-permute-start | bytes 1572872 | tf_op jit(solution)/shard_map/ppermute | solution.py:121
  68.1 18.5 %collective-permute-start.24 = (bf16[8,36,512]{2,1,0:T(8,128)(2,1)S(1)}, bf16[8,36,512]{2,1,0:T(8,128)(2,1)S(1)}, u32[]{:S(2)}, u32[]{:S(2)}) collective-permute-start(bf16[8,36,512]{2,1,0:T(8,128)(2,1)S(1)} %shard_map.149), channel_id=1, source_target_pairs={{2,0},{3,1},{4,2},{5,3},{6,4},{7,5},{8,6},{9,7},{10,8},{11,9},{12,... | collective-permute-start | bytes 884744 | tf_op jit(solution)/shard_map/ppermute | solution.py:385
  73.2 8.0 %collective-permute-start.26 = (bf16[4,16,2048]{2,1,0:T(8,128)(2,1)S(1)}, bf16[4,16,2048]{2,1,0:T(8,128)(2,1)S(1)}, u32[]{:S(2)}, u32[]{:S(2)}) collective-permute-start(bf16[4,16,2048]{2,1,0:T(8,128)(2,1)S(1)} %get-tuple-element.56.refs_10_.refs_2_), channel_id=1, source_target_pairs={{0,4},{1,3},{2,6},{3,1},{4,0},{5,7},{6,2},{7,5},{8,12},{9,11},{10,... | collective-permute-start | bytes 786440 | tf_op jit(solution)/shard_map/ppermute | solution.py:121
  73.2 10.2 %collective-permute-start.27 = (bf16[4,16,2048]{2,1,0:T(8,128)(2,1)S(1)}, bf16[4,16,2048]{2,1,0:T(8,128)(2,1)S(1)}, u32[]{:S(2)}, u32[]{:S(2)}) collective-permute-start(bf16[4,16,2048]{2,1,0:T(8,128)(2,1)S(1)} %get-tuple-element.57.refs_11_.refs_3_), channel_id=1, source_target_pairs={{0,2},{1,5},{2,0},{3,7},{4,6},{5,1},{6,4},{7,3},{8,10},{9,13},{10,... | collective-permute-start | bytes 786440 | tf_op jit(solution)/shard_map/ppermute | solution.py:121
  73.2 15.2 %collective-permute-start.28 = (bf16[4,16,2048]{2,1,0:T(8,128)(2,1)S(1)}, bf16[4,16,2048]{2,1,0:T(8,128)(2,1)S(1)}, u32[]{:S(2)}, u32[]{:S(2)}) collective-permute-start(bf16[4,16,2048]{2,1,0:T(8,128)(2,1)S(1)} %get-tuple-element.56.refs_10_.refs_2_), channel_id=1, source_target_pairs={{0,1},{1,0},{2,3},{3,2},{4,5},{5,4},{6,7},{7,6},{8,9},{9,8},{10,11... | collective-permute-start | bytes 786440 | tf_op jit(solution)/shard_map/ppermute | solution.py:121
  78.1 14.8 %copy-start.5 = (f32[144,256]{1,0:T(8,128)S(1)}, f32[144,256]{1,0:T(8,128)}, u32[]{:S(2)}) copy-start(f32[144,256]{1,0:T(8,128)} %constant.10.clone.refs_13_) | copy-start | bytes 442372
  81.2 7.6 %collective-permute-start.29 = (bf16[4,16,2048]{2,1,0:T(8,128)(2,1)S(1)}, bf16[4,16,2048]{2,1,0:T(8,128)(2,1)S(1)}, u32[]{:S(2)}, u32[]{:S(2)}) collective-permute-start(bf16[4,16,2048]{2,1,0:T(8,128)(2,1)S(1)} %get-tuple-element.57.refs_11_.refs_3_), channel_id=1, source_target_pairs={{0,1},{1,0},{2,3},{3,2},{4,5},{5,4},{6,7},{7,6},{8,9},{9,8},{10,11... | collective-permute-start | bytes 786440 | tf_op jit(solution)/shard_map/ppermute | solution.py:121
  83.5 5.4 %collective-permute-start.30 = (bf16[4,16,2048]{2,1,0:T(8,128)(2,1)S(1)}, bf16[4,16,2048]{2,1,0:T(8,128)(2,1)S(1)}, u32[]{:S(2)}, u32[]{:S(2)}) collective-permute-start(bf16[4,16,2048]{2,1,0:T(8,128)(2,1)S(1)} %collective-permute-done.26.refs_4_), channel_id=1, source_target_pairs={{0,1},{1,0},{2,3},{3,2},{4,5},{5,4},{6,7},{7,6},{8,9},{9,8},{10,11... | collective-permute-start | bytes 786440 | tf_op jit(solution)/shard_map/ppermute | solution.py:121
  86.6 6.4 %collective-permute-start.31 = (bf16[4,16,2048]{2,1,0:T(8,128)(2,1)S(1)}, bf16[4,16,2048]{2,1,0:T(8,128)(2,1)S(1)}, u32[]{:S(2)}, u32[]{:S(2)}) collective-permute-start(bf16[4,16,2048]{2,1,0:T(8,128)(2,1)S(1)} %collective-permute-done.27.refs_5_), channel_id=1, source_target_pairs={{0,1},{1,0},{2,3},{3,2},{4,5},{5,4},{6,7},{7,6},{8,9},{9,8},{10,11... | collective-permute-start | bytes 786440 | tf_op jit(solution)/shard_map/ppermute | solution.py:121
  86.6 1.6 %collective-permute-start.25 = (bf16[2,36,512]{2,1,0:T(8,128)(2,1)S(1)}, bf16[2,36,512]{2,1,0:T(8,128)(2,1)S(1)}, u32[]{:S(2)}, u32[]{:S(2)}) collective-permute-start(bf16[2,36,512]{2,1,0:T(8,128)(2,1)S(1)} %get-tuple-element.64), channel_id=1, source_target_pairs={{1,0},{0,1},{3,2},{2,3},{5,4},{4,5},{7,6},{6,7},{9,8},{8,9},{11,10... | collective-permute-start | bytes 221192 | tf_op jit(solution)/shard_map/ppermute | solution.py:385
  88.2 15.3 %collective-permute-start.35 = (bf16[4,16,4096]{2,1,0:T(8,128)(2,1)S(1)}, bf16[4,16,4096]{2,1,0:T(8,128)(2,1)S(1)}, u32[]{:S(2)}, u32[]{:S(2)}) collective-permute-start(bf16[4,16,4096]{2,1,0:T(8,128)(2,1)S(1)} %get-tuple-element.71.refs_1_), channel_id=1, source_target_pairs={{0,1},{1,0},{2,3},{3,2},{4,5},{5,4},{6,7},{7,6},{8,9},{9,8},{10,11... | collective-permute-start | bytes 1572872 | tf_op jit(solution)/shard_map/ppermute | solution.py:121
  88.4 15.1 %collective-permute-start.36 = (bf16[4,16,4096]{2,1,0:T(8,128)(2,1)S(1)}, bf16[4,16,4096]{2,1,0:T(8,128)(2,1)S(1)}, u32[]{:S(2)}, u32[]{:S(2)}) collective-permute-start(bf16[4,16,4096]{2,1,0:T(8,128)(2,1)S(1)} %get-tuple-element.72.refs_2_), channel_id=1, source_target_pairs={{0,1},{1,0},{2,3},{3,2},{4,5},{5,4},{6,7},{7,6},{8,9},{9,8},{10,11... | collective-permute-start | bytes 1572872 | tf_op jit(solution)/shard_map/ppermute | solution.py:121
  88.9 13.6 %collective-permute-start.33 = (bf16[4,16,4096]{2,1,0:T(8,128)(2,1)S(1)}, bf16[4,16,4096]{2,1,0:T(8,128)(2,1)S(1)}, u32[]{:S(2)}, u32[]{:S(2)}) collective-permute-start(bf16[4,16,4096]{2,1,0:T(8,128)(2,1)S(1)} %get-tuple-element.71.refs_1_), channel_id=1, source_target_pairs={{0,4},{1,3},{2,6},{3,1},{4,0},{5,7},{6,2},{7,5},{8,12},{9,11},{10,... | collective-permute-start | bytes 1572872 | tf_op jit(solution)/shard_map/ppermute | solution.py:121
  88.9 14.0 %collective-permute-start.34 = (bf16[4,16,4096]{2,1,0:T(8,128)(2,1)S(1)}, bf16[4,16,4096]{2,1,0:T(8,128)(2,1)S(1)}, u32[]{:S(2)}, u32[]{:S(2)}) collective-permute-start(bf16[4,16,4096]{2,1,0:T(8,128)(2,1)S(1)} %get-tuple-element.72.refs_2_), channel_id=1, source_target_pairs={{0,2},{1,5},{2,0},{3,7},{4,6},{5,1},{6,4},{7,3},{8,10},{9,13},{10,... | collective-permute-start | bytes 1572872 | tf_op jit(solution)/shard_map/ppermute | solution.py:121
  102.8 2.2 %collective-permute-start.37 = (bf16[4,16,4096]{2,1,0:T(8,128)(2,1)S(1)}, bf16[4,16,4096]{2,1,0:T(8,128)(2,1)S(1)}, u32[]{:S(2)}, u32[]{:S(2)}) collective-permute-start(bf16[4,16,4096]{2,1,0:T(8,128)(2,1)S(1)} %collective-permute-done.33.refs_3_), channel_id=1, source_target_pairs={{0,1},{1,0},{2,3},{3,2},{4,5},{5,4},{6,7},{7,6},{8,9},{9,8},{10,11... | collective-permute-start | bytes 1572872 | tf_op jit(solution)/shard_map/ppermute | solution.py:121
  103.5 2.3 %collective-permute-start.38 = (bf16[4,16,4096]{2,1,0:T(8,128)(2,1)S(1)}, bf16[4,16,4096]{2,1,0:T(8,128)(2,1)S(1)}, u32[]{:S(2)}, u32[]{:S(2)}) collective-permute-start(bf16[4,16,4096]{2,1,0:T(8,128)(2,1)S(1)} %collective-permute-done.34.refs_4_), channel_id=1, source_target_pairs={{0,1},{1,0},{2,3},{3,2},{4,5},{5,4},{6,7},{7,6},{8,9},{9,8},{10,11... | collective-permute-start | bytes 1572872 | tf_op jit(solution)/shard_map/ppermute | solution.py:121
  110.6 1.4 %collective-permute-start.39 = (bf16[2,36,512]{2,1,0:T(8,128)(2,1)S(1)}, bf16[2,36,512]{2,1,0:T(8,128)(2,1)S(1)}, u32[]{:S(2)}, u32[]{:S(2)}) collective-permute-start(bf16[2,36,512]{2,1,0:T(8,128)(2,1)S(1)} %get-tuple-element.75), channel_id=1, source_target_pairs={{1,0},{0,1},{3,2},{2,3},{5,4},{4,5},{7,6},{6,7},{9,8},{8,9},{11,10... | collective-permute-start | bytes 221192 | tf_op jit(solution)/shard_map/ppermute | solution.py:385
  112.0 15.5 %collective-permute-start.40 = (bf16[8,36,512]{2,1,0:T(8,128)(2,1)S(1)}, bf16[8,36,512]{2,1,0:T(8,128)(2,1)S(1)}, u32[]{:S(2)}, u32[]{:S(2)}) collective-permute-start(bf16[8,36,512]{2,1,0:T(8,128)(2,1)S(1)} %shard_map.154), channel_id=1, source_target_pairs={{30,0},{31,1},{0,2},{1,3},{2,4},{3,5},{4,6},{5,7},{6,8},{7,9},{8,1... | collective-permute-start | bytes 884744 | tf_op jit(solution)/shard_map/ppermute | solution.py:385
  126.1 1.3 %collective-permute-start.41 = (bf16[2,36,512]{2,1,0:T(8,128)(2,1)S(1)}, bf16[2,36,512]{2,1,0:T(8,128)(2,1)S(1)}, u32[]{:S(2)}, u32[]{:S(2)}) collective-permute-start(bf16[2,36,512]{2,1,0:T(8,128)(2,1)S(1)} %get-tuple-element.82), channel_id=1, source_target_pairs={{1,0},{0,1},{3,2},{2,3},{5,4},{4,5},{7,6},{6,7},{9,8},{8,9},{11,10... | collective-permute-start | bytes 221192 | tf_op jit(solution)/shard_map/ppermute | solution.py:385
